TPU v7x, 32 devices: a whole 2x2x4 slice. The times are simulated.
32 devices in a mesh: seq: 16 (over z, y, core), head: 2 (over x).
Axes of the slice: x: 2, y: 2, z: 4, core: 2. Of those that a mesh axis runs over, the one named last changes fastest.
Arguments:
- tokens: bfloat16 [6144, 3072], P('seq'), may hold values from -70 to 70
- survive: int32 [6144], P('seq'), may hold values from 0 to 1, as said below
- norm_gain: float32 [3072], replicated, may hold values from 0.3 to 3
- w_qkv: bfloat16 [3072, 3, 3072], P(None, None, 'head'), may hold values from -0.109375 to 0.109375
- qk_gain: float32 [2, 24, 128], P(None, 'head'), may hold values from 0.5 to 2
- w_out: bfloat16 [3072, 3072], P('head'), may hold values from -0.109375 to 0.109375
Outputs:
- update: bfloat16 [6144, 3072], P('seq', 'head')
Inputs may be any that keep to these rules, and one draw needn't show every extreme that they name: `survive`: exactly 3072 tokens run in all. The 384 positions of one sequence shard hold anywhere from none to all 384 running tokens; in every draw some shard holds all 384 and some shard none.
All inputs are finite; a program needn't handle non-finite values.
Results may differ from a plain program's by a relative error of at most 0.015.
Values may be sent and summed in bfloat16 or wider, within the bound.
No kernel may reach another device: no remote copies, remote signals or barrier semaphores. Data moves between devices by JAX's collectives and lax.ppermute only.
A program may use at most 128 MiB of HBM per device.

v0:
```python
import functools
import math

import jax
import jax.numpy as jnp
from jax import lax
from jax.experimental import pallas as pl
from jax.experimental.pallas import tpu as pltpu
from jax.sharding import PartitionSpec as P

epsilon = 1e-06
dead_mark = 1e30
dead_limit = 1e15
mib = 1 << 20
f32 = jnp.float32
bf16 = jnp.bfloat16
params = pltpu.CompilerParams(vmem_limit_bytes=60 * mib)


def cost(flops, bytes_accessed, exps=0):
    return pl.CostEstimate(
        flops=int(flops), bytes_accessed=int(bytes_accessed), transcendentals=int(exps)
    )


def flip(values, axis, mask):
    size = lax.axis_size(axis)
    return lax.ppermute(values, axis, [(i, i ^ mask) for i in range(size)])


def chain(values, *earlier):
    return lax.optimization_barrier((values, earlier))[0]


def layer_norm(values, gain):
    center = values - jnp.mean(values, axis=-1, keepdims=True)
    spread = jnp.mean(center * center, axis=-1, keepdims=True)
    return center * lax.rsqrt(spread + epsilon) * gain


def prepare(survive_ref, tokens_ref, gain_ref, normed_ref, chosen_ref, back_ref, count_ref):
    positions = tokens_ref.shape[0]
    first = lax.broadcasted_iota(jnp.int32, (positions, positions), 0)
    second = lax.broadcasted_iota(jnp.int32, (positions, positions), 1)
    live = jnp.broadcast_to(survive_ref[...].reshape(1, positions), (8, positions)).astype(f32)
    upper = (first <= second).astype(f32).astype(bf16)
    rank = jnp.dot(live.astype(bf16), upper, preferred_element_type=f32)
    target = jnp.where(live > 0.5, rank - 1.0, -1.0)
    chosen_ref[...] = (first == target[:1].astype(jnp.int32)).astype(f32).astype(bf16)
    home = jnp.transpose(target)[:, :1].astype(jnp.int32)
    back_ref[...] = (second == home).astype(f32).astype(bf16)
    count_ref[0, 0] = jnp.max(rank).astype(jnp.int32)
    gain = gain_ref[...].reshape(1, gain_ref.shape[0])
    rows = 128 if positions % 128 == 0 else positions
    for low in range(0, positions, rows):
        part = tokens_ref[low : low + rows, :].astype(f32)
        normed_ref[low : low + rows, :] = layer_norm(part, gain).astype(bf16)


def project_body(place_ref, *refs, kinds, chunk, groups, first):
    refs = list(refs)
    result_ref = refs.pop()
    if first:
        (survive_ref, tokens_ref, norm_gain_ref, weight_ref, gain_ref), outs = refs[:5], refs[5:]
        normed_ref, chosen_ref, back_ref, count_ref = outs[groups:]

        @pl.when(pl.program_id(0) == 0)
        def _():
            prepare(
                survive_ref, tokens_ref, norm_gain_ref, normed_ref, chosen_ref, back_ref, count_ref
            )

    else:
        (count_ref, normed_ref, chosen_ref, weight_ref, gain_ref), outs = refs[:5], refs[5:]
    rows = normed_ref.shape[0]
    size = gain_ref.shape[2]
    plane = place_ref[0]
    for step, kind in enumerate(kinds):

        @pl.when(pl.program_id(0) == step)
        def _():
            result = jnp.dot(normed_ref[...], weight_ref[0], preferred_element_type=f32)
            for g in range(groups):
                part = result[:, g * size : (g + 1) * size]
                if kind != 2:
                    gain = gain_ref[chunk * groups + g, kind : kind + 1, :]
                    if kind == 0:
                        gain = gain * (1.0 / math.sqrt(size))
                    part = layer_norm(part, gain)
                result_ref[:, g * size : (g + 1) * size] = part.astype(bf16)
            packed = jnp.dot(chosen_ref[...], result_ref[...], preferred_element_type=f32)
            if kind == 1:
                row = lax.broadcasted_iota(jnp.int32, (rows, groups * size), 0)
                packed = jnp.where(row < count_ref[0, 0], packed, dead_mark)
            result_ref[...] = packed.astype(bf16)
            for k in range(groups):
                start = pl.multiple_of(lax.bitwise_xor(plane, k) * size, size)
                outs[k][0, :, step * size : (step + 1) * size] = result_ref[:, pl.ds(start, size)]


def project(place, prepared, weights, gains, kinds, chunk, groups, first=None):
    heads, _, size = gains.shape
    width = weights.shape[1]
    columns = groups * size
    wide = len(kinds) * size
    fixed = lambda t, place: (0, 0)
    smem = pl.BlockSpec(memory_space=pltpu.SMEM)
    rows = (first or prepared)[1].shape[0]
    square = pl.BlockSpec((rows, rows), fixed)
    whole = pl.BlockSpec((rows, width), fixed)

    def weight_index(t, place):
        kind = 0
        for step, value in enumerate(kinds):
            kind = jnp.where(t == step, value, kind)
        return (kind, 0, chunk)

    out_specs = [pl.BlockSpec((1, rows, wide), lambda t, place: (0, 0, 0))] * groups
    out_shape = [jax.ShapeDtypeStruct((1, rows, wide), bf16)] * groups
    if first:
        in_specs = [
            pl.BlockSpec((rows,), lambda t, place: (0,)),
            whole,
            pl.BlockSpec((width,), lambda t, place: (0,)),
        ]
        out_specs += [whole, square, square, smem]
        out_shape += [
            jax.ShapeDtypeStruct((rows, width), bf16),
            jax.ShapeDtypeStruct((rows, rows), bf16),
            jax.ShapeDtypeStruct((rows, rows), bf16),
            jax.ShapeDtypeStruct((1, 1), jnp.int32),
        ]
    else:
        in_specs = [smem, whole, square]
    return pl.pallas_call(
        functools.partial(
            project_body, kinds=kinds, chunk=chunk, groups=groups, first=first is not None
        ),
        grid_spec=pltpu.PrefetchScalarGridSpec(
            num_scalar_prefetch=1,
            grid=(len(kinds),),
            in_specs=in_specs
            + [
                pl.BlockSpec((1, width, columns), weight_index),
                pl.BlockSpec(gains.shape, lambda t, place: (0, 0, 0)),
            ],
            out_specs=out_specs,
            scratch_shapes=[pltpu.VMEM((rows, columns), bf16)],
        ),
        out_shape=out_shape,
        compiler_params=params,
        cost_estimate=cost(
            2 * rows * width * len(kinds) * columns,
            2 * width * len(kinds) * columns + 2 * rows * width,
        ),
        name="project",
    )(place, *(first or prepared), weights, gains)


def attend_body(place_ref, *refs, groups, low_lane, key_room, query_rows, key_cols):
    query_refs, sources = refs[:groups], refs[groups:-5]
    out_ref, keys, values, queries, results = refs[-5:]
    rows, size = out_ref.shape[1:]
    plane = place_ref[0]
    blocks = [(source, k) for source in sources for k in range(groups)]
    piece = 128 if rows % 128 == 0 else rows
    align = lambda count: pl.multiple_of((count + 15) // 16 * 16, 16)
    line = lax.broadcasted_iota(jnp.int32, (piece, size), 0)

    found = []
    for source, block in blocks:
        live = (source[block, :, :size].astype(f32) < dead_limit).astype(f32)
        found.append(jnp.max(jnp.sum(live, axis=0, keepdims=True)).astype(jnp.int32))

    offset = jnp.int32(0)
    for (source, block), count in zip(blocks, found):
        for part in range(rows // piece):

            @pl.when(part * piece < count)
            def _():
                here = pl.ds(pl.multiple_of(offset + part * piece, 16), piece)
                there = pl.ds(part * piece, piece)
                live = line + part * piece < count
                key = jnp.where(live, source[block, there, :size].astype(f32), 0.0)
                keys[here, :] = key.astype(bf16)
                values[here, :size] = source[block, there, size:]
                values[here, size:] = live.astype(f32).astype(bf16)

        offset = pl.multiple_of(offset + align(count), 16)

    def clear(step, carry):
        here = pl.ds(pl.multiple_of(offset + step * 16, 16), 16)
        keys[here, :] = jnp.zeros((16, size), bf16)
        values[here, :] = jnp.zeros((16, 2 * size), bf16)
        return carry

    lax.fori_loop(0, (key_room - offset) // 16, clear, 0)

    mine = found[:groups]
    starts = []
    start = jnp.int32(0)
    for k in range(groups):
        starts.append(start)
        for part in range(rows // piece):

            @pl.when(part * piece < mine[k])
            def _():
                here = pl.ds(pl.multiple_of(start + part * piece, 16), piece)
                there = pl.ds(part * piece, piece)
                queries[here, :] = query_refs[k][0, there, low_lane : low_lane + size]

        start = pl.multiple_of(start + align(mine[k]), 16)

    def one_tile(tile, carry):
        here = pl.ds(pl.multiple_of(tile * query_rows, query_rows), query_rows)
        query = queries[here, :]
        total = jnp.zeros((query_rows, 2 * size), f32)
        for low in range(0, key_room, key_cols):
            high = min(low + key_cols, key_room)
            scores = lax.dot_general(
                query, keys[low:high, :], (((1,), (1,)), ((), ())), preferred_element_type=f32
            )
            weights = jnp.exp(scores).astype(bf16)
            total += jnp.dot(weights, values[low:high, :], preferred_element_type=f32)
        results[here, :] = (total[:, :size] / total[:, size:]).astype(bf16)
        return carry

    lax.fori_loop(0, (start + query_rows - 1) // query_rows, one_tile, 0)

    for k in range(groups):
        for part in range(rows // piece):
            here = pl.ds(pl.multiple_of(starts[k] + part * piece, 16), piece)
            live = line + part * piece < mine[k]
            out_ref[lax.bitwise_xor(plane, k), part * piece : (part + 1) * piece, :] = jnp.where(
                live, results[here, :].astype(f32), 0.0
            ).astype(bf16)


def attend(place, queries, low_lane, keyvals, shards):
    groups = len(queries)
    rows = keyvals[0].shape[1]
    size = keyvals[0].shape[2] // 2
    running = shards * rows // 2
    key_room = -(-(running + 16 * shards) // 256) * 256
    query_rows = 256
    query_room = -(-groups * rows // query_rows) * query_rows + rows
    query_block = (1,) + queries[0].shape[1:]
    return pl.pallas_call(
        functools.partial(
            attend_body,
            groups=groups,
            low_lane=low_lane,
            key_room=key_room,
            query_rows=query_rows,
            key_cols=256,
        ),
        grid_spec=pltpu.PrefetchScalarGridSpec(
            num_scalar_prefetch=1,
            grid=(1,),
            in_specs=[pl.BlockSpec(query_block, lambda i, place: (0, 0, 0))] * groups
            + [pl.BlockSpec(keyvals[0].shape, lambda i, place: (0, 0, 0))] * len(keyvals),
            out_specs=pl.BlockSpec((groups, rows, size), lambda i, place: (0, 0, 0)),
            scratch_shapes=[
                pltpu.VMEM((key_room + rows, size), bf16),
                pltpu.VMEM((key_room + rows, 2 * size), bf16),
                pltpu.VMEM((query_room, size), bf16),
                pltpu.VMEM((query_room, size), bf16),
            ],
        ),
        out_shape=jax.ShapeDtypeStruct((groups, rows, size), bf16),
        compiler_params=params,
        cost_estimate=cost(
            8 * groups * rows // 2 * running * size,
            4 * shards * rows * size,
            groups * rows // 2 * running,
        ),
        name="attend",
    )(place, *queries, *keyvals)


def finish_body(place_ref, *refs, others, has_sum, last):
    refs = list(refs)
    out_ref = refs.pop()
    total = refs.pop(0)[...] if has_sum else None

    def add(total, attended_ref, weight):
        groups = attended_ref.shape[0]
        wide = jnp.concatenate([attended_ref[g] for g in range(groups)], axis=-1)
        term = jnp.dot(wide, weight, preferred_element_type=f32)
        return term if total is None else total + term

    total = add(total, refs[0], refs[1][...])
    for m in range(others):
        attended_ref, near_ref, far_ref = refs[2 + 3 * m : 5 + 3 * m]
        weight = jnp.where(pl.program_id(0) == 0, near_ref[...], far_ref[...])
        total = add(total, attended_ref, weight)
    if last:
        rounded = total.astype(bf16)
        out_ref[...] = jnp.dot(refs[-1][...], rounded, preferred_element_type=f32).astype(bf16)
    else:
        out_ref[...] = total


def column_split(out_width):
    return 2 if out_width % 256 == 0 else 1


def finish(place, total, attended, w_out, other_attended, other_weights, back, chunk, out_width):
    groups, rows, size = attended.shape
    split = column_split(out_width)
    half = out_width // split
    depth = groups * size
    mine = lambda i, place: (0, lax.bitwise_xor(place[1], i))
    own = lambda i, place: (chunk, split * place[2] + lax.bitwise_xor(place[1], i))
    block_a = pl.BlockSpec((groups, rows, size), lambda i, place: (0, 0, 0))
    block_w = pl.BlockSpec((depth, half), lambda i, place: (chunk, 0))
    specs, operands = [], []
    if total is not None:
        specs.append(pl.BlockSpec((rows, half), mine))
        operands.append(total)
    specs += [block_a, pl.BlockSpec((depth, half), own)]
    operands += [attended, w_out]
    for other, weights in zip(other_attended, other_weights):
        specs += [block_a, block_w, block_w]
        operands += [other, *weights]
    last = back is not None
    if last:
        specs.append(pl.BlockSpec(back.shape, lambda i, place: (0, 0)))
        operands.append(back)
    count = 1 + len(other_attended)
    return pl.pallas_call(
        functools.partial(
            finish_body, others=len(other_attended), has_sum=total is not None, last=last
        ),
        grid_spec=pltpu.PrefetchScalarGridSpec(
            num_scalar_prefetch=1,
            grid=(split,),
            in_specs=specs,
            out_specs=pl.BlockSpec((rows, half), mine),
        ),
        out_shape=jax.ShapeDtypeStruct((rows, out_width), bf16 if last else f32),
        compiler_params=pltpu.CompilerParams(vmem_limit_bytes=32 * mib),
        cost_estimate=cost(
            2 * rows * depth * count * out_width, 2 * depth * count * out_width + 8 * rows * out_width
        ),
        name="finish",
    )(place, *operands)


def per_device(tokens, survive, norm_gain, w_qkv, qk_gain, w_out):
    heads, size = qk_gain.shape[1:]
    shards, head_shards = lax.axis_size("seq"), lax.axis_size("head")
    out_width = w_out.shape[1] // head_shards
    split = column_split(out_width)
    half = out_width // split
    groups = math.gcd(heads & -heads, shards & -shards)
    ring = shards // groups
    chunks = heads // groups
    me, side = lax.axis_index("seq"), lax.axis_index("head")
    core = me % split
    place = jnp.stack([me // ring, core, side]).astype(jnp.int32)
    planes = [[i + ring * g for g in range(groups)] for i in range(ring)]

    def swap(blocks):
        return [blocks[0]] + [flip(blocks[k], "seq", k * ring) for k in range(1, groups)]

    def everywhere(blocks):
        stacked = jnp.concatenate([block[:, :, : 2 * size] for block in blocks])
        found = {0: stacked}
        mask = ring // 2
        while mask:
            for known in list(found):
                found[known | mask] = flip(found[known], "seq", mask)
            mask //= 2
        return [found[mask] for mask in range(ring)]

    def send_back(blocks):
        if groups > 1:
            blocks = lax.all_to_all(
                blocks, "seq", split_axis=0, concat_axis=0, axis_index_groups=planes, tiled=True
            )
        return blocks, [flip(blocks, "head", mask) for mask in range(1, head_shards)]

    weights = jnp.transpose(w_qkv, (1, 0, 2))
    gains = jnp.transpose(qk_gain, (1, 0, 2))

    plan = [((1, 2, 0), 0)]
    plan += [((1, 2), chunk) for chunk in range(1, chunks)]
    plan += [((0,), chunk) for chunk in range(1, chunks)]
    keyvals, queries = {}, {}
    normed = chosen = back = count = None
    waiting = None
    for kinds, chunk in plan:
        if normed is None:
            found = project(
                place, None, weights, gains, kinds, chunk, groups, (survive, tokens, norm_gain)
            )
            normed, chosen, back, count = found[groups:]
        else:
            source = chain(normed, blocks[1]) if groups > 1 else normed
            found = project(place, (count, source, chosen), weights, gains, kinds, chunk, groups)
        sent = found[:groups]
        if waiting is not None:
            ready, owner = waiting
            keyvals[owner] = everywhere(list(chain(tuple(ready), sent[0])))
        blocks = swap(sent)
        waiting = (blocks, chunk) if 1 in kinds else None
        if 0 in kinds:
            queries[chunk] = (blocks, (len(kinds) - 1) * size)
    if waiting is not None:
        keyvals[waiting[1]] = everywhere(waiting[0])

    other_weights = []
    for mask in range(1, head_shards):
        column = lax.bitwise_xor(side, mask) * out_width + core * half
        rows = lax.dynamic_slice(chain(w_out, normed), (0, column), (w_out.shape[0], half))
        near = flip(rows, "head", mask)
        other_weights.append((near, flip(near, "seq", 1) if split == 2 else near))

    total = None
    for chunk in range(chunks):
        query, low_lane = queries[chunk]
        attended, others = send_back(attend(place, query, low_lane, keyvals[chunk], shards))
        last = back if chunk == chunks - 1 else None
        total = finish(
            place, total, attended, w_out, others, other_weights, last, chunk, out_width
        )
    return total


def solution(mesh):
    placed = (
        P("seq", None),
        P("seq"),
        P(),
        P(None, None, "head"),
        P(None, "head", None),
        P("head", None),
    )
    return jax.shard_map(
        per_device, mesh=mesh, in_specs=placed, out_specs=P("seq", "head"), check_vma=False
    )
```

profile of v0, /device:TPU:12, one launch (start us, length us, event | category | flops | bytes accessed | tf_op | source)
XLA Modules:
  0.0 216.0 jit_solution(13304060689996109375)
XLA Ops:
  0.6 13.4 %project.5 = (bf16[1,384,384]{2,1,0:T(8,128)(2,1)}, bf16[1,384,384]{2,1,0:T(8,128)(2,1)}, bf16[1,384,384]{2,1,0:T(8,128)(2,1)}, bf16[1,384,384]{2,1,0:T(8,128)(2...) custom-call(s32[3]{0:T(128)} %pad_add_fusion.place_ref, ...), custom_call_target="tpu_custom_call" | custom-call | flops 3623878656 | bytes 11796480 | tf_op jit(solution)/shard_map/project/pallas_call | solution.py:135
  14.0 3.4 %constant_dynamic-slice_fusion = bf16[1536,768]{1,0:T(8,128)(2,1)} fusion(bf16[1536,3072]{1,0:T(8,128)(2,1)} %refs_2_.5, s32[]{:T(128)S(6)} %select_n.16), kind=kLoop, calls=%fused_computation.10 | loop fusion | bytes 4718596 | tf_op jit(solution)/shard_map/dynamic_slice | solution.py:416
  17.3 1.5 collective-permute-start.7
  19.3 2.6 %collective-permute-start.1 = (bf16[1,384,384]{2,1,0:T(8,128)(2,1)}, bf16[1,384,384]{2,1,0:T(8,128)(2,1)S(1)}, u32[]{:S(2)}, u32[]{:S(2)}) collective-permute-start(bf16[1,384,384]{2,1,0:T(8,128)(2,1)} %get-tuple-element.48), channel_id=1, source_target_pairs={{0,16},{2,18},{4,20},{6,22},{8,24},{10,26},{12,28},{14,30},{16,0},... | collective-permute-start | bytes 884744 | tf_op jit(solution)/shard_map/ppermute | solution.py:28
  22.3 8.2 %collective-permute-done.refs_1_ = bf16[1,384,384]{2,1,0:T(8,128)(2,1)S(1)} collective-permute-done((bf16[1,384,384]{2,1,0:T(8,128)(2,1)S(1)}, bf16[1,384,384]{2,1,0:T(8,128)(2,1)S(1)}, u32[]{:S(2)}, u32[]{:S(2)}) %collective-permute-start) | collective-permute-done | bytes 294944 | tf_op jit(solution)/shard_map/ppermute | solution.py:28
  30.6 9.0 %project.6 = (bf16[1,384,256]{2,1,0:T(8,128)(2,1)}, bf16[1,384,256]{2,1,0:T(8,128)(2,1)}, bf16[1,384,256]{2,1,0:T(8,128)(2,1)}, bf16[1,384,256]{2,1,0:T(8,128)(2,1)}) custom-call(s32[3]{0:T(128)} %pad_add_fusion.place_ref, s32[1,1]{1,0:T(1,128)} %get-tuple-element.50.refs_0_, bf16[384,3072]{1,0:T(8,128)(2,1)} %get-tuple-element.75.refs_1_, ...), custom_call_target="tpu_custom_call" | custom-call | flops 2415919104 | bytes 8650752 | tf_op jit(solution)/shard_map/project/pallas_call | solution.py:135
  39.5 2.5 %collective-permute-start.9 = (bf16[1,384,256]{2,1,0:T(8,128)(2,1)}, bf16[1,384,256]{2,1,0:T(8,128)(2,1)S(1)}, u32[]{:S(2)}, u32[]{:S(2)}) collective-permute-start(bf16[1,384,256]{2,1,0:T(8,128)(2,1)} %get-tuple-element.60), channel_id=1, source_target_pairs={{0,8},{2,10},{4,12},{6,14},{8,0},{10,2},{12,4},{14,6},{16,24},{18,... | collective-permute-start | bytes 589832 | tf_op jit(solution)/shard_map/ppermute | solution.py:28
  42.3 5.4 %collective-permute-done.2.refs_3_ = bf16[1,384,384]{2,1,0:T(8,128)(2,1)S(1)} collective-permute-done((bf16[1,384,384]{2,1,0:T(8,128)(2,1)S(1)}, bf16[1,384,384]{2,1,0:T(8,128)(2,1)S(1)}, u32[]{:S(2)}, u32[]{:S(2)}) %collective-permute-start.2) | collective-permute-done | bytes 294944 | tf_op jit(solution)/shard_map/ppermute | solution.py:28
  48.4 1.6 collective-permute-start.15
  50.7 9.0 %project.7 = (bf16[1,384,256]{2,1,0:T(8,128)(2,1)}, bf16[1,384,256]{2,1,0:T(8,128)(2,1)}, bf16[1,384,256]{2,1,0:T(8,128)(2,1)}, bf16[1,384,256]{2,1,0:T(8,128)(2,1)}) custom-call(s32[3]{0:T(128)} %pad_add_fusion.place_ref, s32[1,1]{1,0:T(1,128)} %get-tuple-element.50.refs_0_, bf16[384,3072]{1,0:T(8,128)(2,1)} %get-tuple-element.75.refs_1_, ...), custom_call_target="tpu_custom_call" | custom-call | flops 2415919104 | bytes 8650752 | tf_op jit(solution)/shard_map/project/pallas_call | solution.py:135
  59.7 2.6 %collective-permute-done.14 = bf16[1,384,256]{2,1,0:T(8,128)(2,1)S(1)} collective-permute-done((bf16[1,384,256]{2,1,0:T(8,128)(2,1)}, bf16[1,384,256]{2,1,0:T(8,128)(2,1)S(1)}, u32[]{:S(2)}, u32[]{:S(2)}) %collective-permute-start.14) | collective-permute-done | bytes 196640 | tf_op jit(solution)/shard_map/ppermute | solution.py:28
  62.2 4.0 %collective-permute-done.15 = bf16[1,384,256]{2,1,0:T(8,128)(2,1)S(1)} collective-permute-done((bf16[1,384,256]{2,1,0:T(8,128)(2,1)}, bf16[1,384,256]{2,1,0:T(8,128)(2,1)S(1)}, u32[]{:S(2)}, u32[]{:S(2)}) %collective-permute-start.15) | collective-permute-done | bytes 196640 | tf_op jit(solution)/shard_map/ppermute | solution.py:28
  66.9 1.2 collective-permute-start.23
  68.2 1.6 collective-permute-start.24
  69.8 0.7 constant_dynamic-update-slice_fusion.3
  70.5 0.7 constant_dynamic-update-slice_fusion.2
  71.2 1.6 constant_dynamic-update-slice_fusion.1
  72.8 1.6 constant_dynamic-update-slice_fusion.refs_4_
  74.5 6.9 %collective-permute-done.23 = bf16[1,384,256]{2,1,0:T(8,128)(2,1)S(1)} collective-permute-done((bf16[1,384,256]{2,1,0:T(8,128)(2,1)}, bf16[1,384,256]{2,1,0:T(8,128)(2,1)S(1)}, u32[]{:S(2)}, u32[]{:S(2)}) %collective-permute-start.23) | collective-permute-done | bytes 196640 | tf_op jit(solution)/shard_map/ppermute | solution.py:28
  81.9 6.9 %project.8 = (bf16[1,384,128]{2,1,0:T(8,128)(2,1)}, bf16[1,384,128]{2,1,0:T(8,128)(2,1)}, bf16[1,384,128]{2,1,0:T(8,128)(2,1)}, bf16[1,384,128]{2,1,0:T(8,128)(2,1)}) custom-call(s32[3]{0:T(128)} %pad_add_fusion.place_ref, s32[1,1]{1,0:T(1,128)} %get-tuple-element.50.refs_0_, bf16[384,3072]{1,0:T(8,128)(2,1)} %get-tuple-element.75.refs_1_, ...), custom_call_target="tpu_custom_call" | custom-call | flops 1207959552 | bytes 5505024 | tf_op jit(solution)/shard_map/project/pallas_call | solution.py:135
  88.8 3.2 %collective-permute-start.11 = (bf16[1,384,128]{2,1,0:T(8,128)(2,1)}, bf16[1,384,128]{2,1,0:T(8,128)(2,1)S(1)}, u32[]{:S(2)}, u32[]{:S(2)}) collective-permute-start(bf16[1,384,128]{2,1,0:T(8,128)(2,1)} %get-tuple-element.65), channel_id=1, source_target_pairs={{0,8},{2,10},{4,12},{6,14},{8,0},{10,2},{12,4},{14,6},{16,24},{18,... | collective-permute-start | bytes 294920 | tf_op jit(solution)/shard_map/ppermute | solution.py:28
  92.7 0.7 constant_dynamic-update-slice_fusion.6
  93.4 0.7 constant_dynamic-update-slice_fusion.5
  94.0 0.7 constant_dynamic-update-slice_fusion.4.refs_4_
  94.8 1.5 collective-permute-start.26
  97.0 2.0 collective-permute-start.12
  99.0 11.4 %attend.3 = bf16[4,384,128]{2,1,0:T(8,128)(2,1)} custom-call(s32[3]{0:T(128)} %pad_add_fusion.place_ref, bf16[1,384,384]{2,1,0:T(8,128)(2,1)} %get-tuple-element.55.refs_0_, bf16[1,384,384]{2,1,0:T(8,128)(2,1)} %copy-done.9, bf16[1,384,384]{2,1,0:T(8,128)(2,1)} %copy-done.10, bf16[1,384,384]{2,1,0:T(8,128)(2,1)} %copy-done.11, ...), custom_call_target="tpu_custom_call" | custom-call | flops 2415919104 | bytes 3145728 | tf_op jit(solution)/shard_map/attend/pallas_call | solution.py:248
  110.4 11.0 %all-to-all-start = ((bf16[4,384,128]{2,1,0:T(8,128)(2,1)}), bf16[4,384,128]{2,1,0:T(8,128)(2,1)S(1)}, u32[]{:S(2)}, u32[]{:S(2)}) async-start(bf16[4,384,128]{2,1,0:T(8,128)(2,1)} %attend.3), calls=%async_computation | async-start | bytes 786432 | tf_op jit(solution)/shard_map/all_to_all | solution.py:379
  121.5 1.5 collective-permute-start.13
  122.9 11.7 %collective-permute-done.13.refs_3_ = bf16[1,384,128]{2,1,0:T(8,128)(2,1)S(1)} collective-permute-done((bf16[1,384,128]{2,1,0:T(8,128)(2,1)}, bf16[1,384,128]{2,1,0:T(8,128)(2,1)S(1)}, u32[]{:S(2)}, u32[]{:S(2)}) %collective-permute-start.13) | collective-permute-done | bytes 98336 | tf_op jit(solution)/shard_map/ppermute | solution.py:28
  135.2 0.8 copy-done.12
  136.0 11.2 %attend.4 = bf16[4,384,128]{2,1,0:T(8,128)(2,1)} custom-call(s32[3]{0:T(128)} %pad_add_fusion.place_ref, bf16[1,384,128]{2,1,0:T(8,128)(2,1)} %get-tuple-element.64.refs_0_, bf16[1,384,128]{2,1,0:T(8,128)(2,1)} %copy-done.15, bf16[1,384,128]{2,1,0:T(8,128)(2,1)} %collective-permute-done.12.refs_2_, bf16[1,384,128]{2,1,0:T(8,128)(2,1)} %copy-done.18, ...), custom_call_target="tpu_custom_call" | custom-call | flops 2415919104 | bytes 3145728 | tf_op jit(solution)/shard_map/attend/pallas_call | solution.py:248
  147.2 3.4 %all-to-all-start.1 = ((bf16[4,384,128]{2,1,0:T(8,128)(2,1)}), bf16[4,384,128]{2,1,0:T(8,128)(2,1)S(1)}, u32[]{:S(2)}, u32[]{:S(2)}) async-start(bf16[4,384,128]{2,1,0:T(8,128)(2,1)} %attend.4), calls=%async_computation.1 | async-start | bytes 786432 | tf_op jit(solution)/shard_map/all_to_all | solution.py:379
  150.7 6.8 %project.9 = (bf16[1,384,128]{2,1,0:T(8,128)(2,1)}, bf16[1,384,128]{2,1,0:T(8,128)(2,1)}, bf16[1,384,128]{2,1,0:T(8,128)(2,1)}, bf16[1,384,128]{2,1,0:T(8,128)(2,1)}) custom-call(s32[3]{0:T(128)} %pad_add_fusion.place_ref, s32[1,1]{1,0:T(1,128)} %get-tuple-element.50.refs_0_, bf16[384,3072]{1,0:T(8,128)(2,1)} %get-tuple-element.75.refs_1_, ...), custom_call_target="tpu_custom_call" | custom-call | flops 1207959552 | bytes 5505024 | tf_op jit(solution)/shard_map/project/pallas_call | solution.py:135
  157.5 2.8 %collective-permute-start.21 = (bf16[1,384,128]{2,1,0:T(8,128)(2,1)}, bf16[1,384,128]{2,1,0:T(8,128)(2,1)S(1)}, u32[]{:S(2)}, u32[]{:S(2)}) collective-permute-start(bf16[1,384,128]{2,1,0:T(8,128)(2,1)} %get-tuple-element.78), channel_id=1, source_target_pairs={{0,16},{2,18},{4,20},{6,22},{8,24},{10,26},{12,28},{14,30},{16,0},... | collective-permute-start | bytes 294920 | tf_op jit(solution)/shard_map/ppermute | solution.py:28
  160.3 2.3 %collective-permute-done.20.refs_1_ = bf16[1,384,128]{2,1,0:T(8,128)(2,1)S(1)} collective-permute-done((bf16[1,384,128]{2,1,0:T(8,128)(2,1)}, bf16[1,384,128]{2,1,0:T(8,128)(2,1)S(1)}, u32[]{:S(2)}, u32[]{:S(2)}) %collective-permute-start.20) | collective-permute-done | bytes 98336 | tf_op jit(solution)/shard_map/ppermute | solution.py:28
  162.6 1.0 collective-permute-start.22
  164.2 4.8 %collective-permute-done.22.refs_3_ = bf16[1,384,128]{2,1,0:T(8,128)(2,1)S(1)} collective-permute-done((bf16[1,384,128]{2,1,0:T(8,128)(2,1)}, bf16[1,384,128]{2,1,0:T(8,128)(2,1)S(1)}, u32[]{:S(2)}, u32[]{:S(2)}) %collective-permute-start.22) | collective-permute-done | bytes 98336 | tf_op jit(solution)/shard_map/ppermute | solution.py:28
  169.7 11.5 %attend.5 = bf16[4,384,128]{2,1,0:T(8,128)(2,1)} custom-call(s32[3]{0:T(128)} %pad_add_fusion.place_ref, bf16[1,384,128]{2,1,0:T(8,128)(2,1)} %get-tuple-element.76.refs_0_, bf16[1,384,128]{2,1,0:T(8,128)(2,1)} %copy-done.16, bf16[1,384,128]{2,1,0:T(8,128)(2,1)} %copy-done.17, bf16[1,384,128]{2,1,0:T(8,128)(2,1)} %copy-done.19, ...), custom_call_target="tpu_custom_call" | custom-call | flops 2415919104 | bytes 3145728 | tf_op jit(solution)/shard_map/attend/pallas_call | solution.py:248
  181.2 5.4 %all-to-all-start.2 = ((bf16[4,384,128]{2,1,0:T(8,128)(2,1)}), bf16[4,384,128]{2,1,0:T(8,128)(2,1)S(1)}, u32[]{:S(2)}, u32[]{:S(2)}) async-start(bf16[4,384,128]{2,1,0:T(8,128)(2,1)} %attend.5), calls=%async_computation.2 | async-start | bytes 786432 | tf_op jit(solution)/shard_map/all_to_all | solution.py:379
  187.1 1.5 collective-permute-start.19
  188.6 5.4 %all-to-all-done.2.refs_1_ = bf16[4,384,128]{2,1,0:T(8,128)(2,1)S(1)} async-done(((bf16[4,384,128]{2,1,0:T(8,128)(2,1)}), bf16[4,384,128]{2,1,0:T(8,128)(2,1)S(1)}, u32[]{:S(2)}, u32[]{:S(2)}) %all-to-all-start.2) | async-done | bytes 393248 | tf_op jit(solution)/shard_map/all_to_all | solution.py:379
  194.5 4.2 %collective-permute-done.6.refs_2_ = bf16[4,384,128]{2,1,0:T(8,128)(2,1)} collective-permute-done((bf16[4,384,128]{2,1,0:T(8,128)(2,1)S(1)}, bf16[4,384,128]{2,1,0:T(8,128)(2,1)}, u32[]{:S(2)}, u32[]{:S(2)}) %collective-permute-start.6) | collective-permute-done | bytes 393248 | tf_op jit(solution)/shard_map/ppermute | solution.py:28
  198.7 3.7 %copy-done = bf16[1536,3072]{1,0:T(8,128)(2,1)S(1)} copy-done((bf16[1536,3072]{1,0:T(8,128)(2,1)S(1)}, bf16[1536,3072]{1,0:T(8,128)(2,1)}, u32[]{:S(2)}) %copy-start) | copy-done | bytes 9437208
  202.4 3.6 %finish.3.refs_0_ = f32[384,1536]{1,0:T(8,128)S(1)} custom-call(s32[3]{0:T(128)S(1)} %copy-done.2, bf16[4,384,128]{2,1,0:T(8,128)(2,1)S(1)} %all-to-all-done.refs_0_, bf16[1536,3072]{1,0:T(8,128)(2,1)S(1)} %copy-done, bf16[4,384,128]{2,1,0:T(8,128)(2,1)} %collective-permute-done.6.refs_2_, bf16[1536,768]{1,0:T(8,128)(2,1)S(1)} %collective-permute-done.7.refs_3_.refs_4_, ...), custom_call_target="tpu_custom_call" | custom-call | flops 1207959552 | bytes 7864320 | tf_op jit(solution)/shard_map/finish/pallas_call | solution.py:331
  206.0 0.9 collective-permute-done.19.refs_3_
  206.9 3.7 %finish.4.refs_0_ = f32[384,1536]{1,0:T(8,128)S(1)} custom-call(s32[3]{0:T(128)S(1)} %copy-done.2, f32[384,1536]{1,0:T(8,128)S(1)} %finish.3.refs_0_, bf16[4,384,128]{2,1,0:T(8,128)(2,1)S(1)} %all-to-all-done.1.refs_1_, bf16[1536,3072]{1,0:T(8,128)(2,1)S(1)} %copy-done, bf16[4,384,128]{2,1,0:T(8,128)(2,1)} %collective-permute-done.19.refs_3_, ...), custom_call_target="tpu_custom_call" | custom-call | flops 1207959552 | bytes 7864320 | tf_op jit(solution)/shard_map/finish/pallas_call | solution.py:331
  211.0 5.0 %finish.5 = bf16[384,1536]{1,0:T(8,128)(2,1)} custom-call(s32[3]{0:T(128)S(1)} %copy-done.2, f32[384,1536]{1,0:T(8,128)S(1)} %finish.4.refs_0_, bf16[4,384,128]{2,1,0:T(8,128)(2,1)S(1)} %all-to-all-done.2.refs_1_, bf16[1536,3072]{1,0:T(8,128)(2,1)S(1)} %copy-done, bf16[4,384,128]{2,1,0:T(8,128)(2,1)S(1)} %collective-permute-done.28.refs_3_, ...), custom_call_target="tpu_custom_call" | custom-call | flops 1207959552 | bytes 7864320 | tf_op jit(solution)/shard_map/finish/pallas_call | solution.py:331
  (82 shorter events, 9.1 us)
Async XLA Ops:
  13.9 4.9 %copy-start.14 = (bf16[1,384,384]{2,1,0:T(8,128)(2,1)S(1)}, bf16[1,384,384]{2,1,0:T(8,128)(2,1)}, u32[]{:S(2)}) copy-start(bf16[1,384,384]{2,1,0:T(8,128)(2,1)} %get-tuple-element.47) | copy-start | bytes 884740
  14.0 7.9 %copy-start.13 = (bf16[1,384,384]{2,1,0:T(8,128)(2,1)S(1)}, bf16[1,384,384]{2,1,0:T(8,128)(2,1)}, u32[]{:S(2)}) copy-start(bf16[1,384,384]{2,1,0:T(8,128)(2,1)} %get-tuple-element.49) | copy-start | bytes 884740
  17.3 79.5 %collective-permute-start.7 = (bf16[1536,768]{1,0:T(8,128)(2,1)}, bf16[1536,768]{1,0:T(8,128)(2,1)S(1)}, u32[]{:S(2)}, u32[]{:S(2)}) collective-permute-start(bf16[1536,768]{1,0:T(8,128)(2,1)} %constant_dynamic-slice_fusion), channel_id=1, source_target_pairs={{0,1},{1,0},{2,3},{3,2},{4,5},{5,4},{6,7},{7,6},{8,9},{9,8},{10,11... | collective-permute-start | bytes 7077896 | tf_op jit(solution)/shard_map/ppermute | solution.py:28
  18.8 11.7 %collective-permute-start = (bf16[1,384,384]{2,1,0:T(8,128)(2,1)S(1)}, bf16[1,384,384]{2,1,0:T(8,128)(2,1)S(1)}, u32[]{:S(2)}, u32[]{:S(2)}) collective-permute-start(bf16[1,384,384]{2,1,0:T(8,128)(2,1)S(1)} %copy-done.14), channel_id=1, source_target_pairs={{0,8},{2,10},{4,12},{6,14},{8,0},{10,2},{12,4},{14,6},{16,24},{18,... | collective-permute-start | bytes 884744 | tf_op jit(solution)/shard_map/ppermute | solution.py:28
  19.3 23.0 %collective-permute-start.1 = (bf16[1,384,384]{2,1,0:T(8,128)(2,1)}, bf16[1,384,384]{2,1,0:T(8,128)(2,1)S(1)}, u32[]{:S(2)}, u32[]{:S(2)}) collective-permute-start(bf16[1,384,384]{2,1,0:T(8,128)(2,1)} %get-tuple-element.48), channel_id=1, source_target_pairs={{0,16},{2,18},{4,20},{6,22},{8,24},{10,26},{12,28},{14,30},{16,0},... | collective-permute-start | bytes 884744 | tf_op jit(solution)/shard_map/ppermute | solution.py:28
  21.9 25.8 %collective-permute-start.2 = (bf16[1,384,384]{2,1,0:T(8,128)(2,1)S(1)}, bf16[1,384,384]{2,1,0:T(8,128)(2,1)S(1)}, u32[]{:S(2)}, u32[]{:S(2)}) collective-permute-start(bf16[1,384,384]{2,1,0:T(8,128)(2,1)S(1)} %copy-done.13), channel_id=1, source_target_pairs={{0,24},{2,26},{4,28},{6,30},{8,16},{10,18},{12,20},{14,22},{16,8},... | collective-permute-start | bytes 884744 | tf_op jit(solution)/shard_map/ppermute | solution.py:28
  30.6 17.2 %copy-start.9 = (bf16[1,384,384]{2,1,0:T(8,128)(2,1)}, bf16[1,384,384]{2,1,0:T(8,128)(2,1)S(1)}, u32[]{:S(2)}) copy-start(bf16[1,384,384]{2,1,0:T(8,128)(2,1)S(1)} %collective-permute-done.refs_1_) | copy-start | bytes 884740
  30.6 17.1 %copy-start.8 = (bf16[1,384,384]{2,1,0:T(8,128)(2,1)S(1)}, bf16[1,384,384]{2,1,0:T(8,128)(2,1)}, u32[]{:S(2)}) copy-start(bf16[1,384,384]{2,1,0:T(8,128)(2,1)} %get-tuple-element.55.refs_0_) | copy-start | bytes 884740
  39.5 11.1 %collective-permute-start.9 = (bf16[1,384,256]{2,1,0:T(8,128)(2,1)}, bf16[1,384,256]{2,1,0:T(8,128)(2,1)S(1)}, u32[]{:S(2)}, u32[]{:S(2)}) collective-permute-start(bf16[1,384,256]{2,1,0:T(8,128)(2,1)} %get-tuple-element.60), channel_id=1, source_target_pairs={{0,8},{2,10},{4,12},{6,14},{8,0},{10,2},{12,4},{14,6},{16,24},{18,... | collective-permute-start | bytes 589832 | tf_op jit(solution)/shard_map/ppermute | solution.py:28
  42.3 6.1 %copy-start.10 = (bf16[1,384,384]{2,1,0:T(8,128)(2,1)}, bf16[1,384,384]{2,1,0:T(8,128)(2,1)S(1)}, u32[]{:S(2)}) copy-start(bf16[1,384,384]{2,1,0:T(8,128)(2,1)S(1)} %collective-permute-done.1.refs_2_) | copy-start | bytes 884740
  48.4 13.8 %collective-permute-start.14 = (bf16[1,384,256]{2,1,0:T(8,128)(2,1)}, bf16[1,384,256]{2,1,0:T(8,128)(2,1)S(1)}, u32[]{:S(2)}, u32[]{:S(2)}) collective-permute-start(bf16[1,384,256]{2,1,0:T(8,128)(2,1)} %get-tuple-element.68), channel_id=1, source_target_pairs={{0,16},{2,18},{4,20},{6,22},{8,24},{10,26},{12,28},{14,30},{16,0},... | collective-permute-start | bytes 589832 | tf_op jit(solution)/shard_map/ppermute | solution.py:28
  48.4 17.9 %collective-permute-start.15 = (bf16[1,384,256]{2,1,0:T(8,128)(2,1)}, bf16[1,384,256]{2,1,0:T(8,128)(2,1)S(1)}, u32[]{:S(2)}, u32[]{:S(2)}) collective-permute-start(bf16[1,384,256]{2,1,0:T(8,128)(2,1)} %get-tuple-element.69), channel_id=1, source_target_pairs={{0,24},{2,26},{4,28},{6,30},{8,16},{10,18},{12,20},{14,22},{16,8},... | collective-permute-start | bytes 589832 | tf_op jit(solution)/shard_map/ppermute | solution.py:28
  50.1 24.3 %copy-start.3 = (bf16[4,384,256]{2,1,0:T(8,128)(2,1)}, bf16[4,384,256]{2,1,0:T(8,128)(2,1)S(1)}, u32[]{:S(2)}) copy-start(bf16[4,384,256]{2,1,0:T(8,128)(2,1)S(1)} %pad_maximum_fusion.refs_4_) | copy-start | bytes 2359300
  50.1 19.7 %copy-start.5 = (bf16[1,384,256]{2,1,0:T(8,128)(2,1)S(1)}, bf16[1,384,256]{2,1,0:T(8,128)(2,1)}, u32[]{:S(2)}) copy-start(bf16[1,384,256]{2,1,0:T(8,128)(2,1)} %get-tuple-element.71) | copy-start | bytes 589828
  50.1 41.9 %collective-permute-start.4 = (bf16[4,384,256]{2,1,0:T(8,128)(2,1)S(1)}, bf16[4,384,256]{2,1,0:T(8,128)(2,1)}, u32[]{:S(2)}, u32[]{:S(2)}) collective-permute-start(bf16[4,384,256]{2,1,0:T(8,128)(2,1)S(1)} %pad_maximum_fusion.refs_4_), channel_id=1, source_target_pairs={{0,4},{2,6},{4,0},{6,2},{8,12},{10,14},{12,8},{14,10},{16,20},{18,... | collective-permute-start | bytes 2359304 | tf_op jit(solution)/shard_map/ppermute | solution.py:28
  62.2 4.0 %copy-start.6 = (bf16[1,384,256]{2,1,0:T(8,128)(2,1)}, bf16[1,384,256]{2,1,0:T(8,128)(2,1)S(1)}, u32[]{:S(2)}) copy-start(bf16[1,384,256]{2,1,0:T(8,128)(2,1)S(1)} %collective-permute-done.14) | copy-start | bytes 589828
  66.3 8.1 %collective-permute-start.10 = (bf16[1,384,256]{2,1,0:T(8,128)(2,1)}, bf16[1,384,256]{2,1,0:T(8,128)(2,1)S(1)}, u32[]{:S(2)}, u32[]{:S(2)}) collective-permute-start(bf16[1,384,256]{2,1,0:T(8,128)(2,1)} %get-tuple-element.62), channel_id=1, source_target_pairs={{0,8},{2,10},{4,12},{6,14},{8,0},{10,2},{12,4},{14,6},{16,24},{18,... | collective-permute-start | bytes 589832 | tf_op jit(solution)/shard_map/ppermute | solution.py:28
  66.9 14.5 %collective-permute-start.23 = (bf16[1,384,256]{2,1,0:T(8,128)(2,1)}, bf16[1,384,256]{2,1,0:T(8,128)(2,1)S(1)}, u32[]{:S(2)}, u32[]{:S(2)}) collective-permute-start(bf16[1,384,256]{2,1,0:T(8,128)(2,1)} %get-tuple-element.80), channel_id=1, source_target_pairs={{0,16},{2,18},{4,20},{6,22},{8,24},{10,26},{12,28},{14,30},{16,0},... | collective-permute-start | bytes 589832 | tf_op jit(solution)/shard_map/ppermute | solution.py:28
  68.2 20.6 %collective-permute-start.24 = (bf16[1,384,256]{2,1,0:T(8,128)(2,1)}, bf16[1,384,256]{2,1,0:T(8,128)(2,1)S(1)}, u32[]{:S(2)}, u32[]{:S(2)}) collective-permute-start(bf16[1,384,256]{2,1,0:T(8,128)(2,1)} %get-tuple-element.81), channel_id=1, source_target_pairs={{0,24},{2,26},{4,28},{6,30},{8,16},{10,18},{12,20},{14,22},{16,8},... | collective-permute-start | bytes 589832 | tf_op jit(solution)/shard_map/ppermute | solution.py:28
  74.4 17.6 %copy-start.4 = (bf16[1,384,256]{2,1,0:T(8,128)(2,1)S(1)}, bf16[1,384,256]{2,1,0:T(8,128)(2,1)}, u32[]{:S(2)}) copy-start(bf16[1,384,256]{2,1,0:T(8,128)(2,1)} %get-tuple-element.82) | copy-start | bytes 589828
  74.4 21.9 %collective-permute-start.3 = (bf16[4,384,256]{2,1,0:T(8,128)(2,1)S(1)}, bf16[4,384,256]{2,1,0:T(8,128)(2,1)}, u32[]{:S(2)}, u32[]{:S(2)}) collective-permute-start(bf16[4,384,256]{2,1,0:T(8,128)(2,1)S(1)} %pad_maximum_fusion.refs_4_), channel_id=1, source_target_pairs={{0,2},{2,0},{4,6},{6,4},{8,10},{10,8},{12,14},{14,12},{16,18},{18,... | collective-permute-start | bytes 2359304 | tf_op jit(solution)/shard_map/ppermute | solution.py:28
  81.4 15.1 %collective-permute-start.17 = (bf16[4,384,256]{2,1,0:T(8,128)(2,1)}, bf16[4,384,256]{2,1,0:T(8,128)(2,1)}, u32[]{:S(2)}, u32[]{:S(2)}) collective-permute-start(bf16[4,384,256]{2,1,0:T(8,128)(2,1)} %constant_dynamic-update-slice_fusion.refs_4_), channel_id=1, source_target_pairs={{0,4},{2,6},{4,0},{6,2},{8,12},{10,14},{12,8},{14,10},{16,20},{18,... | collective-permute-start | bytes 2359304 | tf_op jit(solution)/shard_map/ppermute | solution.py:28
  88.8 6.0 %collective-permute-start.11 = (bf16[1,384,128]{2,1,0:T(8,128)(2,1)}, bf16[1,384,128]{2,1,0:T(8,128)(2,1)S(1)}, u32[]{:S(2)}, u32[]{:S(2)}) collective-permute-start(bf16[1,384,128]{2,1,0:T(8,128)(2,1)} %get-tuple-element.65), channel_id=1, source_target_pairs={{0,8},{2,10},{4,12},{6,14},{8,0},{10,2},{12,4},{14,6},{16,24},{18,... | collective-permute-start | bytes 294920 | tf_op jit(solution)/shard_map/ppermute | solution.py:28
  92.0 5.0 %collective-permute-start.5 = (bf16[4,384,256]{2,1,0:T(8,128)(2,1)}, bf16[4,384,256]{2,1,0:T(8,128)(2,1)}, u32[]{:S(2)}, u32[]{:S(2)}) collective-permute-start(bf16[4,384,256]{2,1,0:T(8,128)(2,1)} %collective-permute-done.4.refs_6_), channel_id=1, source_target_pairs={{0,2},{2,0},{4,6},{6,4},{8,10},{10,8},{12,14},{14,12},{16,18},{18,... | collective-permute-start | bytes 2359304 | tf_op jit(solution)/shard_map/ppermute | solution.py:28
  94.8 1.5 copy-start.15
  94.8 39.8 %collective-permute-start.26 = (bf16[4,384,256]{2,1,0:T(8,128)(2,1)}, bf16[4,384,256]{2,1,0:T(8,128)(2,1)}, u32[]{:S(2)}, u32[]{:S(2)}) collective-permute-start(bf16[4,384,256]{2,1,0:T(8,128)(2,1)} %constant_dynamic-update-slice_fusion.4.refs_4_), channel_id=1, source_target_pairs={{0,4},{2,6},{4,0},{6,2},{8,12},{10,14},{12,8},{14,10},{16,20},{18,... | collective-permute-start | bytes 2359304 | tf_op jit(solution)/shard_map/ppermute | solution.py:28
  96.3 38.8 %collective-permute-start.16 = (bf16[4,384,256]{2,1,0:T(8,128)(2,1)}, bf16[4,384,256]{2,1,0:T(8,128)(2,1)S(1)}, u32[]{:S(2)}, u32[]{:S(2)}) collective-permute-start(bf16[4,384,256]{2,1,0:T(8,128)(2,1)} %constant_dynamic-update-slice_fusion.refs_4_), channel_id=1, source_target_pairs={{0,2},{2,0},{4,6},{6,4},{8,10},{10,8},{12,14},{14,12},{16,18},{18,... | collective-permute-start | bytes 2359304 | tf_op jit(solution)/shard_map/ppermute | solution.py:28
  96.5 38.6 %collective-permute-start.18 = (bf16[4,384,256]{2,1,0:T(8,128)(2,1)}, bf16[4,384,256]{2,1,0:T(8,128)(2,1)}, u32[]{:S(2)}, u32[]{:S(2)}) collective-permute-start(bf16[4,384,256]{2,1,0:T(8,128)(2,1)} %collective-permute-done.17.refs_6_), channel_id=1, source_target_pairs={{0,2},{2,0},{4,6},{6,4},{8,10},{10,8},{12,14},{14,12},{16,18},{18,... | collective-permute-start | bytes 2359304 | tf_op jit(solution)/shard_map/ppermute | solution.py:28
  96.8 101.9 %collective-permute-start.8 = (bf16[1536,768]{1,0:T(8,128)(2,1)S(1)}, bf16[1536,768]{1,0:T(8,128)(2,1)}, u32[]{:S(2)}, u32[]{:S(2)}) collective-permute-start(bf16[1536,768]{1,0:T(8,128)(2,1)S(1)} %collective-permute-done.7.refs_3_.refs_4_), channel_id=1, source_target_pairs={{0,2},{2,0},{4,6},{6,4},{8,10},{10,8},{12,14},{14,12},{16,18},{18,... | collective-permute-start | bytes 7077896 | tf_op jit(solution)/shard_map/ppermute | solution.py:28
  97.0 24.4 %collective-permute-start.12 = (bf16[1,384,128]{2,1,0:T(8,128)(2,1)}, bf16[1,384,128]{2,1,0:T(8,128)(2,1)}, u32[]{:S(2)}, u32[]{:S(2)}) collective-permute-start(bf16[1,384,128]{2,1,0:T(8,128)(2,1)} %get-tuple-element.66), channel_id=1, source_target_pairs={{0,16},{2,18},{4,20},{6,22},{8,24},{10,26},{12,28},{14,30},{16,0},... | collective-permute-start | bytes 294920 | tf_op jit(solution)/shard_map/ppermute | solution.py:28
  110.4 36.8 %all-to-all-start = ((bf16[4,384,128]{2,1,0:T(8,128)(2,1)}), bf16[4,384,128]{2,1,0:T(8,128)(2,1)S(1)}, u32[]{:S(2)}, u32[]{:S(2)}) async-start(bf16[4,384,128]{2,1,0:T(8,128)(2,1)} %attend.3), calls=%async_computation | async-start | bytes 786432 | tf_op jit(solution)/shard_map/all_to_all | solution.py:379
  121.5 13.2 %collective-permute-start.13 = (bf16[1,384,128]{2,1,0:T(8,128)(2,1)}, bf16[1,384,128]{2,1,0:T(8,128)(2,1)S(1)}, u32[]{:S(2)}, u32[]{:S(2)}) collective-permute-start(bf16[1,384,128]{2,1,0:T(8,128)(2,1)} %get-tuple-element.67), channel_id=1, source_target_pairs={{0,24},{2,26},{4,28},{6,30},{8,16},{10,18},{12,20},{14,22},{16,8},... | collective-permute-start | bytes 294920 | tf_op jit(solution)/shard_map/ppermute | solution.py:28
  134.6 34.5 %collective-permute-start.25 = (bf16[4,384,256]{2,1,0:T(8,128)(2,1)}, bf16[4,384,256]{2,1,0:T(8,128)(2,1)}, u32[]{:S(2)}, u32[]{:S(2)}) collective-permute-start(bf16[4,384,256]{2,1,0:T(8,128)(2,1)} %constant_dynamic-update-slice_fusion.4.refs_4_), channel_id=1, source_target_pairs={{0,2},{2,0},{4,6},{6,4},{8,10},{10,8},{12,14},{14,12},{16,18},{18,... | collective-permute-start | bytes 2359304 | tf_op jit(solution)/shard_map/ppermute | solution.py:28
  134.6 34.4 %collective-permute-start.27 = (bf16[4,384,256]{2,1,0:T(8,128)(2,1)}, bf16[4,384,256]{2,1,0:T(8,128)(2,1)}, u32[]{:S(2)}, u32[]{:S(2)}) collective-permute-start(bf16[4,384,256]{2,1,0:T(8,128)(2,1)} %collective-permute-done.26.refs_6_), channel_id=1, source_target_pairs={{0,2},{2,0},{4,6},{6,4},{8,10},{10,8},{12,14},{14,12},{16,18},{18,... | collective-permute-start | bytes 2359304 | tf_op jit(solution)/shard_map/ppermute | solution.py:28
  135.1 0.9 copy-start.12
  147.2 34.0 %all-to-all-start.1 = ((bf16[4,384,128]{2,1,0:T(8,128)(2,1)}), bf16[4,384,128]{2,1,0:T(8,128)(2,1)S(1)}, u32[]{:S(2)}, u32[]{:S(2)}) async-start(bf16[4,384,128]{2,1,0:T(8,128)(2,1)} %attend.4), calls=%async_computation.1 | async-start | bytes 786432 | tf_op jit(solution)/shard_map/all_to_all | solution.py:379
  157.5 5.1 %collective-permute-start.20 = (bf16[1,384,128]{2,1,0:T(8,128)(2,1)}, bf16[1,384,128]{2,1,0:T(8,128)(2,1)S(1)}, u32[]{:S(2)}, u32[]{:S(2)}) collective-permute-start(bf16[1,384,128]{2,1,0:T(8,128)(2,1)} %get-tuple-element.77), channel_id=1, source_target_pairs={{0,8},{2,10},{4,12},{6,14},{8,0},{10,2},{12,4},{14,6},{16,24},{18,... | collective-permute-start | bytes 294920 | tf_op jit(solution)/shard_map/ppermute | solution.py:28
  157.5 6.7 %collective-permute-start.21 = (bf16[1,384,128]{2,1,0:T(8,128)(2,1)}, bf16[1,384,128]{2,1,0:T(8,128)(2,1)S(1)}, u32[]{:S(2)}, u32[]{:S(2)}) collective-permute-start(bf16[1,384,128]{2,1,0:T(8,128)(2,1)} %get-tuple-element.78), channel_id=1, source_target_pairs={{0,16},{2,18},{4,20},{6,22},{8,24},{10,26},{12,28},{14,30},{16,0},... | collective-permute-start | bytes 294920 | tf_op jit(solution)/shard_map/ppermute | solution.py:28
  162.6 6.5 %copy-start.16 = (bf16[1,384,128]{2,1,0:T(8,128)(2,1)}, bf16[1,384,128]{2,1,0:T(8,128)(2,1)S(1)}, u32[]{:S(2)}) copy-start(bf16[1,384,128]{2,1,0:T(8,128)(2,1)S(1)} %collective-permute-done.20.refs_1_) | copy-start | bytes 294916
  162.6 6.4 %collective-permute-start.22 = (bf16[1,384,128]{2,1,0:T(8,128)(2,1)}, bf16[1,384,128]{2,1,0:T(8,128)(2,1)S(1)}, u32[]{:S(2)}, u32[]{:S(2)}) collective-permute-start(bf16[1,384,128]{2,1,0:T(8,128)(2,1)} %get-tuple-element.79), channel_id=1, source_target_pairs={{0,24},{2,26},{4,28},{6,30},{8,16},{10,18},{12,20},{14,22},{16,8},... | collective-permute-start | bytes 294920 | tf_op jit(solution)/shard_map/ppermute | solution.py:28
  164.2 4.9 %copy-start.17 = (bf16[1,384,128]{2,1,0:T(8,128)(2,1)}, bf16[1,384,128]{2,1,0:T(8,128)(2,1)S(1)}, u32[]{:S(2)}) copy-start(bf16[1,384,128]{2,1,0:T(8,128)(2,1)S(1)} %collective-permute-done.21.refs_2_) | copy-start | bytes 294916
  169.7 29.0 %copy-start.2 = (s32[3]{0:T(128)S(1)}, s32[3]{0:T(128)}, u32[]{:S(2)}) copy-start(s32[3]{0:T(128)} %pad_add_fusion.place_ref) | copy-start | bytes 40
  181.2 12.8 %all-to-all-start.2 = ((bf16[4,384,128]{2,1,0:T(8,128)(2,1)}), bf16[4,384,128]{2,1,0:T(8,128)(2,1)S(1)}, u32[]{:S(2)}, u32[]{:S(2)}) async-start(bf16[4,384,128]{2,1,0:T(8,128)(2,1)} %attend.5), calls=%async_computation.2 | async-start | bytes 786432 | tf_op jit(solution)/shard_map/all_to_all | solution.py:379
  186.5 12.2 %collective-permute-start.6 = (bf16[4,384,128]{2,1,0:T(8,128)(2,1)S(1)}, bf16[4,384,128]{2,1,0:T(8,128)(2,1)}, u32[]{:S(2)}, u32[]{:S(2)}) collective-permute-start(bf16[4,384,128]{2,1,0:T(8,128)(2,1)S(1)} %all-to-all-done.refs_0_), channel_id=1, source_target_pairs={{0,1},{1,0},{2,3},{3,2},{4,5},{5,4},{6,7},{7,6},{8,9},{9,8},{10,11... | collective-permute-start | bytes 1179656 | tf_op jit(solution)/shard_map/ppermute | solution.py:28
  187.1 19.8 %collective-permute-start.19 = (bf16[4,384,128]{2,1,0:T(8,128)(2,1)S(1)}, bf16[4,384,128]{2,1,0:T(8,128)(2,1)}, u32[]{:S(2)}, u32[]{:S(2)}) collective-permute-start(bf16[4,384,128]{2,1,0:T(8,128)(2,1)S(1)} %all-to-all-done.1.refs_1_), channel_id=1, source_target_pairs={{0,1},{1,0},{2,3},{3,2},{4,5},{5,4},{6,7},{7,6},{8,9},{9,8},{10,11... | collective-permute-start | bytes 1179656 | tf_op jit(solution)/shard_map/ppermute | solution.py:28
  194.0 17.1 %collective-permute-start.28 = (bf16[4,384,128]{2,1,0:T(8,128)(2,1)S(1)}, bf16[4,384,128]{2,1,0:T(8,128)(2,1)S(1)}, u32[]{:S(2)}, u32[]{:S(2)}) collective-permute-start(bf16[4,384,128]{2,1,0:T(8,128)(2,1)S(1)} %all-to-all-done.2.refs_1_), channel_id=1, source_target_pairs={{0,1},{1,0},{2,3},{3,2},{4,5},{5,4},{6,7},{7,6},{8,9},{9,8},{10,11... | collective-permute-start | bytes 1179656 | tf_op jit(solution)/shard_map/ppermute | solution.py:28
  198.7 3.7 %copy-start = (bf16[1536,3072]{1,0:T(8,128)(2,1)S(1)}, bf16[1536,3072]{1,0:T(8,128)(2,1)}, u32[]{:S(2)}) copy-start(bf16[1536,3072]{1,0:T(8,128)(2,1)} %refs_2_.5) | copy-start | bytes 28311556
  206.0 5.0 %copy-start.1 = (bf16[384,384]{1,0:T(8,128)(2,1)S(1)}, bf16[384,384]{1,0:T(8,128)(2,1)}, u32[]{:S(2)}) copy-start(bf16[384,384]{1,0:T(8,128)(2,1)} %get-tuple-element.86.refs_6_) | copy-start | bytes 884740
  (4 other events, 2.6 us)
where the time goes:
time: 216 us
  Pallas kernels  91.4 us (42%)
  waiting for transfers between devices  57.9 us (27%)
  starting transfers between devices  48.6 us (22%)
  local copies, waits for them, and re-layouts  17.3 us (8%)
    ppermute x29, waiting for transfers between devices, flip(): return lax.ppermute(values, axis, [(i, i ^ mask) for i in range(size)])  52.5 us
    pallas_call x5, Pallas kernels, project(): pl.pallas_call(functools.partial(project_body, kinds=kinds, chunk=chunk,...  45 us
    pallas_call x3, Pallas kernels, attend(): pl.pallas_call(functools.partial(attend_body, groups=groups, low_lane=low...  34 us
    ppermute x29, starting transfers between devices, flip(): return lax.ppermute(values, axis, [(i, i ^ mask) for i in range(size)])  28.7 us
    all_to_all x3, starting transfers between devices, send_back(): lax.all_to_all(blocks, 'seq', split_axis=0, concat_axis=0, axis_index_gro...  19.8 us
    pallas_call x3, Pallas kernels, finish(): pl.pallas_call(functools.partial(finish_body, others=len(other_attended),...  12.4 us
    unnamed x46, local copies, waits for them, and re-layouts  11.5 us
    all_to_all x3, waiting for transfers between devices, send_back(): lax.all_to_all(blocks, 'seq', split_axis=0, concat_axis=0, axis_index_gro...  5.39 us
  transfers between devices with their start and end apart: 32, of which 14 were waited for; matrix products, arithmetic and copies ran while one was open for 3% of the time, Pallas kernels for 34%

commit v1 on v0

--- a/solution.py
+++ b/solution.py
@@ -26,6 +26,16 @@
 def flip(values, axis, mask):
     size = lax.axis_size(axis)
     return lax.ppermute(values, axis, [(i, i ^ mask) for i in range(size)])
+
+
+def place_half(width):
+    head_shards = lax.axis_size("head")
+    out_width = width // head_shards
+    return out_width // 2 if splits(out_width, head_shards) else out_width
+
+
+def splits(out_width, head_shards):
+    return head_shards == 2 and out_width % 256 == 0
 
 
 def chain(values, *earlier):
@@ -57,29 +67,47 @@
         normed_ref[low : low + rows, :] = layer_norm(part, gain).astype(bf16)
 
 
-def project_body(place_ref, *refs, kinds, chunk, groups, first):
+def project_body(place_ref, *refs, kinds, chunks, groups, first, streams):
     refs = list(refs)
     result_ref = refs.pop()
+    weight_refs, gain_ref = refs[:streams], refs[streams]
+    refs = refs[streams + 1 :]
+    outs = refs[3 + first : 3 + first + groups * len(chunks)]
+    plane = place_ref[0]
     if first:
-        (survive_ref, tokens_ref, norm_gain_ref, weight_ref, gain_ref), outs = refs[:5], refs[5:]
-        normed_ref, chosen_ref, back_ref, count_ref = outs[groups:]
-
-        @pl.when(pl.program_id(0) == 0)
+        survive_ref, tokens_ref, norm_gain_ref, source_ref = refs[:4]
+        normed_ref, chosen_ref, back_ref, count_ref, slice_ref, copy_sem = refs[4 + len(outs) :]
+        half = slice_ref.shape[1]
+        start = pl.multiple_of(place_ref[3] * half, half)
+        copy = pltpu.make_async_copy(source_ref.at[:, pl.ds(start, half)], slice_ref, copy_sem)
+
+        @pl.when(pl.program_id(1) == 0)
         def _():
+            copy.start()
             prepare(
                 survive_ref, tokens_ref, norm_gain_ref, normed_ref, chosen_ref, back_ref, count_ref
             )
 
     else:
-        (count_ref, normed_ref, chosen_ref, weight_ref, gain_ref), outs = refs[:5], refs[5:]
-    rows = normed_ref.shape[0]
+        count_ref, normed_ref, chosen_ref = refs[:3]
+    rows, width = normed_ref.shape
     size = gain_ref.shape[2]
-    plane = place_ref[0]
-    for step, kind in enumerate(kinds):
-
-        @pl.when(pl.program_id(0) == step)
+    depth = width // streams
+    for step in range(len(chunks) * len(kinds)):
+        chunk, kind = chunks[step // len(kinds)], kinds[step % len(kinds)]
+        low = step % len(kinds) * size
+        targets = outs[step // len(kinds) * groups :][:groups]
+
+        @pl.when(pl.program_id(0) * len(kinds) + pl.program_id(1) == step)
         def _():
-            result = jnp.dot(normed_ref[...], weight_ref[0], preferred_element_type=f32)
+            result = sum(
+                jnp.dot(
+                    normed_ref[:, i * depth : (i + 1) * depth],
+                    weight_ref[0],
+                    preferred_element_type=f32,
+                )
+                for i, weight_ref in enumerate(weight_refs)
+            )
             for g in range(groups):
                 part = result[:, g * size : (g + 1) * size]
                 if kind != 2:
@@ -95,66 +123,82 @@
             result_ref[...] = packed.astype(bf16)
             for k in range(groups):
                 start = pl.multiple_of(lax.bitwise_xor(plane, k) * size, size)
-                outs[k][0, :, step * size : (step + 1) * size] = result_ref[:, pl.ds(start, size)]
-
-
-def project(place, prepared, weights, gains, kinds, chunk, groups, first=None):
+                targets[k][0, :, low : low + size] = result_ref[:, pl.ds(start, size)]
+
+    if first:
+
+        @pl.when(pl.program_id(1) == len(kinds) - 1)
+        def _():
+            copy.wait()
+
+
+def project(place, prepared, weights, gains, kinds, chunks, groups, first=None):
     heads, _, size = gains.shape
     width = weights.shape[1]
     columns = groups * size
     wide = len(kinds) * size
-    fixed = lambda t, place: (0, 0)
+    streams = 4 if width % 512 == 0 else 1
+    fixed = lambda c, t, place: (0, 0)
+    line = lambda c, t, place: (0,)
     smem = pl.BlockSpec(memory_space=pltpu.SMEM)
+    anywhere = pl.BlockSpec(memory_space=pl.ANY)
     rows = (first or prepared)[1].shape[0]
     square = pl.BlockSpec((rows, rows), fixed)
     whole = pl.BlockSpec((rows, width), fixed)
 
-    def weight_index(t, place):
+    def weight_index(part, c, t, place):
         kind = 0
         for step, value in enumerate(kinds):
             kind = jnp.where(t == step, value, kind)
-        return (kind, 0, chunk)
-
-    out_specs = [pl.BlockSpec((1, rows, wide), lambda t, place: (0, 0, 0))] * groups
-    out_shape = [jax.ShapeDtypeStruct((1, rows, wide), bf16)] * groups
+        return (kind, part, chunks[0] + c)
+
+    count = groups * len(chunks)
+    out_specs = [pl.BlockSpec((1, rows, wide), lambda c, t, place: (0, 0, 0))] * count
+    out_shape = [jax.ShapeDtypeStruct((1, rows, wide), bf16)] * count
+    scratch = [pltpu.VMEM((rows, columns), bf16)]
     if first:
-        in_specs = [
-            pl.BlockSpec((rows,), lambda t, place: (0,)),
-            whole,
-            pl.BlockSpec((width,), lambda t, place: (0,)),
-        ]
-        out_specs += [whole, square, square, smem]
+        half = place_half(first[3].shape[1])
+        in_specs = [pl.BlockSpec((rows,), line), whole, pl.BlockSpec((width,), line), anywhere]
+        out_specs += [whole, square, square, smem, anywhere]
         out_shape += [
             jax.ShapeDtypeStruct((rows, width), bf16),
             jax.ShapeDtypeStruct((rows, rows), bf16),
             jax.ShapeDtypeStruct((rows, rows), bf16),
             jax.ShapeDtypeStruct((1, 1), jnp.int32),
+            jax.ShapeDtypeStruct((first[3].shape[0], half), bf16),
         ]
+        scratch = [pltpu.SemaphoreType.DMA(())] + scratch
     else:
         in_specs = [smem, whole, square]
     return pl.pallas_call(
         functools.partial(
-            project_body, kinds=kinds, chunk=chunk, groups=groups, first=first is not None
+            project_body,
+            kinds=kinds,
+            chunks=chunks,
+            groups=groups,
+            first=first is not None,
+            streams=streams,
         ),
         grid_spec=pltpu.PrefetchScalarGridSpec(
             num_scalar_prefetch=1,
-            grid=(len(kinds),),
-            in_specs=in_specs
-            + [
-                pl.BlockSpec((1, width, columns), weight_index),
-                pl.BlockSpec(gains.shape, lambda t, place: (0, 0, 0)),
-            ],
+            grid=(len(chunks), len(kinds)),
+            in_specs=[
+                pl.BlockSpec((1, width // streams, columns), functools.partial(weight_index, part))
+                for part in range(streams)
+            ]
+            + [pl.BlockSpec(gains.shape, lambda c, t, place: (0, 0, 0))]
+            + in_specs,
             out_specs=out_specs,
-            scratch_shapes=[pltpu.VMEM((rows, columns), bf16)],
+            scratch_shapes=scratch,
         ),
         out_shape=out_shape,
         compiler_params=params,
         cost_estimate=cost(
-            2 * rows * width * len(kinds) * columns,
-            2 * width * len(kinds) * columns + 2 * rows * width,
+            2 * rows * width * len(kinds) * len(chunks) * columns,
+            2 * width * len(kinds) * len(chunks) * columns + 2 * rows * width,
         ),
         name="project",
-    )(place, *(first or prepared), weights, gains)
+    )(place, *[weights] * streams, gains, *(first or prepared))
 
 
 def attend_body(place_ref, *refs, groups, low_lane, key_room, query_rows, key_cols):
@@ -278,59 +322,65 @@
     )(place, *queries, *keyvals)
 
 
-def finish_body(place_ref, *refs, others, has_sum, last):
+def finish_body(place_ref, *refs, chunks, others, has_sum, last):
     refs = list(refs)
     out_ref = refs.pop()
     total = refs.pop(0)[...] if has_sum else None
-
-    def add(total, attended_ref, weight):
-        groups = attended_ref.shape[0]
-        wide = jnp.concatenate([attended_ref[g] for g in range(groups)], axis=-1)
+    for m in range(1 + others):
+        attended_refs, weight_ref = refs[:chunks], refs[chunks]
+        refs = refs[chunks + 1 :]
+        wide = jnp.concatenate(
+            [ref[g] for ref in attended_refs for g in range(ref.shape[0])], axis=-1
+        )
+        weight = weight_ref[0, 0] if m else weight_ref[...]
         term = jnp.dot(wide, weight, preferred_element_type=f32)
-        return term if total is None else total + term
-
-    total = add(total, refs[0], refs[1][...])
-    for m in range(others):
-        attended_ref, near_ref, far_ref = refs[2 + 3 * m : 5 + 3 * m]
-        weight = jnp.where(pl.program_id(0) == 0, near_ref[...], far_ref[...])
-        total = add(total, attended_ref, weight)
+        total = term if total is None else total + term
     if last:
         rounded = total.astype(bf16)
-        out_ref[...] = jnp.dot(refs[-1][...], rounded, preferred_element_type=f32).astype(bf16)
+        out_ref[...] = jnp.dot(refs[0][...], rounded, preferred_element_type=f32).astype(bf16)
     else:
         out_ref[...] = total
 
 
-def column_split(out_width):
-    return 2 if out_width % 256 == 0 else 1
-
-
-def finish(place, total, attended, w_out, other_attended, other_weights, back, chunk, out_width):
-    groups, rows, size = attended.shape
-    split = column_split(out_width)
-    half = out_width // split
-    depth = groups * size
-    mine = lambda i, place: (0, lax.bitwise_xor(place[1], i))
-    own = lambda i, place: (chunk, split * place[2] + lax.bitwise_xor(place[1], i))
+def finish(place, total, attended, w_out, other_weights, back, first_chunk):
+    groups, rows, size = attended[0][0].shape
+    split, head_shards, _, half = other_weights.shape
+    chunks = len(attended)
+    out_width = split * half
+    depth = chunks * groups * size
+    block = first_chunk // chunks
+    mine = lambda i, place: (0, i)
+    own = lambda i, place: (block, split * place[2] + i)
     block_a = pl.BlockSpec((groups, rows, size), lambda i, place: (0, 0, 0))
-    block_w = pl.BlockSpec((depth, half), lambda i, place: (chunk, 0))
     specs, operands = [], []
     if total is not None:
         specs.append(pl.BlockSpec((rows, half), mine))
         operands.append(total)
-    specs += [block_a, pl.BlockSpec((depth, half), own)]
-    operands += [attended, w_out]
-    for other, weights in zip(other_attended, other_weights):
-        specs += [block_a, block_w, block_w]
-        operands += [other, *weights]
+    for mask in range(head_shards):
+        specs += [block_a] * chunks
+        operands += [found[mask] for found in attended]
+        if mask == 0:
+            specs.append(pl.BlockSpec((depth, half), own))
+            operands.append(w_out)
+        else:
+            specs.append(
+                pl.BlockSpec(
+                    (1, 1, depth, half),
+                    lambda i, place, mask=mask: (i, lax.bitwise_xor(place[2], mask), block, 0),
+                )
+            )
+            operands.append(other_weights)
     last = back is not None
     if last:
         specs.append(pl.BlockSpec(back.shape, lambda i, place: (0, 0)))
         operands.append(back)
-    count = 1 + len(other_attended)
     return pl.pallas_call(
         functools.partial(
-            finish_body, others=len(other_attended), has_sum=total is not None, last=last
+            finish_body,
+            chunks=chunks,
+            others=head_shards - 1,
+            has_sum=total is not None,
+            last=last,
         ),
         grid_spec=pltpu.PrefetchScalarGridSpec(
             num_scalar_prefetch=1,
@@ -341,25 +391,35 @@
         out_shape=jax.ShapeDtypeStruct((rows, out_width), bf16 if last else f32),
         compiler_params=pltpu.CompilerParams(vmem_limit_bytes=32 * mib),
         cost_estimate=cost(
-            2 * rows * depth * count * out_width, 2 * depth * count * out_width + 8 * rows * out_width
+            2 * rows * depth * head_shards * out_width,
+            2 * depth * head_shards * out_width + 8 * rows * out_width,
         ),
         name="finish",
     )(place, *operands)
+
+
+def fetch_weights(w_out, part, head_shards):
+    depth, width = w_out.shape
+    out_width = width // head_shards
+    if not splits(out_width, head_shards):
+        blocks = jnp.transpose(w_out.reshape(depth, head_shards, out_width), (1, 0, 2))
+        return lax.all_to_all(blocks, "head", split_axis=0, concat_axis=0, tiled=True)[None]
+    pairs = [[i, i + 1] for i in range(0, lax.axis_size("seq"), 2)]
+    found = lax.all_gather(part, "head")
+    return lax.all_gather(found, "seq", axis_index_groups=pairs)
 
 
 def per_device(tokens, survive, norm_gain, w_qkv, qk_gain, w_out):
     heads, size = qk_gain.shape[1:]
     shards, head_shards = lax.axis_size("seq"), lax.axis_size("head")
-    out_width = w_out.shape[1] // head_shards
-    split = column_split(out_width)
-    half = out_width // split
     groups = math.gcd(heads & -heads, shards & -shards)
     ring = shards // groups
     chunks = heads // groups
     me, side = lax.axis_index("seq"), lax.axis_index("head")
-    core = me % split
-    place = jnp.stack([me // ring, core, side]).astype(jnp.int32)
     planes = [[i + ring * g for g in range(groups)] for i in range(ring)]
+    split = 2 if splits(w_out.shape[1] // head_shards, head_shards) else 1
+    piece = (1 - side) * split + me % split if split == 2 else side
+    place = jnp.stack([me // ring, me % ring, side, piece]).astype(jnp.int32)
 
     def swap(blocks):
         return [blocks[0]] + [flip(blocks[k], "seq", k * ring) for k in range(1, groups)]
@@ -375,57 +435,53 @@
         return [found[mask] for mask in range(ring)]
 
     def send_back(blocks):
-        if groups > 1:
-            blocks = lax.all_to_all(
-                blocks, "seq", split_axis=0, concat_axis=0, axis_index_groups=planes, tiled=True
-            )
-        return blocks, [flip(blocks, "head", mask) for mask in range(1, head_shards)]
+        if groups == 1:
+            return blocks
+        return lax.all_to_all(
+            blocks, "seq", split_axis=0, concat_axis=0, axis_index_groups=planes, tiled=True
+        )
+
+    def across(blocks):
+        return [blocks] + [flip(blocks, "head", mask) for mask in range(1, head_shards)]
 
     weights = jnp.transpose(w_qkv, (1, 0, 2))
     gains = jnp.transpose(qk_gain, (1, 0, 2))
 
-    plan = [((1, 2, 0), 0)]
-    plan += [((1, 2), chunk) for chunk in range(1, chunks)]
-    plan += [((0,), chunk) for chunk in range(1, chunks)]
+    plan = [((1, 2, 0), (0,))]
+    plan += [((1, 2), (chunk,)) for chunk in range(1, chunks)]
+    plan += [((0,), tuple(range(1, chunks)))] if chunks > 1 else []
     keyvals, queries = {}, {}
-    normed = chosen = back = count = None
     waiting = None
-    for kinds, chunk in plan:
-        if normed is None:
-            found = project(
-                place, None, weights, gains, kinds, chunk, groups, (survive, tokens, norm_gain)
-            )
-            normed, chosen, back, count = found[groups:]
+    for kinds, which in plan:
+        if not queries:
+            operands = (survive, tokens, norm_gain, w_out)
+            found = project(place, None, weights, gains, kinds, which, groups, operands)
+            normed, chosen, back, count, part = found[groups:]
+            other_weights = fetch_weights(w_out, part, head_shards)
         else:
             source = chain(normed, blocks[1]) if groups > 1 else normed
-            found = project(place, (count, source, chosen), weights, gains, kinds, chunk, groups)
-        sent = found[:groups]
+            found = project(place, (count, source, chosen), weights, gains, kinds, which, groups)
         if waiting is not None:
             ready, owner = waiting
-            keyvals[owner] = everywhere(list(chain(tuple(ready), sent[0])))
-        blocks = swap(sent)
-        waiting = (blocks, chunk) if 1 in kinds else None
-        if 0 in kinds:
-            queries[chunk] = (blocks, (len(kinds) - 1) * size)
+            keyvals[owner] = everywhere(list(chain(tuple(ready), found[0])))
+        for i, chunk in enumerate(which):
+            blocks = swap(found[i * groups : (i + 1) * groups])
+            if 0 in kinds:
+                queries[chunk] = (blocks, (len(kinds) - 1) * size)
+        waiting = (blocks, which[0]) if 1 in kinds else None
     if waiting is not None:
         keyvals[waiting[1]] = everywhere(waiting[0])
 
-    other_weights = []
-    for mask in range(1, head_shards):
-        column = lax.bitwise_xor(side, mask) * out_width + core * half
-        rows = lax.dynamic_slice(chain(w_out, normed), (0, column), (w_out.shape[0], half))
-        near = flip(rows, "head", mask)
-        other_weights.append((near, flip(near, "seq", 1) if split == 2 else near))
-
-    total = None
+    attended = []
     for chunk in range(chunks):
         query, low_lane = queries[chunk]
-        attended, others = send_back(attend(place, query, low_lane, keyvals[chunk], shards))
-        last = back if chunk == chunks - 1 else None
-        total = finish(
-            place, total, attended, w_out, others, other_weights, last, chunk, out_width
-        )
-    return total
+        attended.append(send_back(attend(place, query, low_lane, keyvals[chunk], shards)))
+    total = None
+    if chunks > 1:
+        early = [across(found) for found in attended[:-1]]
+        total = finish(place, None, early, w_out, other_weights, None, 0)
+    final = across(attended[-1] if total is None else chain(attended[-1], total))
+    return finish(place, total, [final], w_out, other_weights, back, chunks - 1)
 
 
 def solution(mesh):

time: 216 us -> 358 us (1.66)
  the two profiles are of different devices: /device:TPU:12 before, /device:TPU:0 now
where the time goes in v1:
time: 358 us; the launch traced here: 355 us
  Pallas kernels  141 us (39%)
  waiting for transfers between devices  115 us (32%)
  starting transfers between devices  60.7 us (17%)
  local copies, waits for them, and re-layouts  24.6 us (7%)
  between operations  13.7 us (4%)
    pallas_call x4, Pallas kernels, project(): pl.pallas_call(functools.partial(project_body, kinds=kinds, chunks=chunks...  106 us
    all_gather x1, waiting for transfers between devices, fetch_weights(): found = lax.all_gather(part, 'head')  65.3 us
    ppermute x27, waiting for transfers between devices, flip(): return lax.ppermute(values, axis, [(i, i ^ mask) for i in range(size)])  49.6 us
    ppermute x27, starting transfers between devices, flip(): return lax.ppermute(values, axis, [(i, i ^ mask) for i in range(size)])  44.3 us
    pallas_call x3, Pallas kernels, attend(): pl.pallas_call(functools.partial(attend_body, groups=groups, low_lane=low...  26.6 us
    unnamed x76, local copies, waits for them, and re-layouts  23.8 us
    all_to_all x3, starting transfers between devices, send_back(): lax.all_to_all(blocks, 'seq', split_axis=0, concat_axis=0, axis_index_gro...  16.2 us
    pallas_call x2, Pallas kernels, finish(): pl.pallas_call(functools.partial(finish_body, chunks=chunks, others=head_...  7.79 us
  transfers between devices with their start and end apart: 32, of which 9 were waited for; matrix products, arithmetic and copies ran while one was open for 1% of the time, Pallas kernels for 16%

profile of v1, /device:TPU:0, one launch (start us, length us, event | category | flops | bytes accessed | tf_op | source)
XLA Modules:
  0.0 355.5 jit_solution(11383035071915077550)
XLA Ops:
  7.1 78.3 %project.4 = (bf16[1,384,384]{2,1,0:T(8,128)(2,1)}, bf16[1,384,384]{2,1,0:T(8,128)(2,1)}, bf16[1,384,384]{2,1,0:T(8,128)(2,1)}, bf16[1,384,384]{2,1,0:T(8,128)(2...) custom-call(s32[4]{0:T(128)} %pad_add_fusion.place_ref, ...), custom_call_target="tpu_custom_call" | custom-call | flops 3623878656 | bytes 11796480 | tf_op jit(solution)/shard_map/project/pallas_call | solution.py:173
  85.6 65.3 %all-gather.5.cloned.1.call-done = bf16[3072,768]{1,0:T(8,128)(2,1)} async-done(((bf16[1536,768]{1,0:T(8,128)(2,1)}), bf16[3072,768]{1,0:T(8,128)(2,1)}) %all-gather.5.cloned.1.call-update) | async-done | bytes 4718608 | tf_op jit(solution)/shard_map/all_gather | solution.py:408
  150.9 0.9 copy-done.22
  151.9 1.5 collective-permute-start
  153.4 2.4 collective-permute-start.1
  156.3 9.9 %collective-permute-done.refs_1_ = bf16[1,384,384]{2,1,0:T(8,128)(2,1)S(1)} collective-permute-done((bf16[1,384,384]{2,1,0:T(8,128)(2,1)S(1)}, bf16[1,384,384]{2,1,0:T(8,128)(2,1)S(1)}, u32[]{:S(2)}, u32[]{:S(2)}) %collective-permute-start) | collective-permute-done | bytes 294944 | tf_op jit(solution)/shard_map/ppermute | solution.py:28
  166.1 9.8 %project.5 = (bf16[1,384,256]{2,1,0:T(8,128)(2,1)}, bf16[1,384,256]{2,1,0:T(8,128)(2,1)}, bf16[1,384,256]{2,1,0:T(8,128)(2,1)}, bf16[1,384,256]{2,1,0:T(8,128)(2,1)}) custom-call(s32[4]{0:T(128)} %pad_add_fusion.place_ref, bf16[3,3072,1536]{2,1,0:T(8,128)(2,1)} %bitcast.14, bf16[3,3072,1536]{2,1,0:T(8,128)(2,1)} %bitcast.15, ...), custom_call_target="tpu_custom_call" | custom-call | flops 2415919104 | bytes 8650752 | tf_op jit(solution)/shard_map/project/pallas_call | solution.py:173
  175.9 4.3 %collective-permute-start.11 = (bf16[1,384,256]{2,1,0:T(8,128)(2,1)}, bf16[1,384,256]{2,1,0:T(8,128)(2,1)S(1)}, u32[]{:S(2)}, u32[]{:S(2)}) collective-permute-start(bf16[1,384,256]{2,1,0:T(8,128)(2,1)} %get-tuple-element.67), channel_id=1, source_target_pairs={{0,16},{2,18},{4,20},{6,22},{8,24},{10,26},{12,28},{14,30},{16,0},... | collective-permute-start | bytes 589832 | tf_op jit(solution)/shard_map/ppermute | solution.py:28
  180.5 1.9 collective-permute-start.4
  182.5 1.4 collective-permute-done.6
  183.9 9.0 %project.6 = (bf16[1,384,256]{2,1,0:T(8,128)(2,1)}, bf16[1,384,256]{2,1,0:T(8,128)(2,1)}, bf16[1,384,256]{2,1,0:T(8,128)(2,1)}, bf16[1,384,256]{2,1,0:T(8,128)(2,1)}) custom-call(s32[4]{0:T(128)} %pad_add_fusion.place_ref, bf16[3,3072,1536]{2,1,0:T(8,128)(2,1)} %bitcast.18, bf16[3,3072,1536]{2,1,0:T(8,128)(2,1)} %bitcast.19, ...), custom_call_target="tpu_custom_call" | custom-call | flops 2415919104 | bytes 8650752 | tf_op jit(solution)/shard_map/project/pallas_call | solution.py:173
  192.9 9.1 %collective-permute-start.7 = (bf16[1,384,256]{2,1,0:T(8,128)(2,1)}, bf16[1,384,256]{2,1,0:T(8,128)(2,1)S(1)}, u32[]{:S(2)}, u32[]{:S(2)}) collective-permute-start(bf16[1,384,256]{2,1,0:T(8,128)(2,1)} %get-tuple-element.61), channel_id=1, source_target_pairs={{0,8},{2,10},{4,12},{6,14},{8,0},{10,2},{12,4},{14,6},{16,24},{18,... | collective-permute-start | bytes 589832 | tf_op jit(solution)/shard_map/ppermute | solution.py:28
  202.6 2.1 collective-permute-start.21
  204.7 1.2 collective-permute-done.7
  205.9 4.6 %collective-permute-start.22 = (bf16[1,384,256]{2,1,0:T(8,128)(2,1)}, bf16[1,384,256]{2,1,0:T(8,128)(2,1)S(1)}, u32[]{:S(2)}, u32[]{:S(2)}) collective-permute-start(bf16[1,384,256]{2,1,0:T(8,128)(2,1)} %get-tuple-element.80), channel_id=1, source_target_pairs={{0,24},{2,26},{4,28},{6,30},{8,16},{10,18},{12,20},{14,22},{16,8},... | collective-permute-start | bytes 589832 | tf_op jit(solution)/shard_map/ppermute | solution.py:28
  210.5 9.4 %project.7 = (bf16[1,384,128]{2,1,0:T(8,128)(2,1)}, bf16[1,384,128]{2,1,0:T(8,128)(2,1)}, bf16[1,384,128]{2,1,0:T(8,128)(2,1)}, bf16[1,384,128]{2,1,0:T(8,128)(2...) custom-call(s32[4]{0:T(128)} %pad_add_fusion.place_ref, ...), custom_call_target="tpu_custom_call" | custom-call | flops 2415919104 | bytes 8650752 | tf_op jit(solution)/shard_map/project/pallas_call | solution.py:173
  219.9 0.7 constant_dynamic-update-slice_fusion.7
  220.6 0.7 constant_dynamic-update-slice_fusion.6
  221.3 0.7 constant_dynamic-update-slice_fusion.5
  222.0 0.7 constant_dynamic-update-slice_fusion.4.refs_4_
  222.8 1.5 collective-permute-start.24
  224.8 9.1 %attend.3 = bf16[4,384,128]{2,1,0:T(8,128)(2,1)} custom-call(s32[4]{0:T(128)} %pad_add_fusion.place_ref, bf16[1,384,384]{2,1,0:T(8,128)(2,1)} %get-tuple-element.55.refs_0_, bf16[1,384,384]{2,1,0:T(8,128)(2,1)} %copy-done.14, bf16[1,384,384]{2,1,0:T(8,128)(2,1)} %copy-done.15, bf16[1,384,384]{2,1,0:T(8,128)(2,1)} %copy-done.16, ...), custom_call_target="tpu_custom_call" | custom-call | flops 2415919104 | bytes 3145728 | tf_op jit(solution)/shard_map/attend/pallas_call | solution.py:292
  233.9 7.0 %all-to-all-start = ((bf16[4,384,128]{2,1,0:T(8,128)(2,1)}), bf16[4,384,128]{2,1,0:T(8,128)(2,1)S(1)}, u32[]{:S(2)}, u32[]{:S(2)}) async-start(bf16[4,384,128]{2,1,0:T(8,128)(2,1)} %attend.3), calls=%async_computation | async-start | bytes 786432 | tf_op jit(solution)/shard_map/all_to_all | solution.py:440
  241.0 3.8 %collective-permute-start.10 = (bf16[1,384,128]{2,1,0:T(8,128)(2,1)S(1)}, bf16[1,384,128]{2,1,0:T(8,128)(2,1)S(1)}, u32[]{:S(2)}, u32[]{:S(2)}) collective-permute-start(bf16[1,384,128]{2,1,0:T(8,128)(2,1)S(1)} %copy-done.28), channel_id=1, source_target_pairs={{0,24},{2,26},{4,28},{6,30},{8,16},{10,18},{12,20},{14,22},{16,8},... | collective-permute-start | bytes 294920 | tf_op jit(solution)/shard_map/ppermute | solution.py:28
  244.8 10.2 %collective-permute-done.10.refs_3_ = bf16[1,384,128]{2,1,0:T(8,128)(2,1)S(1)} collective-permute-done((bf16[1,384,128]{2,1,0:T(8,128)(2,1)S(1)}, bf16[1,384,128]{2,1,0:T(8,128)(2,1)S(1)}, u32[]{:S(2)}, u32[]{:S(2)}) %collective-permute-start.10) | collective-permute-done | bytes 98336 | tf_op jit(solution)/shard_map/ppermute | solution.py:28
  255.1 3.8 %collective-permute-start.9 = (bf16[1,384,128]{2,1,0:T(8,128)(2,1)S(1)}, bf16[1,384,128]{2,1,0:T(8,128)(2,1)S(1)}, u32[]{:S(2)}, u32[]{:S(2)}) collective-permute-start(bf16[1,384,128]{2,1,0:T(8,128)(2,1)S(1)} %copy-done.26), channel_id=1, source_target_pairs={{0,16},{2,18},{4,20},{6,22},{8,24},{10,26},{12,28},{14,30},{16,0},... | collective-permute-start | bytes 294920 | tf_op jit(solution)/shard_map/ppermute | solution.py:28
  259.4 2.6 collective-permute-done.9.refs_2_
  262.9 8.7 %attend.4 = bf16[4,384,128]{2,1,0:T(8,128)(2,1)} custom-call(s32[4]{0:T(128)} %pad_add_fusion.place_ref, bf16[1,384,128]{2,1,0:T(8,128)(2,1)} %get-tuple-element.63.refs_0_, bf16[1,384,128]{2,1,0:T(8,128)(2,1)} %copy-done.32, bf16[1,384,128]{2,1,0:T(8,128)(2,1)} %copy-done.34, bf16[1,384,128]{2,1,0:T(8,128)(2,1)} %copy-done.30, ...), custom_call_target="tpu_custom_call" | custom-call | flops 2415919104 | bytes 3145728 | tf_op jit(solution)/shard_map/attend/pallas_call | solution.py:292
  271.5 5.7 %all-to-all-start.1 = ((bf16[4,384,128]{2,1,0:T(8,128)(2,1)}), bf16[4,384,128]{2,1,0:T(8,128)(2,1)S(1)}, u32[]{:S(2)}, u32[]{:S(2)}) async-start(bf16[4,384,128]{2,1,0:T(8,128)(2,1)} %attend.4), calls=%async_computation.1 | async-start | bytes 786432 | tf_op jit(solution)/shard_map/all_to_all | solution.py:440
  277.3 2.0 collective-permute-start.18
  279.3 2.4 collective-permute-start.19
  281.7 6.3 %collective-permute-done.18.refs_1_ = bf16[1,384,128]{2,1,0:T(8,128)(2,1)S(1)} collective-permute-done((bf16[1,384,128]{2,1,0:T(8,128)(2,1)S(1)}, bf16[1,384,128]{2,1,0:T(8,128)(2,1)S(1)}, u32[]{:S(2)}, u32[]{:S(2)}) %collective-permute-start.18) | collective-permute-done | bytes 98336 | tf_op jit(solution)/shard_map/ppermute | solution.py:28
  288.5 8.0 %collective-permute-done.19.refs_2_ = bf16[1,384,128]{2,1,0:T(8,128)(2,1)S(1)} collective-permute-done((bf16[1,384,128]{2,1,0:T(8,128)(2,1)S(1)}, bf16[1,384,128]{2,1,0:T(8,128)(2,1)S(1)}, u32[]{:S(2)}, u32[]{:S(2)}) %collective-permute-start.19) | collective-permute-done | bytes 98336 | tf_op jit(solution)/shard_map/ppermute | solution.py:28
  297.8 8.8 %attend.5 = bf16[4,384,128]{2,1,0:T(8,128)(2,1)} custom-call(s32[4]{0:T(128)} %pad_add_fusion.place_ref, bf16[1,384,128]{2,1,0:T(8,128)(2,1)} %get-tuple-element.75.refs_0_, bf16[1,384,128]{2,1,0:T(8,128)(2,1)} %copy-done.29, bf16[1,384,128]{2,1,0:T(8,128)(2,1)} %copy-done.31, bf16[1,384,128]{2,1,0:T(8,128)(2,1)} %copy-done.33, ...), custom_call_target="tpu_custom_call" | custom-call | flops 2415919104 | bytes 3145728 | tf_op jit(solution)/shard_map/attend/pallas_call | solution.py:292
  306.6 3.5 all-to-all-start.2
  310.1 0.7 copy-done.4
  310.9 0.8 copy-done.6
  311.6 3.7 %copy-done = bf16[1536,3072]{1,0:T(8,128)(2,1)S(1)} copy-done((bf16[1536,3072]{1,0:T(8,128)(2,1)S(1)}, bf16[1536,3072]{1,0:T(8,128)(2,1)}, u32[]{:S(2)}) %copy-start) | copy-done | bytes 9437208
  315.3 3.7 %copy-done.2 = bf16[4,1536,768]{2,1,0:T(8,128)(2,1)S(1)} copy-done((bf16[4,1536,768]{2,1,0:T(8,128)(2,1)S(1)}, bf16[4,1536,768]{2,1,0:T(8,128)(2,1)}, u32[]{:S(2)}) %copy-start.2) | copy-done | bytes 9437208
  319.0 1.0 copy-done.5
  320.0 1.0 copy-done.7
  321.0 3.7 %finish.2.refs_0_ = f32[384,1536]{1,0:T(8,128)S(1)} custom-call(s32[4]{0:T(128)S(1)} %copy-done.9, bf16[4,384,128]{2,1,0:T(8,128)(2,1)S(1)} %all-to-all-done.refs_0_, bf16[4,384,128]{2,1,0:T(8,128)(2,1)S(1)} %all-to-all-done.1.refs_1_, bf16[1536,3072]{1,0:T(8,128)(2,1)S(1)} %copy-done, bf16[4,384,128]{2,1,0:T(8,128)(2,1)S(1)} %copy-done.5, ...), custom_call_target="tpu_custom_call" | custom-call | flops 2415919104 | bytes 11010048 | tf_op jit(solution)/shard_map/finish/pallas_call | solution.py:377
  324.7 1.5 collective-permute-start.26
  326.3 10.0 %collective-permute-done.26.refs_3_ = bf16[4,384,128]{2,1,0:T(8,128)(2,1)S(1)} collective-permute-done((bf16[4,384,128]{2,1,0:T(8,128)(2,1)S(1)}, bf16[4,384,128]{2,1,0:T(8,128)(2,1)S(1)}, u32[]{:S(2)}, u32[]{:S(2)}) %collective-permute-start.26) | collective-permute-done | bytes 393248 | tf_op jit(solution)/shard_map/ppermute | solution.py:28
  336.3 3.7 %copy-done.1 = bf16[1536,3072]{1,0:T(8,128)(2,1)S(1)} copy-done((bf16[1536,3072]{1,0:T(8,128)(2,1)S(1)}, bf16[1536,3072]{1,0:T(8,128)(2,1)}, u32[]{:S(2)}) %copy-start.1) | copy-done | bytes 9437208
  339.9 3.7 %copy-done.3 = bf16[4,1536,768]{2,1,0:T(8,128)(2,1)S(1)} copy-done((bf16[4,1536,768]{2,1,0:T(8,128)(2,1)S(1)}, bf16[4,1536,768]{2,1,0:T(8,128)(2,1)}, u32[]{:S(2)}) %copy-start.3) | copy-done | bytes 9437208
  343.6 1.0 copy-done.8
  344.6 4.1 %finish.3 = bf16[384,1536]{1,0:T(8,128)(2,1)} custom-call(s32[4]{0:T(128)S(1)} %copy-done.9, f32[384,1536]{1,0:T(8,128)S(1)} %finish.2.refs_0_, bf16[4,384,128]{2,1,0:T(8,128)(2,1)S(1)} %all-to-all-done.2.refs_1_, bf16[1536,3072]{1,0:T(8,128)(2,1)S(1)} %copy-done.1, bf16[4,384,128]{2,1,0:T(8,128)(2,1)S(1)} %collective-permute-done.26.refs_3_, ...), custom_call_target="tpu_custom_call" | custom-call | flops 1207959552 | bytes 7864320 | tf_op jit(solution)/shard_map/finish/pallas_call | solution.py:377
  (111 shorter events, 6.0 us)
Async XLA Ops:
  6.5 144.4 %all-gather.5.cloned.1.call-start = ((), (), s32[]{:S(2)}) async-start(), calls=%async_computation.3 | async-start | bytes 7077888 | tf_op jit(solution)/shard_map/all_gather | solution.py:408
  85.4 226.2 %all-gather.7.cloned.1.call-start = ((), (), s32[]{:S(2)}) async-start(), calls=%async_computation.4 | async-start | bytes 14155776 | tf_op jit(solution)/shard_map/all_gather | solution.py:409
  151.9 14.3 %collective-permute-start = (bf16[1,384,384]{2,1,0:T(8,128)(2,1)S(1)}, bf16[1,384,384]{2,1,0:T(8,128)(2,1)S(1)}, u32[]{:S(2)}, u32[]{:S(2)}) collective-permute-start(bf16[1,384,384]{2,1,0:T(8,128)(2,1)S(1)} %copy-done.22), channel_id=1, source_target_pairs={{0,8},{2,10},{4,12},{6,14},{8,0},{10,2},{12,4},{14,6},{16,24},{18,... | collective-permute-start | bytes 884744 | tf_op jit(solution)/shard_map/ppermute | solution.py:28
  153.4 26.9 %collective-permute-start.1 = (bf16[1,384,384]{2,1,0:T(8,128)(2,1)S(1)}, bf16[1,384,384]{2,1,0:T(8,128)(2,1)S(1)}, u32[]{:S(2)}, u32[]{:S(2)}) collective-permute-start(bf16[1,384,384]{2,1,0:T(8,128)(2,1)S(1)} %copy-done.21), channel_id=1, source_target_pairs={{0,16},{2,18},{4,20},{6,22},{8,24},{10,26},{12,28},{14,30},{16,0},... | collective-permute-start | bytes 884744 | tf_op jit(solution)/shard_map/ppermute | solution.py:28
  155.8 24.5 %collective-permute-start.2 = (bf16[1,384,384]{2,1,0:T(8,128)(2,1)S(1)}, bf16[1,384,384]{2,1,0:T(8,128)(2,1)S(1)}, u32[]{:S(2)}, u32[]{:S(2)}) collective-permute-start(bf16[1,384,384]{2,1,0:T(8,128)(2,1)S(1)} %copy-done.20), channel_id=1, source_target_pairs={{0,24},{2,26},{4,28},{6,30},{8,16},{10,18},{12,20},{14,22},{16,8},... | collective-permute-start | bytes 884744 | tf_op jit(solution)/shard_map/ppermute | solution.py:28
  166.1 14.2 %copy-start.14 = (bf16[1,384,384]{2,1,0:T(8,128)(2,1)}, bf16[1,384,384]{2,1,0:T(8,128)(2,1)S(1)}, u32[]{:S(2)}) copy-start(bf16[1,384,384]{2,1,0:T(8,128)(2,1)S(1)} %collective-permute-done.refs_1_) | copy-start | bytes 884740
  166.1 14.2 %copy-start.13 = (bf16[1,384,384]{2,1,0:T(8,128)(2,1)S(1)}, bf16[1,384,384]{2,1,0:T(8,128)(2,1)}, u32[]{:S(2)}) copy-start(bf16[1,384,384]{2,1,0:T(8,128)(2,1)} %get-tuple-element.55.refs_0_) | copy-start | bytes 884740
  175.9 8.0 %collective-permute-start.6 = (bf16[1,384,256]{2,1,0:T(8,128)(2,1)}, bf16[1,384,256]{2,1,0:T(8,128)(2,1)S(1)}, u32[]{:S(2)}, u32[]{:S(2)}) collective-permute-start(bf16[1,384,256]{2,1,0:T(8,128)(2,1)} %get-tuple-element.59), channel_id=1, source_target_pairs={{0,8},{2,10},{4,12},{6,14},{8,0},{10,2},{12,4},{14,6},{16,24},{18,... | collective-permute-start | bytes 589832 | tf_op jit(solution)/shard_map/ppermute | solution.py:28
  175.9 26.1 %collective-permute-start.11 = (bf16[1,384,256]{2,1,0:T(8,128)(2,1)}, bf16[1,384,256]{2,1,0:T(8,128)(2,1)S(1)}, u32[]{:S(2)}, u32[]{:S(2)}) collective-permute-start(bf16[1,384,256]{2,1,0:T(8,128)(2,1)} %get-tuple-element.67), channel_id=1, source_target_pairs={{0,16},{2,18},{4,20},{6,22},{8,24},{10,26},{12,28},{14,30},{16,0},... | collective-permute-start | bytes 589832 | tf_op jit(solution)/shard_map/ppermute | solution.py:28
  180.2 21.9 %collective-permute-start.12 = (bf16[1,384,256]{2,1,0:T(8,128)(2,1)}, bf16[1,384,256]{2,1,0:T(8,128)(2,1)S(1)}, u32[]{:S(2)}, u32[]{:S(2)}) collective-permute-start(bf16[1,384,256]{2,1,0:T(8,128)(2,1)} %get-tuple-element.68), channel_id=1, source_target_pairs={{0,24},{2,26},{4,28},{6,30},{8,16},{10,18},{12,20},{14,22},{16,8},... | collective-permute-start | bytes 589832 | tf_op jit(solution)/shard_map/ppermute | solution.py:28
  180.3 12.6 %copy-start.15 = (bf16[1,384,384]{2,1,0:T(8,128)(2,1)}, bf16[1,384,384]{2,1,0:T(8,128)(2,1)S(1)}, u32[]{:S(2)}) copy-start(bf16[1,384,384]{2,1,0:T(8,128)(2,1)S(1)} %collective-permute-done.1.refs_2_) | copy-start | bytes 884740
  180.3 12.6 %copy-start.16 = (bf16[1,384,384]{2,1,0:T(8,128)(2,1)}, bf16[1,384,384]{2,1,0:T(8,128)(2,1)S(1)}, u32[]{:S(2)}) copy-start(bf16[1,384,384]{2,1,0:T(8,128)(2,1)S(1)} %collective-permute-done.2.refs_3_) | copy-start | bytes 884740
  180.5 22.1 %copy-start.10 = (bf16[4,384,256]{2,1,0:T(8,128)(2,1)}, bf16[4,384,256]{2,1,0:T(8,128)(2,1)S(1)}, u32[]{:S(2)}) copy-start(bf16[4,384,256]{2,1,0:T(8,128)(2,1)S(1)} %pad_maximum_fusion.refs_4_) | copy-start | bytes 2359300
  180.5 21.5 %copy-start.12 = (bf16[1,384,256]{2,1,0:T(8,128)(2,1)S(1)}, bf16[1,384,256]{2,1,0:T(8,128)(2,1)}, u32[]{:S(2)}) copy-start(bf16[1,384,256]{2,1,0:T(8,128)(2,1)} %get-tuple-element.70) | copy-start | bytes 589828
  180.5 30.0 %collective-permute-start.4 = (bf16[4,384,256]{2,1,0:T(8,128)(2,1)S(1)}, bf16[4,384,256]{2,1,0:T(8,128)(2,1)}, u32[]{:S(2)}, u32[]{:S(2)}) collective-permute-start(bf16[4,384,256]{2,1,0:T(8,128)(2,1)S(1)} %pad_maximum_fusion.refs_4_), channel_id=1, source_target_pairs={{0,4},{2,6},{4,0},{6,2},{8,12},{10,14},{12,8},{14,10},{16,20},{18,... | collective-permute-start | bytes 2359304 | tf_op jit(solution)/shard_map/ppermute | solution.py:28
  192.9 13.0 %collective-permute-start.7 = (bf16[1,384,256]{2,1,0:T(8,128)(2,1)}, bf16[1,384,256]{2,1,0:T(8,128)(2,1)S(1)}, u32[]{:S(2)}, u32[]{:S(2)}) collective-permute-start(bf16[1,384,256]{2,1,0:T(8,128)(2,1)} %get-tuple-element.61), channel_id=1, source_target_pairs={{0,8},{2,10},{4,12},{6,14},{8,0},{10,2},{12,4},{14,6},{16,24},{18,... | collective-permute-start | bytes 589832 | tf_op jit(solution)/shard_map/ppermute | solution.py:28
  202.1 22.2 %copy-start.17 = (bf16[4,384,256]{2,1,0:T(8,128)(2,1)}, bf16[4,384,256]{2,1,0:T(8,128)(2,1)S(1)}, u32[]{:S(2)}) copy-start(bf16[4,384,256]{2,1,0:T(8,128)(2,1)S(1)} %constant_dynamic-update-slice_fusion.refs_4_) | copy-start | bytes 2359300
  202.1 22.2 %collective-permute-start.14 = (bf16[4,384,256]{2,1,0:T(8,128)(2,1)S(1)}, bf16[4,384,256]{2,1,0:T(8,128)(2,1)S(1)}, u32[]{:S(2)}, u32[]{:S(2)}) collective-permute-start(bf16[4,384,256]{2,1,0:T(8,128)(2,1)S(1)} %constant_dynamic-update-slice_fusion.refs_4_), channel_id=1, source_target_pairs={{0,4},{2,6},{4,0},{6,2},{8,12},{10,14},{12,8},{14,10},{16,20},{18,... | collective-permute-start | bytes 2359304 | tf_op jit(solution)/shard_map/ppermute | solution.py:28
  202.6 22.2 %collective-permute-start.3 = (bf16[4,384,256]{2,1,0:T(8,128)(2,1)S(1)}, bf16[4,384,256]{2,1,0:T(8,128)(2,1)}, u32[]{:S(2)}, u32[]{:S(2)}) collective-permute-start(bf16[4,384,256]{2,1,0:T(8,128)(2,1)S(1)} %pad_maximum_fusion.refs_4_), channel_id=1, source_target_pairs={{0,2},{2,0},{4,6},{6,4},{8,10},{10,8},{12,14},{14,12},{16,18},{18,... | collective-permute-start | bytes 2359304 | tf_op jit(solution)/shard_map/ppermute | solution.py:28
  202.6 17.3 %collective-permute-start.21 = (bf16[1,384,256]{2,1,0:T(8,128)(2,1)}, bf16[1,384,256]{2,1,0:T(8,128)(2,1)S(1)}, u32[]{:S(2)}, u32[]{:S(2)}) collective-permute-start(bf16[1,384,256]{2,1,0:T(8,128)(2,1)} %get-tuple-element.79), channel_id=1, source_target_pairs={{0,16},{2,18},{4,20},{6,22},{8,24},{10,26},{12,28},{14,30},{16,0},... | collective-permute-start | bytes 589832 | tf_op jit(solution)/shard_map/ppermute | solution.py:28
  205.9 14.0 %copy-start.11 = (bf16[1,384,256]{2,1,0:T(8,128)(2,1)S(1)}, bf16[1,384,256]{2,1,0:T(8,128)(2,1)}, u32[]{:S(2)}) copy-start(bf16[1,384,256]{2,1,0:T(8,128)(2,1)} %get-tuple-element.81) | copy-start | bytes 589828
  205.9 14.0 %collective-permute-start.22 = (bf16[1,384,256]{2,1,0:T(8,128)(2,1)}, bf16[1,384,256]{2,1,0:T(8,128)(2,1)S(1)}, u32[]{:S(2)}, u32[]{:S(2)}) collective-permute-start(bf16[1,384,256]{2,1,0:T(8,128)(2,1)} %get-tuple-element.80), channel_id=1, source_target_pairs={{0,24},{2,26},{4,28},{6,30},{8,16},{10,18},{12,20},{14,22},{16,8},... | collective-permute-start | bytes 589832 | tf_op jit(solution)/shard_map/ppermute | solution.py:28
  210.5 14.3 %collective-permute-start.5 = (bf16[4,384,256]{2,1,0:T(8,128)(2,1)}, bf16[4,384,256]{2,1,0:T(8,128)(2,1)}, u32[]{:S(2)}, u32[]{:S(2)}) collective-permute-start(bf16[4,384,256]{2,1,0:T(8,128)(2,1)} %collective-permute-done.4.refs_6_), channel_id=1, source_target_pairs={{0,2},{2,0},{4,6},{6,4},{8,10},{10,8},{12,14},{14,12},{16,18},{18,... | collective-permute-start | bytes 2359304 | tf_op jit(solution)/shard_map/ppermute | solution.py:28
  222.8 18.2 %copy-start.28 = (bf16[1,384,128]{2,1,0:T(8,128)(2,1)S(1)}, bf16[1,384,128]{2,1,0:T(8,128)(2,1)}, u32[]{:S(2)}) copy-start(bf16[1,384,128]{2,1,0:T(8,128)(2,1)} %get-tuple-element.66) | copy-start | bytes 294916
  222.8 22.1 %copy-start.27 = (bf16[1,384,128]{2,1,0:T(8,128)(2,1)S(1)}, bf16[1,384,128]{2,1,0:T(8,128)(2,1)}, u32[]{:S(2)}) copy-start(bf16[1,384,128]{2,1,0:T(8,128)(2,1)} %get-tuple-element.64) | copy-start | bytes 294916
  222.8 32.3 %copy-start.26 = (bf16[1,384,128]{2,1,0:T(8,128)(2,1)S(1)}, bf16[1,384,128]{2,1,0:T(8,128)(2,1)}, u32[]{:S(2)}) copy-start(bf16[1,384,128]{2,1,0:T(8,128)(2,1)} %get-tuple-element.65) | copy-start | bytes 294916
  222.8 36.1 %collective-permute-start.24 = (bf16[4,384,256]{2,1,0:T(8,128)(2,1)}, bf16[4,384,256]{2,1,0:T(8,128)(2,1)}, u32[]{:S(2)}, u32[]{:S(2)}) collective-permute-start(bf16[4,384,256]{2,1,0:T(8,128)(2,1)} %constant_dynamic-update-slice_fusion.4.refs_4_), channel_id=1, source_target_pairs={{0,4},{2,6},{4,0},{6,2},{8,12},{10,14},{12,8},{14,10},{16,20},{18,... | collective-permute-start | bytes 2359304 | tf_op jit(solution)/shard_map/ppermute | solution.py:28
  224.3 37.7 %collective-permute-start.13 = (bf16[4,384,256]{2,1,0:T(8,128)(2,1)S(1)}, bf16[4,384,256]{2,1,0:T(8,128)(2,1)S(1)}, u32[]{:S(2)}, u32[]{:S(2)}) collective-permute-start(bf16[4,384,256]{2,1,0:T(8,128)(2,1)S(1)} %constant_dynamic-update-slice_fusion.refs_4_), channel_id=1, source_target_pairs={{0,2},{2,0},{4,6},{6,4},{8,10},{10,8},{12,14},{14,12},{16,18},{18,... | collective-permute-start | bytes 2359304 | tf_op jit(solution)/shard_map/ppermute | solution.py:28
  224.3 9.6 %copy-start.18 = (bf16[4,384,256]{2,1,0:T(8,128)(2,1)}, bf16[4,384,256]{2,1,0:T(8,128)(2,1)S(1)}, u32[]{:S(2)}) copy-start(bf16[4,384,256]{2,1,0:T(8,128)(2,1)S(1)} %collective-permute-done.14.refs_6_) | copy-start | bytes 2359300
  224.3 37.6 %collective-permute-start.15 = (bf16[4,384,256]{2,1,0:T(8,128)(2,1)S(1)}, bf16[4,384,256]{2,1,0:T(8,128)(2,1)}, u32[]{:S(2)}, u32[]{:S(2)}) collective-permute-start(bf16[4,384,256]{2,1,0:T(8,128)(2,1)S(1)} %collective-permute-done.14.refs_6_), channel_id=1, source_target_pairs={{0,2},{2,0},{4,6},{6,4},{8,10},{10,8},{12,14},{14,12},{16,18},{18,... | collective-permute-start | bytes 2359304 | tf_op jit(solution)/shard_map/ppermute | solution.py:28
  233.9 37.6 %all-to-all-start = ((bf16[4,384,128]{2,1,0:T(8,128)(2,1)}), bf16[4,384,128]{2,1,0:T(8,128)(2,1)S(1)}, u32[]{:S(2)}, u32[]{:S(2)}) async-start(bf16[4,384,128]{2,1,0:T(8,128)(2,1)} %attend.3), calls=%async_computation | async-start | bytes 786432 | tf_op jit(solution)/shard_map/all_to_all | solution.py:440
  241.0 14.1 %collective-permute-start.10 = (bf16[1,384,128]{2,1,0:T(8,128)(2,1)S(1)}, bf16[1,384,128]{2,1,0:T(8,128)(2,1)S(1)}, u32[]{:S(2)}, u32[]{:S(2)}) collective-permute-start(bf16[1,384,128]{2,1,0:T(8,128)(2,1)S(1)} %copy-done.28), channel_id=1, source_target_pairs={{0,24},{2,26},{4,28},{6,30},{8,16},{10,18},{12,20},{14,22},{16,8},... | collective-permute-start | bytes 294920 | tf_op jit(solution)/shard_map/ppermute | solution.py:28
  244.8 14.1 %collective-permute-start.8 = (bf16[1,384,128]{2,1,0:T(8,128)(2,1)S(1)}, bf16[1,384,128]{2,1,0:T(8,128)(2,1)S(1)}, u32[]{:S(2)}, u32[]{:S(2)}) collective-permute-start(bf16[1,384,128]{2,1,0:T(8,128)(2,1)S(1)} %copy-done.27), channel_id=1, source_target_pairs={{0,8},{2,10},{4,12},{6,14},{8,0},{10,2},{12,4},{14,6},{16,24},{18,... | collective-permute-start | bytes 294920 | tf_op jit(solution)/shard_map/ppermute | solution.py:28
  255.1 22.2 %copy-start.25 = (bf16[1,384,128]{2,1,0:T(8,128)(2,1)S(1)}, bf16[1,384,128]{2,1,0:T(8,128)(2,1)}, u32[]{:S(2)}) copy-start(bf16[1,384,128]{2,1,0:T(8,128)(2,1)} %get-tuple-element.76) | copy-start | bytes 294916
  255.1 24.2 %copy-start.24 = (bf16[1,384,128]{2,1,0:T(8,128)(2,1)S(1)}, bf16[1,384,128]{2,1,0:T(8,128)(2,1)}, u32[]{:S(2)}) copy-start(bf16[1,384,128]{2,1,0:T(8,128)(2,1)} %get-tuple-element.77) | copy-start | bytes 294916
  255.1 26.6 %copy-start.23 = (bf16[1,384,128]{2,1,0:T(8,128)(2,1)S(1)}, bf16[1,384,128]{2,1,0:T(8,128)(2,1)}, u32[]{:S(2)}) copy-start(bf16[1,384,128]{2,1,0:T(8,128)(2,1)} %get-tuple-element.78) | copy-start | bytes 294916
  255.1 6.9 %collective-permute-start.9 = (bf16[1,384,128]{2,1,0:T(8,128)(2,1)S(1)}, bf16[1,384,128]{2,1,0:T(8,128)(2,1)S(1)}, u32[]{:S(2)}, u32[]{:S(2)}) collective-permute-start(bf16[1,384,128]{2,1,0:T(8,128)(2,1)S(1)} %copy-done.26), channel_id=1, source_target_pairs={{0,16},{2,18},{4,20},{6,22},{8,24},{10,26},{12,28},{14,30},{16,0},... | collective-permute-start | bytes 294920 | tf_op jit(solution)/shard_map/ppermute | solution.py:28
  258.9 38.3 %collective-permute-start.23 = (bf16[4,384,256]{2,1,0:T(8,128)(2,1)}, bf16[4,384,256]{2,1,0:T(8,128)(2,1)}, u32[]{:S(2)}, u32[]{:S(2)}) collective-permute-start(bf16[4,384,256]{2,1,0:T(8,128)(2,1)} %constant_dynamic-update-slice_fusion.4.refs_4_), channel_id=1, source_target_pairs={{0,2},{2,0},{4,6},{6,4},{8,10},{10,8},{12,14},{14,12},{16,18},{18,... | collective-permute-start | bytes 2359304 | tf_op jit(solution)/shard_map/ppermute | solution.py:28
  258.9 38.3 %collective-permute-start.25 = (bf16[4,384,256]{2,1,0:T(8,128)(2,1)}, bf16[4,384,256]{2,1,0:T(8,128)(2,1)}, u32[]{:S(2)}, u32[]{:S(2)}) collective-permute-start(bf16[4,384,256]{2,1,0:T(8,128)(2,1)} %collective-permute-done.24.refs_6_), channel_id=1, source_target_pairs={{0,2},{2,0},{4,6},{6,4},{8,10},{10,8},{12,14},{14,12},{16,18},{18,... | collective-permute-start | bytes 2359304 | tf_op jit(solution)/shard_map/ppermute | solution.py:28
  271.5 25.1 %all-to-all-start.1 = ((bf16[4,384,128]{2,1,0:T(8,128)(2,1)}), bf16[4,384,128]{2,1,0:T(8,128)(2,1)S(1)}, u32[]{:S(2)}, u32[]{:S(2)}) async-start(bf16[4,384,128]{2,1,0:T(8,128)(2,1)} %attend.4), calls=%async_computation.1 | async-start | bytes 786432 | tf_op jit(solution)/shard_map/all_to_all | solution.py:440
  277.3 10.7 %collective-permute-start.18 = (bf16[1,384,128]{2,1,0:T(8,128)(2,1)S(1)}, bf16[1,384,128]{2,1,0:T(8,128)(2,1)S(1)}, u32[]{:S(2)}, u32[]{:S(2)}) collective-permute-start(bf16[1,384,128]{2,1,0:T(8,128)(2,1)S(1)} %copy-done.25), channel_id=1, source_target_pairs={{0,8},{2,10},{4,12},{6,14},{8,0},{10,2},{12,4},{14,6},{16,24},{18,... | collective-permute-start | bytes 294920 | tf_op jit(solution)/shard_map/ppermute | solution.py:28
  279.3 17.3 %collective-permute-start.19 = (bf16[1,384,128]{2,1,0:T(8,128)(2,1)S(1)}, bf16[1,384,128]{2,1,0:T(8,128)(2,1)S(1)}, u32[]{:S(2)}, u32[]{:S(2)}) collective-permute-start(bf16[1,384,128]{2,1,0:T(8,128)(2,1)S(1)} %copy-done.24), channel_id=1, source_target_pairs={{0,16},{2,18},{4,20},{6,22},{8,24},{10,26},{12,28},{14,30},{16,0},... | collective-permute-start | bytes 294920 | tf_op jit(solution)/shard_map/ppermute | solution.py:28
  281.6 15.5 %collective-permute-start.20 = (bf16[1,384,128]{2,1,0:T(8,128)(2,1)S(1)}, bf16[1,384,128]{2,1,0:T(8,128)(2,1)S(1)}, u32[]{:S(2)}, u32[]{:S(2)}) collective-permute-start(bf16[1,384,128]{2,1,0:T(8,128)(2,1)S(1)} %copy-done.23), channel_id=1, source_target_pairs={{0,24},{2,26},{4,28},{6,30},{8,16},{10,18},{12,20},{14,22},{16,8},... | collective-permute-start | bytes 294920 | tf_op jit(solution)/shard_map/ppermute | solution.py:28
  288.0 22.1 %collective-permute-start.16 = (bf16[4,384,128]{2,1,0:T(8,128)(2,1)S(1)}, bf16[4,384,128]{2,1,0:T(8,128)(2,1)S(1)}, u32[]{:S(2)}, u32[]{:S(2)}) collective-permute-start(bf16[4,384,128]{2,1,0:T(8,128)(2,1)S(1)} %all-to-all-done.refs_0_), channel_id=1, source_target_pairs={{0,1},{1,0},{2,3},{3,2},{4,5},{5,4},{6,7},{7,6},{8,9},{9,8},{10,11... | collective-permute-start | bytes 1179656 | tf_op jit(solution)/shard_map/ppermute | solution.py:28
  296.6 14.3 %collective-permute-start.17 = (bf16[4,384,128]{2,1,0:T(8,128)(2,1)S(1)}, bf16[4,384,128]{2,1,0:T(8,128)(2,1)S(1)}, u32[]{:S(2)}, u32[]{:S(2)}) collective-permute-start(bf16[4,384,128]{2,1,0:T(8,128)(2,1)S(1)} %all-to-all-done.1.refs_1_), channel_id=1, source_target_pairs={{0,1},{1,0},{2,3},{3,2},{4,5},{5,4},{6,7},{7,6},{8,9},{9,8},{10,11... | collective-permute-start | bytes 1179656 | tf_op jit(solution)/shard_map/ppermute | solution.py:28
  297.8 13.8 %copy-start.9 = (s32[4]{0:T(128)S(1)}, s32[4]{0:T(128)}, u32[]{:S(2)}) copy-start(s32[4]{0:T(128)} %pad_add_fusion.place_ref) | copy-start | bytes 52
  306.6 18.1 %all-to-all-start.2 = ((bf16[4,384,128]{2,1,0:T(8,128)(2,1)}), bf16[4,384,128]{2,1,0:T(8,128)(2,1)S(1)}, u32[]{:S(2)}, u32[]{:S(2)}) async-start(bf16[4,384,128]{2,1,0:T(8,128)(2,1)} %attend.5), calls=%async_computation.2 | async-start | bytes 786432 | tf_op jit(solution)/shard_map/all_to_all | solution.py:440
  324.7 11.5 %collective-permute-start.26 = (bf16[4,384,128]{2,1,0:T(8,128)(2,1)S(1)}, bf16[4,384,128]{2,1,0:T(8,128)(2,1)S(1)}, u32[]{:S(2)}, u32[]{:S(2)}) collective-permute-start(bf16[4,384,128]{2,1,0:T(8,128)(2,1)S(1)} %all-to-all-done.2.refs_1_), channel_id=1, source_target_pairs={{0,1},{1,0},{2,3},{3,2},{4,5},{5,4},{6,7},{7,6},{8,9},{9,8},{10,11... | collective-permute-start | bytes 1179656 | tf_op jit(solution)/shard_map/ppermute | solution.py:28
  (19 other events, 49.5 us)
Sparse Core Ops, SparseCore 0:
  85.5 65.3 all-gather.4
  152.5 21.8 all-gather.6

commit v2 on v1

--- a/solution.py
+++ b/solution.py
@@ -26,16 +26,6 @@
 def flip(values, axis, mask):
     size = lax.axis_size(axis)
     return lax.ppermute(values, axis, [(i, i ^ mask) for i in range(size)])
-
-
-def place_half(width):
-    head_shards = lax.axis_size("head")
-    out_width = width // head_shards
-    return out_width // 2 if splits(out_width, head_shards) else out_width
-
-
-def splits(out_width, head_shards):
-    return head_shards == 2 and out_width % 256 == 0
 
 
 def chain(values, *earlier):
@@ -67,47 +57,30 @@
         normed_ref[low : low + rows, :] = layer_norm(part, gain).astype(bf16)
 
 
-def project_body(place_ref, *refs, kinds, chunks, groups, first, streams):
+def project_body(place_ref, *refs, steps, groups, first):
     refs = list(refs)
     result_ref = refs.pop()
-    weight_refs, gain_ref = refs[:streams], refs[streams]
-    refs = refs[streams + 1 :]
-    outs = refs[3 + first : 3 + first + groups * len(chunks)]
-    plane = place_ref[0]
+    weight_ref, gain_ref = refs[:2]
     if first:
-        survive_ref, tokens_ref, norm_gain_ref, source_ref = refs[:4]
-        normed_ref, chosen_ref, back_ref, count_ref, slice_ref, copy_sem = refs[4 + len(outs) :]
-        half = slice_ref.shape[1]
-        start = pl.multiple_of(place_ref[3] * half, half)
-        copy = pltpu.make_async_copy(source_ref.at[:, pl.ds(start, half)], slice_ref, copy_sem)
-
-        @pl.when(pl.program_id(1) == 0)
+        survive_ref, tokens_ref, norm_gain_ref = refs[2:5]
+        outs, (normed_ref, chosen_ref, back_ref, count_ref) = refs[5:-4], refs[-4:]
+
+        @pl.when(pl.program_id(0) == 0)
         def _():
-            copy.start()
             prepare(
                 survive_ref, tokens_ref, norm_gain_ref, normed_ref, chosen_ref, back_ref, count_ref
             )
 
     else:
-        count_ref, normed_ref, chosen_ref = refs[:3]
-    rows, width = normed_ref.shape
+        (count_ref, normed_ref, chosen_ref), outs = refs[2:5], refs[5:]
+    rows = normed_ref.shape[0]
     size = gain_ref.shape[2]
-    depth = width // streams
-    for step in range(len(chunks) * len(kinds)):
-        chunk, kind = chunks[step // len(kinds)], kinds[step % len(kinds)]
-        low = step % len(kinds) * size
-        targets = outs[step // len(kinds) * groups :][:groups]
-
-        @pl.when(pl.program_id(0) * len(kinds) + pl.program_id(1) == step)
+    plane = place_ref[0]
+    for step, (kind, chunk, target, low) in enumerate(steps):
+
+        @pl.when(pl.program_id(0) == step)
         def _():
-            result = sum(
-                jnp.dot(
-                    normed_ref[:, i * depth : (i + 1) * depth],
-                    weight_ref[0],
-                    preferred_element_type=f32,
-                )
-                for i, weight_ref in enumerate(weight_refs)
-            )
+            result = jnp.dot(normed_ref[...], weight_ref[0], preferred_element_type=f32)
             for g in range(groups):
                 part = result[:, g * size : (g + 1) * size]
                 if kind != 2:
@@ -123,82 +96,70 @@
             result_ref[...] = packed.astype(bf16)
             for k in range(groups):
                 start = pl.multiple_of(lax.bitwise_xor(plane, k) * size, size)
-                targets[k][0, :, low : low + size] = result_ref[:, pl.ds(start, size)]
-
-    if first:
-
-        @pl.when(pl.program_id(1) == len(kinds) - 1)
-        def _():
-            copy.wait()
-
-
-def project(place, prepared, weights, gains, kinds, chunks, groups, first=None):
-    heads, _, size = gains.shape
+                found = result_ref[:, pl.ds(start, size)]
+                outs[target * groups + k][0, :, low : low + size] = found
+
+
+def project(place, prepared, weights, gains, sets, groups, first=None):
+    size = gains.shape[2]
     width = weights.shape[1]
     columns = groups * size
-    wide = len(kinds) * size
-    streams = 4 if width % 512 == 0 else 1
-    fixed = lambda c, t, place: (0, 0)
-    line = lambda c, t, place: (0,)
+    fixed = lambda t, place: (0, 0)
+    line = lambda t, place: (0,)
     smem = pl.BlockSpec(memory_space=pltpu.SMEM)
-    anywhere = pl.BlockSpec(memory_space=pl.ANY)
     rows = (first or prepared)[1].shape[0]
     square = pl.BlockSpec((rows, rows), fixed)
     whole = pl.BlockSpec((rows, width), fixed)
-
-    def weight_index(part, c, t, place):
-        kind = 0
-        for step, value in enumerate(kinds):
-            kind = jnp.where(t == step, value, kind)
-        return (kind, part, chunks[0] + c)
-
-    count = groups * len(chunks)
-    out_specs = [pl.BlockSpec((1, rows, wide), lambda c, t, place: (0, 0, 0))] * count
-    out_shape = [jax.ShapeDtypeStruct((1, rows, wide), bf16)] * count
-    scratch = [pltpu.VMEM((rows, columns), bf16)]
+    steps = [
+        (kind, chunk, target, i * size)
+        for target, (kinds, chunk) in enumerate(sets)
+        for i, kind in enumerate(kinds)
+    ]
+
+    def weight_index(t, place):
+        kind, chunk = steps[0][:2]
+        for step, found in enumerate(steps):
+            kind = jnp.where(t == step, found[0], kind)
+            chunk = jnp.where(t == step, found[1], chunk)
+        return (kind, 0, chunk)
+
+    widths = [len(kinds) * size for kinds, _ in sets for _ in range(groups)]
+    out_specs = [pl.BlockSpec((1, rows, wide), lambda t, place: (0, 0, 0)) for wide in widths]
+    out_shape = [jax.ShapeDtypeStruct((1, rows, wide), bf16) for wide in widths]
     if first:
-        half = place_half(first[3].shape[1])
-        in_specs = [pl.BlockSpec((rows,), line), whole, pl.BlockSpec((width,), line), anywhere]
-        out_specs += [whole, square, square, smem, anywhere]
+        in_specs = [pl.BlockSpec((rows,), line), whole, pl.BlockSpec((width,), line)]
+        out_specs += [whole, square, square, smem]
         out_shape += [
             jax.ShapeDtypeStruct((rows, width), bf16),
             jax.ShapeDtypeStruct((rows, rows), bf16),
             jax.ShapeDtypeStruct((rows, rows), bf16),
             jax.ShapeDtypeStruct((1, 1), jnp.int32),
-            jax.ShapeDtypeStruct((first[3].shape[0], half), bf16),
         ]
-        scratch = [pltpu.SemaphoreType.DMA(())] + scratch
     else:
         in_specs = [smem, whole, square]
-    return pl.pallas_call(
-        functools.partial(
-            project_body,
-            kinds=kinds,
-            chunks=chunks,
-            groups=groups,
-            first=first is not None,
-            streams=streams,
-        ),
+    found = pl.pallas_call(
+        functools.partial(project_body, steps=steps, groups=groups, first=first is not None),
         grid_spec=pltpu.PrefetchScalarGridSpec(
             num_scalar_prefetch=1,
-            grid=(len(chunks), len(kinds)),
+            grid=(len(steps),),
             in_specs=[
-                pl.BlockSpec((1, width // streams, columns), functools.partial(weight_index, part))
-                for part in range(streams)
+                pl.BlockSpec((1, width, columns), weight_index),
+                pl.BlockSpec(gains.shape, lambda t, place: (0, 0, 0)),
             ]
-            + [pl.BlockSpec(gains.shape, lambda c, t, place: (0, 0, 0))]
             + in_specs,
             out_specs=out_specs,
-            scratch_shapes=scratch,
+            scratch_shapes=[pltpu.VMEM((rows, columns), bf16)],
         ),
         out_shape=out_shape,
         compiler_params=params,
         cost_estimate=cost(
-            2 * rows * width * len(kinds) * len(chunks) * columns,
-            2 * width * len(kinds) * len(chunks) * columns + 2 * rows * width,
+            2 * rows * width * len(steps) * columns,
+            2 * width * len(steps) * columns + 2 * rows * width,
         ),
         name="project",
-    )(place, *[weights] * streams, gains, *(first or prepared))
+    )(place, weights, gains, *(first or prepared))
+    blocks = [found[i * groups : (i + 1) * groups] for i in range(len(sets))]
+    return blocks, found[len(sets) * groups :]
 
 
 def attend_body(place_ref, *refs, groups, low_lane, key_room, query_rows, key_cols):
@@ -389,7 +350,7 @@
             out_specs=pl.BlockSpec((rows, half), mine),
         ),
         out_shape=jax.ShapeDtypeStruct((rows, out_width), bf16 if last else f32),
-        compiler_params=pltpu.CompilerParams(vmem_limit_bytes=32 * mib),
+        compiler_params=params,
         cost_estimate=cost(
             2 * rows * depth * head_shards * out_width,
             2 * depth * head_shards * out_width + 8 * rows * out_width,
@@ -398,14 +359,25 @@
     )(place, *operands)
 
 
-def fetch_weights(w_out, part, head_shards):
+def splits(out_width, head_shards):
+    return head_shards == 2 and out_width % 256 == 0
+
+
+def fetch_weights(w_out, me, side, head_shards):
     depth, width = w_out.shape
     out_width = width // head_shards
     if not splits(out_width, head_shards):
         blocks = jnp.transpose(w_out.reshape(depth, head_shards, out_width), (1, 0, 2))
-        return lax.all_to_all(blocks, "head", split_axis=0, concat_axis=0, tiled=True)[None]
+        return lax.all_to_all(blocks, "head", split_axis=0, concat_axis=0, tiled=True)
+    half = out_width // 2
+    column = (1 - side) * out_width + (me % 2) * half
+    return lax.all_gather(lax.dynamic_slice(w_out, (0, column), (depth, half)), "head")
+
+
+def share_weights(found, out_width, head_shards):
+    if not splits(out_width, head_shards):
+        return found[None]
     pairs = [[i, i + 1] for i in range(0, lax.axis_size("seq"), 2)]
-    found = lax.all_gather(part, "head")
     return lax.all_gather(found, "seq", axis_index_groups=pairs)
 
 
@@ -416,21 +388,24 @@
     ring = shards // groups
     chunks = heads // groups
     me, side = lax.axis_index("seq"), lax.axis_index("head")
+    place = jnp.stack([me // ring, me % ring, side]).astype(jnp.int32)
     planes = [[i + ring * g for g in range(groups)] for i in range(ring)]
-    split = 2 if splits(w_out.shape[1] // head_shards, head_shards) else 1
-    piece = (1 - side) * split + me % split if split == 2 else side
-    place = jnp.stack([me // ring, me % ring, side, piece]).astype(jnp.int32)
 
     def swap(blocks):
         return [blocks[0]] + [flip(blocks[k], "seq", k * ring) for k in range(1, groups)]
 
-    def everywhere(blocks):
-        stacked = jnp.concatenate([block[:, :, : 2 * size] for block in blocks])
+    def stack(blocks):
+        return jnp.concatenate([block[:, :, : 2 * size] for block in blocks])
+
+    def everywhere(stacked, gate):
         found = {0: stacked}
         mask = ring // 2
         while mask:
             for known in list(found):
-                found[known | mask] = flip(found[known], "seq", mask)
+                source = found[known]
+                if gate is not None and mask < ring // 2:
+                    source = chain(source, gate)
+                found[known | mask] = flip(source, "seq", mask)
             mask //= 2
         return [found[mask] for mask in range(ring)]
 
@@ -447,39 +422,48 @@
     weights = jnp.transpose(w_qkv, (1, 0, 2))
     gains = jnp.transpose(qk_gain, (1, 0, 2))
 
-    plan = [((1, 2, 0), (0,))]
-    plan += [((1, 2), (chunk,)) for chunk in range(1, chunks)]
-    plan += [((0,), tuple(range(1, chunks)))] if chunks > 1 else []
-    keyvals, queries = {}, {}
-    waiting = None
-    for kinds, which in plan:
-        if not queries:
-            operands = (survive, tokens, norm_gain, w_out)
-            found = project(place, None, weights, gains, kinds, which, groups, operands)
-            normed, chosen, back, count, part = found[groups:]
-            other_weights = fetch_weights(w_out, part, head_shards)
+    plan = [[((1, 2, 0), 0)]]
+    plan += [[((1, 2), chunk)] for chunk in range(1, chunks)]
+    if chunks > 1:
+        plan[1] += [((0,), chunk) for chunk in range(1, chunks)]
+    arrived, stacks, later, fetched, gate = [], [], [], None, None
+    for i, sets in enumerate(plan):
+        if i == 0:
+            operands = (survive, tokens, norm_gain)
+            blocks, rest = project(place, None, weights, gains, sets, groups, operands)
+            normed, chosen, back, count = rest
         else:
-            source = chain(normed, blocks[1]) if groups > 1 else normed
-            found = project(place, (count, source, chosen), weights, gains, kinds, which, groups)
-        if waiting is not None:
-            ready, owner = waiting
-            keyvals[owner] = everywhere(list(chain(tuple(ready), found[0])))
-        for i, chunk in enumerate(which):
-            blocks = swap(found[i * groups : (i + 1) * groups])
-            if 0 in kinds:
-                queries[chunk] = (blocks, (len(kinds) - 1) * size)
-        waiting = (blocks, which[0]) if 1 in kinds else None
-    if waiting is not None:
-        keyvals[waiting[1]] = everywhere(waiting[0])
+            source = chain(normed, stacks[i - 2]) if i > 1 else normed
+            prepared = (count, source, chosen)
+            blocks, _ = project(place, prepared, weights, gains, sets, groups)
+            stacks.append(stack(list(chain(tuple(arrived[i - 1]), blocks[0][0]))))
+        if i == min(1, chunks - 1):
+            later = blocks[1:]
+            fetched = fetch_weights(chain(w_out, blocks[0][0]), me, side, head_shards)
+        arrived.append(swap(blocks[0]))
+        gate = blocks[0][0]
 
     attended = []
+    query, low_lane = arrived[0], 2 * size
     for chunk in range(chunks):
-        query, low_lane = queries[chunk]
-        attended.append(send_back(attend(place, query, low_lane, keyvals[chunk], shards)))
+        if chunk == chunks - 1:
+            stacks.append(stack(list(chain(tuple(arrived[-1]), *attended[:1]))))
+        upcoming = None
+        if chunk < chunks - 1:
+            upcoming = swap(list(chain(tuple(later[chunk]), stacks[min(chunk + 1, len(stacks) - 1)])))
+        keyvals = everywhere(stacks[chunk], gate)
+        before = (stacks[-1],) + tuple(attended[-1:])
+        query = [chain(query[0], *before)] + list(query[1:])
+        attended.append(attend(place, query, low_lane, keyvals, shards))
+        query, low_lane = upcoming, 0
+        gate = tuple(upcoming[1:]) if upcoming else None
+    out_width = w_out.shape[1] // head_shards
+    other_weights = share_weights(chain(fetched, attended[-1]), out_width, head_shards)
+    attended = [send_back(found) for found in attended]
     total = None
     if chunks > 1:
-        early = [across(found) for found in attended[:-1]]
-        total = finish(place, None, early, w_out, other_weights, None, 0)
+        sooner = [across(found) for found in attended[:-1]]
+        total = finish(place, None, sooner, w_out, other_weights, None, 0)
     final = across(attended[-1] if total is None else chain(attended[-1], total))
     return finish(place, total, [final], w_out, other_weights, back, chunks - 1)
 

time: 358 us -> 243 us (0.68)
  Pallas kernels: 141 us -> 79.1 us
  waiting for transfers between devices: 115 us -> 77.7 us
  local copies, waits for them, and re-layouts: 24.6 us -> 7.57 us
  starting transfers between devices: 60.7 us -> 47.9 us
  blocking collectives: 0 us -> 12.8 us
    pallas_call x4 -> x3, Pallas kernels: 106 us -> 35.9 us  [project(): pl.pallas_call(functools.partial(project_body, steps=steps, groups=groups...]
    all_gather x2, waiting for transfers between devices: 65.3 us -> 0.01 us  [the longest x1 0.01 us: fetch_weights(): lax.all_gather(lax.dynamic_slice(w_out, (0, column), (depth, half)), 'head')]
    ppermute x27, waiting for transfers between devices: 49.6 us -> 69.5 us  [flip(): return lax.ppermute(values, axis, [(i, i ^ mask) for i in range(size)])]
    unnamed x76 -> x82, local copies, waits for them, and re-layouts: 23.8 us -> 4.28 us
    all_to_all x0 -> x1, blocking collectives: none -> 12.8 us  [send_back(): lax.all_to_all(blocks, 'seq', split_axis=0, concat_axis=0, axis_index_gro...]
    all_to_all x3 -> x2, starting transfers between devices: 16.2 us -> 6.92 us  [send_back(): lax.all_to_all(blocks, 'seq', split_axis=0, concat_axis=0, axis_index_gro...]
    all_to_all x3 -> x2, waiting for transfers between devices: 0.01 us -> 8.14 us  [send_back(): lax.all_to_all(blocks, 'seq', split_axis=0, concat_axis=0, axis_index_gro...]
    pallas_call x2, Pallas kernels: 7.79 us -> 13 us  [finish(): pl.pallas_call(functools.partial(finish_body, chunks=chunks, others=head_...]
  transfers between devices with their start and end apart: 32 -> 31, of which waited for: 9 -> 15; matrix products, arithmetic and copies ran while one was open for 1% -> 0% of each run, Pallas kernels for 16% -> 19%
where the time goes in v2:
time: 243 us; the launch traced here: 239 us
  Pallas kernels  79.1 us (33%)
  waiting for transfers between devices  77.7 us (32%)
  starting transfers between devices  47.9 us (20%)
  between operations  13.8 us (6%)
  blocking collectives  12.8 us (5%)
  local copies, waits for them, and re-layouts  7.57 us (3%)
    ppermute x27, waiting for transfers between devices, flip(): return lax.ppermute(values, axis, [(i, i ^ mask) for i in range(size)])  69.5 us
    ppermute x27, starting transfers between devices, flip(): return lax.ppermute(values, axis, [(i, i ^ mask) for i in range(size)])  40.7 us
    pallas_call x3, Pallas kernels, project(): pl.pallas_call(functools.partial(project_body, steps=steps, groups=groups...  35.9 us
    pallas_call x3, Pallas kernels, attend(): pl.pallas_call(functools.partial(attend_body, groups=groups, low_lane=low...  30.2 us
    pallas_call x2, Pallas kernels, finish(): pl.pallas_call(functools.partial(finish_body, chunks=chunks, others=head_...  13 us
    all_to_all x1, blocking collectives, send_back(): lax.all_to_all(blocks, 'seq', split_axis=0, concat_axis=0, axis_index_gro...  12.8 us
    all_to_all x2, waiting for transfers between devices, send_back(): lax.all_to_all(blocks, 'seq', split_axis=0, concat_axis=0, axis_index_gro...  8.14 us
    all_to_all x2, starting transfers between devices, send_back(): lax.all_to_all(blocks, 'seq', split_axis=0, concat_axis=0, axis_index_gro...  6.92 us
  transfers between devices with their start and end apart: 31, of which 15 were waited for; matrix products, arithmetic and copies ran while one was open for 0% of the time, Pallas kernels for 19%

profile of v2, /device:TPU:0, one launch (start us, length us, event | category | flops | bytes accessed | tf_op | source)
XLA Modules:
  0.0 239.5 jit_solution(10340619334945181543)
XLA Ops:
  7.1 13.4 %project.3 = (bf16[1,384,384]{2,1,0:T(8,128)(2,1)}, bf16[1,384,384]{2,1,0:T(8,128)(2,1)}, bf16[1,384,384]{2,1,0:T(8,128)(2,1)}, bf16[1,384,384]{2,1,0:T(8,128)(2...) custom-call(s32[3]{0:T(128)} %pad_add_fusion.place_ref, ...), custom_call_target="tpu_custom_call" | custom-call | flops 3623878656 | bytes 11796480 | tf_op jit(solution)/shard_map/project/pallas_call | solution.py:140
  20.5 13.7 %project.4 = (bf16[1,384,256]{2,1,0:T(8,128)(2,1)}, bf16[1,384,256]{2,1,0:T(8,128)(2,1)}, bf16[1,384,256]{2,1,0:T(8,128)(2,1)}, bf16[1,384,256]{2,1,0:T(8,128)(2...) custom-call(s32[3]{0:T(128)} %pad_add_fusion.place_ref, ...), custom_call_target="tpu_custom_call" | custom-call | flops 4831838208 | bytes 14942208 | tf_op jit(solution)/shard_map/project/pallas_call | solution.py:140
  34.2 3.2 %constant_dynamic-slice_fusion = bf16[1536,768]{1,0:T(8,128)(2,1)} fusion(bf16[1536,3072]{1,0:T(8,128)(2,1)} %refs_2_.5, s32[]{:T(128)S(6)} %select_n.21), kind=kLoop, calls=%fused_computation.10 | loop fusion | bytes 4718596 | tf_op jit(solution)/shard_map/dynamic_slice | solution.py:374
  38.3 3.0 %collective-permute-start.3 = (bf16[1,384,384]{2,1,0:T(8,128)(2,1)S(1)}, bf16[1,384,384]{2,1,0:T(8,128)(2,1)S(1)}, u32[]{:S(2)}, u32[]{:S(2)}) collective-permute-start(bf16[1,384,384]{2,1,0:T(8,128)(2,1)S(1)} %copy-done.22), channel_id=1, source_target_pairs={{0,8},{2,10},{4,12},{6,14},{8,0},{10,2},{12,4},{14,6},{16,24},{18,... | collective-permute-start | bytes 884744 | tf_op jit(solution)/shard_map/ppermute | solution.py:28
  41.3 2.6 %collective-permute-start.4 = (bf16[1,384,384]{2,1,0:T(8,128)(2,1)S(1)}, bf16[1,384,384]{2,1,0:T(8,128)(2,1)S(1)}, u32[]{:S(2)}, u32[]{:S(2)}) collective-permute-start(bf16[1,384,384]{2,1,0:T(8,128)(2,1)S(1)} %copy-done.21), channel_id=1, source_target_pairs={{0,16},{2,18},{4,20},{6,22},{8,24},{10,26},{12,28},{14,30},{16,0},... | collective-permute-start | bytes 884744 | tf_op jit(solution)/shard_map/ppermute | solution.py:28
  43.9 10.0 %collective-permute-done.3.refs_1_ = bf16[1,384,384]{2,1,0:T(8,128)(2,1)S(1)} collective-permute-done((bf16[1,384,384]{2,1,0:T(8,128)(2,1)S(1)}, bf16[1,384,384]{2,1,0:T(8,128)(2,1)S(1)}, u32[]{:S(2)}, u32[]{:S(2)}) %collective-permute-start.3) | collective-permute-done | bytes 294944 | tf_op jit(solution)/shard_map/ppermute | solution.py:28
  53.9 10.9 %collective-permute-done.4.refs_2_ = bf16[1,384,384]{2,1,0:T(8,128)(2,1)S(1)} collective-permute-done((bf16[1,384,384]{2,1,0:T(8,128)(2,1)S(1)}, bf16[1,384,384]{2,1,0:T(8,128)(2,1)S(1)}, u32[]{:S(2)}, u32[]{:S(2)}) %collective-permute-start.4) | collective-permute-done | bytes 294944 | tf_op jit(solution)/shard_map/ppermute | solution.py:28
  65.1 1.6 collective-permute-start.7
  66.7 8.8 %project.5 = (bf16[1,384,256]{2,1,0:T(8,128)(2,1)}, bf16[1,384,256]{2,1,0:T(8,128)(2,1)}, bf16[1,384,256]{2,1,0:T(8,128)(2,1)}, bf16[1,384,256]{2,1,0:T(8,128)(2,1)}) custom-call(s32[3]{0:T(128)} %pad_add_fusion.place_ref, bf16[3,3072,1536]{2,1,0:T(8,128)(2,1)} %bitcast.9, f32[12,2,128]{2,1,0:T(2,128)} %bitcast.15, s32[1,1]{1,0:T(1,128)} %get-tuple-element.63.refs_2_, ...), custom_call_target="tpu_custom_call" | custom-call | flops 2415919104 | bytes 8650752 | tf_op jit(solution)/shard_map/project/pallas_call | solution.py:140
  75.6 6.4 %collective-permute-done.7.refs_6_ = bf16[4,384,256]{2,1,0:T(8,128)(2,1)} collective-permute-done((bf16[4,384,256]{2,1,0:T(8,128)(2,1)S(1)}, bf16[4,384,256]{2,1,0:T(8,128)(2,1)}, u32[]{:S(2)}, u32[]{:S(2)}) %collective-permute-start.7) | collective-permute-done | bytes 786464 | tf_op jit(solution)/shard_map/ppermute | solution.py:28
  82.1 6.9 %collective-permute-start = (bf16[1,384,256]{2,1,0:T(8,128)(2,1)S(1)}, bf16[1,384,256]{2,1,0:T(8,128)(2,1)S(1)}, u32[]{:S(2)}, u32[]{:S(2)}) collective-permute-start(bf16[1,384,256]{2,1,0:T(8,128)(2,1)S(1)} %copy-done.25), channel_id=1, source_target_pairs={{0,8},{2,10},{4,12},{6,14},{8,0},{10,2},{12,4},{14,6},{16,24},{18,... | collective-permute-start | bytes 589832 | tf_op jit(solution)/shard_map/ppermute | solution.py:28
  89.0 1.1 collective-permute-start.1
  90.1 1.5 collective-permute-start.2
  91.5 6.8 %collective-permute-done = bf16[1,384,256]{2,1,0:T(8,128)(2,1)S(1)} collective-permute-done((bf16[1,384,256]{2,1,0:T(8,128)(2,1)S(1)}, bf16[1,384,256]{2,1,0:T(8,128)(2,1)S(1)}, u32[]{:S(2)}, u32[]{:S(2)}) %collective-permute-start) | collective-permute-done | bytes 196640 | tf_op jit(solution)/shard_map/ppermute | solution.py:28
  98.3 7.7 %collective-permute-done.1 = bf16[1,384,256]{2,1,0:T(8,128)(2,1)S(1)} collective-permute-done((bf16[1,384,256]{2,1,0:T(8,128)(2,1)S(1)}, bf16[1,384,256]{2,1,0:T(8,128)(2,1)S(1)}, u32[]{:S(2)}, u32[]{:S(2)}) %collective-permute-start.1) | collective-permute-done | bytes 196640 | tf_op jit(solution)/shard_map/ppermute | solution.py:28
  106.2 1.6 collective-permute-start.13
  107.7 4.1 %collective-permute-start.17 = (bf16[1,384,256]{2,1,0:T(8,128)(2,1)}, bf16[1,384,256]{2,1,0:T(8,128)(2,1)S(1)}, u32[]{:S(2)}, u32[]{:S(2)}) collective-permute-start(bf16[1,384,256]{2,1,0:T(8,128)(2,1)} %get-tuple-element.103), channel_id=1, source_target_pairs={{0,8},{2,10},{4,12},{6,14},{8,0},{10,2},{12,4},{14,6},{16,24},{18,... | collective-permute-start | bytes 589832 | tf_op jit(solution)/shard_map/ppermute | solution.py:28
  111.8 1.0 collective-permute-start.18
  112.9 1.5 collective-permute-start.19
  114.5 10.1 %attend.3 = bf16[4,384,128]{2,1,0:T(8,128)(2,1)} custom-call(s32[3]{0:T(128)} %pad_add_fusion.place_ref, bf16[1,384,384]{2,1,0:T(8,128)(2,1)} %get-tuple-element.83.refs_0_, bf16[1,384,384]{2,1,0:T(8,128)(2,1)} %copy-done.11, bf16[1,384,384]{2,1,0:T(8,128)(2,1)} %copy-done.12, bf16[1,384,384]{2,1,0:T(8,128)(2,1)} %copy-done.13, ...), custom_call_target="tpu_custom_call" | custom-call | flops 2415919104 | bytes 3145728 | tf_op jit(solution)/shard_map/attend/pallas_call | solution.py:253
  124.6 4.6 %collective-permute-done.18 = bf16[1,384,256]{2,1,0:T(8,128)(2,1)S(1)} collective-permute-done((bf16[1,384,256]{2,1,0:T(8,128)(2,1)}, bf16[1,384,256]{2,1,0:T(8,128)(2,1)S(1)}, u32[]{:S(2)}, u32[]{:S(2)}) %collective-permute-start.18) | collective-permute-done | bytes 196640 | tf_op jit(solution)/shard_map/ppermute | solution.py:28
  129.9 3.7 %collective-permute-start.10 = (bf16[1,384,128]{2,1,0:T(8,128)(2,1)S(1)}, bf16[1,384,128]{2,1,0:T(8,128)(2,1)S(1)}, u32[]{:S(2)}, u32[]{:S(2)}) collective-permute-start(bf16[1,384,128]{2,1,0:T(8,128)(2,1)S(1)} %copy-done.31), channel_id=1, source_target_pairs={{0,16},{2,18},{4,20},{6,22},{8,24},{10,26},{12,28},{14,30},{16,0},... | collective-permute-start | bytes 294920 | tf_op jit(solution)/shard_map/ppermute | solution.py:28
  133.5 1.3 collective-permute-start.11
  134.9 4.1 %collective-permute-done.10.refs_2_ = bf16[1,384,128]{2,1,0:T(8,128)(2,1)S(1)} collective-permute-done((bf16[1,384,128]{2,1,0:T(8,128)(2,1)S(1)}, bf16[1,384,128]{2,1,0:T(8,128)(2,1)S(1)}, u32[]{:S(2)}, u32[]{:S(2)}) %collective-permute-start.10) | collective-permute-done | bytes 98336 | tf_op jit(solution)/shard_map/ppermute | solution.py:28
  139.0 1.3 collective-permute-done.11.refs_3_
  141.5 0.7 collective-permute-start.20
  142.2 1.6 collective-permute-start.21
  143.8 3.6 %collective-permute-done.20.refs_1_ = bf16[1,384,128]{2,1,0:T(8,128)(2,1)S(1)} collective-permute-done((bf16[1,384,128]{2,1,0:T(8,128)(2,1)S(1)}, bf16[1,384,128]{2,1,0:T(8,128)(2,1)S(1)}, u32[]{:S(2)}, u32[]{:S(2)}) %collective-permute-start.20) | collective-permute-done | bytes 98336 | tf_op jit(solution)/shard_map/ppermute | solution.py:28
  147.4 2.3 collective-permute-start.22
  149.8 2.0 collective-permute-done.21.refs_2_
  151.8 2.2 collective-permute-done.22.refs_3_
  154.5 0.9 copy-done.19
  155.4 9.9 %attend.4 = bf16[4,384,128]{2,1,0:T(8,128)(2,1)} custom-call(s32[3]{0:T(128)} %pad_add_fusion.place_ref, bf16[1,384,128]{2,1,0:T(8,128)(2,1)} %get-tuple-element.91.refs_0_, bf16[1,384,128]{2,1,0:T(8,128)(2,1)} %copy-done.34, bf16[1,384,128]{2,1,0:T(8,128)(2,1)} %copy-done.32, bf16[1,384,128]{2,1,0:T(8,128)(2,1)} %copy-done.33, ...), custom_call_target="tpu_custom_call" | custom-call | flops 2415919104 | bytes 3145728 | tf_op jit(solution)/shard_map/attend/pallas_call | solution.py:253
  165.3 10.1 %attend.5 = bf16[4,384,128]{2,1,0:T(8,128)(2,1)} custom-call(s32[3]{0:T(128)} %pad_add_fusion.place_ref, bf16[1,384,128]{2,1,0:T(8,128)(2,1)} %get-tuple-element.110.refs_0_, bf16[1,384,128]{2,1,0:T(8,128)(2,1)} %copy-done.35, bf16[1,384,128]{2,1,0:T(8,128)(2,1)} %copy-done.36, bf16[1,384,128]{2,1,0:T(8,128)(2,1)} %copy-done.37, ...), custom_call_target="tpu_custom_call" | custom-call | flops 2415919104 | bytes 3145728 | tf_op jit(solution)/shard_map/attend/pallas_call | solution.py:253
  175.5 1.0 copy-done.4
  176.5 12.8 %all_to_all.15.refs_1_ = bf16[4,384,128]{2,1,0:T(8,128)(2,1)S(1)} all-to-all(bf16[4,384,128]{2,1,0:T(8,128)(2,1)S(1)} %copy-done.4), channel_id=1, replica_groups={{0,8,16,24},{2,10,18,26},{4,12,20,28},{6,14,22,30},{1,9,17,25},{3,11,19..., dimensions={0} | all-to-all | bytes 786432 | tf_op jit(solution)/shard_map/all_to_all | solution.py:415
  189.3 3.5 %all-to-all-start = ((bf16[4,384,128]{2,1,0:T(8,128)(2,1)}), bf16[4,384,128]{2,1,0:T(8,128)(2,1)S(1)}, u32[]{:S(2)}, u32[]{:S(2)}) async-start(bf16[4,384,128]{2,1,0:T(8,128)(2,1)} %attend.3), calls=%async_computation | async-start | bytes 786432 | tf_op jit(solution)/shard_map/all_to_all | solution.py:415
  192.8 1.6 collective-permute-start.16
  194.3 8.1 %all-to-all-done.refs_0_ = bf16[4,384,128]{2,1,0:T(8,128)(2,1)S(1)} async-done(((bf16[4,384,128]{2,1,0:T(8,128)(2,1)}), bf16[4,384,128]{2,1,0:T(8,128)(2,1)S(1)}, u32[]{:S(2)}, u32[]{:S(2)}) %all-to-all-start) | async-done | bytes 393248 | tf_op jit(solution)/shard_map/all_to_all | solution.py:415
  202.5 1.5 collective-permute-start.15
  203.9 3.5 %all-to-all-start.2 = ((bf16[4,384,128]{2,1,0:T(8,128)(2,1)}), bf16[4,384,128]{2,1,0:T(8,128)(2,1)S(1)}, u32[]{:S(2)}, u32[]{:S(2)}) async-start(bf16[4,384,128]{2,1,0:T(8,128)(2,1)} %attend.5), calls=%async_computation.2 | async-start | bytes 786432 | tf_op jit(solution)/shard_map/all_to_all | solution.py:415
  207.4 2.8 %collective-permute-done.15.refs_3_ = bf16[4,384,128]{2,1,0:T(8,128)(2,1)S(1)} collective-permute-done((bf16[4,384,128]{2,1,0:T(8,128)(2,1)S(1)}, bf16[4,384,128]{2,1,0:T(8,128)(2,1)S(1)}, u32[]{:S(2)}, u32[]{:S(2)}) %collective-permute-start.15) | collective-permute-done | bytes 393248 | tf_op jit(solution)/shard_map/ppermute | solution.py:28
  210.3 0.7 copy-done.6
  211.0 6.9 %finish.2.refs_0_ = f32[384,1536]{1,0:T(8,128)} custom-call(s32[3]{0:T(128)} %pad_add_fusion.place_ref, bf16[4,384,128]{2,1,0:T(8,128)(2,1)} %copy-done.2, bf16[4,384,128]{2,1,0:T(8,128)(2,1)} %copy-done.1, bf16[1536,3072]{1,0:T(8,128)(2,1)} %refs_2_.5, bf16[4,384,128]{2,1,0:T(8,128)(2,1)} %copy-done.6, bf16[4,384,128]{2,1,0:T(8,128)(2,1)} %copy-done.5, ...), custom_call_target="tpu_custom_call" | custom-call | flops 2415919104 | bytes 11010048 | tf_op jit(solution)/shard_map/finish/pallas_call | solution.py:338
  217.9 1.5 collective-permute-start.26
  219.4 6.3 %collective-permute-done.26.refs_3_ = bf16[4,384,128]{2,1,0:T(8,128)(2,1)S(1)} collective-permute-done((bf16[4,384,128]{2,1,0:T(8,128)(2,1)S(1)}, bf16[4,384,128]{2,1,0:T(8,128)(2,1)S(1)}, u32[]{:S(2)}, u32[]{:S(2)}) %collective-permute-start.26) | collective-permute-done | bytes 393248 | tf_op jit(solution)/shard_map/ppermute | solution.py:28
  225.7 0.8 copy-done.7
  226.5 6.2 %finish.3 = bf16[384,1536]{1,0:T(8,128)(2,1)} custom-call(s32[3]{0:T(128)} %pad_add_fusion.place_ref, f32[384,1536]{1,0:T(8,128)} %finish.2.refs_0_, bf16[4,384,128]{2,1,0:T(8,128)(2,1)} %copy-done, bf16[1536,3072]{1,0:T(8,128)(2,1)} %refs_2_.5, bf16[4,384,128]{2,1,0:T(8,128)(2,1)} %copy-done.7, bf16[2,2,1536,768]{3,2,1,0:T(8,128)(2,1)} %bitcast.11, ...), custom_call_target="tpu_custom_call" | custom-call | flops 1207959552 | bytes 7864320 | tf_op jit(solution)/shard_map/finish/pallas_call | solution.py:338
  (116 shorter events, 4.3 us)
Async XLA Ops:
  6.5 168.9 %all-gather.5.cloned.1.call-start = ((), (), s32[]{:S(2)}) async-start(), calls=%async_computation.3 | async-start | bytes 7077888 | tf_op jit(solution)/shard_map/all_gather | solution.py:374
  37.4 27.5 %copy-start.10 = (bf16[1,384,384]{2,1,0:T(8,128)(2,1)S(1)}, bf16[1,384,384]{2,1,0:T(8,128)(2,1)}, u32[]{:S(2)}) copy-start(bf16[1,384,384]{2,1,0:T(8,128)(2,1)} %get-tuple-element.83.refs_0_) | copy-start | bytes 884740
  37.4 172.9 %all-gather.7.cloned.1.call-start = ((), (), s32[]{:S(2)}) async-start(), calls=%async_computation.4 | async-start | bytes 14155776 | tf_op jit(solution)/shard_map/all_gather | solution.py:381
  38.3 15.6 %collective-permute-start.3 = (bf16[1,384,384]{2,1,0:T(8,128)(2,1)S(1)}, bf16[1,384,384]{2,1,0:T(8,128)(2,1)S(1)}, u32[]{:S(2)}, u32[]{:S(2)}) collective-permute-start(bf16[1,384,384]{2,1,0:T(8,128)(2,1)S(1)} %copy-done.22), channel_id=1, source_target_pairs={{0,8},{2,10},{4,12},{6,14},{8,0},{10,2},{12,4},{14,6},{16,24},{18,... | collective-permute-start | bytes 884744 | tf_op jit(solution)/shard_map/ppermute | solution.py:28
  41.3 23.5 %collective-permute-start.4 = (bf16[1,384,384]{2,1,0:T(8,128)(2,1)S(1)}, bf16[1,384,384]{2,1,0:T(8,128)(2,1)S(1)}, u32[]{:S(2)}, u32[]{:S(2)}) collective-permute-start(bf16[1,384,384]{2,1,0:T(8,128)(2,1)S(1)} %copy-done.21), channel_id=1, source_target_pairs={{0,16},{2,18},{4,20},{6,22},{8,24},{10,26},{12,28},{14,30},{16,0},... | collective-permute-start | bytes 884744 | tf_op jit(solution)/shard_map/ppermute | solution.py:28
  43.9 20.9 %collective-permute-start.5 = (bf16[1,384,384]{2,1,0:T(8,128)(2,1)S(1)}, bf16[1,384,384]{2,1,0:T(8,128)(2,1)S(1)}, u32[]{:S(2)}, u32[]{:S(2)}) collective-permute-start(bf16[1,384,384]{2,1,0:T(8,128)(2,1)S(1)} %copy-done.20), channel_id=1, source_target_pairs={{0,24},{2,26},{4,28},{6,30},{8,16},{10,18},{12,20},{14,22},{16,8},... | collective-permute-start | bytes 884744 | tf_op jit(solution)/shard_map/ppermute | solution.py:28
  53.9 21.6 %copy-start.11 = (bf16[1,384,384]{2,1,0:T(8,128)(2,1)}, bf16[1,384,384]{2,1,0:T(8,128)(2,1)S(1)}, u32[]{:S(2)}) copy-start(bf16[1,384,384]{2,1,0:T(8,128)(2,1)S(1)} %collective-permute-done.3.refs_1_) | copy-start | bytes 884740
  65.0 17.0 %copy-start.25 = (bf16[1,384,256]{2,1,0:T(8,128)(2,1)S(1)}, bf16[1,384,256]{2,1,0:T(8,128)(2,1)}, u32[]{:S(2)}) copy-start(bf16[1,384,256]{2,1,0:T(8,128)(2,1)} %get-tuple-element.67) | copy-start | bytes 589828
  65.0 23.9 %copy-start.24 = (bf16[1,384,256]{2,1,0:T(8,128)(2,1)S(1)}, bf16[1,384,256]{2,1,0:T(8,128)(2,1)}, u32[]{:S(2)}) copy-start(bf16[1,384,256]{2,1,0:T(8,128)(2,1)} %get-tuple-element.68) | copy-start | bytes 589828
  65.1 25.0 %copy-start.23 = (bf16[1,384,256]{2,1,0:T(8,128)(2,1)S(1)}, bf16[1,384,256]{2,1,0:T(8,128)(2,1)}, u32[]{:S(2)}) copy-start(bf16[1,384,256]{2,1,0:T(8,128)(2,1)} %get-tuple-element.69) | copy-start | bytes 589828
  65.1 41.0 %copy-start.8 = (bf16[1,384,256]{2,1,0:T(8,128)(2,1)S(1)}, bf16[1,384,256]{2,1,0:T(8,128)(2,1)}, u32[]{:S(2)}) copy-start(bf16[1,384,256]{2,1,0:T(8,128)(2,1)} %get-tuple-element.79) | copy-start | bytes 589828
  65.1 17.0 %collective-permute-start.7 = (bf16[4,384,256]{2,1,0:T(8,128)(2,1)S(1)}, bf16[4,384,256]{2,1,0:T(8,128)(2,1)}, u32[]{:S(2)}, u32[]{:S(2)}) collective-permute-start(bf16[4,384,256]{2,1,0:T(8,128)(2,1)S(1)} %pad_maximum_fusion.refs_4_), channel_id=1, source_target_pairs={{0,4},{2,6},{4,0},{6,2},{8,12},{10,14},{12,8},{14,10},{16,20},{18,... | collective-permute-start | bytes 2359304 | tf_op jit(solution)/shard_map/ppermute | solution.py:28
  75.5 37.3 %collective-permute-start.6 = (bf16[4,384,256]{2,1,0:T(8,128)(2,1)S(1)}, bf16[4,384,256]{2,1,0:T(8,128)(2,1)S(1)}, u32[]{:S(2)}, u32[]{:S(2)}) collective-permute-start(bf16[4,384,256]{2,1,0:T(8,128)(2,1)S(1)} %pad_maximum_fusion.refs_4_), channel_id=1, source_target_pairs={{0,2},{2,0},{4,6},{6,4},{8,10},{10,8},{12,14},{14,12},{16,18},{18,... | collective-permute-start | bytes 2359304 | tf_op jit(solution)/shard_map/ppermute | solution.py:28
  82.1 32.4 %collective-permute-start.8 = (bf16[4,384,256]{2,1,0:T(8,128)(2,1)}, bf16[4,384,256]{2,1,0:T(8,128)(2,1)}, u32[]{:S(2)}, u32[]{:S(2)}) collective-permute-start(bf16[4,384,256]{2,1,0:T(8,128)(2,1)} %collective-permute-done.7.refs_6_), channel_id=1, source_target_pairs={{0,2},{2,0},{4,6},{6,4},{8,10},{10,8},{12,14},{14,12},{16,18},{18,... | collective-permute-start | bytes 2359304 | tf_op jit(solution)/shard_map/ppermute | solution.py:28
  82.1 16.3 %collective-permute-start = (bf16[1,384,256]{2,1,0:T(8,128)(2,1)S(1)}, bf16[1,384,256]{2,1,0:T(8,128)(2,1)S(1)}, u32[]{:S(2)}, u32[]{:S(2)}) collective-permute-start(bf16[1,384,256]{2,1,0:T(8,128)(2,1)S(1)} %copy-done.25), channel_id=1, source_target_pairs={{0,8},{2,10},{4,12},{6,14},{8,0},{10,2},{12,4},{14,6},{16,24},{18,... | collective-permute-start | bytes 589832 | tf_op jit(solution)/shard_map/ppermute | solution.py:28
  89.0 17.1 %collective-permute-start.1 = (bf16[1,384,256]{2,1,0:T(8,128)(2,1)S(1)}, bf16[1,384,256]{2,1,0:T(8,128)(2,1)S(1)}, u32[]{:S(2)}, u32[]{:S(2)}) collective-permute-start(bf16[1,384,256]{2,1,0:T(8,128)(2,1)S(1)} %copy-done.24), channel_id=1, source_target_pairs={{0,16},{2,18},{4,20},{6,22},{8,24},{10,26},{12,28},{14,30},{16,0},... | collective-permute-start | bytes 589832 | tf_op jit(solution)/shard_map/ppermute | solution.py:28
  90.1 16.0 %collective-permute-start.2 = (bf16[1,384,256]{2,1,0:T(8,128)(2,1)S(1)}, bf16[1,384,256]{2,1,0:T(8,128)(2,1)S(1)}, u32[]{:S(2)}, u32[]{:S(2)}) collective-permute-start(bf16[1,384,256]{2,1,0:T(8,128)(2,1)S(1)} %copy-done.23), channel_id=1, source_target_pairs={{0,24},{2,26},{4,28},{6,30},{8,16},{10,18},{12,20},{14,22},{16,8},... | collective-permute-start | bytes 589832 | tf_op jit(solution)/shard_map/ppermute | solution.py:28
  106.2 34.8 %copy-start.14 = (bf16[4,384,256]{2,1,0:T(8,128)(2,1)}, bf16[4,384,256]{2,1,0:T(8,128)(2,1)S(1)}, u32[]{:S(2)}) copy-start(bf16[4,384,256]{2,1,0:T(8,128)(2,1)S(1)} %constant_dynamic-update-slice_fusion.refs_4_) | copy-start | bytes 2359300
  106.2 34.8 %collective-permute-start.13 = (bf16[4,384,256]{2,1,0:T(8,128)(2,1)S(1)}, bf16[4,384,256]{2,1,0:T(8,128)(2,1)S(1)}, u32[]{:S(2)}, u32[]{:S(2)}) collective-permute-start(bf16[4,384,256]{2,1,0:T(8,128)(2,1)S(1)} %constant_dynamic-update-slice_fusion.refs_4_), channel_id=1, source_target_pairs={{0,4},{2,6},{4,0},{6,2},{8,12},{10,14},{12,8},{14,10},{16,20},{18,... | collective-permute-start | bytes 2359304 | tf_op jit(solution)/shard_map/ppermute | solution.py:28
  107.7 16.9 %collective-permute-start.17 = (bf16[1,384,256]{2,1,0:T(8,128)(2,1)}, bf16[1,384,256]{2,1,0:T(8,128)(2,1)S(1)}, u32[]{:S(2)}, u32[]{:S(2)}) collective-permute-start(bf16[1,384,256]{2,1,0:T(8,128)(2,1)} %get-tuple-element.103), channel_id=1, source_target_pairs={{0,8},{2,10},{4,12},{6,14},{8,0},{10,2},{12,4},{14,6},{16,24},{18,... | collective-permute-start | bytes 589832 | tf_op jit(solution)/shard_map/ppermute | solution.py:28
  111.8 17.3 %collective-permute-start.18 = (bf16[1,384,256]{2,1,0:T(8,128)(2,1)}, bf16[1,384,256]{2,1,0:T(8,128)(2,1)S(1)}, u32[]{:S(2)}, u32[]{:S(2)}) collective-permute-start(bf16[1,384,256]{2,1,0:T(8,128)(2,1)} %get-tuple-element.104), channel_id=1, source_target_pairs={{0,16},{2,18},{4,20},{6,22},{8,24},{10,26},{12,28},{14,30},{16,0},... | collective-permute-start | bytes 589832 | tf_op jit(solution)/shard_map/ppermute | solution.py:28
  112.9 17.0 %copy-start.31 = (bf16[1,384,128]{2,1,0:T(8,128)(2,1)S(1)}, bf16[1,384,128]{2,1,0:T(8,128)(2,1)}, u32[]{:S(2)}) copy-start(bf16[1,384,128]{2,1,0:T(8,128)(2,1)} %get-tuple-element.93) | copy-start | bytes 294916
  112.9 20.7 %copy-start.30 = (bf16[1,384,128]{2,1,0:T(8,128)(2,1)S(1)}, bf16[1,384,128]{2,1,0:T(8,128)(2,1)}, u32[]{:S(2)}) copy-start(bf16[1,384,128]{2,1,0:T(8,128)(2,1)} %get-tuple-element.94) | copy-start | bytes 294916
  112.9 22.0 %copy-start.29 = (bf16[1,384,128]{2,1,0:T(8,128)(2,1)S(1)}, bf16[1,384,128]{2,1,0:T(8,128)(2,1)}, u32[]{:S(2)}) copy-start(bf16[1,384,128]{2,1,0:T(8,128)(2,1)} %get-tuple-element.92) | copy-start | bytes 294916
  112.9 28.6 %copy-start.28 = (bf16[1,384,128]{2,1,0:T(8,128)(2,1)S(1)}, bf16[1,384,128]{2,1,0:T(8,128)(2,1)}, u32[]{:S(2)}) copy-start(bf16[1,384,128]{2,1,0:T(8,128)(2,1)} %get-tuple-element.111) | copy-start | bytes 294916
  112.9 29.3 %copy-start.27 = (bf16[1,384,128]{2,1,0:T(8,128)(2,1)S(1)}, bf16[1,384,128]{2,1,0:T(8,128)(2,1)}, u32[]{:S(2)}) copy-start(bf16[1,384,128]{2,1,0:T(8,128)(2,1)} %get-tuple-element.112) | copy-start | bytes 294916
  112.9 34.5 %copy-start.26 = (bf16[1,384,128]{2,1,0:T(8,128)(2,1)S(1)}, bf16[1,384,128]{2,1,0:T(8,128)(2,1)}, u32[]{:S(2)}) copy-start(bf16[1,384,128]{2,1,0:T(8,128)(2,1)} %get-tuple-element.113) | copy-start | bytes 294916
  112.9 16.3 %collective-permute-start.19 = (bf16[1,384,256]{2,1,0:T(8,128)(2,1)}, bf16[1,384,256]{2,1,0:T(8,128)(2,1)S(1)}, u32[]{:S(2)}, u32[]{:S(2)}) collective-permute-start(bf16[1,384,256]{2,1,0:T(8,128)(2,1)} %get-tuple-element.105), channel_id=1, source_target_pairs={{0,24},{2,26},{4,28},{6,30},{8,16},{10,18},{12,20},{14,22},{16,8},... | collective-permute-start | bytes 589832 | tf_op jit(solution)/shard_map/ppermute | solution.py:28
  129.3 36.0 %copy-start.15 = (bf16[4,384,256]{2,1,0:T(8,128)(2,1)}, bf16[4,384,256]{2,1,0:T(8,128)(2,1)S(1)}, u32[]{:S(2)}) copy-start(bf16[4,384,256]{2,1,0:T(8,128)(2,1)S(1)} %constant_dynamic-update-slice_fusion.4.refs_4_) | copy-start | bytes 2359300
  129.3 24.7 %collective-permute-start.24 = (bf16[4,384,256]{2,1,0:T(8,128)(2,1)S(1)}, bf16[4,384,256]{2,1,0:T(8,128)(2,1)S(1)}, u32[]{:S(2)}, u32[]{:S(2)}) collective-permute-start(bf16[4,384,256]{2,1,0:T(8,128)(2,1)S(1)} %constant_dynamic-update-slice_fusion.4.refs_4_), channel_id=1, source_target_pairs={{0,4},{2,6},{4,0},{6,2},{8,12},{10,14},{12,8},{14,10},{16,20},{18,... | collective-permute-start | bytes 2359304 | tf_op jit(solution)/shard_map/ppermute | solution.py:28
  129.9 9.1 %collective-permute-start.10 = (bf16[1,384,128]{2,1,0:T(8,128)(2,1)S(1)}, bf16[1,384,128]{2,1,0:T(8,128)(2,1)S(1)}, u32[]{:S(2)}, u32[]{:S(2)}) collective-permute-start(bf16[1,384,128]{2,1,0:T(8,128)(2,1)S(1)} %copy-done.31), channel_id=1, source_target_pairs={{0,16},{2,18},{4,20},{6,22},{8,24},{10,26},{12,28},{14,30},{16,0},... | collective-permute-start | bytes 294920 | tf_op jit(solution)/shard_map/ppermute | solution.py:28
  133.5 6.8 %collective-permute-start.11 = (bf16[1,384,128]{2,1,0:T(8,128)(2,1)S(1)}, bf16[1,384,128]{2,1,0:T(8,128)(2,1)S(1)}, u32[]{:S(2)}, u32[]{:S(2)}) collective-permute-start(bf16[1,384,128]{2,1,0:T(8,128)(2,1)S(1)} %copy-done.30), channel_id=1, source_target_pairs={{0,24},{2,26},{4,28},{6,30},{8,16},{10,18},{12,20},{14,22},{16,8},... | collective-permute-start | bytes 294920 | tf_op jit(solution)/shard_map/ppermute | solution.py:28
  134.9 6.1 %collective-permute-start.9 = (bf16[1,384,128]{2,1,0:T(8,128)(2,1)S(1)}, bf16[1,384,128]{2,1,0:T(8,128)(2,1)S(1)}, u32[]{:S(2)}, u32[]{:S(2)}) collective-permute-start(bf16[1,384,128]{2,1,0:T(8,128)(2,1)S(1)} %copy-done.29), channel_id=1, source_target_pairs={{0,8},{2,10},{4,12},{6,14},{8,0},{10,2},{12,4},{14,6},{16,24},{18,... | collective-permute-start | bytes 294920 | tf_op jit(solution)/shard_map/ppermute | solution.py:28
  139.0 16.4 %copy-start.32 = (bf16[1,384,128]{2,1,0:T(8,128)(2,1)}, bf16[1,384,128]{2,1,0:T(8,128)(2,1)S(1)}, u32[]{:S(2)}) copy-start(bf16[1,384,128]{2,1,0:T(8,128)(2,1)S(1)} %collective-permute-done.10.refs_2_) | copy-start | bytes 294916
  141.0 13.5 %collective-permute-start.12 = (bf16[4,384,256]{2,1,0:T(8,128)(2,1)S(1)}, bf16[4,384,256]{2,1,0:T(8,128)(2,1)S(1)}, u32[]{:S(2)}, u32[]{:S(2)}) collective-permute-start(bf16[4,384,256]{2,1,0:T(8,128)(2,1)S(1)} %constant_dynamic-update-slice_fusion.refs_4_), channel_id=1, source_target_pairs={{0,2},{2,0},{4,6},{6,4},{8,10},{10,8},{12,14},{14,12},{16,18},{18,... | collective-permute-start | bytes 2359304 | tf_op jit(solution)/shard_map/ppermute | solution.py:28
  141.0 14.3 %collective-permute-start.14 = (bf16[4,384,256]{2,1,0:T(8,128)(2,1)S(1)}, bf16[4,384,256]{2,1,0:T(8,128)(2,1)}, u32[]{:S(2)}, u32[]{:S(2)}) collective-permute-start(bf16[4,384,256]{2,1,0:T(8,128)(2,1)S(1)} %collective-permute-done.13.refs_6_), channel_id=1, source_target_pairs={{0,2},{2,0},{4,6},{6,4},{8,10},{10,8},{12,14},{14,12},{16,18},{18,... | collective-permute-start | bytes 2359304 | tf_op jit(solution)/shard_map/ppermute | solution.py:28
  141.5 5.9 %collective-permute-start.20 = (bf16[1,384,128]{2,1,0:T(8,128)(2,1)S(1)}, bf16[1,384,128]{2,1,0:T(8,128)(2,1)S(1)}, u32[]{:S(2)}, u32[]{:S(2)}) collective-permute-start(bf16[1,384,128]{2,1,0:T(8,128)(2,1)S(1)} %copy-done.28), channel_id=1, source_target_pairs={{0,8},{2,10},{4,12},{6,14},{8,0},{10,2},{12,4},{14,6},{16,24},{18,... | collective-permute-start | bytes 294920 | tf_op jit(solution)/shard_map/ppermute | solution.py:28
  142.2 9.5 %collective-permute-start.21 = (bf16[1,384,128]{2,1,0:T(8,128)(2,1)S(1)}, bf16[1,384,128]{2,1,0:T(8,128)(2,1)S(1)}, u32[]{:S(2)}, u32[]{:S(2)}) collective-permute-start(bf16[1,384,128]{2,1,0:T(8,128)(2,1)S(1)} %copy-done.27), channel_id=1, source_target_pairs={{0,16},{2,18},{4,20},{6,22},{8,24},{10,26},{12,28},{14,30},{16,0},... | collective-permute-start | bytes 294920 | tf_op jit(solution)/shard_map/ppermute | solution.py:28
  147.4 17.9 %copy-start.35 = (bf16[1,384,128]{2,1,0:T(8,128)(2,1)}, bf16[1,384,128]{2,1,0:T(8,128)(2,1)S(1)}, u32[]{:S(2)}) copy-start(bf16[1,384,128]{2,1,0:T(8,128)(2,1)S(1)} %collective-permute-done.20.refs_1_) | copy-start | bytes 294916
  147.4 6.5 %collective-permute-start.22 = (bf16[1,384,128]{2,1,0:T(8,128)(2,1)S(1)}, bf16[1,384,128]{2,1,0:T(8,128)(2,1)S(1)}, u32[]{:S(2)}, u32[]{:S(2)}) collective-permute-start(bf16[1,384,128]{2,1,0:T(8,128)(2,1)S(1)} %copy-done.26), channel_id=1, source_target_pairs={{0,24},{2,26},{4,28},{6,30},{8,16},{10,18},{12,20},{14,22},{16,8},... | collective-permute-start | bytes 294920 | tf_op jit(solution)/shard_map/ppermute | solution.py:28
  154.0 11.3 %collective-permute-start.23 = (bf16[4,384,256]{2,1,0:T(8,128)(2,1)S(1)}, bf16[4,384,256]{2,1,0:T(8,128)(2,1)}, u32[]{:S(2)}, u32[]{:S(2)}) collective-permute-start(bf16[4,384,256]{2,1,0:T(8,128)(2,1)S(1)} %constant_dynamic-update-slice_fusion.4.refs_4_), channel_id=1, source_target_pairs={{0,2},{2,0},{4,6},{6,4},{8,10},{10,8},{12,14},{14,12},{16,18},{18,... | collective-permute-start | bytes 2359304 | tf_op jit(solution)/shard_map/ppermute | solution.py:28
  154.0 11.3 %collective-permute-start.25 = (bf16[4,384,256]{2,1,0:T(8,128)(2,1)S(1)}, bf16[4,384,256]{2,1,0:T(8,128)(2,1)}, u32[]{:S(2)}, u32[]{:S(2)}) collective-permute-start(bf16[4,384,256]{2,1,0:T(8,128)(2,1)S(1)} %collective-permute-done.24.refs_6_), channel_id=1, source_target_pairs={{0,2},{2,0},{4,6},{6,4},{8,10},{10,8},{12,14},{14,12},{16,18},{18,... | collective-permute-start | bytes 2359304 | tf_op jit(solution)/shard_map/ppermute | solution.py:28
  189.3 21.0 %copy-start.1 = (bf16[4,384,128]{2,1,0:T(8,128)(2,1)}, bf16[4,384,128]{2,1,0:T(8,128)(2,1)S(1)}, u32[]{:S(2)}) copy-start(bf16[4,384,128]{2,1,0:T(8,128)(2,1)S(1)} %all_to_all.15.refs_1_) | copy-start | bytes 1179652
  189.3 13.2 %all-to-all-start = ((bf16[4,384,128]{2,1,0:T(8,128)(2,1)}), bf16[4,384,128]{2,1,0:T(8,128)(2,1)S(1)}, u32[]{:S(2)}, u32[]{:S(2)}) async-start(bf16[4,384,128]{2,1,0:T(8,128)(2,1)} %attend.3), calls=%async_computation | async-start | bytes 786432 | tf_op jit(solution)/shard_map/all_to_all | solution.py:415
  192.8 14.6 %collective-permute-start.16 = (bf16[4,384,128]{2,1,0:T(8,128)(2,1)S(1)}, bf16[4,384,128]{2,1,0:T(8,128)(2,1)S(1)}, u32[]{:S(2)}, u32[]{:S(2)}) collective-permute-start(bf16[4,384,128]{2,1,0:T(8,128)(2,1)S(1)} %all_to_all.15.refs_1_), channel_id=1, source_target_pairs={{0,1},{1,0},{2,3},{3,2},{4,5},{5,4},{6,7},{7,6},{8,9},{9,8},{10,11... | collective-permute-start | bytes 1179656 | tf_op jit(solution)/shard_map/ppermute | solution.py:28
  202.5 7.8 %collective-permute-start.15 = (bf16[4,384,128]{2,1,0:T(8,128)(2,1)S(1)}, bf16[4,384,128]{2,1,0:T(8,128)(2,1)S(1)}, u32[]{:S(2)}, u32[]{:S(2)}) collective-permute-start(bf16[4,384,128]{2,1,0:T(8,128)(2,1)S(1)} %all-to-all-done.refs_0_), channel_id=1, source_target_pairs={{0,1},{1,0},{2,3},{3,2},{4,5},{5,4},{6,7},{7,6},{8,9},{9,8},{10,11... | collective-permute-start | bytes 1179656 | tf_op jit(solution)/shard_map/ppermute | solution.py:28
  203.9 13.9 %all-to-all-start.2 = ((bf16[4,384,128]{2,1,0:T(8,128)(2,1)}), bf16[4,384,128]{2,1,0:T(8,128)(2,1)S(1)}, u32[]{:S(2)}, u32[]{:S(2)}) async-start(bf16[4,384,128]{2,1,0:T(8,128)(2,1)} %attend.5), calls=%async_computation.2 | async-start | bytes 786432 | tf_op jit(solution)/shard_map/all_to_all | solution.py:415
  217.9 7.8 %collective-permute-start.26 = (bf16[4,384,128]{2,1,0:T(8,128)(2,1)S(1)}, bf16[4,384,128]{2,1,0:T(8,128)(2,1)S(1)}, u32[]{:S(2)}, u32[]{:S(2)}) collective-permute-start(bf16[4,384,128]{2,1,0:T(8,128)(2,1)S(1)} %all-to-all-done.2.refs_1_), channel_id=1, source_target_pairs={{0,1},{1,0},{2,3},{3,2},{4,5},{5,4},{6,7},{7,6},{8,9},{9,8},{10,11... | collective-permute-start | bytes 1179656 | tf_op jit(solution)/shard_map/ppermute | solution.py:28
  (21 other events, 163.3 us)
Sparse Core Ops, SparseCore 0:
  37.5 65.3 all-gather.4
  175.6 23.9 all-gather.6

commit v3 on v2

--- a/solution.py
+++ b/solution.py
@@ -162,10 +162,11 @@
     return blocks, found[len(sets) * groups :]
 
 
-def attend_body(place_ref, *refs, groups, low_lane, key_room, query_rows, key_cols):
-    query_refs, sources = refs[:groups], refs[groups:-5]
-    out_ref, keys, values, queries, results = refs[-5:]
-    rows, size = out_ref.shape[1:]
+def attend_body(place_ref, *refs, groups, ordered, low_lane, key_room, query_rows, key_cols):
+    outs = 1 if ordered else groups
+    query_refs, sources, out_refs = refs[:groups], refs[groups : -4 - outs], refs[-4 - outs : -4]
+    keys, values, queries, results = refs[-4:]
+    rows, size = out_refs[0].shape[1:]
     plane = place_ref[0]
     blocks = [(source, k) for source in sources for k in range(groups)]
     piece = 128 if rows % 128 == 0 else rows
@@ -236,12 +237,12 @@
         for part in range(rows // piece):
             here = pl.ds(pl.multiple_of(starts[k] + part * piece, 16), piece)
             live = line + part * piece < mine[k]
-            out_ref[lax.bitwise_xor(plane, k), part * piece : (part + 1) * piece, :] = jnp.where(
-                live, results[here, :].astype(f32), 0.0
-            ).astype(bf16)
-
-
-def attend(place, queries, low_lane, keyvals, shards):
+            kept = jnp.where(live, results[here, :].astype(f32), 0.0).astype(bf16)
+            block = lax.bitwise_xor(plane, k) if ordered else 0
+            out_refs[0 if ordered else k][block, part * piece : (part + 1) * piece, :] = kept
+
+
+def attend(place, queries, low_lane, keyvals, shards, ordered):
     groups = len(queries)
     rows = keyvals[0].shape[1]
     size = keyvals[0].shape[2] // 2
@@ -250,10 +251,12 @@
     query_rows = 256
     query_room = -(-groups * rows // query_rows) * query_rows + rows
     query_block = (1,) + queries[0].shape[1:]
+    outs, wide = (1, groups) if ordered else (groups, 1)
     return pl.pallas_call(
         functools.partial(
             attend_body,
             groups=groups,
+            ordered=ordered,
             low_lane=low_lane,
             key_room=key_room,
             query_rows=query_rows,
@@ -264,7 +267,7 @@
             grid=(1,),
             in_specs=[pl.BlockSpec(query_block, lambda i, place: (0, 0, 0))] * groups
             + [pl.BlockSpec(keyvals[0].shape, lambda i, place: (0, 0, 0))] * len(keyvals),
-            out_specs=pl.BlockSpec((groups, rows, size), lambda i, place: (0, 0, 0)),
+            out_specs=[pl.BlockSpec((wide, rows, size), lambda i, place: (0, 0, 0))] * outs,
             scratch_shapes=[
                 pltpu.VMEM((key_room + rows, size), bf16),
                 pltpu.VMEM((key_room + rows, 2 * size), bf16),
@@ -272,7 +275,7 @@
                 pltpu.VMEM((query_room, size), bf16),
             ],
         ),
-        out_shape=jax.ShapeDtypeStruct((groups, rows, size), bf16),
+        out_shape=[jax.ShapeDtypeStruct((wide, rows, size), bf16)] * outs,
         compiler_params=params,
         cost_estimate=cost(
             8 * groups * rows // 2 * running * size,
@@ -283,16 +286,21 @@
     )(place, *queries, *keyvals)
 
 
-def finish_body(place_ref, *refs, chunks, others, has_sum, last):
+def finish_body(place_ref, *refs, chunks, others, has_sum, last, ordered):
     refs = list(refs)
+    wide_ref = refs.pop()
     out_ref = refs.pop()
     total = refs.pop(0)[...] if has_sum else None
     for m in range(1 + others):
         attended_refs, weight_ref = refs[:chunks], refs[chunks]
         refs = refs[chunks + 1 :]
-        wide = jnp.concatenate(
-            [ref[g] for ref in attended_refs for g in range(ref.shape[0])], axis=-1
-        )
+        for i, ref in enumerate(attended_refs):
+            groups, _, size = ref.shape
+            for g in range(groups):
+                head = i * groups + (g if ordered else lax.bitwise_xor(place_ref[0], g))
+                start = head * size if ordered else pl.multiple_of(head * size, size)
+                wide_ref[:, pl.ds(start, size)] = ref[g]
+        wide = wide_ref[...]
         weight = weight_ref[0, 0] if m else weight_ref[...]
         term = jnp.dot(wide, weight, preferred_element_type=f32)
         total = term if total is None else total + term
@@ -303,7 +311,7 @@
         out_ref[...] = total
 
 
-def finish(place, total, attended, w_out, other_weights, back, first_chunk):
+def finish(place, total, attended, w_out, other_weights, back, first_chunk, ordered):
     groups, rows, size = attended[0][0].shape
     split, head_shards, _, half = other_weights.shape
     chunks = len(attended)
@@ -342,12 +350,14 @@
             others=head_shards - 1,
             has_sum=total is not None,
             last=last,
+            ordered=ordered,
         ),
         grid_spec=pltpu.PrefetchScalarGridSpec(
             num_scalar_prefetch=1,
             grid=(split,),
             in_specs=specs,
             out_specs=pl.BlockSpec((rows, half), mine),
+            scratch_shapes=[pltpu.VMEM((rows, depth), bf16)],
         ),
         out_shape=jax.ShapeDtypeStruct((rows, out_width), bf16 if last else f32),
         compiler_params=params,
@@ -422,50 +432,67 @@
     weights = jnp.transpose(w_qkv, (1, 0, 2))
     gains = jnp.transpose(qk_gain, (1, 0, 2))
 
-    plan = [[((1, 2, 0), 0)]]
-    plan += [[((1, 2), chunk)] for chunk in range(1, chunks)]
+    def later(values, *earlier):
+        return jnp.maximum(chain(values, *earlier), 0)
+
+    def first(blocks):
+        return blocks[min(1, groups - 1)]
+
+    def send(blocks, *earlier):
+        return swap(list(chain(tuple(blocks), *earlier)) if earlier else blocks)
+
+    operands = (survive, tokens, norm_gain)
+    sets = [((1, 2, 0), 0)]
+    (blocks,), rest = project(place, None, weights, gains, sets, groups, operands)
+    normed, chosen, back, count = rest
+    arrived = [swap(blocks)]
+    fetched = fetch_weights(chain(w_out, later(count)), me, side, head_shards)
+
+    rest, asked = range(1, chunks), []
     if chunks > 1:
-        plan[1] += [((0,), chunk) for chunk in range(1, chunks)]
-    arrived, stacks, later, fetched, gate = [], [], [], None, None
-    for i, sets in enumerate(plan):
-        if i == 0:
-            operands = (survive, tokens, norm_gain)
-            blocks, rest = project(place, None, weights, gains, sets, groups, operands)
-            normed, chosen, back, count = rest
-        else:
-            source = chain(normed, stacks[i - 2]) if i > 1 else normed
-            prepared = (count, source, chosen)
-            blocks, _ = project(place, prepared, weights, gains, sets, groups)
-            stacks.append(stack(list(chain(tuple(arrived[i - 1]), blocks[0][0]))))
-        if i == min(1, chunks - 1):
-            later = blocks[1:]
-            fetched = fetch_weights(chain(w_out, blocks[0][0]), me, side, head_shards)
-        arrived.append(swap(blocks[0]))
-        gate = blocks[0][0]
-
-    attended = []
+        prepared = (count, chain(normed, first(arrived[0])), chosen)
+        sets = [((1, 2), chunk) for chunk in rest]
+        made, _ = project(place, prepared, weights, gains, sets, groups)
+        stacks = [stack(list(chain(tuple(arrived[0]), made[0][0])))]
+        arrived.append(send(made[0]))
+        for blocks in made[1:]:
+            arrived.append(send(blocks, first(arrived[-1])))
+        hop = flip(stacks[0], "seq", ring // 2) if ring > 1 else stacks[0]
+        stacks.append(stack(arrived[1]))
+        ready = later(count, hop, stacks[1])
+        sets = [((0,), chunk) for chunk in rest]
+        made, _ = project(place, (ready, normed, chosen), weights, gains, sets, groups)
+        gate = made[0][0]
+        stacks += [stack(blocks) for blocks in arrived[2:]]
+        for blocks in made:
+            asked.append(send(blocks, first(asked[-1]) if asked else stacks[-1]))
+    else:
+        gate, stacks = None, [stack(arrived[0])]
+
+    attended, returned = [], []
     query, low_lane = arrived[0], 2 * size
     for chunk in range(chunks):
-        if chunk == chunks - 1:
-            stacks.append(stack(list(chain(tuple(arrived[-1]), *attended[:1]))))
-        upcoming = None
-        if chunk < chunks - 1:
-            upcoming = swap(list(chain(tuple(later[chunk]), stacks[min(chunk + 1, len(stacks) - 1)])))
+        final = chunk == chunks - 1
         keyvals = everywhere(stacks[chunk], gate)
-        before = (stacks[-1],) + tuple(attended[-1:])
-        query = [chain(query[0], *before)] + list(query[1:])
-        attended.append(attend(place, query, low_lane, keyvals, shards))
-        query, low_lane = upcoming, 0
-        gate = tuple(upcoming[1:]) if upcoming else None
-    out_width = w_out.shape[1] // head_shards
-    other_weights = share_weights(chain(fetched, attended[-1]), out_width, head_shards)
-    attended = [send_back(found) for found in attended]
+        before = (stacks[-1],) + tuple(attended[-1:]) + tuple(returned[:1] if final else [])
+        ready = later(place, *query[1:], *before)
+        found = attend(ready, query, low_lane, keyvals, shards, not final)
+        attended.append(found[0])
+        if chunk == max(chunks - 2, 0):
+            out_width = w_out.shape[1] // head_shards
+            other_weights = share_weights(chain(fetched, found[0]), out_width, head_shards)
+        if final:
+            returned.append(jnp.concatenate(swap(found)))
+        else:
+            returned.append(send_back(found[0]))
+            query, low_lane = asked[chunk], 0
+            gate = tuple(query)
     total = None
     if chunks > 1:
-        sooner = [across(found) for found in attended[:-1]]
-        total = finish(place, None, sooner, w_out, other_weights, None, 0)
-    final = across(attended[-1] if total is None else chain(attended[-1], total))
-    return finish(place, total, [final], w_out, other_weights, back, chunks - 1)
+        sooner = [across(found) for found in returned[:-1]]
+        total = finish(place, None, sooner, w_out, other_weights, None, 0, True)
+    last = across(returned[-1] if total is None else chain(returned[-1], total))
+    return finish(place, total, [last], w_out, other_weights, back, chunks - 1, False)
 
 
 def solution(mesh):

time: 243 us -> 226 us (0.930)
  blocking collectives: 12.8 us -> 0 us
  waiting for transfers between devices: 77.7 us -> 72.5 us
  other arithmetic: 0.68 us -> 3.22 us
    all_to_all x1 -> x0, blocking collectives: 12.8 us -> none  [send_back(): lax.all_to_all(blocks, 'seq', split_axis=0, concat_axis=0, axis_index_gro...]
    ppermute x27 -> x30, waiting for transfers between devices: 69.5 us -> 62.4 us  [flip(): return lax.ppermute(values, axis, [(i, i ^ mask) for i in range(size)])]
    ppermute x27 -> x30, starting transfers between devices: 40.7 us -> 39.2 us  [flip(): return lax.ppermute(values, axis, [(i, i ^ mask) for i in range(size)])]
  transfers between devices with their start and end apart: 31 -> 34, of which waited for: 15 -> 13; matrix products, arithmetic and copies ran while one was open for 0% -> 2% of each run, Pallas kernels for 19% -> 30%
where the time goes in v3:
time: 226 us; the launch traced here: 224 us
  Pallas kernels  79.6 us (35%)
  waiting for transfers between devices  72.5 us (32%)
  starting transfers between devices  46.9 us (21%)
  between operations  14.5 us (6%)
  local copies, waits for them, and re-layouts  6.98 us (3%)
  other arithmetic  3.22 us (1%)
    ppermute x30, waiting for transfers between devices, flip(): return lax.ppermute(values, axis, [(i, i ^ mask) for i in range(size)])  62.4 us
    ppermute x30, starting transfers between devices, flip(): return lax.ppermute(values, axis, [(i, i ^ mask) for i in range(size)])  39.2 us
    pallas_call x3, Pallas kernels, project(): pl.pallas_call(functools.partial(project_body, steps=steps, groups=groups...  36 us
    pallas_call x3, Pallas kernels, attend(): pl.pallas_call(functools.partial(attend_body, groups=groups, ordered=orde...  30.1 us
    pallas_call x2, Pallas kernels, finish(): pl.pallas_call(functools.partial(finish_body, chunks=chunks, others=head_...  13.5 us
    all_to_all x2, waiting for transfers between devices, send_back(): lax.all_to_all(blocks, 'seq', split_axis=0, concat_axis=0, axis_index_gro...  10.1 us
    all_to_all x2, starting transfers between devices, send_back(): lax.all_to_all(blocks, 'seq', split_axis=0, concat_axis=0, axis_index_gro...  7.67 us
  transfers between devices with their start and end apart: 34, of which 13 were waited for; matrix products, arithmetic and copies ran while one was open for 2% of the time, Pallas kernels for 30%

profile of v3, /device:TPU:0, one launch (start us, length us, event | category | flops | bytes accessed | tf_op | source)
XLA Modules:
  0.0 223.7 jit_solution(4585442030391096683)
XLA Ops:
  6.5 3.2 %constant_dynamic-slice_fusion = bf16[1536,768]{1,0:T(8,128)(2,1)} fusion(bf16[1536,3072]{1,0:T(8,128)(2,1)} %refs_2_.5, s32[]{:T(128)S(6)} %select_n.21), kind=kLoop, calls=%fused_computation.14 | loop fusion | bytes 4718596 | tf_op jit(solution)/shard_map/dynamic_slice | solution.py:384
  10.4 13.8 %project.3 = (bf16[1,384,384]{2,1,0:T(8,128)(2,1)}, bf16[1,384,384]{2,1,0:T(8,128)(2,1)}, bf16[1,384,384]{2,1,0:T(8,128)(2,1)}, bf16[1,384,384]{2,1,0:T(8,128)(2...) custom-call(s32[3]{0:T(128)} %pad_add_fusion.place_ref, ...), custom_call_target="tpu_custom_call" | custom-call | flops 3623878656 | bytes 11796480 | tf_op jit(solution)/shard_map/project/pallas_call | solution.py:140
  24.3 3.1 %collective-permute-start = (bf16[1,384,384]{2,1,0:T(8,128)(2,1)}, bf16[1,384,384]{2,1,0:T(8,128)(2,1)S(1)}, u32[]{:S(2)}, u32[]{:S(2)}) collective-permute-start(bf16[1,384,384]{2,1,0:T(8,128)(2,1)} %get-tuple-element.62), channel_id=1, source_target_pairs={{0,8},{2,10},{4,12},{6,14},{8,0},{10,2},{12,4},{14,6},{16,24},{18,... | collective-permute-start | bytes 884744 | tf_op jit(solution)/shard_map/ppermute | solution.py:28
  27.4 2.6 %collective-permute-start.1 = (bf16[1,384,384]{2,1,0:T(8,128)(2,1)}, bf16[1,384,384]{2,1,0:T(8,128)(2,1)S(1)}, u32[]{:S(2)}, u32[]{:S(2)}) collective-permute-start(bf16[1,384,384]{2,1,0:T(8,128)(2,1)} %get-tuple-element.63), channel_id=1, source_target_pairs={{0,16},{2,18},{4,20},{6,22},{8,24},{10,26},{12,28},{14,30},{16,0},... | collective-permute-start | bytes 884744 | tf_op jit(solution)/shard_map/ppermute | solution.py:28
  30.0 10.1 %collective-permute-done.refs_1_ = bf16[1,384,384]{2,1,0:T(8,128)(2,1)S(1)} collective-permute-done((bf16[1,384,384]{2,1,0:T(8,128)(2,1)}, bf16[1,384,384]{2,1,0:T(8,128)(2,1)S(1)}, u32[]{:S(2)}, u32[]{:S(2)}) %collective-permute-start) | collective-permute-done | bytes 294944 | tf_op jit(solution)/shard_map/ppermute | solution.py:28
  40.1 13.3 %project.4 = (bf16[1,384,256]{2,1,0:T(8,128)(2,1)}, bf16[1,384,256]{2,1,0:T(8,128)(2,1)}, bf16[1,384,256]{2,1,0:T(8,128)(2,1)}, bf16[1,384,256]{2,1,0:T(8,128)(2...) custom-call(s32[3]{0:T(128)} %pad_add_fusion.place_ref, ...), custom_call_target="tpu_custom_call" | custom-call | flops 4831838208 | bytes 14942208 | tf_op jit(solution)/shard_map/project/pallas_call | solution.py:140
  53.7 1.8 collective-permute-start.7
  55.5 2.8 %collective-permute-start.3 = (bf16[1,384,256]{2,1,0:T(8,128)(2,1)S(1)}, bf16[1,384,256]{2,1,0:T(8,128)(2,1)S(1)}, u32[]{:S(2)}, u32[]{:S(2)}) collective-permute-start(bf16[1,384,256]{2,1,0:T(8,128)(2,1)S(1)} %copy-done.22), channel_id=1, source_target_pairs={{0,8},{2,10},{4,12},{6,14},{8,0},{10,2},{12,4},{14,6},{16,24},{18,... | collective-permute-start | bytes 589832 | tf_op jit(solution)/shard_map/ppermute | solution.py:28
  58.3 1.1 collective-permute-start.8
  59.4 1.5 collective-permute-start.9
  60.9 3.6 %collective-permute-done.3 = bf16[1,384,256]{2,1,0:T(8,128)(2,1)S(1)} collective-permute-done((bf16[1,384,256]{2,1,0:T(8,128)(2,1)S(1)}, bf16[1,384,256]{2,1,0:T(8,128)(2,1)S(1)}, u32[]{:S(2)}, u32[]{:S(2)}) %collective-permute-start.3) | collective-permute-done | bytes 196640 | tf_op jit(solution)/shard_map/ppermute | solution.py:28
  64.5 10.4 %collective-permute-done.8 = bf16[1,384,256]{2,1,0:T(8,128)(2,1)S(1)} collective-permute-done((bf16[1,384,256]{2,1,0:T(8,128)(2,1)S(1)}, bf16[1,384,256]{2,1,0:T(8,128)(2,1)S(1)}, u32[]{:S(2)}, u32[]{:S(2)}) %collective-permute-start.8) | collective-permute-done | bytes 196640 | tf_op jit(solution)/shard_map/ppermute | solution.py:28
  75.5 2.7 %collective-permute-start.4 = (bf16[1,384,256]{2,1,0:T(8,128)(2,1)}, bf16[1,384,256]{2,1,0:T(8,128)(2,1)S(1)}, u32[]{:S(2)}, u32[]{:S(2)}) collective-permute-start(bf16[1,384,256]{2,1,0:T(8,128)(2,1)} %get-tuple-element.75), channel_id=1, source_target_pairs={{0,8},{2,10},{4,12},{6,14},{8,0},{10,2},{12,4},{14,6},{16,24},{18,... | collective-permute-start | bytes 589832 | tf_op jit(solution)/shard_map/ppermute | solution.py:28
  78.2 1.0 collective-permute-start.5
  79.2 1.4 collective-permute-start.6
  80.6 0.9 copy-done.16
  82.2 8.9 %project.5 = (bf16[1,384,128]{2,1,0:T(8,128)(2,1)}, bf16[1,384,128]{2,1,0:T(8,128)(2,1)}, bf16[1,384,128]{2,1,0:T(8,128)(2,1)}, bf16[1,384,128]{2,1,0:T(8,128)(2...) custom-call(s32[3]{0:T(128)} %pad_add_fusion.place_ref, ...), custom_call_target="tpu_custom_call" | custom-call | flops 2415919104 | bytes 8650752 | tf_op jit(solution)/shard_map/project/pallas_call | solution.py:140
  91.7 2.5 %collective-permute-done.5 = bf16[1,384,256]{2,1,0:T(8,128)(2,1)S(1)} collective-permute-done((bf16[1,384,256]{2,1,0:T(8,128)(2,1)}, bf16[1,384,256]{2,1,0:T(8,128)(2,1)S(1)}, u32[]{:S(2)}, u32[]{:S(2)}) %collective-permute-start.5) | collective-permute-done | bytes 196640 | tf_op jit(solution)/shard_map/ppermute | solution.py:28
  94.2 2.7 %collective-permute-start.12 = (bf16[1,384,128]{2,1,0:T(8,128)(2,1)}, bf16[1,384,128]{2,1,0:T(8,128)(2,1)S(1)}, u32[]{:S(2)}, u32[]{:S(2)}) collective-permute-start(bf16[1,384,128]{2,1,0:T(8,128)(2,1)} %get-tuple-element.94), channel_id=1, source_target_pairs={{0,8},{2,10},{4,12},{6,14},{8,0},{10,2},{12,4},{14,6},{16,24},{18,... | collective-permute-start | bytes 294920 | tf_op jit(solution)/shard_map/ppermute | solution.py:28
  96.9 1.6 collective-permute-start.13
  98.5 2.3 %collective-permute-done.12.refs_1_ = bf16[1,384,128]{2,1,0:T(8,128)(2,1)S(1)} collective-permute-done((bf16[1,384,128]{2,1,0:T(8,128)(2,1)}, bf16[1,384,128]{2,1,0:T(8,128)(2,1)S(1)}, u32[]{:S(2)}, u32[]{:S(2)}) %collective-permute-start.12) | collective-permute-done | bytes 98336 | tf_op jit(solution)/shard_map/ppermute | solution.py:28
  100.8 2.4 %collective-permute-start.14 = (bf16[1,384,128]{2,1,0:T(8,128)(2,1)}, bf16[1,384,128]{2,1,0:T(8,128)(2,1)S(1)}, u32[]{:S(2)}, u32[]{:S(2)}) collective-permute-start(bf16[1,384,128]{2,1,0:T(8,128)(2,1)} %get-tuple-element.96), channel_id=1, source_target_pairs={{0,24},{2,26},{4,28},{6,30},{8,16},{10,18},{12,20},{14,22},{16,8},... | collective-permute-start | bytes 294920 | tf_op jit(solution)/shard_map/ppermute | solution.py:28
  103.1 2.5 %collective-permute-done.13.refs_2_ = bf16[1,384,128]{2,1,0:T(8,128)(2,1)S(1)} collective-permute-done((bf16[1,384,128]{2,1,0:T(8,128)(2,1)}, bf16[1,384,128]{2,1,0:T(8,128)(2,1)S(1)}, u32[]{:S(2)}, u32[]{:S(2)}) %collective-permute-start.13) | collective-permute-done | bytes 98336 | tf_op jit(solution)/shard_map/ppermute | solution.py:28
  105.6 1.9 collective-permute-done.14.refs_3_
  108.6 0.9 copy-done.19
  109.6 10.1 %attend.3 = bf16[4,384,128]{2,1,0:T(8,128)(2,1)} custom-call(s32[3]{0:T(128)} %broadcast_maximum_fusion.2.place_ref, bf16[1,384,384]{2,1,0:T(8,128)(2,1)} %get-tuple-element.81.refs_0_, bf16[1,384,384]{2,1,0:T(8,128)(2,1)} %copy-done.10, bf16[1,384,384]{2,1,0:T(8,128)(2,1)} %copy-done.11, bf16[1,384,384]{2,1,0:T(8,128)(2,1)} %copy-done.12, ...), custom_call_target="tpu_custom_call" | custom-call | flops 2415919104 | bytes 3145728 | tf_op jit(solution)/shard_map/attend/pallas_call | solution.py:255
  120.2 9.9 %attend.4 = bf16[4,384,128]{2,1,0:T(8,128)(2,1)} custom-call(s32[3]{0:T(128)} %broadcast_maximum_fusion.1.place_ref, bf16[1,384,128]{2,1,0:T(8,128)(2,1)} %get-tuple-element.98.refs_0_, bf16[1,384,128]{2,1,0:T(8,128)(2,1)} %copy-done.29, bf16[1,384,128]{2,1,0:T(8,128)(2,1)} %copy-done.30, bf16[1,384,128]{2,1,0:T(8,128)(2,1)} %copy-done.31, ...), custom_call_target="tpu_custom_call" | custom-call | flops 2415919104 | bytes 3145728 | tf_op jit(solution)/shard_map/attend/pallas_call | solution.py:255
  130.3 3.8 %all-to-all-start = ((bf16[4,384,128]{2,1,0:T(8,128)(2,1)}), bf16[4,384,128]{2,1,0:T(8,128)(2,1)S(1)}, u32[]{:S(2)}, u32[]{:S(2)}) async-start(bf16[4,384,128]{2,1,0:T(8,128)(2,1)} %attend.3), calls=%async_computation | async-start | bytes 786432 | tf_op jit(solution)/shard_map/all_to_all | solution.py:425
  134.1 2.0 collective-permute-start.20
  136.1 2.4 %collective-permute-start.21 = (bf16[1,384,128]{2,1,0:T(8,128)(2,1)S(1)}, bf16[1,384,128]{2,1,0:T(8,128)(2,1)S(1)}, u32[]{:S(2)}, u32[]{:S(2)}) collective-permute-start(bf16[1,384,128]{2,1,0:T(8,128)(2,1)S(1)} %copy-done.24), channel_id=1, source_target_pairs={{0,16},{2,18},{4,20},{6,22},{8,24},{10,26},{12,28},{14,30},{16,0},... | collective-permute-start | bytes 294920 | tf_op jit(solution)/shard_map/ppermute | solution.py:28
  138.6 6.7 %collective-permute-done.20.refs_1_ = bf16[1,384,128]{2,1,0:T(8,128)(2,1)S(1)} collective-permute-done((bf16[1,384,128]{2,1,0:T(8,128)(2,1)S(1)}, bf16[1,384,128]{2,1,0:T(8,128)(2,1)S(1)}, u32[]{:S(2)}, u32[]{:S(2)}) %collective-permute-start.20) | collective-permute-done | bytes 98336 | tf_op jit(solution)/shard_map/ppermute | solution.py:28
  145.2 8.3 %collective-permute-done.21.refs_2_ = bf16[1,384,128]{2,1,0:T(8,128)(2,1)S(1)} collective-permute-done((bf16[1,384,128]{2,1,0:T(8,128)(2,1)S(1)}, bf16[1,384,128]{2,1,0:T(8,128)(2,1)S(1)}, u32[]{:S(2)}, u32[]{:S(2)}) %collective-permute-start.21) | collective-permute-done | bytes 98336 | tf_op jit(solution)/shard_map/ppermute | solution.py:28
  154.1 3.9 %all-to-all-start.1 = ((bf16[4,384,128]{2,1,0:T(8,128)(2,1)}), bf16[4,384,128]{2,1,0:T(8,128)(2,1)S(1)}, u32[]{:S(2)}, u32[]{:S(2)}) async-start(bf16[4,384,128]{2,1,0:T(8,128)(2,1)} %attend.4), calls=%async_computation.1 | async-start | bytes 786432 | tf_op jit(solution)/shard_map/all_to_all | solution.py:425
  158.0 1.4 collective-permute-start.18
  159.9 10.1 %all-to-all-done.1.refs_1_ = bf16[4,384,128]{2,1,0:T(8,128)(2,1)S(1)} async-done(((bf16[4,384,128]{2,1,0:T(8,128)(2,1)}), bf16[4,384,128]{2,1,0:T(8,128)(2,1)S(1)}, u32[]{:S(2)}, u32[]{:S(2)}) %all-to-all-start.1) | async-done | bytes 393248 | tf_op jit(solution)/shard_map/all_to_all | solution.py:425
  169.9 1.4 collective-permute-start.19
  171.4 10.1 %attend.5 = (bf16[1,384,128]{2,1,0:T(8,128)(2,1)}, bf16[1,384,128]{2,1,0:T(8,128)(2,1)}, bf16[1,384,128]{2,1,0:T(8,128)(2,1)}, bf16[1,384,128]{2,1,0:T(8,128)(2,1)}) custom-call(s32[3]{0:T(128)} %broadcast_maximum_fusion.place_ref, bf16[1,384,128]{2,1,0:T(8,128)(2,1)} %get-tuple-element.110.refs_0_, bf16[1,384,128]{2,1,0:T(8,128)(2,1)} %copy-done.26, ...), custom_call_target="tpu_custom_call" | custom-call | flops 2415919104 | bytes 3145728 | tf_op jit(solution)/shard_map/attend/pallas_call | solution.py:255
  181.5 2.7 %collective-permute-start.27 = (bf16[1,384,128]{2,1,0:T(8,128)(2,1)}, bf16[1,384,128]{2,1,0:T(8,128)(2,1)S(1)}, u32[]{:S(2)}, u32[]{:S(2)}) collective-permute-start(bf16[1,384,128]{2,1,0:T(8,128)(2,1)} %get-tuple-element.115), channel_id=1, source_target_pairs={{0,16},{2,18},{4,20},{6,22},{8,24},{10,26},{12,28},{14,30},{16,0},... | collective-permute-start | bytes 294920 | tf_op jit(solution)/shard_map/ppermute | solution.py:28
  184.3 1.7 collective-permute-start.28
  185.9 0.8 collective-permute-done.26
  186.7 5.2 %collective-permute-done.27 = bf16[1,384,128]{2,1,0:T(8,128)(2,1)S(1)} collective-permute-done((bf16[1,384,128]{2,1,0:T(8,128)(2,1)}, bf16[1,384,128]{2,1,0:T(8,128)(2,1)S(1)}, u32[]{:S(2)}, u32[]{:S(2)}) %collective-permute-start.27) | collective-permute-done | bytes 98336 | tf_op jit(solution)/shard_map/ppermute | solution.py:28
  191.9 0.9 pad_maximum_fusion.1.refs_1_
  192.9 0.7 copy-done.4
  193.8 7.2 %finish.2.refs_0_ = f32[384,1536]{1,0:T(8,128)} custom-call(s32[3]{0:T(128)} %pad_add_fusion.place_ref, bf16[4,384,128]{2,1,0:T(8,128)(2,1)} %copy-done, bf16[4,384,128]{2,1,0:T(8,128)(2,1)} %copy-done.1, bf16[1536,3072]{1,0:T(8,128)(2,1)} %refs_2_.5, bf16[4,384,128]{2,1,0:T(8,128)(2,1)} %copy-done.4, bf16[4,384,128]{2,1,0:T(8,128)(2,1)} %copy-done.5, ...), custom_call_target="tpu_custom_call" | custom-call | flops 2415919104 | bytes 11010048 | tf_op jit(solution)/shard_map/finish/pallas_call | solution.py:346
  200.9 0.6 collective-permute-start.29
  201.6 8.2 %collective-permute-done.29.refs_3_ = bf16[4,384,128]{2,1,0:T(8,128)(2,1)S(1)} collective-permute-done((bf16[4,384,128]{2,1,0:T(8,128)(2,1)S(1)}, bf16[4,384,128]{2,1,0:T(8,128)(2,1)S(1)}, u32[]{:S(2)}, u32[]{:S(2)}) %collective-permute-start.29) | collective-permute-done | bytes 393248 | tf_op jit(solution)/shard_map/ppermute | solution.py:28
  209.8 0.8 copy-done.6
  210.6 6.3 %finish.3 = bf16[384,1536]{1,0:T(8,128)(2,1)} custom-call(s32[3]{0:T(128)} %pad_add_fusion.place_ref, f32[384,1536]{1,0:T(8,128)} %finish.2.refs_0_, bf16[4,384,128]{2,1,0:T(8,128)(2,1)} %copy-done.2, bf16[1536,3072]{1,0:T(8,128)(2,1)} %refs_2_.5, bf16[4,384,128]{2,1,0:T(8,128)(2,1)} %copy-done.6, bf16[2,2,1536,768]{3,2,1,0:T(8,128)(2,1)} %bitcast.11, ...), custom_call_target="tpu_custom_call" | custom-call | flops 1207959552 | bytes 7864320 | tf_op jit(solution)/shard_map/finish/pallas_call | solution.py:346
  (113 shorter events, 5.2 us)
Async XLA Ops:
  6.5 123.6 %all-gather.5.cloned.1.call-start = ((), (), s32[]{:S(2)}) async-start(), calls=%async_computation.2 | async-start | bytes 7077888 | tf_op jit(solution)/shard_map/all_gather | solution.py:384
  9.8 183.1 %all-gather.7.cloned.1.call-start = ((), (), s32[]{:S(2)}) async-start(), calls=%async_computation.3 | async-start | bytes 14155776 | tf_op jit(solution)/shard_map/all_gather | solution.py:391
  24.3 15.8 %collective-permute-start = (bf16[1,384,384]{2,1,0:T(8,128)(2,1)}, bf16[1,384,384]{2,1,0:T(8,128)(2,1)S(1)}, u32[]{:S(2)}, u32[]{:S(2)}) collective-permute-start(bf16[1,384,384]{2,1,0:T(8,128)(2,1)} %get-tuple-element.62), channel_id=1, source_target_pairs={{0,8},{2,10},{4,12},{6,14},{8,0},{10,2},{12,4},{14,6},{16,24},{18,... | collective-permute-start | bytes 884744 | tf_op jit(solution)/shard_map/ppermute | solution.py:28
  27.4 26.1 %collective-permute-start.1 = (bf16[1,384,384]{2,1,0:T(8,128)(2,1)}, bf16[1,384,384]{2,1,0:T(8,128)(2,1)S(1)}, u32[]{:S(2)}, u32[]{:S(2)}) collective-permute-start(bf16[1,384,384]{2,1,0:T(8,128)(2,1)} %get-tuple-element.63), channel_id=1, source_target_pairs={{0,16},{2,18},{4,20},{6,22},{8,24},{10,26},{12,28},{14,30},{16,0},... | collective-permute-start | bytes 884744 | tf_op jit(solution)/shard_map/ppermute | solution.py:28
  30.0 23.5 %collective-permute-start.2 = (bf16[1,384,384]{2,1,0:T(8,128)(2,1)}, bf16[1,384,384]{2,1,0:T(8,128)(2,1)S(1)}, u32[]{:S(2)}, u32[]{:S(2)}) collective-permute-start(bf16[1,384,384]{2,1,0:T(8,128)(2,1)} %get-tuple-element.64), channel_id=1, source_target_pairs={{0,24},{2,26},{4,28},{6,30},{8,16},{10,18},{12,20},{14,22},{16,8},... | collective-permute-start | bytes 884744 | tf_op jit(solution)/shard_map/ppermute | solution.py:28
  53.5 21.4 %copy-start.11 = (bf16[1,384,384]{2,1,0:T(8,128)(2,1)}, bf16[1,384,384]{2,1,0:T(8,128)(2,1)S(1)}, u32[]{:S(2)}) copy-start(bf16[1,384,384]{2,1,0:T(8,128)(2,1)S(1)} %collective-permute-done.1.refs_2_) | copy-start | bytes 884740
  53.5 21.4 %copy-start.12 = (bf16[1,384,384]{2,1,0:T(8,128)(2,1)}, bf16[1,384,384]{2,1,0:T(8,128)(2,1)S(1)}, u32[]{:S(2)}) copy-start(bf16[1,384,384]{2,1,0:T(8,128)(2,1)S(1)} %collective-permute-done.2.refs_3_) | copy-start | bytes 884740
  53.5 22.0 %copy-start.7 = (bf16[1,384,256]{2,1,0:T(8,128)(2,1)S(1)}, bf16[1,384,256]{2,1,0:T(8,128)(2,1)}, u32[]{:S(2)}) copy-start(bf16[1,384,256]{2,1,0:T(8,128)(2,1)} %get-tuple-element.74) | copy-start | bytes 589828
  53.7 37.4 %copy-start.3 = (bf16[4,384,256]{2,1,0:T(8,128)(2,1)}, bf16[4,384,256]{2,1,0:T(8,128)(2,1)S(1)}, u32[]{:S(2)}) copy-start(bf16[4,384,256]{2,1,0:T(8,128)(2,1)S(1)} %pad_maximum_fusion.refs_4_) | copy-start | bytes 2359300
  53.7 26.9 %collective-permute-start.7 = (bf16[4,384,256]{2,1,0:T(8,128)(2,1)S(1)}, bf16[4,384,256]{2,1,0:T(8,128)(2,1)S(1)}, u32[]{:S(2)}, u32[]{:S(2)}) collective-permute-start(bf16[4,384,256]{2,1,0:T(8,128)(2,1)S(1)} %pad_maximum_fusion.refs_4_), channel_id=1, source_target_pairs={{0,4},{2,6},{4,0},{6,2},{8,12},{10,14},{12,8},{14,10},{16,20},{18,... | collective-permute-start | bytes 2359304 | tf_op jit(solution)/shard_map/ppermute | solution.py:28
  55.5 9.0 %collective-permute-start.3 = (bf16[1,384,256]{2,1,0:T(8,128)(2,1)S(1)}, bf16[1,384,256]{2,1,0:T(8,128)(2,1)S(1)}, u32[]{:S(2)}, u32[]{:S(2)}) collective-permute-start(bf16[1,384,256]{2,1,0:T(8,128)(2,1)S(1)} %copy-done.22), channel_id=1, source_target_pairs={{0,8},{2,10},{4,12},{6,14},{8,0},{10,2},{12,4},{14,6},{16,24},{18,... | collective-permute-start | bytes 589832 | tf_op jit(solution)/shard_map/ppermute | solution.py:28
  58.3 16.5 %collective-permute-start.8 = (bf16[1,384,256]{2,1,0:T(8,128)(2,1)S(1)}, bf16[1,384,256]{2,1,0:T(8,128)(2,1)S(1)}, u32[]{:S(2)}, u32[]{:S(2)}) collective-permute-start(bf16[1,384,256]{2,1,0:T(8,128)(2,1)S(1)} %copy-done.21), channel_id=1, source_target_pairs={{0,16},{2,18},{4,20},{6,22},{8,24},{10,26},{12,28},{14,30},{16,0},... | collective-permute-start | bytes 589832 | tf_op jit(solution)/shard_map/ppermute | solution.py:28
  59.4 15.4 %collective-permute-start.9 = (bf16[1,384,256]{2,1,0:T(8,128)(2,1)S(1)}, bf16[1,384,256]{2,1,0:T(8,128)(2,1)S(1)}, u32[]{:S(2)}, u32[]{:S(2)}) collective-permute-start(bf16[1,384,256]{2,1,0:T(8,128)(2,1)S(1)} %copy-done.20), channel_id=1, source_target_pairs={{0,24},{2,26},{4,28},{6,30},{8,16},{10,18},{12,20},{14,22},{16,8},... | collective-permute-start | bytes 589832 | tf_op jit(solution)/shard_map/ppermute | solution.py:28
  74.9 32.6 %copy-start.14 = (bf16[4,384,256]{2,1,0:T(8,128)(2,1)}, bf16[4,384,256]{2,1,0:T(8,128)(2,1)S(1)}, u32[]{:S(2)}) copy-start(bf16[4,384,256]{2,1,0:T(8,128)(2,1)S(1)} %constant_dynamic-update-slice_fusion.4.refs_4_) | copy-start | bytes 2359300
  74.9 32.6 %collective-permute-start.16 = (bf16[4,384,256]{2,1,0:T(8,128)(2,1)S(1)}, bf16[4,384,256]{2,1,0:T(8,128)(2,1)}, u32[]{:S(2)}, u32[]{:S(2)}) collective-permute-start(bf16[4,384,256]{2,1,0:T(8,128)(2,1)S(1)} %constant_dynamic-update-slice_fusion.4.refs_4_), channel_id=1, source_target_pairs={{0,4},{2,6},{4,0},{6,2},{8,12},{10,14},{12,8},{14,10},{16,20},{18,... | collective-permute-start | bytes 2359304 | tf_op jit(solution)/shard_map/ppermute | solution.py:28
  75.5 15.7 %collective-permute-start.4 = (bf16[1,384,256]{2,1,0:T(8,128)(2,1)}, bf16[1,384,256]{2,1,0:T(8,128)(2,1)S(1)}, u32[]{:S(2)}, u32[]{:S(2)}) collective-permute-start(bf16[1,384,256]{2,1,0:T(8,128)(2,1)} %get-tuple-element.75), channel_id=1, source_target_pairs={{0,8},{2,10},{4,12},{6,14},{8,0},{10,2},{12,4},{14,6},{16,24},{18,... | collective-permute-start | bytes 589832 | tf_op jit(solution)/shard_map/ppermute | solution.py:28
  78.2 16.0 %collective-permute-start.5 = (bf16[1,384,256]{2,1,0:T(8,128)(2,1)}, bf16[1,384,256]{2,1,0:T(8,128)(2,1)S(1)}, u32[]{:S(2)}, u32[]{:S(2)}) collective-permute-start(bf16[1,384,256]{2,1,0:T(8,128)(2,1)} %get-tuple-element.76), channel_id=1, source_target_pairs={{0,16},{2,18},{4,20},{6,22},{8,24},{10,26},{12,28},{14,30},{16,0},... | collective-permute-start | bytes 589832 | tf_op jit(solution)/shard_map/ppermute | solution.py:28
  79.2 14.9 %collective-permute-start.6 = (bf16[1,384,256]{2,1,0:T(8,128)(2,1)}, bf16[1,384,256]{2,1,0:T(8,128)(2,1)S(1)}, u32[]{:S(2)}, u32[]{:S(2)}) collective-permute-start(bf16[1,384,256]{2,1,0:T(8,128)(2,1)} %get-tuple-element.77), channel_id=1, source_target_pairs={{0,24},{2,26},{4,28},{6,30},{8,16},{10,18},{12,20},{14,22},{16,8},... | collective-permute-start | bytes 589832 | tf_op jit(solution)/shard_map/ppermute | solution.py:28
  82.2 25.9 %copy-start.15 = (s32[3]{0:T(128)S(1)}, s32[3]{0:T(128)}, u32[]{:S(2)}) copy-start(s32[3]{0:T(128)} %pad_add_fusion.place_ref) | copy-start | bytes 40
  91.1 17.5 %collective-permute-start.11 = (bf16[4,384,256]{2,1,0:T(8,128)(2,1)S(1)}, bf16[4,384,256]{2,1,0:T(8,128)(2,1)S(1)}, u32[]{:S(2)}, u32[]{:S(2)}) collective-permute-start(bf16[4,384,256]{2,1,0:T(8,128)(2,1)S(1)} %copy-done.17), channel_id=1, source_target_pairs={{0,2},{2,0},{4,6},{6,4},{8,10},{10,8},{12,14},{14,12},{16,18},{18,... | collective-permute-start | bytes 2359304 | tf_op jit(solution)/shard_map/ppermute | solution.py:28
  91.2 18.4 %collective-permute-start.10 = (bf16[4,384,256]{2,1,0:T(8,128)(2,1)S(1)}, bf16[4,384,256]{2,1,0:T(8,128)(2,1)}, u32[]{:S(2)}, u32[]{:S(2)}) collective-permute-start(bf16[4,384,256]{2,1,0:T(8,128)(2,1)S(1)} %pad_maximum_fusion.refs_4_), channel_id=1, source_target_pairs={{0,2},{2,0},{4,6},{6,4},{8,10},{10,8},{12,14},{14,12},{16,18},{18,... | collective-permute-start | bytes 2359304 | tf_op jit(solution)/shard_map/ppermute | solution.py:28
  94.2 59.3 %copy-start.13 = (bf16[4,384,256]{2,1,0:T(8,128)(2,1)}, bf16[4,384,256]{2,1,0:T(8,128)(2,1)S(1)}, u32[]{:S(2)}) copy-start(bf16[4,384,256]{2,1,0:T(8,128)(2,1)S(1)} %constant_dynamic-update-slice_fusion.refs_4_) | copy-start | bytes 2359300
  94.2 6.6 %collective-permute-start.12 = (bf16[1,384,128]{2,1,0:T(8,128)(2,1)}, bf16[1,384,128]{2,1,0:T(8,128)(2,1)S(1)}, u32[]{:S(2)}, u32[]{:S(2)}) collective-permute-start(bf16[1,384,128]{2,1,0:T(8,128)(2,1)} %get-tuple-element.94), channel_id=1, source_target_pairs={{0,8},{2,10},{4,12},{6,14},{8,0},{10,2},{12,4},{14,6},{16,24},{18,... | collective-permute-start | bytes 294920 | tf_op jit(solution)/shard_map/ppermute | solution.py:28
  96.9 8.7 %collective-permute-start.13 = (bf16[1,384,128]{2,1,0:T(8,128)(2,1)}, bf16[1,384,128]{2,1,0:T(8,128)(2,1)S(1)}, u32[]{:S(2)}, u32[]{:S(2)}) collective-permute-start(bf16[1,384,128]{2,1,0:T(8,128)(2,1)} %get-tuple-element.95), channel_id=1, source_target_pairs={{0,16},{2,18},{4,20},{6,22},{8,24},{10,26},{12,28},{14,30},{16,0},... | collective-permute-start | bytes 294920 | tf_op jit(solution)/shard_map/ppermute | solution.py:28
  100.8 19.4 %copy-start.29 = (bf16[1,384,128]{2,1,0:T(8,128)(2,1)}, bf16[1,384,128]{2,1,0:T(8,128)(2,1)S(1)}, u32[]{:S(2)}) copy-start(bf16[1,384,128]{2,1,0:T(8,128)(2,1)S(1)} %collective-permute-done.12.refs_1_) | copy-start | bytes 294916
  100.8 6.7 %collective-permute-start.14 = (bf16[1,384,128]{2,1,0:T(8,128)(2,1)}, bf16[1,384,128]{2,1,0:T(8,128)(2,1)S(1)}, u32[]{:S(2)}, u32[]{:S(2)}) collective-permute-start(bf16[1,384,128]{2,1,0:T(8,128)(2,1)} %get-tuple-element.96), channel_id=1, source_target_pairs={{0,24},{2,26},{4,28},{6,30},{8,16},{10,18},{12,20},{14,22},{16,8},... | collective-permute-start | bytes 294920 | tf_op jit(solution)/shard_map/ppermute | solution.py:28
  105.6 14.6 %copy-start.30 = (bf16[1,384,128]{2,1,0:T(8,128)(2,1)}, bf16[1,384,128]{2,1,0:T(8,128)(2,1)S(1)}, u32[]{:S(2)}) copy-start(bf16[1,384,128]{2,1,0:T(8,128)(2,1)S(1)} %collective-permute-done.13.refs_2_) | copy-start | bytes 294916
  107.5 12.7 %collective-permute-start.15 = (bf16[4,384,256]{2,1,0:T(8,128)(2,1)S(1)}, bf16[4,384,256]{2,1,0:T(8,128)(2,1)}, u32[]{:S(2)}, u32[]{:S(2)}) collective-permute-start(bf16[4,384,256]{2,1,0:T(8,128)(2,1)S(1)} %constant_dynamic-update-slice_fusion.4.refs_4_), channel_id=1, source_target_pairs={{0,2},{2,0},{4,6},{6,4},{8,10},{10,8},{12,14},{14,12},{16,18},{18,... | collective-permute-start | bytes 2359304 | tf_op jit(solution)/shard_map/ppermute | solution.py:28
  107.5 12.7 %collective-permute-start.17 = (bf16[4,384,256]{2,1,0:T(8,128)(2,1)}, bf16[4,384,256]{2,1,0:T(8,128)(2,1)}, u32[]{:S(2)}, u32[]{:S(2)}) collective-permute-start(bf16[4,384,256]{2,1,0:T(8,128)(2,1)} %collective-permute-done.16.refs_6_), channel_id=1, source_target_pairs={{0,2},{2,0},{4,6},{6,4},{8,10},{10,8},{12,14},{14,12},{16,18},{18,... | collective-permute-start | bytes 2359304 | tf_op jit(solution)/shard_map/ppermute | solution.py:28
  130.2 23.5 %collective-permute-start.24 = (bf16[4,384,256]{2,1,0:T(8,128)(2,1)S(1)}, bf16[4,384,256]{2,1,0:T(8,128)(2,1)S(1)}, u32[]{:S(2)}, u32[]{:S(2)}) collective-permute-start(bf16[4,384,256]{2,1,0:T(8,128)(2,1)S(1)} %constant_dynamic-update-slice_fusion.refs_4_), channel_id=1, source_target_pairs={{0,4},{2,6},{4,0},{6,2},{8,12},{10,14},{12,8},{14,10},{16,20},{18,... | collective-permute-start | bytes 2359304 | tf_op jit(solution)/shard_map/ppermute | solution.py:28
  130.3 23.8 %all-to-all-start = ((bf16[4,384,128]{2,1,0:T(8,128)(2,1)}), bf16[4,384,128]{2,1,0:T(8,128)(2,1)S(1)}, u32[]{:S(2)}, u32[]{:S(2)}) async-start(bf16[4,384,128]{2,1,0:T(8,128)(2,1)} %attend.3), calls=%async_computation | async-start | bytes 786432 | tf_op jit(solution)/shard_map/all_to_all | solution.py:425
  134.1 11.1 %collective-permute-start.20 = (bf16[1,384,128]{2,1,0:T(8,128)(2,1)S(1)}, bf16[1,384,128]{2,1,0:T(8,128)(2,1)S(1)}, u32[]{:S(2)}, u32[]{:S(2)}) collective-permute-start(bf16[1,384,128]{2,1,0:T(8,128)(2,1)S(1)} %copy-done.25), channel_id=1, source_target_pairs={{0,8},{2,10},{4,12},{6,14},{8,0},{10,2},{12,4},{14,6},{16,24},{18,... | collective-permute-start | bytes 294920 | tf_op jit(solution)/shard_map/ppermute | solution.py:28
  136.1 17.4 %collective-permute-start.21 = (bf16[1,384,128]{2,1,0:T(8,128)(2,1)S(1)}, bf16[1,384,128]{2,1,0:T(8,128)(2,1)S(1)}, u32[]{:S(2)}, u32[]{:S(2)}) collective-permute-start(bf16[1,384,128]{2,1,0:T(8,128)(2,1)S(1)} %copy-done.24), channel_id=1, source_target_pairs={{0,16},{2,18},{4,20},{6,22},{8,24},{10,26},{12,28},{14,30},{16,0},... | collective-permute-start | bytes 294920 | tf_op jit(solution)/shard_map/ppermute | solution.py:28
  138.5 15.0 %collective-permute-start.22 = (bf16[1,384,128]{2,1,0:T(8,128)(2,1)S(1)}, bf16[1,384,128]{2,1,0:T(8,128)(2,1)S(1)}, u32[]{:S(2)}, u32[]{:S(2)}) collective-permute-start(bf16[1,384,128]{2,1,0:T(8,128)(2,1)S(1)} %copy-done.23), channel_id=1, source_target_pairs={{0,24},{2,26},{4,28},{6,30},{8,16},{10,18},{12,20},{14,22},{16,8},... | collective-permute-start | bytes 294920 | tf_op jit(solution)/shard_map/ppermute | solution.py:28
  145.2 26.1 %copy-start.26 = (bf16[1,384,128]{2,1,0:T(8,128)(2,1)}, bf16[1,384,128]{2,1,0:T(8,128)(2,1)S(1)}, u32[]{:S(2)}) copy-start(bf16[1,384,128]{2,1,0:T(8,128)(2,1)S(1)} %collective-permute-done.20.refs_1_) | copy-start | bytes 294916
  153.5 17.8 %copy-start.27 = (bf16[1,384,128]{2,1,0:T(8,128)(2,1)}, bf16[1,384,128]{2,1,0:T(8,128)(2,1)S(1)}, u32[]{:S(2)}) copy-start(bf16[1,384,128]{2,1,0:T(8,128)(2,1)S(1)} %collective-permute-done.21.refs_2_) | copy-start | bytes 294916
  153.5 17.8 %copy-start.28 = (bf16[1,384,128]{2,1,0:T(8,128)(2,1)}, bf16[1,384,128]{2,1,0:T(8,128)(2,1)S(1)}, u32[]{:S(2)}) copy-start(bf16[1,384,128]{2,1,0:T(8,128)(2,1)S(1)} %collective-permute-done.22.refs_3_) | copy-start | bytes 294916
  153.5 17.8 %collective-permute-start.23 = (bf16[4,384,256]{2,1,0:T(8,128)(2,1)S(1)}, bf16[4,384,256]{2,1,0:T(8,128)(2,1)}, u32[]{:S(2)}, u32[]{:S(2)}) collective-permute-start(bf16[4,384,256]{2,1,0:T(8,128)(2,1)S(1)} %constant_dynamic-update-slice_fusion.refs_4_), channel_id=1, source_target_pairs={{0,2},{2,0},{4,6},{6,4},{8,10},{10,8},{12,14},{14,12},{16,18},{18,... | collective-permute-start | bytes 2359304 | tf_op jit(solution)/shard_map/ppermute | solution.py:28
  153.7 17.7 %copy-start.18 = (bf16[4,384,256]{2,1,0:T(8,128)(2,1)}, bf16[4,384,256]{2,1,0:T(8,128)(2,1)S(1)}, u32[]{:S(2)}) copy-start(bf16[4,384,256]{2,1,0:T(8,128)(2,1)S(1)} %collective-permute-done.24.refs_6_) | copy-start | bytes 2359300
  153.7 17.6 %collective-permute-start.25 = (bf16[4,384,256]{2,1,0:T(8,128)(2,1)S(1)}, bf16[4,384,256]{2,1,0:T(8,128)(2,1)}, u32[]{:S(2)}, u32[]{:S(2)}) collective-permute-start(bf16[4,384,256]{2,1,0:T(8,128)(2,1)S(1)} %collective-permute-done.24.refs_6_), channel_id=1, source_target_pairs={{0,2},{2,0},{4,6},{6,4},{8,10},{10,8},{12,14},{14,12},{16,18},{18,... | collective-permute-start | bytes 2359304 | tf_op jit(solution)/shard_map/ppermute | solution.py:28
  154.1 27.3 %copy-start = (bf16[4,384,128]{2,1,0:T(8,128)(2,1)}, bf16[4,384,128]{2,1,0:T(8,128)(2,1)S(1)}, u32[]{:S(2)}) copy-start(bf16[4,384,128]{2,1,0:T(8,128)(2,1)S(1)} %all-to-all-done.refs_0_) | copy-start | bytes 1179652
  154.1 15.8 %all-to-all-start.1 = ((bf16[4,384,128]{2,1,0:T(8,128)(2,1)}), bf16[4,384,128]{2,1,0:T(8,128)(2,1)S(1)}, u32[]{:S(2)}, u32[]{:S(2)}) async-start(bf16[4,384,128]{2,1,0:T(8,128)(2,1)} %attend.4), calls=%async_computation.1 | async-start | bytes 786432 | tf_op jit(solution)/shard_map/all_to_all | solution.py:425
  158.0 34.8 %collective-permute-start.18 = (bf16[4,384,128]{2,1,0:T(8,128)(2,1)S(1)}, bf16[4,384,128]{2,1,0:T(8,128)(2,1)S(1)}, u32[]{:S(2)}, u32[]{:S(2)}) collective-permute-start(bf16[4,384,128]{2,1,0:T(8,128)(2,1)S(1)} %all-to-all-done.refs_0_), channel_id=1, source_target_pairs={{0,1},{1,0},{2,3},{3,2},{4,5},{5,4},{6,7},{7,6},{8,9},{9,8},{10,11... | collective-permute-start | bytes 1179656 | tf_op jit(solution)/shard_map/ppermute | solution.py:28
  169.9 22.9 %collective-permute-start.19 = (bf16[4,384,128]{2,1,0:T(8,128)(2,1)S(1)}, bf16[4,384,128]{2,1,0:T(8,128)(2,1)S(1)}, u32[]{:S(2)}, u32[]{:S(2)}) collective-permute-start(bf16[4,384,128]{2,1,0:T(8,128)(2,1)S(1)} %all-to-all-done.1.refs_1_), channel_id=1, source_target_pairs={{0,1},{1,0},{2,3},{3,2},{4,5},{5,4},{6,7},{7,6},{8,9},{9,8},{10,11... | collective-permute-start | bytes 1179656 | tf_op jit(solution)/shard_map/ppermute | solution.py:28
  181.5 5.2 %collective-permute-start.26 = (bf16[1,384,128]{2,1,0:T(8,128)(2,1)}, bf16[1,384,128]{2,1,0:T(8,128)(2,1)S(1)}, u32[]{:S(2)}, u32[]{:S(2)}) collective-permute-start(bf16[1,384,128]{2,1,0:T(8,128)(2,1)} %get-tuple-element.114), channel_id=1, source_target_pairs={{0,8},{2,10},{4,12},{6,14},{8,0},{10,2},{12,4},{14,6},{16,24},{18,... | collective-permute-start | bytes 294920 | tf_op jit(solution)/shard_map/ppermute | solution.py:28
  181.5 10.3 %collective-permute-start.27 = (bf16[1,384,128]{2,1,0:T(8,128)(2,1)}, bf16[1,384,128]{2,1,0:T(8,128)(2,1)S(1)}, u32[]{:S(2)}, u32[]{:S(2)}) collective-permute-start(bf16[1,384,128]{2,1,0:T(8,128)(2,1)} %get-tuple-element.115), channel_id=1, source_target_pairs={{0,16},{2,18},{4,20},{6,22},{8,24},{10,26},{12,28},{14,30},{16,0},... | collective-permute-start | bytes 294920 | tf_op jit(solution)/shard_map/ppermute | solution.py:28
  184.3 7.6 %collective-permute-start.28 = (bf16[1,384,128]{2,1,0:T(8,128)(2,1)}, bf16[1,384,128]{2,1,0:T(8,128)(2,1)S(1)}, u32[]{:S(2)}, u32[]{:S(2)}) collective-permute-start(bf16[1,384,128]{2,1,0:T(8,128)(2,1)} %get-tuple-element.116), channel_id=1, source_target_pairs={{0,24},{2,26},{4,28},{6,30},{8,16},{10,18},{12,20},{14,22},{16,8},... | collective-permute-start | bytes 294920 | tf_op jit(solution)/shard_map/ppermute | solution.py:28
  200.9 8.8 %collective-permute-start.29 = (bf16[4,384,128]{2,1,0:T(8,128)(2,1)S(1)}, bf16[4,384,128]{2,1,0:T(8,128)(2,1)S(1)}, u32[]{:S(2)}, u32[]{:S(2)}) collective-permute-start(bf16[4,384,128]{2,1,0:T(8,128)(2,1)S(1)} %pad_maximum_fusion.1.refs_1_), channel_id=1, source_target_pairs={{0,1},{1,0},{2,3},{3,2},{4,5},{5,4},{6,7},{7,6},{8,9},{9,8},{10,11... | collective-permute-start | bytes 1179656 | tf_op jit(solution)/shard_map/ppermute | solution.py:28
  (18 other events, 111.0 us)
Sparse Core Ops, SparseCore 0:
  9.9 65.3 all-gather.4
  130.3 21.4 all-gather.6

commit v4 on v3

--- a/solution.py
+++ b/solution.py
@@ -76,7 +76,7 @@
     rows = normed_ref.shape[0]
     size = gain_ref.shape[2]
     plane = place_ref[0]
-    for step, (kind, chunk, target, low) in enumerate(steps):
+    for step, (kind, chunk, target, row, low) in enumerate(steps):
 
         @pl.when(pl.program_id(0) == step)
         def _():
@@ -91,13 +91,13 @@
                 result_ref[:, g * size : (g + 1) * size] = part.astype(bf16)
             packed = jnp.dot(chosen_ref[...], result_ref[...], preferred_element_type=f32)
             if kind == 1:
-                row = lax.broadcasted_iota(jnp.int32, (rows, groups * size), 0)
-                packed = jnp.where(row < count_ref[0, 0], packed, dead_mark)
+                line = lax.broadcasted_iota(jnp.int32, (rows, groups * size), 0)
+                packed = jnp.where(line < count_ref[0, 0], packed, dead_mark)
             result_ref[...] = packed.astype(bf16)
             for k in range(groups):
                 start = pl.multiple_of(lax.bitwise_xor(plane, k) * size, size)
                 found = result_ref[:, pl.ds(start, size)]
-                outs[target * groups + k][0, :, low : low + size] = found
+                outs[target * groups + k][row, :, low : low + size] = found
 
 
 def project(place, prepared, weights, gains, sets, groups, first=None):
@@ -111,8 +111,9 @@
     square = pl.BlockSpec((rows, rows), fixed)
     whole = pl.BlockSpec((rows, width), fixed)
     steps = [
-        (kind, chunk, target, i * size)
-        for target, (kinds, chunk) in enumerate(sets)
+        (kind, chunk, target, row, i * size)
+        for target, (kinds, which) in enumerate(sets)
+        for row, chunk in enumerate(which)
         for i, kind in enumerate(kinds)
     ]
 
@@ -123,9 +124,11 @@
             chunk = jnp.where(t == step, found[1], chunk)
         return (kind, 0, chunk)
 
-    widths = [len(kinds) * size for kinds, _ in sets for _ in range(groups)]
-    out_specs = [pl.BlockSpec((1, rows, wide), lambda t, place: (0, 0, 0)) for wide in widths]
-    out_shape = [jax.ShapeDtypeStruct((1, rows, wide), bf16) for wide in widths]
+    shapes = [
+        (len(which), rows, len(kinds) * size) for kinds, which in sets for _ in range(groups)
+    ]
+    out_specs = [pl.BlockSpec(shape, lambda t, place: (0, 0, 0)) for shape in shapes]
+    out_shape = [jax.ShapeDtypeStruct(shape, bf16) for shape in shapes]
     if first:
         in_specs = [pl.BlockSpec((rows,), line), whole, pl.BlockSpec((width,), line)]
         out_specs += [whole, square, square, smem]
@@ -242,7 +245,7 @@
             out_refs[0 if ordered else k][block, part * piece : (part + 1) * piece, :] = kept
 
 
-def attend(place, queries, low_lane, keyvals, shards, ordered):
+def attend(place, queries, which, low_lane, keyvals, shards, ordered):
     groups = len(queries)
     rows = keyvals[0].shape[1]
     size = keyvals[0].shape[2] // 2
@@ -265,7 +268,7 @@
         grid_spec=pltpu.PrefetchScalarGridSpec(
             num_scalar_prefetch=1,
             grid=(1,),
-            in_specs=[pl.BlockSpec(query_block, lambda i, place: (0, 0, 0))] * groups
+            in_specs=[pl.BlockSpec(query_block, lambda i, place: (which, 0, 0))] * groups
             + [pl.BlockSpec(keyvals[0].shape, lambda i, place: (0, 0, 0))] * len(keyvals),
             out_specs=[pl.BlockSpec((wide, rows, size), lambda i, place: (0, 0, 0))] * outs,
             scratch_shapes=[
@@ -360,7 +363,7 @@
             scratch_shapes=[pltpu.VMEM((rows, depth), bf16)],
         ),
         out_shape=jax.ShapeDtypeStruct((rows, out_width), bf16 if last else f32),
-        compiler_params=params,
+        compiler_params=pltpu.CompilerParams(vmem_limit_bytes=40 * mib),
         cost_estimate=cost(
             2 * rows * depth * head_shards * out_width,
             2 * depth * head_shards * out_width + 8 * rows * out_width,
@@ -373,14 +376,15 @@
     return head_shards == 2 and out_width % 256 == 0
 
 
-def fetch_weights(w_out, me, side, head_shards):
+def fetch_weights(w_out, me, side, head_shards, arrived):
     depth, width = w_out.shape
     out_width = width // head_shards
     if not splits(out_width, head_shards):
         blocks = jnp.transpose(w_out.reshape(depth, head_shards, out_width), (1, 0, 2))
         return lax.all_to_all(blocks, "head", split_axis=0, concat_axis=0, tiled=True)
     half = out_width // 2
-    column = (1 - side) * out_width + (me % 2) * half
+    nothing = jnp.minimum(jnp.abs(arrived[0, 0, 0]).astype(jnp.int32), 0)
+    column = (1 - side) * out_width + (me % 2) * half + nothing
     return lax.all_gather(lax.dynamic_slice(w_out, (0, column), (depth, half)), "head")
 
 
@@ -442,16 +446,16 @@
         return swap(list(chain(tuple(blocks), *earlier)) if earlier else blocks)
 
     operands = (survive, tokens, norm_gain)
-    sets = [((1, 2, 0), 0)]
+    sets = [((1, 2, 0), (0,))]
     (blocks,), rest = project(place, None, weights, gains, sets, groups, operands)
     normed, chosen, back, count = rest
     arrived = [swap(blocks)]
-    fetched = fetch_weights(chain(w_out, later(count)), me, side, head_shards)
-
-    rest, asked = range(1, chunks), []
+    fetched = fetch_weights(w_out, me, side, head_shards, first(arrived[0]))
+
+    rest, asked, hops = range(1, chunks), None, []
     if chunks > 1:
         prepared = (count, chain(normed, first(arrived[0])), chosen)
-        sets = [((1, 2), chunk) for chunk in rest]
+        sets = [((1, 2), (chunk,)) for chunk in rest]
         made, _ = project(place, prepared, weights, gains, sets, groups)
         stacks = [stack(list(chain(tuple(arrived[0]), made[0][0])))]
         arrived.append(send(made[0]))
@@ -460,12 +464,12 @@
         hop = flip(stacks[0], "seq", ring // 2) if ring > 1 else stacks[0]
         stacks.append(stack(arrived[1]))
         ready = later(count, hop, stacks[1])
-        sets = [((0,), chunk) for chunk in rest]
-        made, _ = project(place, (ready, normed, chosen), weights, gains, sets, groups)
-        gate = made[0][0]
+        sets = [((0,), tuple(rest))]
+        (made,), _ = project(place, (ready, normed, chosen), weights, gains, sets, groups)
+        gate = made[0]
         stacks += [stack(blocks) for blocks in arrived[2:]]
-        for blocks in made:
-            asked.append(send(blocks, first(asked[-1]) if asked else stacks[-1]))
+        asked = send(made, stacks[-1])
+        hops = [flip(stacks[-1], "seq", ring // 2)] if ring > 1 else []
     else:
         gate, stacks = None, [stack(arrived[0])]
 
@@ -474,24 +478,24 @@
     for chunk in range(chunks):
         final = chunk == chunks - 1
         keyvals = everywhere(stacks[chunk], gate)
-        before = (stacks[-1],) + tuple(attended[-1:]) + tuple(returned[:1] if final else [])
+        before = [stacks[-1]] + attended[-1:] + (hops if chunk else []) + (returned[:1] if final else [])
         ready = later(place, *query[1:], *before)
-        found = attend(ready, query, low_lane, keyvals, shards, not final)
+        row = max(chunk - 1, 0)
+        found = attend(ready, query, row, low_lane, keyvals, shards, not final)
         attended.append(found[0])
-        if chunk == max(chunks - 2, 0):
-            out_width = w_out.shape[1] // head_shards
-            other_weights = share_weights(chain(fetched, found[0]), out_width, head_shards)
-        if final:
-            returned.append(jnp.concatenate(swap(found)))
-        else:
-            returned.append(send_back(found[0]))
-            query, low_lane = asked[chunk], 0
-            gate = tuple(query)
+        returned.append(jnp.concatenate(swap(found)) if final else send_back(found[0]))
+        if not final:
+            query, low_lane = asked, 0
+            gate = tuple(asked)
+    out_width = w_out.shape[1] // head_shards
+    if chunks > 1:
+        fetched = chain(fetched, first(asked))
+    other_weights = share_weights(fetched, out_width, head_shards)
     total = None
     if chunks > 1:
         sooner = [across(found) for found in returned[:-1]]
         total = finish(place, None, sooner, w_out, other_weights, None, 0, True)
-    last = across(returned[-1] if total is None else chain(returned[-1], total))
+    last = across(returned[-1])
     return finish(place, total, [last], w_out, other_weights, back, chunks - 1, False)
 
 

time: 226 us -> 231 us (1.022)
  the two profiles are of different devices: /device:TPU:0 before, /device:TPU:6 now
where the time goes in v4:
time: 231 us; the launch traced here: 230 us
  Pallas kernels  80.4 us (35%)
  waiting for transfers between devices  61.8 us (27%)
  starting transfers between devices  56.4 us (24%)
  between operations  15 us (6%)
  local copies, waits for them, and re-layouts  14 us (6%)
    ppermute x27, waiting for transfers between devices, flip(): return lax.ppermute(values, axis, [(i, i ^ mask) for i in range(size)])  61.8 us
    ppermute x27, starting transfers between devices, flip(): return lax.ppermute(values, axis, [(i, i ^ mask) for i in range(size)])  47.8 us
    pallas_call x3, Pallas kernels, project(): pl.pallas_call(functools.partial(project_body, steps=steps, groups=groups...  36 us
    pallas_call x3, Pallas kernels, attend(): pl.pallas_call(functools.partial(attend_body, groups=groups, ordered=orde...  33.9 us
    pallas_call x2, Pallas kernels, finish(): pl.pallas_call(functools.partial(finish_body, chunks=chunks, others=head_...  10.5 us
    unnamed x59, local copies, waits for them, and re-layouts  8.87 us
    all_to_all x2, starting transfers between devices, send_back(): lax.all_to_all(blocks, 'seq', split_axis=0, concat_axis=0, axis_index_gro...  8.44 us
  transfers between devices with their start and end apart: 31, of which 13 were waited for; matrix products, arithmetic and copies ran while one was open for 1% of the time, Pallas kernels for 27%

profile of v4, /device:TPU:6, one launch (start us, length us, event | category | flops | bytes accessed | tf_op | source)
XLA Modules:
  0.0 230.0 jit_solution(7815481524754702233)
XLA Ops:
  6.5 0.7 pad_add_fusion.place_ref
  7.2 13.4 %project.3 = (bf16[1,384,384]{2,1,0:T(8,128)(2,1)}, bf16[1,384,384]{2,1,0:T(8,128)(2,1)}, bf16[1,384,384]{2,1,0:T(8,128)(2,1)}, bf16[1,384,384]{2,1,0:T(8,128)(2...) custom-call(s32[3]{0:T(128)} %pad_add_fusion.place_ref, ...), custom_call_target="tpu_custom_call" | custom-call | flops 3623878656 | bytes 11796480 | tf_op jit(solution)/shard_map/project/pallas_call | solution.py:143
  20.6 1.6 collective-permute-start
  22.2 7.4 %collective-permute-done.refs_1_ = bf16[1,384,384]{2,1,0:T(8,128)(2,1)S(1)} collective-permute-done((bf16[1,384,384]{2,1,0:T(8,128)(2,1)}, bf16[1,384,384]{2,1,0:T(8,128)(2,1)S(1)}, u32[]{:S(2)}, u32[]{:S(2)}) %collective-permute-start) | collective-permute-done | bytes 294944 | tf_op jit(solution)/shard_map/ppermute | solution.py:28
  30.8 4.5 %constant_dynamic-slice_fusion = bf16[1536,768]{1,0:T(8,128)(2,1)} fusion(bf16[1536,3072]{1,0:T(8,128)(2,1)} %refs_2_.5, s32[]{:T(128)S(6)} %select_n.21), kind=kLoop, calls=%fused_computation.17 | loop fusion | bytes 4718596 | tf_op jit(solution)/shard_map/dynamic_slice | solution.py:388
  35.6 0.7 copy-done.17
  36.3 2.6 %collective-permute-start.1 = (bf16[1,384,384]{2,1,0:T(8,128)(2,1)S(1)}, bf16[1,384,384]{2,1,0:T(8,128)(2,1)S(1)}, u32[]{:S(2)}, u32[]{:S(2)}) collective-permute-start(bf16[1,384,384]{2,1,0:T(8,128)(2,1)S(1)} %copy-done.17), channel_id=1, source_target_pairs={{0,16},{2,18},{4,20},{6,22},{8,24},{10,26},{12,28},{14,30},{16,0},... | collective-permute-start | bytes 884744 | tf_op jit(solution)/shard_map/ppermute | solution.py:28
  38.9 1.3 collective-permute-start.2
  40.2 14.1 %project.4 = (bf16[1,384,256]{2,1,0:T(8,128)(2,1)}, bf16[1,384,256]{2,1,0:T(8,128)(2,1)}, bf16[1,384,256]{2,1,0:T(8,128)(2,1)}, bf16[1,384,256]{2,1,0:T(8,128)(2...) custom-call(s32[3]{0:T(128)} %pad_add_fusion.place_ref, ...), custom_call_target="tpu_custom_call" | custom-call | flops 4831838208 | bytes 14942208 | tf_op jit(solution)/shard_map/project/pallas_call | solution.py:143
  54.4 2.7 %collective-permute-start.8 = (bf16[1,384,256]{2,1,0:T(8,128)(2,1)}, bf16[1,384,256]{2,1,0:T(8,128)(2,1)S(1)}, u32[]{:S(2)}, u32[]{:S(2)}) collective-permute-start(bf16[1,384,256]{2,1,0:T(8,128)(2,1)} %get-tuple-element.76), channel_id=1, source_target_pairs={{0,16},{2,18},{4,20},{6,22},{8,24},{10,26},{12,28},{14,30},{16,0},... | collective-permute-start | bytes 589832 | tf_op jit(solution)/shard_map/ppermute | solution.py:28
  57.2 1.7 collective-permute-start.9
  58.8 1.1 collective-permute-done.1.refs_2_
  60.2 0.6 collective-permute-start.7
  60.8 1.2 collective-permute-done.3
  61.9 13.2 %collective-permute-start.4 = (bf16[1,384,256]{2,1,0:T(8,128)(2,1)S(1)}, bf16[1,384,256]{2,1,0:T(8,128)(2,1)S(1)}, u32[]{:S(2)}, u32[]{:S(2)}) collective-permute-start(bf16[1,384,256]{2,1,0:T(8,128)(2,1)S(1)} %copy-done.23), channel_id=1, source_target_pairs={{0,8},{2,10},{4,12},{6,14},{8,0},{10,2},{12,4},{14,6},{16,24},{18,... | collective-permute-start | bytes 589832 | tf_op jit(solution)/shard_map/ppermute | solution.py:28
  75.1 1.1 collective-permute-start.5
  76.2 1.6 collective-permute-done.8
  77.8 2.5 %collective-permute-start.6 = (bf16[1,384,256]{2,1,0:T(8,128)(2,1)S(1)}, bf16[1,384,256]{2,1,0:T(8,128)(2,1)S(1)}, u32[]{:S(2)}, u32[]{:S(2)}) collective-permute-start(bf16[1,384,256]{2,1,0:T(8,128)(2,1)S(1)} %copy-done.21), channel_id=1, source_target_pairs={{0,24},{2,26},{4,28},{6,30},{8,16},{10,18},{12,20},{14,22},{16,8},... | collective-permute-start | bytes 589832 | tf_op jit(solution)/shard_map/ppermute | solution.py:28
  80.4 1.2 collective-permute-done.4
  81.7 13.0 %collective-permute-done.5 = bf16[1,384,256]{2,1,0:T(8,128)(2,1)S(1)} collective-permute-done((bf16[1,384,256]{2,1,0:T(8,128)(2,1)S(1)}, bf16[1,384,256]{2,1,0:T(8,128)(2,1)S(1)}, u32[]{:S(2)}, u32[]{:S(2)}) %collective-permute-start.5) | collective-permute-done | bytes 196640 | tf_op jit(solution)/shard_map/ppermute | solution.py:28
  94.8 0.9 copy-done.12
  96.3 8.6 %project.5 = (bf16[2,384,128]{2,1,0:T(8,128)(2,1)}, bf16[2,384,128]{2,1,0:T(8,128)(2,1)}, bf16[2,384,128]{2,1,0:T(8,128)(2,1)}, bf16[2,384,128]{2,1,0:T(8,128)(2,1)}) custom-call(s32[3]{0:T(128)} %pad_add_fusion.place_ref, bf16[3,3072,1536]{2,1,0:T(8,128)(2,1)} %bitcast.10, f32[12,2,128]{2,1,0:T(2,128)} %bitcast.16, s32[1,1]{1,0:T(1,128)S(6)} %max.13.refs_2_, ...), custom_call_target="tpu_custom_call" | custom-call | flops 2415919104 | bytes 8650752 | tf_op jit(solution)/shard_map/project/pallas_call | solution.py:143
  104.8 3.8 %collective-permute-start.12 = (bf16[2,384,128]{2,1,0:T(8,128)(2,1)}, bf16[2,384,128]{2,1,0:T(8,128)(2,1)S(1)}, u32[]{:S(2)}, u32[]{:S(2)}) collective-permute-start(bf16[2,384,128]{2,1,0:T(8,128)(2,1)} %get-tuple-element.85), channel_id=1, source_target_pairs={{0,8},{2,10},{4,12},{6,14},{8,0},{10,2},{12,4},{14,6},{16,24},{18,... | collective-permute-start | bytes 589832 | tf_op jit(solution)/shard_map/ppermute | solution.py:28
  108.6 5.3 %collective-permute-done.12.refs_1_ = bf16[2,384,128]{2,1,0:T(8,128)(2,1)S(1)} collective-permute-done((bf16[2,384,128]{2,1,0:T(8,128)(2,1)}, bf16[2,384,128]{2,1,0:T(8,128)(2,1)S(1)}, u32[]{:S(2)}, u32[]{:S(2)}) %collective-permute-start.12) | collective-permute-done | bytes 196640 | tf_op jit(solution)/shard_map/ppermute | solution.py:28
  113.9 0.6 copy-done.18
  115.6 3.8 %collective-permute-start.13 = (bf16[2,384,128]{2,1,0:T(8,128)(2,1)S(1)}, bf16[2,384,128]{2,1,0:T(8,128)(2,1)S(1)}, u32[]{:S(2)}, u32[]{:S(2)}) collective-permute-start(bf16[2,384,128]{2,1,0:T(8,128)(2,1)S(1)} %copy-done.24), channel_id=1, source_target_pairs={{0,16},{2,18},{4,20},{6,22},{8,24},{10,26},{12,28},{14,30},{16,0},... | collective-permute-start | bytes 589832 | tf_op jit(solution)/shard_map/ppermute | solution.py:28
  119.4 1.5 collective-permute-start.15
  120.9 7.9 %collective-permute-done.13.refs_2_ = bf16[2,384,128]{2,1,0:T(8,128)(2,1)S(1)} collective-permute-done((bf16[2,384,128]{2,1,0:T(8,128)(2,1)S(1)}, bf16[2,384,128]{2,1,0:T(8,128)(2,1)S(1)}, u32[]{:S(2)}, u32[]{:S(2)}) %collective-permute-start.13) | collective-permute-done | bytes 196640 | tf_op jit(solution)/shard_map/ppermute | solution.py:28
  128.7 2.4 %collective-permute-start.14 = (bf16[2,384,128]{2,1,0:T(8,128)(2,1)}, bf16[2,384,128]{2,1,0:T(8,128)(2,1)S(1)}, u32[]{:S(2)}, u32[]{:S(2)}) collective-permute-start(bf16[2,384,128]{2,1,0:T(8,128)(2,1)} %get-tuple-element.87), channel_id=1, source_target_pairs={{0,24},{2,26},{4,28},{6,30},{8,16},{10,18},{12,20},{14,22},{16,8},... | collective-permute-start | bytes 589832 | tf_op jit(solution)/shard_map/ppermute | solution.py:28
  131.1 6.5 %collective-permute-done.14.refs_3_ = bf16[2,384,128]{2,1,0:T(8,128)(2,1)S(1)} collective-permute-done((bf16[2,384,128]{2,1,0:T(8,128)(2,1)}, bf16[2,384,128]{2,1,0:T(8,128)(2,1)S(1)}, u32[]{:S(2)}, u32[]{:S(2)}) %collective-permute-start.14) | collective-permute-done | bytes 196640 | tf_op jit(solution)/shard_map/ppermute | solution.py:28
  138.6 0.9 copy-done.14
  139.5 11.6 %attend.3 = bf16[4,384,128]{2,1,0:T(8,128)(2,1)} custom-call(s32[3]{0:T(128)} %broadcast_maximum_fusion.2.place_ref, bf16[1,384,384]{2,1,0:T(8,128)(2,1)} %get-tuple-element.72.refs_0_, bf16[1,384,384]{2,1,0:T(8,128)(2,1)} %copy-done.7, bf16[1,384,384]{2,1,0:T(8,128)(2,1)} %copy-done.8, bf16[1,384,384]{2,1,0:T(8,128)(2,1)} %copy-done.9, ...), custom_call_target="tpu_custom_call" | custom-call | flops 2415919104 | bytes 3145728 | tf_op jit(solution)/shard_map/attend/pallas_call | solution.py:258
  151.1 3.5 %all-to-all-start = ((bf16[4,384,128]{2,1,0:T(8,128)(2,1)}), bf16[4,384,128]{2,1,0:T(8,128)(2,1)S(1)}, u32[]{:S(2)}, u32[]{:S(2)}) async-start(bf16[4,384,128]{2,1,0:T(8,128)(2,1)} %attend.3), calls=%async_computation | async-start | bytes 786432 | tf_op jit(solution)/shard_map/all_to_all | solution.py:429
  155.7 11.2 %attend.4 = bf16[4,384,128]{2,1,0:T(8,128)(2,1)} custom-call(s32[3]{0:T(128)} %broadcast_maximum_fusion.1.place_ref, bf16[2,384,128]{2,1,0:T(8,128)(2,1)} %get-tuple-element.89.refs_0_, bf16[2,384,128]{2,1,0:T(8,128)(2,1)} %copy-done.18, bf16[2,384,128]{2,1,0:T(8,128)(2,1)} %copy-done.19, bf16[2,384,128]{2,1,0:T(8,128)(2,1)} %copy-done.20, ...), custom_call_target="tpu_custom_call" | custom-call | flops 2415919104 | bytes 3145728 | tf_op jit(solution)/shard_map/attend/pallas_call | solution.py:258
  166.9 5.0 %all-to-all-start.1 = ((bf16[4,384,128]{2,1,0:T(8,128)(2,1)}), bf16[4,384,128]{2,1,0:T(8,128)(2,1)S(1)}, u32[]{:S(2)}, u32[]{:S(2)}) async-start(bf16[4,384,128]{2,1,0:T(8,128)(2,1)} %attend.4), calls=%async_computation.1 | async-start | bytes 786432 | tf_op jit(solution)/shard_map/all_to_all | solution.py:429
  172.4 0.9 copy-done.15
  173.3 11.1 %attend.5 = (bf16[1,384,128]{2,1,0:T(8,128)(2,1)}, bf16[1,384,128]{2,1,0:T(8,128)(2,1)}, bf16[1,384,128]{2,1,0:T(8,128)(2,1)}, bf16[1,384,128]{2,1,0:T(8,128)(2,1)}) custom-call(s32[3]{0:T(128)} %broadcast_maximum_fusion.place_ref, bf16[2,384,128]{2,1,0:T(8,128)(2,1)} %get-tuple-element.89.refs_0_, bf16[2,384,128]{2,1,0:T(8,128)(2,1)} %copy-done.18, ...), custom_call_target="tpu_custom_call" | custom-call | flops 2415919104 | bytes 3145728 | tf_op jit(solution)/shard_map/attend/pallas_call | solution.py:258
  184.3 2.0 collective-permute-start.23
  186.4 2.4 %collective-permute-start.24 = (bf16[1,384,128]{2,1,0:T(8,128)(2,1)}, bf16[1,384,128]{2,1,0:T(8,128)(2,1)S(1)}, u32[]{:S(2)}, u32[]{:S(2)}) collective-permute-start(bf16[1,384,128]{2,1,0:T(8,128)(2,1)} %get-tuple-element.98), channel_id=1, source_target_pairs={{0,16},{2,18},{4,20},{6,22},{8,24},{10,26},{12,28},{14,30},{16,0},... | collective-permute-start | bytes 294920 | tf_op jit(solution)/shard_map/ppermute | solution.py:28
  189.2 0.9 constant_dynamic-update-slice_fusion.11
  190.2 1.7 collective-permute-start.20
  191.8 1.5 collective-permute-done.24
  193.3 2.1 collective-permute-done.25
  195.9 4.9 %collective-permute-done.19.refs_3_ = bf16[4,384,128]{2,1,0:T(8,128)(2,1)S(1)} collective-permute-done((bf16[4,384,128]{2,1,0:T(8,128)(2,1)S(1)}, bf16[4,384,128]{2,1,0:T(8,128)(2,1)S(1)}, u32[]{:S(2)}, u32[]{:S(2)}) %collective-permute-start.19) | collective-permute-done | bytes 393248 | tf_op jit(solution)/shard_map/ppermute | solution.py:28
  200.8 8.1 %collective-permute-done.20.refs_4_ = bf16[4,384,128]{2,1,0:T(8,128)(2,1)S(1)} collective-permute-done((bf16[4,384,128]{2,1,0:T(8,128)(2,1)S(1)}, bf16[4,384,128]{2,1,0:T(8,128)(2,1)S(1)}, u32[]{:S(2)}, u32[]{:S(2)}) %collective-permute-start.20) | collective-permute-done | bytes 393248 | tf_op jit(solution)/shard_map/ppermute | solution.py:28
  208.9 3.7 %copy-done = bf16[1536,3072]{1,0:T(8,128)(2,1)S(1)} copy-done((bf16[1536,3072]{1,0:T(8,128)(2,1)S(1)}, bf16[1536,3072]{1,0:T(8,128)(2,1)}, u32[]{:S(2)}) %copy-start) | copy-done | bytes 9437208
  212.6 5.4 %finish.2.refs_0_ = f32[384,1536]{1,0:T(8,128)S(1)} custom-call(s32[3]{0:T(128)S(1)} %copy-done.2, bf16[4,384,128]{2,1,0:T(8,128)(2,1)S(1)} %all-to-all-done.refs_0_, bf16[4,384,128]{2,1,0:T(8,128)(2,1)S(1)} %all-to-all-done.1.refs_1_, bf16[1536,3072]{1,0:T(8,128)(2,1)S(1)} %copy-done, bf16[4,384,128]{2,1,0:T(8,128)(2,1)S(1)} %collective-permute-done.19.refs_3_, ...), custom_call_target="tpu_custom_call" | custom-call | flops 2415919104 | bytes 11010048 | tf_op jit(solution)/shard_map/finish/pallas_call | solution.py:349
  218.0 5.2 %finish.3 = bf16[384,1536]{1,0:T(8,128)(2,1)} custom-call(s32[3]{0:T(128)S(1)} %copy-done.2, f32[384,1536]{1,0:T(8,128)S(1)} %finish.2.refs_0_, bf16[4,384,128]{2,1,0:T(8,128)(2,1)S(1)} %constant_dynamic-update-slice_fusion.8.refs_1_, bf16[1536,3072]{1,0:T(8,128)(2,1)S(1)} %copy-done, bf16[4,384,128]{2,1,0:T(8,128)(2,1)S(1)} %collective-permute-done.26.refs_3_, ...), custom_call_target="tpu_custom_call" | custom-call | flops 1207959552 | bytes 7864320 | tf_op jit(solution)/shard_map/finish/pallas_call | solution.py:349
  (97 shorter events, 5.9 us)
Async XLA Ops:
  6.5 107.4 %all-gather.5.cloned.1.call-start = ((), (), s32[]{:S(2)}) async-start(), calls=%async_computation.2 | async-start | bytes 7077888 | tf_op jit(solution)/shard_map/all_gather | solution.py:388
  20.6 9.0 %collective-permute-start = (bf16[1,384,384]{2,1,0:T(8,128)(2,1)}, bf16[1,384,384]{2,1,0:T(8,128)(2,1)S(1)}, u32[]{:S(2)}, u32[]{:S(2)}) collective-permute-start(bf16[1,384,384]{2,1,0:T(8,128)(2,1)} %get-tuple-element.53), channel_id=1, source_target_pairs={{0,8},{2,10},{4,12},{6,14},{8,0},{10,2},{12,4},{14,6},{16,24},{18,... | collective-permute-start | bytes 884744 | tf_op jit(solution)/shard_map/ppermute | solution.py:28
  29.6 30.4 %copy-start.7 = (bf16[1,384,384]{2,1,0:T(8,128)(2,1)}, bf16[1,384,384]{2,1,0:T(8,128)(2,1)S(1)}, u32[]{:S(2)}) copy-start(bf16[1,384,384]{2,1,0:T(8,128)(2,1)S(1)} %collective-permute-done.refs_1_) | copy-start | bytes 884740
  35.4 173.6 %all-gather.7.cloned.1.call-start = ((), (), s32[]{:S(2)}) async-start(), calls=%async_computation.3 | async-start | bytes 14155776 | tf_op jit(solution)/shard_map/all_gather | solution.py:395
  36.3 23.6 %collective-permute-start.1 = (bf16[1,384,384]{2,1,0:T(8,128)(2,1)S(1)}, bf16[1,384,384]{2,1,0:T(8,128)(2,1)S(1)}, u32[]{:S(2)}, u32[]{:S(2)}) collective-permute-start(bf16[1,384,384]{2,1,0:T(8,128)(2,1)S(1)} %copy-done.17), channel_id=1, source_target_pairs={{0,16},{2,18},{4,20},{6,22},{8,24},{10,26},{12,28},{14,30},{16,0},... | collective-permute-start | bytes 884744 | tf_op jit(solution)/shard_map/ppermute | solution.py:28
  38.9 21.0 %collective-permute-start.2 = (bf16[1,384,384]{2,1,0:T(8,128)(2,1)S(1)}, bf16[1,384,384]{2,1,0:T(8,128)(2,1)S(1)}, u32[]{:S(2)}, u32[]{:S(2)}) collective-permute-start(bf16[1,384,384]{2,1,0:T(8,128)(2,1)S(1)} %copy-done.16), channel_id=1, source_target_pairs={{0,24},{2,26},{4,28},{6,30},{8,16},{10,18},{12,20},{14,22},{16,8},... | collective-permute-start | bytes 884744 | tf_op jit(solution)/shard_map/ppermute | solution.py:28
  40.2 19.7 %copy-start.6 = (bf16[1,384,384]{2,1,0:T(8,128)(2,1)S(1)}, bf16[1,384,384]{2,1,0:T(8,128)(2,1)}, u32[]{:S(2)}) copy-start(bf16[1,384,384]{2,1,0:T(8,128)(2,1)} %get-tuple-element.72.refs_0_) | copy-start | bytes 884740
  54.3 6.4 %copy-start.5 = (bf16[1,384,256]{2,1,0:T(8,128)(2,1)S(1)}, bf16[1,384,256]{2,1,0:T(8,128)(2,1)}, u32[]{:S(2)}) copy-start(bf16[1,384,256]{2,1,0:T(8,128)(2,1)} %get-tuple-element.71) | copy-start | bytes 589828
  54.3 7.6 %copy-start.23 = (bf16[1,384,256]{2,1,0:T(8,128)(2,1)S(1)}, bf16[1,384,256]{2,1,0:T(8,128)(2,1)}, u32[]{:S(2)}) copy-start(bf16[1,384,256]{2,1,0:T(8,128)(2,1)} %get-tuple-element.66) | copy-start | bytes 589828
  54.3 20.8 %copy-start.22 = (bf16[1,384,256]{2,1,0:T(8,128)(2,1)S(1)}, bf16[1,384,256]{2,1,0:T(8,128)(2,1)}, u32[]{:S(2)}) copy-start(bf16[1,384,256]{2,1,0:T(8,128)(2,1)} %get-tuple-element.67) | copy-start | bytes 589828
  54.3 21.8 %copy-start.4 = (bf16[1,384,256]{2,1,0:T(8,128)(2,1)S(1)}, bf16[1,384,256]{2,1,0:T(8,128)(2,1)}, u32[]{:S(2)}) copy-start(bf16[1,384,256]{2,1,0:T(8,128)(2,1)} %get-tuple-element.65) | copy-start | bytes 589828
  54.3 23.5 %copy-start.21 = (bf16[1,384,256]{2,1,0:T(8,128)(2,1)S(1)}, bf16[1,384,256]{2,1,0:T(8,128)(2,1)}, u32[]{:S(2)}) copy-start(bf16[1,384,256]{2,1,0:T(8,128)(2,1)} %get-tuple-element.68) | copy-start | bytes 589828
  54.4 7.6 %collective-permute-start.3 = (bf16[1,384,256]{2,1,0:T(8,128)(2,1)}, bf16[1,384,256]{2,1,0:T(8,128)(2,1)S(1)}, u32[]{:S(2)}, u32[]{:S(2)}) collective-permute-start(bf16[1,384,256]{2,1,0:T(8,128)(2,1)} %get-tuple-element.64), channel_id=1, source_target_pairs={{0,8},{2,10},{4,12},{6,14},{8,0},{10,2},{12,4},{14,6},{16,24},{18,... | collective-permute-start | bytes 589832 | tf_op jit(solution)/shard_map/ppermute | solution.py:28
  54.4 23.4 %collective-permute-start.8 = (bf16[1,384,256]{2,1,0:T(8,128)(2,1)}, bf16[1,384,256]{2,1,0:T(8,128)(2,1)S(1)}, u32[]{:S(2)}, u32[]{:S(2)}) collective-permute-start(bf16[1,384,256]{2,1,0:T(8,128)(2,1)} %get-tuple-element.76), channel_id=1, source_target_pairs={{0,16},{2,18},{4,20},{6,22},{8,24},{10,26},{12,28},{14,30},{16,0},... | collective-permute-start | bytes 589832 | tf_op jit(solution)/shard_map/ppermute | solution.py:28
  57.2 23.2 %collective-permute-start.9 = (bf16[1,384,256]{2,1,0:T(8,128)(2,1)}, bf16[1,384,256]{2,1,0:T(8,128)(2,1)S(1)}, u32[]{:S(2)}, u32[]{:S(2)}) collective-permute-start(bf16[1,384,256]{2,1,0:T(8,128)(2,1)} %get-tuple-element.77), channel_id=1, source_target_pairs={{0,24},{2,26},{4,28},{6,30},{8,16},{10,18},{12,20},{14,22},{16,8},... | collective-permute-start | bytes 589832 | tf_op jit(solution)/shard_map/ppermute | solution.py:28
  59.9 20.4 %copy-start.8 = (bf16[1,384,384]{2,1,0:T(8,128)(2,1)}, bf16[1,384,384]{2,1,0:T(8,128)(2,1)S(1)}, u32[]{:S(2)}) copy-start(bf16[1,384,384]{2,1,0:T(8,128)(2,1)S(1)} %collective-permute-done.1.refs_2_) | copy-start | bytes 884740
  59.9 20.5 %copy-start.9 = (bf16[1,384,384]{2,1,0:T(8,128)(2,1)}, bf16[1,384,384]{2,1,0:T(8,128)(2,1)S(1)}, u32[]{:S(2)}) copy-start(bf16[1,384,384]{2,1,0:T(8,128)(2,1)S(1)} %collective-permute-done.2.refs_3_) | copy-start | bytes 884740
  60.1 55.0 %copy-start.3 = (bf16[4,384,256]{2,1,0:T(8,128)(2,1)}, bf16[4,384,256]{2,1,0:T(8,128)(2,1)S(1)}, u32[]{:S(2)}) copy-start(bf16[4,384,256]{2,1,0:T(8,128)(2,1)S(1)} %pad_maximum_fusion.refs_4_) | copy-start | bytes 2359300
  60.2 34.6 %collective-permute-start.7 = (bf16[4,384,256]{2,1,0:T(8,128)(2,1)S(1)}, bf16[4,384,256]{2,1,0:T(8,128)(2,1)S(1)}, u32[]{:S(2)}, u32[]{:S(2)}) collective-permute-start(bf16[4,384,256]{2,1,0:T(8,128)(2,1)S(1)} %pad_maximum_fusion.refs_4_), channel_id=1, source_target_pairs={{0,4},{2,6},{4,0},{6,2},{8,12},{10,14},{12,8},{14,10},{16,20},{18,... | collective-permute-start | bytes 2359304 | tf_op jit(solution)/shard_map/ppermute | solution.py:28
  61.9 19.7 %collective-permute-start.4 = (bf16[1,384,256]{2,1,0:T(8,128)(2,1)S(1)}, bf16[1,384,256]{2,1,0:T(8,128)(2,1)S(1)}, u32[]{:S(2)}, u32[]{:S(2)}) collective-permute-start(bf16[1,384,256]{2,1,0:T(8,128)(2,1)S(1)} %copy-done.23), channel_id=1, source_target_pairs={{0,8},{2,10},{4,12},{6,14},{8,0},{10,2},{12,4},{14,6},{16,24},{18,... | collective-permute-start | bytes 589832 | tf_op jit(solution)/shard_map/ppermute | solution.py:28
  75.1 19.6 %collective-permute-start.5 = (bf16[1,384,256]{2,1,0:T(8,128)(2,1)S(1)}, bf16[1,384,256]{2,1,0:T(8,128)(2,1)S(1)}, u32[]{:S(2)}, u32[]{:S(2)}) collective-permute-start(bf16[1,384,256]{2,1,0:T(8,128)(2,1)S(1)} %copy-done.22), channel_id=1, source_target_pairs={{0,16},{2,18},{4,20},{6,22},{8,24},{10,26},{12,28},{14,30},{16,0},... | collective-permute-start | bytes 589832 | tf_op jit(solution)/shard_map/ppermute | solution.py:28
  77.8 16.9 %collective-permute-start.6 = (bf16[1,384,256]{2,1,0:T(8,128)(2,1)S(1)}, bf16[1,384,256]{2,1,0:T(8,128)(2,1)S(1)}, u32[]{:S(2)}, u32[]{:S(2)}) collective-permute-start(bf16[1,384,256]{2,1,0:T(8,128)(2,1)S(1)} %copy-done.21), channel_id=1, source_target_pairs={{0,24},{2,26},{4,28},{6,30},{8,16},{10,18},{12,20},{14,22},{16,8},... | collective-permute-start | bytes 589832 | tf_op jit(solution)/shard_map/ppermute | solution.py:28
  80.4 57.2 %copy-start.11 = (bf16[4,384,256]{2,1,0:T(8,128)(2,1)}, bf16[4,384,256]{2,1,0:T(8,128)(2,1)S(1)}, u32[]{:S(2)}) copy-start(bf16[4,384,256]{2,1,0:T(8,128)(2,1)S(1)} %constant_dynamic-update-slice_fusion.4.refs_4_) | copy-start | bytes 2359300
  94.7 59.9 %copy-start.10 = (bf16[4,384,256]{2,1,0:T(8,128)(2,1)}, bf16[4,384,256]{2,1,0:T(8,128)(2,1)S(1)}, u32[]{:S(2)}) copy-start(bf16[4,384,256]{2,1,0:T(8,128)(2,1)S(1)} %constant_dynamic-update-slice_fusion.refs_4_) | copy-start | bytes 2359300
  104.8 9.1 %collective-permute-start.12 = (bf16[2,384,128]{2,1,0:T(8,128)(2,1)}, bf16[2,384,128]{2,1,0:T(8,128)(2,1)S(1)}, u32[]{:S(2)}, u32[]{:S(2)}) collective-permute-start(bf16[2,384,128]{2,1,0:T(8,128)(2,1)} %get-tuple-element.85), channel_id=1, source_target_pairs={{0,8},{2,10},{4,12},{6,14},{8,0},{10,2},{12,4},{14,6},{16,24},{18,... | collective-permute-start | bytes 589832 | tf_op jit(solution)/shard_map/ppermute | solution.py:28
  113.9 24.2 %copy-start.2 = (s32[3]{0:T(128)S(1)}, s32[3]{0:T(128)}, u32[]{:S(2)}) copy-start(s32[3]{0:T(128)} %pad_add_fusion.place_ref) | copy-start | bytes 40
  114.6 23.0 %collective-permute-start.17 = (bf16[4,384,256]{2,1,0:T(8,128)(2,1)S(1)}, bf16[4,384,256]{2,1,0:T(8,128)(2,1)}, u32[]{:S(2)}, u32[]{:S(2)}) collective-permute-start(bf16[4,384,256]{2,1,0:T(8,128)(2,1)S(1)} %constant_dynamic-update-slice_fusion.4.refs_4_), channel_id=1, source_target_pairs={{0,4},{2,6},{4,0},{6,2},{8,12},{10,14},{12,8},{14,10},{16,20},{18,... | collective-permute-start | bytes 2359304 | tf_op jit(solution)/shard_map/ppermute | solution.py:28
  115.1 23.5 %collective-permute-start.11 = (bf16[4,384,256]{2,1,0:T(8,128)(2,1)S(1)}, bf16[4,384,256]{2,1,0:T(8,128)(2,1)S(1)}, u32[]{:S(2)}, u32[]{:S(2)}) collective-permute-start(bf16[4,384,256]{2,1,0:T(8,128)(2,1)S(1)} %copy-done.13), channel_id=1, source_target_pairs={{0,2},{2,0},{4,6},{6,4},{8,10},{10,8},{12,14},{14,12},{16,18},{18,... | collective-permute-start | bytes 2359304 | tf_op jit(solution)/shard_map/ppermute | solution.py:28
  115.1 24.4 %collective-permute-start.10 = (bf16[4,384,256]{2,1,0:T(8,128)(2,1)S(1)}, bf16[4,384,256]{2,1,0:T(8,128)(2,1)}, u32[]{:S(2)}, u32[]{:S(2)}) collective-permute-start(bf16[4,384,256]{2,1,0:T(8,128)(2,1)S(1)} %pad_maximum_fusion.refs_4_), channel_id=1, source_target_pairs={{0,2},{2,0},{4,6},{6,4},{8,10},{10,8},{12,14},{14,12},{16,18},{18,... | collective-permute-start | bytes 2359304 | tf_op jit(solution)/shard_map/ppermute | solution.py:28
  115.6 13.1 %collective-permute-start.13 = (bf16[2,384,128]{2,1,0:T(8,128)(2,1)S(1)}, bf16[2,384,128]{2,1,0:T(8,128)(2,1)S(1)}, u32[]{:S(2)}, u32[]{:S(2)}) collective-permute-start(bf16[2,384,128]{2,1,0:T(8,128)(2,1)S(1)} %copy-done.24), channel_id=1, source_target_pairs={{0,16},{2,18},{4,20},{6,22},{8,24},{10,26},{12,28},{14,30},{16,0},... | collective-permute-start | bytes 589832 | tf_op jit(solution)/shard_map/ppermute | solution.py:28
  119.4 35.3 %collective-permute-start.15 = (bf16[4,384,256]{2,1,0:T(8,128)(2,1)S(1)}, bf16[4,384,256]{2,1,0:T(8,128)(2,1)}, u32[]{:S(2)}, u32[]{:S(2)}) collective-permute-start(bf16[4,384,256]{2,1,0:T(8,128)(2,1)S(1)} %constant_dynamic-update-slice_fusion.refs_4_), channel_id=1, source_target_pairs={{0,4},{2,6},{4,0},{6,2},{8,12},{10,14},{12,8},{14,10},{16,20},{18,... | collective-permute-start | bytes 2359304 | tf_op jit(solution)/shard_map/ppermute | solution.py:28
  128.7 27.0 %copy-start.19 = (bf16[2,384,128]{2,1,0:T(8,128)(2,1)}, bf16[2,384,128]{2,1,0:T(8,128)(2,1)S(1)}, u32[]{:S(2)}) copy-start(bf16[2,384,128]{2,1,0:T(8,128)(2,1)S(1)} %collective-permute-done.13.refs_2_) | copy-start | bytes 589828
  128.7 8.9 %collective-permute-start.14 = (bf16[2,384,128]{2,1,0:T(8,128)(2,1)}, bf16[2,384,128]{2,1,0:T(8,128)(2,1)S(1)}, u32[]{:S(2)}, u32[]{:S(2)}) collective-permute-start(bf16[2,384,128]{2,1,0:T(8,128)(2,1)} %get-tuple-element.87), channel_id=1, source_target_pairs={{0,24},{2,26},{4,28},{6,30},{8,16},{10,18},{12,20},{14,22},{16,8},... | collective-permute-start | bytes 589832 | tf_op jit(solution)/shard_map/ppermute | solution.py:28
  137.6 18.1 %copy-start.20 = (bf16[2,384,128]{2,1,0:T(8,128)(2,1)}, bf16[2,384,128]{2,1,0:T(8,128)(2,1)S(1)}, u32[]{:S(2)}) copy-start(bf16[2,384,128]{2,1,0:T(8,128)(2,1)S(1)} %collective-permute-done.14.refs_3_) | copy-start | bytes 589828
  137.6 18.1 %collective-permute-start.18 = (bf16[4,384,256]{2,1,0:T(8,128)(2,1)}, bf16[4,384,256]{2,1,0:T(8,128)(2,1)}, u32[]{:S(2)}, u32[]{:S(2)}) collective-permute-start(bf16[4,384,256]{2,1,0:T(8,128)(2,1)} %collective-permute-done.17.refs_6_), channel_id=1, source_target_pairs={{0,2},{2,0},{4,6},{6,4},{8,10},{10,8},{12,14},{14,12},{16,18},{18,... | collective-permute-start | bytes 2359304 | tf_op jit(solution)/shard_map/ppermute | solution.py:28
  137.6 18.1 %collective-permute-start.16 = (bf16[4,384,256]{2,1,0:T(8,128)(2,1)S(1)}, bf16[4,384,256]{2,1,0:T(8,128)(2,1)}, u32[]{:S(2)}, u32[]{:S(2)}) collective-permute-start(bf16[4,384,256]{2,1,0:T(8,128)(2,1)S(1)} %constant_dynamic-update-slice_fusion.4.refs_4_), channel_id=1, source_target_pairs={{0,2},{2,0},{4,6},{6,4},{8,10},{10,8},{12,14},{14,12},{16,18},{18,... | collective-permute-start | bytes 2359304 | tf_op jit(solution)/shard_map/ppermute | solution.py:28
  151.1 15.7 %all-to-all-start = ((bf16[4,384,128]{2,1,0:T(8,128)(2,1)}), bf16[4,384,128]{2,1,0:T(8,128)(2,1)S(1)}, u32[]{:S(2)}, u32[]{:S(2)}) async-start(bf16[4,384,128]{2,1,0:T(8,128)(2,1)} %attend.3), calls=%async_computation | async-start | bytes 786432 | tf_op jit(solution)/shard_map/all_to_all | solution.py:429
  154.6 17.8 %collective-permute-start.21 = (bf16[4,384,256]{2,1,0:T(8,128)(2,1)S(1)}, bf16[4,384,256]{2,1,0:T(8,128)(2,1)S(1)}, u32[]{:S(2)}, u32[]{:S(2)}) collective-permute-start(bf16[4,384,256]{2,1,0:T(8,128)(2,1)S(1)} %constant_dynamic-update-slice_fusion.refs_4_), channel_id=1, source_target_pairs={{0,2},{2,0},{4,6},{6,4},{8,10},{10,8},{12,14},{14,12},{16,18},{18,... | collective-permute-start | bytes 2359304 | tf_op jit(solution)/shard_map/ppermute | solution.py:28
  154.7 17.7 %collective-permute-start.22 = (bf16[4,384,256]{2,1,0:T(8,128)(2,1)}, bf16[4,384,256]{2,1,0:T(8,128)(2,1)}, u32[]{:S(2)}, u32[]{:S(2)}) collective-permute-start(bf16[4,384,256]{2,1,0:T(8,128)(2,1)} %collective-permute-done.15.refs_6_), channel_id=1, source_target_pairs={{0,2},{2,0},{4,6},{6,4},{8,10},{10,8},{12,14},{14,12},{16,18},{18,... | collective-permute-start | bytes 2359304 | tf_op jit(solution)/shard_map/ppermute | solution.py:28
  166.9 23.3 %all-to-all-start.1 = ((bf16[4,384,128]{2,1,0:T(8,128)(2,1)}), bf16[4,384,128]{2,1,0:T(8,128)(2,1)S(1)}, u32[]{:S(2)}, u32[]{:S(2)}) async-start(bf16[4,384,128]{2,1,0:T(8,128)(2,1)} %attend.4), calls=%async_computation.1 | async-start | bytes 786432 | tf_op jit(solution)/shard_map/all_to_all | solution.py:429
  184.3 5.8 %collective-permute-start.23 = (bf16[1,384,128]{2,1,0:T(8,128)(2,1)}, bf16[1,384,128]{2,1,0:T(8,128)(2,1)S(1)}, u32[]{:S(2)}, u32[]{:S(2)}) collective-permute-start(bf16[1,384,128]{2,1,0:T(8,128)(2,1)} %get-tuple-element.97), channel_id=1, source_target_pairs={{0,8},{2,10},{4,12},{6,14},{8,0},{10,2},{12,4},{14,6},{16,24},{18,... | collective-permute-start | bytes 294920 | tf_op jit(solution)/shard_map/ppermute | solution.py:28
  186.4 6.9 %collective-permute-start.24 = (bf16[1,384,128]{2,1,0:T(8,128)(2,1)}, bf16[1,384,128]{2,1,0:T(8,128)(2,1)S(1)}, u32[]{:S(2)}, u32[]{:S(2)}) collective-permute-start(bf16[1,384,128]{2,1,0:T(8,128)(2,1)} %get-tuple-element.98), channel_id=1, source_target_pairs={{0,16},{2,18},{4,20},{6,22},{8,24},{10,26},{12,28},{14,30},{16,0},... | collective-permute-start | bytes 294920 | tf_op jit(solution)/shard_map/ppermute | solution.py:28
  188.7 6.7 %collective-permute-start.25 = (bf16[1,384,128]{2,1,0:T(8,128)(2,1)}, bf16[1,384,128]{2,1,0:T(8,128)(2,1)S(1)}, u32[]{:S(2)}, u32[]{:S(2)}) collective-permute-start(bf16[1,384,128]{2,1,0:T(8,128)(2,1)} %get-tuple-element.99), channel_id=1, source_target_pairs={{0,24},{2,26},{4,28},{6,30},{8,16},{10,18},{12,20},{14,22},{16,8},... | collective-permute-start | bytes 294920 | tf_op jit(solution)/shard_map/ppermute | solution.py:28
  188.8 12.1 %collective-permute-start.19 = (bf16[4,384,128]{2,1,0:T(8,128)(2,1)S(1)}, bf16[4,384,128]{2,1,0:T(8,128)(2,1)S(1)}, u32[]{:S(2)}, u32[]{:S(2)}) collective-permute-start(bf16[4,384,128]{2,1,0:T(8,128)(2,1)S(1)} %all-to-all-done.refs_0_), channel_id=1, source_target_pairs={{0,1},{1,0},{2,3},{3,2},{4,5},{5,4},{6,7},{7,6},{8,9},{9,8},{10,11... | collective-permute-start | bytes 1179656 | tf_op jit(solution)/shard_map/ppermute | solution.py:28
  190.2 18.8 %collective-permute-start.20 = (bf16[4,384,128]{2,1,0:T(8,128)(2,1)S(1)}, bf16[4,384,128]{2,1,0:T(8,128)(2,1)S(1)}, u32[]{:S(2)}, u32[]{:S(2)}) collective-permute-start(bf16[4,384,128]{2,1,0:T(8,128)(2,1)S(1)} %all-to-all-done.1.refs_1_), channel_id=1, source_target_pairs={{0,1},{1,0},{2,3},{3,2},{4,5},{5,4},{6,7},{7,6},{8,9},{9,8},{10,11... | collective-permute-start | bytes 1179656 | tf_op jit(solution)/shard_map/ppermute | solution.py:28
  195.4 22.6 %collective-permute-start.26 = (bf16[4,384,128]{2,1,0:T(8,128)(2,1)S(1)}, bf16[4,384,128]{2,1,0:T(8,128)(2,1)S(1)}, u32[]{:S(2)}, u32[]{:S(2)}) collective-permute-start(bf16[4,384,128]{2,1,0:T(8,128)(2,1)S(1)} %constant_dynamic-update-slice_fusion.8.refs_1_), channel_id=1, source_target_pairs={{0,1},{1,0},{2,3},{3,2},{4,5},{5,4},{6,7},{7,6},{8,9},{9,8},{10,11... | collective-permute-start | bytes 1179656 | tf_op jit(solution)/shard_map/ppermute | solution.py:28
  208.9 3.7 %copy-start = (bf16[1536,3072]{1,0:T(8,128)(2,1)S(1)}, bf16[1536,3072]{1,0:T(8,128)(2,1)}, u32[]{:S(2)}) copy-start(bf16[1536,3072]{1,0:T(8,128)(2,1)} %refs_2_.5) | copy-start | bytes 28311556
  212.6 5.4 %copy-start.1 = (bf16[384,384]{1,0:T(8,128)(2,1)S(1)}, bf16[384,384]{1,0:T(8,128)(2,1)}, u32[]{:S(2)}) copy-start(bf16[384,384]{1,0:T(8,128)(2,1)} %get-tuple-element.100.refs_5_) | copy-start | bytes 884740
  (8 other events, 10.8 us)
Sparse Core Ops, SparseCore 0:
  35.5 62.9 all-gather.4
  114.1 23.4 all-gather.6

commit v5 on v4

--- a/solution.py
+++ b/solution.py
@@ -376,15 +376,14 @@
     return head_shards == 2 and out_width % 256 == 0
 
 
-def fetch_weights(w_out, me, side, head_shards, arrived):
+def fetch_weights(w_out, me, side, head_shards):
     depth, width = w_out.shape
     out_width = width // head_shards
     if not splits(out_width, head_shards):
         blocks = jnp.transpose(w_out.reshape(depth, head_shards, out_width), (1, 0, 2))
         return lax.all_to_all(blocks, "head", split_axis=0, concat_axis=0, tiled=True)
     half = out_width // 2
-    nothing = jnp.minimum(jnp.abs(arrived[0, 0, 0]).astype(jnp.int32), 0)
-    column = (1 - side) * out_width + (me % 2) * half + nothing
+    column = (1 - side) * out_width + (me % 2) * half
     return lax.all_gather(lax.dynamic_slice(w_out, (0, column), (depth, half)), "head")
 
 
@@ -450,28 +449,26 @@
     (blocks,), rest = project(place, None, weights, gains, sets, groups, operands)
     normed, chosen, back, count = rest
     arrived = [swap(blocks)]
-    fetched = fetch_weights(w_out, me, side, head_shards, first(arrived[0]))
+    fetched = fetch_weights(w_out, me, side, head_shards)
 
     rest, asked, hops = range(1, chunks), None, []
-    if chunks > 1:
-        prepared = (count, chain(normed, first(arrived[0])), chosen)
-        sets = [((1, 2), (chunk,)) for chunk in rest]
-        made, _ = project(place, prepared, weights, gains, sets, groups)
-        stacks = [stack(list(chain(tuple(arrived[0]), made[0][0])))]
-        arrived.append(send(made[0]))
-        for blocks in made[1:]:
-            arrived.append(send(blocks, first(arrived[-1])))
-        hop = flip(stacks[0], "seq", ring // 2) if ring > 1 else stacks[0]
-        stacks.append(stack(arrived[1]))
-        ready = later(count, hop, stacks[1])
-        sets = [((0,), tuple(rest))]
-        (made,), _ = project(place, (ready, normed, chosen), weights, gains, sets, groups)
-        gate = made[0]
-        stacks += [stack(blocks) for blocks in arrived[2:]]
-        asked = send(made, stacks[-1])
-        hops = [flip(stacks[-1], "seq", ring // 2)] if ring > 1 else []
-    else:
-        gate, stacks = None, [stack(arrived[0])]
+    gate, stacks = None, []
+    for chunk in rest:
+        source = chain(normed, first(arrived[-1]), *stacks[-1:])
+        sets = [((1, 2), (chunk,))]
+        if chunk == chunks - 1:
+            sets.append(((0,), tuple(rest)))
+        made, _ = project(place, (count, source, chosen), weights, gains, sets, groups)
+        gate = made[0][0]
+        stacks.append(stack(list(chain(tuple(arrived[-1]), gate))))
+        arrived.append(swap(made[0]))
+        if chunk == chunks - 1:
+            asked = send(made[1], first(arrived[-1]))
+    stacks.append(stack(arrived[-1]))
+    if chunks > 1 and ring > 1:
+        hops = [flip(stacks[-1], "seq", ring // 2)]
+    out_width = w_out.shape[1] // head_shards
+    other_weights = share_weights(chain(fetched, gate), out_width, head_shards)
 
     attended, returned = [], []
     query, low_lane = arrived[0], 2 * size
@@ -487,10 +484,6 @@
         if not final:
             query, low_lane = asked, 0
             gate = tuple(asked)
-    out_width = w_out.shape[1] // head_shards
-    if chunks > 1:
-        fetched = chain(fetched, first(asked))
-    other_weights = share_weights(fetched, out_width, head_shards)
     total = None
     if chunks > 1:
         sooner = [across(found) for found in returned[:-1]]

time: 231 us -> 225 us (0.974)
  the two profiles are of different devices: /device:TPU:6 before, /device:TPU:0 now
where the time goes in v5:
time: 225 us; the launch traced here: 224 us
  Pallas kernels  77 us (34%)
  waiting for transfers between devices  76.4 us (34%)
  starting transfers between devices  44.7 us (20%)
  between operations  13.8 us (6%)
  local copies, waits for them, and re-layouts  9.84 us (4%)
    ppermute x27, waiting for transfers between devices, flip(): return lax.ppermute(values, axis, [(i, i ^ mask) for i in range(size)])  70.1 us
    pallas_call x3, Pallas kernels, project(): pl.pallas_call(functools.partial(project_body, steps=steps, groups=groups...  36.4 us
    ppermute x27, starting transfers between devices, flip(): return lax.ppermute(values, axis, [(i, i ^ mask) for i in range(size)])  34.8 us
    pallas_call x3, Pallas kernels, attend(): pl.pallas_call(functools.partial(attend_body, groups=groups, ordered=orde...  30.1 us
    pallas_call x2, Pallas kernels, finish(): pl.pallas_call(functools.partial(finish_body, chunks=chunks, others=head_...  10.5 us
    all_to_all x2, starting transfers between devices, send_back(): lax.all_to_all(blocks, 'seq', split_axis=0, concat_axis=0, axis_index_gro...  9.9 us
    unnamed x59, local copies, waits for them, and re-layouts  6.5 us
    all_gather x1, waiting for transfers between devices, fetch_weights(): lax.all_gather(lax.dynamic_slice(w_out, (0, column), (depth, half)), 'head')  6.23 us
  transfers between devices with their start and end apart: 31, of which 13 were waited for; matrix products, arithmetic and copies ran while one was open for 1% of the time, Pallas kernels for 32%

profile of v5, /device:TPU:0, one launch (start us, length us, event | category | flops | bytes accessed | tf_op | source)
XLA Modules:
  0.0 224.0 jit_solution(7071683725830741572)
XLA Ops:
  6.5 3.2 %constant_dynamic-slice_fusion = bf16[1536,768]{1,0:T(8,128)(2,1)} fusion(bf16[1536,3072]{1,0:T(8,128)(2,1)} %refs_2_.5, s32[]{:T(128)S(6)} %select_n.21), kind=kLoop, calls=%fused_computation.17 | loop fusion | bytes 4718596 | tf_op jit(solution)/shard_map/dynamic_slice | solution.py:387
  9.9 0.6 pad_add_fusion.place_ref
  10.4 13.8 %project.3 = (bf16[1,384,384]{2,1,0:T(8,128)(2,1)}, bf16[1,384,384]{2,1,0:T(8,128)(2,1)}, bf16[1,384,384]{2,1,0:T(8,128)(2,1)}, bf16[1,384,384]{2,1,0:T(8,128)(2...) custom-call(s32[3]{0:T(128)} %pad_add_fusion.place_ref, ...), custom_call_target="tpu_custom_call" | custom-call | flops 3623878656 | bytes 11796480 | tf_op jit(solution)/shard_map/project/pallas_call | solution.py:143
  24.3 3.1 %collective-permute-start = (bf16[1,384,384]{2,1,0:T(8,128)(2,1)}, bf16[1,384,384]{2,1,0:T(8,128)(2,1)S(1)}, u32[]{:S(2)}, u32[]{:S(2)}) collective-permute-start(bf16[1,384,384]{2,1,0:T(8,128)(2,1)} %get-tuple-element.53), channel_id=1, source_target_pairs={{0,8},{2,10},{4,12},{6,14},{8,0},{10,2},{12,4},{14,6},{16,24},{18,... | collective-permute-start | bytes 884744 | tf_op jit(solution)/shard_map/ppermute | solution.py:28
  27.4 2.6 %collective-permute-start.1 = (bf16[1,384,384]{2,1,0:T(8,128)(2,1)}, bf16[1,384,384]{2,1,0:T(8,128)(2,1)S(1)}, u32[]{:S(2)}, u32[]{:S(2)}) collective-permute-start(bf16[1,384,384]{2,1,0:T(8,128)(2,1)} %get-tuple-element.54), channel_id=1, source_target_pairs={{0,16},{2,18},{4,20},{6,22},{8,24},{10,26},{12,28},{14,30},{16,0},... | collective-permute-start | bytes 884744 | tf_op jit(solution)/shard_map/ppermute | solution.py:28
  30.0 10.1 %collective-permute-done.refs_1_ = bf16[1,384,384]{2,1,0:T(8,128)(2,1)S(1)} collective-permute-done((bf16[1,384,384]{2,1,0:T(8,128)(2,1)}, bf16[1,384,384]{2,1,0:T(8,128)(2,1)S(1)}, u32[]{:S(2)}, u32[]{:S(2)}) %collective-permute-start) | collective-permute-done | bytes 294944 | tf_op jit(solution)/shard_map/ppermute | solution.py:28
  40.1 8.8 %project.4 = (bf16[1,384,256]{2,1,0:T(8,128)(2,1)}, bf16[1,384,256]{2,1,0:T(8,128)(2,1)}, bf16[1,384,256]{2,1,0:T(8,128)(2,1)}, bf16[1,384,256]{2,1,0:T(8,128)(2,1)}) custom-call(s32[3]{0:T(128)} %pad_add_fusion.place_ref, bf16[3,3072,1536]{2,1,0:T(8,128)(2,1)} %bitcast.8, f32[12,2,128]{2,1,0:T(2,128)} %bitcast.14, s32[1,1]{1,0:T(1,128)} %get-tuple-element.56.refs_2_, ...), custom_call_target="tpu_custom_call" | custom-call | flops 2415919104 | bytes 8650752 | tf_op jit(solution)/shard_map/project/pallas_call | solution.py:143
  49.0 2.1 collective-permute-done.1.refs_2_
  51.3 4.0 %collective-permute-done.3 = bf16[1,384,256]{2,1,0:T(8,128)(2,1)S(1)} collective-permute-done((bf16[1,384,256]{2,1,0:T(8,128)(2,1)}, bf16[1,384,256]{2,1,0:T(8,128)(2,1)S(1)}, u32[]{:S(2)}, u32[]{:S(2)}) %collective-permute-start.3) | collective-permute-done | bytes 196640 | tf_op jit(solution)/shard_map/ppermute | solution.py:28
  55.3 13.7 %project.5 = (bf16[1,384,256]{2,1,0:T(8,128)(2,1)}, bf16[1,384,256]{2,1,0:T(8,128)(2,1)}, bf16[1,384,256]{2,1,0:T(8,128)(2,1)}, bf16[1,384,256]{2,1,0:T(8,128)(2...) custom-call(s32[3]{0:T(128)} %pad_add_fusion.place_ref, ...), custom_call_target="tpu_custom_call" | custom-call | flops 4831838208 | bytes 14942208 | tf_op jit(solution)/shard_map/project/pallas_call | solution.py:143
  69.1 6.2 %all-gather.5.cloned.1.call-done = bf16[3072,768]{1,0:T(8,128)(2,1)} async-done(((bf16[1536,768]{1,0:T(8,128)(2,1)}), bf16[3072,768]{1,0:T(8,128)(2,1)}) %all-gather.5.cloned.1.call-update) | async-done | bytes 4718608 | tf_op jit(solution)/shard_map/all_gather | solution.py:387
  75.4 0.8 copy-done.24
  76.2 2.4 %collective-permute-start.14 = (bf16[1,384,256]{2,1,0:T(8,128)(2,1)S(1)}, bf16[1,384,256]{2,1,0:T(8,128)(2,1)S(1)}, u32[]{:S(2)}, u32[]{:S(2)}) collective-permute-start(bf16[1,384,256]{2,1,0:T(8,128)(2,1)S(1)} %copy-done.24), channel_id=1, source_target_pairs={{0,16},{2,18},{4,20},{6,22},{8,24},{10,26},{12,28},{14,30},{16,0},... | collective-permute-start | bytes 589832 | tf_op jit(solution)/shard_map/ppermute | solution.py:28
  78.6 1.4 collective-permute-start.15
  80.1 1.5 collective-permute-start.8
  81.6 11.7 %collective-permute-done.14 = bf16[1,384,256]{2,1,0:T(8,128)(2,1)S(1)} collective-permute-done((bf16[1,384,256]{2,1,0:T(8,128)(2,1)S(1)}, bf16[1,384,256]{2,1,0:T(8,128)(2,1)S(1)}, u32[]{:S(2)}, u32[]{:S(2)}) %collective-permute-start.14) | collective-permute-done | bytes 196640 | tf_op jit(solution)/shard_map/ppermute | solution.py:28
  93.4 1.5 collective-permute-start.17
  94.9 5.6 %collective-permute-start.5 = (bf16[1,384,256]{2,1,0:T(8,128)(2,1)S(1)}, bf16[1,384,256]{2,1,0:T(8,128)(2,1)S(1)}, u32[]{:S(2)}, u32[]{:S(2)}) collective-permute-start(bf16[1,384,256]{2,1,0:T(8,128)(2,1)S(1)} %copy-done.20), channel_id=1, source_target_pairs={{0,16},{2,18},{4,20},{6,22},{8,24},{10,26},{12,28},{14,30},{16,0},... | collective-permute-start | bytes 589832 | tf_op jit(solution)/shard_map/ppermute | solution.py:28
  100.5 0.5 collective-permute-start.6
  101.7 12.3 %collective-permute-done.5 = bf16[1,384,256]{2,1,0:T(8,128)(2,1)S(1)} collective-permute-done((bf16[1,384,256]{2,1,0:T(8,128)(2,1)S(1)}, bf16[1,384,256]{2,1,0:T(8,128)(2,1)S(1)}, u32[]{:S(2)}, u32[]{:S(2)}) %collective-permute-start.5) | collective-permute-done | bytes 196640 | tf_op jit(solution)/shard_map/ppermute | solution.py:28
  114.0 3.5 %collective-permute-start.11 = (bf16[2,384,128]{2,1,0:T(8,128)(2,1)S(1)}, bf16[2,384,128]{2,1,0:T(8,128)(2,1)S(1)}, u32[]{:S(2)}, u32[]{:S(2)}) collective-permute-start(bf16[2,384,128]{2,1,0:T(8,128)(2,1)S(1)} %copy-done.15), channel_id=1, source_target_pairs={{0,16},{2,18},{4,20},{6,22},{8,24},{10,26},{12,28},{14,30},{16,0},... | collective-permute-start | bytes 589832 | tf_op jit(solution)/shard_map/ppermute | solution.py:28
  117.5 6.0 %collective-permute-done.10.refs_1_ = bf16[2,384,128]{2,1,0:T(8,128)(2,1)S(1)} collective-permute-done((bf16[2,384,128]{2,1,0:T(8,128)(2,1)S(1)}, bf16[2,384,128]{2,1,0:T(8,128)(2,1)S(1)}, u32[]{:S(2)}, u32[]{:S(2)}) %collective-permute-start.10) | collective-permute-done | bytes 196640 | tf_op jit(solution)/shard_map/ppermute | solution.py:28
  123.5 0.5 collective-permute-start.13
  124.1 2.6 %collective-permute-done.11.refs_2_ = bf16[2,384,128]{2,1,0:T(8,128)(2,1)S(1)} collective-permute-done((bf16[2,384,128]{2,1,0:T(8,128)(2,1)S(1)}, bf16[2,384,128]{2,1,0:T(8,128)(2,1)S(1)}, u32[]{:S(2)}, u32[]{:S(2)}) %collective-permute-start.11) | collective-permute-done | bytes 196640 | tf_op jit(solution)/shard_map/ppermute | solution.py:28
  126.7 3.3 %collective-permute-start.12 = (bf16[2,384,128]{2,1,0:T(8,128)(2,1)S(1)}, bf16[2,384,128]{2,1,0:T(8,128)(2,1)S(1)}, u32[]{:S(2)}, u32[]{:S(2)}) collective-permute-start(bf16[2,384,128]{2,1,0:T(8,128)(2,1)S(1)} %copy-done.14), channel_id=1, source_target_pairs={{0,24},{2,26},{4,28},{6,30},{8,16},{10,18},{12,20},{14,22},{16,8},... | collective-permute-start | bytes 589832 | tf_op jit(solution)/shard_map/ppermute | solution.py:28
  130.0 4.8 %collective-permute-done.12.refs_3_ = bf16[2,384,128]{2,1,0:T(8,128)(2,1)S(1)} collective-permute-done((bf16[2,384,128]{2,1,0:T(8,128)(2,1)S(1)}, bf16[2,384,128]{2,1,0:T(8,128)(2,1)S(1)}, u32[]{:S(2)}, u32[]{:S(2)}) %collective-permute-start.12) | collective-permute-done | bytes 196640 | tf_op jit(solution)/shard_map/ppermute | solution.py:28
  134.8 0.5 collective-permute-start.18
  135.8 0.9 copy-done.13
  136.7 10.2 %attend.3 = bf16[4,384,128]{2,1,0:T(8,128)(2,1)} custom-call(s32[3]{0:T(128)} %broadcast_maximum_fusion.2.place_ref, bf16[1,384,384]{2,1,0:T(8,128)(2,1)} %get-tuple-element.63.refs_0_, bf16[1,384,384]{2,1,0:T(8,128)(2,1)} %copy-done.7, bf16[1,384,384]{2,1,0:T(8,128)(2,1)} %copy-done.8, bf16[1,384,384]{2,1,0:T(8,128)(2,1)} %copy-done.9, ...), custom_call_target="tpu_custom_call" | custom-call | flops 2415919104 | bytes 3145728 | tf_op jit(solution)/shard_map/attend/pallas_call | solution.py:258
  146.9 4.8 %all-to-all-start = ((bf16[4,384,128]{2,1,0:T(8,128)(2,1)}), bf16[4,384,128]{2,1,0:T(8,128)(2,1)S(1)}, u32[]{:S(2)}, u32[]{:S(2)}) async-start(bf16[4,384,128]{2,1,0:T(8,128)(2,1)} %attend.3), calls=%async_computation | async-start | bytes 786432 | tf_op jit(solution)/shard_map/all_to_all | solution.py:428
  152.2 0.5 broadcast_maximum_fusion.1.place_ref
  152.7 10.1 %attend.4 = bf16[4,384,128]{2,1,0:T(8,128)(2,1)} custom-call(s32[3]{0:T(128)} %broadcast_maximum_fusion.1.place_ref, bf16[2,384,128]{2,1,0:T(8,128)(2,1)} %get-tuple-element.83.refs_0_, bf16[2,384,128]{2,1,0:T(8,128)(2,1)} %copy-done.16, bf16[2,384,128]{2,1,0:T(8,128)(2,1)} %copy-done.18, bf16[2,384,128]{2,1,0:T(8,128)(2,1)} %copy-done.21, ...), custom_call_target="tpu_custom_call" | custom-call | flops 2415919104 | bytes 3145728 | tf_op jit(solution)/shard_map/attend/pallas_call | solution.py:258
  162.9 5.1 %all-to-all-start.1 = ((bf16[4,384,128]{2,1,0:T(8,128)(2,1)}), bf16[4,384,128]{2,1,0:T(8,128)(2,1)S(1)}, u32[]{:S(2)}, u32[]{:S(2)}) async-start(bf16[4,384,128]{2,1,0:T(8,128)(2,1)} %attend.4), calls=%async_computation.1 | async-start | bytes 786432 | tf_op jit(solution)/shard_map/all_to_all | solution.py:428
  168.0 0.6 broadcast_maximum_fusion.place_ref
  168.5 9.8 %attend.5 = (bf16[1,384,128]{2,1,0:T(8,128)(2,1)}, bf16[1,384,128]{2,1,0:T(8,128)(2,1)}, bf16[1,384,128]{2,1,0:T(8,128)(2,1)}, bf16[1,384,128]{2,1,0:T(8,128)(2,1)}) custom-call(s32[3]{0:T(128)} %broadcast_maximum_fusion.place_ref, bf16[2,384,128]{2,1,0:T(8,128)(2,1)} %get-tuple-element.83.refs_0_, bf16[2,384,128]{2,1,0:T(8,128)(2,1)} %copy-done.16, ...), custom_call_target="tpu_custom_call" | custom-call | flops 2415919104 | bytes 3145728 | tf_op jit(solution)/shard_map/attend/pallas_call | solution.py:258
  178.4 2.0 collective-permute-start.23
  180.4 2.4 %collective-permute-start.24 = (bf16[1,384,128]{2,1,0:T(8,128)(2,1)}, bf16[1,384,128]{2,1,0:T(8,128)(2,1)S(1)}, u32[]{:S(2)}, u32[]{:S(2)}) collective-permute-start(bf16[1,384,128]{2,1,0:T(8,128)(2,1)} %get-tuple-element.98), channel_id=1, source_target_pairs={{0,16},{2,18},{4,20},{6,22},{8,24},{10,26},{12,28},{14,30},{16,0},... | collective-permute-start | bytes 294920 | tf_op jit(solution)/shard_map/ppermute | solution.py:28
  182.8 0.6 collective-permute-start.19
  183.3 0.9 constant_dynamic-update-slice_fusion.11
  184.3 1.5 collective-permute-start.20
  185.8 1.5 collective-permute-done.24
  187.3 2.1 collective-permute-done.25
  189.4 0.6 collective-permute-start.26
  190.0 4.8 %collective-permute-done.19.refs_3_ = bf16[4,384,128]{2,1,0:T(8,128)(2,1)S(1)} collective-permute-done((bf16[4,384,128]{2,1,0:T(8,128)(2,1)S(1)}, bf16[4,384,128]{2,1,0:T(8,128)(2,1)S(1)}, u32[]{:S(2)}, u32[]{:S(2)}) %collective-permute-start.19) | collective-permute-done | bytes 393248 | tf_op jit(solution)/shard_map/ppermute | solution.py:28
  194.8 8.1 %collective-permute-done.20.refs_4_ = bf16[4,384,128]{2,1,0:T(8,128)(2,1)S(1)} collective-permute-done((bf16[4,384,128]{2,1,0:T(8,128)(2,1)S(1)}, bf16[4,384,128]{2,1,0:T(8,128)(2,1)S(1)}, u32[]{:S(2)}, u32[]{:S(2)}) %collective-permute-start.20) | collective-permute-done | bytes 393248 | tf_op jit(solution)/shard_map/ppermute | solution.py:28
  202.9 3.7 %copy-done = bf16[1536,3072]{1,0:T(8,128)(2,1)S(1)} copy-done((bf16[1536,3072]{1,0:T(8,128)(2,1)S(1)}, bf16[1536,3072]{1,0:T(8,128)(2,1)}, u32[]{:S(2)}) %copy-start) | copy-done | bytes 9437208
  206.6 5.4 %finish.2.refs_0_ = f32[384,1536]{1,0:T(8,128)S(1)} custom-call(s32[3]{0:T(128)S(1)} %copy-done.2, bf16[4,384,128]{2,1,0:T(8,128)(2,1)S(1)} %all-to-all-done.refs_0_, bf16[4,384,128]{2,1,0:T(8,128)(2,1)S(1)} %all-to-all-done.1.refs_1_, bf16[1536,3072]{1,0:T(8,128)(2,1)S(1)} %copy-done, bf16[4,384,128]{2,1,0:T(8,128)(2,1)S(1)} %collective-permute-done.19.refs_3_, ...), custom_call_target="tpu_custom_call" | custom-call | flops 2415919104 | bytes 11010048 | tf_op jit(solution)/shard_map/finish/pallas_call | solution.py:349
  212.0 5.2 %finish.3 = bf16[384,1536]{1,0:T(8,128)(2,1)} custom-call(s32[3]{0:T(128)S(1)} %copy-done.2, f32[384,1536]{1,0:T(8,128)S(1)} %finish.2.refs_0_, bf16[4,384,128]{2,1,0:T(8,128)(2,1)S(1)} %constant_dynamic-update-slice_fusion.8.refs_1_, bf16[1536,3072]{1,0:T(8,128)(2,1)S(1)} %copy-done, bf16[4,384,128]{2,1,0:T(8,128)(2,1)S(1)} %collective-permute-done.26.refs_3_, ...), custom_call_target="tpu_custom_call" | custom-call | flops 1207959552 | bytes 7864320 | tf_op jit(solution)/shard_map/finish/pallas_call | solution.py:349
  (96 shorter events, 2.2 us)
Async XLA Ops:
  6.5 68.8 %all-gather.5.cloned.1.call-start = ((), (), s32[]{:S(2)}) async-start(), calls=%async_computation.2 | async-start | bytes 7077888 | tf_op jit(solution)/shard_map/all_gather | solution.py:387
  9.8 193.1 %all-gather.7.cloned.1.call-start = ((), (), s32[]{:S(2)}) async-start(), calls=%async_computation.3 | async-start | bytes 14155776 | tf_op jit(solution)/shard_map/all_gather | solution.py:394
  24.3 15.9 %collective-permute-start = (bf16[1,384,384]{2,1,0:T(8,128)(2,1)}, bf16[1,384,384]{2,1,0:T(8,128)(2,1)S(1)}, u32[]{:S(2)}, u32[]{:S(2)}) collective-permute-start(bf16[1,384,384]{2,1,0:T(8,128)(2,1)} %get-tuple-element.53), channel_id=1, source_target_pairs={{0,8},{2,10},{4,12},{6,14},{8,0},{10,2},{12,4},{14,6},{16,24},{18,... | collective-permute-start | bytes 884744 | tf_op jit(solution)/shard_map/ppermute | solution.py:28
  27.4 23.7 %collective-permute-start.1 = (bf16[1,384,384]{2,1,0:T(8,128)(2,1)}, bf16[1,384,384]{2,1,0:T(8,128)(2,1)S(1)}, u32[]{:S(2)}, u32[]{:S(2)}) collective-permute-start(bf16[1,384,384]{2,1,0:T(8,128)(2,1)} %get-tuple-element.54), channel_id=1, source_target_pairs={{0,16},{2,18},{4,20},{6,22},{8,24},{10,26},{12,28},{14,30},{16,0},... | collective-permute-start | bytes 884744 | tf_op jit(solution)/shard_map/ppermute | solution.py:28
  30.0 21.1 %collective-permute-start.2 = (bf16[1,384,384]{2,1,0:T(8,128)(2,1)}, bf16[1,384,384]{2,1,0:T(8,128)(2,1)S(1)}, u32[]{:S(2)}, u32[]{:S(2)}) collective-permute-start(bf16[1,384,384]{2,1,0:T(8,128)(2,1)} %get-tuple-element.55), channel_id=1, source_target_pairs={{0,24},{2,26},{4,28},{6,30},{8,16},{10,18},{12,20},{14,22},{16,8},... | collective-permute-start | bytes 884744 | tf_op jit(solution)/shard_map/ppermute | solution.py:28
  49.0 6.4 %collective-permute-start.3 = (bf16[1,384,256]{2,1,0:T(8,128)(2,1)}, bf16[1,384,256]{2,1,0:T(8,128)(2,1)S(1)}, u32[]{:S(2)}, u32[]{:S(2)}) collective-permute-start(bf16[1,384,256]{2,1,0:T(8,128)(2,1)} %get-tuple-element.60), channel_id=1, source_target_pairs={{0,8},{2,10},{4,12},{6,14},{8,0},{10,2},{12,4},{14,6},{16,24},{18,... | collective-permute-start | bytes 589832 | tf_op jit(solution)/shard_map/ppermute | solution.py:28
  51.1 18.0 %copy-start.8 = (bf16[1,384,384]{2,1,0:T(8,128)(2,1)}, bf16[1,384,384]{2,1,0:T(8,128)(2,1)S(1)}, u32[]{:S(2)}) copy-start(bf16[1,384,384]{2,1,0:T(8,128)(2,1)S(1)} %collective-permute-done.1.refs_2_) | copy-start | bytes 884740
  51.1 18.0 %copy-start.9 = (bf16[1,384,384]{2,1,0:T(8,128)(2,1)}, bf16[1,384,384]{2,1,0:T(8,128)(2,1)S(1)}, u32[]{:S(2)}) copy-start(bf16[1,384,384]{2,1,0:T(8,128)(2,1)S(1)} %collective-permute-done.2.refs_3_) | copy-start | bytes 884740
  51.3 49.8 %copy-start.3 = (bf16[4,384,256]{2,1,0:T(8,128)(2,1)}, bf16[4,384,256]{2,1,0:T(8,128)(2,1)S(1)}, u32[]{:S(2)}) copy-start(bf16[4,384,256]{2,1,0:T(8,128)(2,1)S(1)} %pad_maximum_fusion.refs_4_) | copy-start | bytes 2359300
  75.3 18.0 %copy-start.4 = (bf16[1,384,256]{2,1,0:T(8,128)(2,1)S(1)}, bf16[1,384,256]{2,1,0:T(8,128)(2,1)}, u32[]{:S(2)}) copy-start(bf16[1,384,256]{2,1,0:T(8,128)(2,1)} %get-tuple-element.86) | copy-start | bytes 589828
  75.3 19.6 %copy-start.20 = (bf16[1,384,256]{2,1,0:T(8,128)(2,1)S(1)}, bf16[1,384,256]{2,1,0:T(8,128)(2,1)}, u32[]{:S(2)}) copy-start(bf16[1,384,256]{2,1,0:T(8,128)(2,1)} %get-tuple-element.70) | copy-start | bytes 589828
  75.3 25.2 %copy-start.19 = (bf16[1,384,256]{2,1,0:T(8,128)(2,1)S(1)}, bf16[1,384,256]{2,1,0:T(8,128)(2,1)}, u32[]{:S(2)}) copy-start(bf16[1,384,256]{2,1,0:T(8,128)(2,1)} %get-tuple-element.71) | copy-start | bytes 589828
  75.3 25.7 %copy-start.5 = (bf16[1,384,256]{2,1,0:T(8,128)(2,1)S(1)}, bf16[1,384,256]{2,1,0:T(8,128)(2,1)}, u32[]{:S(2)}) copy-start(bf16[1,384,256]{2,1,0:T(8,128)(2,1)} %get-tuple-element.68) | copy-start | bytes 589828
  75.4 38.6 %copy-start.17 = (bf16[2,384,128]{2,1,0:T(8,128)(2,1)S(1)}, bf16[2,384,128]{2,1,0:T(8,128)(2,1)}, u32[]{:S(2)}) copy-start(bf16[2,384,128]{2,1,0:T(8,128)(2,1)} %get-tuple-element.79) | copy-start | bytes 589828
  75.4 38.7 %copy-start.15 = (bf16[2,384,128]{2,1,0:T(8,128)(2,1)S(1)}, bf16[2,384,128]{2,1,0:T(8,128)(2,1)}, u32[]{:S(2)}) copy-start(bf16[2,384,128]{2,1,0:T(8,128)(2,1)} %get-tuple-element.80) | copy-start | bytes 589828
  75.4 51.3 %copy-start.14 = (bf16[2,384,128]{2,1,0:T(8,128)(2,1)S(1)}, bf16[2,384,128]{2,1,0:T(8,128)(2,1)}, u32[]{:S(2)}) copy-start(bf16[2,384,128]{2,1,0:T(8,128)(2,1)} %get-tuple-element.81) | copy-start | bytes 589828
  75.4 59.9 %copy-start.2 = (s32[3]{0:T(128)S(1)}, s32[3]{0:T(128)}, u32[]{:S(2)}) copy-start(s32[3]{0:T(128)} %pad_add_fusion.place_ref) | copy-start | bytes 40
  76.2 17.0 %collective-permute-start.14 = (bf16[1,384,256]{2,1,0:T(8,128)(2,1)S(1)}, bf16[1,384,256]{2,1,0:T(8,128)(2,1)S(1)}, u32[]{:S(2)}, u32[]{:S(2)}) collective-permute-start(bf16[1,384,256]{2,1,0:T(8,128)(2,1)S(1)} %copy-done.24), channel_id=1, source_target_pairs={{0,16},{2,18},{4,20},{6,22},{8,24},{10,26},{12,28},{14,30},{16,0},... | collective-permute-start | bytes 589832 | tf_op jit(solution)/shard_map/ppermute | solution.py:28
  78.6 14.6 %collective-permute-start.15 = (bf16[1,384,256]{2,1,0:T(8,128)(2,1)S(1)}, bf16[1,384,256]{2,1,0:T(8,128)(2,1)S(1)}, u32[]{:S(2)}, u32[]{:S(2)}) collective-permute-start(bf16[1,384,256]{2,1,0:T(8,128)(2,1)S(1)} %copy-done.23), channel_id=1, source_target_pairs={{0,24},{2,26},{4,28},{6,30},{8,16},{10,18},{12,20},{14,22},{16,8},... | collective-permute-start | bytes 589832 | tf_op jit(solution)/shard_map/ppermute | solution.py:28
  80.1 21.0 %collective-permute-start.8 = (bf16[4,384,256]{2,1,0:T(8,128)(2,1)S(1)}, bf16[4,384,256]{2,1,0:T(8,128)(2,1)S(1)}, u32[]{:S(2)}, u32[]{:S(2)}) collective-permute-start(bf16[4,384,256]{2,1,0:T(8,128)(2,1)S(1)} %pad_maximum_fusion.refs_4_), channel_id=1, source_target_pairs={{0,4},{2,6},{4,0},{6,2},{8,12},{10,14},{12,8},{14,10},{16,20},{18,... | collective-permute-start | bytes 2359304 | tf_op jit(solution)/shard_map/ppermute | solution.py:28
  81.6 19.6 %collective-permute-start.4 = (bf16[1,384,256]{2,1,0:T(8,128)(2,1)S(1)}, bf16[1,384,256]{2,1,0:T(8,128)(2,1)S(1)}, u32[]{:S(2)}, u32[]{:S(2)}) collective-permute-start(bf16[1,384,256]{2,1,0:T(8,128)(2,1)S(1)} %copy-done.22), channel_id=1, source_target_pairs={{0,8},{2,10},{4,12},{6,14},{8,0},{10,2},{12,4},{14,6},{16,24},{18,... | collective-permute-start | bytes 589832 | tf_op jit(solution)/shard_map/ppermute | solution.py:28
  93.4 53.5 %copy-start.11 = (bf16[4,384,256]{2,1,0:T(8,128)(2,1)}, bf16[4,384,256]{2,1,0:T(8,128)(2,1)S(1)}, u32[]{:S(2)}) copy-start(bf16[4,384,256]{2,1,0:T(8,128)(2,1)S(1)} %constant_dynamic-update-slice_fusion.4.refs_4_) | copy-start | bytes 2359300
  93.4 41.4 %collective-permute-start.17 = (bf16[4,384,256]{2,1,0:T(8,128)(2,1)S(1)}, bf16[4,384,256]{2,1,0:T(8,128)(2,1)}, u32[]{:S(2)}, u32[]{:S(2)}) collective-permute-start(bf16[4,384,256]{2,1,0:T(8,128)(2,1)S(1)} %constant_dynamic-update-slice_fusion.4.refs_4_), channel_id=1, source_target_pairs={{0,4},{2,6},{4,0},{6,2},{8,12},{10,14},{12,8},{14,10},{16,20},{18,... | collective-permute-start | bytes 2359304 | tf_op jit(solution)/shard_map/ppermute | solution.py:28
  94.9 19.1 %collective-permute-start.5 = (bf16[1,384,256]{2,1,0:T(8,128)(2,1)S(1)}, bf16[1,384,256]{2,1,0:T(8,128)(2,1)S(1)}, u32[]{:S(2)}, u32[]{:S(2)}) collective-permute-start(bf16[1,384,256]{2,1,0:T(8,128)(2,1)S(1)} %copy-done.20), channel_id=1, source_target_pairs={{0,16},{2,18},{4,20},{6,22},{8,24},{10,26},{12,28},{14,30},{16,0},... | collective-permute-start | bytes 589832 | tf_op jit(solution)/shard_map/ppermute | solution.py:28
  100.5 13.5 %collective-permute-start.6 = (bf16[1,384,256]{2,1,0:T(8,128)(2,1)S(1)}, bf16[1,384,256]{2,1,0:T(8,128)(2,1)S(1)}, u32[]{:S(2)}, u32[]{:S(2)}) collective-permute-start(bf16[1,384,256]{2,1,0:T(8,128)(2,1)S(1)} %copy-done.19), channel_id=1, source_target_pairs={{0,24},{2,26},{4,28},{6,30},{8,16},{10,18},{12,20},{14,22},{16,8},... | collective-permute-start | bytes 589832 | tf_op jit(solution)/shard_map/ppermute | solution.py:28
  101.1 34.7 %copy-start.12 = (bf16[4,384,256]{2,1,0:T(8,128)(2,1)}, bf16[4,384,256]{2,1,0:T(8,128)(2,1)S(1)}, u32[]{:S(2)}) copy-start(bf16[4,384,256]{2,1,0:T(8,128)(2,1)S(1)} %collective-permute-done.8.refs_6_) | copy-start | bytes 2359300
  101.1 34.7 %collective-permute-start.7 = (bf16[4,384,256]{2,1,0:T(8,128)(2,1)S(1)}, bf16[4,384,256]{2,1,0:T(8,128)(2,1)S(1)}, u32[]{:S(2)}, u32[]{:S(2)}) collective-permute-start(bf16[4,384,256]{2,1,0:T(8,128)(2,1)S(1)} %pad_maximum_fusion.refs_4_), channel_id=1, source_target_pairs={{0,2},{2,0},{4,6},{6,4},{8,10},{10,8},{12,14},{14,12},{16,18},{18,... | collective-permute-start | bytes 2359304 | tf_op jit(solution)/shard_map/ppermute | solution.py:28
  101.2 35.5 %collective-permute-start.9 = (bf16[4,384,256]{2,1,0:T(8,128)(2,1)S(1)}, bf16[4,384,256]{2,1,0:T(8,128)(2,1)}, u32[]{:S(2)}, u32[]{:S(2)}) collective-permute-start(bf16[4,384,256]{2,1,0:T(8,128)(2,1)S(1)} %collective-permute-done.8.refs_6_), channel_id=1, source_target_pairs={{0,2},{2,0},{4,6},{6,4},{8,10},{10,8},{12,14},{14,12},{16,18},{18,... | collective-permute-start | bytes 2359304 | tf_op jit(solution)/shard_map/ppermute | solution.py:28
  114.0 9.6 %collective-permute-start.10 = (bf16[2,384,128]{2,1,0:T(8,128)(2,1)S(1)}, bf16[2,384,128]{2,1,0:T(8,128)(2,1)S(1)}, u32[]{:S(2)}, u32[]{:S(2)}) collective-permute-start(bf16[2,384,128]{2,1,0:T(8,128)(2,1)S(1)} %copy-done.17), channel_id=1, source_target_pairs={{0,8},{2,10},{4,12},{6,14},{8,0},{10,2},{12,4},{14,6},{16,24},{18,... | collective-permute-start | bytes 589832 | tf_op jit(solution)/shard_map/ppermute | solution.py:28
  114.0 12.6 %collective-permute-start.11 = (bf16[2,384,128]{2,1,0:T(8,128)(2,1)S(1)}, bf16[2,384,128]{2,1,0:T(8,128)(2,1)S(1)}, u32[]{:S(2)}, u32[]{:S(2)}) collective-permute-start(bf16[2,384,128]{2,1,0:T(8,128)(2,1)S(1)} %copy-done.15), channel_id=1, source_target_pairs={{0,16},{2,18},{4,20},{6,22},{8,24},{10,26},{12,28},{14,30},{16,0},... | collective-permute-start | bytes 589832 | tf_op jit(solution)/shard_map/ppermute | solution.py:28
  117.5 34.2 %copy-start.10 = (bf16[4,384,256]{2,1,0:T(8,128)(2,1)}, bf16[4,384,256]{2,1,0:T(8,128)(2,1)S(1)}, u32[]{:S(2)}) copy-start(bf16[4,384,256]{2,1,0:T(8,128)(2,1)S(1)} %constant_dynamic-update-slice_fusion.refs_4_) | copy-start | bytes 2359300
  123.5 29.2 %copy-start.16 = (bf16[2,384,128]{2,1,0:T(8,128)(2,1)}, bf16[2,384,128]{2,1,0:T(8,128)(2,1)S(1)}, u32[]{:S(2)}) copy-start(bf16[2,384,128]{2,1,0:T(8,128)(2,1)S(1)} %collective-permute-done.10.refs_1_) | copy-start | bytes 589828
  123.5 28.1 %collective-permute-start.13 = (bf16[4,384,256]{2,1,0:T(8,128)(2,1)S(1)}, bf16[4,384,256]{2,1,0:T(8,128)(2,1)}, u32[]{:S(2)}, u32[]{:S(2)}) collective-permute-start(bf16[4,384,256]{2,1,0:T(8,128)(2,1)S(1)} %constant_dynamic-update-slice_fusion.refs_4_), channel_id=1, source_target_pairs={{0,4},{2,6},{4,0},{6,2},{8,12},{10,14},{12,8},{14,10},{16,20},{18,... | collective-permute-start | bytes 2359304 | tf_op jit(solution)/shard_map/ppermute | solution.py:28
  126.7 26.0 %copy-start.18 = (bf16[2,384,128]{2,1,0:T(8,128)(2,1)}, bf16[2,384,128]{2,1,0:T(8,128)(2,1)S(1)}, u32[]{:S(2)}) copy-start(bf16[2,384,128]{2,1,0:T(8,128)(2,1)S(1)} %collective-permute-done.11.refs_2_) | copy-start | bytes 589828
  126.7 8.1 %collective-permute-start.12 = (bf16[2,384,128]{2,1,0:T(8,128)(2,1)S(1)}, bf16[2,384,128]{2,1,0:T(8,128)(2,1)S(1)}, u32[]{:S(2)}, u32[]{:S(2)}) collective-permute-start(bf16[2,384,128]{2,1,0:T(8,128)(2,1)S(1)} %copy-done.14), channel_id=1, source_target_pairs={{0,24},{2,26},{4,28},{6,30},{8,16},{10,18},{12,20},{14,22},{16,8},... | collective-permute-start | bytes 589832 | tf_op jit(solution)/shard_map/ppermute | solution.py:28
  134.8 17.9 %copy-start.21 = (bf16[2,384,128]{2,1,0:T(8,128)(2,1)}, bf16[2,384,128]{2,1,0:T(8,128)(2,1)S(1)}, u32[]{:S(2)}) copy-start(bf16[2,384,128]{2,1,0:T(8,128)(2,1)S(1)} %collective-permute-done.12.refs_3_) | copy-start | bytes 589828
  134.8 17.9 %collective-permute-start.16 = (bf16[4,384,256]{2,1,0:T(8,128)(2,1)S(1)}, bf16[4,384,256]{2,1,0:T(8,128)(2,1)}, u32[]{:S(2)}, u32[]{:S(2)}) collective-permute-start(bf16[4,384,256]{2,1,0:T(8,128)(2,1)S(1)} %constant_dynamic-update-slice_fusion.4.refs_4_), channel_id=1, source_target_pairs={{0,2},{2,0},{4,6},{6,4},{8,10},{10,8},{12,14},{14,12},{16,18},{18,... | collective-permute-start | bytes 2359304 | tf_op jit(solution)/shard_map/ppermute | solution.py:28
  134.8 17.9 %collective-permute-start.18 = (bf16[4,384,256]{2,1,0:T(8,128)(2,1)}, bf16[4,384,256]{2,1,0:T(8,128)(2,1)}, u32[]{:S(2)}, u32[]{:S(2)}) collective-permute-start(bf16[4,384,256]{2,1,0:T(8,128)(2,1)} %collective-permute-done.17.refs_6_), channel_id=1, source_target_pairs={{0,2},{2,0},{4,6},{6,4},{8,10},{10,8},{12,14},{14,12},{16,18},{18,... | collective-permute-start | bytes 2359304 | tf_op jit(solution)/shard_map/ppermute | solution.py:28
  146.9 16.0 %all-to-all-start = ((bf16[4,384,128]{2,1,0:T(8,128)(2,1)}), bf16[4,384,128]{2,1,0:T(8,128)(2,1)S(1)}, u32[]{:S(2)}, u32[]{:S(2)}) async-start(bf16[4,384,128]{2,1,0:T(8,128)(2,1)} %attend.3), calls=%async_computation | async-start | bytes 786432 | tf_op jit(solution)/shard_map/all_to_all | solution.py:428
  151.7 16.8 %collective-permute-start.21 = (bf16[4,384,256]{2,1,0:T(8,128)(2,1)S(1)}, bf16[4,384,256]{2,1,0:T(8,128)(2,1)}, u32[]{:S(2)}, u32[]{:S(2)}) collective-permute-start(bf16[4,384,256]{2,1,0:T(8,128)(2,1)S(1)} %constant_dynamic-update-slice_fusion.refs_4_), channel_id=1, source_target_pairs={{0,2},{2,0},{4,6},{6,4},{8,10},{10,8},{12,14},{14,12},{16,18},{18,... | collective-permute-start | bytes 2359304 | tf_op jit(solution)/shard_map/ppermute | solution.py:28
  151.7 16.8 %collective-permute-start.22 = (bf16[4,384,256]{2,1,0:T(8,128)(2,1)}, bf16[4,384,256]{2,1,0:T(8,128)(2,1)}, u32[]{:S(2)}, u32[]{:S(2)}) collective-permute-start(bf16[4,384,256]{2,1,0:T(8,128)(2,1)} %collective-permute-done.13.refs_6_), channel_id=1, source_target_pairs={{0,2},{2,0},{4,6},{6,4},{8,10},{10,8},{12,14},{14,12},{16,18},{18,... | collective-permute-start | bytes 2359304 | tf_op jit(solution)/shard_map/ppermute | solution.py:28
  162.9 21.4 %all-to-all-start.1 = ((bf16[4,384,128]{2,1,0:T(8,128)(2,1)}), bf16[4,384,128]{2,1,0:T(8,128)(2,1)S(1)}, u32[]{:S(2)}, u32[]{:S(2)}) async-start(bf16[4,384,128]{2,1,0:T(8,128)(2,1)} %attend.4), calls=%async_computation.1 | async-start | bytes 786432 | tf_op jit(solution)/shard_map/all_to_all | solution.py:428
  178.4 5.9 %collective-permute-start.23 = (bf16[1,384,128]{2,1,0:T(8,128)(2,1)}, bf16[1,384,128]{2,1,0:T(8,128)(2,1)S(1)}, u32[]{:S(2)}, u32[]{:S(2)}) collective-permute-start(bf16[1,384,128]{2,1,0:T(8,128)(2,1)} %get-tuple-element.97), channel_id=1, source_target_pairs={{0,8},{2,10},{4,12},{6,14},{8,0},{10,2},{12,4},{14,6},{16,24},{18,... | collective-permute-start | bytes 294920 | tf_op jit(solution)/shard_map/ppermute | solution.py:28
  180.4 6.9 %collective-permute-start.24 = (bf16[1,384,128]{2,1,0:T(8,128)(2,1)}, bf16[1,384,128]{2,1,0:T(8,128)(2,1)S(1)}, u32[]{:S(2)}, u32[]{:S(2)}) collective-permute-start(bf16[1,384,128]{2,1,0:T(8,128)(2,1)} %get-tuple-element.98), channel_id=1, source_target_pairs={{0,16},{2,18},{4,20},{6,22},{8,24},{10,26},{12,28},{14,30},{16,0},... | collective-permute-start | bytes 294920 | tf_op jit(solution)/shard_map/ppermute | solution.py:28
  182.7 6.7 %collective-permute-start.25 = (bf16[1,384,128]{2,1,0:T(8,128)(2,1)}, bf16[1,384,128]{2,1,0:T(8,128)(2,1)S(1)}, u32[]{:S(2)}, u32[]{:S(2)}) collective-permute-start(bf16[1,384,128]{2,1,0:T(8,128)(2,1)} %get-tuple-element.99), channel_id=1, source_target_pairs={{0,24},{2,26},{4,28},{6,30},{8,16},{10,18},{12,20},{14,22},{16,8},... | collective-permute-start | bytes 294920 | tf_op jit(solution)/shard_map/ppermute | solution.py:28
  182.8 12.1 %collective-permute-start.19 = (bf16[4,384,128]{2,1,0:T(8,128)(2,1)S(1)}, bf16[4,384,128]{2,1,0:T(8,128)(2,1)S(1)}, u32[]{:S(2)}, u32[]{:S(2)}) collective-permute-start(bf16[4,384,128]{2,1,0:T(8,128)(2,1)S(1)} %all-to-all-done.refs_0_), channel_id=1, source_target_pairs={{0,1},{1,0},{2,3},{3,2},{4,5},{5,4},{6,7},{7,6},{8,9},{9,8},{10,11... | collective-permute-start | bytes 1179656 | tf_op jit(solution)/shard_map/ppermute | solution.py:28
  184.3 18.6 %collective-permute-start.20 = (bf16[4,384,128]{2,1,0:T(8,128)(2,1)S(1)}, bf16[4,384,128]{2,1,0:T(8,128)(2,1)S(1)}, u32[]{:S(2)}, u32[]{:S(2)}) collective-permute-start(bf16[4,384,128]{2,1,0:T(8,128)(2,1)S(1)} %all-to-all-done.1.refs_1_), channel_id=1, source_target_pairs={{0,1},{1,0},{2,3},{3,2},{4,5},{5,4},{6,7},{7,6},{8,9},{9,8},{10,11... | collective-permute-start | bytes 1179656 | tf_op jit(solution)/shard_map/ppermute | solution.py:28
  189.4 22.6 %collective-permute-start.26 = (bf16[4,384,128]{2,1,0:T(8,128)(2,1)S(1)}, bf16[4,384,128]{2,1,0:T(8,128)(2,1)S(1)}, u32[]{:S(2)}, u32[]{:S(2)}) collective-permute-start(bf16[4,384,128]{2,1,0:T(8,128)(2,1)S(1)} %constant_dynamic-update-slice_fusion.8.refs_1_), channel_id=1, source_target_pairs={{0,1},{1,0},{2,3},{3,2},{4,5},{5,4},{6,7},{7,6},{8,9},{9,8},{10,11... | collective-permute-start | bytes 1179656 | tf_op jit(solution)/shard_map/ppermute | solution.py:28
  (8 other events, 42.4 us)
Sparse Core Ops, SparseCore 0:
  9.9 65.3 all-gather.4
  76.9 21.8 all-gather.6

commit v6 on v4

--- a/solution.py
+++ b/solution.py
@@ -289,110 +289,88 @@
     )(place, *queries, *keyvals)
 
 
-def finish_body(place_ref, *refs, chunks, others, has_sum, last, ordered):
-    refs = list(refs)
-    wide_ref = refs.pop()
-    out_ref = refs.pop()
-    total = refs.pop(0)[...] if has_sum else None
-    for m in range(1 + others):
-        attended_refs, weight_ref = refs[:chunks], refs[chunks]
-        refs = refs[chunks + 1 :]
+def finish_body(place_ref, *refs, chunks, has_sum, ordered):
+    attended_refs, weight_ref = refs[:chunks], refs[chunks]
+    out_ref, wide_ref = refs[-2:]
+
+    @pl.when(pl.program_id(0) == 0)
+    def _():
         for i, ref in enumerate(attended_refs):
             groups, _, size = ref.shape
             for g in range(groups):
                 head = i * groups + (g if ordered else lax.bitwise_xor(place_ref[0], g))
                 start = head * size if ordered else pl.multiple_of(head * size, size)
                 wide_ref[:, pl.ds(start, size)] = ref[g]
-        wide = wide_ref[...]
-        weight = weight_ref[0, 0] if m else weight_ref[...]
-        term = jnp.dot(wide, weight, preferred_element_type=f32)
-        total = term if total is None else total + term
-    if last:
-        rounded = total.astype(bf16)
-        out_ref[...] = jnp.dot(refs[0][...], rounded, preferred_element_type=f32).astype(bf16)
-    else:
-        out_ref[...] = total
-
-
-def finish(place, total, attended, w_out, other_weights, back, first_chunk, ordered):
-    groups, rows, size = attended[0][0].shape
-    split, head_shards, _, half = other_weights.shape
+
+    total = jnp.dot(wide_ref[...], weight_ref[...], preferred_element_type=f32)
+    if has_sum:
+        total += refs[chunks + 1][...]
+    out_ref[...] = total.astype(out_ref.dtype)
+
+
+def finish(place, attended, w_out, first_chunk, ordered, total=None, mask=None, kind=f32):
+    groups, rows, size = attended[0].shape
+    head_shards = lax.axis_size("head")
+    out_width = w_out.shape[1] // head_shards
     chunks = len(attended)
-    out_width = split * half
     depth = chunks * groups * size
     block = first_chunk // chunks
-    mine = lambda i, place: (0, i)
-    own = lambda i, place: (block, split * place[2] + i)
-    block_a = pl.BlockSpec((groups, rows, size), lambda i, place: (0, 0, 0))
-    specs, operands = [], []
+    parts = 2 if out_width % 256 == 0 else 1
+    tile = out_width // parts
+    count = parts * (head_shards if mask is None else 1)
+
+    def column(i, place):
+        return i if mask is None else lax.bitwise_xor(place[2], mask) * parts + i
+
+    specs = [pl.BlockSpec((groups, rows, size), lambda i, place: (0, 0, 0))] * chunks
+    specs.append(pl.BlockSpec((depth, tile), lambda i, place: (block, column(i, place))))
+    operands = [*attended, w_out]
     if total is not None:
-        specs.append(pl.BlockSpec((rows, half), mine))
+        specs.append(pl.BlockSpec((rows, tile), lambda i, place: (0, column(i, place))))
         operands.append(total)
-    for mask in range(head_shards):
-        specs += [block_a] * chunks
-        operands += [found[mask] for found in attended]
-        if mask == 0:
-            specs.append(pl.BlockSpec((depth, half), own))
-            operands.append(w_out)
-        else:
-            specs.append(
-                pl.BlockSpec(
-                    (1, 1, depth, half),
-                    lambda i, place, mask=mask: (i, lax.bitwise_xor(place[2], mask), block, 0),
-                )
-            )
-            operands.append(other_weights)
-    last = back is not None
-    if last:
-        specs.append(pl.BlockSpec(back.shape, lambda i, place: (0, 0)))
-        operands.append(back)
     return pl.pallas_call(
         functools.partial(
-            finish_body,
-            chunks=chunks,
-            others=head_shards - 1,
-            has_sum=total is not None,
-            last=last,
-            ordered=ordered,
+            finish_body, chunks=chunks, has_sum=total is not None, ordered=ordered
         ),
         grid_spec=pltpu.PrefetchScalarGridSpec(
             num_scalar_prefetch=1,
-            grid=(split,),
+            grid=(count,),
             in_specs=specs,
-            out_specs=pl.BlockSpec((rows, half), mine),
+            out_specs=pl.BlockSpec((rows, tile), lambda i, place: (0, i)),
             scratch_shapes=[pltpu.VMEM((rows, depth), bf16)],
         ),
-        out_shape=jax.ShapeDtypeStruct((rows, out_width), bf16 if last else f32),
-        compiler_params=pltpu.CompilerParams(vmem_limit_bytes=40 * mib),
+        out_shape=jax.ShapeDtypeStruct((rows, tile * count), kind),
+        compiler_params=params,
         cost_estimate=cost(
-            2 * rows * depth * head_shards * out_width,
-            2 * depth * head_shards * out_width + 8 * rows * out_width,
+            2 * rows * depth * tile * count, 2 * depth * tile * count + 8 * rows * tile * count
         ),
         name="finish",
     )(place, *operands)
 
 
-def splits(out_width, head_shards):
-    return head_shards == 2 and out_width % 256 == 0
-
-
-def fetch_weights(w_out, me, side, head_shards, arrived):
-    depth, width = w_out.shape
-    out_width = width // head_shards
-    if not splits(out_width, head_shards):
-        blocks = jnp.transpose(w_out.reshape(depth, head_shards, out_width), (1, 0, 2))
-        return lax.all_to_all(blocks, "head", split_axis=0, concat_axis=0, tiled=True)
-    half = out_width // 2
-    nothing = jnp.minimum(jnp.abs(arrived[0, 0, 0]).astype(jnp.int32), 0)
-    column = (1 - side) * out_width + (me % 2) * half + nothing
-    return lax.all_gather(lax.dynamic_slice(w_out, (0, column), (depth, half)), "head")
-
-
-def share_weights(found, out_width, head_shards):
-    if not splits(out_width, head_shards):
-        return found[None]
-    pairs = [[i, i + 1] for i in range(0, lax.axis_size("seq"), 2)]
-    return lax.all_gather(found, "seq", axis_index_groups=pairs)
+def close_body(back_ref, mine_ref, *refs):
+    out_ref = refs[-1]
+    total = mine_ref[...]
+    for ref in refs[:-1]:
+        total += ref[...].astype(f32)
+    rounded = total.astype(bf16)
+    out_ref[...] = jnp.dot(back_ref[...], rounded, preferred_element_type=f32).astype(bf16)
+
+
+def close(back, mine, others):
+    rows, width = mine.shape
+    parts = 4 if width % 512 == 0 else 1
+    tile = pl.BlockSpec((rows, width // parts), lambda i: (0, i))
+    return pl.pallas_call(
+        close_body,
+        grid=(parts,),
+        in_specs=[pl.BlockSpec((rows, rows), lambda i: (0, 0))] + [tile] * (1 + len(others)),
+        out_specs=tile,
+        out_shape=jax.ShapeDtypeStruct((rows, width), bf16),
+        compiler_params=params,
+        cost_estimate=cost(2 * rows * rows * width, 10 * rows * width),
+        name="close",
+    )(back, mine, *others)
 
 
 def per_device(tokens, survive, norm_gain, w_qkv, qk_gain, w_out):
@@ -430,9 +408,6 @@
             blocks, "seq", split_axis=0, concat_axis=0, axis_index_groups=planes, tiled=True
         )
 
-    def across(blocks):
-        return [blocks] + [flip(blocks, "head", mask) for mask in range(1, head_shards)]
-
     weights = jnp.transpose(w_qkv, (1, 0, 2))
     gains = jnp.transpose(qk_gain, (1, 0, 2))
 
@@ -450,7 +425,6 @@
     (blocks,), rest = project(place, None, weights, gains, sets, groups, operands)
     normed, chosen, back, count = rest
     arrived = [swap(blocks)]
-    fetched = fetch_weights(w_out, me, side, head_shards, first(arrived[0]))
 
     rest, asked, hops = range(1, chunks), None, []
     if chunks > 1:
@@ -485,18 +459,13 @@
         attended.append(found[0])
         returned.append(jnp.concatenate(swap(found)) if final else send_back(found[0]))
         if not final:
-            query, low_lane = asked, 0
-            gate = tuple(asked)
-    out_width = w_out.shape[1] // head_shards
-    if chunks > 1:
-        fetched = chain(fetched, first(asked))
-    other_weights = share_weights(fetched, out_width, head_shards)
-    total = None
-    if chunks > 1:
-        sooner = [across(found) for found in returned[:-1]]
-        total = finish(place, None, sooner, w_out, other_weights, None, 0, True)
-    last = across(returned[-1])
-    return finish(place, total, [last], w_out, other_weights, back, chunks - 1, False)
+            query, low_lane, gate = asked, 0, None
+    total = finish(place, returned[:-1], w_out, 0, True) if chunks > 1 else None
+    final = functools.partial(finish, place, returned[-1:], w_out, chunks - 1, False)
+    sent = [final(total=total, mask=mask, kind=bf16) for mask in range(1, head_shards)]
+    others = [flip(part, "head", mask) for mask, part in enumerate(sent, 1)]
+    mine = final(total=chain(total, *sent) if chunks > 1 else None, mask=0)
+    return close(back, mine, others)
 
 
 def solution(mesh):

time: 231 us -> 200 us (0.87)
  the two profiles are of different devices: /device:TPU:6 before, /device:TPU:0 now
where the time goes in v6:
time: 200 us; the launch traced here: 199 us
  Pallas kernels  83.2 us (42%)
  waiting for transfers between devices  59.3 us (30%)
  starting transfers between devices  48 us (24%)
  local copies, waits for them, and re-layouts  4.85 us (2%)
  other arithmetic  2.39 us (1%)
    ppermute x25, waiting for transfers between devices, flip(): return lax.ppermute(values, axis, [(i, i ^ mask) for i in range(size)])  58.8 us
    ppermute x25, starting transfers between devices, flip(): return lax.ppermute(values, axis, [(i, i ^ mask) for i in range(size)])  40.3 us
    pallas_call x3, Pallas kernels, project(): pl.pallas_call(functools.partial(project_body, steps=steps, groups=groups...  35.5 us
    pallas_call x3, Pallas kernels, attend(): pl.pallas_call(functools.partial(attend_body, groups=groups, ordered=orde...  26.5 us
    pallas_call x3, Pallas kernels, finish(): pl.pallas_call(functools.partial(finish_body, chunks=chunks, has_sum=tota...  16.7 us
    all_to_all x2, starting transfers between devices, send_back(): lax.all_to_all(blocks, 'seq', split_axis=0, concat_axis=0, axis_index_gro...  7.72 us
    unnamed x57, local copies, waits for them, and re-layouts  4.74 us
    pallas_call x1, Pallas kernels, close(): pl.pallas_call(close_body, grid=(parts,), in_specs=[pl.BlockSpec((rows, r...  4.56 us
  transfers between devices with their start and end apart: 27, of which 9 were waited for; matrix products, arithmetic and copies ran while one was open for 1% of the time, Pallas kernels for 27%

profile of v6, /device:TPU:0, one launch (start us, length us, event | category | flops | bytes accessed | tf_op | source)
XLA Modules:
  0.0 198.8 jit_solution(5232977429728030873)
XLA Ops:
  0.0 0.6 pad_add_fusion.place_ref
  0.6 13.4 %project.3 = (bf16[1,384,384]{2,1,0:T(8,128)(2,1)}, bf16[1,384,384]{2,1,0:T(8,128)(2,1)}, bf16[1,384,384]{2,1,0:T(8,128)(2,1)}, bf16[1,384,384]{2,1,0:T(8,128)(2...) custom-call(s32[3]{0:T(128)} %pad_add_fusion.place_ref, ...), custom_call_target="tpu_custom_call" | custom-call | flops 3623878656 | bytes 11796480 | tf_op jit(solution)/shard_map/project/pallas_call | solution.py:143
  14.0 3.1 %collective-permute-start = (bf16[1,384,384]{2,1,0:T(8,128)(2,1)}, bf16[1,384,384]{2,1,0:T(8,128)(2,1)S(1)}, u32[]{:S(2)}, u32[]{:S(2)}) collective-permute-start(bf16[1,384,384]{2,1,0:T(8,128)(2,1)} %get-tuple-element.52), channel_id=1, source_target_pairs={{0,8},{2,10},{4,12},{6,14},{8,0},{10,2},{12,4},{14,6},{16,24},{18,... | collective-permute-start | bytes 884744 | tf_op jit(solution)/shard_map/ppermute | solution.py:28
  17.1 2.6 %collective-permute-start.1 = (bf16[1,384,384]{2,1,0:T(8,128)(2,1)}, bf16[1,384,384]{2,1,0:T(8,128)(2,1)S(1)}, u32[]{:S(2)}, u32[]{:S(2)}) collective-permute-start(bf16[1,384,384]{2,1,0:T(8,128)(2,1)} %get-tuple-element.53), channel_id=1, source_target_pairs={{0,16},{2,18},{4,20},{6,22},{8,24},{10,26},{12,28},{14,30},{16,0},... | collective-permute-start | bytes 884744 | tf_op jit(solution)/shard_map/ppermute | solution.py:28
  19.7 10.2 %collective-permute-done.refs_1_ = bf16[1,384,384]{2,1,0:T(8,128)(2,1)S(1)} collective-permute-done((bf16[1,384,384]{2,1,0:T(8,128)(2,1)}, bf16[1,384,384]{2,1,0:T(8,128)(2,1)S(1)}, u32[]{:S(2)}, u32[]{:S(2)}) %collective-permute-start) | collective-permute-done | bytes 294944 | tf_op jit(solution)/shard_map/ppermute | solution.py:28
  29.9 13.3 %project.4 = (bf16[1,384,256]{2,1,0:T(8,128)(2,1)}, bf16[1,384,256]{2,1,0:T(8,128)(2,1)}, bf16[1,384,256]{2,1,0:T(8,128)(2,1)}, bf16[1,384,256]{2,1,0:T(8,128)(2...) custom-call(s32[3]{0:T(128)} %pad_add_fusion.place_ref, ...), custom_call_target="tpu_custom_call" | custom-call | flops 4831838208 | bytes 14942208 | tf_op jit(solution)/shard_map/project/pallas_call | solution.py:143
  43.4 1.7 collective-permute-start.3
  45.2 2.9 %collective-permute-start.4 = (bf16[1,384,256]{2,1,0:T(8,128)(2,1)S(1)}, bf16[1,384,256]{2,1,0:T(8,128)(2,1)S(1)}, u32[]{:S(2)}, u32[]{:S(2)}) collective-permute-start(bf16[1,384,256]{2,1,0:T(8,128)(2,1)S(1)} %copy-done.23), channel_id=1, source_target_pairs={{0,8},{2,10},{4,12},{6,14},{8,0},{10,2},{12,4},{14,6},{16,24},{18,... | collective-permute-start | bytes 589832 | tf_op jit(solution)/shard_map/ppermute | solution.py:28
  48.1 1.1 collective-permute-start.5
  49.2 1.5 collective-permute-start.6
  50.6 6.1 %collective-permute-done.4 = bf16[1,384,256]{2,1,0:T(8,128)(2,1)S(1)} collective-permute-done((bf16[1,384,256]{2,1,0:T(8,128)(2,1)S(1)}, bf16[1,384,256]{2,1,0:T(8,128)(2,1)S(1)}, u32[]{:S(2)}, u32[]{:S(2)}) %collective-permute-start.4) | collective-permute-done | bytes 196640 | tf_op jit(solution)/shard_map/ppermute | solution.py:28
  56.7 2.6 %collective-permute-start.8 = (bf16[1,384,256]{2,1,0:T(8,128)(2,1)}, bf16[1,384,256]{2,1,0:T(8,128)(2,1)S(1)}, u32[]{:S(2)}, u32[]{:S(2)}) collective-permute-start(bf16[1,384,256]{2,1,0:T(8,128)(2,1)} %get-tuple-element.77), channel_id=1, source_target_pairs={{0,16},{2,18},{4,20},{6,22},{8,24},{10,26},{12,28},{14,30},{16,0},... | collective-permute-start | bytes 589832 | tf_op jit(solution)/shard_map/ppermute | solution.py:28
  59.3 6.0 %collective-permute-done.5 = bf16[1,384,256]{2,1,0:T(8,128)(2,1)S(1)} collective-permute-done((bf16[1,384,256]{2,1,0:T(8,128)(2,1)S(1)}, bf16[1,384,256]{2,1,0:T(8,128)(2,1)S(1)}, u32[]{:S(2)}, u32[]{:S(2)}) %collective-permute-start.5) | collective-permute-done | bytes 196640 | tf_op jit(solution)/shard_map/ppermute | solution.py:28
  65.3 2.5 %collective-permute-start.9 = (bf16[1,384,256]{2,1,0:T(8,128)(2,1)}, bf16[1,384,256]{2,1,0:T(8,128)(2,1)S(1)}, u32[]{:S(2)}, u32[]{:S(2)}) collective-permute-start(bf16[1,384,256]{2,1,0:T(8,128)(2,1)} %get-tuple-element.78), channel_id=1, source_target_pairs={{0,24},{2,26},{4,28},{6,30},{8,16},{10,18},{12,20},{14,22},{16,8},... | collective-permute-start | bytes 589832 | tf_op jit(solution)/shard_map/ppermute | solution.py:28
  67.8 0.6 collective-permute-start.17
  69.1 8.8 %project.5 = (bf16[2,384,128]{2,1,0:T(8,128)(2,1)}, bf16[2,384,128]{2,1,0:T(8,128)(2,1)}, bf16[2,384,128]{2,1,0:T(8,128)(2,1)}, bf16[2,384,128]{2,1,0:T(8,128)(2,1)}) custom-call(s32[3]{0:T(128)} %pad_add_fusion.place_ref, bf16[3,3072,1536]{2,1,0:T(8,128)(2,1)} %bitcast.7, f32[12,2,128]{2,1,0:T(2,128)} %bitcast.10, s32[1,1]{1,0:T(1,128)S(6)} %max.12.refs_2_, ...), custom_call_target="tpu_custom_call" | custom-call | flops 2415919104 | bytes 8650752 | tf_op jit(solution)/shard_map/project/pallas_call | solution.py:143
  77.9 0.5 collective-permute-start.14
  78.4 2.9 %collective-permute-done.8 = bf16[1,384,256]{2,1,0:T(8,128)(2,1)S(1)} collective-permute-done((bf16[1,384,256]{2,1,0:T(8,128)(2,1)}, bf16[1,384,256]{2,1,0:T(8,128)(2,1)S(1)}, u32[]{:S(2)}, u32[]{:S(2)}) %collective-permute-start.8) | collective-permute-done | bytes 196640 | tf_op jit(solution)/shard_map/ppermute | solution.py:28
  81.4 0.6 collective-permute-start.15
  82.0 8.1 %collective-permute-start.10 = (bf16[2,384,128]{2,1,0:T(8,128)(2,1)}, bf16[2,384,128]{2,1,0:T(8,128)(2,1)S(1)}, u32[]{:S(2)}, u32[]{:S(2)}) collective-permute-start(bf16[2,384,128]{2,1,0:T(8,128)(2,1)} %get-tuple-element.79), channel_id=1, source_target_pairs={{0,8},{2,10},{4,12},{6,14},{8,0},{10,2},{12,4},{14,6},{16,24},{18,... | collective-permute-start | bytes 589832 | tf_op jit(solution)/shard_map/ppermute | solution.py:28
  90.0 5.1 %collective-permute-done.10.refs_1_ = bf16[2,384,128]{2,1,0:T(8,128)(2,1)S(1)} collective-permute-done((bf16[2,384,128]{2,1,0:T(8,128)(2,1)}, bf16[2,384,128]{2,1,0:T(8,128)(2,1)S(1)}, u32[]{:S(2)}, u32[]{:S(2)}) %collective-permute-start.10) | collective-permute-done | bytes 196640 | tf_op jit(solution)/shard_map/ppermute | solution.py:28
  95.1 0.5 collective-permute-start.18
  96.1 2.2 %collective-permute-start.11 = (bf16[2,384,128]{2,1,0:T(8,128)(2,1)}, bf16[2,384,128]{2,1,0:T(8,128)(2,1)S(1)}, u32[]{:S(2)}, u32[]{:S(2)}) collective-permute-start(bf16[2,384,128]{2,1,0:T(8,128)(2,1)} %get-tuple-element.80), channel_id=1, source_target_pairs={{0,16},{2,18},{4,20},{6,22},{8,24},{10,26},{12,28},{14,30},{16,0},... | collective-permute-start | bytes 589832 | tf_op jit(solution)/shard_map/ppermute | solution.py:28
  98.3 0.9 copy-done.16
  99.2 1.9 collective-permute-start.12
  101.1 8.9 %attend.3 = bf16[4,384,128]{2,1,0:T(8,128)(2,1)} custom-call(s32[3]{0:T(128)} %broadcast_maximum_fusion.2.place_ref, bf16[1,384,384]{2,1,0:T(8,128)(2,1)} %get-tuple-element.59.refs_0_, bf16[1,384,384]{2,1,0:T(8,128)(2,1)} %copy-done.8, bf16[1,384,384]{2,1,0:T(8,128)(2,1)} %copy-done.9, bf16[1,384,384]{2,1,0:T(8,128)(2,1)} %copy-done.10, ...), custom_call_target="tpu_custom_call" | custom-call | flops 2415919104 | bytes 3145728 | tf_op jit(solution)/shard_map/attend/pallas_call | solution.py:258
  110.0 3.5 %all-to-all-start = ((bf16[4,384,128]{2,1,0:T(8,128)(2,1)}), bf16[4,384,128]{2,1,0:T(8,128)(2,1)S(1)}, u32[]{:S(2)}, u32[]{:S(2)}) async-start(bf16[4,384,128]{2,1,0:T(8,128)(2,1)} %attend.3), calls=%async_computation | async-start | bytes 786432 | tf_op jit(solution)/shard_map/all_to_all | solution.py:407
  113.5 2.1 %collective-permute-start.19 = (bf16[4,384,256]{2,1,0:T(8,128)(2,1)S(1)}, bf16[4,384,256]{2,1,0:T(8,128)(2,1)S(1)}, u32[]{:S(2)}, u32[]{:S(2)}) collective-permute-start(bf16[4,384,256]{2,1,0:T(8,128)(2,1)S(1)} %constant_dynamic-update-slice_fusion.4.refs_4_), channel_id=1, source_target_pairs={{0,2},{2,0},{4,6},{6,4},{8,10},{10,8},{12,14},{14,12},{16,18},{18,... | collective-permute-start | bytes 2359304 | tf_op jit(solution)/shard_map/ppermute | solution.py:28
  115.7 0.6 broadcast_maximum_fusion.1.place_ref
  116.4 8.7 %attend.4 = bf16[4,384,128]{2,1,0:T(8,128)(2,1)} custom-call(s32[3]{0:T(128)} %broadcast_maximum_fusion.1.place_ref, bf16[2,384,128]{2,1,0:T(8,128)(2,1)} %get-tuple-element.86.refs_0_, bf16[2,384,128]{2,1,0:T(8,128)(2,1)} %copy-done.18, bf16[2,384,128]{2,1,0:T(8,128)(2,1)} %copy-done.19, bf16[2,384,128]{2,1,0:T(8,128)(2,1)} %copy-done.20, ...), custom_call_target="tpu_custom_call" | custom-call | flops 2415919104 | bytes 3145728 | tf_op jit(solution)/shard_map/attend/pallas_call | solution.py:258
  125.0 0.5 all-to-all-done.refs_0_
  125.5 4.3 %all-to-all-start.1 = ((bf16[4,384,128]{2,1,0:T(8,128)(2,1)}), bf16[4,384,128]{2,1,0:T(8,128)(2,1)S(1)}, u32[]{:S(2)}, u32[]{:S(2)}) async-start(bf16[4,384,128]{2,1,0:T(8,128)(2,1)} %attend.4), calls=%async_computation.1 | async-start | bytes 786432 | tf_op jit(solution)/shard_map/all_to_all | solution.py:407
  129.8 0.6 broadcast_maximum_fusion.place_ref
  130.4 0.9 copy-done.17
  131.3 8.9 %attend.5 = (bf16[1,384,128]{2,1,0:T(8,128)(2,1)}, bf16[1,384,128]{2,1,0:T(8,128)(2,1)}, bf16[1,384,128]{2,1,0:T(8,128)(2,1)}, bf16[1,384,128]{2,1,0:T(8,128)(2,1)}) custom-call(s32[3]{0:T(128)} %broadcast_maximum_fusion.place_ref, bf16[2,384,128]{2,1,0:T(8,128)(2,1)} %get-tuple-element.86.refs_0_, bf16[2,384,128]{2,1,0:T(8,128)(2,1)} %copy-done.18, ...), custom_call_target="tpu_custom_call" | custom-call | flops 2415919104 | bytes 3145728 | tf_op jit(solution)/shard_map/attend/pallas_call | solution.py:258
  140.1 2.0 %collective-permute-start.21 = (bf16[1,384,128]{2,1,0:T(8,128)(2,1)}, bf16[1,384,128]{2,1,0:T(8,128)(2,1)S(1)}, u32[]{:S(2)}, u32[]{:S(2)}) collective-permute-start(bf16[1,384,128]{2,1,0:T(8,128)(2,1)} %get-tuple-element.89), channel_id=1, source_target_pairs={{0,8},{2,10},{4,12},{6,14},{8,0},{10,2},{12,4},{14,6},{16,24},{18,... | collective-permute-start | bytes 294920 | tf_op jit(solution)/shard_map/ppermute | solution.py:28
  142.2 2.4 %collective-permute-start.22 = (bf16[1,384,128]{2,1,0:T(8,128)(2,1)}, bf16[1,384,128]{2,1,0:T(8,128)(2,1)S(1)}, u32[]{:S(2)}, u32[]{:S(2)}) collective-permute-start(bf16[1,384,128]{2,1,0:T(8,128)(2,1)} %get-tuple-element.90), channel_id=1, source_target_pairs={{0,16},{2,18},{4,20},{6,22},{8,24},{10,26},{12,28},{14,30},{16,0},... | collective-permute-start | bytes 294920 | tf_op jit(solution)/shard_map/ppermute | solution.py:28
  144.6 0.9 constant_dynamic-update-slice_fusion.11
  145.6 3.5 %collective-permute-done.22 = bf16[1,384,128]{2,1,0:T(8,128)(2,1)S(1)} collective-permute-done((bf16[1,384,128]{2,1,0:T(8,128)(2,1)}, bf16[1,384,128]{2,1,0:T(8,128)(2,1)S(1)}, u32[]{:S(2)}, u32[]{:S(2)}) %collective-permute-start.22) | collective-permute-done | bytes 98336 | tf_op jit(solution)/shard_map/ppermute | solution.py:28
  149.1 3.1 %collective-permute-done.23 = bf16[1,384,128]{2,1,0:T(8,128)(2,1)S(1)} collective-permute-done((bf16[1,384,128]{2,1,0:T(8,128)(2,1)}, bf16[1,384,128]{2,1,0:T(8,128)(2,1)S(1)}, u32[]{:S(2)}, u32[]{:S(2)}) %collective-permute-start.23) | collective-permute-done | bytes 98336 | tf_op jit(solution)/shard_map/ppermute | solution.py:28
  152.3 0.8 copy-done.2
  153.0 8.1 %finish.3.refs_2_ = f32[384,3072]{1,0:T(8,128)} custom-call(s32[3]{0:T(128)} %pad_add_fusion.place_ref, bf16[4,384,128]{2,1,0:T(8,128)(2,1)} %copy-done.1, bf16[4,384,128]{2,1,0:T(8,128)(2,1)} %copy-done.2, bf16[1536,3072]{1,0:T(8,128)(2,1)} %refs_1_.3), custom_call_target="tpu_custom_call" | custom-call | flops 2415919104 | bytes 15728640 | tf_op jit(solution)/shard_map/finish/pallas_call | solution.py:331
  161.1 4.2 %finish.4 = bf16[384,1536]{1,0:T(8,128)(2,1)} custom-call(s32[3]{0:T(128)} %pad_add_fusion.place_ref, bf16[4,384,128]{2,1,0:T(8,128)(2,1)} %copy-done, bf16[1536,3072]{1,0:T(8,128)(2,1)} %refs_1_.3, f32[384,3072]{1,0:T(8,128)} %finish.3.refs_2_), custom_call_target="tpu_custom_call" | custom-call | flops 603979776 | bytes 6291456 | tf_op jit(solution)/shard_map/finish/pallas_call | solution.py:331
  165.3 1.5 collective-permute-start.24
  166.8 4.5 %finish.5.mine_ref = f32[384,1536]{1,0:T(8,128)} custom-call(s32[3]{0:T(128)} %pad_add_fusion.place_ref, bf16[4,384,128]{2,1,0:T(8,128)(2,1)} %copy-done, bf16[1536,3072]{1,0:T(8,128)(2,1)} %refs_1_.3, f32[384,3072]{1,0:T(8,128)} %finish.3.refs_2_), custom_call_target="tpu_custom_call" | custom-call | flops 603979776 | bytes 6291456 | tf_op jit(solution)/shard_map/finish/pallas_call | solution.py:331
  171.3 21.9 %collective-permute-done.24.refs_0_ = bf16[384,1536]{1,0:T(8,128)(2,1)S(1)} collective-permute-done((bf16[384,1536]{1,0:T(8,128)(2,1)}, bf16[384,1536]{1,0:T(8,128)(2,1)S(1)}, u32[]{:S(2)}, u32[]{:S(2)}) %collective-permute-start.24) | collective-permute-done | bytes 1179680 | tf_op jit(solution)/shard_map/ppermute | solution.py:28
  193.2 1.1 copy-done.3
  194.3 4.6 %close.1 = bf16[384,1536]{1,0:T(8,128)(2,1)} custom-call(bf16[384,384]{1,0:T(8,128)(2,1)} %get-tuple-element.49.back_ref, f32[384,1536]{1,0:T(8,128)} %finish.5.mine_ref, bf16[384,1536]{1,0:T(8,128)(2,1)} %copy-done.3), custom_call_target="tpu_custom_call" | custom-call | flops 452984832 | bytes 5898240 | tf_op jit(solution)/shard_map/close/pallas_call | solution.py:364
  (85 shorter events, 1.1 us)
Async XLA Ops:
  14.0 15.9 %collective-permute-start = (bf16[1,384,384]{2,1,0:T(8,128)(2,1)}, bf16[1,384,384]{2,1,0:T(8,128)(2,1)S(1)}, u32[]{:S(2)}, u32[]{:S(2)}) collective-permute-start(bf16[1,384,384]{2,1,0:T(8,128)(2,1)} %get-tuple-element.52), channel_id=1, source_target_pairs={{0,8},{2,10},{4,12},{6,14},{8,0},{10,2},{12,4},{14,6},{16,24},{18,... | collective-permute-start | bytes 884744 | tf_op jit(solution)/shard_map/ppermute | solution.py:28
  17.1 26.1 %collective-permute-start.1 = (bf16[1,384,384]{2,1,0:T(8,128)(2,1)}, bf16[1,384,384]{2,1,0:T(8,128)(2,1)S(1)}, u32[]{:S(2)}, u32[]{:S(2)}) collective-permute-start(bf16[1,384,384]{2,1,0:T(8,128)(2,1)} %get-tuple-element.53), channel_id=1, source_target_pairs={{0,16},{2,18},{4,20},{6,22},{8,24},{10,26},{12,28},{14,30},{16,0},... | collective-permute-start | bytes 884744 | tf_op jit(solution)/shard_map/ppermute | solution.py:28
  19.7 23.5 %collective-permute-start.2 = (bf16[1,384,384]{2,1,0:T(8,128)(2,1)}, bf16[1,384,384]{2,1,0:T(8,128)(2,1)S(1)}, u32[]{:S(2)}, u32[]{:S(2)}) collective-permute-start(bf16[1,384,384]{2,1,0:T(8,128)(2,1)} %get-tuple-element.54), channel_id=1, source_target_pairs={{0,24},{2,26},{4,28},{6,30},{8,16},{10,18},{12,20},{14,22},{16,8},... | collective-permute-start | bytes 884744 | tf_op jit(solution)/shard_map/ppermute | solution.py:28
  29.9 13.4 %copy-start.8 = (bf16[1,384,384]{2,1,0:T(8,128)(2,1)}, bf16[1,384,384]{2,1,0:T(8,128)(2,1)S(1)}, u32[]{:S(2)}) copy-start(bf16[1,384,384]{2,1,0:T(8,128)(2,1)S(1)} %collective-permute-done.refs_1_) | copy-start | bytes 884740
  29.9 13.4 %copy-start.7 = (bf16[1,384,384]{2,1,0:T(8,128)(2,1)S(1)}, bf16[1,384,384]{2,1,0:T(8,128)(2,1)}, u32[]{:S(2)}) copy-start(bf16[1,384,384]{2,1,0:T(8,128)(2,1)} %get-tuple-element.59.refs_0_) | copy-start | bytes 884740
  43.1 2.1 %copy-start.23 = (bf16[1,384,256]{2,1,0:T(8,128)(2,1)S(1)}, bf16[1,384,256]{2,1,0:T(8,128)(2,1)}, u32[]{:S(2)}) copy-start(bf16[1,384,256]{2,1,0:T(8,128)(2,1)} %get-tuple-element.63) | copy-start | bytes 589828
  43.1 4.9 %copy-start.22 = (bf16[1,384,256]{2,1,0:T(8,128)(2,1)S(1)}, bf16[1,384,256]{2,1,0:T(8,128)(2,1)}, u32[]{:S(2)}) copy-start(bf16[1,384,256]{2,1,0:T(8,128)(2,1)} %get-tuple-element.64) | copy-start | bytes 589828
  43.1 6.0 %copy-start.21 = (bf16[1,384,256]{2,1,0:T(8,128)(2,1)S(1)}, bf16[1,384,256]{2,1,0:T(8,128)(2,1)}, u32[]{:S(2)}) copy-start(bf16[1,384,256]{2,1,0:T(8,128)(2,1)} %get-tuple-element.65) | copy-start | bytes 589828
  43.1 7.5 %copy-start.6 = (bf16[1,384,256]{2,1,0:T(8,128)(2,1)S(1)}, bf16[1,384,256]{2,1,0:T(8,128)(2,1)}, u32[]{:S(2)}) copy-start(bf16[1,384,256]{2,1,0:T(8,128)(2,1)} %get-tuple-element.58) | copy-start | bytes 589828
  43.2 24.6 %copy-start.9 = (bf16[1,384,384]{2,1,0:T(8,128)(2,1)}, bf16[1,384,384]{2,1,0:T(8,128)(2,1)S(1)}, u32[]{:S(2)}) copy-start(bf16[1,384,384]{2,1,0:T(8,128)(2,1)S(1)} %collective-permute-done.1.refs_2_) | copy-start | bytes 884740
  43.2 24.6 %copy-start.10 = (bf16[1,384,384]{2,1,0:T(8,128)(2,1)}, bf16[1,384,384]{2,1,0:T(8,128)(2,1)S(1)}, u32[]{:S(2)}) copy-start(bf16[1,384,384]{2,1,0:T(8,128)(2,1)S(1)} %collective-permute-done.2.refs_3_) | copy-start | bytes 884740
  43.2 25.2 %copy-start.5 = (bf16[1,384,256]{2,1,0:T(8,128)(2,1)S(1)}, bf16[1,384,256]{2,1,0:T(8,128)(2,1)}, u32[]{:S(2)}) copy-start(bf16[1,384,256]{2,1,0:T(8,128)(2,1)} %get-tuple-element.75) | copy-start | bytes 589828
  43.4 34.5 %copy-start.4 = (bf16[4,384,256]{2,1,0:T(8,128)(2,1)}, bf16[4,384,256]{2,1,0:T(8,128)(2,1)S(1)}, u32[]{:S(2)}) copy-start(bf16[4,384,256]{2,1,0:T(8,128)(2,1)S(1)} %pad_maximum_fusion.refs_4_) | copy-start | bytes 2359300
  43.4 25.0 %collective-permute-start.3 = (bf16[4,384,256]{2,1,0:T(8,128)(2,1)S(1)}, bf16[4,384,256]{2,1,0:T(8,128)(2,1)S(1)}, u32[]{:S(2)}, u32[]{:S(2)}) collective-permute-start(bf16[4,384,256]{2,1,0:T(8,128)(2,1)S(1)} %pad_maximum_fusion.refs_4_), channel_id=1, source_target_pairs={{0,4},{2,6},{4,0},{6,2},{8,12},{10,14},{12,8},{14,10},{16,20},{18,... | collective-permute-start | bytes 2359304 | tf_op jit(solution)/shard_map/ppermute | solution.py:28
  45.2 11.5 %collective-permute-start.4 = (bf16[1,384,256]{2,1,0:T(8,128)(2,1)S(1)}, bf16[1,384,256]{2,1,0:T(8,128)(2,1)S(1)}, u32[]{:S(2)}, u32[]{:S(2)}) collective-permute-start(bf16[1,384,256]{2,1,0:T(8,128)(2,1)S(1)} %copy-done.23), channel_id=1, source_target_pairs={{0,8},{2,10},{4,12},{6,14},{8,0},{10,2},{12,4},{14,6},{16,24},{18,... | collective-permute-start | bytes 589832 | tf_op jit(solution)/shard_map/ppermute | solution.py:28
  48.1 17.2 %collective-permute-start.5 = (bf16[1,384,256]{2,1,0:T(8,128)(2,1)S(1)}, bf16[1,384,256]{2,1,0:T(8,128)(2,1)S(1)}, u32[]{:S(2)}, u32[]{:S(2)}) collective-permute-start(bf16[1,384,256]{2,1,0:T(8,128)(2,1)S(1)} %copy-done.22), channel_id=1, source_target_pairs={{0,16},{2,18},{4,20},{6,22},{8,24},{10,26},{12,28},{14,30},{16,0},... | collective-permute-start | bytes 589832 | tf_op jit(solution)/shard_map/ppermute | solution.py:28
  49.2 18.6 %collective-permute-start.6 = (bf16[1,384,256]{2,1,0:T(8,128)(2,1)S(1)}, bf16[1,384,256]{2,1,0:T(8,128)(2,1)S(1)}, u32[]{:S(2)}, u32[]{:S(2)}) collective-permute-start(bf16[1,384,256]{2,1,0:T(8,128)(2,1)S(1)} %copy-done.21), channel_id=1, source_target_pairs={{0,24},{2,26},{4,28},{6,30},{8,16},{10,18},{12,20},{14,22},{16,8},... | collective-permute-start | bytes 589832 | tf_op jit(solution)/shard_map/ppermute | solution.py:28
  56.7 21.2 %collective-permute-start.7 = (bf16[1,384,256]{2,1,0:T(8,128)(2,1)}, bf16[1,384,256]{2,1,0:T(8,128)(2,1)S(1)}, u32[]{:S(2)}, u32[]{:S(2)}) collective-permute-start(bf16[1,384,256]{2,1,0:T(8,128)(2,1)} %get-tuple-element.76), channel_id=1, source_target_pairs={{0,8},{2,10},{4,12},{6,14},{8,0},{10,2},{12,4},{14,6},{16,24},{18,... | collective-permute-start | bytes 589832 | tf_op jit(solution)/shard_map/ppermute | solution.py:28
  56.7 24.6 %collective-permute-start.8 = (bf16[1,384,256]{2,1,0:T(8,128)(2,1)}, bf16[1,384,256]{2,1,0:T(8,128)(2,1)S(1)}, u32[]{:S(2)}, u32[]{:S(2)}) collective-permute-start(bf16[1,384,256]{2,1,0:T(8,128)(2,1)} %get-tuple-element.77), channel_id=1, source_target_pairs={{0,16},{2,18},{4,20},{6,22},{8,24},{10,26},{12,28},{14,30},{16,0},... | collective-permute-start | bytes 589832 | tf_op jit(solution)/shard_map/ppermute | solution.py:28
  65.3 16.1 %collective-permute-start.9 = (bf16[1,384,256]{2,1,0:T(8,128)(2,1)}, bf16[1,384,256]{2,1,0:T(8,128)(2,1)S(1)}, u32[]{:S(2)}, u32[]{:S(2)}) collective-permute-start(bf16[1,384,256]{2,1,0:T(8,128)(2,1)} %get-tuple-element.78), channel_id=1, source_target_pairs={{0,24},{2,26},{4,28},{6,30},{8,16},{10,18},{12,20},{14,22},{16,8},... | collective-permute-start | bytes 589832 | tf_op jit(solution)/shard_map/ppermute | solution.py:28
  67.8 27.3 %copy-start.12 = (bf16[4,384,256]{2,1,0:T(8,128)(2,1)}, bf16[4,384,256]{2,1,0:T(8,128)(2,1)S(1)}, u32[]{:S(2)}) copy-start(bf16[4,384,256]{2,1,0:T(8,128)(2,1)S(1)} %constant_dynamic-update-slice_fusion.refs_4_) | copy-start | bytes 2359300
  67.8 27.3 %collective-permute-start.17 = (bf16[4,384,256]{2,1,0:T(8,128)(2,1)S(1)}, bf16[4,384,256]{2,1,0:T(8,128)(2,1)}, u32[]{:S(2)}, u32[]{:S(2)}) collective-permute-start(bf16[4,384,256]{2,1,0:T(8,128)(2,1)S(1)} %constant_dynamic-update-slice_fusion.refs_4_), channel_id=1, source_target_pairs={{0,4},{2,6},{4,0},{6,2},{8,12},{10,14},{12,8},{14,10},{16,20},{18,... | collective-permute-start | bytes 2359304 | tf_op jit(solution)/shard_map/ppermute | solution.py:28
  68.5 9.5 %copy-start.14 = (bf16[4,384,256]{2,1,0:T(8,128)(2,1)}, bf16[4,384,256]{2,1,0:T(8,128)(2,1)S(1)}, u32[]{:S(2)}) copy-start(bf16[4,384,256]{2,1,0:T(8,128)(2,1)S(1)} %collective-permute-done.3.refs_6_) | copy-start | bytes 2359300
  69.1 26.5 %copy-start.13 = (s32[3]{0:T(128)S(1)}, s32[3]{0:T(128)}, u32[]{:S(2)}) copy-start(s32[3]{0:T(128)} %pad_add_fusion.place_ref) | copy-start | bytes 40
  77.9 18.2 %collective-permute-start.13 = (bf16[4,384,256]{2,1,0:T(8,128)(2,1)S(1)}, bf16[4,384,256]{2,1,0:T(8,128)(2,1)S(1)}, u32[]{:S(2)}, u32[]{:S(2)}) collective-permute-start(bf16[4,384,256]{2,1,0:T(8,128)(2,1)S(1)} %pad_maximum_fusion.refs_4_), channel_id=1, source_target_pairs={{0,2},{2,0},{4,6},{6,4},{8,10},{10,8},{12,14},{14,12},{16,18},{18,... | collective-permute-start | bytes 2359304 | tf_op jit(solution)/shard_map/ppermute | solution.py:28
  77.9 20.4 %collective-permute-start.14 = (bf16[4,384,256]{2,1,0:T(8,128)(2,1)S(1)}, bf16[4,384,256]{2,1,0:T(8,128)(2,1)S(1)}, u32[]{:S(2)}, u32[]{:S(2)}) collective-permute-start(bf16[4,384,256]{2,1,0:T(8,128)(2,1)S(1)} %collective-permute-done.3.refs_6_), channel_id=1, source_target_pairs={{0,2},{2,0},{4,6},{6,4},{8,10},{10,8},{12,14},{14,12},{16,18},{18,... | collective-permute-start | bytes 2359304 | tf_op jit(solution)/shard_map/ppermute | solution.py:28
  81.4 32.1 %copy-start.11 = (bf16[4,384,256]{2,1,0:T(8,128)(2,1)}, bf16[4,384,256]{2,1,0:T(8,128)(2,1)S(1)}, u32[]{:S(2)}) copy-start(bf16[4,384,256]{2,1,0:T(8,128)(2,1)S(1)} %constant_dynamic-update-slice_fusion.4.refs_4_) | copy-start | bytes 2359300
  81.4 34.2 %collective-permute-start.15 = (bf16[4,384,256]{2,1,0:T(8,128)(2,1)S(1)}, bf16[4,384,256]{2,1,0:T(8,128)(2,1)}, u32[]{:S(2)}, u32[]{:S(2)}) collective-permute-start(bf16[4,384,256]{2,1,0:T(8,128)(2,1)S(1)} %constant_dynamic-update-slice_fusion.4.refs_4_), channel_id=1, source_target_pairs={{0,4},{2,6},{4,0},{6,2},{8,12},{10,14},{12,8},{14,10},{16,20},{18,... | collective-permute-start | bytes 2359304 | tf_op jit(solution)/shard_map/ppermute | solution.py:28
  82.0 13.1 %collective-permute-start.10 = (bf16[2,384,128]{2,1,0:T(8,128)(2,1)}, bf16[2,384,128]{2,1,0:T(8,128)(2,1)S(1)}, u32[]{:S(2)}, u32[]{:S(2)}) collective-permute-start(bf16[2,384,128]{2,1,0:T(8,128)(2,1)} %get-tuple-element.79), channel_id=1, source_target_pairs={{0,8},{2,10},{4,12},{6,14},{8,0},{10,2},{12,4},{14,6},{16,24},{18,... | collective-permute-start | bytes 589832 | tf_op jit(solution)/shard_map/ppermute | solution.py:28
  95.1 21.2 %copy-start.18 = (bf16[2,384,128]{2,1,0:T(8,128)(2,1)}, bf16[2,384,128]{2,1,0:T(8,128)(2,1)S(1)}, u32[]{:S(2)}) copy-start(bf16[2,384,128]{2,1,0:T(8,128)(2,1)S(1)} %collective-permute-done.10.refs_1_) | copy-start | bytes 589828
  95.1 21.2 %collective-permute-start.16 = (bf16[4,384,256]{2,1,0:T(8,128)(2,1)S(1)}, bf16[4,384,256]{2,1,0:T(8,128)(2,1)}, u32[]{:S(2)}, u32[]{:S(2)}) collective-permute-start(bf16[4,384,256]{2,1,0:T(8,128)(2,1)S(1)} %constant_dynamic-update-slice_fusion.refs_4_), channel_id=1, source_target_pairs={{0,2},{2,0},{4,6},{6,4},{8,10},{10,8},{12,14},{14,12},{16,18},{18,... | collective-permute-start | bytes 2359304 | tf_op jit(solution)/shard_map/ppermute | solution.py:28
  95.1 21.2 %collective-permute-start.18 = (bf16[4,384,256]{2,1,0:T(8,128)(2,1)}, bf16[4,384,256]{2,1,0:T(8,128)(2,1)}, u32[]{:S(2)}, u32[]{:S(2)}) collective-permute-start(bf16[4,384,256]{2,1,0:T(8,128)(2,1)} %collective-permute-done.17.refs_6_), channel_id=1, source_target_pairs={{0,2},{2,0},{4,6},{6,4},{8,10},{10,8},{12,14},{14,12},{16,18},{18,... | collective-permute-start | bytes 2359304 | tf_op jit(solution)/shard_map/ppermute | solution.py:28
  96.1 2.2 %copy-start.15 = (bf16[4,384,256]{2,1,0:T(8,128)(2,1)}, bf16[4,384,256]{2,1,0:T(8,128)(2,1)S(1)}, u32[]{:S(2)}) copy-start(bf16[4,384,256]{2,1,0:T(8,128)(2,1)S(1)} %collective-permute-done.13.refs_5_) | copy-start | bytes 2359300
  96.1 17.4 %collective-permute-start.11 = (bf16[2,384,128]{2,1,0:T(8,128)(2,1)}, bf16[2,384,128]{2,1,0:T(8,128)(2,1)S(1)}, u32[]{:S(2)}, u32[]{:S(2)}) collective-permute-start(bf16[2,384,128]{2,1,0:T(8,128)(2,1)} %get-tuple-element.80), channel_id=1, source_target_pairs={{0,16},{2,18},{4,20},{6,22},{8,24},{10,26},{12,28},{14,30},{16,0},... | collective-permute-start | bytes 589832 | tf_op jit(solution)/shard_map/ppermute | solution.py:28
  99.2 16.5 %collective-permute-start.12 = (bf16[2,384,128]{2,1,0:T(8,128)(2,1)}, bf16[2,384,128]{2,1,0:T(8,128)(2,1)S(1)}, u32[]{:S(2)}, u32[]{:S(2)}) collective-permute-start(bf16[2,384,128]{2,1,0:T(8,128)(2,1)} %get-tuple-element.81), channel_id=1, source_target_pairs={{0,24},{2,26},{4,28},{6,30},{8,16},{10,18},{12,20},{14,22},{16,8},... | collective-permute-start | bytes 589832 | tf_op jit(solution)/shard_map/ppermute | solution.py:28
  110.0 15.5 %all-to-all-start = ((bf16[4,384,128]{2,1,0:T(8,128)(2,1)}), bf16[4,384,128]{2,1,0:T(8,128)(2,1)S(1)}, u32[]{:S(2)}, u32[]{:S(2)}) async-start(bf16[4,384,128]{2,1,0:T(8,128)(2,1)} %attend.3), calls=%async_computation | async-start | bytes 786432 | tf_op jit(solution)/shard_map/all_to_all | solution.py:407
  113.5 2.8 %copy-start.19 = (bf16[2,384,128]{2,1,0:T(8,128)(2,1)}, bf16[2,384,128]{2,1,0:T(8,128)(2,1)S(1)}, u32[]{:S(2)}) copy-start(bf16[2,384,128]{2,1,0:T(8,128)(2,1)S(1)} %collective-permute-done.11.refs_2_) | copy-start | bytes 589828
  113.5 16.9 %collective-permute-start.19 = (bf16[4,384,256]{2,1,0:T(8,128)(2,1)S(1)}, bf16[4,384,256]{2,1,0:T(8,128)(2,1)S(1)}, u32[]{:S(2)}, u32[]{:S(2)}) collective-permute-start(bf16[4,384,256]{2,1,0:T(8,128)(2,1)S(1)} %constant_dynamic-update-slice_fusion.4.refs_4_), channel_id=1, source_target_pairs={{0,2},{2,0},{4,6},{6,4},{8,10},{10,8},{12,14},{14,12},{16,18},{18,... | collective-permute-start | bytes 2359304 | tf_op jit(solution)/shard_map/ppermute | solution.py:28
  115.6 14.8 %collective-permute-start.20 = (bf16[4,384,256]{2,1,0:T(8,128)(2,1)}, bf16[4,384,256]{2,1,0:T(8,128)(2,1)}, u32[]{:S(2)}, u32[]{:S(2)}) collective-permute-start(bf16[4,384,256]{2,1,0:T(8,128)(2,1)} %collective-permute-done.15.refs_6_), channel_id=1, source_target_pairs={{0,2},{2,0},{4,6},{6,4},{8,10},{10,8},{12,14},{14,12},{16,18},{18,... | collective-permute-start | bytes 2359304 | tf_op jit(solution)/shard_map/ppermute | solution.py:28
  125.5 14.6 %copy-start.1 = (bf16[4,384,128]{2,1,0:T(8,128)(2,1)}, bf16[4,384,128]{2,1,0:T(8,128)(2,1)S(1)}, u32[]{:S(2)}) copy-start(bf16[4,384,128]{2,1,0:T(8,128)(2,1)S(1)} %all-to-all-done.refs_0_) | copy-start | bytes 1179652
  125.5 26.7 %all-to-all-start.1 = ((bf16[4,384,128]{2,1,0:T(8,128)(2,1)}), bf16[4,384,128]{2,1,0:T(8,128)(2,1)S(1)}, u32[]{:S(2)}, u32[]{:S(2)}) async-start(bf16[4,384,128]{2,1,0:T(8,128)(2,1)} %attend.4), calls=%async_computation.1 | async-start | bytes 786432 | tf_op jit(solution)/shard_map/all_to_all | solution.py:407
  130.4 0.9 copy-start.17
  140.1 5.4 %collective-permute-start.21 = (bf16[1,384,128]{2,1,0:T(8,128)(2,1)}, bf16[1,384,128]{2,1,0:T(8,128)(2,1)S(1)}, u32[]{:S(2)}, u32[]{:S(2)}) collective-permute-start(bf16[1,384,128]{2,1,0:T(8,128)(2,1)} %get-tuple-element.89), channel_id=1, source_target_pairs={{0,8},{2,10},{4,12},{6,14},{8,0},{10,2},{12,4},{14,6},{16,24},{18,... | collective-permute-start | bytes 294920 | tf_op jit(solution)/shard_map/ppermute | solution.py:28
  142.2 6.9 %collective-permute-start.22 = (bf16[1,384,128]{2,1,0:T(8,128)(2,1)}, bf16[1,384,128]{2,1,0:T(8,128)(2,1)S(1)}, u32[]{:S(2)}, u32[]{:S(2)}) collective-permute-start(bf16[1,384,128]{2,1,0:T(8,128)(2,1)} %get-tuple-element.90), channel_id=1, source_target_pairs={{0,16},{2,18},{4,20},{6,22},{8,24},{10,26},{12,28},{14,30},{16,0},... | collective-permute-start | bytes 294920 | tf_op jit(solution)/shard_map/ppermute | solution.py:28
  144.5 7.7 %collective-permute-start.23 = (bf16[1,384,128]{2,1,0:T(8,128)(2,1)}, bf16[1,384,128]{2,1,0:T(8,128)(2,1)S(1)}, u32[]{:S(2)}, u32[]{:S(2)}) collective-permute-start(bf16[1,384,128]{2,1,0:T(8,128)(2,1)} %get-tuple-element.91), channel_id=1, source_target_pairs={{0,24},{2,26},{4,28},{6,30},{8,16},{10,18},{12,20},{14,22},{16,8},... | collective-permute-start | bytes 294920 | tf_op jit(solution)/shard_map/ppermute | solution.py:28
  152.2 8.9 %copy-start = (bf16[4,384,128]{2,1,0:T(8,128)(2,1)}, bf16[4,384,128]{2,1,0:T(8,128)(2,1)S(1)}, u32[]{:S(2)}) copy-start(bf16[4,384,128]{2,1,0:T(8,128)(2,1)S(1)} %constant_dynamic-update-slice_fusion.8.refs_0_) | copy-start | bytes 1179652
  165.3 27.9 %collective-permute-start.24 = (bf16[384,1536]{1,0:T(8,128)(2,1)}, bf16[384,1536]{1,0:T(8,128)(2,1)S(1)}, u32[]{:S(2)}, u32[]{:S(2)}) collective-permute-start(bf16[384,1536]{1,0:T(8,128)(2,1)} %finish.4), channel_id=1, source_target_pairs={{0,1},{1,0},{2,3},{3,2},{4,5},{5,4},{6,7},{7,6},{8,9},{9,8},{10,11... | collective-permute-start | bytes 3538952 | tf_op jit(solution)/shard_map/ppermute | solution.py:28
  193.2 1.1 copy-start.3
  (3 other events, 2.4 us)

commit v7 on v6

--- a/solution.py
+++ b/solution.py
@@ -289,6 +289,10 @@
     )(place, *queries, *keyvals)
 
 
+def pieces_of(width):
+    return 2 if width % 256 == 0 else 1
+
+
 def finish_body(place_ref, *refs, chunks, has_sum, ordered):
     attended_refs, weight_ref = refs[:chunks], refs[chunks]
     out_ref, wide_ref = refs[-2:]
@@ -308,19 +312,19 @@
     out_ref[...] = total.astype(out_ref.dtype)
 
 
-def finish(place, attended, w_out, first_chunk, ordered, total=None, mask=None, kind=f32):
+def finish(place, attended, w_out, first_chunk, ordered, total=None, mask=None, piece=None, kind=f32):
     groups, rows, size = attended[0].shape
     head_shards = lax.axis_size("head")
     out_width = w_out.shape[1] // head_shards
     chunks = len(attended)
     depth = chunks * groups * size
     block = first_chunk // chunks
-    parts = 2 if out_width % 256 == 0 else 1
+    parts = pieces_of(out_width)
     tile = out_width // parts
-    count = parts * (head_shards if mask is None else 1)
+    count = parts * head_shards if mask is None else parts if piece is None else 1
 
     def column(i, place):
-        return i if mask is None else lax.bitwise_xor(place[2], mask) * parts + i
+        return i if mask is None else lax.bitwise_xor(place[2], mask) * parts + i + (piece or 0)
 
     specs = [pl.BlockSpec((groups, rows, size), lambda i, place: (0, 0, 0))] * chunks
     specs.append(pl.BlockSpec((depth, tile), lambda i, place: (block, column(i, place))))
@@ -348,29 +352,38 @@
     )(place, *operands)
 
 
-def close_body(back_ref, mine_ref, *refs):
+def close_body(back_ref, mine_ref, *refs, pieces, sub):
     out_ref = refs[-1]
     total = mine_ref[...]
-    for ref in refs[:-1]:
-        total += ref[...].astype(f32)
+    for low in range(0, len(refs) - 1, pieces):
+        found = refs[low][...]
+        for piece in range(1, pieces):
+            found = jnp.where(pl.program_id(0) >= piece * sub, refs[low + piece][...], found)
+        total += found.astype(f32)
     rounded = total.astype(bf16)
     out_ref[...] = jnp.dot(back_ref[...], rounded, preferred_element_type=f32).astype(bf16)
 
 
 def close(back, mine, others):
     rows, width = mine.shape
-    parts = 4 if width % 512 == 0 else 1
-    tile = pl.BlockSpec((rows, width // parts), lambda i: (0, i))
+    pieces = len(others[0])
+    sub = pieces_of(width // pieces)
+    shape = (rows, width // pieces // sub)
+    tile = pl.BlockSpec(shape, lambda i: (0, i))
+    came = [
+        pl.BlockSpec(shape, lambda i, low=piece * sub: (0, jnp.clip(i - low, 0, sub - 1)))
+        for piece in range(pieces)
+    ]
     return pl.pallas_call(
-        close_body,
-        grid=(parts,),
-        in_specs=[pl.BlockSpec((rows, rows), lambda i: (0, 0))] + [tile] * (1 + len(others)),
+        functools.partial(close_body, pieces=pieces, sub=sub),
+        grid=(pieces * sub,),
+        in_specs=[pl.BlockSpec((rows, rows), lambda i: (0, 0)), tile] + came * len(others),
         out_specs=tile,
         out_shape=jax.ShapeDtypeStruct((rows, width), bf16),
         compiler_params=params,
         cost_estimate=cost(2 * rows * rows * width, 10 * rows * width),
         name="close",
-    )(back, mine, *others)
+    )(back, mine, *[part for parts in others for part in parts])
 
 
 def per_device(tokens, survive, norm_gain, w_qkv, qk_gain, w_out):
@@ -389,15 +402,12 @@
     def stack(blocks):
         return jnp.concatenate([block[:, :, : 2 * size] for block in blocks])
 
-    def everywhere(stacked, gate):
+    def everywhere(stacked):
         found = {0: stacked}
         mask = ring // 2
         while mask:
             for known in list(found):
-                source = found[known]
-                if gate is not None and mask < ring // 2:
-                    source = chain(source, gate)
-                found[known | mask] = flip(source, "seq", mask)
+                found[known | mask] = flip(found[known], "seq", mask)
             mask //= 2
         return [found[mask] for mask in range(ring)]
 
@@ -427,44 +437,56 @@
     arrived = [swap(blocks)]
 
     rest, asked, hops = range(1, chunks), None, []
+    stacks = []
+    for chunk in rest:
+        source = chain(normed, stacks[-1] if stacks else first(arrived[0]))
+        sets = [((1, 2), (chunk,))]
+        (made,), _ = project(place, (count, source, chosen), weights, gains, sets, groups)
+        if chunk == 1:
+            stacks.append(stack(list(chain(tuple(arrived[0]), made[0]))))
+            arrived.append(send(made))
+        else:
+            arrived.append(send(made, first(arrived[-1])))
+            stacks.append(stack(arrived[chunk - 1]))
     if chunks > 1:
-        prepared = (count, chain(normed, first(arrived[0])), chosen)
-        sets = [((1, 2), (chunk,)) for chunk in rest]
-        made, _ = project(place, prepared, weights, gains, sets, groups)
-        stacks = [stack(list(chain(tuple(arrived[0]), made[0][0])))]
-        arrived.append(send(made[0]))
-        for blocks in made[1:]:
-            arrived.append(send(blocks, first(arrived[-1])))
         hop = flip(stacks[0], "seq", ring // 2) if ring > 1 else stacks[0]
-        stacks.append(stack(arrived[1]))
-        ready = later(count, hop, stacks[1])
+        ready = later(count, hop, stacks[-1])
         sets = [((0,), tuple(rest))]
         (made,), _ = project(place, (ready, normed, chosen), weights, gains, sets, groups)
-        gate = made[0]
-        stacks += [stack(blocks) for blocks in arrived[2:]]
+    stacks.append(stack(arrived[-1]))
+    if chunks > 1:
         asked = send(made, stacks[-1])
         hops = [flip(stacks[-1], "seq", ring // 2)] if ring > 1 else []
-    else:
-        gate, stacks = None, [stack(arrived[0])]
 
     attended, returned = [], []
     query, low_lane = arrived[0], 2 * size
     for chunk in range(chunks):
         final = chunk == chunks - 1
-        keyvals = everywhere(stacks[chunk], gate)
+        keyvals = everywhere(stacks[chunk])
         before = [stacks[-1]] + attended[-1:] + (hops if chunk else []) + (returned[:1] if final else [])
         ready = later(place, *query[1:], *before)
         row = max(chunk - 1, 0)
         found = attend(ready, query, row, low_lane, keyvals, shards, not final)
         attended.append(found[0])
-        returned.append(jnp.concatenate(swap(found)) if final else send_back(found[0]))
-        if not final:
-            query, low_lane, gate = asked, 0, None
-    total = finish(place, returned[:-1], w_out, 0, True) if chunks > 1 else None
+        if final:
+            came = swap(found)
+            returned.append(jnp.concatenate(came))
+        else:
+            returned.append(send_back(found[0]))
+            query, low_lane = asked, 0
+    total = None
+    if chunks > 1:
+        sooner = list(chain(tuple(returned[:-1]), first(came)))
+        total = finish(place, sooner, w_out, 0, True)
     final = functools.partial(finish, place, returned[-1:], w_out, chunks - 1, False)
-    sent = [final(total=total, mask=mask, kind=bf16) for mask in range(1, head_shards)]
-    others = [flip(part, "head", mask) for mask, part in enumerate(sent, 1)]
-    mine = final(total=chain(total, *sent) if chunks > 1 else None, mask=0)
+    pieces = range(pieces_of(w_out.shape[1] // head_shards))
+    sent = [
+        [final(total=total, mask=mask, piece=piece, kind=bf16) for piece in pieces]
+        for mask in range(1, head_shards)
+    ]
+    others = [[flip(part, "head", mask) for part in parts] for mask, parts in enumerate(sent, 1)]
+    last = [part for parts in sent for part in parts]
+    mine = final(total=chain(total, *last) if chunks > 1 else None, mask=0)
     return close(back, mine, others)
 
 

time: 200 us -> 209 us (1.045)
  Pallas kernels: 83.2 us -> 98.4 us
  waiting for transfers between devices: 59.3 us -> 52.4 us
    pallas_call x3, Pallas kernels: 26.5 us -> 33.9 us  [attend(): pl.pallas_call(functools.partial(attend_body, groups=groups, ordered=orde...]
    ppermute x25 -> x26, waiting for transfers between devices: 58.8 us -> 52.4 us  [flip(): return lax.ppermute(values, axis, [(i, i ^ mask) for i in range(size)])]
    pallas_call x3 -> x4, Pallas kernels: 35.5 us -> 39.8 us  [project(): pl.pallas_call(functools.partial(project_body, steps=steps, groups=groups...]
    pallas_call x3 -> x4, Pallas kernels: 16.7 us -> 20.1 us  [finish(): pl.pallas_call(functools.partial(finish_body, chunks=chunks, has_sum=tota...]
    unnamed x57 -> x51, local copies, waits for them, and re-layouts: 4.74 us -> 3.72 us
    ppermute x25 -> x26, starting transfers between devices: 40.3 us -> 40 us  [flip(): return lax.ppermute(values, axis, [(i, i ^ mask) for i in range(size)])]
  transfers between devices with their start and end apart: 27 -> 28, of which waited for: 9 -> 9; matrix products, arithmetic and copies ran while one was open for 1% -> 2% of each run, Pallas kernels for 27% -> 31%
where the time goes in v7:
time: 209 us; the launch traced here: 207 us
  Pallas kernels  98.4 us (47%)
  waiting for transfers between devices  52.4 us (25%)
  starting transfers between devices  49.4 us (24%)
  local copies, waits for them, and re-layouts  3.82 us (2%)
  other arithmetic  2.43 us (1%)
    ppermute x26, waiting for transfers between devices, flip(): return lax.ppermute(values, axis, [(i, i ^ mask) for i in range(size)])  52.4 us
    ppermute x26, starting transfers between devices, flip(): return lax.ppermute(values, axis, [(i, i ^ mask) for i in range(size)])  40 us
    pallas_call x4, Pallas kernels, project(): pl.pallas_call(functools.partial(project_body, steps=steps, groups=groups...  39.8 us
    pallas_call x3, Pallas kernels, attend(): pl.pallas_call(functools.partial(attend_body, groups=groups, ordered=orde...  33.9 us
    pallas_call x4, Pallas kernels, finish(): pl.pallas_call(functools.partial(finish_body, chunks=chunks, has_sum=tota...  20.1 us
    all_to_all x2, starting transfers between devices, send_back(): lax.all_to_all(blocks, 'seq', split_axis=0, concat_axis=0, axis_index_gro...  9.35 us
    pallas_call x1, Pallas kernels, close(): pl.pallas_call(functools.partial(close_body, pieces=pieces, sub=sub), gri...  4.71 us
  transfers between devices with their start and end apart: 28, of which 9 were waited for; matrix products, arithmetic and copies ran while one was open for 2% of the time, Pallas kernels for 31%

profile of v7, /device:TPU:0, one launch (start us, length us, event | category | flops | bytes accessed | tf_op | source)
XLA Modules:
  0.0 207.5 jit_solution(8671278405910925411)
XLA Ops:
  0.0 0.6 pad_add_fusion.place_ref
  0.6 13.4 %project.4 = (bf16[1,384,384]{2,1,0:T(8,128)(2,1)}, bf16[1,384,384]{2,1,0:T(8,128)(2,1)}, bf16[1,384,384]{2,1,0:T(8,128)(2,1)}, bf16[1,384,384]{2,1,0:T(8,128)(2...) custom-call(s32[3]{0:T(128)} %pad_add_fusion.place_ref, ...), custom_call_target="tpu_custom_call" | custom-call | flops 3623878656 | bytes 11796480 | tf_op jit(solution)/shard_map/project/pallas_call | solution.py:143
  14.0 3.1 %collective-permute-start = (bf16[1,384,384]{2,1,0:T(8,128)(2,1)}, bf16[1,384,384]{2,1,0:T(8,128)(2,1)S(1)}, u32[]{:S(2)}, u32[]{:S(2)}) collective-permute-start(bf16[1,384,384]{2,1,0:T(8,128)(2,1)} %get-tuple-element.53), channel_id=1, source_target_pairs={{0,8},{2,10},{4,12},{6,14},{8,0},{10,2},{12,4},{14,6},{16,24},{18,... | collective-permute-start | bytes 884744 | tf_op jit(solution)/shard_map/ppermute | solution.py:28
  17.1 2.6 %collective-permute-start.1 = (bf16[1,384,384]{2,1,0:T(8,128)(2,1)}, bf16[1,384,384]{2,1,0:T(8,128)(2,1)S(1)}, u32[]{:S(2)}, u32[]{:S(2)}) collective-permute-start(bf16[1,384,384]{2,1,0:T(8,128)(2,1)} %get-tuple-element.54), channel_id=1, source_target_pairs={{0,16},{2,18},{4,20},{6,22},{8,24},{10,26},{12,28},{14,30},{16,0},... | collective-permute-start | bytes 884744 | tf_op jit(solution)/shard_map/ppermute | solution.py:28
  19.7 10.2 %collective-permute-done.refs_1_ = bf16[1,384,384]{2,1,0:T(8,128)(2,1)S(1)} collective-permute-done((bf16[1,384,384]{2,1,0:T(8,128)(2,1)}, bf16[1,384,384]{2,1,0:T(8,128)(2,1)S(1)}, u32[]{:S(2)}, u32[]{:S(2)}) %collective-permute-start) | collective-permute-done | bytes 294944 | tf_op jit(solution)/shard_map/ppermute | solution.py:28
  29.9 8.9 %project.5 = (bf16[1,384,256]{2,1,0:T(8,128)(2,1)}, bf16[1,384,256]{2,1,0:T(8,128)(2,1)}, bf16[1,384,256]{2,1,0:T(8,128)(2,1)}, bf16[1,384,256]{2,1,0:T(8,128)(2,1)}) custom-call(s32[3]{0:T(128)} %pad_add_fusion.place_ref, bf16[3,3072,1536]{2,1,0:T(8,128)(2,1)} %bitcast.6, f32[12,2,128]{2,1,0:T(2,128)} %bitcast.10, s32[1,1]{1,0:T(1,128)} %get-tuple-element.67.refs_2_, ...), custom_call_target="tpu_custom_call" | custom-call | flops 2415919104 | bytes 8650752 | tf_op jit(solution)/shard_map/project/pallas_call | solution.py:143
  38.8 2.0 collective-permute-done.1.refs_2_
  41.0 1.6 collective-permute-start.3
  42.6 5.5 %collective-permute-start.4 = (bf16[1,384,256]{2,1,0:T(8,128)(2,1)S(1)}, bf16[1,384,256]{2,1,0:T(8,128)(2,1)S(1)}, u32[]{:S(2)}, u32[]{:S(2)}) collective-permute-start(bf16[1,384,256]{2,1,0:T(8,128)(2,1)S(1)} %copy-done.20), channel_id=1, source_target_pairs={{0,8},{2,10},{4,12},{6,14},{8,0},{10,2},{12,4},{14,6},{16,24},{18,... | collective-permute-start | bytes 589832 | tf_op jit(solution)/shard_map/ppermute | solution.py:28
  48.1 1.1 collective-permute-start.5
  49.1 1.5 collective-permute-start.6
  50.6 8.9 %project.7 = (bf16[1,384,256]{2,1,0:T(8,128)(2,1)}, bf16[1,384,256]{2,1,0:T(8,128)(2,1)}, bf16[1,384,256]{2,1,0:T(8,128)(2,1)}, bf16[1,384,256]{2,1,0:T(8,128)(2,1)}) custom-call(s32[3]{0:T(128)} %pad_add_fusion.place_ref, bf16[3,3072,1536]{2,1,0:T(8,128)(2,1)} %bitcast.7, f32[12,2,128]{2,1,0:T(2,128)} %bitcast.11, s32[1,1]{1,0:T(1,128)} %get-tuple-element.67.refs_2_, ...), custom_call_target="tpu_custom_call" | custom-call | flops 2415919104 | bytes 8650752 | tf_op jit(solution)/shard_map/project/pallas_call | solution.py:143
  59.6 1.0 collective-permute-start.7
  60.6 4.6 %collective-permute-done.5 = bf16[1,384,256]{2,1,0:T(8,128)(2,1)S(1)} collective-permute-done((bf16[1,384,256]{2,1,0:T(8,128)(2,1)S(1)}, bf16[1,384,256]{2,1,0:T(8,128)(2,1)S(1)}, u32[]{:S(2)}, u32[]{:S(2)}) %collective-permute-start.5) | collective-permute-done | bytes 196640 | tf_op jit(solution)/shard_map/ppermute | solution.py:28
  65.2 0.6 collective-permute-start.17
  65.8 5.0 %collective-permute-start.8 = (bf16[1,384,256]{2,1,0:T(8,128)(2,1)}, bf16[1,384,256]{2,1,0:T(8,128)(2,1)S(1)}, u32[]{:S(2)}, u32[]{:S(2)}) collective-permute-start(bf16[1,384,256]{2,1,0:T(8,128)(2,1)} %get-tuple-element.79), channel_id=1, source_target_pairs={{0,16},{2,18},{4,20},{6,22},{8,24},{10,26},{12,28},{14,30},{16,0},... | collective-permute-start | bytes 589832 | tf_op jit(solution)/shard_map/ppermute | solution.py:28
  70.9 0.9 constant_dynamic-update-slice_fusion.7
  71.8 1.4 collective-permute-start.9
  73.3 11.7 %collective-permute-done.8 = bf16[1,384,256]{2,1,0:T(8,128)(2,1)S(1)} collective-permute-done((bf16[1,384,256]{2,1,0:T(8,128)(2,1)}, bf16[1,384,256]{2,1,0:T(8,128)(2,1)S(1)}, u32[]{:S(2)}, u32[]{:S(2)}) %collective-permute-start.8) | collective-permute-done | bytes 196640 | tf_op jit(solution)/shard_map/ppermute | solution.py:28
  85.0 1.6 collective-permute-start.15
  87.3 8.6 %project.6 = (bf16[2,384,128]{2,1,0:T(8,128)(2,1)}, bf16[2,384,128]{2,1,0:T(8,128)(2,1)}, bf16[2,384,128]{2,1,0:T(8,128)(2,1)}, bf16[2,384,128]{2,1,0:T(8,128)(2,1)}) custom-call(s32[3]{0:T(128)} %pad_add_fusion.place_ref, bf16[3,3072,1536]{2,1,0:T(8,128)(2,1)} %bitcast.8, f32[12,2,128]{2,1,0:T(2,128)} %bitcast.12, s32[1,1]{1,0:T(1,128)S(6)} %max.12.refs_2_, ...), custom_call_target="tpu_custom_call" | custom-call | flops 2415919104 | bytes 8650752 | tf_op jit(solution)/shard_map/project/pallas_call | solution.py:143
  95.9 3.6 %collective-permute-start.10 = (bf16[2,384,128]{2,1,0:T(8,128)(2,1)}, bf16[2,384,128]{2,1,0:T(8,128)(2,1)S(1)}, u32[]{:S(2)}, u32[]{:S(2)}) collective-permute-start(bf16[2,384,128]{2,1,0:T(8,128)(2,1)} %get-tuple-element.81), channel_id=1, source_target_pairs={{0,8},{2,10},{4,12},{6,14},{8,0},{10,2},{12,4},{14,6},{16,24},{18,... | collective-permute-start | bytes 589832 | tf_op jit(solution)/shard_map/ppermute | solution.py:28
  99.7 0.5 broadcast_maximum_fusion.2.place_ref
  100.2 5.0 %collective-permute-done.10.refs_1_ = bf16[2,384,128]{2,1,0:T(8,128)(2,1)S(1)} collective-permute-done((bf16[2,384,128]{2,1,0:T(8,128)(2,1)}, bf16[2,384,128]{2,1,0:T(8,128)(2,1)S(1)}, u32[]{:S(2)}, u32[]{:S(2)}) %collective-permute-start.10) | collective-permute-done | bytes 196640 | tf_op jit(solution)/shard_map/ppermute | solution.py:28
  105.3 1.7 collective-permute-start.11
  106.9 2.4 %collective-permute-start.12 = (bf16[2,384,128]{2,1,0:T(8,128)(2,1)}, bf16[2,384,128]{2,1,0:T(8,128)(2,1)S(1)}, u32[]{:S(2)}, u32[]{:S(2)}) collective-permute-start(bf16[2,384,128]{2,1,0:T(8,128)(2,1)} %get-tuple-element.83), channel_id=1, source_target_pairs={{0,24},{2,26},{4,28},{6,30},{8,16},{10,18},{12,20},{14,22},{16,8},... | collective-permute-start | bytes 589832 | tf_op jit(solution)/shard_map/ppermute | solution.py:28
  109.4 11.4 %attend.3 = bf16[4,384,128]{2,1,0:T(8,128)(2,1)} custom-call(s32[3]{0:T(128)} %broadcast_maximum_fusion.2.place_ref, bf16[1,384,384]{2,1,0:T(8,128)(2,1)} %get-tuple-element.60.refs_0_, bf16[1,384,384]{2,1,0:T(8,128)(2,1)} %copy-done.9, bf16[1,384,384]{2,1,0:T(8,128)(2,1)} %copy-done.10, bf16[1,384,384]{2,1,0:T(8,128)(2,1)} %copy-done.11, ...), custom_call_target="tpu_custom_call" | custom-call | flops 2415919104 | bytes 3145728 | tf_op jit(solution)/shard_map/attend/pallas_call | solution.py:258
  120.8 3.5 %all-to-all-start = ((bf16[4,384,128]{2,1,0:T(8,128)(2,1)}), bf16[4,384,128]{2,1,0:T(8,128)(2,1)S(1)}, u32[]{:S(2)}, u32[]{:S(2)}) async-start(bf16[4,384,128]{2,1,0:T(8,128)(2,1)} %attend.3), calls=%async_computation | async-start | bytes 786432 | tf_op jit(solution)/shard_map/all_to_all | solution.py:417
  124.8 0.6 broadcast_maximum_fusion.1.place_ref
  125.5 11.2 %attend.4 = bf16[4,384,128]{2,1,0:T(8,128)(2,1)} custom-call(s32[3]{0:T(128)} %broadcast_maximum_fusion.1.place_ref, bf16[2,384,128]{2,1,0:T(8,128)(2,1)} %get-tuple-element.86.refs_0_, bf16[2,384,128]{2,1,0:T(8,128)(2,1)} %copy-done.15, bf16[2,384,128]{2,1,0:T(8,128)(2,1)} %copy-done.16, bf16[2,384,128]{2,1,0:T(8,128)(2,1)} %copy-done.17, ...), custom_call_target="tpu_custom_call" | custom-call | flops 2415919104 | bytes 3145728 | tf_op jit(solution)/shard_map/attend/pallas_call | solution.py:258
  136.7 5.9 %all-to-all-start.1 = ((bf16[4,384,128]{2,1,0:T(8,128)(2,1)}), bf16[4,384,128]{2,1,0:T(8,128)(2,1)S(1)}, u32[]{:S(2)}, u32[]{:S(2)}) async-start(bf16[4,384,128]{2,1,0:T(8,128)(2,1)} %attend.4), calls=%async_computation.1 | async-start | bytes 786432 | tf_op jit(solution)/shard_map/all_to_all | solution.py:417
  142.6 0.6 broadcast_maximum_fusion.place_ref
  143.2 11.3 %attend.5 = (bf16[1,384,128]{2,1,0:T(8,128)(2,1)}, bf16[1,384,128]{2,1,0:T(8,128)(2,1)}, bf16[1,384,128]{2,1,0:T(8,128)(2,1)}, bf16[1,384,128]{2,1,0:T(8,128)(2,1)}) custom-call(s32[3]{0:T(128)} %broadcast_maximum_fusion.place_ref, bf16[2,384,128]{2,1,0:T(8,128)(2,1)} %get-tuple-element.86.refs_0_, bf16[2,384,128]{2,1,0:T(8,128)(2,1)} %copy-done.15, ...), custom_call_target="tpu_custom_call" | custom-call | flops 2415919104 | bytes 3145728 | tf_op jit(solution)/shard_map/attend/pallas_call | solution.py:258
  154.5 2.2 %collective-permute-start.21 = (bf16[1,384,128]{2,1,0:T(8,128)(2,1)}, bf16[1,384,128]{2,1,0:T(8,128)(2,1)S(1)}, u32[]{:S(2)}, u32[]{:S(2)}) collective-permute-start(bf16[1,384,128]{2,1,0:T(8,128)(2,1)} %get-tuple-element.89), channel_id=1, source_target_pairs={{0,8},{2,10},{4,12},{6,14},{8,0},{10,2},{12,4},{14,6},{16,24},{18,... | collective-permute-start | bytes 294920 | tf_op jit(solution)/shard_map/ppermute | solution.py:28
  156.7 2.2 %collective-permute-start.22 = (bf16[1,384,128]{2,1,0:T(8,128)(2,1)}, bf16[1,384,128]{2,1,0:T(8,128)(2,1)S(1)}, u32[]{:S(2)}, u32[]{:S(2)}) collective-permute-start(bf16[1,384,128]{2,1,0:T(8,128)(2,1)} %get-tuple-element.90), channel_id=1, source_target_pairs={{0,16},{2,18},{4,20},{6,22},{8,24},{10,26},{12,28},{14,30},{16,0},... | collective-permute-start | bytes 294920 | tf_op jit(solution)/shard_map/ppermute | solution.py:28
  159.2 0.9 constant_dynamic-update-slice_fusion.11
  160.1 3.4 %collective-permute-done.22 = bf16[1,384,128]{2,1,0:T(8,128)(2,1)S(1)} collective-permute-done((bf16[1,384,128]{2,1,0:T(8,128)(2,1)}, bf16[1,384,128]{2,1,0:T(8,128)(2,1)S(1)}, u32[]{:S(2)}, u32[]{:S(2)}) %collective-permute-start.22) | collective-permute-done | bytes 98336 | tf_op jit(solution)/shard_map/ppermute | solution.py:28
  163.5 2.1 %collective-permute-done.23 = bf16[1,384,128]{2,1,0:T(8,128)(2,1)S(1)} collective-permute-done((bf16[1,384,128]{2,1,0:T(8,128)(2,1)}, bf16[1,384,128]{2,1,0:T(8,128)(2,1)S(1)}, u32[]{:S(2)}, u32[]{:S(2)}) %collective-permute-start.23) | collective-permute-done | bytes 98336 | tf_op jit(solution)/shard_map/ppermute | solution.py:28
  165.7 0.8 copy-done.2
  166.4 8.1 %finish.4.refs_2_ = f32[384,3072]{1,0:T(8,128)} custom-call(s32[3]{0:T(128)} %pad_add_fusion.place_ref, bf16[4,384,128]{2,1,0:T(8,128)(2,1)} %copy-done.1, bf16[4,384,128]{2,1,0:T(8,128)(2,1)} %copy-done.2, bf16[1536,3072]{1,0:T(8,128)(2,1)} %refs_1_.5), custom_call_target="tpu_custom_call" | custom-call | flops 2415919104 | bytes 15728640 | tf_op jit(solution)/shard_map/finish/pallas_call | solution.py:335
  174.6 3.6 %finish.5 = bf16[384,768]{1,0:T(8,128)(2,1)} custom-call(s32[3]{0:T(128)} %pad_add_fusion.place_ref, bf16[4,384,128]{2,1,0:T(8,128)(2,1)} %copy-done, bf16[1536,3072]{1,0:T(8,128)(2,1)} %refs_1_.5, f32[384,3072]{1,0:T(8,128)} %finish.4.refs_2_), custom_call_target="tpu_custom_call" | custom-call | flops 301989888 | bytes 3145728 | tf_op jit(solution)/shard_map/finish/pallas_call | solution.py:335
  178.2 3.8 %finish.6 = bf16[384,768]{1,0:T(8,128)(2,1)} custom-call(s32[3]{0:T(128)} %pad_add_fusion.place_ref, bf16[4,384,128]{2,1,0:T(8,128)(2,1)} %copy-done, bf16[1536,3072]{1,0:T(8,128)(2,1)} %refs_1_.5, f32[384,3072]{1,0:T(8,128)} %finish.4.refs_2_), custom_call_target="tpu_custom_call" | custom-call | flops 301989888 | bytes 3145728 | tf_op jit(solution)/shard_map/finish/pallas_call | solution.py:335
  182.0 1.5 collective-permute-start.24
  184.0 4.5 %finish.7.mine_ref = f32[384,1536]{1,0:T(8,128)} custom-call(s32[3]{0:T(128)} %pad_add_fusion.place_ref, bf16[4,384,128]{2,1,0:T(8,128)(2,1)} %copy-done, bf16[1536,3072]{1,0:T(8,128)(2,1)} %refs_1_.5, f32[384,3072]{1,0:T(8,128)} %finish.4.refs_2_), custom_call_target="tpu_custom_call" | custom-call | flops 603979776 | bytes 6291456 | tf_op jit(solution)/shard_map/finish/pallas_call | solution.py:335
  188.5 7.1 %collective-permute-done.24.refs_0_ = bf16[384,768]{1,0:T(8,128)(2,1)S(1)} collective-permute-done((bf16[384,768]{1,0:T(8,128)(2,1)S(1)}, bf16[384,768]{1,0:T(8,128)(2,1)S(1)}, u32[]{:S(2)}, u32[]{:S(2)}) %collective-permute-start.24) | collective-permute-done | bytes 589856 | tf_op jit(solution)/shard_map/ppermute | solution.py:28
  195.6 6.3 %collective-permute-done.25.refs_1_ = bf16[384,768]{1,0:T(8,128)(2,1)S(1)} collective-permute-done((bf16[384,768]{1,0:T(8,128)(2,1)}, bf16[384,768]{1,0:T(8,128)(2,1)S(1)}, u32[]{:S(2)}, u32[]{:S(2)}) %collective-permute-start.25) | collective-permute-done | bytes 589856 | tf_op jit(solution)/shard_map/ppermute | solution.py:28
  201.9 0.8 copy-done.5
  202.7 4.7 %close.1 = bf16[384,1536]{1,0:T(8,128)(2,1)} custom-call(bf16[384,384]{1,0:T(8,128)(2,1)} %get-tuple-element.50.back_ref, f32[384,1536]{1,0:T(8,128)} %finish.7.mine_ref, bf16[384,768]{1,0:T(8,128)(2,1)} %copy-done.4, bf16[384,768]{1,0:T(8,128)(2,1)} %copy-done.5), custom_call_target="tpu_custom_call" | custom-call | flops 452984832 | bytes 5898240 | tf_op jit(solution)/shard_map/close/pallas_call | solution.py:377
  (83 shorter events, 2.1 us)
Async XLA Ops:
  14.0 15.9 %collective-permute-start = (bf16[1,384,384]{2,1,0:T(8,128)(2,1)}, bf16[1,384,384]{2,1,0:T(8,128)(2,1)S(1)}, u32[]{:S(2)}, u32[]{:S(2)}) collective-permute-start(bf16[1,384,384]{2,1,0:T(8,128)(2,1)} %get-tuple-element.53), channel_id=1, source_target_pairs={{0,8},{2,10},{4,12},{6,14},{8,0},{10,2},{12,4},{14,6},{16,24},{18,... | collective-permute-start | bytes 884744 | tf_op jit(solution)/shard_map/ppermute | solution.py:28
  17.1 23.7 %collective-permute-start.1 = (bf16[1,384,384]{2,1,0:T(8,128)(2,1)}, bf16[1,384,384]{2,1,0:T(8,128)(2,1)S(1)}, u32[]{:S(2)}, u32[]{:S(2)}) collective-permute-start(bf16[1,384,384]{2,1,0:T(8,128)(2,1)} %get-tuple-element.54), channel_id=1, source_target_pairs={{0,16},{2,18},{4,20},{6,22},{8,24},{10,26},{12,28},{14,30},{16,0},... | collective-permute-start | bytes 884744 | tf_op jit(solution)/shard_map/ppermute | solution.py:28
  19.7 21.1 %collective-permute-start.2 = (bf16[1,384,384]{2,1,0:T(8,128)(2,1)}, bf16[1,384,384]{2,1,0:T(8,128)(2,1)S(1)}, u32[]{:S(2)}, u32[]{:S(2)}) collective-permute-start(bf16[1,384,384]{2,1,0:T(8,128)(2,1)} %get-tuple-element.55), channel_id=1, source_target_pairs={{0,24},{2,26},{4,28},{6,30},{8,16},{10,18},{12,20},{14,22},{16,8},... | collective-permute-start | bytes 884744 | tf_op jit(solution)/shard_map/ppermute | solution.py:28
  29.9 11.0 %copy-start.9 = (bf16[1,384,384]{2,1,0:T(8,128)(2,1)}, bf16[1,384,384]{2,1,0:T(8,128)(2,1)S(1)}, u32[]{:S(2)}) copy-start(bf16[1,384,384]{2,1,0:T(8,128)(2,1)S(1)} %collective-permute-done.refs_1_) | copy-start | bytes 884740
  29.9 11.0 %copy-start.8 = (bf16[1,384,384]{2,1,0:T(8,128)(2,1)S(1)}, bf16[1,384,384]{2,1,0:T(8,128)(2,1)}, u32[]{:S(2)}) copy-start(bf16[1,384,384]{2,1,0:T(8,128)(2,1)} %get-tuple-element.60.refs_0_) | copy-start | bytes 884740
  38.8 3.8 %copy-start.20 = (bf16[1,384,256]{2,1,0:T(8,128)(2,1)S(1)}, bf16[1,384,256]{2,1,0:T(8,128)(2,1)}, u32[]{:S(2)}) copy-start(bf16[1,384,256]{2,1,0:T(8,128)(2,1)} %get-tuple-element.64) | copy-start | bytes 589828
  38.8 9.3 %copy-start.19 = (bf16[1,384,256]{2,1,0:T(8,128)(2,1)S(1)}, bf16[1,384,256]{2,1,0:T(8,128)(2,1)}, u32[]{:S(2)}) copy-start(bf16[1,384,256]{2,1,0:T(8,128)(2,1)} %get-tuple-element.65) | copy-start | bytes 589828
  38.8 10.4 %copy-start.18 = (bf16[1,384,256]{2,1,0:T(8,128)(2,1)S(1)}, bf16[1,384,256]{2,1,0:T(8,128)(2,1)}, u32[]{:S(2)}) copy-start(bf16[1,384,256]{2,1,0:T(8,128)(2,1)} %get-tuple-element.66) | copy-start | bytes 589828
  40.8 18.7 %copy-start.10 = (bf16[1,384,384]{2,1,0:T(8,128)(2,1)}, bf16[1,384,384]{2,1,0:T(8,128)(2,1)S(1)}, u32[]{:S(2)}) copy-start(bf16[1,384,384]{2,1,0:T(8,128)(2,1)S(1)} %collective-permute-done.1.refs_2_) | copy-start | bytes 884740
  40.8 18.7 %copy-start.11 = (bf16[1,384,384]{2,1,0:T(8,128)(2,1)}, bf16[1,384,384]{2,1,0:T(8,128)(2,1)S(1)}, u32[]{:S(2)}) copy-start(bf16[1,384,384]{2,1,0:T(8,128)(2,1)S(1)} %collective-permute-done.2.refs_3_) | copy-start | bytes 884740
  41.0 18.5 %copy-start.3 = (bf16[4,384,256]{2,1,0:T(8,128)(2,1)}, bf16[4,384,256]{2,1,0:T(8,128)(2,1)S(1)}, u32[]{:S(2)}) copy-start(bf16[4,384,256]{2,1,0:T(8,128)(2,1)S(1)} %pad_maximum_fusion.refs_4_) | copy-start | bytes 2359300
  41.0 32.2 %collective-permute-start.3 = (bf16[4,384,256]{2,1,0:T(8,128)(2,1)S(1)}, bf16[4,384,256]{2,1,0:T(8,128)(2,1)}, u32[]{:S(2)}, u32[]{:S(2)}) collective-permute-start(bf16[4,384,256]{2,1,0:T(8,128)(2,1)S(1)} %pad_maximum_fusion.refs_4_), channel_id=1, source_target_pairs={{0,4},{2,6},{4,0},{6,2},{8,12},{10,14},{12,8},{14,10},{16,20},{18,... | collective-permute-start | bytes 2359304 | tf_op jit(solution)/shard_map/ppermute | solution.py:28
  42.6 53.3 %collective-permute-start.13 = (bf16[4,384,256]{2,1,0:T(8,128)(2,1)S(1)}, bf16[4,384,256]{2,1,0:T(8,128)(2,1)}, u32[]{:S(2)}, u32[]{:S(2)}) collective-permute-start(bf16[4,384,256]{2,1,0:T(8,128)(2,1)S(1)} %pad_maximum_fusion.refs_4_), channel_id=1, source_target_pairs={{0,2},{2,0},{4,6},{6,4},{8,10},{10,8},{12,14},{14,12},{16,18},{18,... | collective-permute-start | bytes 2359304 | tf_op jit(solution)/shard_map/ppermute | solution.py:28
  42.6 17.0 %collective-permute-start.4 = (bf16[1,384,256]{2,1,0:T(8,128)(2,1)S(1)}, bf16[1,384,256]{2,1,0:T(8,128)(2,1)S(1)}, u32[]{:S(2)}, u32[]{:S(2)}) collective-permute-start(bf16[1,384,256]{2,1,0:T(8,128)(2,1)S(1)} %copy-done.20), channel_id=1, source_target_pairs={{0,8},{2,10},{4,12},{6,14},{8,0},{10,2},{12,4},{14,6},{16,24},{18,... | collective-permute-start | bytes 589832 | tf_op jit(solution)/shard_map/ppermute | solution.py:28
  48.1 17.1 %collective-permute-start.5 = (bf16[1,384,256]{2,1,0:T(8,128)(2,1)S(1)}, bf16[1,384,256]{2,1,0:T(8,128)(2,1)S(1)}, u32[]{:S(2)}, u32[]{:S(2)}) collective-permute-start(bf16[1,384,256]{2,1,0:T(8,128)(2,1)S(1)} %copy-done.19), channel_id=1, source_target_pairs={{0,16},{2,18},{4,20},{6,22},{8,24},{10,26},{12,28},{14,30},{16,0},... | collective-permute-start | bytes 589832 | tf_op jit(solution)/shard_map/ppermute | solution.py:28
  49.1 10.4 %copy-start.7 = (bf16[1,384,256]{2,1,0:T(8,128)(2,1)S(1)}, bf16[1,384,256]{2,1,0:T(8,128)(2,1)}, u32[]{:S(2)}) copy-start(bf16[1,384,256]{2,1,0:T(8,128)(2,1)} %get-tuple-element.59) | copy-start | bytes 589828
  49.1 16.1 %collective-permute-start.6 = (bf16[1,384,256]{2,1,0:T(8,128)(2,1)S(1)}, bf16[1,384,256]{2,1,0:T(8,128)(2,1)S(1)}, u32[]{:S(2)}, u32[]{:S(2)}) collective-permute-start(bf16[1,384,256]{2,1,0:T(8,128)(2,1)S(1)} %copy-done.18), channel_id=1, source_target_pairs={{0,24},{2,26},{4,28},{6,30},{8,16},{10,18},{12,20},{14,22},{16,8},... | collective-permute-start | bytes 589832 | tf_op jit(solution)/shard_map/ppermute | solution.py:28
  59.6 12.2 %collective-permute-start.7 = (bf16[1,384,256]{2,1,0:T(8,128)(2,1)}, bf16[1,384,256]{2,1,0:T(8,128)(2,1)S(1)}, u32[]{:S(2)}, u32[]{:S(2)}) collective-permute-start(bf16[1,384,256]{2,1,0:T(8,128)(2,1)} %get-tuple-element.78), channel_id=1, source_target_pairs={{0,8},{2,10},{4,12},{6,14},{8,0},{10,2},{12,4},{14,6},{16,24},{18,... | collective-permute-start | bytes 589832 | tf_op jit(solution)/shard_map/ppermute | solution.py:28
  65.2 30.7 %copy-start.13 = (bf16[4,384,256]{2,1,0:T(8,128)(2,1)}, bf16[4,384,256]{2,1,0:T(8,128)(2,1)S(1)}, u32[]{:S(2)}) copy-start(bf16[4,384,256]{2,1,0:T(8,128)(2,1)S(1)} %constant_dynamic-update-slice_fusion.refs_4_) | copy-start | bytes 2359300
  65.2 34.2 %collective-permute-start.17 = (bf16[4,384,256]{2,1,0:T(8,128)(2,1)S(1)}, bf16[4,384,256]{2,1,0:T(8,128)(2,1)}, u32[]{:S(2)}, u32[]{:S(2)}) collective-permute-start(bf16[4,384,256]{2,1,0:T(8,128)(2,1)S(1)} %constant_dynamic-update-slice_fusion.refs_4_), channel_id=1, source_target_pairs={{0,4},{2,6},{4,0},{6,2},{8,12},{10,14},{12,8},{14,10},{16,20},{18,... | collective-permute-start | bytes 2359304 | tf_op jit(solution)/shard_map/ppermute | solution.py:28
  65.8 19.1 %collective-permute-start.8 = (bf16[1,384,256]{2,1,0:T(8,128)(2,1)}, bf16[1,384,256]{2,1,0:T(8,128)(2,1)S(1)}, u32[]{:S(2)}, u32[]{:S(2)}) collective-permute-start(bf16[1,384,256]{2,1,0:T(8,128)(2,1)} %get-tuple-element.79), channel_id=1, source_target_pairs={{0,16},{2,18},{4,20},{6,22},{8,24},{10,26},{12,28},{14,30},{16,0},... | collective-permute-start | bytes 589832 | tf_op jit(solution)/shard_map/ppermute | solution.py:28
  71.8 13.1 %collective-permute-start.9 = (bf16[1,384,256]{2,1,0:T(8,128)(2,1)}, bf16[1,384,256]{2,1,0:T(8,128)(2,1)S(1)}, u32[]{:S(2)}, u32[]{:S(2)}) collective-permute-start(bf16[1,384,256]{2,1,0:T(8,128)(2,1)} %get-tuple-element.80), channel_id=1, source_target_pairs={{0,24},{2,26},{4,28},{6,30},{8,16},{10,18},{12,20},{14,22},{16,8},... | collective-permute-start | bytes 589832 | tf_op jit(solution)/shard_map/ppermute | solution.py:28
  73.2 33.7 %collective-permute-start.14 = (bf16[4,384,256]{2,1,0:T(8,128)(2,1)}, bf16[4,384,256]{2,1,0:T(8,128)(2,1)}, u32[]{:S(2)}, u32[]{:S(2)}) collective-permute-start(bf16[4,384,256]{2,1,0:T(8,128)(2,1)} %collective-permute-done.3.refs_6_), channel_id=1, source_target_pairs={{0,2},{2,0},{4,6},{6,4},{8,10},{10,8},{12,14},{14,12},{16,18},{18,... | collective-permute-start | bytes 2359304 | tf_op jit(solution)/shard_map/ppermute | solution.py:28
  85.0 39.3 %copy-start.12 = (bf16[4,384,256]{2,1,0:T(8,128)(2,1)}, bf16[4,384,256]{2,1,0:T(8,128)(2,1)S(1)}, u32[]{:S(2)}) copy-start(bf16[4,384,256]{2,1,0:T(8,128)(2,1)S(1)} %constant_dynamic-update-slice_fusion.4.refs_4_) | copy-start | bytes 2359300
  85.0 39.3 %collective-permute-start.15 = (bf16[4,384,256]{2,1,0:T(8,128)(2,1)S(1)}, bf16[4,384,256]{2,1,0:T(8,128)(2,1)}, u32[]{:S(2)}, u32[]{:S(2)}) collective-permute-start(bf16[4,384,256]{2,1,0:T(8,128)(2,1)S(1)} %constant_dynamic-update-slice_fusion.4.refs_4_), channel_id=1, source_target_pairs={{0,4},{2,6},{4,0},{6,2},{8,12},{10,14},{12,8},{14,10},{16,20},{18,... | collective-permute-start | bytes 2359304 | tf_op jit(solution)/shard_map/ppermute | solution.py:28
  86.6 38.8 %collective-permute-start.16 = (bf16[4,384,256]{2,1,0:T(8,128)(2,1)S(1)}, bf16[4,384,256]{2,1,0:T(8,128)(2,1)}, u32[]{:S(2)}, u32[]{:S(2)}) collective-permute-start(bf16[4,384,256]{2,1,0:T(8,128)(2,1)S(1)} %constant_dynamic-update-slice_fusion.refs_4_), channel_id=1, source_target_pairs={{0,2},{2,0},{4,6},{6,4},{8,10},{10,8},{12,14},{14,12},{16,18},{18,... | collective-permute-start | bytes 2359304 | tf_op jit(solution)/shard_map/ppermute | solution.py:28
  87.3 12.4 %copy-start.14 = (s32[3]{0:T(128)S(1)}, s32[3]{0:T(128)}, u32[]{:S(2)}) copy-start(s32[3]{0:T(128)} %pad_add_fusion.place_ref) | copy-start | bytes 40
  95.9 9.3 %collective-permute-start.10 = (bf16[2,384,128]{2,1,0:T(8,128)(2,1)}, bf16[2,384,128]{2,1,0:T(8,128)(2,1)S(1)}, u32[]{:S(2)}, u32[]{:S(2)}) collective-permute-start(bf16[2,384,128]{2,1,0:T(8,128)(2,1)} %get-tuple-element.81), channel_id=1, source_target_pairs={{0,8},{2,10},{4,12},{6,14},{8,0},{10,2},{12,4},{14,6},{16,24},{18,... | collective-permute-start | bytes 589832 | tf_op jit(solution)/shard_map/ppermute | solution.py:28
  99.5 25.9 %collective-permute-start.18 = (bf16[4,384,256]{2,1,0:T(8,128)(2,1)}, bf16[4,384,256]{2,1,0:T(8,128)(2,1)}, u32[]{:S(2)}, u32[]{:S(2)}) collective-permute-start(bf16[4,384,256]{2,1,0:T(8,128)(2,1)} %collective-permute-done.17.refs_6_), channel_id=1, source_target_pairs={{0,2},{2,0},{4,6},{6,4},{8,10},{10,8},{12,14},{14,12},{16,18},{18,... | collective-permute-start | bytes 2359304 | tf_op jit(solution)/shard_map/ppermute | solution.py:28
  105.3 15.5 %copy-start.15 = (bf16[2,384,128]{2,1,0:T(8,128)(2,1)}, bf16[2,384,128]{2,1,0:T(8,128)(2,1)S(1)}, u32[]{:S(2)}) copy-start(bf16[2,384,128]{2,1,0:T(8,128)(2,1)S(1)} %collective-permute-done.10.refs_1_) | copy-start | bytes 589828
  105.3 19.0 %collective-permute-start.11 = (bf16[2,384,128]{2,1,0:T(8,128)(2,1)}, bf16[2,384,128]{2,1,0:T(8,128)(2,1)S(1)}, u32[]{:S(2)}, u32[]{:S(2)}) collective-permute-start(bf16[2,384,128]{2,1,0:T(8,128)(2,1)} %get-tuple-element.82), channel_id=1, source_target_pairs={{0,16},{2,18},{4,20},{6,22},{8,24},{10,26},{12,28},{14,30},{16,0},... | collective-permute-start | bytes 589832 | tf_op jit(solution)/shard_map/ppermute | solution.py:28
  106.9 17.9 %collective-permute-start.12 = (bf16[2,384,128]{2,1,0:T(8,128)(2,1)}, bf16[2,384,128]{2,1,0:T(8,128)(2,1)S(1)}, u32[]{:S(2)}, u32[]{:S(2)}) collective-permute-start(bf16[2,384,128]{2,1,0:T(8,128)(2,1)} %get-tuple-element.83), channel_id=1, source_target_pairs={{0,24},{2,26},{4,28},{6,30},{8,16},{10,18},{12,20},{14,22},{16,8},... | collective-permute-start | bytes 589832 | tf_op jit(solution)/shard_map/ppermute | solution.py:28
  120.8 15.9 %all-to-all-start = ((bf16[4,384,128]{2,1,0:T(8,128)(2,1)}), bf16[4,384,128]{2,1,0:T(8,128)(2,1)S(1)}, u32[]{:S(2)}, u32[]{:S(2)}) async-start(bf16[4,384,128]{2,1,0:T(8,128)(2,1)} %attend.3), calls=%async_computation | async-start | bytes 786432 | tf_op jit(solution)/shard_map/all_to_all | solution.py:417
  124.2 1.2 copy-start.16
  124.3 18.9 %collective-permute-start.19 = (bf16[4,384,256]{2,1,0:T(8,128)(2,1)S(1)}, bf16[4,384,256]{2,1,0:T(8,128)(2,1)}, u32[]{:S(2)}, u32[]{:S(2)}) collective-permute-start(bf16[4,384,256]{2,1,0:T(8,128)(2,1)S(1)} %constant_dynamic-update-slice_fusion.4.refs_4_), channel_id=1, source_target_pairs={{0,2},{2,0},{4,6},{6,4},{8,10},{10,8},{12,14},{14,12},{16,18},{18,... | collective-permute-start | bytes 2359304 | tf_op jit(solution)/shard_map/ppermute | solution.py:28
  124.3 18.9 %collective-permute-start.20 = (bf16[4,384,256]{2,1,0:T(8,128)(2,1)}, bf16[4,384,256]{2,1,0:T(8,128)(2,1)}, u32[]{:S(2)}, u32[]{:S(2)}) collective-permute-start(bf16[4,384,256]{2,1,0:T(8,128)(2,1)} %collective-permute-done.15.refs_6_), channel_id=1, source_target_pairs={{0,2},{2,0},{4,6},{6,4},{8,10},{10,8},{12,14},{14,12},{16,18},{18,... | collective-permute-start | bytes 2359304 | tf_op jit(solution)/shard_map/ppermute | solution.py:28
  136.7 17.8 %copy-start.1 = (bf16[4,384,128]{2,1,0:T(8,128)(2,1)}, bf16[4,384,128]{2,1,0:T(8,128)(2,1)S(1)}, u32[]{:S(2)}) copy-start(bf16[4,384,128]{2,1,0:T(8,128)(2,1)S(1)} %all-to-all-done.refs_0_) | copy-start | bytes 1179652
  136.7 28.9 %all-to-all-start.1 = ((bf16[4,384,128]{2,1,0:T(8,128)(2,1)}), bf16[4,384,128]{2,1,0:T(8,128)(2,1)S(1)}, u32[]{:S(2)}, u32[]{:S(2)}) async-start(bf16[4,384,128]{2,1,0:T(8,128)(2,1)} %attend.4), calls=%async_computation.1 | async-start | bytes 786432 | tf_op jit(solution)/shard_map/all_to_all | solution.py:417
  154.5 5.6 %collective-permute-start.21 = (bf16[1,384,128]{2,1,0:T(8,128)(2,1)}, bf16[1,384,128]{2,1,0:T(8,128)(2,1)S(1)}, u32[]{:S(2)}, u32[]{:S(2)}) collective-permute-start(bf16[1,384,128]{2,1,0:T(8,128)(2,1)} %get-tuple-element.89), channel_id=1, source_target_pairs={{0,8},{2,10},{4,12},{6,14},{8,0},{10,2},{12,4},{14,6},{16,24},{18,... | collective-permute-start | bytes 294920 | tf_op jit(solution)/shard_map/ppermute | solution.py:28
  156.7 6.8 %collective-permute-start.22 = (bf16[1,384,128]{2,1,0:T(8,128)(2,1)}, bf16[1,384,128]{2,1,0:T(8,128)(2,1)S(1)}, u32[]{:S(2)}, u32[]{:S(2)}) collective-permute-start(bf16[1,384,128]{2,1,0:T(8,128)(2,1)} %get-tuple-element.90), channel_id=1, source_target_pairs={{0,16},{2,18},{4,20},{6,22},{8,24},{10,26},{12,28},{14,30},{16,0},... | collective-permute-start | bytes 294920 | tf_op jit(solution)/shard_map/ppermute | solution.py:28
  158.9 6.7 %collective-permute-start.23 = (bf16[1,384,128]{2,1,0:T(8,128)(2,1)}, bf16[1,384,128]{2,1,0:T(8,128)(2,1)S(1)}, u32[]{:S(2)}, u32[]{:S(2)}) collective-permute-start(bf16[1,384,128]{2,1,0:T(8,128)(2,1)} %get-tuple-element.91), channel_id=1, source_target_pairs={{0,24},{2,26},{4,28},{6,30},{8,16},{10,18},{12,20},{14,22},{16,8},... | collective-permute-start | bytes 294920 | tf_op jit(solution)/shard_map/ppermute | solution.py:28
  165.6 8.9 %copy-start = (bf16[4,384,128]{2,1,0:T(8,128)(2,1)}, bf16[4,384,128]{2,1,0:T(8,128)(2,1)S(1)}, u32[]{:S(2)}) copy-start(bf16[4,384,128]{2,1,0:T(8,128)(2,1)S(1)} %constant_dynamic-update-slice_fusion.8.refs_0_) | copy-start | bytes 1179652
  165.6 0.8 copy-start.2
  178.2 3.8 %copy-start.6 = (bf16[384,768]{1,0:T(8,128)(2,1)S(1)}, bf16[384,768]{1,0:T(8,128)(2,1)}, u32[]{:S(2)}) copy-start(bf16[384,768]{1,0:T(8,128)(2,1)} %finish.5) | copy-start | bytes 1769476
  182.0 13.6 %collective-permute-start.24 = (bf16[384,768]{1,0:T(8,128)(2,1)S(1)}, bf16[384,768]{1,0:T(8,128)(2,1)S(1)}, u32[]{:S(2)}, u32[]{:S(2)}) collective-permute-start(bf16[384,768]{1,0:T(8,128)(2,1)S(1)} %copy-done.6), channel_id=1, source_target_pairs={{0,1},{1,0},{2,3},{3,2},{4,5},{5,4},{6,7},{7,6},{8,9},{9,8},{10,11... | collective-permute-start | bytes 1769480 | tf_op jit(solution)/shard_map/ppermute | solution.py:28
  183.5 18.4 %collective-permute-start.25 = (bf16[384,768]{1,0:T(8,128)(2,1)}, bf16[384,768]{1,0:T(8,128)(2,1)S(1)}, u32[]{:S(2)}, u32[]{:S(2)}) collective-permute-start(bf16[384,768]{1,0:T(8,128)(2,1)} %finish.6), channel_id=1, source_target_pairs={{0,1},{1,0},{2,3},{3,2},{4,5},{5,4},{6,7},{7,6},{8,9},{9,8},{10,11... | collective-permute-start | bytes 1769480 | tf_op jit(solution)/shard_map/ppermute | solution.py:28
  195.6 6.3 %copy-start.4 = (bf16[384,768]{1,0:T(8,128)(2,1)}, bf16[384,768]{1,0:T(8,128)(2,1)S(1)}, u32[]{:S(2)}) copy-start(bf16[384,768]{1,0:T(8,128)(2,1)S(1)} %collective-permute-done.24.refs_0_) | copy-start | bytes 1769476
  201.9 0.8 copy-start.5
  (1 other events, 0.7 us)

commit v8 on v6

--- a/solution.py
+++ b/solution.py
@@ -289,63 +289,48 @@
     )(place, *queries, *keyvals)
 
 
-def finish_body(place_ref, *refs, chunks, has_sum, ordered):
-    attended_refs, weight_ref = refs[:chunks], refs[chunks]
-    out_ref, wide_ref = refs[-2:]
+def finish_body(place_ref, *refs, ordered):
+    chunks = len(ordered)
+    attended_refs, weight_ref, out_ref, wide_ref = refs[:chunks], *refs[chunks:]
 
     @pl.when(pl.program_id(0) == 0)
     def _():
         for i, ref in enumerate(attended_refs):
             groups, _, size = ref.shape
             for g in range(groups):
-                head = i * groups + (g if ordered else lax.bitwise_xor(place_ref[0], g))
-                start = head * size if ordered else pl.multiple_of(head * size, size)
+                if ordered[i]:
+                    start = (i * groups + g) * size
+                else:
+                    head = i * groups + lax.bitwise_xor(place_ref[0], g)
+                    start = pl.multiple_of(head * size, size)
                 wide_ref[:, pl.ds(start, size)] = ref[g]
 
     total = jnp.dot(wide_ref[...], weight_ref[...], preferred_element_type=f32)
-    if has_sum:
-        total += refs[chunks + 1][...]
     out_ref[...] = total.astype(out_ref.dtype)
 
 
-def finish(place, attended, w_out, first_chunk, ordered, total=None, mask=None, kind=f32):
+def finish(place, attended, ordered, w_out, mask, kind):
     groups, rows, size = attended[0].shape
-    head_shards = lax.axis_size("head")
-    out_width = w_out.shape[1] // head_shards
-    chunks = len(attended)
-    depth = chunks * groups * size
-    block = first_chunk // chunks
-    parts = 2 if out_width % 256 == 0 else 1
+    depth = w_out.shape[0]
+    out_width = w_out.shape[1] // lax.axis_size("head")
+    parts = 4 if out_width % 512 == 0 else 1
     tile = out_width // parts
-    count = parts * (head_shards if mask is None else 1)
-
-    def column(i, place):
-        return i if mask is None else lax.bitwise_xor(place[2], mask) * parts + i
-
-    specs = [pl.BlockSpec((groups, rows, size), lambda i, place: (0, 0, 0))] * chunks
-    specs.append(pl.BlockSpec((depth, tile), lambda i, place: (block, column(i, place))))
-    operands = [*attended, w_out]
-    if total is not None:
-        specs.append(pl.BlockSpec((rows, tile), lambda i, place: (0, column(i, place))))
-        operands.append(total)
+    column = lambda i, place: (0, lax.bitwise_xor(place[2], mask) * parts + i)
     return pl.pallas_call(
-        functools.partial(
-            finish_body, chunks=chunks, has_sum=total is not None, ordered=ordered
-        ),
+        functools.partial(finish_body, ordered=ordered),
         grid_spec=pltpu.PrefetchScalarGridSpec(
             num_scalar_prefetch=1,
-            grid=(count,),
-            in_specs=specs,
+            grid=(parts,),
+            in_specs=[pl.BlockSpec((groups, rows, size), lambda i, place: (0, 0, 0))] * len(attended)
+            + [pl.BlockSpec((depth, tile), column)],
             out_specs=pl.BlockSpec((rows, tile), lambda i, place: (0, i)),
             scratch_shapes=[pltpu.VMEM((rows, depth), bf16)],
         ),
-        out_shape=jax.ShapeDtypeStruct((rows, tile * count), kind),
+        out_shape=jax.ShapeDtypeStruct((rows, out_width), kind),
         compiler_params=params,
-        cost_estimate=cost(
-            2 * rows * depth * tile * count, 2 * depth * tile * count + 8 * rows * tile * count
-        ),
+        cost_estimate=cost(2 * rows * depth * out_width, 2 * depth * out_width + 4 * rows * out_width),
         name="finish",
-    )(place, *operands)
+    )(place, *attended, w_out)
 
 
 def close_body(back_ref, mine_ref, *refs):
@@ -442,16 +427,19 @@
         (made,), _ = project(place, (ready, normed, chosen), weights, gains, sets, groups)
         gate = made[0]
         stacks += [stack(blocks) for blocks in arrived[2:]]
-        asked = send(made, stacks[-1])
+        keyvals = everywhere(stacks[0], gate)
+        asked = send(made, stacks[-1], *keyvals)
         hops = [flip(stacks[-1], "seq", ring // 2)] if ring > 1 else []
     else:
-        gate, stacks = None, [stack(arrived[0])]
+        stacks = [stack(arrived[0])]
+        keyvals = everywhere(stacks[0], None)
 
     attended, returned = [], []
     query, low_lane = arrived[0], 2 * size
     for chunk in range(chunks):
         final = chunk == chunks - 1
-        keyvals = everywhere(stacks[chunk], gate)
+        if chunk:
+            keyvals = everywhere(stacks[chunk], None)
         before = [stacks[-1]] + attended[-1:] + (hops if chunk else []) + (returned[:1] if final else [])
         ready = later(place, *query[1:], *before)
         row = max(chunk - 1, 0)
@@ -459,13 +447,13 @@
         attended.append(found[0])
         returned.append(jnp.concatenate(swap(found)) if final else send_back(found[0]))
         if not final:
-            query, low_lane, gate = asked, 0, None
-    total = finish(place, returned[:-1], w_out, 0, True) if chunks > 1 else None
-    final = functools.partial(finish, place, returned[-1:], w_out, chunks - 1, False)
-    sent = [final(total=total, mask=mask, kind=bf16) for mask in range(1, head_shards)]
+            query, low_lane = asked, 0
+    ordered = (True,) * (chunks - 1) + (False,)
+    final = functools.partial(finish, place, returned, ordered, w_out)
+    sent = [final(mask, bf16) for mask in range(1, head_shards)]
     others = [flip(part, "head", mask) for mask, part in enumerate(sent, 1)]
-    mine = final(total=chain(total, *sent) if chunks > 1 else None, mask=0)
-    return close(back, mine, others)
+    returned[0] = chain(returned[0], *sent)
+    return close(back, final(0, f32), others)
 
 
 def solution(mesh):

time: 200 us -> 203 us (1.015)
  waiting for transfers between devices: 59.3 us -> 75.1 us
  starting transfers between devices: 48 us -> 39.8 us
  Pallas kernels: 83.2 us -> 80.7 us
    ppermute x25, waiting for transfers between devices: 58.8 us -> 72.9 us  [flip(): return lax.ppermute(values, axis, [(i, i ^ mask) for i in range(size)])]
    ppermute x25, starting transfers between devices: 40.3 us -> 32.9 us  [flip(): return lax.ppermute(values, axis, [(i, i ^ mask) for i in range(size)])]
    pallas_call x3 -> x2, Pallas kernels: 16.7 us -> 14.4 us  [finish(): pl.pallas_call(functools.partial(finish_body, ordered=ordered), grid_spec...]
    unnamed x57 -> x59, local copies, waits for them, and re-layouts: 4.74 us -> 4.55 us
where the time goes in v8:
time: 203 us
  Pallas kernels  80.7 us (40%)
  waiting for transfers between devices  75.1 us (37%)
  starting transfers between devices  39.8 us (20%)
  local copies, waits for them, and re-layouts  4.65 us (2%)
  other arithmetic  2.29 us (1%)
    ppermute x25, waiting for transfers between devices, flip(): return lax.ppermute(values, axis, [(i, i ^ mask) for i in range(size)])  72.9 us
    pallas_call x3, Pallas kernels, project(): pl.pallas_call(functools.partial(project_body, steps=steps, groups=groups...  35.4 us
    ppermute x25, starting transfers between devices, flip(): return lax.ppermute(values, axis, [(i, i ^ mask) for i in range(size)])  32.9 us
    pallas_call x3, Pallas kernels, attend(): pl.pallas_call(functools.partial(attend_body, groups=groups, ordered=orde...  26.3 us
    pallas_call x2, Pallas kernels, finish(): pl.pallas_call(functools.partial(finish_body, ordered=ordered), grid_spec...  14.4 us
    all_to_all x2, starting transfers between devices, send_back(): lax.all_to_all(blocks, 'seq', split_axis=0, concat_axis=0, axis_index_gro...  6.92 us
    pallas_call x1, Pallas kernels, close(): pl.pallas_call(close_body, grid=(parts,), in_specs=[pl.BlockSpec((rows, r...  4.56 us
    unnamed x59, local copies, waits for them, and re-layouts  4.55 us
  transfers between devices with their start and end apart: 27, of which 9 were waited for; matrix products, arithmetic and copies ran while one was open for 1% of the time, Pallas kernels for 27%

profile of v8, /device:TPU:0, one launch (start us, length us, event | category | flops | bytes accessed | tf_op | source)
XLA Modules:
  0.0 203.5 jit_solution(14055977963060708198)
XLA Ops:
  0.0 0.6 pad_add_fusion.place_ref
  0.6 13.4 %project.3 = (bf16[1,384,384]{2,1,0:T(8,128)(2,1)}, bf16[1,384,384]{2,1,0:T(8,128)(2,1)}, bf16[1,384,384]{2,1,0:T(8,128)(2,1)}, bf16[1,384,384]{2,1,0:T(8,128)(2...) custom-call(s32[3]{0:T(128)} %pad_add_fusion.place_ref, ...), custom_call_target="tpu_custom_call" | custom-call | flops 3623878656 | bytes 11796480 | tf_op jit(solution)/shard_map/project/pallas_call | solution.py:143
  14.0 3.1 %collective-permute-start = (bf16[1,384,384]{2,1,0:T(8,128)(2,1)}, bf16[1,384,384]{2,1,0:T(8,128)(2,1)S(1)}, u32[]{:S(2)}, u32[]{:S(2)}) collective-permute-start(bf16[1,384,384]{2,1,0:T(8,128)(2,1)} %get-tuple-element.50), channel_id=1, source_target_pairs={{0,8},{2,10},{4,12},{6,14},{8,0},{10,2},{12,4},{14,6},{16,24},{18,... | collective-permute-start | bytes 884744 | tf_op jit(solution)/shard_map/ppermute | solution.py:28
  17.1 2.6 %collective-permute-start.1 = (bf16[1,384,384]{2,1,0:T(8,128)(2,1)}, bf16[1,384,384]{2,1,0:T(8,128)(2,1)S(1)}, u32[]{:S(2)}, u32[]{:S(2)}) collective-permute-start(bf16[1,384,384]{2,1,0:T(8,128)(2,1)} %get-tuple-element.51), channel_id=1, source_target_pairs={{0,16},{2,18},{4,20},{6,22},{8,24},{10,26},{12,28},{14,30},{16,0},... | collective-permute-start | bytes 884744 | tf_op jit(solution)/shard_map/ppermute | solution.py:28
  19.7 10.2 %collective-permute-done.refs_1_ = bf16[1,384,384]{2,1,0:T(8,128)(2,1)S(1)} collective-permute-done((bf16[1,384,384]{2,1,0:T(8,128)(2,1)}, bf16[1,384,384]{2,1,0:T(8,128)(2,1)S(1)}, u32[]{:S(2)}, u32[]{:S(2)}) %collective-permute-start) | collective-permute-done | bytes 294944 | tf_op jit(solution)/shard_map/ppermute | solution.py:28
  29.8 13.2 %project.4 = (bf16[1,384,256]{2,1,0:T(8,128)(2,1)}, bf16[1,384,256]{2,1,0:T(8,128)(2,1)}, bf16[1,384,256]{2,1,0:T(8,128)(2,1)}, bf16[1,384,256]{2,1,0:T(8,128)(2...) custom-call(s32[3]{0:T(128)} %pad_add_fusion.place_ref, ...), custom_call_target="tpu_custom_call" | custom-call | flops 4831838208 | bytes 14942208 | tf_op jit(solution)/shard_map/project/pallas_call | solution.py:143
  43.2 3.8 %collective-permute-start.8 = (bf16[1,384,256]{2,1,0:T(8,128)(2,1)}, bf16[1,384,256]{2,1,0:T(8,128)(2,1)S(1)}, u32[]{:S(2)}, u32[]{:S(2)}) collective-permute-start(bf16[1,384,256]{2,1,0:T(8,128)(2,1)} %get-tuple-element.73), channel_id=1, source_target_pairs={{0,16},{2,18},{4,20},{6,22},{8,24},{10,26},{12,28},{14,30},{16,0},... | collective-permute-start | bytes 589832 | tf_op jit(solution)/shard_map/ppermute | solution.py:28
  46.9 0.6 collective-permute-start.9
  47.7 0.1 pad_maximum_fusion.refs_4_
  47.8 1.8 collective-permute-start.7
  49.6 3.0 %collective-permute-done.3 = bf16[1,384,256]{2,1,0:T(8,128)(2,1)S(1)} collective-permute-done((bf16[1,384,256]{2,1,0:T(8,128)(2,1)}, bf16[1,384,256]{2,1,0:T(8,128)(2,1)S(1)}, u32[]{:S(2)}, u32[]{:S(2)}) %collective-permute-start.3) | collective-permute-done | bytes 196640 | tf_op jit(solution)/shard_map/ppermute | solution.py:28
  52.5 3.1 %collective-permute-start.5 = (bf16[1,384,256]{2,1,0:T(8,128)(2,1)S(1)}, bf16[1,384,256]{2,1,0:T(8,128)(2,1)S(1)}, u32[]{:S(2)}, u32[]{:S(2)}) collective-permute-start(bf16[1,384,256]{2,1,0:T(8,128)(2,1)S(1)} %copy-done.21), channel_id=1, source_target_pairs={{0,16},{2,18},{4,20},{6,22},{8,24},{10,26},{12,28},{14,30},{16,0},... | collective-permute-start | bytes 589832 | tf_op jit(solution)/shard_map/ppermute | solution.py:28
  55.6 5.8 %collective-permute-done.8 = bf16[1,384,256]{2,1,0:T(8,128)(2,1)S(1)} collective-permute-done((bf16[1,384,256]{2,1,0:T(8,128)(2,1)}, bf16[1,384,256]{2,1,0:T(8,128)(2,1)S(1)}, u32[]{:S(2)}, u32[]{:S(2)}) %collective-permute-start.8) | collective-permute-done | bytes 196640 | tf_op jit(solution)/shard_map/ppermute | solution.py:28
  61.4 2.5 %collective-permute-start.6 = (bf16[1,384,256]{2,1,0:T(8,128)(2,1)S(1)}, bf16[1,384,256]{2,1,0:T(8,128)(2,1)S(1)}, u32[]{:S(2)}, u32[]{:S(2)}) collective-permute-start(bf16[1,384,256]{2,1,0:T(8,128)(2,1)S(1)} %copy-done.19), channel_id=1, source_target_pairs={{0,24},{2,26},{4,28},{6,30},{8,16},{10,18},{12,20},{14,22},{16,8},... | collective-permute-start | bytes 589832 | tf_op jit(solution)/shard_map/ppermute | solution.py:28
  64.0 1.5 collective-permute-start.17
  65.6 12.6 %collective-permute-done.5 = bf16[1,384,256]{2,1,0:T(8,128)(2,1)S(1)} collective-permute-done((bf16[1,384,256]{2,1,0:T(8,128)(2,1)S(1)}, bf16[1,384,256]{2,1,0:T(8,128)(2,1)S(1)}, u32[]{:S(2)}, u32[]{:S(2)}) %collective-permute-start.5) | collective-permute-done | bytes 196640 | tf_op jit(solution)/shard_map/ppermute | solution.py:28
  78.9 8.8 %project.5 = (bf16[2,384,128]{2,1,0:T(8,128)(2,1)}, bf16[2,384,128]{2,1,0:T(8,128)(2,1)}, bf16[2,384,128]{2,1,0:T(8,128)(2,1)}, bf16[2,384,128]{2,1,0:T(8,128)(2,1)}) custom-call(s32[3]{0:T(128)} %pad_add_fusion.place_ref, bf16[3,3072,1536]{2,1,0:T(8,128)(2,1)} %bitcast.7, f32[12,2,128]{2,1,0:T(2,128)} %bitcast.10, s32[1,1]{1,0:T(1,128)S(6)} %max.13.refs_2_, ...), custom_call_target="tpu_custom_call" | custom-call | flops 2415919104 | bytes 8650752 | tf_op jit(solution)/shard_map/project/pallas_call | solution.py:143
  87.7 0.5 collective-permute-start.10
  88.2 1.6 collective-permute-start.15
  89.8 0.5 collective-permute-start.18
  90.3 0.5 broadcast_maximum_fusion.2.place_ref
  90.9 0.2 collective-permute-done.10.refs_5_
  91.1 2.6 %collective-permute-start.13 = (bf16[2,384,128]{2,1,0:T(8,128)(2,1)}, bf16[2,384,128]{2,1,0:T(8,128)(2,1)S(1)}, u32[]{:S(2)}, u32[]{:S(2)}) collective-permute-start(bf16[2,384,128]{2,1,0:T(8,128)(2,1)} %get-tuple-element.83), channel_id=1, source_target_pairs={{0,16},{2,18},{4,20},{6,22},{8,24},{10,26},{12,28},{14,30},{16,0},... | collective-permute-start | bytes 589832 | tf_op jit(solution)/shard_map/ppermute | solution.py:28
  93.7 14.1 %collective-permute-done.15.refs_6_ = bf16[4,384,256]{2,1,0:T(8,128)(2,1)S(1)} collective-permute-done((bf16[4,384,256]{2,1,0:T(8,128)(2,1)S(1)}, bf16[4,384,256]{2,1,0:T(8,128)(2,1)S(1)}, u32[]{:S(2)}, u32[]{:S(2)}) %collective-permute-start.15) | collective-permute-done | bytes 786464 | tf_op jit(solution)/shard_map/ppermute | solution.py:28
  107.8 0.9 copy-done.15
  108.7 2.1 %collective-permute-start.14 = (bf16[2,384,128]{2,1,0:T(8,128)(2,1)}, bf16[2,384,128]{2,1,0:T(8,128)(2,1)S(1)}, u32[]{:S(2)}, u32[]{:S(2)}) collective-permute-start(bf16[2,384,128]{2,1,0:T(8,128)(2,1)} %get-tuple-element.84), channel_id=1, source_target_pairs={{0,24},{2,26},{4,28},{6,30},{8,16},{10,18},{12,20},{14,22},{16,8},... | collective-permute-start | bytes 589832 | tf_op jit(solution)/shard_map/ppermute | solution.py:28
  110.8 9.0 %attend.3 = bf16[4,384,128]{2,1,0:T(8,128)(2,1)} custom-call(s32[3]{0:T(128)} %broadcast_maximum_fusion.2.place_ref, bf16[1,384,384]{2,1,0:T(8,128)(2,1)} %get-tuple-element.69.refs_0_, bf16[1,384,384]{2,1,0:T(8,128)(2,1)} %copy-done.8, bf16[1,384,384]{2,1,0:T(8,128)(2,1)} %copy-done.9, bf16[1,384,384]{2,1,0:T(8,128)(2,1)} %copy-done.10, ...), custom_call_target="tpu_custom_call" | custom-call | flops 2415919104 | bytes 3145728 | tf_op jit(solution)/shard_map/attend/pallas_call | solution.py:258
  119.8 3.5 %all-to-all-start = ((bf16[4,384,128]{2,1,0:T(8,128)(2,1)}), bf16[4,384,128]{2,1,0:T(8,128)(2,1)S(1)}, u32[]{:S(2)}, u32[]{:S(2)}) async-start(bf16[4,384,128]{2,1,0:T(8,128)(2,1)} %attend.3), calls=%async_computation | async-start | bytes 786432 | tf_op jit(solution)/shard_map/all_to_all | solution.py:392
  123.3 0.3 collective-permute-start.19
  123.6 0.4 collective-permute-start.20
  123.9 0.6 broadcast_maximum_fusion.1.place_ref
  124.6 8.7 %attend.4 = bf16[4,384,128]{2,1,0:T(8,128)(2,1)} custom-call(s32[3]{0:T(128)} %broadcast_maximum_fusion.1.place_ref, bf16[2,384,128]{2,1,0:T(8,128)(2,1)} %get-tuple-element.86.refs_0_, bf16[2,384,128]{2,1,0:T(8,128)(2,1)} %copy-done.20, bf16[2,384,128]{2,1,0:T(8,128)(2,1)} %copy-done.22, bf16[2,384,128]{2,1,0:T(8,128)(2,1)} %copy-done.24, ...), custom_call_target="tpu_custom_call" | custom-call | flops 2415919104 | bytes 3145728 | tf_op jit(solution)/shard_map/attend/pallas_call | solution.py:258
  133.3 2.3 %all-to-all-done.refs_0_ = bf16[4,384,128]{2,1,0:T(8,128)(2,1)S(1)} async-done(((bf16[4,384,128]{2,1,0:T(8,128)(2,1)}), bf16[4,384,128]{2,1,0:T(8,128)(2,1)S(1)}, u32[]{:S(2)}, u32[]{:S(2)}) %all-to-all-start) | async-done | bytes 393248 | tf_op jit(solution)/shard_map/all_to_all | solution.py:392
  135.5 3.5 %all-to-all-start.1 = ((bf16[4,384,128]{2,1,0:T(8,128)(2,1)}), bf16[4,384,128]{2,1,0:T(8,128)(2,1)S(1)}, u32[]{:S(2)}, u32[]{:S(2)}) async-start(bf16[4,384,128]{2,1,0:T(8,128)(2,1)} %attend.4), calls=%async_computation.1 | async-start | bytes 786432 | tf_op jit(solution)/shard_map/all_to_all | solution.py:392
  139.0 0.5 broadcast_maximum_fusion.place_ref
  139.5 8.6 %attend.5 = (bf16[1,384,128]{2,1,0:T(8,128)(2,1)}, bf16[1,384,128]{2,1,0:T(8,128)(2,1)}, bf16[1,384,128]{2,1,0:T(8,128)(2,1)}, bf16[1,384,128]{2,1,0:T(8,128)(2,1)}) custom-call(s32[3]{0:T(128)} %broadcast_maximum_fusion.place_ref, bf16[2,384,128]{2,1,0:T(8,128)(2,1)} %get-tuple-element.86.refs_0_, bf16[2,384,128]{2,1,0:T(8,128)(2,1)} %copy-done.20, ...), custom_call_target="tpu_custom_call" | custom-call | flops 2415919104 | bytes 3145728 | tf_op jit(solution)/shard_map/attend/pallas_call | solution.py:258
  148.1 2.0 collective-permute-start.21
  150.1 2.4 %collective-permute-start.22 = (bf16[1,384,128]{2,1,0:T(8,128)(2,1)}, bf16[1,384,128]{2,1,0:T(8,128)(2,1)S(1)}, u32[]{:S(2)}, u32[]{:S(2)}) collective-permute-start(bf16[1,384,128]{2,1,0:T(8,128)(2,1)} %get-tuple-element.90), channel_id=1, source_target_pairs={{0,16},{2,18},{4,20},{6,22},{8,24},{10,26},{12,28},{14,30},{16,0},... | collective-permute-start | bytes 294920 | tf_op jit(solution)/shard_map/ppermute | solution.py:28
  152.6 0.9 constant_dynamic-update-slice_fusion.11
  153.5 7.5 %collective-permute-done.22 = bf16[1,384,128]{2,1,0:T(8,128)(2,1)S(1)} collective-permute-done((bf16[1,384,128]{2,1,0:T(8,128)(2,1)}, bf16[1,384,128]{2,1,0:T(8,128)(2,1)S(1)}, u32[]{:S(2)}, u32[]{:S(2)}) %collective-permute-start.22) | collective-permute-done | bytes 98336 | tf_op jit(solution)/shard_map/ppermute | solution.py:28
  161.2 0.7 copy-done.2
  161.9 0.7 copy-done.1
  162.6 7.0 %finish.2 = bf16[384,1536]{1,0:T(8,128)(2,1)} custom-call(s32[3]{0:T(128)} %pad_add_fusion.place_ref, bf16[4,384,128]{2,1,0:T(8,128)(2,1)} %copy-done, bf16[4,384,128]{2,1,0:T(8,128)(2,1)} %copy-done.1, bf16[4,384,128]{2,1,0:T(8,128)(2,1)} %copy-done.2, bf16[1536,3072]{1,0:T(8,128)(2,1)} %refs_3_.5), custom_call_target="tpu_custom_call" | custom-call | flops 1811939328 | bytes 7077888 | tf_op jit(solution)/shard_map/finish/pallas_call | solution.py:319
  169.7 1.5 collective-permute-start.24
  171.1 7.3 %finish.3.mine_ref = f32[384,1536]{1,0:T(8,128)} custom-call(s32[3]{0:T(128)} %pad_add_fusion.place_ref, bf16[4,384,128]{2,1,0:T(8,128)(2,1)} %copy-done, bf16[4,384,128]{2,1,0:T(8,128)(2,1)} %copy-done.1, bf16[4,384,128]{2,1,0:T(8,128)(2,1)} %copy-done.2, bf16[1536,3072]{1,0:T(8,128)(2,1)} %refs_3_.5), custom_call_target="tpu_custom_call" | custom-call | flops 1811939328 | bytes 7077888 | tf_op jit(solution)/shard_map/finish/pallas_call | solution.py:319
  178.5 19.4 %collective-permute-done.24.refs_0_ = bf16[384,1536]{1,0:T(8,128)(2,1)S(1)} collective-permute-done((bf16[384,1536]{1,0:T(8,128)(2,1)}, bf16[384,1536]{1,0:T(8,128)(2,1)S(1)}, u32[]{:S(2)}, u32[]{:S(2)}) %collective-permute-start.24) | collective-permute-done | bytes 1179680 | tf_op jit(solution)/shard_map/ppermute | solution.py:28
  197.9 1.0 copy-done.3
  198.9 4.6 %close.1 = bf16[384,1536]{1,0:T(8,128)(2,1)} custom-call(bf16[384,384]{1,0:T(8,128)(2,1)} %get-tuple-element.49.back_ref, f32[384,1536]{1,0:T(8,128)} %finish.3.mine_ref, bf16[384,1536]{1,0:T(8,128)(2,1)} %copy-done.3), custom_call_target="tpu_custom_call" | custom-call | flops 452984832 | bytes 5898240 | tf_op jit(solution)/shard_map/close/pallas_call | solution.py:349
  (86 shorter events, 0.6 us)
Async XLA Ops:
  14.0 15.9 %collective-permute-start = (bf16[1,384,384]{2,1,0:T(8,128)(2,1)}, bf16[1,384,384]{2,1,0:T(8,128)(2,1)S(1)}, u32[]{:S(2)}, u32[]{:S(2)}) collective-permute-start(bf16[1,384,384]{2,1,0:T(8,128)(2,1)} %get-tuple-element.50), channel_id=1, source_target_pairs={{0,8},{2,10},{4,12},{6,14},{8,0},{10,2},{12,4},{14,6},{16,24},{18,... | collective-permute-start | bytes 884744 | tf_op jit(solution)/shard_map/ppermute | solution.py:28
  17.1 30.5 %collective-permute-start.1 = (bf16[1,384,384]{2,1,0:T(8,128)(2,1)}, bf16[1,384,384]{2,1,0:T(8,128)(2,1)S(1)}, u32[]{:S(2)}, u32[]{:S(2)}) collective-permute-start(bf16[1,384,384]{2,1,0:T(8,128)(2,1)} %get-tuple-element.51), channel_id=1, source_target_pairs={{0,16},{2,18},{4,20},{6,22},{8,24},{10,26},{12,28},{14,30},{16,0},... | collective-permute-start | bytes 884744 | tf_op jit(solution)/shard_map/ppermute | solution.py:28
  19.7 27.9 %collective-permute-start.2 = (bf16[1,384,384]{2,1,0:T(8,128)(2,1)}, bf16[1,384,384]{2,1,0:T(8,128)(2,1)S(1)}, u32[]{:S(2)}, u32[]{:S(2)}) collective-permute-start(bf16[1,384,384]{2,1,0:T(8,128)(2,1)} %get-tuple-element.52), channel_id=1, source_target_pairs={{0,24},{2,26},{4,28},{6,30},{8,16},{10,18},{12,20},{14,22},{16,8},... | collective-permute-start | bytes 884744 | tf_op jit(solution)/shard_map/ppermute | solution.py:28
  29.8 17.8 %copy-start.8 = (bf16[1,384,384]{2,1,0:T(8,128)(2,1)}, bf16[1,384,384]{2,1,0:T(8,128)(2,1)S(1)}, u32[]{:S(2)}) copy-start(bf16[1,384,384]{2,1,0:T(8,128)(2,1)S(1)} %collective-permute-done.refs_1_) | copy-start | bytes 884740
  29.8 17.7 %copy-start.7 = (bf16[1,384,384]{2,1,0:T(8,128)(2,1)S(1)}, bf16[1,384,384]{2,1,0:T(8,128)(2,1)}, u32[]{:S(2)}) copy-start(bf16[1,384,384]{2,1,0:T(8,128)(2,1)} %get-tuple-element.69.refs_0_) | copy-start | bytes 884740
  43.1 6.5 %copy-start.6 = (bf16[1,384,256]{2,1,0:T(8,128)(2,1)S(1)}, bf16[1,384,256]{2,1,0:T(8,128)(2,1)}, u32[]{:S(2)}) copy-start(bf16[1,384,256]{2,1,0:T(8,128)(2,1)} %get-tuple-element.68) | copy-start | bytes 589828
  43.1 9.5 %copy-start.23 = (bf16[1,384,256]{2,1,0:T(8,128)(2,1)S(1)}, bf16[1,384,256]{2,1,0:T(8,128)(2,1)}, u32[]{:S(2)}) copy-start(bf16[1,384,256]{2,1,0:T(8,128)(2,1)} %get-tuple-element.63) | copy-start | bytes 589828
  43.1 9.5 %copy-start.21 = (bf16[1,384,256]{2,1,0:T(8,128)(2,1)S(1)}, bf16[1,384,256]{2,1,0:T(8,128)(2,1)}, u32[]{:S(2)}) copy-start(bf16[1,384,256]{2,1,0:T(8,128)(2,1)} %get-tuple-element.64) | copy-start | bytes 589828
  43.1 18.3 %copy-start.19 = (bf16[1,384,256]{2,1,0:T(8,128)(2,1)S(1)}, bf16[1,384,256]{2,1,0:T(8,128)(2,1)}, u32[]{:S(2)}) copy-start(bf16[1,384,256]{2,1,0:T(8,128)(2,1)} %get-tuple-element.65) | copy-start | bytes 589828
  43.1 9.4 %collective-permute-start.3 = (bf16[1,384,256]{2,1,0:T(8,128)(2,1)}, bf16[1,384,256]{2,1,0:T(8,128)(2,1)S(1)}, u32[]{:S(2)}, u32[]{:S(2)}) collective-permute-start(bf16[1,384,256]{2,1,0:T(8,128)(2,1)} %get-tuple-element.61), channel_id=1, source_target_pairs={{0,8},{2,10},{4,12},{6,14},{8,0},{10,2},{12,4},{14,6},{16,24},{18,... | collective-permute-start | bytes 589832 | tf_op jit(solution)/shard_map/ppermute | solution.py:28
  43.2 18.2 %collective-permute-start.8 = (bf16[1,384,256]{2,1,0:T(8,128)(2,1)}, bf16[1,384,256]{2,1,0:T(8,128)(2,1)S(1)}, u32[]{:S(2)}, u32[]{:S(2)}) collective-permute-start(bf16[1,384,256]{2,1,0:T(8,128)(2,1)} %get-tuple-element.73), channel_id=1, source_target_pairs={{0,16},{2,18},{4,20},{6,22},{8,24},{10,26},{12,28},{14,30},{16,0},... | collective-permute-start | bytes 589832 | tf_op jit(solution)/shard_map/ppermute | solution.py:28
  46.9 17.0 %collective-permute-start.9 = (bf16[1,384,256]{2,1,0:T(8,128)(2,1)}, bf16[1,384,256]{2,1,0:T(8,128)(2,1)S(1)}, u32[]{:S(2)}, u32[]{:S(2)}) collective-permute-start(bf16[1,384,256]{2,1,0:T(8,128)(2,1)} %get-tuple-element.74), channel_id=1, source_target_pairs={{0,24},{2,26},{4,28},{6,30},{8,16},{10,18},{12,20},{14,22},{16,8},... | collective-permute-start | bytes 589832 | tf_op jit(solution)/shard_map/ppermute | solution.py:28
  47.5 16.4 %copy-start.9 = (bf16[1,384,384]{2,1,0:T(8,128)(2,1)}, bf16[1,384,384]{2,1,0:T(8,128)(2,1)S(1)}, u32[]{:S(2)}) copy-start(bf16[1,384,384]{2,1,0:T(8,128)(2,1)S(1)} %collective-permute-done.1.refs_2_) | copy-start | bytes 884740
  47.6 16.4 %copy-start.10 = (bf16[1,384,384]{2,1,0:T(8,128)(2,1)}, bf16[1,384,384]{2,1,0:T(8,128)(2,1)S(1)}, u32[]{:S(2)}) copy-start(bf16[1,384,384]{2,1,0:T(8,128)(2,1)S(1)} %collective-permute-done.2.refs_3_) | copy-start | bytes 884740
  47.6 18.0 %copy-start.5 = (bf16[1,384,256]{2,1,0:T(8,128)(2,1)S(1)}, bf16[1,384,256]{2,1,0:T(8,128)(2,1)}, u32[]{:S(2)}) copy-start(bf16[1,384,256]{2,1,0:T(8,128)(2,1)} %get-tuple-element.62) | copy-start | bytes 589828
  47.8 39.9 %copy-start.4 = (bf16[4,384,256]{2,1,0:T(8,128)(2,1)}, bf16[4,384,256]{2,1,0:T(8,128)(2,1)S(1)}, u32[]{:S(2)}) copy-start(bf16[4,384,256]{2,1,0:T(8,128)(2,1)S(1)} %pad_maximum_fusion.refs_4_) | copy-start | bytes 2359300
  47.8 30.4 %collective-permute-start.7 = (bf16[4,384,256]{2,1,0:T(8,128)(2,1)S(1)}, bf16[4,384,256]{2,1,0:T(8,128)(2,1)S(1)}, u32[]{:S(2)}, u32[]{:S(2)}) collective-permute-start(bf16[4,384,256]{2,1,0:T(8,128)(2,1)S(1)} %pad_maximum_fusion.refs_4_), channel_id=1, source_target_pairs={{0,4},{2,6},{4,0},{6,2},{8,12},{10,14},{12,8},{14,10},{16,20},{18,... | collective-permute-start | bytes 2359304 | tf_op jit(solution)/shard_map/ppermute | solution.py:28
  52.5 13.0 %collective-permute-start.4 = (bf16[1,384,256]{2,1,0:T(8,128)(2,1)S(1)}, bf16[1,384,256]{2,1,0:T(8,128)(2,1)S(1)}, u32[]{:S(2)}, u32[]{:S(2)}) collective-permute-start(bf16[1,384,256]{2,1,0:T(8,128)(2,1)S(1)} %copy-done.23), channel_id=1, source_target_pairs={{0,8},{2,10},{4,12},{6,14},{8,0},{10,2},{12,4},{14,6},{16,24},{18,... | collective-permute-start | bytes 589832 | tf_op jit(solution)/shard_map/ppermute | solution.py:28
  52.5 25.7 %collective-permute-start.5 = (bf16[1,384,256]{2,1,0:T(8,128)(2,1)S(1)}, bf16[1,384,256]{2,1,0:T(8,128)(2,1)S(1)}, u32[]{:S(2)}, u32[]{:S(2)}) collective-permute-start(bf16[1,384,256]{2,1,0:T(8,128)(2,1)S(1)} %copy-done.21), channel_id=1, source_target_pairs={{0,16},{2,18},{4,20},{6,22},{8,24},{10,26},{12,28},{14,30},{16,0},... | collective-permute-start | bytes 589832 | tf_op jit(solution)/shard_map/ppermute | solution.py:28
  61.4 26.8 %collective-permute-start.6 = (bf16[1,384,256]{2,1,0:T(8,128)(2,1)S(1)}, bf16[1,384,256]{2,1,0:T(8,128)(2,1)S(1)}, u32[]{:S(2)}, u32[]{:S(2)}) collective-permute-start(bf16[1,384,256]{2,1,0:T(8,128)(2,1)S(1)} %copy-done.19), channel_id=1, source_target_pairs={{0,24},{2,26},{4,28},{6,30},{8,16},{10,18},{12,20},{14,22},{16,8},... | collective-permute-start | bytes 589832 | tf_op jit(solution)/shard_map/ppermute | solution.py:28
  64.0 25.8 %copy-start.11 = (bf16[4,384,256]{2,1,0:T(8,128)(2,1)}, bf16[4,384,256]{2,1,0:T(8,128)(2,1)S(1)}, u32[]{:S(2)}) copy-start(bf16[4,384,256]{2,1,0:T(8,128)(2,1)S(1)} %constant_dynamic-update-slice_fusion.4.refs_4_) | copy-start | bytes 2359300
  64.0 25.8 %collective-permute-start.17 = (bf16[4,384,256]{2,1,0:T(8,128)(2,1)S(1)}, bf16[4,384,256]{2,1,0:T(8,128)(2,1)}, u32[]{:S(2)}, u32[]{:S(2)}) collective-permute-start(bf16[4,384,256]{2,1,0:T(8,128)(2,1)S(1)} %constant_dynamic-update-slice_fusion.4.refs_4_), channel_id=1, source_target_pairs={{0,4},{2,6},{4,0},{6,2},{8,12},{10,14},{12,8},{14,10},{16,20},{18,... | collective-permute-start | bytes 2359304 | tf_op jit(solution)/shard_map/ppermute | solution.py:28
  78.3 9.4 %copy-start.14 = (bf16[4,384,256]{2,1,0:T(8,128)(2,1)}, bf16[4,384,256]{2,1,0:T(8,128)(2,1)S(1)}, u32[]{:S(2)}) copy-start(bf16[4,384,256]{2,1,0:T(8,128)(2,1)S(1)} %collective-permute-done.7.refs_6_) | copy-start | bytes 2359300
  78.8 11.5 %copy-start.13 = (s32[3]{0:T(128)S(1)}, s32[3]{0:T(128)}, u32[]{:S(2)}) copy-start(s32[3]{0:T(128)} %pad_add_fusion.place_ref) | copy-start | bytes 40
  87.7 3.2 %collective-permute-start.11 = (bf16[4,384,256]{2,1,0:T(8,128)(2,1)S(1)}, bf16[4,384,256]{2,1,0:T(8,128)(2,1)S(1)}, u32[]{:S(2)}, u32[]{:S(2)}) collective-permute-start(bf16[4,384,256]{2,1,0:T(8,128)(2,1)S(1)} %collective-permute-done.7.refs_6_), channel_id=1, source_target_pairs={{0,2},{2,0},{4,6},{6,4},{8,10},{10,8},{12,14},{14,12},{16,18},{18,... | collective-permute-start | bytes 2359304 | tf_op jit(solution)/shard_map/ppermute | solution.py:28
  87.7 3.4 %collective-permute-start.10 = (bf16[4,384,256]{2,1,0:T(8,128)(2,1)S(1)}, bf16[4,384,256]{2,1,0:T(8,128)(2,1)S(1)}, u32[]{:S(2)}, u32[]{:S(2)}) collective-permute-start(bf16[4,384,256]{2,1,0:T(8,128)(2,1)S(1)} %pad_maximum_fusion.refs_4_), channel_id=1, source_target_pairs={{0,2},{2,0},{4,6},{6,4},{8,10},{10,8},{12,14},{14,12},{16,18},{18,... | collective-permute-start | bytes 2359304 | tf_op jit(solution)/shard_map/ppermute | solution.py:28
  88.2 35.1 %copy-start.12 = (bf16[4,384,256]{2,1,0:T(8,128)(2,1)}, bf16[4,384,256]{2,1,0:T(8,128)(2,1)S(1)}, u32[]{:S(2)}) copy-start(bf16[4,384,256]{2,1,0:T(8,128)(2,1)S(1)} %constant_dynamic-update-slice_fusion.refs_4_) | copy-start | bytes 2359300
  88.2 19.6 %collective-permute-start.15 = (bf16[4,384,256]{2,1,0:T(8,128)(2,1)S(1)}, bf16[4,384,256]{2,1,0:T(8,128)(2,1)S(1)}, u32[]{:S(2)}, u32[]{:S(2)}) collective-permute-start(bf16[4,384,256]{2,1,0:T(8,128)(2,1)S(1)} %constant_dynamic-update-slice_fusion.refs_4_), channel_id=1, source_target_pairs={{0,4},{2,6},{4,0},{6,2},{8,12},{10,14},{12,8},{14,10},{16,20},{18,... | collective-permute-start | bytes 2359304 | tf_op jit(solution)/shard_map/ppermute | solution.py:28
  89.8 34.7 %collective-permute-start.16 = (bf16[4,384,256]{2,1,0:T(8,128)(2,1)S(1)}, bf16[4,384,256]{2,1,0:T(8,128)(2,1)}, u32[]{:S(2)}, u32[]{:S(2)}) collective-permute-start(bf16[4,384,256]{2,1,0:T(8,128)(2,1)S(1)} %constant_dynamic-update-slice_fusion.4.refs_4_), channel_id=1, source_target_pairs={{0,2},{2,0},{4,6},{6,4},{8,10},{10,8},{12,14},{14,12},{16,18},{18,... | collective-permute-start | bytes 2359304 | tf_op jit(solution)/shard_map/ppermute | solution.py:28
  89.8 34.7 %collective-permute-start.18 = (bf16[4,384,256]{2,1,0:T(8,128)(2,1)}, bf16[4,384,256]{2,1,0:T(8,128)(2,1)}, u32[]{:S(2)}, u32[]{:S(2)}) collective-permute-start(bf16[4,384,256]{2,1,0:T(8,128)(2,1)} %collective-permute-done.17.refs_6_), channel_id=1, source_target_pairs={{0,2},{2,0},{4,6},{6,4},{8,10},{10,8},{12,14},{14,12},{16,18},{18,... | collective-permute-start | bytes 2359304 | tf_op jit(solution)/shard_map/ppermute | solution.py:28
  90.9 16.9 %copy-start.17 = (bf16[4,384,256]{2,1,0:T(8,128)(2,1)}, bf16[4,384,256]{2,1,0:T(8,128)(2,1)S(1)}, u32[]{:S(2)}) copy-start(bf16[4,384,256]{2,1,0:T(8,128)(2,1)S(1)} %collective-permute-done.11.refs_7_) | copy-start | bytes 2359300
  91.1 16.7 %copy-start.18 = (bf16[4,384,256]{2,1,0:T(8,128)(2,1)}, bf16[4,384,256]{2,1,0:T(8,128)(2,1)S(1)}, u32[]{:S(2)}) copy-start(bf16[4,384,256]{2,1,0:T(8,128)(2,1)S(1)} %collective-permute-done.10.refs_5_) | copy-start | bytes 2359300
  91.1 32.2 %collective-permute-start.12 = (bf16[2,384,128]{2,1,0:T(8,128)(2,1)}, bf16[2,384,128]{2,1,0:T(8,128)(2,1)S(1)}, u32[]{:S(2)}, u32[]{:S(2)}) collective-permute-start(bf16[2,384,128]{2,1,0:T(8,128)(2,1)} %get-tuple-element.82), channel_id=1, source_target_pairs={{0,8},{2,10},{4,12},{6,14},{8,0},{10,2},{12,4},{14,6},{16,24},{18,... | collective-permute-start | bytes 589832 | tf_op jit(solution)/shard_map/ppermute | solution.py:28
  91.1 32.5 %collective-permute-start.13 = (bf16[2,384,128]{2,1,0:T(8,128)(2,1)}, bf16[2,384,128]{2,1,0:T(8,128)(2,1)S(1)}, u32[]{:S(2)}, u32[]{:S(2)}) collective-permute-start(bf16[2,384,128]{2,1,0:T(8,128)(2,1)} %get-tuple-element.83), channel_id=1, source_target_pairs={{0,16},{2,18},{4,20},{6,22},{8,24},{10,26},{12,28},{14,30},{16,0},... | collective-permute-start | bytes 589832 | tf_op jit(solution)/shard_map/ppermute | solution.py:28
  108.7 15.2 %collective-permute-start.14 = (bf16[2,384,128]{2,1,0:T(8,128)(2,1)}, bf16[2,384,128]{2,1,0:T(8,128)(2,1)S(1)}, u32[]{:S(2)}, u32[]{:S(2)}) collective-permute-start(bf16[2,384,128]{2,1,0:T(8,128)(2,1)} %get-tuple-element.84), channel_id=1, source_target_pairs={{0,24},{2,26},{4,28},{6,30},{8,16},{10,18},{12,20},{14,22},{16,8},... | collective-permute-start | bytes 589832 | tf_op jit(solution)/shard_map/ppermute | solution.py:28
  110.7 12.8 %copy-start.16 = (bf16[4,384,256]{2,1,0:T(8,128)(2,1)S(1)}, bf16[4,384,256]{2,1,0:T(8,128)(2,1)}, u32[]{:S(2)}) copy-start(bf16[4,384,256]{2,1,0:T(8,128)(2,1)} %copy-done.15) | copy-start | bytes 2359300
  119.8 15.7 %all-to-all-start = ((bf16[4,384,128]{2,1,0:T(8,128)(2,1)}), bf16[4,384,128]{2,1,0:T(8,128)(2,1)S(1)}, u32[]{:S(2)}, u32[]{:S(2)}) async-start(bf16[4,384,128]{2,1,0:T(8,128)(2,1)} %attend.3), calls=%async_computation | async-start | bytes 786432 | tf_op jit(solution)/shard_map/all_to_all | solution.py:392
  123.3 1.2 copy-start.20
  123.3 16.2 %collective-permute-start.19 = (bf16[4,384,256]{2,1,0:T(8,128)(2,1)S(1)}, bf16[4,384,256]{2,1,0:T(8,128)(2,1)}, u32[]{:S(2)}, u32[]{:S(2)}) collective-permute-start(bf16[4,384,256]{2,1,0:T(8,128)(2,1)S(1)} %constant_dynamic-update-slice_fusion.refs_4_), channel_id=1, source_target_pairs={{0,2},{2,0},{4,6},{6,4},{8,10},{10,8},{12,14},{14,12},{16,18},{18,... | collective-permute-start | bytes 2359304 | tf_op jit(solution)/shard_map/ppermute | solution.py:28
  123.5 1.0 copy-start.22
  123.6 16.0 %collective-permute-start.20 = (bf16[4,384,256]{2,1,0:T(8,128)(2,1)S(1)}, bf16[4,384,256]{2,1,0:T(8,128)(2,1)}, u32[]{:S(2)}, u32[]{:S(2)}) collective-permute-start(bf16[4,384,256]{2,1,0:T(8,128)(2,1)S(1)} %copy-done.16), channel_id=1, source_target_pairs={{0,2},{2,0},{4,6},{6,4},{8,10},{10,8},{12,14},{14,12},{16,18},{18,... | collective-permute-start | bytes 2359304 | tf_op jit(solution)/shard_map/ppermute | solution.py:28
  135.5 12.6 %copy-start = (bf16[4,384,128]{2,1,0:T(8,128)(2,1)}, bf16[4,384,128]{2,1,0:T(8,128)(2,1)S(1)}, u32[]{:S(2)}) copy-start(bf16[4,384,128]{2,1,0:T(8,128)(2,1)S(1)} %all-to-all-done.refs_0_) | copy-start | bytes 1179652
  135.5 25.6 %all-to-all-start.1 = ((bf16[4,384,128]{2,1,0:T(8,128)(2,1)}), bf16[4,384,128]{2,1,0:T(8,128)(2,1)S(1)}, u32[]{:S(2)}, u32[]{:S(2)}) async-start(bf16[4,384,128]{2,1,0:T(8,128)(2,1)} %attend.4), calls=%async_computation.1 | async-start | bytes 786432 | tf_op jit(solution)/shard_map/all_to_all | solution.py:392
  148.1 5.4 %collective-permute-start.21 = (bf16[1,384,128]{2,1,0:T(8,128)(2,1)}, bf16[1,384,128]{2,1,0:T(8,128)(2,1)S(1)}, u32[]{:S(2)}, u32[]{:S(2)}) collective-permute-start(bf16[1,384,128]{2,1,0:T(8,128)(2,1)} %get-tuple-element.89), channel_id=1, source_target_pairs={{0,8},{2,10},{4,12},{6,14},{8,0},{10,2},{12,4},{14,6},{16,24},{18,... | collective-permute-start | bytes 294920 | tf_op jit(solution)/shard_map/ppermute | solution.py:28
  150.1 10.9 %collective-permute-start.22 = (bf16[1,384,128]{2,1,0:T(8,128)(2,1)}, bf16[1,384,128]{2,1,0:T(8,128)(2,1)S(1)}, u32[]{:S(2)}, u32[]{:S(2)}) collective-permute-start(bf16[1,384,128]{2,1,0:T(8,128)(2,1)} %get-tuple-element.90), channel_id=1, source_target_pairs={{0,16},{2,18},{4,20},{6,22},{8,24},{10,26},{12,28},{14,30},{16,0},... | collective-permute-start | bytes 294920 | tf_op jit(solution)/shard_map/ppermute | solution.py:28
  152.5 8.6 %collective-permute-start.23 = (bf16[1,384,128]{2,1,0:T(8,128)(2,1)}, bf16[1,384,128]{2,1,0:T(8,128)(2,1)S(1)}, u32[]{:S(2)}, u32[]{:S(2)}) collective-permute-start(bf16[1,384,128]{2,1,0:T(8,128)(2,1)} %get-tuple-element.91), channel_id=1, source_target_pairs={{0,24},{2,26},{4,28},{6,30},{8,16},{10,18},{12,20},{14,22},{16,8},... | collective-permute-start | bytes 294920 | tf_op jit(solution)/shard_map/ppermute | solution.py:28
  169.7 28.2 %collective-permute-start.24 = (bf16[384,1536]{1,0:T(8,128)(2,1)}, bf16[384,1536]{1,0:T(8,128)(2,1)S(1)}, u32[]{:S(2)}, u32[]{:S(2)}) collective-permute-start(bf16[384,1536]{1,0:T(8,128)(2,1)} %finish.2), channel_id=1, source_target_pairs={{0,1},{1,0},{2,3},{3,2},{4,5},{5,4},{6,7},{7,6},{8,9},{9,8},{10,11... | collective-permute-start | bytes 3538952 | tf_op jit(solution)/shard_map/ppermute | solution.py:28
  197.9 1.0 copy-start.3
  (4 other events, 3.0 us)

commit v9 on v8

--- a/solution.py
+++ b/solution.py
@@ -165,13 +165,13 @@
     return blocks, found[len(sets) * groups :]
 
 
-def attend_body(place_ref, *refs, groups, ordered, low_lane, key_room, query_rows, key_cols):
+def attend_body(place_ref, *refs, groups, ordered, gathered, low_lane, key_room, query_rows, key_cols):
     outs = 1 if ordered else groups
-    query_refs, sources, out_refs = refs[:groups], refs[groups : -4 - outs], refs[-4 - outs : -4]
-    keys, values, queries, results = refs[-4:]
+    query_refs, sources, out_refs = refs[:groups], refs[groups : -5 - outs], refs[-5 - outs : -5]
+    keys, values, queries, results, counts = refs[-5:]
     rows, size = out_refs[0].shape[1:]
     plane = place_ref[0]
-    blocks = [(source, k) for source in sources for k in range(groups)]
+    blocks = [(source, k) for source in sources for k in range(source.shape[0])]
     piece = 128 if rows % 128 == 0 else rows
     align = lambda count: pl.multiple_of((count + 15) // 16 * 16, 16)
     line = lax.broadcasted_iota(jnp.int32, (piece, size), 0)
@@ -179,7 +179,8 @@
     found = []
     for source, block in blocks:
         live = (source[block, :, :size].astype(f32) < dead_limit).astype(f32)
-        found.append(jnp.max(jnp.sum(live, axis=0, keepdims=True)).astype(jnp.int32))
+        counts[len(found)] = jnp.max(jnp.sum(live, axis=0, keepdims=True)).astype(jnp.int32)
+        found.append(counts[len(found)])
 
     offset = jnp.int32(0)
     for (source, block), count in zip(blocks, found):
@@ -205,7 +206,8 @@
 
     lax.fori_loop(0, (key_room - offset) // 16, clear, 0)
 
-    mine = found[:groups]
+    own = place_ref[1] * groups if gathered else 0
+    mine = [counts[own + k] for k in range(groups)]
     starts = []
     start = jnp.int32(0)
     for k in range(groups):
@@ -260,6 +262,7 @@
             attend_body,
             groups=groups,
             ordered=ordered,
+            gathered=len(keyvals) == 1,
             low_lane=low_lane,
             key_room=key_room,
             query_rows=query_rows,
@@ -276,6 +279,7 @@
                 pltpu.VMEM((key_room + rows, 2 * size), bf16),
                 pltpu.VMEM((query_room, size), bf16),
                 pltpu.VMEM((query_room, size), bf16),
+                pltpu.SMEM((shards,), jnp.int32),
             ],
         ),
         out_shape=[jax.ShapeDtypeStruct((wide, rows, size), bf16)] * outs,
@@ -367,6 +371,7 @@
     me, side = lax.axis_index("seq"), lax.axis_index("head")
     place = jnp.stack([me // ring, me % ring, side]).astype(jnp.int32)
     planes = [[i + ring * g for g in range(groups)] for i in range(ring)]
+    rings = [[i + ring * g for i in range(ring)] for g in range(groups)]
 
     def swap(blocks):
         return [blocks[0]] + [flip(blocks[k], "seq", k * ring) for k in range(1, groups)]
@@ -374,15 +379,16 @@
     def stack(blocks):
         return jnp.concatenate([block[:, :, : 2 * size] for block in blocks])
 
-    def everywhere(stacked, gate):
-        found = {0: stacked}
-        mask = ring // 2
+    def gather(stacked):
+        return [lax.all_gather(stacked, "seq", axis=0, tiled=True, axis_index_groups=rings)]
+
+    def everywhere(stacked, hop):
+        if hop is None:
+            return gather(stacked)
+        found, mask = {0: stacked, ring // 2: hop}, ring // 4
         while mask:
             for known in list(found):
-                source = found[known]
-                if gate is not None and mask < ring // 2:
-                    source = chain(source, gate)
-                found[known | mask] = flip(source, "seq", mask)
+                found[known | mask] = flip(found[known], "seq", mask)
             mask //= 2
         return [found[mask] for mask in range(ring)]
 
@@ -411,7 +417,7 @@
     normed, chosen, back, count = rest
     arrived = [swap(blocks)]
 
-    rest, asked, hops = range(1, chunks), None, []
+    rest, asked, hop = range(1, chunks), None, None
     if chunks > 1:
         prepared = (count, chain(normed, first(arrived[0])), chosen)
         sets = [((1, 2), (chunk,)) for chunk in rest]
@@ -420,33 +426,36 @@
         arrived.append(send(made[0]))
         for blocks in made[1:]:
             arrived.append(send(blocks, first(arrived[-1])))
-        hop = flip(stacks[0], "seq", ring // 2) if ring > 1 else stacks[0]
         stacks.append(stack(arrived[1]))
-        ready = later(count, hop, stacks[1])
         sets = [((0,), tuple(rest))]
+        ready = later(count, stacks[1])
         (made,), _ = project(place, (ready, normed, chosen), weights, gains, sets, groups)
-        gate = made[0]
-        stacks += [stack(blocks) for blocks in arrived[2:]]
-        keyvals = everywhere(stacks[0], gate)
-        asked = send(made, stacks[-1], *keyvals)
-        hops = [flip(stacks[-1], "seq", ring // 2)] if ring > 1 else []
+        stacks += [stack(list(chain(tuple(blocks), made[0]))) for blocks in arrived[2:]]
+        asked = send(made, stacks[-1])
+        if ring > 1 and groups > 1:
+            hop = flip(stacks[-1], "seq", ring // 2)
     else:
         stacks = [stack(arrived[0])]
-        keyvals = everywhere(stacks[0], None)
 
     attended, returned = [], []
     query, low_lane = arrived[0], 2 * size
     for chunk in range(chunks):
         final = chunk == chunks - 1
+        keyvals = everywhere(stacks[chunk], hop if final else None)
+        before = [stacks[-1]] + attended[-1:]
         if chunk:
-            keyvals = everywhere(stacks[chunk], None)
-        before = [stacks[-1]] + attended[-1:] + (hops if chunk else []) + (returned[:1] if final else [])
+            before += [hop] if hop is not None else []
+        elif asked is not None:
+            before.append(first(asked))
+        before += returned[:1] if final else []
         ready = later(place, *query[1:], *before)
         row = max(chunk - 1, 0)
         found = attend(ready, query, row, low_lane, keyvals, shards, not final)
         attended.append(found[0])
-        returned.append(jnp.concatenate(swap(found)) if final else send_back(found[0]))
-        if not final:
+        if final:
+            returned.append(jnp.concatenate(swap(found)))
+        else:
+            returned.append(send_back(found[0]))
             query, low_lane = asked, 0
     ordered = (True,) * (chunks - 1) + (False,)
     final = functools.partial(finish, place, returned, ordered, w_out)

time: 203 us -> 214 us (1.054); the launches traced: 203 us -> 212 us
  between operations: 0.95 us -> 14.3 us
  waiting for transfers between devices: 75.1 us -> 66.5 us
    ppermute x25 -> x19, waiting for transfers between devices: 72.9 us -> 65.6 us  [flip(): return lax.ppermute(values, axis, [(i, i ^ mask) for i in range(size)])]
    all_to_all x2, starting transfers between devices: 6.92 us -> 11.5 us  [send_back(): lax.all_to_all(blocks, 'seq', split_axis=0, concat_axis=0, axis_index_gro...]
    ppermute x25 -> x19, starting transfers between devices: 32.9 us -> 29.7 us  [flip(): return lax.ppermute(values, axis, [(i, i ^ mask) for i in range(size)])]
    all_to_all x2, waiting for transfers between devices: 2.27 us -> 0.01 us  [send_back(): lax.all_to_all(blocks, 'seq', split_axis=0, concat_axis=0, axis_index_gro...]
    unnamed x59 -> x57, local copies, waits for them, and re-layouts: 4.55 us -> 5.35 us
  transfers between devices with their start and end apart: 27 -> 23, of which waited for: 9 -> 10; matrix products, arithmetic and copies ran while one was open for 1% -> 1% of each run, Pallas kernels for 27% -> 26%
where the time goes in v9:
time: 214 us; the launch traced here: 212 us
  Pallas kernels  80.9 us (38%)
  waiting for transfers between devices  66.5 us (31%)
  starting transfers between devices  41.4 us (19%)
  between operations  14.3 us (7%)
  local copies, waits for them, and re-layouts  5.45 us (3%)
  other arithmetic  3.34 us (2%)
    ppermute x19, waiting for transfers between devices, flip(): return lax.ppermute(values, axis, [(i, i ^ mask) for i in range(size)])  65.6 us
    pallas_call x3, Pallas kernels, project(): pl.pallas_call(functools.partial(project_body, steps=steps, groups=groups...  35.4 us
    ppermute x19, starting transfers between devices, flip(): return lax.ppermute(values, axis, [(i, i ^ mask) for i in range(size)])  29.7 us
    pallas_call x3, Pallas kernels, attend(): pl.pallas_call(functools.partial(attend_body, groups=groups, ordered=orde...  26.6 us
    pallas_call x2, Pallas kernels, finish(): pl.pallas_call(functools.partial(finish_body, ordered=ordered), grid_spec...  14.3 us
    all_to_all x2, starting transfers between devices, send_back(): lax.all_to_all(blocks, 'seq', split_axis=0, concat_axis=0, axis_index_gro...  11.5 us
    unnamed x57, local copies, waits for them, and re-layouts  5.35 us
    pallas_call x1, Pallas kernels, close(): pl.pallas_call(close_body, grid=(parts,), in_specs=[pl.BlockSpec((rows, r...  4.56 us
  transfers between devices with their start and end apart: 23, of which 10 were waited for; matrix products, arithmetic and copies ran while one was open for 1% of the time, Pallas kernels for 26%

profile of v9, /device:TPU:0, one launch (start us, length us, event | category | flops | bytes accessed | tf_op | source)
XLA Modules:
  0.0 212.0 jit_solution(3198521689383026283)
XLA Ops:
  6.5 0.6 pad_add_fusion.place_ref
  7.1 13.4 %project.3 = (bf16[1,384,384]{2,1,0:T(8,128)(2,1)}, bf16[1,384,384]{2,1,0:T(8,128)(2,1)}, bf16[1,384,384]{2,1,0:T(8,128)(2,1)}, bf16[1,384,384]{2,1,0:T(8,128)(2...) custom-call(s32[3]{0:T(128)} %pad_add_fusion.place_ref, ...), custom_call_target="tpu_custom_call" | custom-call | flops 3623878656 | bytes 11796480 | tf_op jit(solution)/shard_map/project/pallas_call | solution.py:143
  20.5 3.1 %collective-permute-start = (bf16[1,384,384]{2,1,0:T(8,128)(2,1)}, bf16[1,384,384]{2,1,0:T(8,128)(2,1)S(1)}, u32[]{:S(2)}, u32[]{:S(2)}) collective-permute-start(bf16[1,384,384]{2,1,0:T(8,128)(2,1)} %get-tuple-element.52), channel_id=1, source_target_pairs={{0,8},{2,10},{4,12},{6,14},{8,0},{10,2},{12,4},{14,6},{16,24},{18,... | collective-permute-start | bytes 884744 | tf_op jit(solution)/shard_map/ppermute | solution.py:28
  23.6 2.6 %collective-permute-start.1 = (bf16[1,384,384]{2,1,0:T(8,128)(2,1)}, bf16[1,384,384]{2,1,0:T(8,128)(2,1)S(1)}, u32[]{:S(2)}, u32[]{:S(2)}) collective-permute-start(bf16[1,384,384]{2,1,0:T(8,128)(2,1)} %get-tuple-element.53), channel_id=1, source_target_pairs={{0,16},{2,18},{4,20},{6,22},{8,24},{10,26},{12,28},{14,30},{16,0},... | collective-permute-start | bytes 884744 | tf_op jit(solution)/shard_map/ppermute | solution.py:28
  26.2 10.2 %collective-permute-done.refs_1_ = bf16[1,384,384]{2,1,0:T(8,128)(2,1)S(1)} collective-permute-done((bf16[1,384,384]{2,1,0:T(8,128)(2,1)}, bf16[1,384,384]{2,1,0:T(8,128)(2,1)S(1)}, u32[]{:S(2)}, u32[]{:S(2)}) %collective-permute-start) | collective-permute-done | bytes 294944 | tf_op jit(solution)/shard_map/ppermute | solution.py:28
  36.4 13.2 %project.4 = (bf16[1,384,256]{2,1,0:T(8,128)(2,1)}, bf16[1,384,256]{2,1,0:T(8,128)(2,1)}, bf16[1,384,256]{2,1,0:T(8,128)(2,1)}, bf16[1,384,256]{2,1,0:T(8,128)(2...) custom-call(s32[3]{0:T(128)} %pad_add_fusion.place_ref, ...), custom_call_target="tpu_custom_call" | custom-call | flops 4831838208 | bytes 14942208 | tf_op jit(solution)/shard_map/project/pallas_call | solution.py:143
  49.8 1.0 pad_maximum_fusion
  50.8 0.2 all-gather.5.cloned.1.call-start
  51.1 3.1 %collective-permute-start.3 = (bf16[1,384,256]{2,1,0:T(8,128)(2,1)S(1)}, bf16[1,384,256]{2,1,0:T(8,128)(2,1)S(1)}, u32[]{:S(2)}, u32[]{:S(2)}) collective-permute-start(bf16[1,384,256]{2,1,0:T(8,128)(2,1)S(1)} %copy-done.23), channel_id=1, source_target_pairs={{0,8},{2,10},{4,12},{6,14},{8,0},{10,2},{12,4},{14,6},{16,24},{18,... | collective-permute-start | bytes 589832 | tf_op jit(solution)/shard_map/ppermute | solution.py:28
  54.2 1.1 collective-permute-start.7
  55.3 1.4 collective-permute-start.8
  56.8 3.7 %collective-permute-done.3 = bf16[1,384,256]{2,1,0:T(8,128)(2,1)S(1)} collective-permute-done((bf16[1,384,256]{2,1,0:T(8,128)(2,1)S(1)}, bf16[1,384,256]{2,1,0:T(8,128)(2,1)S(1)}, u32[]{:S(2)}, u32[]{:S(2)}) %collective-permute-start.3) | collective-permute-done | bytes 196640 | tf_op jit(solution)/shard_map/ppermute | solution.py:28
  60.5 10.4 %collective-permute-done.7 = bf16[1,384,256]{2,1,0:T(8,128)(2,1)S(1)} collective-permute-done((bf16[1,384,256]{2,1,0:T(8,128)(2,1)S(1)}, bf16[1,384,256]{2,1,0:T(8,128)(2,1)S(1)}, u32[]{:S(2)}, u32[]{:S(2)}) %collective-permute-start.7) | collective-permute-done | bytes 196640 | tf_op jit(solution)/shard_map/ppermute | solution.py:28
  71.0 0.9 copy-done.3
  71.9 2.7 %collective-permute-start.4 = (bf16[1,384,256]{2,1,0:T(8,128)(2,1)S(1)}, bf16[1,384,256]{2,1,0:T(8,128)(2,1)S(1)}, u32[]{:S(2)}, u32[]{:S(2)}) collective-permute-start(bf16[1,384,256]{2,1,0:T(8,128)(2,1)S(1)} %copy-done.17), channel_id=1, source_target_pairs={{0,8},{2,10},{4,12},{6,14},{8,0},{10,2},{12,4},{14,6},{16,24},{18,... | collective-permute-start | bytes 589832 | tf_op jit(solution)/shard_map/ppermute | solution.py:28
  74.6 1.0 collective-permute-start.5
  75.6 1.4 collective-permute-start.6
  77.7 8.8 %project.5 = (bf16[2,384,128]{2,1,0:T(8,128)(2,1)}, bf16[2,384,128]{2,1,0:T(8,128)(2,1)}, bf16[2,384,128]{2,1,0:T(8,128)(2,1)}, bf16[2,384,128]{2,1,0:T(8,128)(2,1)}) custom-call(s32[3]{0:T(128)} %pad_add_fusion.place_ref, bf16[3,3072,1536]{2,1,0:T(8,128)(2,1)} %bitcast.7, f32[12,2,128]{2,1,0:T(2,128)} %bitcast.10, s32[1,1]{1,0:T(1,128)S(6)} %max.12.refs_2_, ...), custom_call_target="tpu_custom_call" | custom-call | flops 2415919104 | bytes 8650752 | tf_op jit(solution)/shard_map/project/pallas_call | solution.py:143
  86.5 4.2 %collective-permute-done.5 = bf16[1,384,256]{2,1,0:T(8,128)(2,1)S(1)} collective-permute-done((bf16[1,384,256]{2,1,0:T(8,128)(2,1)S(1)}, bf16[1,384,256]{2,1,0:T(8,128)(2,1)S(1)}, u32[]{:S(2)}, u32[]{:S(2)}) %collective-permute-start.5) | collective-permute-done | bytes 196640 | tf_op jit(solution)/shard_map/ppermute | solution.py:28
  90.8 1.6 collective-permute-start.12
  92.3 2.7 %collective-permute-start.9 = (bf16[2,384,128]{2,1,0:T(8,128)(2,1)}, bf16[2,384,128]{2,1,0:T(8,128)(2,1)S(1)}, u32[]{:S(2)}, u32[]{:S(2)}) collective-permute-start(bf16[2,384,128]{2,1,0:T(8,128)(2,1)} %get-tuple-element.80), channel_id=1, source_target_pairs={{0,8},{2,10},{4,12},{6,14},{8,0},{10,2},{12,4},{14,6},{16,24},{18,... | collective-permute-start | bytes 589832 | tf_op jit(solution)/shard_map/ppermute | solution.py:28
  95.0 1.4 collective-permute-start.10
  96.4 1.5 collective-permute-start.11
  97.9 3.3 %collective-permute-done.9.refs_1_ = bf16[2,384,128]{2,1,0:T(8,128)(2,1)S(1)} collective-permute-done((bf16[2,384,128]{2,1,0:T(8,128)(2,1)}, bf16[2,384,128]{2,1,0:T(8,128)(2,1)S(1)}, u32[]{:S(2)}, u32[]{:S(2)}) %collective-permute-start.9) | collective-permute-done | bytes 196640 | tf_op jit(solution)/shard_map/ppermute | solution.py:28
  101.2 0.6 broadcast_maximum_fusion.2.place_ref
  101.8 9.0 %attend.3 = bf16[4,384,128]{2,1,0:T(8,128)(2,1)} custom-call(s32[3]{0:T(128)} %broadcast_maximum_fusion.2.place_ref, bf16[1,384,384]{2,1,0:T(8,128)(2,1)} %get-tuple-element.83.refs_0_, bf16[1,384,384]{2,1,0:T(8,128)(2,1)} %copy-done.8, bf16[1,384,384]{2,1,0:T(8,128)(2,1)} %copy-done.9, bf16[1,384,384]{2,1,0:T(8,128)(2,1)} %copy-done.10, ...), custom_call_target="tpu_custom_call" | custom-call | flops 2415919104 | bytes 3145728 | tf_op jit(solution)/shard_map/attend/pallas_call | solution.py:260
  110.8 4.6 %all-to-all-start = ((bf16[4,384,128]{2,1,0:T(8,128)(2,1)}), bf16[4,384,128]{2,1,0:T(8,128)(2,1)S(1)}, u32[]{:S(2)}, u32[]{:S(2)}) async-start(bf16[4,384,128]{2,1,0:T(8,128)(2,1)} %attend.3), calls=%async_computation | async-start | bytes 786432 | tf_op jit(solution)/shard_map/all_to_all | solution.py:398
  115.4 7.3 %collective-permute-done.12.refs_6_ = bf16[4,384,256]{2,1,0:T(8,128)(2,1)S(1)} collective-permute-done((bf16[4,384,256]{2,1,0:T(8,128)(2,1)S(1)}, bf16[4,384,256]{2,1,0:T(8,128)(2,1)S(1)}, u32[]{:S(2)}, u32[]{:S(2)}) %collective-permute-start.12) | collective-permute-done | bytes 786464 | tf_op jit(solution)/shard_map/ppermute | solution.py:28
  122.7 0.6 broadcast_maximum_fusion.1.place_ref
  123.3 0.9 all-gather.5.cloned.1.call-done.refs_4_
  124.2 8.8 %attend.4 = bf16[4,384,128]{2,1,0:T(8,128)(2,1)} custom-call(s32[3]{0:T(128)} %broadcast_maximum_fusion.1.place_ref, bf16[2,384,128]{2,1,0:T(8,128)(2,1)} %get-tuple-element.90.refs_0_, bf16[2,384,128]{2,1,0:T(8,128)(2,1)} %copy-done.18, bf16[2,384,128]{2,1,0:T(8,128)(2,1)} %copy-done.19, bf16[2,384,128]{2,1,0:T(8,128)(2,1)} %copy-done.20, ...), custom_call_target="tpu_custom_call" | custom-call | flops 2415919104 | bytes 3145728 | tf_op jit(solution)/shard_map/attend/pallas_call | solution.py:260
  133.1 6.9 %all-to-all-start.1 = ((bf16[4,384,128]{2,1,0:T(8,128)(2,1)}), bf16[4,384,128]{2,1,0:T(8,128)(2,1)S(1)}, u32[]{:S(2)}, u32[]{:S(2)}) async-start(bf16[4,384,128]{2,1,0:T(8,128)(2,1)} %attend.4), calls=%async_computation.1 | async-start | bytes 786432 | tf_op jit(solution)/shard_map/all_to_all | solution.py:398
  140.0 0.6 broadcast_maximum_fusion.place_ref
  140.6 0.9 copy-done.14
  141.4 8.8 %attend.5 = (bf16[1,384,128]{2,1,0:T(8,128)(2,1)}, bf16[1,384,128]{2,1,0:T(8,128)(2,1)}, bf16[1,384,128]{2,1,0:T(8,128)(2,1)}, bf16[1,384,128]{2,1,0:T(8,128)(2,1)}) custom-call(s32[3]{0:T(128)} %broadcast_maximum_fusion.place_ref, bf16[2,384,128]{2,1,0:T(8,128)(2,1)} %get-tuple-element.90.refs_0_, bf16[2,384,128]{2,1,0:T(8,128)(2,1)} %copy-done.18, ...), custom_call_target="tpu_custom_call" | custom-call | flops 2415919104 | bytes 3145728 | tf_op jit(solution)/shard_map/attend/pallas_call | solution.py:260
  150.3 2.1 collective-permute-start.15
  152.4 2.4 %collective-permute-start.16 = (bf16[1,384,128]{2,1,0:T(8,128)(2,1)}, bf16[1,384,128]{2,1,0:T(8,128)(2,1)S(1)}, u32[]{:S(2)}, u32[]{:S(2)}) collective-permute-start(bf16[1,384,128]{2,1,0:T(8,128)(2,1)} %get-tuple-element.94), channel_id=1, source_target_pairs={{0,16},{2,18},{4,20},{6,22},{8,24},{10,26},{12,28},{14,30},{16,0},... | collective-permute-start | bytes 294920 | tf_op jit(solution)/shard_map/ppermute | solution.py:28
  154.8 0.9 constant_dynamic-update-slice_fusion.11
  155.7 3.8 %collective-permute-done.16 = bf16[1,384,128]{2,1,0:T(8,128)(2,1)S(1)} collective-permute-done((bf16[1,384,128]{2,1,0:T(8,128)(2,1)}, bf16[1,384,128]{2,1,0:T(8,128)(2,1)S(1)}, u32[]{:S(2)}, u32[]{:S(2)}) %collective-permute-start.16) | collective-permute-done | bytes 98336 | tf_op jit(solution)/shard_map/ppermute | solution.py:28
  159.6 2.8 %collective-permute-done.17 = bf16[1,384,128]{2,1,0:T(8,128)(2,1)S(1)} collective-permute-done((bf16[1,384,128]{2,1,0:T(8,128)(2,1)}, bf16[1,384,128]{2,1,0:T(8,128)(2,1)S(1)}, u32[]{:S(2)}, u32[]{:S(2)}) %collective-permute-start.17) | collective-permute-done | bytes 98336 | tf_op jit(solution)/shard_map/ppermute | solution.py:28
  162.4 0.7 copy-done.2
  163.1 0.7 copy-done.1
  163.9 7.0 %finish.2 = bf16[384,1536]{1,0:T(8,128)(2,1)} custom-call(s32[3]{0:T(128)} %pad_add_fusion.place_ref, bf16[4,384,128]{2,1,0:T(8,128)(2,1)} %copy-done, bf16[4,384,128]{2,1,0:T(8,128)(2,1)} %copy-done.1, bf16[4,384,128]{2,1,0:T(8,128)(2,1)} %copy-done.2, bf16[1536,3072]{1,0:T(8,128)(2,1)} %refs_3_.5), custom_call_target="tpu_custom_call" | custom-call | flops 1811939328 | bytes 7077888 | tf_op jit(solution)/shard_map/finish/pallas_call | solution.py:323
  170.9 1.5 collective-permute-start.18
  172.4 7.3 %finish.3.mine_ref = f32[384,1536]{1,0:T(8,128)} custom-call(s32[3]{0:T(128)} %pad_add_fusion.place_ref, bf16[4,384,128]{2,1,0:T(8,128)(2,1)} %copy-done, bf16[4,384,128]{2,1,0:T(8,128)(2,1)} %copy-done.1, bf16[4,384,128]{2,1,0:T(8,128)(2,1)} %copy-done.2, bf16[1536,3072]{1,0:T(8,128)(2,1)} %refs_3_.5), custom_call_target="tpu_custom_call" | custom-call | flops 1811939328 | bytes 7077888 | tf_op jit(solution)/shard_map/finish/pallas_call | solution.py:323
  179.7 19.9 %collective-permute-done.18.refs_0_ = bf16[384,1536]{1,0:T(8,128)(2,1)S(1)} collective-permute-done((bf16[384,1536]{1,0:T(8,128)(2,1)}, bf16[384,1536]{1,0:T(8,128)(2,1)S(1)}, u32[]{:S(2)}, u32[]{:S(2)}) %collective-permute-start.18) | collective-permute-done | bytes 1179680 | tf_op jit(solution)/shard_map/ppermute | solution.py:28
  199.6 1.1 copy-done.4
  200.6 4.6 %close.1 = bf16[384,1536]{1,0:T(8,128)(2,1)} custom-call(bf16[384,384]{1,0:T(8,128)(2,1)} %get-tuple-element.51.back_ref, f32[384,1536]{1,0:T(8,128)} %finish.3.mine_ref, bf16[384,1536]{1,0:T(8,128)(2,1)} %copy-done.4), custom_call_target="tpu_custom_call" | custom-call | flops 452984832 | bytes 5898240 | tf_op jit(solution)/shard_map/close/pallas_call | solution.py:353
  (78 shorter events, 0.5 us)
Async XLA Ops:
  6.5 95.3 %all-gather.3.cloned.1.call-start = ((), (), s32[]{:S(2)}) async-start(), calls=%async_computation.2 | async-start | bytes 3932160 | tf_op jit(solution)/shard_map/all_gather | solution.py:383
  20.5 15.9 %collective-permute-start = (bf16[1,384,384]{2,1,0:T(8,128)(2,1)}, bf16[1,384,384]{2,1,0:T(8,128)(2,1)S(1)}, u32[]{:S(2)}, u32[]{:S(2)}) collective-permute-start(bf16[1,384,384]{2,1,0:T(8,128)(2,1)} %get-tuple-element.52), channel_id=1, source_target_pairs={{0,8},{2,10},{4,12},{6,14},{8,0},{10,2},{12,4},{14,6},{16,24},{18,... | collective-permute-start | bytes 884744 | tf_op jit(solution)/shard_map/ppermute | solution.py:28
  23.6 26.0 %collective-permute-start.1 = (bf16[1,384,384]{2,1,0:T(8,128)(2,1)}, bf16[1,384,384]{2,1,0:T(8,128)(2,1)S(1)}, u32[]{:S(2)}, u32[]{:S(2)}) collective-permute-start(bf16[1,384,384]{2,1,0:T(8,128)(2,1)} %get-tuple-element.53), channel_id=1, source_target_pairs={{0,16},{2,18},{4,20},{6,22},{8,24},{10,26},{12,28},{14,30},{16,0},... | collective-permute-start | bytes 884744 | tf_op jit(solution)/shard_map/ppermute | solution.py:28
  26.2 23.5 %collective-permute-start.2 = (bf16[1,384,384]{2,1,0:T(8,128)(2,1)}, bf16[1,384,384]{2,1,0:T(8,128)(2,1)S(1)}, u32[]{:S(2)}, u32[]{:S(2)}) collective-permute-start(bf16[1,384,384]{2,1,0:T(8,128)(2,1)} %get-tuple-element.54), channel_id=1, source_target_pairs={{0,24},{2,26},{4,28},{6,30},{8,16},{10,18},{12,20},{14,22},{16,8},... | collective-permute-start | bytes 884744 | tf_op jit(solution)/shard_map/ppermute | solution.py:28
  36.4 13.4 %copy-start.8 = (bf16[1,384,384]{2,1,0:T(8,128)(2,1)}, bf16[1,384,384]{2,1,0:T(8,128)(2,1)S(1)}, u32[]{:S(2)}) copy-start(bf16[1,384,384]{2,1,0:T(8,128)(2,1)S(1)} %collective-permute-done.refs_1_) | copy-start | bytes 884740
  36.4 13.4 %copy-start.7 = (bf16[1,384,384]{2,1,0:T(8,128)(2,1)S(1)}, bf16[1,384,384]{2,1,0:T(8,128)(2,1)}, u32[]{:S(2)}) copy-start(bf16[1,384,384]{2,1,0:T(8,128)(2,1)} %get-tuple-element.83.refs_0_) | copy-start | bytes 884740
  49.6 1.4 copy-start.23
  49.6 4.6 %copy-start.22 = (bf16[1,384,256]{2,1,0:T(8,128)(2,1)S(1)}, bf16[1,384,256]{2,1,0:T(8,128)(2,1)}, u32[]{:S(2)}) copy-start(bf16[1,384,256]{2,1,0:T(8,128)(2,1)} %get-tuple-element.69) | copy-start | bytes 589828
  49.6 5.7 %copy-start.21 = (bf16[1,384,256]{2,1,0:T(8,128)(2,1)S(1)}, bf16[1,384,256]{2,1,0:T(8,128)(2,1)}, u32[]{:S(2)}) copy-start(bf16[1,384,256]{2,1,0:T(8,128)(2,1)} %get-tuple-element.70) | copy-start | bytes 589828
  49.7 7.1 %copy-start.6 = (bf16[1,384,256]{2,1,0:T(8,128)(2,1)S(1)}, bf16[1,384,256]{2,1,0:T(8,128)(2,1)}, u32[]{:S(2)}) copy-start(bf16[1,384,256]{2,1,0:T(8,128)(2,1)} %get-tuple-element.68) | copy-start | bytes 589828
  49.7 10.9 %copy-start.9 = (bf16[1,384,384]{2,1,0:T(8,128)(2,1)}, bf16[1,384,384]{2,1,0:T(8,128)(2,1)S(1)}, u32[]{:S(2)}) copy-start(bf16[1,384,384]{2,1,0:T(8,128)(2,1)S(1)} %collective-permute-done.1.refs_2_) | copy-start | bytes 884740
  49.7 10.8 %copy-start.10 = (bf16[1,384,384]{2,1,0:T(8,128)(2,1)}, bf16[1,384,384]{2,1,0:T(8,128)(2,1)S(1)}, u32[]{:S(2)}) copy-start(bf16[1,384,384]{2,1,0:T(8,128)(2,1)S(1)} %collective-permute-done.2.refs_3_) | copy-start | bytes 884740
  49.8 22.1 %copy-start.17 = (bf16[1,384,256]{2,1,0:T(8,128)(2,1)S(1)}, bf16[1,384,256]{2,1,0:T(8,128)(2,1)}, u32[]{:S(2)}) copy-start(bf16[1,384,256]{2,1,0:T(8,128)(2,1)} %get-tuple-element.65) | copy-start | bytes 589828
  49.8 24.8 %copy-start.16 = (bf16[1,384,256]{2,1,0:T(8,128)(2,1)S(1)}, bf16[1,384,256]{2,1,0:T(8,128)(2,1)}, u32[]{:S(2)}) copy-start(bf16[1,384,256]{2,1,0:T(8,128)(2,1)} %get-tuple-element.66) | copy-start | bytes 589828
  49.8 25.8 %copy-start.15 = (bf16[1,384,256]{2,1,0:T(8,128)(2,1)S(1)}, bf16[1,384,256]{2,1,0:T(8,128)(2,1)}, u32[]{:S(2)}) copy-start(bf16[1,384,256]{2,1,0:T(8,128)(2,1)} %get-tuple-element.67) | copy-start | bytes 589828
  50.8 73.4 %all-gather.5.cloned.1.call-start = ((), (), s32[]{:S(2)}) async-start(), calls=%async_computation.3 | async-start | bytes 3932160 | tf_op jit(solution)/shard_map/all_gather | solution.py:383
  51.1 9.4 %collective-permute-start.3 = (bf16[1,384,256]{2,1,0:T(8,128)(2,1)S(1)}, bf16[1,384,256]{2,1,0:T(8,128)(2,1)S(1)}, u32[]{:S(2)}, u32[]{:S(2)}) collective-permute-start(bf16[1,384,256]{2,1,0:T(8,128)(2,1)S(1)} %copy-done.23), channel_id=1, source_target_pairs={{0,8},{2,10},{4,12},{6,14},{8,0},{10,2},{12,4},{14,6},{16,24},{18,... | collective-permute-start | bytes 589832 | tf_op jit(solution)/shard_map/ppermute | solution.py:28
  54.2 16.7 %collective-permute-start.7 = (bf16[1,384,256]{2,1,0:T(8,128)(2,1)S(1)}, bf16[1,384,256]{2,1,0:T(8,128)(2,1)S(1)}, u32[]{:S(2)}, u32[]{:S(2)}) collective-permute-start(bf16[1,384,256]{2,1,0:T(8,128)(2,1)S(1)} %copy-done.22), channel_id=1, source_target_pairs={{0,16},{2,18},{4,20},{6,22},{8,24},{10,26},{12,28},{14,30},{16,0},... | collective-permute-start | bytes 589832 | tf_op jit(solution)/shard_map/ppermute | solution.py:28
  55.3 15.6 %collective-permute-start.8 = (bf16[1,384,256]{2,1,0:T(8,128)(2,1)S(1)}, bf16[1,384,256]{2,1,0:T(8,128)(2,1)S(1)}, u32[]{:S(2)}, u32[]{:S(2)}) collective-permute-start(bf16[1,384,256]{2,1,0:T(8,128)(2,1)S(1)} %copy-done.21), channel_id=1, source_target_pairs={{0,24},{2,26},{4,28},{6,30},{8,16},{10,18},{12,20},{14,22},{16,8},... | collective-permute-start | bytes 589832 | tf_op jit(solution)/shard_map/ppermute | solution.py:28
  71.0 0.9 copy-start.3
  71.9 14.6 %collective-permute-start.4 = (bf16[1,384,256]{2,1,0:T(8,128)(2,1)S(1)}, bf16[1,384,256]{2,1,0:T(8,128)(2,1)S(1)}, u32[]{:S(2)}, u32[]{:S(2)}) collective-permute-start(bf16[1,384,256]{2,1,0:T(8,128)(2,1)S(1)} %copy-done.17), channel_id=1, source_target_pairs={{0,8},{2,10},{4,12},{6,14},{8,0},{10,2},{12,4},{14,6},{16,24},{18,... | collective-permute-start | bytes 589832 | tf_op jit(solution)/shard_map/ppermute | solution.py:28
  74.6 16.1 %collective-permute-start.5 = (bf16[1,384,256]{2,1,0:T(8,128)(2,1)S(1)}, bf16[1,384,256]{2,1,0:T(8,128)(2,1)S(1)}, u32[]{:S(2)}, u32[]{:S(2)}) collective-permute-start(bf16[1,384,256]{2,1,0:T(8,128)(2,1)S(1)} %copy-done.16), channel_id=1, source_target_pairs={{0,16},{2,18},{4,20},{6,22},{8,24},{10,26},{12,28},{14,30},{16,0},... | collective-permute-start | bytes 589832 | tf_op jit(solution)/shard_map/ppermute | solution.py:28
  75.6 15.0 %collective-permute-start.6 = (bf16[1,384,256]{2,1,0:T(8,128)(2,1)S(1)}, bf16[1,384,256]{2,1,0:T(8,128)(2,1)S(1)}, u32[]{:S(2)}, u32[]{:S(2)}) collective-permute-start(bf16[1,384,256]{2,1,0:T(8,128)(2,1)S(1)} %copy-done.15), channel_id=1, source_target_pairs={{0,24},{2,26},{4,28},{6,30},{8,16},{10,18},{12,20},{14,22},{16,8},... | collective-permute-start | bytes 589832 | tf_op jit(solution)/shard_map/ppermute | solution.py:28
  77.7 13.0 %copy-start.5 = (bf16[1,384,256]{2,1,0:T(8,128)(2,1)S(1)}, bf16[1,384,256]{2,1,0:T(8,128)(2,1)}, u32[]{:S(2)}) copy-start(bf16[1,384,256]{2,1,0:T(8,128)(2,1)} %get-tuple-element.73) | copy-start | bytes 589828
  77.7 23.5 %copy-start.12 = (s32[3]{0:T(128)S(1)}, s32[3]{0:T(128)}, u32[]{:S(2)}) copy-start(s32[3]{0:T(128)} %pad_add_fusion.place_ref) | copy-start | bytes 40
  90.7 24.6 %copy-start.11 = (bf16[4,384,256]{2,1,0:T(8,128)(2,1)}, bf16[4,384,256]{2,1,0:T(8,128)(2,1)S(1)}, u32[]{:S(2)}) copy-start(bf16[4,384,256]{2,1,0:T(8,128)(2,1)S(1)} %constant_dynamic-update-slice_fusion.4.refs_4_) | copy-start | bytes 2359300
  90.8 31.9 %collective-permute-start.12 = (bf16[4,384,256]{2,1,0:T(8,128)(2,1)S(1)}, bf16[4,384,256]{2,1,0:T(8,128)(2,1)S(1)}, u32[]{:S(2)}, u32[]{:S(2)}) collective-permute-start(bf16[4,384,256]{2,1,0:T(8,128)(2,1)S(1)} %constant_dynamic-update-slice_fusion.4.refs_4_), channel_id=1, source_target_pairs={{0,4},{2,6},{4,0},{6,2},{8,12},{10,14},{12,8},{14,10},{16,20},{18,... | collective-permute-start | bytes 2359304 | tf_op jit(solution)/shard_map/ppermute | solution.py:28
  92.3 8.9 %collective-permute-start.9 = (bf16[2,384,128]{2,1,0:T(8,128)(2,1)}, bf16[2,384,128]{2,1,0:T(8,128)(2,1)S(1)}, u32[]{:S(2)}, u32[]{:S(2)}) collective-permute-start(bf16[2,384,128]{2,1,0:T(8,128)(2,1)} %get-tuple-element.80), channel_id=1, source_target_pairs={{0,8},{2,10},{4,12},{6,14},{8,0},{10,2},{12,4},{14,6},{16,24},{18,... | collective-permute-start | bytes 589832 | tf_op jit(solution)/shard_map/ppermute | solution.py:28
  95.0 27.6 %collective-permute-start.10 = (bf16[2,384,128]{2,1,0:T(8,128)(2,1)}, bf16[2,384,128]{2,1,0:T(8,128)(2,1)S(1)}, u32[]{:S(2)}, u32[]{:S(2)}) collective-permute-start(bf16[2,384,128]{2,1,0:T(8,128)(2,1)} %get-tuple-element.87), channel_id=1, source_target_pairs={{0,16},{2,18},{4,20},{6,22},{8,24},{10,26},{12,28},{14,30},{16,0},... | collective-permute-start | bytes 589832 | tf_op jit(solution)/shard_map/ppermute | solution.py:28
  96.4 26.2 %collective-permute-start.11 = (bf16[2,384,128]{2,1,0:T(8,128)(2,1)}, bf16[2,384,128]{2,1,0:T(8,128)(2,1)S(1)}, u32[]{:S(2)}, u32[]{:S(2)}) collective-permute-start(bf16[2,384,128]{2,1,0:T(8,128)(2,1)} %get-tuple-element.88), channel_id=1, source_target_pairs={{0,24},{2,26},{4,28},{6,30},{8,16},{10,18},{12,20},{14,22},{16,8},... | collective-permute-start | bytes 589832 | tf_op jit(solution)/shard_map/ppermute | solution.py:28
  101.2 9.6 %copy-start.18 = (bf16[2,384,128]{2,1,0:T(8,128)(2,1)}, bf16[2,384,128]{2,1,0:T(8,128)(2,1)S(1)}, u32[]{:S(2)}) copy-start(bf16[2,384,128]{2,1,0:T(8,128)(2,1)S(1)} %collective-permute-done.9.refs_1_) | copy-start | bytes 589828
  110.8 22.3 %all-to-all-start = ((bf16[4,384,128]{2,1,0:T(8,128)(2,1)}), bf16[4,384,128]{2,1,0:T(8,128)(2,1)S(1)}, u32[]{:S(2)}, u32[]{:S(2)}) async-start(bf16[4,384,128]{2,1,0:T(8,128)(2,1)} %attend.3), calls=%async_computation | async-start | bytes 786432 | tf_op jit(solution)/shard_map/all_to_all | solution.py:398
  115.4 25.2 %collective-permute-start.13 = (bf16[4,384,256]{2,1,0:T(8,128)(2,1)S(1)}, bf16[4,384,256]{2,1,0:T(8,128)(2,1)S(1)}, u32[]{:S(2)}, u32[]{:S(2)}) collective-permute-start(bf16[4,384,256]{2,1,0:T(8,128)(2,1)S(1)} %constant_dynamic-update-slice_fusion.4.refs_4_), channel_id=1, source_target_pairs={{0,2},{2,0},{4,6},{6,4},{8,10},{10,8},{12,14},{14,12},{16,18},{18,... | collective-permute-start | bytes 2359304 | tf_op jit(solution)/shard_map/ppermute | solution.py:28
  122.6 10.4 %copy-start.13 = (bf16[4,384,256]{2,1,0:T(8,128)(2,1)}, bf16[4,384,256]{2,1,0:T(8,128)(2,1)S(1)}, u32[]{:S(2)}) copy-start(bf16[4,384,256]{2,1,0:T(8,128)(2,1)S(1)} %collective-permute-done.12.refs_6_) | copy-start | bytes 2359300
  122.6 17.9 %collective-permute-start.14 = (bf16[4,384,256]{2,1,0:T(8,128)(2,1)S(1)}, bf16[4,384,256]{2,1,0:T(8,128)(2,1)}, u32[]{:S(2)}, u32[]{:S(2)}) collective-permute-start(bf16[4,384,256]{2,1,0:T(8,128)(2,1)S(1)} %collective-permute-done.12.refs_6_), channel_id=1, source_target_pairs={{0,2},{2,0},{4,6},{6,4},{8,10},{10,8},{12,14},{14,12},{16,18},{18,... | collective-permute-start | bytes 2359304 | tf_op jit(solution)/shard_map/ppermute | solution.py:28
  122.6 1.6 copy-start.19
  122.7 1.6 copy-start.20
  133.0 17.3 %copy-start = (bf16[4,384,128]{2,1,0:T(8,128)(2,1)}, bf16[4,384,128]{2,1,0:T(8,128)(2,1)S(1)}, u32[]{:S(2)}) copy-start(bf16[4,384,128]{2,1,0:T(8,128)(2,1)S(1)} %all-to-all-done.refs_0_) | copy-start | bytes 1179652
  133.1 29.4 %all-to-all-start.1 = ((bf16[4,384,128]{2,1,0:T(8,128)(2,1)}), bf16[4,384,128]{2,1,0:T(8,128)(2,1)S(1)}, u32[]{:S(2)}, u32[]{:S(2)}) async-start(bf16[4,384,128]{2,1,0:T(8,128)(2,1)} %attend.4), calls=%async_computation.1 | async-start | bytes 786432 | tf_op jit(solution)/shard_map/all_to_all | solution.py:398
  140.6 0.9 copy-start.14
  150.3 5.4 %collective-permute-start.15 = (bf16[1,384,128]{2,1,0:T(8,128)(2,1)}, bf16[1,384,128]{2,1,0:T(8,128)(2,1)S(1)}, u32[]{:S(2)}, u32[]{:S(2)}) collective-permute-start(bf16[1,384,128]{2,1,0:T(8,128)(2,1)} %get-tuple-element.93), channel_id=1, source_target_pairs={{0,8},{2,10},{4,12},{6,14},{8,0},{10,2},{12,4},{14,6},{16,24},{18,... | collective-permute-start | bytes 294920 | tf_op jit(solution)/shard_map/ppermute | solution.py:28
  152.4 7.2 %collective-permute-start.16 = (bf16[1,384,128]{2,1,0:T(8,128)(2,1)}, bf16[1,384,128]{2,1,0:T(8,128)(2,1)S(1)}, u32[]{:S(2)}, u32[]{:S(2)}) collective-permute-start(bf16[1,384,128]{2,1,0:T(8,128)(2,1)} %get-tuple-element.94), channel_id=1, source_target_pairs={{0,16},{2,18},{4,20},{6,22},{8,24},{10,26},{12,28},{14,30},{16,0},... | collective-permute-start | bytes 294920 | tf_op jit(solution)/shard_map/ppermute | solution.py:28
  154.7 7.7 %collective-permute-start.17 = (bf16[1,384,128]{2,1,0:T(8,128)(2,1)}, bf16[1,384,128]{2,1,0:T(8,128)(2,1)S(1)}, u32[]{:S(2)}, u32[]{:S(2)}) collective-permute-start(bf16[1,384,128]{2,1,0:T(8,128)(2,1)} %get-tuple-element.95), channel_id=1, source_target_pairs={{0,24},{2,26},{4,28},{6,30},{8,16},{10,18},{12,20},{14,22},{16,8},... | collective-permute-start | bytes 294920 | tf_op jit(solution)/shard_map/ppermute | solution.py:28
  162.4 0.7 copy-start.2
  163.1 0.7 copy-start.1
  170.9 28.6 %collective-permute-start.18 = (bf16[384,1536]{1,0:T(8,128)(2,1)}, bf16[384,1536]{1,0:T(8,128)(2,1)S(1)}, u32[]{:S(2)}, u32[]{:S(2)}) collective-permute-start(bf16[384,1536]{1,0:T(8,128)(2,1)} %finish.2), channel_id=1, source_target_pairs={{0,1},{1,0},{2,3},{3,2},{4,5},{5,4},{6,7},{7,6},{8,9},{9,8},{10,11... | collective-permute-start | bytes 3538952 | tf_op jit(solution)/shard_map/ppermute | solution.py:28
  199.6 1.1 copy-start.4
Sparse Core Ops, SparseCore 0:
  51.0 30.2 all-gather.2
  82.8 41.3 all-gather.4

commit v10 on v9

--- a/solution.py
+++ b/solution.py
@@ -382,15 +382,18 @@
     def gather(stacked):
         return [lax.all_gather(stacked, "seq", axis=0, tiled=True, axis_index_groups=rings)]
 
-    def everywhere(stacked, hop):
+    def everywhere(stacked, hop, gate):
         if hop is None:
             return gather(stacked)
         found, mask = {0: stacked, ring // 2: hop}, ring // 4
         while mask:
             for known in list(found):
-                found[known | mask] = flip(found[known], "seq", mask)
+                found[known | mask] = flip(chain(found[known], gate), "seq", mask)
             mask //= 2
         return [found[mask] for mask in range(ring)]
+
+    def hop(stacked):
+        return flip(stacked, "seq", ring // 2) if ring > 1 and groups > 1 else None
 
     def send_back(blocks):
         if groups == 1:
@@ -417,7 +420,7 @@
     normed, chosen, back, count = rest
     arrived = [swap(blocks)]
 
-    rest, asked, hop = range(1, chunks), None, None
+    rest, asked, hops = range(1, chunks), None, [None]
     if chunks > 1:
         prepared = (count, chain(normed, first(arrived[0])), chosen)
         sets = [((1, 2), (chunk,)) for chunk in rest]
@@ -427,13 +430,14 @@
         for blocks in made[1:]:
             arrived.append(send(blocks, first(arrived[-1])))
         stacks.append(stack(arrived[1]))
+        hops.append(hop(stacks[1]))
         sets = [((0,), tuple(rest))]
         ready = later(count, stacks[1])
         (made,), _ = project(place, (ready, normed, chosen), weights, gains, sets, groups)
-        stacks += [stack(list(chain(tuple(blocks), made[0]))) for blocks in arrived[2:]]
+        earlier = [made[0]] + [found for found in hops if found is not None]
+        stacks += [stack(list(chain(tuple(blocks), *earlier))) for blocks in arrived[2:]]
         asked = send(made, stacks[-1])
-        if ring > 1 and groups > 1:
-            hop = flip(stacks[-1], "seq", ring // 2)
+        hops += [hop(stacked) for stacked in stacks[2:]]
     else:
         stacks = [stack(arrived[0])]
 
@@ -441,10 +445,10 @@
     query, low_lane = arrived[0], 2 * size
     for chunk in range(chunks):
         final = chunk == chunks - 1
-        keyvals = everywhere(stacks[chunk], hop if final else None)
+        keyvals = everywhere(stacks[chunk], hops[chunk], tuple(attended[-1:]))
         before = [stacks[-1]] + attended[-1:]
         if chunk:
-            before += [hop] if hop is not None else []
+            before += [hops[-1]] if hops[-1] is not None else []
         elif asked is not None:
             before.append(first(asked))
         before += returned[:1] if final else []

time: 214 us -> 225 us (1.051)
  waiting for transfers between devices: 66.5 us -> 77.3 us
    ppermute x19 -> x22, waiting for transfers between devices: 65.6 us -> 77.3 us  [flip(): return lax.ppermute(values, axis, [(i, i ^ mask) for i in range(size)])]
    ppermute x19 -> x22, starting transfers between devices: 29.7 us -> 33.2 us  [flip(): return lax.ppermute(values, axis, [(i, i ^ mask) for i in range(size)])]
    unnamed x57 -> x59, local copies, waits for them, and re-layouts: 5.35 us -> 4.63 us
  transfers between devices with their start and end apart: 23 -> 25, of which waited for: 10 -> 10; matrix products, arithmetic and copies ran while one was open for 1% -> 1% of each run, Pallas kernels for 26% -> 25%
where the time goes in v10:
time: 225 us; the launch traced here: 224 us
  Pallas kernels  80.9 us (36%)
  waiting for transfers between devices  77.3 us (34%)
  starting transfers between devices  43.3 us (19%)
  between operations  14.3 us (6%)
  local copies, waits for them, and re-layouts  4.74 us (2%)
  other arithmetic  3.31 us (1%)
    ppermute x22, waiting for transfers between devices, flip(): return lax.ppermute(values, axis, [(i, i ^ mask) for i in range(size)])  77.3 us
    pallas_call x3, Pallas kernels, project(): pl.pallas_call(functools.partial(project_body, steps=steps, groups=groups...  35.5 us
    ppermute x22, starting transfers between devices, flip(): return lax.ppermute(values, axis, [(i, i ^ mask) for i in range(size)])  33.2 us
    pallas_call x3, Pallas kernels, attend(): pl.pallas_call(functools.partial(attend_body, groups=groups, ordered=orde...  26.5 us
    pallas_call x2, Pallas kernels, finish(): pl.pallas_call(functools.partial(finish_body, ordered=ordered), grid_spec...  14.4 us
    all_to_all x2, starting transfers between devices, send_back(): lax.all_to_all(blocks, 'seq', split_axis=0, concat_axis=0, axis_index_gro...  10.1 us
    unnamed x59, local copies, waits for them, and re-layouts  4.63 us
    pallas_call x1, Pallas kernels, close(): pl.pallas_call(close_body, grid=(parts,), in_specs=[pl.BlockSpec((rows, r...  4.56 us
  transfers between devices with their start and end apart: 25, of which 10 were waited for; matrix products, arithmetic and copies ran while one was open for 1% of the time, Pallas kernels for 25%

profile of v10, /device:TPU:0, one launch (start us, length us, event | category | flops | bytes accessed | tf_op | source)
XLA Modules:
  0.0 224.0 jit_solution(10101954987779346410)
XLA Ops:
  6.5 0.6 pad_add_fusion.place_ref
  7.1 13.4 %project.3 = (bf16[1,384,384]{2,1,0:T(8,128)(2,1)}, bf16[1,384,384]{2,1,0:T(8,128)(2,1)}, bf16[1,384,384]{2,1,0:T(8,128)(2,1)}, bf16[1,384,384]{2,1,0:T(8,128)(2...) custom-call(s32[3]{0:T(128)} %pad_add_fusion.place_ref, ...), custom_call_target="tpu_custom_call" | custom-call | flops 3623878656 | bytes 11796480 | tf_op jit(solution)/shard_map/project/pallas_call | solution.py:143
  20.5 3.1 %collective-permute-start = (bf16[1,384,384]{2,1,0:T(8,128)(2,1)}, bf16[1,384,384]{2,1,0:T(8,128)(2,1)S(1)}, u32[]{:S(2)}, u32[]{:S(2)}) collective-permute-start(bf16[1,384,384]{2,1,0:T(8,128)(2,1)} %get-tuple-element.56), channel_id=1, source_target_pairs={{0,8},{2,10},{4,12},{6,14},{8,0},{10,2},{12,4},{14,6},{16,24},{18,... | collective-permute-start | bytes 884744 | tf_op jit(solution)/shard_map/ppermute | solution.py:28
  23.6 2.6 %collective-permute-start.1 = (bf16[1,384,384]{2,1,0:T(8,128)(2,1)}, bf16[1,384,384]{2,1,0:T(8,128)(2,1)S(1)}, u32[]{:S(2)}, u32[]{:S(2)}) collective-permute-start(bf16[1,384,384]{2,1,0:T(8,128)(2,1)} %get-tuple-element.57), channel_id=1, source_target_pairs={{0,16},{2,18},{4,20},{6,22},{8,24},{10,26},{12,28},{14,30},{16,0},... | collective-permute-start | bytes 884744 | tf_op jit(solution)/shard_map/ppermute | solution.py:28
  26.2 10.2 %collective-permute-done.refs_1_ = bf16[1,384,384]{2,1,0:T(8,128)(2,1)S(1)} collective-permute-done((bf16[1,384,384]{2,1,0:T(8,128)(2,1)}, bf16[1,384,384]{2,1,0:T(8,128)(2,1)S(1)}, u32[]{:S(2)}, u32[]{:S(2)}) %collective-permute-start) | collective-permute-done | bytes 294944 | tf_op jit(solution)/shard_map/ppermute | solution.py:28
  36.4 13.3 %project.4 = (bf16[1,384,256]{2,1,0:T(8,128)(2,1)}, bf16[1,384,256]{2,1,0:T(8,128)(2,1)}, bf16[1,384,256]{2,1,0:T(8,128)(2,1)}, bf16[1,384,256]{2,1,0:T(8,128)(2...) custom-call(s32[3]{0:T(128)} %pad_add_fusion.place_ref, ...), custom_call_target="tpu_custom_call" | custom-call | flops 4831838208 | bytes 14942208 | tf_op jit(solution)/shard_map/project/pallas_call | solution.py:143
  49.9 1.0 pad_maximum_fusion
  50.9 3.1 %collective-permute-start.3 = (bf16[1,384,256]{2,1,0:T(8,128)(2,1)S(1)}, bf16[1,384,256]{2,1,0:T(8,128)(2,1)S(1)}, u32[]{:S(2)}, u32[]{:S(2)}) collective-permute-start(bf16[1,384,256]{2,1,0:T(8,128)(2,1)S(1)} %copy-done.24), channel_id=1, source_target_pairs={{0,8},{2,10},{4,12},{6,14},{8,0},{10,2},{12,4},{14,6},{16,24},{18,... | collective-permute-start | bytes 589832 | tf_op jit(solution)/shard_map/ppermute | solution.py:28
  54.0 1.1 collective-permute-start.7
  55.1 1.4 collective-permute-start.8
  56.6 3.7 %collective-permute-done.3 = bf16[1,384,256]{2,1,0:T(8,128)(2,1)S(1)} collective-permute-done((bf16[1,384,256]{2,1,0:T(8,128)(2,1)S(1)}, bf16[1,384,256]{2,1,0:T(8,128)(2,1)S(1)}, u32[]{:S(2)}, u32[]{:S(2)}) %collective-permute-start.3) | collective-permute-done | bytes 196640 | tf_op jit(solution)/shard_map/ppermute | solution.py:28
  60.3 10.4 %collective-permute-done.7 = bf16[1,384,256]{2,1,0:T(8,128)(2,1)S(1)} collective-permute-done((bf16[1,384,256]{2,1,0:T(8,128)(2,1)S(1)}, bf16[1,384,256]{2,1,0:T(8,128)(2,1)S(1)}, u32[]{:S(2)}, u32[]{:S(2)}) %collective-permute-start.7) | collective-permute-done | bytes 196640 | tf_op jit(solution)/shard_map/ppermute | solution.py:28
  70.7 1.6 collective-permute-start.9
  72.3 2.6 %collective-permute-start.4 = (bf16[1,384,256]{2,1,0:T(8,128)(2,1)S(1)}, bf16[1,384,256]{2,1,0:T(8,128)(2,1)S(1)}, u32[]{:S(2)}, u32[]{:S(2)}) collective-permute-start(bf16[1,384,256]{2,1,0:T(8,128)(2,1)S(1)} %copy-done.17), channel_id=1, source_target_pairs={{0,8},{2,10},{4,12},{6,14},{8,0},{10,2},{12,4},{14,6},{16,24},{18,... | collective-permute-start | bytes 589832 | tf_op jit(solution)/shard_map/ppermute | solution.py:28
  75.0 1.0 collective-permute-start.5
  76.0 1.5 collective-permute-start.6
  78.1 8.9 %project.5 = (bf16[2,384,128]{2,1,0:T(8,128)(2,1)}, bf16[2,384,128]{2,1,0:T(8,128)(2,1)}, bf16[2,384,128]{2,1,0:T(8,128)(2,1)}, bf16[2,384,128]{2,1,0:T(8,128)(2,1)}) custom-call(s32[3]{0:T(128)} %pad_add_fusion.place_ref, bf16[3,3072,1536]{2,1,0:T(8,128)(2,1)} %bitcast.7, f32[12,2,128]{2,1,0:T(2,128)} %bitcast.10, s32[1,1]{1,0:T(1,128)S(6)} %max.12.refs_2_, ...), custom_call_target="tpu_custom_call" | custom-call | flops 2415919104 | bytes 8650752 | tf_op jit(solution)/shard_map/project/pallas_call | solution.py:143
  87.0 3.7 %collective-permute-done.5 = bf16[1,384,256]{2,1,0:T(8,128)(2,1)S(1)} collective-permute-done((bf16[1,384,256]{2,1,0:T(8,128)(2,1)S(1)}, bf16[1,384,256]{2,1,0:T(8,128)(2,1)S(1)}, u32[]{:S(2)}, u32[]{:S(2)}) %collective-permute-start.5) | collective-permute-done | bytes 196640 | tf_op jit(solution)/shard_map/ppermute | solution.py:28
  90.7 5.9 %collective-permute-done.9.refs_6_ = bf16[4,384,256]{2,1,0:T(8,128)(2,1)} collective-permute-done((bf16[4,384,256]{2,1,0:T(8,128)(2,1)S(1)}, bf16[4,384,256]{2,1,0:T(8,128)(2,1)}, u32[]{:S(2)}, u32[]{:S(2)}) %collective-permute-start.9) | collective-permute-done | bytes 786464 | tf_op jit(solution)/shard_map/ppermute | solution.py:28
  96.8 1.6 collective-permute-start.10
  98.3 0.6 collective-permute-start.13
  98.9 3.9 %collective-permute-done.10.refs_1_ = bf16[2,384,128]{2,1,0:T(8,128)(2,1)S(1)} collective-permute-done((bf16[2,384,128]{2,1,0:T(8,128)(2,1)}, bf16[2,384,128]{2,1,0:T(8,128)(2,1)S(1)}, u32[]{:S(2)}, u32[]{:S(2)}) %collective-permute-start.10) | collective-permute-done | bytes 196640 | tf_op jit(solution)/shard_map/ppermute | solution.py:28
  102.7 0.6 broadcast_maximum_fusion.2.place_ref
  103.4 9.1 %attend.3 = bf16[4,384,128]{2,1,0:T(8,128)(2,1)} custom-call(s32[3]{0:T(128)} %broadcast_maximum_fusion.2.place_ref, bf16[1,384,384]{2,1,0:T(8,128)(2,1)} %get-tuple-element.87.refs_0_, bf16[1,384,384]{2,1,0:T(8,128)(2,1)} %copy-done.7, bf16[1,384,384]{2,1,0:T(8,128)(2,1)} %copy-done.8, bf16[1,384,384]{2,1,0:T(8,128)(2,1)} %copy-done.9, ...), custom_call_target="tpu_custom_call" | custom-call | flops 2415919104 | bytes 3145728 | tf_op jit(solution)/shard_map/attend/pallas_call | solution.py:260
  113.0 3.3 %collective-permute-start.11 = (bf16[2,384,128]{2,1,0:T(8,128)(2,1)S(1)}, bf16[2,384,128]{2,1,0:T(8,128)(2,1)S(1)}, u32[]{:S(2)}, u32[]{:S(2)}) collective-permute-start(bf16[2,384,128]{2,1,0:T(8,128)(2,1)S(1)} %copy-done.19), channel_id=1, source_target_pairs={{0,16},{2,18},{4,20},{6,22},{8,24},{10,26},{12,28},{14,30},{16,0},... | collective-permute-start | bytes 589832 | tf_op jit(solution)/shard_map/ppermute | solution.py:28
  116.3 1.2 collective-permute-start.12
  117.5 3.9 %all-to-all-start = ((bf16[4,384,128]{2,1,0:T(8,128)(2,1)}), bf16[4,384,128]{2,1,0:T(8,128)(2,1)S(1)}, u32[]{:S(2)}, u32[]{:S(2)}) async-start(bf16[4,384,128]{2,1,0:T(8,128)(2,1)} %attend.3), calls=%async_computation | async-start | bytes 786432 | tf_op jit(solution)/shard_map/all_to_all | solution.py:401
  121.3 13.3 %collective-permute-done.11.refs_2_ = bf16[2,384,128]{2,1,0:T(8,128)(2,1)S(1)} collective-permute-done((bf16[2,384,128]{2,1,0:T(8,128)(2,1)S(1)}, bf16[2,384,128]{2,1,0:T(8,128)(2,1)S(1)}, u32[]{:S(2)}, u32[]{:S(2)}) %collective-permute-start.11) | collective-permute-done | bytes 196640 | tf_op jit(solution)/shard_map/ppermute | solution.py:28
  134.7 0.6 broadcast_maximum_fusion.1.place_ref
  135.4 8.7 %attend.4 = bf16[4,384,128]{2,1,0:T(8,128)(2,1)} custom-call(s32[3]{0:T(128)} %broadcast_maximum_fusion.1.place_ref, bf16[2,384,128]{2,1,0:T(8,128)(2,1)} %get-tuple-element.94.refs_0_, bf16[2,384,128]{2,1,0:T(8,128)(2,1)} %copy-done.15, bf16[2,384,128]{2,1,0:T(8,128)(2,1)} %copy-done.20, bf16[2,384,128]{2,1,0:T(8,128)(2,1)} %copy-done.21, ...), custom_call_target="tpu_custom_call" | custom-call | flops 2415919104 | bytes 3145728 | tf_op jit(solution)/shard_map/attend/pallas_call | solution.py:260
  144.1 2.1 collective-permute-start.16
  146.3 6.2 %all-to-all-start.1 = ((bf16[4,384,128]{2,1,0:T(8,128)(2,1)}), bf16[4,384,128]{2,1,0:T(8,128)(2,1)S(1)}, u32[]{:S(2)}, u32[]{:S(2)}) async-start(bf16[4,384,128]{2,1,0:T(8,128)(2,1)} %attend.4), calls=%async_computation.1 | async-start | bytes 786432 | tf_op jit(solution)/shard_map/all_to_all | solution.py:401
  152.5 0.5 broadcast_maximum_fusion.place_ref
  153.0 0.9 copy-done.13
  153.9 8.7 %attend.5 = (bf16[1,384,128]{2,1,0:T(8,128)(2,1)}, bf16[1,384,128]{2,1,0:T(8,128)(2,1)}, bf16[1,384,128]{2,1,0:T(8,128)(2,1)}, bf16[1,384,128]{2,1,0:T(8,128)(2,1)}) custom-call(s32[3]{0:T(128)} %broadcast_maximum_fusion.place_ref, bf16[2,384,128]{2,1,0:T(8,128)(2,1)} %get-tuple-element.94.refs_0_, bf16[2,384,128]{2,1,0:T(8,128)(2,1)} %copy-done.15, ...), custom_call_target="tpu_custom_call" | custom-call | flops 2415919104 | bytes 3145728 | tf_op jit(solution)/shard_map/attend/pallas_call | solution.py:260
  162.6 2.0 collective-permute-start.18
  164.6 2.4 %collective-permute-start.19 = (bf16[1,384,128]{2,1,0:T(8,128)(2,1)}, bf16[1,384,128]{2,1,0:T(8,128)(2,1)S(1)}, u32[]{:S(2)}, u32[]{:S(2)}) collective-permute-start(bf16[1,384,128]{2,1,0:T(8,128)(2,1)} %get-tuple-element.102), channel_id=1, source_target_pairs={{0,16},{2,18},{4,20},{6,22},{8,24},{10,26},{12,28},{14,30},{16,0},... | collective-permute-start | bytes 294920 | tf_op jit(solution)/shard_map/ppermute | solution.py:28
  167.1 0.9 constant_dynamic-update-slice_fusion.11
  168.0 3.5 %collective-permute-done.19 = bf16[1,384,128]{2,1,0:T(8,128)(2,1)S(1)} collective-permute-done((bf16[1,384,128]{2,1,0:T(8,128)(2,1)}, bf16[1,384,128]{2,1,0:T(8,128)(2,1)S(1)}, u32[]{:S(2)}, u32[]{:S(2)}) %collective-permute-start.19) | collective-permute-done | bytes 98336 | tf_op jit(solution)/shard_map/ppermute | solution.py:28
  171.5 3.1 %collective-permute-done.20 = bf16[1,384,128]{2,1,0:T(8,128)(2,1)S(1)} collective-permute-done((bf16[1,384,128]{2,1,0:T(8,128)(2,1)}, bf16[1,384,128]{2,1,0:T(8,128)(2,1)S(1)}, u32[]{:S(2)}, u32[]{:S(2)}) %collective-permute-start.20) | collective-permute-done | bytes 98336 | tf_op jit(solution)/shard_map/ppermute | solution.py:28
  174.7 0.7 copy-done.2
  175.4 0.7 copy-done.1
  176.2 7.0 %finish.2 = bf16[384,1536]{1,0:T(8,128)(2,1)} custom-call(s32[3]{0:T(128)} %pad_add_fusion.place_ref, bf16[4,384,128]{2,1,0:T(8,128)(2,1)} %copy-done, bf16[4,384,128]{2,1,0:T(8,128)(2,1)} %copy-done.1, bf16[4,384,128]{2,1,0:T(8,128)(2,1)} %copy-done.2, bf16[1536,3072]{1,0:T(8,128)(2,1)} %refs_3_.5), custom_call_target="tpu_custom_call" | custom-call | flops 1811939328 | bytes 7077888 | tf_op jit(solution)/shard_map/finish/pallas_call | solution.py:323
  183.2 1.5 collective-permute-start.21
  184.7 7.3 %finish.3.mine_ref = f32[384,1536]{1,0:T(8,128)} custom-call(s32[3]{0:T(128)} %pad_add_fusion.place_ref, bf16[4,384,128]{2,1,0:T(8,128)(2,1)} %copy-done, bf16[4,384,128]{2,1,0:T(8,128)(2,1)} %copy-done.1, bf16[4,384,128]{2,1,0:T(8,128)(2,1)} %copy-done.2, bf16[1536,3072]{1,0:T(8,128)(2,1)} %refs_3_.5), custom_call_target="tpu_custom_call" | custom-call | flops 1811939328 | bytes 7077888 | tf_op jit(solution)/shard_map/finish/pallas_call | solution.py:323
  192.0 19.5 %collective-permute-done.21.refs_0_ = bf16[384,1536]{1,0:T(8,128)(2,1)S(1)} collective-permute-done((bf16[384,1536]{1,0:T(8,128)(2,1)}, bf16[384,1536]{1,0:T(8,128)(2,1)S(1)}, u32[]{:S(2)}, u32[]{:S(2)}) %collective-permute-start.21) | collective-permute-done | bytes 1179680 | tf_op jit(solution)/shard_map/ppermute | solution.py:28
  211.5 1.0 copy-done.3
  212.6 4.6 %close.1 = bf16[384,1536]{1,0:T(8,128)(2,1)} custom-call(bf16[384,384]{1,0:T(8,128)(2,1)} %get-tuple-element.55.back_ref, f32[384,1536]{1,0:T(8,128)} %finish.3.mine_ref, bf16[384,1536]{1,0:T(8,128)(2,1)} %copy-done.3), custom_call_target="tpu_custom_call" | custom-call | flops 452984832 | bytes 5898240 | tf_op jit(solution)/shard_map/close/pallas_call | solution.py:353
  (83 shorter events, 1.2 us)
Async XLA Ops:
  6.5 96.8 %all-gather.2.cloned.1.call-start = ((), (), s32[]{:S(2)}) async-start(), calls=%async_computation.2 | async-start | bytes 3932160 | tf_op jit(solution)/shard_map/all_gather | solution.py:383
  20.5 15.9 %collective-permute-start = (bf16[1,384,384]{2,1,0:T(8,128)(2,1)}, bf16[1,384,384]{2,1,0:T(8,128)(2,1)S(1)}, u32[]{:S(2)}, u32[]{:S(2)}) collective-permute-start(bf16[1,384,384]{2,1,0:T(8,128)(2,1)} %get-tuple-element.56), channel_id=1, source_target_pairs={{0,8},{2,10},{4,12},{6,14},{8,0},{10,2},{12,4},{14,6},{16,24},{18,... | collective-permute-start | bytes 884744 | tf_op jit(solution)/shard_map/ppermute | solution.py:28
  23.6 26.1 %collective-permute-start.1 = (bf16[1,384,384]{2,1,0:T(8,128)(2,1)}, bf16[1,384,384]{2,1,0:T(8,128)(2,1)S(1)}, u32[]{:S(2)}, u32[]{:S(2)}) collective-permute-start(bf16[1,384,384]{2,1,0:T(8,128)(2,1)} %get-tuple-element.57), channel_id=1, source_target_pairs={{0,16},{2,18},{4,20},{6,22},{8,24},{10,26},{12,28},{14,30},{16,0},... | collective-permute-start | bytes 884744 | tf_op jit(solution)/shard_map/ppermute | solution.py:28
  26.2 23.5 %collective-permute-start.2 = (bf16[1,384,384]{2,1,0:T(8,128)(2,1)}, bf16[1,384,384]{2,1,0:T(8,128)(2,1)S(1)}, u32[]{:S(2)}, u32[]{:S(2)}) collective-permute-start(bf16[1,384,384]{2,1,0:T(8,128)(2,1)} %get-tuple-element.58), channel_id=1, source_target_pairs={{0,24},{2,26},{4,28},{6,30},{8,16},{10,18},{12,20},{14,22},{16,8},... | collective-permute-start | bytes 884744 | tf_op jit(solution)/shard_map/ppermute | solution.py:28
  36.4 13.4 %copy-start.7 = (bf16[1,384,384]{2,1,0:T(8,128)(2,1)}, bf16[1,384,384]{2,1,0:T(8,128)(2,1)S(1)}, u32[]{:S(2)}) copy-start(bf16[1,384,384]{2,1,0:T(8,128)(2,1)S(1)} %collective-permute-done.refs_1_) | copy-start | bytes 884740
  36.4 13.4 %copy-start.6 = (bf16[1,384,384]{2,1,0:T(8,128)(2,1)S(1)}, bf16[1,384,384]{2,1,0:T(8,128)(2,1)}, u32[]{:S(2)}) copy-start(bf16[1,384,384]{2,1,0:T(8,128)(2,1)} %get-tuple-element.87.refs_0_) | copy-start | bytes 884740
  49.7 1.2 copy-start.24
  49.7 4.3 %copy-start.23 = (bf16[1,384,256]{2,1,0:T(8,128)(2,1)S(1)}, bf16[1,384,256]{2,1,0:T(8,128)(2,1)}, u32[]{:S(2)}) copy-start(bf16[1,384,256]{2,1,0:T(8,128)(2,1)} %get-tuple-element.73) | copy-start | bytes 589828
  49.7 5.4 %copy-start.22 = (bf16[1,384,256]{2,1,0:T(8,128)(2,1)S(1)}, bf16[1,384,256]{2,1,0:T(8,128)(2,1)}, u32[]{:S(2)}) copy-start(bf16[1,384,256]{2,1,0:T(8,128)(2,1)} %get-tuple-element.74) | copy-start | bytes 589828
  49.7 6.9 %copy-start.5 = (bf16[1,384,256]{2,1,0:T(8,128)(2,1)S(1)}, bf16[1,384,256]{2,1,0:T(8,128)(2,1)}, u32[]{:S(2)}) copy-start(bf16[1,384,256]{2,1,0:T(8,128)(2,1)} %get-tuple-element.72) | copy-start | bytes 589828
  49.7 10.6 %copy-start.8 = (bf16[1,384,384]{2,1,0:T(8,128)(2,1)}, bf16[1,384,384]{2,1,0:T(8,128)(2,1)S(1)}, u32[]{:S(2)}) copy-start(bf16[1,384,384]{2,1,0:T(8,128)(2,1)S(1)} %collective-permute-done.1.refs_2_) | copy-start | bytes 884740
  49.7 10.6 %copy-start.9 = (bf16[1,384,384]{2,1,0:T(8,128)(2,1)}, bf16[1,384,384]{2,1,0:T(8,128)(2,1)S(1)}, u32[]{:S(2)}) copy-start(bf16[1,384,384]{2,1,0:T(8,128)(2,1)S(1)} %collective-permute-done.2.refs_3_) | copy-start | bytes 884740
  49.8 22.6 %copy-start.17 = (bf16[1,384,256]{2,1,0:T(8,128)(2,1)S(1)}, bf16[1,384,256]{2,1,0:T(8,128)(2,1)}, u32[]{:S(2)}) copy-start(bf16[1,384,256]{2,1,0:T(8,128)(2,1)} %get-tuple-element.69) | copy-start | bytes 589828
  49.8 25.2 %copy-start.16 = (bf16[1,384,256]{2,1,0:T(8,128)(2,1)S(1)}, bf16[1,384,256]{2,1,0:T(8,128)(2,1)}, u32[]{:S(2)}) copy-start(bf16[1,384,256]{2,1,0:T(8,128)(2,1)} %get-tuple-element.70) | copy-start | bytes 589828
  49.8 26.2 %copy-start.14 = (bf16[1,384,256]{2,1,0:T(8,128)(2,1)S(1)}, bf16[1,384,256]{2,1,0:T(8,128)(2,1)}, u32[]{:S(2)}) copy-start(bf16[1,384,256]{2,1,0:T(8,128)(2,1)} %get-tuple-element.71) | copy-start | bytes 589828
  50.9 9.4 %collective-permute-start.3 = (bf16[1,384,256]{2,1,0:T(8,128)(2,1)S(1)}, bf16[1,384,256]{2,1,0:T(8,128)(2,1)S(1)}, u32[]{:S(2)}, u32[]{:S(2)}) collective-permute-start(bf16[1,384,256]{2,1,0:T(8,128)(2,1)S(1)} %copy-done.24), channel_id=1, source_target_pairs={{0,8},{2,10},{4,12},{6,14},{8,0},{10,2},{12,4},{14,6},{16,24},{18,... | collective-permute-start | bytes 589832 | tf_op jit(solution)/shard_map/ppermute | solution.py:28
  54.0 16.7 %collective-permute-start.7 = (bf16[1,384,256]{2,1,0:T(8,128)(2,1)S(1)}, bf16[1,384,256]{2,1,0:T(8,128)(2,1)S(1)}, u32[]{:S(2)}, u32[]{:S(2)}) collective-permute-start(bf16[1,384,256]{2,1,0:T(8,128)(2,1)S(1)} %copy-done.23), channel_id=1, source_target_pairs={{0,16},{2,18},{4,20},{6,22},{8,24},{10,26},{12,28},{14,30},{16,0},... | collective-permute-start | bytes 589832 | tf_op jit(solution)/shard_map/ppermute | solution.py:28
  55.1 15.6 %collective-permute-start.8 = (bf16[1,384,256]{2,1,0:T(8,128)(2,1)S(1)}, bf16[1,384,256]{2,1,0:T(8,128)(2,1)S(1)}, u32[]{:S(2)}, u32[]{:S(2)}) collective-permute-start(bf16[1,384,256]{2,1,0:T(8,128)(2,1)S(1)} %copy-done.22), channel_id=1, source_target_pairs={{0,24},{2,26},{4,28},{6,30},{8,16},{10,18},{12,20},{14,22},{16,8},... | collective-permute-start | bytes 589832 | tf_op jit(solution)/shard_map/ppermute | solution.py:28
  70.7 41.7 %copy-start.10 = (bf16[4,384,256]{2,1,0:T(8,128)(2,1)}, bf16[4,384,256]{2,1,0:T(8,128)(2,1)S(1)}, u32[]{:S(2)}) copy-start(bf16[4,384,256]{2,1,0:T(8,128)(2,1)S(1)} %constant_dynamic-update-slice_fusion.refs_4_) | copy-start | bytes 2359300
  70.7 25.9 %collective-permute-start.9 = (bf16[4,384,256]{2,1,0:T(8,128)(2,1)S(1)}, bf16[4,384,256]{2,1,0:T(8,128)(2,1)}, u32[]{:S(2)}, u32[]{:S(2)}) collective-permute-start(bf16[4,384,256]{2,1,0:T(8,128)(2,1)S(1)} %constant_dynamic-update-slice_fusion.refs_4_), channel_id=1, source_target_pairs={{0,4},{2,6},{4,0},{6,2},{8,12},{10,14},{12,8},{14,10},{16,20},{18,... | collective-permute-start | bytes 2359304 | tf_op jit(solution)/shard_map/ppermute | solution.py:28
  72.3 14.7 %collective-permute-start.4 = (bf16[1,384,256]{2,1,0:T(8,128)(2,1)S(1)}, bf16[1,384,256]{2,1,0:T(8,128)(2,1)S(1)}, u32[]{:S(2)}, u32[]{:S(2)}) collective-permute-start(bf16[1,384,256]{2,1,0:T(8,128)(2,1)S(1)} %copy-done.17), channel_id=1, source_target_pairs={{0,8},{2,10},{4,12},{6,14},{8,0},{10,2},{12,4},{14,6},{16,24},{18,... | collective-permute-start | bytes 589832 | tf_op jit(solution)/shard_map/ppermute | solution.py:28
  75.0 15.8 %collective-permute-start.5 = (bf16[1,384,256]{2,1,0:T(8,128)(2,1)S(1)}, bf16[1,384,256]{2,1,0:T(8,128)(2,1)S(1)}, u32[]{:S(2)}, u32[]{:S(2)}) collective-permute-start(bf16[1,384,256]{2,1,0:T(8,128)(2,1)S(1)} %copy-done.16), channel_id=1, source_target_pairs={{0,16},{2,18},{4,20},{6,22},{8,24},{10,26},{12,28},{14,30},{16,0},... | collective-permute-start | bytes 589832 | tf_op jit(solution)/shard_map/ppermute | solution.py:28
  76.0 14.7 %collective-permute-start.6 = (bf16[1,384,256]{2,1,0:T(8,128)(2,1)S(1)}, bf16[1,384,256]{2,1,0:T(8,128)(2,1)S(1)}, u32[]{:S(2)}, u32[]{:S(2)}) collective-permute-start(bf16[1,384,256]{2,1,0:T(8,128)(2,1)S(1)} %copy-done.14), channel_id=1, source_target_pairs={{0,24},{2,26},{4,28},{6,30},{8,16},{10,18},{12,20},{14,22},{16,8},... | collective-permute-start | bytes 589832 | tf_op jit(solution)/shard_map/ppermute | solution.py:28
  78.1 18.6 %copy-start.4 = (bf16[1,384,256]{2,1,0:T(8,128)(2,1)S(1)}, bf16[1,384,256]{2,1,0:T(8,128)(2,1)}, u32[]{:S(2)}) copy-start(bf16[1,384,256]{2,1,0:T(8,128)(2,1)} %get-tuple-element.77) | copy-start | bytes 589828
  78.1 24.6 %copy-start.12 = (s32[3]{0:T(128)S(1)}, s32[3]{0:T(128)}, u32[]{:S(2)}) copy-start(s32[3]{0:T(128)} %pad_add_fusion.place_ref) | copy-start | bytes 40
  96.7 47.4 %copy-start.11 = (bf16[4,384,256]{2,1,0:T(8,128)(2,1)}, bf16[4,384,256]{2,1,0:T(8,128)(2,1)S(1)}, u32[]{:S(2)}) copy-start(bf16[4,384,256]{2,1,0:T(8,128)(2,1)S(1)} %constant_dynamic-update-slice_fusion.4.refs_4_) | copy-start | bytes 2359300
  96.8 6.0 %collective-permute-start.10 = (bf16[2,384,128]{2,1,0:T(8,128)(2,1)}, bf16[2,384,128]{2,1,0:T(8,128)(2,1)S(1)}, u32[]{:S(2)}, u32[]{:S(2)}) collective-permute-start(bf16[2,384,128]{2,1,0:T(8,128)(2,1)} %get-tuple-element.84), channel_id=1, source_target_pairs={{0,8},{2,10},{4,12},{6,14},{8,0},{10,2},{12,4},{14,6},{16,24},{18,... | collective-permute-start | bytes 589832 | tf_op jit(solution)/shard_map/ppermute | solution.py:28
  98.3 36.4 %collective-permute-start.13 = (bf16[4,384,256]{2,1,0:T(8,128)(2,1)S(1)}, bf16[4,384,256]{2,1,0:T(8,128)(2,1)}, u32[]{:S(2)}, u32[]{:S(2)}) collective-permute-start(bf16[4,384,256]{2,1,0:T(8,128)(2,1)S(1)} %constant_dynamic-update-slice_fusion.4.refs_4_), channel_id=1, source_target_pairs={{0,4},{2,6},{4,0},{6,2},{8,12},{10,14},{12,8},{14,10},{16,20},{18,... | collective-permute-start | bytes 2359304 | tf_op jit(solution)/shard_map/ppermute | solution.py:28
  102.7 9.7 %copy-start.15 = (bf16[2,384,128]{2,1,0:T(8,128)(2,1)}, bf16[2,384,128]{2,1,0:T(8,128)(2,1)S(1)}, u32[]{:S(2)}) copy-start(bf16[2,384,128]{2,1,0:T(8,128)(2,1)S(1)} %collective-permute-done.10.refs_1_) | copy-start | bytes 589828
  103.3 9.6 %copy-start.19 = (bf16[2,384,128]{2,1,0:T(8,128)(2,1)S(1)}, bf16[2,384,128]{2,1,0:T(8,128)(2,1)}, u32[]{:S(2)}) copy-start(bf16[2,384,128]{2,1,0:T(8,128)(2,1)} %get-tuple-element.91) | copy-start | bytes 589828
  103.3 12.9 %copy-start.18 = (bf16[2,384,128]{2,1,0:T(8,128)(2,1)S(1)}, bf16[2,384,128]{2,1,0:T(8,128)(2,1)}, u32[]{:S(2)}) copy-start(bf16[2,384,128]{2,1,0:T(8,128)(2,1)} %get-tuple-element.92) | copy-start | bytes 589828
  112.5 22.8 %collective-permute-start.14 = (bf16[4,384,256]{2,1,0:T(8,128)(2,1)S(1)}, bf16[4,384,256]{2,1,0:T(8,128)(2,1)}, u32[]{:S(2)}, u32[]{:S(2)}) collective-permute-start(bf16[4,384,256]{2,1,0:T(8,128)(2,1)S(1)} %constant_dynamic-update-slice_fusion.refs_4_), channel_id=1, source_target_pairs={{0,2},{2,0},{4,6},{6,4},{8,10},{10,8},{12,14},{14,12},{16,18},{18,... | collective-permute-start | bytes 2359304 | tf_op jit(solution)/shard_map/ppermute | solution.py:28
  112.7 22.6 %collective-permute-start.15 = (bf16[4,384,256]{2,1,0:T(8,128)(2,1)}, bf16[4,384,256]{2,1,0:T(8,128)(2,1)}, u32[]{:S(2)}, u32[]{:S(2)}) collective-permute-start(bf16[4,384,256]{2,1,0:T(8,128)(2,1)} %collective-permute-done.9.refs_6_), channel_id=1, source_target_pairs={{0,2},{2,0},{4,6},{6,4},{8,10},{10,8},{12,14},{14,12},{16,18},{18,... | collective-permute-start | bytes 2359304 | tf_op jit(solution)/shard_map/ppermute | solution.py:28
  113.0 21.7 %collective-permute-start.11 = (bf16[2,384,128]{2,1,0:T(8,128)(2,1)S(1)}, bf16[2,384,128]{2,1,0:T(8,128)(2,1)S(1)}, u32[]{:S(2)}, u32[]{:S(2)}) collective-permute-start(bf16[2,384,128]{2,1,0:T(8,128)(2,1)S(1)} %copy-done.19), channel_id=1, source_target_pairs={{0,16},{2,18},{4,20},{6,22},{8,24},{10,26},{12,28},{14,30},{16,0},... | collective-permute-start | bytes 589832 | tf_op jit(solution)/shard_map/ppermute | solution.py:28
  116.3 18.4 %collective-permute-start.12 = (bf16[2,384,128]{2,1,0:T(8,128)(2,1)S(1)}, bf16[2,384,128]{2,1,0:T(8,128)(2,1)S(1)}, u32[]{:S(2)}, u32[]{:S(2)}) collective-permute-start(bf16[2,384,128]{2,1,0:T(8,128)(2,1)S(1)} %copy-done.18), channel_id=1, source_target_pairs={{0,24},{2,26},{4,28},{6,30},{8,16},{10,18},{12,20},{14,22},{16,8},... | collective-permute-start | bytes 589832 | tf_op jit(solution)/shard_map/ppermute | solution.py:28
  117.5 28.8 %all-to-all-start = ((bf16[4,384,128]{2,1,0:T(8,128)(2,1)}), bf16[4,384,128]{2,1,0:T(8,128)(2,1)S(1)}, u32[]{:S(2)}, u32[]{:S(2)}) async-start(bf16[4,384,128]{2,1,0:T(8,128)(2,1)} %attend.3), calls=%async_computation | async-start | bytes 786432 | tf_op jit(solution)/shard_map/all_to_all | solution.py:401
  134.7 0.7 copy-start.21
  144.1 8.9 %collective-permute-start.16 = (bf16[4,384,256]{2,1,0:T(8,128)(2,1)S(1)}, bf16[4,384,256]{2,1,0:T(8,128)(2,1)S(1)}, u32[]{:S(2)}, u32[]{:S(2)}) collective-permute-start(bf16[4,384,256]{2,1,0:T(8,128)(2,1)S(1)} %constant_dynamic-update-slice_fusion.4.refs_4_), channel_id=1, source_target_pairs={{0,2},{2,0},{4,6},{6,4},{8,10},{10,8},{12,14},{14,12},{16,18},{18,... | collective-permute-start | bytes 2359304 | tf_op jit(solution)/shard_map/ppermute | solution.py:28
  146.2 6.8 %collective-permute-start.17 = (bf16[4,384,256]{2,1,0:T(8,128)(2,1)}, bf16[4,384,256]{2,1,0:T(8,128)(2,1)}, u32[]{:S(2)}, u32[]{:S(2)}) collective-permute-start(bf16[4,384,256]{2,1,0:T(8,128)(2,1)} %collective-permute-done.13.refs_6_), channel_id=1, source_target_pairs={{0,2},{2,0},{4,6},{6,4},{8,10},{10,8},{12,14},{14,12},{16,18},{18,... | collective-permute-start | bytes 2359304 | tf_op jit(solution)/shard_map/ppermute | solution.py:28
  146.3 16.3 %copy-start = (bf16[4,384,128]{2,1,0:T(8,128)(2,1)}, bf16[4,384,128]{2,1,0:T(8,128)(2,1)S(1)}, u32[]{:S(2)}) copy-start(bf16[4,384,128]{2,1,0:T(8,128)(2,1)S(1)} %all-to-all-done.refs_0_) | copy-start | bytes 1179652
  146.3 28.4 %all-to-all-start.1 = ((bf16[4,384,128]{2,1,0:T(8,128)(2,1)}), bf16[4,384,128]{2,1,0:T(8,128)(2,1)S(1)}, u32[]{:S(2)}, u32[]{:S(2)}) async-start(bf16[4,384,128]{2,1,0:T(8,128)(2,1)} %attend.4), calls=%async_computation.1 | async-start | bytes 786432 | tf_op jit(solution)/shard_map/all_to_all | solution.py:401
  153.0 0.9 copy-start.13
  162.6 5.4 %collective-permute-start.18 = (bf16[1,384,128]{2,1,0:T(8,128)(2,1)}, bf16[1,384,128]{2,1,0:T(8,128)(2,1)S(1)}, u32[]{:S(2)}, u32[]{:S(2)}) collective-permute-start(bf16[1,384,128]{2,1,0:T(8,128)(2,1)} %get-tuple-element.101), channel_id=1, source_target_pairs={{0,8},{2,10},{4,12},{6,14},{8,0},{10,2},{12,4},{14,6},{16,24},{18,... | collective-permute-start | bytes 294920 | tf_op jit(solution)/shard_map/ppermute | solution.py:28
  164.6 6.9 %collective-permute-start.19 = (bf16[1,384,128]{2,1,0:T(8,128)(2,1)}, bf16[1,384,128]{2,1,0:T(8,128)(2,1)S(1)}, u32[]{:S(2)}, u32[]{:S(2)}) collective-permute-start(bf16[1,384,128]{2,1,0:T(8,128)(2,1)} %get-tuple-element.102), channel_id=1, source_target_pairs={{0,16},{2,18},{4,20},{6,22},{8,24},{10,26},{12,28},{14,30},{16,0},... | collective-permute-start | bytes 294920 | tf_op jit(solution)/shard_map/ppermute | solution.py:28
  167.0 7.7 %collective-permute-start.20 = (bf16[1,384,128]{2,1,0:T(8,128)(2,1)}, bf16[1,384,128]{2,1,0:T(8,128)(2,1)S(1)}, u32[]{:S(2)}, u32[]{:S(2)}) collective-permute-start(bf16[1,384,128]{2,1,0:T(8,128)(2,1)} %get-tuple-element.103), channel_id=1, source_target_pairs={{0,24},{2,26},{4,28},{6,30},{8,16},{10,18},{12,20},{14,22},{16,8},... | collective-permute-start | bytes 294920 | tf_op jit(solution)/shard_map/ppermute | solution.py:28
  174.7 0.7 copy-start.2
  183.2 28.3 %collective-permute-start.21 = (bf16[384,1536]{1,0:T(8,128)(2,1)}, bf16[384,1536]{1,0:T(8,128)(2,1)S(1)}, u32[]{:S(2)}, u32[]{:S(2)}) collective-permute-start(bf16[384,1536]{1,0:T(8,128)(2,1)} %finish.2), channel_id=1, source_target_pairs={{0,1},{1,0},{2,3},{3,2},{4,5},{5,4},{6,7},{7,6},{8,9},{9,8},{10,11... | collective-permute-start | bytes 3538952 | tf_op jit(solution)/shard_map/ppermute | solution.py:28
  211.5 1.0 copy-start.3
  (2 other events, 1.4 us)
Sparse Core Ops, SparseCore 0:
  51.0 39.7 all-gather.1

commit v11 on v8

--- a/solution.py
+++ b/solution.py
@@ -57,7 +57,7 @@
         normed_ref[low : low + rows, :] = layer_norm(part, gain).astype(bf16)
 
 
-def project_body(place_ref, *refs, steps, groups, first):
+def project_body(place_ref, *refs, steps, groups, first, joined):
     refs = list(refs)
     result_ref = refs.pop()
     weight_ref, gain_ref = refs[:2]
@@ -95,12 +95,15 @@
                 packed = jnp.where(line < count_ref[0, 0], packed, dead_mark)
             result_ref[...] = packed.astype(bf16)
             for k in range(groups):
-                start = pl.multiple_of(lax.bitwise_xor(plane, k) * size, size)
-                found = result_ref[:, pl.ds(start, size)]
-                outs[target * groups + k][row, :, low : low + size] = found
-
-
-def project(place, prepared, weights, gains, sets, groups, first=None):
+                if joined:
+                    outs[k // groups][k, row] = result_ref[:, k * size : (k + 1) * size]
+                else:
+                    start = pl.multiple_of(lax.bitwise_xor(plane, k) * size, size)
+                    found = result_ref[:, pl.ds(start, size)]
+                    outs[target * groups + k][row, :, low : low + size] = found
+
+
+def project(place, prepared, weights, gains, sets, groups, first=None, joined=False):
     size = gains.shape[2]
     width = weights.shape[1]
     columns = groups * size
@@ -127,7 +130,11 @@
     shapes = [
         (len(which), rows, len(kinds) * size) for kinds, which in sets for _ in range(groups)
     ]
-    out_specs = [pl.BlockSpec(shape, lambda t, place: (0, 0, 0)) for shape in shapes]
+    if joined:
+        shapes = [(groups, len(sets[0][1]), rows, size)]
+    out_specs = [
+        pl.BlockSpec(shape, lambda t, place, zeros=(0,) * len(shape): zeros) for shape in shapes
+    ]
     out_shape = [jax.ShapeDtypeStruct(shape, bf16) for shape in shapes]
     if first:
         in_specs = [pl.BlockSpec((rows,), line), whole, pl.BlockSpec((width,), line)]
@@ -141,7 +148,9 @@
     else:
         in_specs = [smem, whole, square]
     found = pl.pallas_call(
-        functools.partial(project_body, steps=steps, groups=groups, first=first is not None),
+        functools.partial(
+            project_body, steps=steps, groups=groups, first=first is not None, joined=joined
+        ),
         grid_spec=pltpu.PrefetchScalarGridSpec(
             num_scalar_prefetch=1,
             grid=(len(steps),),
@@ -161,13 +170,15 @@
         ),
         name="project",
     )(place, weights, gains, *(first or prepared))
+    if joined:
+        return found[0], []
     blocks = [found[i * groups : (i + 1) * groups] for i in range(len(sets))]
     return blocks, found[len(sets) * groups :]
 
 
-def attend_body(place_ref, *refs, groups, ordered, low_lane, key_room, query_rows, key_cols):
+def attend_body(place_ref, *refs, groups, asked, joined, ordered, low_lane, key_room, query_rows, key_cols):
     outs = 1 if ordered else groups
-    query_refs, sources, out_refs = refs[:groups], refs[groups : -4 - outs], refs[-4 - outs : -4]
+    query_refs, sources, out_refs = refs[:asked], refs[asked : -4 - outs], refs[-4 - outs : -4]
     keys, values, queries, results = refs[-4:]
     rows, size = out_refs[0].shape[1:]
     plane = place_ref[0]
@@ -216,7 +227,11 @@
             def _():
                 here = pl.ds(pl.multiple_of(start + part * piece, 16), piece)
                 there = pl.ds(part * piece, piece)
-                queries[here, :] = query_refs[k][0, there, low_lane : low_lane + size]
+                if joined:
+                    found = query_refs[0][lax.bitwise_xor(plane, k), 0, there, :]
+                else:
+                    found = query_refs[k][0, there, low_lane : low_lane + size]
+                queries[here, :] = found
 
         start = pl.multiple_of(start + align(mine[k]), 16)
 
@@ -246,19 +261,25 @@
 
 
 def attend(place, queries, which, low_lane, keyvals, shards, ordered):
-    groups = len(queries)
+    groups = keyvals[0].shape[0]
+    joined = queries[0].ndim == 4
     rows = keyvals[0].shape[1]
     size = keyvals[0].shape[2] // 2
     running = shards * rows // 2
     key_room = -(-(running + 16 * shards) // 256) * 256
     query_rows = 256
     query_room = -(-groups * rows // query_rows) * query_rows + rows
-    query_block = (1,) + queries[0].shape[1:]
+    if joined:
+        query_block = pl.BlockSpec((groups, 1, rows, size), lambda i, place: (0, which, 0, 0))
+    else:
+        query_block = pl.BlockSpec((1,) + queries[0].shape[1:], lambda i, place: (which, 0, 0))
     outs, wide = (1, groups) if ordered else (groups, 1)
     return pl.pallas_call(
         functools.partial(
             attend_body,
             groups=groups,
+            asked=len(queries),
+            joined=joined,
             ordered=ordered,
             low_lane=low_lane,
             key_room=key_room,
@@ -268,7 +289,7 @@
         grid_spec=pltpu.PrefetchScalarGridSpec(
             num_scalar_prefetch=1,
             grid=(1,),
-            in_specs=[pl.BlockSpec(query_block, lambda i, place: (which, 0, 0))] * groups
+            in_specs=[query_block] * len(queries)
             + [pl.BlockSpec(keyvals[0].shape, lambda i, place: (0, 0, 0))] * len(keyvals),
             out_specs=[pl.BlockSpec((wide, rows, size), lambda i, place: (0, 0, 0))] * outs,
             scratch_shapes=[
@@ -335,7 +356,7 @@
 
 def close_body(back_ref, mine_ref, *refs):
     out_ref = refs[-1]
-    total = mine_ref[...]
+    total = mine_ref[...].astype(f32)
     for ref in refs[:-1]:
         total += ref[...].astype(f32)
     rounded = total.astype(bf16)
@@ -424,36 +445,35 @@
         stacks.append(stack(arrived[1]))
         ready = later(count, hop, stacks[1])
         sets = [((0,), tuple(rest))]
-        (made,), _ = project(place, (ready, normed, chosen), weights, gains, sets, groups)
-        gate = made[0]
-        stacks += [stack(blocks) for blocks in arrived[2:]]
-        keyvals = everywhere(stacks[0], gate)
-        asked = send(made, stacks[-1], *keyvals)
+        made, _ = project(
+            place, (ready, normed, chosen), weights, gains, sets, groups, joined=True
+        )
+        gate = made
+        stacks += [stack(list(chain(tuple(blocks), made))) for blocks in arrived[2:]]
+        asked = [send_back(made)]
         hops = [flip(stacks[-1], "seq", ring // 2)] if ring > 1 else []
     else:
-        stacks = [stack(arrived[0])]
-        keyvals = everywhere(stacks[0], None)
+        gate, stacks = None, [stack(arrived[0])]
 
     attended, returned = [], []
     query, low_lane = arrived[0], 2 * size
     for chunk in range(chunks):
         final = chunk == chunks - 1
-        if chunk:
-            keyvals = everywhere(stacks[chunk], None)
+        keyvals = everywhere(stacks[chunk], gate)
         before = [stacks[-1]] + attended[-1:] + (hops if chunk else []) + (returned[:1] if final else [])
-        ready = later(place, *query[1:], *before)
+        ready = later(place, *query[1 if chunk == 0 else 0 :], *before)
         row = max(chunk - 1, 0)
         found = attend(ready, query, row, low_lane, keyvals, shards, not final)
         attended.append(found[0])
         returned.append(jnp.concatenate(swap(found)) if final else send_back(found[0]))
         if not final:
-            query, low_lane = asked, 0
+            query, low_lane, gate = asked, 0, None
     ordered = (True,) * (chunks - 1) + (False,)
     final = functools.partial(finish, place, returned, ordered, w_out)
     sent = [final(mask, bf16) for mask in range(1, head_shards)]
     others = [flip(part, "head", mask) for mask, part in enumerate(sent, 1)]
     returned[0] = chain(returned[0], *sent)
-    return close(back, final(0, f32), others)
+    return close(back, final(0, bf16), others)
 
 
 def solution(mesh):

time: 203 us -> 190 us (0.936); the launches traced: 203 us -> 186 us
  waiting for transfers between devices: 75.1 us -> 44.2 us
  starting transfers between devices: 39.8 us -> 48.3 us
  Pallas kernels: 80.7 us -> 83.9 us
    ppermute x25 -> x22, waiting for transfers between devices: 72.9 us -> 44.2 us  [flip(): return lax.ppermute(values, axis, [(i, i ^ mask) for i in range(size)])]
    all_to_all x2 -> x3, starting transfers between devices: 6.92 us -> 21.3 us  [send_back(): lax.all_to_all(blocks, 'seq', split_axis=0, concat_axis=0, axis_index_gro...]
    ppermute x25 -> x22, starting transfers between devices: 32.9 us -> 27 us  [flip(): return lax.ppermute(values, axis, [(i, i ^ mask) for i in range(size)])]
    pallas_call x3, Pallas kernels: 26.3 us -> 29.9 us  [attend(): pl.pallas_call(functools.partial(attend_body, groups=groups, asked=len(qu...]
    all_to_all x2 -> x3, waiting for transfers between devices: 2.27 us -> 0.01 us  [send_back(): lax.all_to_all(blocks, 'seq', split_axis=0, concat_axis=0, axis_index_gro...]
    unnamed x59 -> x45, local copies, waits for them, and re-layouts: 4.55 us -> 5.69 us
  transfers between devices with their start and end apart: 27 -> 25, of which waited for: 9 -> 8; matrix products, arithmetic and copies ran while one was open for 1% -> 3% of each run, Pallas kernels for 27% -> 32%
where the time goes in v11:
time: 190 us; the launch traced here: 186 us
  Pallas kernels  83.9 us (44%)
  starting transfers between devices  48.3 us (25%)
  waiting for transfers between devices  44.2 us (23%)
  local copies, waits for them, and re-layouts  6.46 us (3%)
  other arithmetic  2.39 us (1%)
    ppermute x22, waiting for transfers between devices, flip(): return lax.ppermute(values, axis, [(i, i ^ mask) for i in range(size)])  44.2 us
    pallas_call x3, Pallas kernels, project(): pl.pallas_call(functools.partial(project_body, steps=steps, groups=groups...  35.5 us
    pallas_call x3, Pallas kernels, attend(): pl.pallas_call(functools.partial(attend_body, groups=groups, asked=len(qu...  29.9 us
    ppermute x22, starting transfers between devices, flip(): return lax.ppermute(values, axis, [(i, i ^ mask) for i in range(size)])  27 us
    all_to_all x3, starting transfers between devices, send_back(): lax.all_to_all(blocks, 'seq', split_axis=0, concat_axis=0, axis_index_gro...  21.3 us
    pallas_call x2, Pallas kernels, finish(): pl.pallas_call(functools.partial(finish_body, ordered=ordered), grid_spec...  14.2 us
    unnamed x45, local copies, waits for them, and re-layouts  5.69 us
    pallas_call x1, Pallas kernels, close(): pl.pallas_call(close_body, grid=(parts,), in_specs=[pl.BlockSpec((rows, r...  4.37 us
  transfers between devices with their start and end apart: 25, of which 8 were waited for; matrix products, arithmetic and copies ran while one was open for 3% of the time, Pallas kernels for 32%

profile of v11, /device:TPU:0, one launch (start us, length us, event | category | flops | bytes accessed | tf_op | source)
XLA Modules:
  0.0 186.0 jit_solution(16168265039026038358)
XLA Ops:
  0.0 0.6 pad_add_fusion.place_ref
  0.6 13.4 %project.3 = (bf16[1,384,384]{2,1,0:T(8,128)(2,1)}, bf16[1,384,384]{2,1,0:T(8,128)(2,1)}, bf16[1,384,384]{2,1,0:T(8,128)(2,1)}, bf16[1,384,384]{2,1,0:T(8,128)(2...) custom-call(s32[3]{0:T(128)} %pad_add_fusion.place_ref, ...), custom_call_target="tpu_custom_call" | custom-call | flops 3623878656 | bytes 11796480 | tf_op jit(solution)/shard_map/project/pallas_call | solution.py:150
  14.1 3.1 %collective-permute-start = (bf16[1,384,384]{2,1,0:T(8,128)(2,1)}, bf16[1,384,384]{2,1,0:T(8,128)(2,1)S(1)}, u32[]{:S(2)}, u32[]{:S(2)}) collective-permute-start(bf16[1,384,384]{2,1,0:T(8,128)(2,1)} %get-tuple-element.46), channel_id=1, source_target_pairs={{0,8},{2,10},{4,12},{6,14},{8,0},{10,2},{12,4},{14,6},{16,24},{18,... | collective-permute-start | bytes 884744 | tf_op jit(solution)/shard_map/ppermute | solution.py:28
  17.2 2.6 %collective-permute-start.1 = (bf16[1,384,384]{2,1,0:T(8,128)(2,1)}, bf16[1,384,384]{2,1,0:T(8,128)(2,1)S(1)}, u32[]{:S(2)}, u32[]{:S(2)}) collective-permute-start(bf16[1,384,384]{2,1,0:T(8,128)(2,1)} %get-tuple-element.47), channel_id=1, source_target_pairs={{0,16},{2,18},{4,20},{6,22},{8,24},{10,26},{12,28},{14,30},{16,0},... | collective-permute-start | bytes 884744 | tf_op jit(solution)/shard_map/ppermute | solution.py:28
  19.8 10.2 %collective-permute-done.refs_1_ = bf16[1,384,384]{2,1,0:T(8,128)(2,1)S(1)} collective-permute-done((bf16[1,384,384]{2,1,0:T(8,128)(2,1)}, bf16[1,384,384]{2,1,0:T(8,128)(2,1)S(1)}, u32[]{:S(2)}, u32[]{:S(2)}) %collective-permute-start) | collective-permute-done | bytes 294944 | tf_op jit(solution)/shard_map/ppermute | solution.py:28
  29.9 13.2 %project.4 = (bf16[1,384,256]{2,1,0:T(8,128)(2,1)}, bf16[1,384,256]{2,1,0:T(8,128)(2,1)}, bf16[1,384,256]{2,1,0:T(8,128)(2,1)}, bf16[1,384,256]{2,1,0:T(8,128)(2...) custom-call(s32[3]{0:T(128)} %pad_add_fusion.place_ref, ...), custom_call_target="tpu_custom_call" | custom-call | flops 4831838208 | bytes 14942208 | tf_op jit(solution)/shard_map/project/pallas_call | solution.py:150
  43.3 0.1 pad_maximum_fusion.refs_4_
  43.4 1.8 collective-permute-start.7
  45.2 2.9 %collective-permute-start.3 = (bf16[1,384,256]{2,1,0:T(8,128)(2,1)S(1)}, bf16[1,384,256]{2,1,0:T(8,128)(2,1)S(1)}, u32[]{:S(2)}, u32[]{:S(2)}) collective-permute-start(bf16[1,384,256]{2,1,0:T(8,128)(2,1)S(1)} %copy-done.17), channel_id=1, source_target_pairs={{0,8},{2,10},{4,12},{6,14},{8,0},{10,2},{12,4},{14,6},{16,24},{18,... | collective-permute-start | bytes 589832 | tf_op jit(solution)/shard_map/ppermute | solution.py:28
  48.1 1.1 collective-permute-start.8
  49.2 1.5 collective-permute-start.9
  50.7 0.7 constant_dynamic-update-slice_fusion.3
  51.4 5.3 %collective-permute-done.3 = bf16[1,384,256]{2,1,0:T(8,128)(2,1)S(1)} collective-permute-done((bf16[1,384,256]{2,1,0:T(8,128)(2,1)S(1)}, bf16[1,384,256]{2,1,0:T(8,128)(2,1)S(1)}, u32[]{:S(2)}, u32[]{:S(2)}) %collective-permute-start.3) | collective-permute-done | bytes 196640 | tf_op jit(solution)/shard_map/ppermute | solution.py:28
  56.7 2.6 %collective-permute-start.5 = (bf16[1,384,256]{2,1,0:T(8,128)(2,1)}, bf16[1,384,256]{2,1,0:T(8,128)(2,1)S(1)}, u32[]{:S(2)}, u32[]{:S(2)}) collective-permute-start(bf16[1,384,256]{2,1,0:T(8,128)(2,1)} %get-tuple-element.60), channel_id=1, source_target_pairs={{0,16},{2,18},{4,20},{6,22},{8,24},{10,26},{12,28},{14,30},{16,0},... | collective-permute-start | bytes 589832 | tf_op jit(solution)/shard_map/ppermute | solution.py:28
  59.3 0.7 constant_dynamic-update-slice_fusion.2
  59.9 5.4 %collective-permute-done.8 = bf16[1,384,256]{2,1,0:T(8,128)(2,1)S(1)} collective-permute-done((bf16[1,384,256]{2,1,0:T(8,128)(2,1)S(1)}, bf16[1,384,256]{2,1,0:T(8,128)(2,1)S(1)}, u32[]{:S(2)}, u32[]{:S(2)}) %collective-permute-start.8) | collective-permute-done | bytes 196640 | tf_op jit(solution)/shard_map/ppermute | solution.py:28
  65.4 2.5 %collective-permute-start.6 = (bf16[1,384,256]{2,1,0:T(8,128)(2,1)}, bf16[1,384,256]{2,1,0:T(8,128)(2,1)S(1)}, u32[]{:S(2)}, u32[]{:S(2)}) collective-permute-start(bf16[1,384,256]{2,1,0:T(8,128)(2,1)} %get-tuple-element.61), channel_id=1, source_target_pairs={{0,24},{2,26},{4,28},{6,30},{8,16},{10,18},{12,20},{14,22},{16,8},... | collective-permute-start | bytes 589832 | tf_op jit(solution)/shard_map/ppermute | solution.py:28
  67.8 0.7 constant_dynamic-update-slice_fusion.1
  68.5 0.7 constant_dynamic-update-slice_fusion.refs_1_
  69.2 0.5 collective-permute-start.14
  70.3 8.8 %project.5 = bf16[4,2,384,128]{3,2,1,0:T(8,128)(2,1)} custom-call(s32[3]{0:T(128)} %pad_add_fusion.place_ref, bf16[3,3072,1536]{2,1,0:T(8,128)(2,1)} %bitcast.7, f32[12,2,128]{2,1,0:T(2,128)} %bitcast.10, s32[1,1]{1,0:T(1,128)S(6)} %max.12.refs_2_, bf16[384,3072]{1,0:T(8,128)(2,1)} %get-tuple-element.51.refs_3_, bf16[384,384]{1,0:T(8,128)(2,1)} %get-tuple-element.52.refs_4_), custom_call_target="tpu_custom_call" | custom-call | flops 2415919104 | bytes 8650752 | tf_op jit(solution)/shard_map/project/pallas_call | solution.py:150
  79.1 11.1 %all-to-all-start.1 = ((bf16[4,2,384,128]{3,2,1,0:T(8,128)(2,1)}), bf16[4,2,384,128]{3,2,1,0:T(8,128)(2,1)S(1)}, u32[]{:S(2)}, u32[]{:S(2)}) async-start(bf16[4,2,384,128]{3,2,1,0:T(8,128)(2,1)} %project.5), calls=%async_computation.1 | async-start | bytes 1572864 | tf_op jit(solution)/shard_map/all_to_all | solution.py:413
  90.2 0.5 collective-permute-start.10
  90.9 1.6 collective-permute-start.12
  92.4 0.5 collective-permute-start.15
  93.0 0.5 broadcast_maximum_fusion.2.place_ref
  93.5 0.3 collective-permute-done.10.refs_5_
  93.8 10.1 %attend.3 = bf16[4,384,128]{2,1,0:T(8,128)(2,1)} custom-call(s32[3]{0:T(128)} %broadcast_maximum_fusion.2.place_ref, bf16[1,384,384]{2,1,0:T(8,128)(2,1)} %get-tuple-element.64.refs_0_, bf16[1,384,384]{2,1,0:T(8,128)(2,1)} %copy-done.9, bf16[1,384,384]{2,1,0:T(8,128)(2,1)} %copy-done.10, bf16[1,384,384]{2,1,0:T(8,128)(2,1)} %copy-done.11, ...), custom_call_target="tpu_custom_call" | custom-call | flops 2415919104 | bytes 3145728 | tf_op jit(solution)/shard_map/attend/pallas_call | solution.py:277
  103.9 5.1 %all-to-all-start = ((bf16[4,384,128]{2,1,0:T(8,128)(2,1)}), bf16[4,384,128]{2,1,0:T(8,128)(2,1)S(1)}, u32[]{:S(2)}, u32[]{:S(2)}) async-start(bf16[4,384,128]{2,1,0:T(8,128)(2,1)} %attend.3), calls=%async_computation | async-start | bytes 786432 | tf_op jit(solution)/shard_map/all_to_all | solution.py:413
  109.0 1.4 collective-permute-done.12.refs_3_
  110.4 0.6 broadcast_maximum_fusion.1.place_ref
  111.0 9.9 %attend.4 = bf16[4,384,128]{2,1,0:T(8,128)(2,1)} custom-call(s32[3]{0:T(128)} %broadcast_maximum_fusion.1.place_ref, bf16[4,2,384,128]{3,2,1,0:T(8,128)(2,1)} %copy-done.5, bf16[4,384,256]{2,1,0:T(8,128)(2,1)} %constant_dynamic-update-slice_fusion.refs_1_, bf16[4,384,256]{2,1,0:T(8,128)(2,1)} %collective-permute-done.13.refs_2_, ...), custom_call_target="tpu_custom_call" | custom-call | flops 2415919104 | bytes 3145728 | tf_op jit(solution)/shard_map/attend/pallas_call | solution.py:277
  121.0 5.1 %all-to-all-start.2 = ((bf16[4,384,128]{2,1,0:T(8,128)(2,1)}), bf16[4,384,128]{2,1,0:T(8,128)(2,1)S(1)}, u32[]{:S(2)}, u32[]{:S(2)}) async-start(bf16[4,384,128]{2,1,0:T(8,128)(2,1)} %attend.4), calls=%async_computation.2 | async-start | bytes 786432 | tf_op jit(solution)/shard_map/all_to_all | solution.py:413
  126.1 0.6 broadcast_maximum_fusion.place_ref
  126.6 9.8 %attend.5 = (bf16[1,384,128]{2,1,0:T(8,128)(2,1)}, bf16[1,384,128]{2,1,0:T(8,128)(2,1)}, bf16[1,384,128]{2,1,0:T(8,128)(2,1)}, bf16[1,384,128]{2,1,0:T(8,128)(2,1)}) custom-call(s32[3]{0:T(128)} %broadcast_maximum_fusion.place_ref, bf16[4,2,384,128]{3,2,1,0:T(8,128)(2,1)} %copy-done.5, bf16[4,384,256]{2,1,0:T(8,128)(2,1)} %copy-done.12, ...), custom_call_target="tpu_custom_call" | custom-call | flops 2415919104 | bytes 3145728 | tf_op jit(solution)/shard_map/attend/pallas_call | solution.py:277
  136.5 2.0 %collective-permute-start.18 = (bf16[1,384,128]{2,1,0:T(8,128)(2,1)}, bf16[1,384,128]{2,1,0:T(8,128)(2,1)S(1)}, u32[]{:S(2)}, u32[]{:S(2)}) collective-permute-start(bf16[1,384,128]{2,1,0:T(8,128)(2,1)} %get-tuple-element.81), channel_id=1, source_target_pairs={{0,8},{2,10},{4,12},{6,14},{8,0},{10,2},{12,4},{14,6},{16,24},{18,... | collective-permute-start | bytes 294920 | tf_op jit(solution)/shard_map/ppermute | solution.py:28
  138.5 2.4 %collective-permute-start.19 = (bf16[1,384,128]{2,1,0:T(8,128)(2,1)}, bf16[1,384,128]{2,1,0:T(8,128)(2,1)S(1)}, u32[]{:S(2)}, u32[]{:S(2)}) collective-permute-start(bf16[1,384,128]{2,1,0:T(8,128)(2,1)} %get-tuple-element.82), channel_id=1, source_target_pairs={{0,16},{2,18},{4,20},{6,22},{8,24},{10,26},{12,28},{14,30},{16,0},... | collective-permute-start | bytes 294920 | tf_op jit(solution)/shard_map/ppermute | solution.py:28
  140.9 0.9 constant_dynamic-update-slice_fusion.11
  141.9 3.9 %collective-permute-done.19 = bf16[1,384,128]{2,1,0:T(8,128)(2,1)S(1)} collective-permute-done((bf16[1,384,128]{2,1,0:T(8,128)(2,1)}, bf16[1,384,128]{2,1,0:T(8,128)(2,1)S(1)}, u32[]{:S(2)}, u32[]{:S(2)}) %collective-permute-start.19) | collective-permute-done | bytes 98336 | tf_op jit(solution)/shard_map/ppermute | solution.py:28
  145.8 1.8 collective-permute-done.20
  147.6 0.8 copy-done.2
  148.4 0.7 copy-done.1
  149.1 7.0 %finish.2 = bf16[384,1536]{1,0:T(8,128)(2,1)} custom-call(s32[3]{0:T(128)} %pad_add_fusion.place_ref, bf16[4,384,128]{2,1,0:T(8,128)(2,1)} %copy-done, bf16[4,384,128]{2,1,0:T(8,128)(2,1)} %copy-done.1, bf16[4,384,128]{2,1,0:T(8,128)(2,1)} %copy-done.2, bf16[1536,3072]{1,0:T(8,128)(2,1)} %refs_3_.5), custom_call_target="tpu_custom_call" | custom-call | flops 1811939328 | bytes 7077888 | tf_op jit(solution)/shard_map/finish/pallas_call | solution.py:340
  156.2 1.5 collective-permute-start.21
  157.7 7.1 %finish.3.mine_ref = bf16[384,1536]{1,0:T(8,128)(2,1)} custom-call(s32[3]{0:T(128)} %pad_add_fusion.place_ref, bf16[4,384,128]{2,1,0:T(8,128)(2,1)} %copy-done, bf16[4,384,128]{2,1,0:T(8,128)(2,1)} %copy-done.1, bf16[4,384,128]{2,1,0:T(8,128)(2,1)} %copy-done.2, bf16[1536,3072]{1,0:T(8,128)(2,1)} %refs_3_.5), custom_call_target="tpu_custom_call" | custom-call | flops 1811939328 | bytes 7077888 | tf_op jit(solution)/shard_map/finish/pallas_call | solution.py:340
  164.8 15.8 %collective-permute-done.21.refs_0_ = bf16[384,1536]{1,0:T(8,128)(2,1)S(1)} collective-permute-done((bf16[384,1536]{1,0:T(8,128)(2,1)}, bf16[384,1536]{1,0:T(8,128)(2,1)S(1)}, u32[]{:S(2)}, u32[]{:S(2)}) %collective-permute-start.21) | collective-permute-done | bytes 1179680 | tf_op jit(solution)/shard_map/ppermute | solution.py:28
  180.6 1.0 copy-done.3
  181.7 4.4 %close.1 = bf16[384,1536]{1,0:T(8,128)(2,1)} custom-call(bf16[384,384]{1,0:T(8,128)(2,1)} %get-tuple-element.45.back_ref, bf16[384,1536]{1,0:T(8,128)(2,1)} %finish.3.mine_ref, bf16[384,1536]{1,0:T(8,128)(2,1)} %copy-done.3), custom_call_target="tpu_custom_call" | custom-call | flops 452984832 | bytes 5898240 | tf_op jit(solution)/shard_map/close/pallas_call | solution.py:370
  (68 shorter events, 0.4 us)
Async XLA Ops:
  14.1 15.9 %collective-permute-start = (bf16[1,384,384]{2,1,0:T(8,128)(2,1)}, bf16[1,384,384]{2,1,0:T(8,128)(2,1)S(1)}, u32[]{:S(2)}, u32[]{:S(2)}) collective-permute-start(bf16[1,384,384]{2,1,0:T(8,128)(2,1)} %get-tuple-element.46), channel_id=1, source_target_pairs={{0,8},{2,10},{4,12},{6,14},{8,0},{10,2},{12,4},{14,6},{16,24},{18,... | collective-permute-start | bytes 884744 | tf_op jit(solution)/shard_map/ppermute | solution.py:28
  17.2 26.0 %collective-permute-start.1 = (bf16[1,384,384]{2,1,0:T(8,128)(2,1)}, bf16[1,384,384]{2,1,0:T(8,128)(2,1)S(1)}, u32[]{:S(2)}, u32[]{:S(2)}) collective-permute-start(bf16[1,384,384]{2,1,0:T(8,128)(2,1)} %get-tuple-element.47), channel_id=1, source_target_pairs={{0,16},{2,18},{4,20},{6,22},{8,24},{10,26},{12,28},{14,30},{16,0},... | collective-permute-start | bytes 884744 | tf_op jit(solution)/shard_map/ppermute | solution.py:28
  19.8 23.4 %collective-permute-start.2 = (bf16[1,384,384]{2,1,0:T(8,128)(2,1)}, bf16[1,384,384]{2,1,0:T(8,128)(2,1)S(1)}, u32[]{:S(2)}, u32[]{:S(2)}) collective-permute-start(bf16[1,384,384]{2,1,0:T(8,128)(2,1)} %get-tuple-element.48), channel_id=1, source_target_pairs={{0,24},{2,26},{4,28},{6,30},{8,16},{10,18},{12,20},{14,22},{16,8},... | collective-permute-start | bytes 884744 | tf_op jit(solution)/shard_map/ppermute | solution.py:28
  29.9 13.3 %copy-start.9 = (bf16[1,384,384]{2,1,0:T(8,128)(2,1)}, bf16[1,384,384]{2,1,0:T(8,128)(2,1)S(1)}, u32[]{:S(2)}) copy-start(bf16[1,384,384]{2,1,0:T(8,128)(2,1)S(1)} %collective-permute-done.refs_1_) | copy-start | bytes 884740
  29.9 13.3 %copy-start.8 = (bf16[1,384,384]{2,1,0:T(8,128)(2,1)S(1)}, bf16[1,384,384]{2,1,0:T(8,128)(2,1)}, u32[]{:S(2)}) copy-start(bf16[1,384,384]{2,1,0:T(8,128)(2,1)} %get-tuple-element.64.refs_0_) | copy-start | bytes 884740
  43.1 2.1 %copy-start.17 = (bf16[1,384,256]{2,1,0:T(8,128)(2,1)S(1)}, bf16[1,384,256]{2,1,0:T(8,128)(2,1)}, u32[]{:S(2)}) copy-start(bf16[1,384,256]{2,1,0:T(8,128)(2,1)} %get-tuple-element.57) | copy-start | bytes 589828
  43.1 5.0 %copy-start.16 = (bf16[1,384,256]{2,1,0:T(8,128)(2,1)S(1)}, bf16[1,384,256]{2,1,0:T(8,128)(2,1)}, u32[]{:S(2)}) copy-start(bf16[1,384,256]{2,1,0:T(8,128)(2,1)} %get-tuple-element.68) | copy-start | bytes 589828
  43.1 6.1 %copy-start.15 = (bf16[1,384,256]{2,1,0:T(8,128)(2,1)S(1)}, bf16[1,384,256]{2,1,0:T(8,128)(2,1)}, u32[]{:S(2)}) copy-start(bf16[1,384,256]{2,1,0:T(8,128)(2,1)} %get-tuple-element.69) | copy-start | bytes 589828
  43.1 7.5 %copy-start.7 = (bf16[1,384,256]{2,1,0:T(8,128)(2,1)S(1)}, bf16[1,384,256]{2,1,0:T(8,128)(2,1)}, u32[]{:S(2)}) copy-start(bf16[1,384,256]{2,1,0:T(8,128)(2,1)} %get-tuple-element.63) | copy-start | bytes 589828
  43.2 26.0 %copy-start.10 = (bf16[1,384,384]{2,1,0:T(8,128)(2,1)}, bf16[1,384,384]{2,1,0:T(8,128)(2,1)S(1)}, u32[]{:S(2)}) copy-start(bf16[1,384,384]{2,1,0:T(8,128)(2,1)S(1)} %collective-permute-done.1.refs_2_) | copy-start | bytes 884740
  43.2 26.0 %copy-start.11 = (bf16[1,384,384]{2,1,0:T(8,128)(2,1)}, bf16[1,384,384]{2,1,0:T(8,128)(2,1)S(1)}, u32[]{:S(2)}) copy-start(bf16[1,384,384]{2,1,0:T(8,128)(2,1)S(1)} %collective-permute-done.2.refs_3_) | copy-start | bytes 884740
  43.4 46.8 %copy-start.4 = (bf16[4,384,256]{2,1,0:T(8,128)(2,1)}, bf16[4,384,256]{2,1,0:T(8,128)(2,1)S(1)}, u32[]{:S(2)}) copy-start(bf16[4,384,256]{2,1,0:T(8,128)(2,1)S(1)} %pad_maximum_fusion.refs_4_) | copy-start | bytes 2359300
  43.4 26.3 %collective-permute-start.7 = (bf16[4,384,256]{2,1,0:T(8,128)(2,1)S(1)}, bf16[4,384,256]{2,1,0:T(8,128)(2,1)}, u32[]{:S(2)}, u32[]{:S(2)}) collective-permute-start(bf16[4,384,256]{2,1,0:T(8,128)(2,1)S(1)} %pad_maximum_fusion.refs_4_), channel_id=1, source_target_pairs={{0,4},{2,6},{4,0},{6,2},{8,12},{10,14},{12,8},{14,10},{16,20},{18,... | collective-permute-start | bytes 2359304 | tf_op jit(solution)/shard_map/ppermute | solution.py:28
  45.2 11.5 %collective-permute-start.3 = (bf16[1,384,256]{2,1,0:T(8,128)(2,1)S(1)}, bf16[1,384,256]{2,1,0:T(8,128)(2,1)S(1)}, u32[]{:S(2)}, u32[]{:S(2)}) collective-permute-start(bf16[1,384,256]{2,1,0:T(8,128)(2,1)S(1)} %copy-done.17), channel_id=1, source_target_pairs={{0,8},{2,10},{4,12},{6,14},{8,0},{10,2},{12,4},{14,6},{16,24},{18,... | collective-permute-start | bytes 589832 | tf_op jit(solution)/shard_map/ppermute | solution.py:28
  48.1 17.2 %collective-permute-start.8 = (bf16[1,384,256]{2,1,0:T(8,128)(2,1)S(1)}, bf16[1,384,256]{2,1,0:T(8,128)(2,1)S(1)}, u32[]{:S(2)}, u32[]{:S(2)}) collective-permute-start(bf16[1,384,256]{2,1,0:T(8,128)(2,1)S(1)} %copy-done.16), channel_id=1, source_target_pairs={{0,16},{2,18},{4,20},{6,22},{8,24},{10,26},{12,28},{14,30},{16,0},... | collective-permute-start | bytes 589832 | tf_op jit(solution)/shard_map/ppermute | solution.py:28
  49.2 19.3 %collective-permute-start.9 = (bf16[1,384,256]{2,1,0:T(8,128)(2,1)S(1)}, bf16[1,384,256]{2,1,0:T(8,128)(2,1)S(1)}, u32[]{:S(2)}, u32[]{:S(2)}) collective-permute-start(bf16[1,384,256]{2,1,0:T(8,128)(2,1)S(1)} %copy-done.15), channel_id=1, source_target_pairs={{0,24},{2,26},{4,28},{6,30},{8,16},{10,18},{12,20},{14,22},{16,8},... | collective-permute-start | bytes 589832 | tf_op jit(solution)/shard_map/ppermute | solution.py:28
  56.7 33.5 %collective-permute-start.4 = (bf16[1,384,256]{2,1,0:T(8,128)(2,1)}, bf16[1,384,256]{2,1,0:T(8,128)(2,1)S(1)}, u32[]{:S(2)}, u32[]{:S(2)}) collective-permute-start(bf16[1,384,256]{2,1,0:T(8,128)(2,1)} %get-tuple-element.59), channel_id=1, source_target_pairs={{0,8},{2,10},{4,12},{6,14},{8,0},{10,2},{12,4},{14,6},{16,24},{18,... | collective-permute-start | bytes 589832 | tf_op jit(solution)/shard_map/ppermute | solution.py:28
  56.7 34.1 %collective-permute-start.5 = (bf16[1,384,256]{2,1,0:T(8,128)(2,1)}, bf16[1,384,256]{2,1,0:T(8,128)(2,1)S(1)}, u32[]{:S(2)}, u32[]{:S(2)}) collective-permute-start(bf16[1,384,256]{2,1,0:T(8,128)(2,1)} %get-tuple-element.60), channel_id=1, source_target_pairs={{0,16},{2,18},{4,20},{6,22},{8,24},{10,26},{12,28},{14,30},{16,0},... | collective-permute-start | bytes 589832 | tf_op jit(solution)/shard_map/ppermute | solution.py:28
  65.4 25.4 %collective-permute-start.6 = (bf16[1,384,256]{2,1,0:T(8,128)(2,1)}, bf16[1,384,256]{2,1,0:T(8,128)(2,1)S(1)}, u32[]{:S(2)}, u32[]{:S(2)}) collective-permute-start(bf16[1,384,256]{2,1,0:T(8,128)(2,1)} %get-tuple-element.61), channel_id=1, source_target_pairs={{0,24},{2,26},{4,28},{6,30},{8,16},{10,18},{12,20},{14,22},{16,8},... | collective-permute-start | bytes 589832 | tf_op jit(solution)/shard_map/ppermute | solution.py:28
  69.2 23.2 %collective-permute-start.14 = (bf16[4,384,256]{2,1,0:T(8,128)(2,1)}, bf16[4,384,256]{2,1,0:T(8,128)(2,1)}, u32[]{:S(2)}, u32[]{:S(2)}) collective-permute-start(bf16[4,384,256]{2,1,0:T(8,128)(2,1)} %constant_dynamic-update-slice_fusion.refs_1_), channel_id=1, source_target_pairs={{0,4},{2,6},{4,0},{6,2},{8,12},{10,14},{12,8},{14,10},{16,20},{18,... | collective-permute-start | bytes 2359304 | tf_op jit(solution)/shard_map/ppermute | solution.py:28
  70.3 20.5 %copy-start.6 = (bf16[1,384,256]{2,1,0:T(8,128)(2,1)S(1)}, bf16[1,384,256]{2,1,0:T(8,128)(2,1)}, u32[]{:S(2)}) copy-start(bf16[1,384,256]{2,1,0:T(8,128)(2,1)} %get-tuple-element.71) | copy-start | bytes 589828
  79.1 13.9 %copy-start.13 = (s32[3]{0:T(128)S(1)}, s32[3]{0:T(128)}, u32[]{:S(2)}) copy-start(s32[3]{0:T(128)} %pad_add_fusion.place_ref) | copy-start | bytes 40
  79.1 24.8 %all-to-all-start.1 = ((bf16[4,2,384,128]{3,2,1,0:T(8,128)(2,1)}), bf16[4,2,384,128]{3,2,1,0:T(8,128)(2,1)S(1)}, u32[]{:S(2)}, u32[]{:S(2)}) async-start(bf16[4,2,384,128]{3,2,1,0:T(8,128)(2,1)} %project.5), calls=%async_computation.1 | async-start | bytes 1572864 | tf_op jit(solution)/shard_map/all_to_all | solution.py:413
  90.2 3.3 %collective-permute-start.11 = (bf16[4,384,256]{2,1,0:T(8,128)(2,1)}, bf16[4,384,256]{2,1,0:T(8,128)(2,1)}, u32[]{:S(2)}, u32[]{:S(2)}) collective-permute-start(bf16[4,384,256]{2,1,0:T(8,128)(2,1)} %collective-permute-done.7.refs_6_), channel_id=1, source_target_pairs={{0,2},{2,0},{4,6},{6,4},{8,10},{10,8},{12,14},{14,12},{16,18},{18,... | collective-permute-start | bytes 2359304 | tf_op jit(solution)/shard_map/ppermute | solution.py:28
  90.2 3.5 %collective-permute-start.10 = (bf16[4,384,256]{2,1,0:T(8,128)(2,1)S(1)}, bf16[4,384,256]{2,1,0:T(8,128)(2,1)}, u32[]{:S(2)}, u32[]{:S(2)}) collective-permute-start(bf16[4,384,256]{2,1,0:T(8,128)(2,1)S(1)} %pad_maximum_fusion.refs_4_), channel_id=1, source_target_pairs={{0,2},{2,0},{4,6},{6,4},{8,10},{10,8},{12,14},{14,12},{16,18},{18,... | collective-permute-start | bytes 2359304 | tf_op jit(solution)/shard_map/ppermute | solution.py:28
  90.8 18.2 %copy-start.12 = (bf16[4,384,256]{2,1,0:T(8,128)(2,1)}, bf16[4,384,256]{2,1,0:T(8,128)(2,1)S(1)}, u32[]{:S(2)}) copy-start(bf16[4,384,256]{2,1,0:T(8,128)(2,1)S(1)} %constant_dynamic-update-slice_fusion.4.refs_1_) | copy-start | bytes 2359300
  90.9 19.6 %collective-permute-start.12 = (bf16[4,384,256]{2,1,0:T(8,128)(2,1)S(1)}, bf16[4,384,256]{2,1,0:T(8,128)(2,1)S(1)}, u32[]{:S(2)}, u32[]{:S(2)}) collective-permute-start(bf16[4,384,256]{2,1,0:T(8,128)(2,1)S(1)} %constant_dynamic-update-slice_fusion.4.refs_1_), channel_id=1, source_target_pairs={{0,4},{2,6},{4,0},{6,2},{8,12},{10,14},{12,8},{14,10},{16,20},{18,... | collective-permute-start | bytes 2359304 | tf_op jit(solution)/shard_map/ppermute | solution.py:28
  92.4 18.6 %collective-permute-start.13 = (bf16[4,384,256]{2,1,0:T(8,128)(2,1)}, bf16[4,384,256]{2,1,0:T(8,128)(2,1)}, u32[]{:S(2)}, u32[]{:S(2)}) collective-permute-start(bf16[4,384,256]{2,1,0:T(8,128)(2,1)} %constant_dynamic-update-slice_fusion.refs_1_), channel_id=1, source_target_pairs={{0,2},{2,0},{4,6},{6,4},{8,10},{10,8},{12,14},{14,12},{16,18},{18,... | collective-permute-start | bytes 2359304 | tf_op jit(solution)/shard_map/ppermute | solution.py:28
  92.4 18.6 %collective-permute-start.15 = (bf16[4,384,256]{2,1,0:T(8,128)(2,1)}, bf16[4,384,256]{2,1,0:T(8,128)(2,1)}, u32[]{:S(2)}, u32[]{:S(2)}) collective-permute-start(bf16[4,384,256]{2,1,0:T(8,128)(2,1)} %collective-permute-done.14.refs_3_), channel_id=1, source_target_pairs={{0,2},{2,0},{4,6},{6,4},{8,10},{10,8},{12,14},{14,12},{16,18},{18,... | collective-permute-start | bytes 2359304 | tf_op jit(solution)/shard_map/ppermute | solution.py:28
  103.9 7.1 %copy-start.5 = (bf16[4,2,384,128]{3,2,1,0:T(8,128)(2,1)}, bf16[4,2,384,128]{3,2,1,0:T(8,128)(2,1)S(1)}, u32[]{:S(2)}) copy-start(bf16[4,2,384,128]{3,2,1,0:T(8,128)(2,1)S(1)} %all-to-all-done.1.refs_0_) | copy-start | bytes 2359300
  103.9 17.1 %all-to-all-start = ((bf16[4,384,128]{2,1,0:T(8,128)(2,1)}), bf16[4,384,128]{2,1,0:T(8,128)(2,1)S(1)}, u32[]{:S(2)}, u32[]{:S(2)}) async-start(bf16[4,384,128]{2,1,0:T(8,128)(2,1)} %attend.3), calls=%async_computation | async-start | bytes 786432 | tf_op jit(solution)/shard_map/all_to_all | solution.py:413
  109.0 17.6 %collective-permute-start.16 = (bf16[4,384,256]{2,1,0:T(8,128)(2,1)S(1)}, bf16[4,384,256]{2,1,0:T(8,128)(2,1)}, u32[]{:S(2)}, u32[]{:S(2)}) collective-permute-start(bf16[4,384,256]{2,1,0:T(8,128)(2,1)S(1)} %constant_dynamic-update-slice_fusion.4.refs_1_), channel_id=1, source_target_pairs={{0,2},{2,0},{4,6},{6,4},{8,10},{10,8},{12,14},{14,12},{16,18},{18,... | collective-permute-start | bytes 2359304 | tf_op jit(solution)/shard_map/ppermute | solution.py:28
  110.4 10.5 %copy-start.14 = (bf16[4,384,256]{2,1,0:T(8,128)(2,1)}, bf16[4,384,256]{2,1,0:T(8,128)(2,1)S(1)}, u32[]{:S(2)}) copy-start(bf16[4,384,256]{2,1,0:T(8,128)(2,1)S(1)} %collective-permute-done.12.refs_3_) | copy-start | bytes 2359300
  110.4 16.2 %collective-permute-start.17 = (bf16[4,384,256]{2,1,0:T(8,128)(2,1)S(1)}, bf16[4,384,256]{2,1,0:T(8,128)(2,1)}, u32[]{:S(2)}, u32[]{:S(2)}) collective-permute-start(bf16[4,384,256]{2,1,0:T(8,128)(2,1)S(1)} %collective-permute-done.12.refs_3_), channel_id=1, source_target_pairs={{0,2},{2,0},{4,6},{6,4},{8,10},{10,8},{12,14},{14,12},{16,18},{18,... | collective-permute-start | bytes 2359304 | tf_op jit(solution)/shard_map/ppermute | solution.py:28
  121.0 15.5 %copy-start = (bf16[4,384,128]{2,1,0:T(8,128)(2,1)}, bf16[4,384,128]{2,1,0:T(8,128)(2,1)S(1)}, u32[]{:S(2)}) copy-start(bf16[4,384,128]{2,1,0:T(8,128)(2,1)S(1)} %all-to-all-done.refs_0_) | copy-start | bytes 1179652
  121.0 26.7 %all-to-all-start.2 = ((bf16[4,384,128]{2,1,0:T(8,128)(2,1)}), bf16[4,384,128]{2,1,0:T(8,128)(2,1)S(1)}, u32[]{:S(2)}, u32[]{:S(2)}) async-start(bf16[4,384,128]{2,1,0:T(8,128)(2,1)} %attend.4), calls=%async_computation.2 | async-start | bytes 786432 | tf_op jit(solution)/shard_map/all_to_all | solution.py:413
  136.5 5.4 %collective-permute-start.18 = (bf16[1,384,128]{2,1,0:T(8,128)(2,1)}, bf16[1,384,128]{2,1,0:T(8,128)(2,1)S(1)}, u32[]{:S(2)}, u32[]{:S(2)}) collective-permute-start(bf16[1,384,128]{2,1,0:T(8,128)(2,1)} %get-tuple-element.81), channel_id=1, source_target_pairs={{0,8},{2,10},{4,12},{6,14},{8,0},{10,2},{12,4},{14,6},{16,24},{18,... | collective-permute-start | bytes 294920 | tf_op jit(solution)/shard_map/ppermute | solution.py:28
  138.5 7.3 %collective-permute-start.19 = (bf16[1,384,128]{2,1,0:T(8,128)(2,1)}, bf16[1,384,128]{2,1,0:T(8,128)(2,1)S(1)}, u32[]{:S(2)}, u32[]{:S(2)}) collective-permute-start(bf16[1,384,128]{2,1,0:T(8,128)(2,1)} %get-tuple-element.82), channel_id=1, source_target_pairs={{0,16},{2,18},{4,20},{6,22},{8,24},{10,26},{12,28},{14,30},{16,0},... | collective-permute-start | bytes 294920 | tf_op jit(solution)/shard_map/ppermute | solution.py:28
  140.9 6.7 %collective-permute-start.20 = (bf16[1,384,128]{2,1,0:T(8,128)(2,1)}, bf16[1,384,128]{2,1,0:T(8,128)(2,1)S(1)}, u32[]{:S(2)}, u32[]{:S(2)}) collective-permute-start(bf16[1,384,128]{2,1,0:T(8,128)(2,1)} %get-tuple-element.83), channel_id=1, source_target_pairs={{0,24},{2,26},{4,28},{6,30},{8,16},{10,18},{12,20},{14,22},{16,8},... | collective-permute-start | bytes 294920 | tf_op jit(solution)/shard_map/ppermute | solution.py:28
  147.6 0.8 copy-start.2
  148.4 0.7 copy-start.1
  156.2 24.4 %collective-permute-start.21 = (bf16[384,1536]{1,0:T(8,128)(2,1)}, bf16[384,1536]{1,0:T(8,128)(2,1)S(1)}, u32[]{:S(2)}, u32[]{:S(2)}) collective-permute-start(bf16[384,1536]{1,0:T(8,128)(2,1)} %finish.2), channel_id=1, source_target_pairs={{0,1},{1,0},{2,3},{3,2},{4,5},{5,4},{6,7},{7,6},{8,9},{9,8},{10,11... | collective-permute-start | bytes 3538952 | tf_op jit(solution)/shard_map/ppermute | solution.py:28
  180.6 1.0 copy-start.3

commit v12 on v11

--- a/solution.py
+++ b/solution.py
@@ -96,7 +96,8 @@
             result_ref[...] = packed.astype(bf16)
             for k in range(groups):
                 if joined:
-                    outs[k // groups][k, row] = result_ref[:, k * size : (k + 1) * size]
+                    found = result_ref[:, k * size : (k + 1) * size]
+                    outs[target][k, row, :, low : low + size] = found
                 else:
                     start = pl.multiple_of(lax.bitwise_xor(plane, k) * size, size)
                     found = result_ref[:, pl.ds(start, size)]
@@ -131,7 +132,7 @@
         (len(which), rows, len(kinds) * size) for kinds, which in sets for _ in range(groups)
     ]
     if joined:
-        shapes = [(groups, len(sets[0][1]), rows, size)]
+        shapes = [(groups, len(which), rows, len(kinds) * size) for kinds, which in sets]
     out_specs = [
         pl.BlockSpec(shape, lambda t, place, zeros=(0,) * len(shape): zeros) for shape in shapes
     ]
@@ -171,15 +172,15 @@
         name="project",
     )(place, weights, gains, *(first or prepared))
     if joined:
-        return found[0], []
+        return found[: len(sets)], []
     blocks = [found[i * groups : (i + 1) * groups] for i in range(len(sets))]
     return blocks, found[len(sets) * groups :]
 
 
 def attend_body(place_ref, *refs, groups, asked, joined, ordered, low_lane, key_room, query_rows, key_cols):
     outs = 1 if ordered else groups
-    query_refs, sources, out_refs = refs[:asked], refs[asked : -4 - outs], refs[-4 - outs : -4]
-    keys, values, queries, results = refs[-4:]
+    query_refs, sources, out_refs = refs[:asked], refs[asked : -5 - outs], refs[-5 - outs : -5]
+    keys, values, queries, results, counts = refs[-5:]
     rows, size = out_refs[0].shape[1:]
     plane = place_ref[0]
     blocks = [(source, k) for source in sources for k in range(groups)]
@@ -190,7 +191,8 @@
     found = []
     for source, block in blocks:
         live = (source[block, :, :size].astype(f32) < dead_limit).astype(f32)
-        found.append(jnp.max(jnp.sum(live, axis=0, keepdims=True)).astype(jnp.int32))
+        counts[len(found)] = jnp.max(jnp.sum(live, axis=0, keepdims=True)).astype(jnp.int32)
+        found.append(counts[len(found)])
 
     offset = jnp.int32(0)
     for (source, block), count in zip(blocks, found):
@@ -216,7 +218,7 @@
 
     lax.fori_loop(0, (key_room - offset) // 16, clear, 0)
 
-    mine = found[:groups]
+    mine = [counts[lax.bitwise_xor(plane, k) if joined else k] for k in range(groups)]
     starts = []
     start = jnp.int32(0)
     for k in range(groups):
@@ -297,6 +299,7 @@
                 pltpu.VMEM((key_room + rows, 2 * size), bf16),
                 pltpu.VMEM((query_room, size), bf16),
                 pltpu.VMEM((query_room, size), bf16),
+                pltpu.SMEM((shards,), jnp.int32),
             ],
         ),
         out_shape=[jax.ShapeDtypeStruct((wide, rows, size), bf16)] * outs,
@@ -436,21 +439,19 @@
     if chunks > 1:
         prepared = (count, chain(normed, first(arrived[0])), chosen)
         sets = [((1, 2), (chunk,)) for chunk in rest]
-        made, _ = project(place, prepared, weights, gains, sets, groups)
-        stacks = [stack(list(chain(tuple(arrived[0]), made[0][0])))]
-        arrived.append(send(made[0]))
-        for blocks in made[1:]:
-            arrived.append(send(blocks, first(arrived[-1])))
+        made, _ = project(place, prepared, weights, gains, sets, groups, joined=True)
+        stacks = [stack(list(chain(tuple(arrived[0]), made[0])))]
+        shape = (groups, survive.shape[0], 2 * size)
+        for blocks in made:
+            stacks.append(send_back(chain(blocks.reshape(shape), stacks[-1])))
         hop = flip(stacks[0], "seq", ring // 2) if ring > 1 else stacks[0]
-        stacks.append(stack(arrived[1]))
+        sets = [((0,), tuple(rest))]
         ready = later(count, hop, stacks[1])
-        sets = [((0,), tuple(rest))]
-        made, _ = project(
+        (gate,), _ = project(
             place, (ready, normed, chosen), weights, gains, sets, groups, joined=True
         )
-        gate = made
-        stacks += [stack(list(chain(tuple(blocks), made))) for blocks in arrived[2:]]
-        asked = [send_back(made)]
+        stacks[2:] = [chain(blocks, gate) for blocks in stacks[2:]]
+        asked = [send_back(gate)]
         hops = [flip(stacks[-1], "seq", ring // 2)] if ring > 1 else []
     else:
         gate, stacks = None, [stack(arrived[0])]
@@ -460,7 +461,8 @@
     for chunk in range(chunks):
         final = chunk == chunks - 1
         keyvals = everywhere(stacks[chunk], gate)
-        before = [stacks[-1]] + attended[-1:] + (hops if chunk else []) + (returned[:1] if final else [])
+        before = ([stacks[-1]] if chunk else []) + attended[-1:]
+        before += (hops if chunk else []) + (returned[:1] if final else [])
         ready = later(place, *query[1 if chunk == 0 else 0 :], *before)
         row = max(chunk - 1, 0)
         found = attend(ready, query, row, low_lane, keyvals, shards, not final)

time: 190 us -> 207 us (1.089); the launches traced: 186 us -> 208 us
  blocking collectives: 0 us -> 23.5 us
  starting transfers between devices: 48.3 us -> 33.3 us
  waiting for transfers between devices: 44.2 us -> 54.3 us
  Pallas kernels: 83.9 us -> 87.5 us
    all_to_all x0 -> x1, blocking collectives: none -> 23.5 us  [send_back(): lax.all_to_all(blocks, 'seq', split_axis=0, concat_axis=0, axis_index_gro...]
    ppermute x22 -> x16, starting transfers between devices: 27 us -> 16.3 us  [flip(): return lax.ppermute(values, axis, [(i, i ^ mask) for i in range(size)])]
    ppermute x22 -> x16, waiting for transfers between devices: 44.2 us -> 52.8 us  [flip(): return lax.ppermute(values, axis, [(i, i ^ mask) for i in range(size)])]
    all_to_all x3 -> x4, starting transfers between devices: 21.3 us -> 16.9 us  [send_back(): lax.all_to_all(blocks, 'seq', split_axis=0, concat_axis=0, axis_index_gro...]
    pallas_call x3, Pallas kernels: 29.9 us -> 33.9 us  [attend(): pl.pallas_call(functools.partial(attend_body, groups=groups, asked=len(qu...]
    unnamed x45 -> x33, local copies, waits for them, and re-layouts: 5.69 us -> 5.76 us
  transfers between devices with their start and end apart: 25 -> 20, of which waited for: 8 -> 7; matrix products, arithmetic and copies ran while one was open for 3% -> 1% of each run, Pallas kernels for 32% -> 30%
where the time goes in v12:
time: 207 us; the launch traced here: 208 us
  Pallas kernels  87.5 us (42%)
  waiting for transfers between devices  54.3 us (26%)
  starting transfers between devices  33.3 us (16%)
  blocking collectives  23.5 us (11%)
  local copies, waits for them, and re-layouts  5.83 us (3%)
  other arithmetic  2.25 us (1%)
    ppermute x16, waiting for transfers between devices, flip(): return lax.ppermute(values, axis, [(i, i ^ mask) for i in range(size)])  52.8 us
    pallas_call x3, Pallas kernels, project(): pl.pallas_call(functools.partial(project_body, steps=steps, groups=groups...  35.1 us
    pallas_call x3, Pallas kernels, attend(): pl.pallas_call(functools.partial(attend_body, groups=groups, asked=len(qu...  33.9 us
    all_to_all x1, blocking collectives, send_back(): lax.all_to_all(blocks, 'seq', split_axis=0, concat_axis=0, axis_index_gro...  23.5 us
    all_to_all x4, starting transfers between devices, send_back(): lax.all_to_all(blocks, 'seq', split_axis=0, concat_axis=0, axis_index_gro...  16.9 us
    ppermute x16, starting transfers between devices, flip(): return lax.ppermute(values, axis, [(i, i ^ mask) for i in range(size)])  16.3 us
    pallas_call x2, Pallas kernels, finish(): pl.pallas_call(functools.partial(finish_body, ordered=ordered), grid_spec...  14.1 us
    unnamed x33, local copies, waits for them, and re-layouts  5.76 us
  transfers between devices with their start and end apart: 20, of which 7 were waited for; matrix products, arithmetic and copies ran while one was open for 1% of the time, Pallas kernels for 30%

profile of v12, /device:TPU:0, one launch (start us, length us, event | category | flops | bytes accessed | tf_op | source)
XLA Modules:
  0.0 207.6 jit_solution(4208346027721057050)
XLA Ops:
  0.0 0.6 pad_add_fusion.place_ref
  0.6 13.4 %project.3 = (bf16[1,384,384]{2,1,0:T(8,128)(2,1)}, bf16[1,384,384]{2,1,0:T(8,128)(2,1)}, bf16[1,384,384]{2,1,0:T(8,128)(2,1)}, bf16[1,384,384]{2,1,0:T(8,128)(2...) custom-call(s32[3]{0:T(128)} %pad_add_fusion.place_ref, ...), custom_call_target="tpu_custom_call" | custom-call | flops 3623878656 | bytes 11796480 | tf_op jit(solution)/shard_map/project/pallas_call | solution.py:151
  14.0 3.1 %collective-permute-start = (bf16[1,384,384]{2,1,0:T(8,128)(2,1)}, bf16[1,384,384]{2,1,0:T(8,128)(2,1)S(1)}, u32[]{:S(2)}, u32[]{:S(2)}) collective-permute-start(bf16[1,384,384]{2,1,0:T(8,128)(2,1)} %get-tuple-element.35), channel_id=1, source_target_pairs={{0,8},{2,10},{4,12},{6,14},{8,0},{10,2},{12,4},{14,6},{16,24},{18,... | collective-permute-start | bytes 884744 | tf_op jit(solution)/shard_map/ppermute | solution.py:28
  17.1 2.6 %collective-permute-start.1 = (bf16[1,384,384]{2,1,0:T(8,128)(2,1)}, bf16[1,384,384]{2,1,0:T(8,128)(2,1)S(1)}, u32[]{:S(2)}, u32[]{:S(2)}) collective-permute-start(bf16[1,384,384]{2,1,0:T(8,128)(2,1)} %get-tuple-element.36), channel_id=1, source_target_pairs={{0,16},{2,18},{4,20},{6,22},{8,24},{10,26},{12,28},{14,30},{16,0},... | collective-permute-start | bytes 884744 | tf_op jit(solution)/shard_map/ppermute | solution.py:28
  19.7 0.0 collective-permute-start.2
  19.7 10.2 %collective-permute-done.refs_1_ = bf16[1,384,384]{2,1,0:T(8,128)(2,1)S(1)} collective-permute-done((bf16[1,384,384]{2,1,0:T(8,128)(2,1)}, bf16[1,384,384]{2,1,0:T(8,128)(2,1)S(1)}, u32[]{:S(2)}, u32[]{:S(2)}) %collective-permute-start) | collective-permute-done | bytes 294944 | tf_op jit(solution)/shard_map/ppermute | solution.py:28
  29.9 13.3 %project.4 = (bf16[4,1,384,256]{3,2,1,0:T(8,128)(2,1)}, bf16[4,1,384,256]{3,2,1,0:T(8,128)(2,1)}) custom-call(s32[3]{0:T(128)} %pad_add_fusion.place_ref, bf16[3,3072,1536]{2,1,0:T(8,128)(2,1)} %bitcast.8, f32[12,2,128]{2,1,0:T(2,128)} %bitcast.12, s32[1,1]{1,0:T(1,128)} %get-tuple-element.50.refs_2_, bf16[384,3072]{1,0:T(8,128)(2,1)} %get-tuple-element.42.refs_3_, ...), custom_call_target="tpu_custom_call" | custom-call | flops 4831838208 | bytes 14942208 | tf_op jit(solution)/shard_map/project/pallas_call | solution.py:151
  43.1 0.0 collective-permute-done.1.refs_2_
  43.1 0.0 collective-permute-done.2.refs_3_
  43.3 0.1 pad_maximum_fusion.refs_4_
  43.4 0.0 copy-start.7
  43.4 1.4 copy-done.8
  44.7 23.5 %all_to_all.25.refs_1_ = bf16[4,384,256]{2,1,0:T(8,128)(2,1)S(1)} all-to-all(bf16[4,384,256]{2,1,0:T(8,128)(2,1)S(1)} %bitcast.10), channel_id=1, replica_groups={{0,8,16,24},{2,10,18,26},{4,12,20,28},{6,14,22,30},{1,9,17,25},{3,11,19..., dimensions={0} | all-to-all | bytes 1572864 | tf_op jit(solution)/shard_map/all_to_all | solution.py:416
  68.3 3.7 %all-to-all-start.3 = ((bf16[4,384,256]{2,1,0:T(8,128)(2,1)}), bf16[4,384,256]{2,1,0:T(8,128)(2,1)S(1)}, u32[]{:S(2)}, u32[]{:S(2)}) async-start(bf16[4,384,256]{2,1,0:T(8,128)(2,1)} %bitcast.6), calls=%async_computation.3 | async-start | bytes 1572864 | tf_op jit(solution)/shard_map/all_to_all | solution.py:416
  72.0 1.6 collective-permute-start.3
  73.5 16.7 %collective-permute-done.3.refs_6_ = bf16[4,384,256]{2,1,0:T(8,128)(2,1)} collective-permute-done((bf16[4,384,256]{2,1,0:T(8,128)(2,1)S(1)}, bf16[4,384,256]{2,1,0:T(8,128)(2,1)}, u32[]{:S(2)}, u32[]{:S(2)}) %collective-permute-start.3) | collective-permute-done | bytes 786464 | tf_op jit(solution)/shard_map/ppermute | solution.py:28
  90.9 1.6 collective-permute-start.8
  92.5 8.5 %project.5 = bf16[4,2,384,128]{3,2,1,0:T(8,128)(2,1)} custom-call(s32[3]{0:T(128)} %pad_add_fusion.place_ref, bf16[3,3072,1536]{2,1,0:T(8,128)(2,1)} %bitcast.9, f32[12,2,128]{2,1,0:T(2,128)} %bitcast.13, s32[1,1]{1,0:T(1,128)S(6)} %max.13.refs_2_, bf16[384,3072]{1,0:T(8,128)(2,1)} %get-tuple-element.42.refs_3_, bf16[384,384]{1,0:T(8,128)(2,1)} %get-tuple-element.43.refs_4_), custom_call_target="tpu_custom_call" | custom-call | flops 2415919104 | bytes 8650752 | tf_op jit(solution)/shard_map/project/pallas_call | solution.py:151
  101.0 4.5 %all-to-all-start.2 = ((bf16[4,2,384,128]{3,2,1,0:T(8,128)(2,1)}), bf16[4,2,384,128]{3,2,1,0:T(8,128)(2,1)S(1)}, u32[]{:S(2)}, u32[]{:S(2)}) async-start(bf16[4,2,384,128]{3,2,1,0:T(8,128)(2,1)} %project.5), calls=%async_computation.2 | async-start | bytes 1572864 | tf_op jit(solution)/shard_map/all_to_all | solution.py:416
  105.5 0.5 collective-permute-start.5
  106.0 0.5 collective-permute-start.6
  106.5 1.7 collective-permute-done.8.refs_3_
  108.2 0.5 broadcast_maximum_fusion.2.place_ref
  108.7 0.9 copy-done.14
  109.7 0.3 collective-permute-done.5.refs_7_
  110.0 11.4 %attend.3 = bf16[4,384,128]{2,1,0:T(8,128)(2,1)} custom-call(s32[3]{0:T(128)} %broadcast_maximum_fusion.2.place_ref, bf16[1,384,384]{2,1,0:T(8,128)(2,1)} %get-tuple-element.45.refs_0_, bf16[1,384,384]{2,1,0:T(8,128)(2,1)} %copy-done.10, bf16[1,384,384]{2,1,0:T(8,128)(2,1)} %copy-done.11, bf16[1,384,384]{2,1,0:T(8,128)(2,1)} %copy-done.12, ...), custom_call_target="tpu_custom_call" | custom-call | flops 2415919104 | bytes 3145728 | tf_op jit(solution)/shard_map/attend/pallas_call | solution.py:279
  121.4 1.5 all-to-all-done.2.refs_0_
  122.9 3.6 %all-to-all-start.1 = ((bf16[4,384,128]{2,1,0:T(8,128)(2,1)}), bf16[4,384,128]{2,1,0:T(8,128)(2,1)S(1)}, u32[]{:S(2)}, u32[]{:S(2)}) async-start(bf16[4,384,128]{2,1,0:T(8,128)(2,1)} %attend.3), calls=%async_computation.1 | async-start | bytes 786432 | tf_op jit(solution)/shard_map/all_to_all | solution.py:416
  126.6 0.1 collective-permute-start.10
  126.6 0.4 collective-permute-start.11
  127.1 0.5 broadcast_maximum_fusion.1.place_ref
  127.6 11.2 %attend.4 = bf16[4,384,128]{2,1,0:T(8,128)(2,1)} custom-call(s32[3]{0:T(128)} %broadcast_maximum_fusion.1.place_ref, bf16[4,2,384,128]{3,2,1,0:T(8,128)(2,1)} %copy-done.6, bf16[4,384,256]{2,1,0:T(8,128)(2,1)} %copy-done.5, bf16[4,384,256]{2,1,0:T(8,128)(2,1)} %collective-permute-done.7.refs_2_, bf16[4,384,256]{2,1,0:T(8,128)(2,1)} %collective-permute-done.8.refs_3_, ...), custom_call_target="tpu_custom_call" | custom-call | flops 2415919104 | bytes 3145728 | tf_op jit(solution)/shard_map/attend/pallas_call | solution.py:279
  138.8 5.1 %all-to-all-start.4 = ((bf16[4,384,128]{2,1,0:T(8,128)(2,1)}), bf16[4,384,128]{2,1,0:T(8,128)(2,1)S(1)}, u32[]{:S(2)}, u32[]{:S(2)}) async-start(bf16[4,384,128]{2,1,0:T(8,128)(2,1)} %attend.4), calls=%async_computation.4 | async-start | bytes 786432 | tf_op jit(solution)/shard_map/all_to_all | solution.py:416
  143.9 0.5 broadcast_maximum_fusion.place_ref
  144.4 11.3 %attend.5 = (bf16[1,384,128]{2,1,0:T(8,128)(2,1)}, bf16[1,384,128]{2,1,0:T(8,128)(2,1)}, bf16[1,384,128]{2,1,0:T(8,128)(2,1)}, bf16[1,384,128]{2,1,0:T(8,128)(2,1)}) custom-call(s32[3]{0:T(128)} %broadcast_maximum_fusion.place_ref, bf16[4,2,384,128]{3,2,1,0:T(8,128)(2,1)} %copy-done.6, bf16[4,384,256]{2,1,0:T(8,128)(2,1)} %copy-done.4, ...), custom_call_target="tpu_custom_call" | custom-call | flops 2415919104 | bytes 3145728 | tf_op jit(solution)/shard_map/attend/pallas_call | solution.py:279
  155.7 2.0 collective-permute-start.12
  157.7 2.4 %collective-permute-start.13 = (bf16[1,384,128]{2,1,0:T(8,128)(2,1)}, bf16[1,384,128]{2,1,0:T(8,128)(2,1)S(1)}, u32[]{:S(2)}, u32[]{:S(2)}) collective-permute-start(bf16[1,384,128]{2,1,0:T(8,128)(2,1)} %get-tuple-element.60), channel_id=1, source_target_pairs={{0,16},{2,18},{4,20},{6,22},{8,24},{10,26},{12,28},{14,30},{16,0},... | collective-permute-start | bytes 294920 | tf_op jit(solution)/shard_map/ppermute | solution.py:28
  160.1 0.1 collective-permute-start.14
  160.1 0.9 constant_dynamic-update-slice_fusion.3
  161.1 6.9 %collective-permute-done.13 = bf16[1,384,128]{2,1,0:T(8,128)(2,1)S(1)} collective-permute-done((bf16[1,384,128]{2,1,0:T(8,128)(2,1)}, bf16[1,384,128]{2,1,0:T(8,128)(2,1)S(1)}, u32[]{:S(2)}, u32[]{:S(2)}) %collective-permute-start.13) | collective-permute-done | bytes 98336 | tf_op jit(solution)/shard_map/ppermute | solution.py:28
  168.1 0.7 copy-done.2
  168.8 0.7 copy-done.1
  169.6 7.0 %finish.2 = bf16[384,1536]{1,0:T(8,128)(2,1)} custom-call(s32[3]{0:T(128)} %pad_add_fusion.place_ref, bf16[4,384,128]{2,1,0:T(8,128)(2,1)} %copy-done, bf16[4,384,128]{2,1,0:T(8,128)(2,1)} %copy-done.1, bf16[4,384,128]{2,1,0:T(8,128)(2,1)} %copy-done.2, bf16[1536,3072]{1,0:T(8,128)(2,1)} %refs_3_.5), custom_call_target="tpu_custom_call" | custom-call | flops 1811939328 | bytes 7077888 | tf_op jit(solution)/shard_map/finish/pallas_call | solution.py:343
  176.6 1.5 collective-permute-start.15
  178.1 7.1 %finish.3.mine_ref = bf16[384,1536]{1,0:T(8,128)(2,1)} custom-call(s32[3]{0:T(128)} %pad_add_fusion.place_ref, bf16[4,384,128]{2,1,0:T(8,128)(2,1)} %copy-done, bf16[4,384,128]{2,1,0:T(8,128)(2,1)} %copy-done.1, bf16[4,384,128]{2,1,0:T(8,128)(2,1)} %copy-done.2, bf16[1536,3072]{1,0:T(8,128)(2,1)} %refs_3_.5), custom_call_target="tpu_custom_call" | custom-call | flops 1811939328 | bytes 7077888 | tf_op jit(solution)/shard_map/finish/pallas_call | solution.py:343
  185.2 17.0 %collective-permute-done.15.refs_0_ = bf16[384,1536]{1,0:T(8,128)(2,1)S(1)} collective-permute-done((bf16[384,1536]{1,0:T(8,128)(2,1)}, bf16[384,1536]{1,0:T(8,128)(2,1)S(1)}, u32[]{:S(2)}, u32[]{:S(2)}) %collective-permute-start.15) | collective-permute-done | bytes 1179680 | tf_op jit(solution)/shard_map/ppermute | solution.py:28
  202.2 1.0 copy-done.3
  203.2 4.4 %close.1 = bf16[384,1536]{1,0:T(8,128)(2,1)} custom-call(bf16[384,384]{1,0:T(8,128)(2,1)} %get-tuple-element.34.back_ref, bf16[384,1536]{1,0:T(8,128)(2,1)} %finish.3.mine_ref, bf16[384,1536]{1,0:T(8,128)(2,1)} %copy-done.3), custom_call_target="tpu_custom_call" | custom-call | flops 452984832 | bytes 5898240 | tf_op jit(solution)/shard_map/close/pallas_call | solution.py:373
  (45 shorter events, 0.2 us)
Async XLA Ops:
  14.0 15.9 %collective-permute-start = (bf16[1,384,384]{2,1,0:T(8,128)(2,1)}, bf16[1,384,384]{2,1,0:T(8,128)(2,1)S(1)}, u32[]{:S(2)}, u32[]{:S(2)}) collective-permute-start(bf16[1,384,384]{2,1,0:T(8,128)(2,1)} %get-tuple-element.35), channel_id=1, source_target_pairs={{0,8},{2,10},{4,12},{6,14},{8,0},{10,2},{12,4},{14,6},{16,24},{18,... | collective-permute-start | bytes 884744 | tf_op jit(solution)/shard_map/ppermute | solution.py:28
  17.1 26.0 %collective-permute-start.1 = (bf16[1,384,384]{2,1,0:T(8,128)(2,1)}, bf16[1,384,384]{2,1,0:T(8,128)(2,1)S(1)}, u32[]{:S(2)}, u32[]{:S(2)}) collective-permute-start(bf16[1,384,384]{2,1,0:T(8,128)(2,1)} %get-tuple-element.36), channel_id=1, source_target_pairs={{0,16},{2,18},{4,20},{6,22},{8,24},{10,26},{12,28},{14,30},{16,0},... | collective-permute-start | bytes 884744 | tf_op jit(solution)/shard_map/ppermute | solution.py:28
  19.7 23.5 %collective-permute-start.2 = (bf16[1,384,384]{2,1,0:T(8,128)(2,1)}, bf16[1,384,384]{2,1,0:T(8,128)(2,1)S(1)}, u32[]{:S(2)}, u32[]{:S(2)}) collective-permute-start(bf16[1,384,384]{2,1,0:T(8,128)(2,1)} %get-tuple-element.37), channel_id=1, source_target_pairs={{0,24},{2,26},{4,28},{6,30},{8,16},{10,18},{12,20},{14,22},{16,8},... | collective-permute-start | bytes 884744 | tf_op jit(solution)/shard_map/ppermute | solution.py:28
  29.9 13.3 %copy-start.10 = (bf16[1,384,384]{2,1,0:T(8,128)(2,1)}, bf16[1,384,384]{2,1,0:T(8,128)(2,1)S(1)}, u32[]{:S(2)}) copy-start(bf16[1,384,384]{2,1,0:T(8,128)(2,1)S(1)} %collective-permute-done.refs_1_) | copy-start | bytes 884740
  29.9 13.4 %copy-start.9 = (bf16[1,384,384]{2,1,0:T(8,128)(2,1)S(1)}, bf16[1,384,384]{2,1,0:T(8,128)(2,1)}, u32[]{:S(2)}) copy-start(bf16[1,384,384]{2,1,0:T(8,128)(2,1)} %get-tuple-element.45.refs_0_) | copy-start | bytes 884740
  43.1 1.6 copy-start.8
  43.1 25.1 %copy-start.11 = (bf16[1,384,384]{2,1,0:T(8,128)(2,1)}, bf16[1,384,384]{2,1,0:T(8,128)(2,1)S(1)}, u32[]{:S(2)}) copy-start(bf16[1,384,384]{2,1,0:T(8,128)(2,1)S(1)} %collective-permute-done.1.refs_2_) | copy-start | bytes 884740
  43.1 25.1 %copy-start.12 = (bf16[1,384,384]{2,1,0:T(8,128)(2,1)}, bf16[1,384,384]{2,1,0:T(8,128)(2,1)S(1)}, u32[]{:S(2)}) copy-start(bf16[1,384,384]{2,1,0:T(8,128)(2,1)S(1)} %collective-permute-done.2.refs_3_) | copy-start | bytes 884740
  43.4 62.1 %copy-start.7 = (bf16[4,384,256]{2,1,0:T(8,128)(2,1)}, bf16[4,384,256]{2,1,0:T(8,128)(2,1)S(1)}, u32[]{:S(2)}) copy-start(bf16[4,384,256]{2,1,0:T(8,128)(2,1)S(1)} %pad_maximum_fusion.refs_4_) | copy-start | bytes 2359300
  68.3 38.3 %copy-start.5 = (bf16[4,384,256]{2,1,0:T(8,128)(2,1)}, bf16[4,384,256]{2,1,0:T(8,128)(2,1)S(1)}, u32[]{:S(2)}) copy-start(bf16[4,384,256]{2,1,0:T(8,128)(2,1)S(1)} %all_to_all.25.refs_1_) | copy-start | bytes 2359300
  68.3 32.7 %all-to-all-start.3 = ((bf16[4,384,256]{2,1,0:T(8,128)(2,1)}), bf16[4,384,256]{2,1,0:T(8,128)(2,1)S(1)}, u32[]{:S(2)}, u32[]{:S(2)}) async-start(bf16[4,384,256]{2,1,0:T(8,128)(2,1)} %bitcast.6), calls=%async_computation.3 | async-start | bytes 1572864 | tf_op jit(solution)/shard_map/all_to_all | solution.py:416
  72.0 18.2 %collective-permute-start.3 = (bf16[4,384,256]{2,1,0:T(8,128)(2,1)S(1)}, bf16[4,384,256]{2,1,0:T(8,128)(2,1)}, u32[]{:S(2)}, u32[]{:S(2)}) collective-permute-start(bf16[4,384,256]{2,1,0:T(8,128)(2,1)S(1)} %pad_maximum_fusion.refs_4_), channel_id=1, source_target_pairs={{0,4},{2,6},{4,0},{6,2},{8,12},{10,14},{12,8},{14,10},{16,20},{18,... | collective-permute-start | bytes 2359304 | tf_op jit(solution)/shard_map/ppermute | solution.py:28
  90.9 17.3 %copy-start.13 = (s32[3]{0:T(128)S(1)}, s32[3]{0:T(128)}, u32[]{:S(2)}) copy-start(s32[3]{0:T(128)} %pad_add_fusion.place_ref) | copy-start | bytes 40
  90.9 17.3 %collective-permute-start.8 = (bf16[4,384,256]{2,1,0:T(8,128)(2,1)S(1)}, bf16[4,384,256]{2,1,0:T(8,128)(2,1)}, u32[]{:S(2)}, u32[]{:S(2)}) collective-permute-start(bf16[4,384,256]{2,1,0:T(8,128)(2,1)S(1)} %all_to_all.25.refs_1_), channel_id=1, source_target_pairs={{0,4},{2,6},{4,0},{6,2},{8,12},{10,14},{12,8},{14,10},{16,20},{18,... | collective-permute-start | bytes 2359304 | tf_op jit(solution)/shard_map/ppermute | solution.py:28
  101.0 25.6 %copy-start.4 = (bf16[4,384,256]{2,1,0:T(8,128)(2,1)}, bf16[4,384,256]{2,1,0:T(8,128)(2,1)S(1)}, u32[]{:S(2)}) copy-start(bf16[4,384,256]{2,1,0:T(8,128)(2,1)S(1)} %all-to-all-done.3.refs_1_) | copy-start | bytes 2359300
  101.0 21.9 %all-to-all-start.2 = ((bf16[4,2,384,128]{3,2,1,0:T(8,128)(2,1)}), bf16[4,2,384,128]{3,2,1,0:T(8,128)(2,1)S(1)}, u32[]{:S(2)}, u32[]{:S(2)}) async-start(bf16[4,2,384,128]{3,2,1,0:T(8,128)(2,1)} %project.5), calls=%async_computation.2 | async-start | bytes 1572864 | tf_op jit(solution)/shard_map/all_to_all | solution.py:416
  105.5 3.2 %collective-permute-start.4 = (bf16[4,384,256]{2,1,0:T(8,128)(2,1)S(1)}, bf16[4,384,256]{2,1,0:T(8,128)(2,1)S(1)}, u32[]{:S(2)}, u32[]{:S(2)}) collective-permute-start(bf16[4,384,256]{2,1,0:T(8,128)(2,1)S(1)} %pad_maximum_fusion.refs_4_), channel_id=1, source_target_pairs={{0,2},{2,0},{4,6},{6,4},{8,10},{10,8},{12,14},{14,12},{16,18},{18,... | collective-permute-start | bytes 2359304 | tf_op jit(solution)/shard_map/ppermute | solution.py:28
  105.5 4.5 %collective-permute-start.5 = (bf16[4,384,256]{2,1,0:T(8,128)(2,1)}, bf16[4,384,256]{2,1,0:T(8,128)(2,1)}, u32[]{:S(2)}, u32[]{:S(2)}) collective-permute-start(bf16[4,384,256]{2,1,0:T(8,128)(2,1)} %collective-permute-done.3.refs_6_), channel_id=1, source_target_pairs={{0,2},{2,0},{4,6},{6,4},{8,10},{10,8},{12,14},{14,12},{16,18},{18,... | collective-permute-start | bytes 2359304 | tf_op jit(solution)/shard_map/ppermute | solution.py:28
  106.0 20.6 %collective-permute-start.6 = (bf16[4,384,256]{2,1,0:T(8,128)(2,1)S(1)}, bf16[4,384,256]{2,1,0:T(8,128)(2,1)}, u32[]{:S(2)}, u32[]{:S(2)}) collective-permute-start(bf16[4,384,256]{2,1,0:T(8,128)(2,1)S(1)} %all-to-all-done.3.refs_1_), channel_id=1, source_target_pairs={{0,4},{2,6},{4,0},{6,2},{8,12},{10,14},{12,8},{14,10},{16,20},{18,... | collective-permute-start | bytes 2359304 | tf_op jit(solution)/shard_map/ppermute | solution.py:28
  106.5 21.1 %collective-permute-start.7 = (bf16[4,384,256]{2,1,0:T(8,128)(2,1)S(1)}, bf16[4,384,256]{2,1,0:T(8,128)(2,1)}, u32[]{:S(2)}, u32[]{:S(2)}) collective-permute-start(bf16[4,384,256]{2,1,0:T(8,128)(2,1)S(1)} %all_to_all.25.refs_1_), channel_id=1, source_target_pairs={{0,2},{2,0},{4,6},{6,4},{8,10},{10,8},{12,14},{14,12},{16,18},{18,... | collective-permute-start | bytes 2359304 | tf_op jit(solution)/shard_map/ppermute | solution.py:28
  108.2 19.4 %collective-permute-start.9 = (bf16[4,384,256]{2,1,0:T(8,128)(2,1)}, bf16[4,384,256]{2,1,0:T(8,128)(2,1)}, u32[]{:S(2)}, u32[]{:S(2)}) collective-permute-start(bf16[4,384,256]{2,1,0:T(8,128)(2,1)} %collective-permute-done.8.refs_3_), channel_id=1, source_target_pairs={{0,2},{2,0},{4,6},{6,4},{8,10},{10,8},{12,14},{14,12},{16,18},{18,... | collective-permute-start | bytes 2359304 | tf_op jit(solution)/shard_map/ppermute | solution.py:28
  108.7 0.9 copy-start.14
  122.9 4.7 %copy-start.6 = (bf16[4,2,384,128]{3,2,1,0:T(8,128)(2,1)}, bf16[4,2,384,128]{3,2,1,0:T(8,128)(2,1)S(1)}, u32[]{:S(2)}) copy-start(bf16[4,2,384,128]{3,2,1,0:T(8,128)(2,1)S(1)} %all-to-all-done.2.refs_0_) | copy-start | bytes 2359300
  122.9 15.9 %all-to-all-start.1 = ((bf16[4,384,128]{2,1,0:T(8,128)(2,1)}), bf16[4,384,128]{2,1,0:T(8,128)(2,1)S(1)}, u32[]{:S(2)}, u32[]{:S(2)}) async-start(bf16[4,384,128]{2,1,0:T(8,128)(2,1)} %attend.3), calls=%async_computation.1 | async-start | bytes 786432 | tf_op jit(solution)/shard_map/all_to_all | solution.py:416
  126.6 17.8 %collective-permute-start.10 = (bf16[4,384,256]{2,1,0:T(8,128)(2,1)S(1)}, bf16[4,384,256]{2,1,0:T(8,128)(2,1)}, u32[]{:S(2)}, u32[]{:S(2)}) collective-permute-start(bf16[4,384,256]{2,1,0:T(8,128)(2,1)S(1)} %all-to-all-done.3.refs_1_), channel_id=1, source_target_pairs={{0,2},{2,0},{4,6},{6,4},{8,10},{10,8},{12,14},{14,12},{16,18},{18,... | collective-permute-start | bytes 2359304 | tf_op jit(solution)/shard_map/ppermute | solution.py:28
  126.6 17.7 %collective-permute-start.11 = (bf16[4,384,256]{2,1,0:T(8,128)(2,1)}, bf16[4,384,256]{2,1,0:T(8,128)(2,1)}, u32[]{:S(2)}, u32[]{:S(2)}) collective-permute-start(bf16[4,384,256]{2,1,0:T(8,128)(2,1)} %collective-permute-done.6.refs_3_), channel_id=1, source_target_pairs={{0,2},{2,0},{4,6},{6,4},{8,10},{10,8},{12,14},{14,12},{16,18},{18,... | collective-permute-start | bytes 2359304 | tf_op jit(solution)/shard_map/ppermute | solution.py:28
  138.8 16.9 %copy-start = (bf16[4,384,128]{2,1,0:T(8,128)(2,1)}, bf16[4,384,128]{2,1,0:T(8,128)(2,1)S(1)}, u32[]{:S(2)}) copy-start(bf16[4,384,128]{2,1,0:T(8,128)(2,1)S(1)} %all-to-all-done.1.refs_0_) | copy-start | bytes 1179652
  138.8 29.3 %all-to-all-start.4 = ((bf16[4,384,128]{2,1,0:T(8,128)(2,1)}), bf16[4,384,128]{2,1,0:T(8,128)(2,1)S(1)}, u32[]{:S(2)}, u32[]{:S(2)}) async-start(bf16[4,384,128]{2,1,0:T(8,128)(2,1)} %attend.4), calls=%async_computation.4 | async-start | bytes 786432 | tf_op jit(solution)/shard_map/all_to_all | solution.py:416
  155.7 5.4 %collective-permute-start.12 = (bf16[1,384,128]{2,1,0:T(8,128)(2,1)}, bf16[1,384,128]{2,1,0:T(8,128)(2,1)S(1)}, u32[]{:S(2)}, u32[]{:S(2)}) collective-permute-start(bf16[1,384,128]{2,1,0:T(8,128)(2,1)} %get-tuple-element.59), channel_id=1, source_target_pairs={{0,8},{2,10},{4,12},{6,14},{8,0},{10,2},{12,4},{14,6},{16,24},{18,... | collective-permute-start | bytes 294920 | tf_op jit(solution)/shard_map/ppermute | solution.py:28
  157.7 10.3 %collective-permute-start.13 = (bf16[1,384,128]{2,1,0:T(8,128)(2,1)}, bf16[1,384,128]{2,1,0:T(8,128)(2,1)S(1)}, u32[]{:S(2)}, u32[]{:S(2)}) collective-permute-start(bf16[1,384,128]{2,1,0:T(8,128)(2,1)} %get-tuple-element.60), channel_id=1, source_target_pairs={{0,16},{2,18},{4,20},{6,22},{8,24},{10,26},{12,28},{14,30},{16,0},... | collective-permute-start | bytes 294920 | tf_op jit(solution)/shard_map/ppermute | solution.py:28
  160.1 8.0 %collective-permute-start.14 = (bf16[1,384,128]{2,1,0:T(8,128)(2,1)}, bf16[1,384,128]{2,1,0:T(8,128)(2,1)S(1)}, u32[]{:S(2)}, u32[]{:S(2)}) collective-permute-start(bf16[1,384,128]{2,1,0:T(8,128)(2,1)} %get-tuple-element.61), channel_id=1, source_target_pairs={{0,24},{2,26},{4,28},{6,30},{8,16},{10,18},{12,20},{14,22},{16,8},... | collective-permute-start | bytes 294920 | tf_op jit(solution)/shard_map/ppermute | solution.py:28
  168.1 0.7 copy-start.2
  168.8 0.7 copy-start.1
  176.6 25.6 %collective-permute-start.15 = (bf16[384,1536]{1,0:T(8,128)(2,1)}, bf16[384,1536]{1,0:T(8,128)(2,1)S(1)}, u32[]{:S(2)}, u32[]{:S(2)}) collective-permute-start(bf16[384,1536]{1,0:T(8,128)(2,1)} %finish.2), channel_id=1, source_target_pairs={{0,1},{1,0},{2,3},{3,2},{4,5},{5,4},{6,7},{7,6},{8,9},{9,8},{10,11... | collective-permute-start | bytes 3538952 | tf_op jit(solution)/shard_map/ppermute | solution.py:28
  202.2 1.0 copy-start.3

commit v13 on v11

--- a/solution.py
+++ b/solution.py
@@ -95,8 +95,8 @@
                 packed = jnp.where(line < count_ref[0, 0], packed, dead_mark)
             result_ref[...] = packed.astype(bf16)
             for k in range(groups):
-                if joined:
-                    outs[k // groups][k, row] = result_ref[:, k * size : (k + 1) * size]
+                if joined and kind == 0:
+                    outs[-1][k, row] = result_ref[:, k * size : (k + 1) * size]
                 else:
                     start = pl.multiple_of(lax.bitwise_xor(plane, k) * size, size)
                     found = result_ref[:, pl.ds(start, size)]
@@ -131,7 +131,7 @@
         (len(which), rows, len(kinds) * size) for kinds, which in sets for _ in range(groups)
     ]
     if joined:
-        shapes = [(groups, len(sets[0][1]), rows, size)]
+        shapes = shapes[:-groups] + [(groups, len(sets[-1][1]), rows, size)]
     out_specs = [
         pl.BlockSpec(shape, lambda t, place, zeros=(0,) * len(shape): zeros) for shape in shapes
     ]
@@ -171,7 +171,8 @@
         name="project",
     )(place, weights, gains, *(first or prepared))
     if joined:
-        return found[0], []
+        blocks = [found[i * groups : (i + 1) * groups] for i in range(len(sets) - 1)]
+        return blocks, found[-1]
     blocks = [found[i * groups : (i + 1) * groups] for i in range(len(sets))]
     return blocks, found[len(sets) * groups :]
 
@@ -435,23 +436,16 @@
     rest, asked, hops = range(1, chunks), None, []
     if chunks > 1:
         prepared = (count, chain(normed, first(arrived[0])), chosen)
-        sets = [((1, 2), (chunk,)) for chunk in rest]
-        made, _ = project(place, prepared, weights, gains, sets, groups)
+        sets = [((1, 2), (chunk,)) for chunk in rest] + [((0,), tuple(rest))]
+        made, wanted = project(place, prepared, weights, gains, sets, groups, joined=True)
         stacks = [stack(list(chain(tuple(arrived[0]), made[0][0])))]
         arrived.append(send(made[0]))
         for blocks in made[1:]:
             arrived.append(send(blocks, first(arrived[-1])))
-        hop = flip(stacks[0], "seq", ring // 2) if ring > 1 else stacks[0]
-        stacks.append(stack(arrived[1]))
-        ready = later(count, hop, stacks[1])
-        sets = [((0,), tuple(rest))]
-        made, _ = project(
-            place, (ready, normed, chosen), weights, gains, sets, groups, joined=True
-        )
-        gate = made
-        stacks += [stack(list(chain(tuple(blocks), made))) for blocks in arrived[2:]]
-        asked = [send_back(made)]
-        hops = [flip(stacks[-1], "seq", ring // 2)] if ring > 1 else []
+        gate = stack(arrived[1])
+        stacks.append(gate)
+        asked = [send_back(chain(wanted, gate))]
+        hops = []
     else:
         gate, stacks = None, [stack(arrived[0])]
 
@@ -465,6 +459,10 @@
         row = max(chunk - 1, 0)
         found = attend(ready, query, row, low_lane, keyvals, shards, not final)
         attended.append(found[0])
+        if chunk == 0:
+            stacks += [stack(list(chain(tuple(blocks), found[0]))) for blocks in arrived[2:]]
+            if chunks > 1 and ring > 1:
+                hops = [flip(stacks[-1], "seq", ring // 2)]
         returned.append(jnp.concatenate(swap(found)) if final else send_back(found[0]))
         if not final:
             query, low_lane, gate = asked, 0, None

time: 190 us -> 198 us (1.042); the launches traced: 186 us -> 197 us
  waiting for transfers between devices: 44.2 us -> 68.8 us
  starting transfers between devices: 48.3 us -> 37.9 us
  Pallas kernels: 83.9 us -> 80.1 us
    ppermute x22, waiting for transfers between devices: 44.2 us -> 61.7 us  [flip(): return lax.ppermute(values, axis, [(i, i ^ mask) for i in range(size)])]
    all_to_all x3, starting transfers between devices: 21.3 us -> 10.8 us  [send_back(): lax.all_to_all(blocks, 'seq', split_axis=0, concat_axis=0, axis_index_gro...]
    all_to_all x3, waiting for transfers between devices: 0.01 us -> 7.15 us  [send_back(): lax.all_to_all(blocks, 'seq', split_axis=0, concat_axis=0, axis_index_gro...]
    pallas_call x3 -> x2, Pallas kernels: 35.5 us -> 31.5 us  [project(): pl.pallas_call(functools.partial(project_body, steps=steps, groups=groups...]
    unnamed x45 -> x49, local copies, waits for them, and re-layouts: 5.69 us -> 6.59 us
  transfers between devices with their start and end apart: 25 -> 25, of which waited for: 8 -> 10; matrix products, arithmetic and copies ran while one was open for 3% -> 3% of each run, Pallas kernels for 32% -> 28%
where the time goes in v13:
time: 198 us; the launch traced here: 197 us
  Pallas kernels  80.1 us (40%)
  waiting for transfers between devices  68.8 us (35%)
  starting transfers between devices  37.9 us (19%)
  local copies, waits for them, and re-layouts  7.36 us (4%)
  other arithmetic  2.23 us (1%)
    ppermute x22, waiting for transfers between devices, flip(): return lax.ppermute(values, axis, [(i, i ^ mask) for i in range(size)])  61.7 us
    pallas_call x2, Pallas kernels, project(): pl.pallas_call(functools.partial(project_body, steps=steps, groups=groups...  31.5 us
    pallas_call x3, Pallas kernels, attend(): pl.pallas_call(functools.partial(attend_body, groups=groups, asked=len(qu...  30.1 us
    ppermute x22, starting transfers between devices, flip(): return lax.ppermute(values, axis, [(i, i ^ mask) for i in range(size)])  27 us
    pallas_call x2, Pallas kernels, finish(): pl.pallas_call(functools.partial(finish_body, ordered=ordered), grid_spec...  14.1 us
    all_to_all x3, starting transfers between devices, send_back(): lax.all_to_all(blocks, 'seq', split_axis=0, concat_axis=0, axis_index_gro...  10.8 us
    all_to_all x3, waiting for transfers between devices, send_back(): lax.all_to_all(blocks, 'seq', split_axis=0, concat_axis=0, axis_index_gro...  7.15 us
    unnamed x49, local copies, waits for them, and re-layouts  6.59 us
  transfers between devices with their start and end apart: 25, of which 10 were waited for; matrix products, arithmetic and copies ran while one was open for 3% of the time, Pallas kernels for 28%

profile of v13, /device:TPU:0, one launch (start us, length us, event | category | flops | bytes accessed | tf_op | source)
XLA Modules:
  0.0 196.7 jit_solution(14701612862129950351)
XLA Ops:
  0.0 0.6 pad_add_fusion.place_ref
  0.6 13.4 %project.2 = (bf16[1,384,384]{2,1,0:T(8,128)(2,1)}, bf16[1,384,384]{2,1,0:T(8,128)(2,1)}, bf16[1,384,384]{2,1,0:T(8,128)(2,1)}, bf16[1,384,384]{2,1,0:T(8,128)(2...) custom-call(s32[3]{0:T(128)} %pad_add_fusion.place_ref, ...), custom_call_target="tpu_custom_call" | custom-call | flops 3623878656 | bytes 11796480 | tf_op jit(solution)/shard_map/project/pallas_call | solution.py:150
  14.0 3.1 %collective-permute-start = (bf16[1,384,384]{2,1,0:T(8,128)(2,1)}, bf16[1,384,384]{2,1,0:T(8,128)(2,1)S(1)}, u32[]{:S(2)}, u32[]{:S(2)}) collective-permute-start(bf16[1,384,384]{2,1,0:T(8,128)(2,1)} %get-tuple-element.47), channel_id=1, source_target_pairs={{0,8},{2,10},{4,12},{6,14},{8,0},{10,2},{12,4},{14,6},{16,24},{18,... | collective-permute-start | bytes 884744 | tf_op jit(solution)/shard_map/ppermute | solution.py:28
  17.0 2.6 %collective-permute-start.1 = (bf16[1,384,384]{2,1,0:T(8,128)(2,1)}, bf16[1,384,384]{2,1,0:T(8,128)(2,1)S(1)}, u32[]{:S(2)}, u32[]{:S(2)}) collective-permute-start(bf16[1,384,384]{2,1,0:T(8,128)(2,1)} %get-tuple-element.48), channel_id=1, source_target_pairs={{0,16},{2,18},{4,20},{6,22},{8,24},{10,26},{12,28},{14,30},{16,0},... | collective-permute-start | bytes 884744 | tf_op jit(solution)/shard_map/ppermute | solution.py:28
  19.6 10.2 %collective-permute-done.refs_1_ = bf16[1,384,384]{2,1,0:T(8,128)(2,1)S(1)} collective-permute-done((bf16[1,384,384]{2,1,0:T(8,128)(2,1)}, bf16[1,384,384]{2,1,0:T(8,128)(2,1)S(1)}, u32[]{:S(2)}, u32[]{:S(2)}) %collective-permute-start) | collective-permute-done | bytes 294944 | tf_op jit(solution)/shard_map/ppermute | solution.py:28
  29.8 18.1 %project.3 = (bf16[1,384,256]{2,1,0:T(8,128)(2,1)}, bf16[1,384,256]{2,1,0:T(8,128)(2,1)}, bf16[1,384,256]{2,1,0:T(8,128)(2,1)}, bf16[1,384,256]{2,1,0:T(8,128)(2...) custom-call(s32[3]{0:T(128)} %pad_add_fusion.place_ref, ...), custom_call_target="tpu_custom_call" | custom-call | flops 7247757312 | bytes 21233664 | tf_op jit(solution)/shard_map/project/pallas_call | solution.py:150
  48.3 1.8 collective-permute-start.7
  50.0 3.6 %collective-permute-start.4 = (bf16[1,384,256]{2,1,0:T(8,128)(2,1)S(1)}, bf16[1,384,256]{2,1,0:T(8,128)(2,1)S(1)}, u32[]{:S(2)}, u32[]{:S(2)}) collective-permute-start(bf16[1,384,256]{2,1,0:T(8,128)(2,1)S(1)} %copy-done.18), channel_id=1, source_target_pairs={{0,16},{2,18},{4,20},{6,22},{8,24},{10,26},{12,28},{14,30},{16,0},... | collective-permute-start | bytes 589832 | tf_op jit(solution)/shard_map/ppermute | solution.py:28
  53.6 0.8 collective-permute-start.5
  54.4 0.7 constant_dynamic-update-slice_fusion.3
  55.1 3.3 %collective-permute-done.3 = bf16[1,384,256]{2,1,0:T(8,128)(2,1)S(1)} collective-permute-done((bf16[1,384,256]{2,1,0:T(8,128)(2,1)S(1)}, bf16[1,384,256]{2,1,0:T(8,128)(2,1)S(1)}, u32[]{:S(2)}, u32[]{:S(2)}) %collective-permute-start.3) | collective-permute-done | bytes 196640 | tf_op jit(solution)/shard_map/ppermute | solution.py:28
  58.4 0.7 constant_dynamic-update-slice_fusion.2
  59.1 8.6 %collective-permute-done.4 = bf16[1,384,256]{2,1,0:T(8,128)(2,1)S(1)} collective-permute-done((bf16[1,384,256]{2,1,0:T(8,128)(2,1)S(1)}, bf16[1,384,256]{2,1,0:T(8,128)(2,1)S(1)}, u32[]{:S(2)}, u32[]{:S(2)}) %collective-permute-start.4) | collective-permute-done | bytes 196640 | tf_op jit(solution)/shard_map/ppermute | solution.py:28
  67.7 0.7 constant_dynamic-update-slice_fusion.1
  68.4 0.7 constant_dynamic-update-slice_fusion.refs_1_
  69.1 0.5 collective-permute-start.8
  69.6 0.8 collective-permute-start.14
  70.4 3.2 %collective-permute-start.10 = (bf16[1,384,256]{2,1,0:T(8,128)(2,1)}, bf16[1,384,256]{2,1,0:T(8,128)(2,1)S(1)}, u32[]{:S(2)}, u32[]{:S(2)}) collective-permute-start(bf16[1,384,256]{2,1,0:T(8,128)(2,1)} %get-tuple-element.74), channel_id=1, source_target_pairs={{0,16},{2,18},{4,20},{6,22},{8,24},{10,26},{12,28},{14,30},{16,0},... | collective-permute-start | bytes 589832 | tf_op jit(solution)/shard_map/ppermute | solution.py:28
  73.6 1.2 collective-permute-start.11
  74.8 3.9 %all-to-all-start.1 = ((bf16[4,2,384,128]{3,2,1,0:T(8,128)(2,1)}), bf16[4,2,384,128]{3,2,1,0:T(8,128)(2,1)S(1)}, u32[]{:S(2)}, u32[]{:S(2)}) async-start(bf16[4,2,384,128]{3,2,1,0:T(8,128)(2,1)} %get-tuple-element.67), calls=%async_computation.1 | async-start | bytes 1572864 | tf_op jit(solution)/shard_map/all_to_all | solution.py:414
  78.7 0.5 broadcast_maximum_fusion.2.place_ref
  79.3 2.1 %collective-permute-start.9 = (bf16[1,384,256]{2,1,0:T(8,128)(2,1)S(1)}, bf16[1,384,256]{2,1,0:T(8,128)(2,1)S(1)}, u32[]{:S(2)}, u32[]{:S(2)}) collective-permute-start(bf16[1,384,256]{2,1,0:T(8,128)(2,1)S(1)} %copy-done.15), channel_id=1, source_target_pairs={{0,8},{2,10},{4,12},{6,14},{8,0},{10,2},{12,4},{14,6},{16,24},{18,... | collective-permute-start | bytes 589832 | tf_op jit(solution)/shard_map/ppermute | solution.py:28
  81.4 0.9 copy-done.14
  82.3 10.3 %attend.3 = bf16[4,384,128]{2,1,0:T(8,128)(2,1)} custom-call(s32[3]{0:T(128)} %broadcast_maximum_fusion.2.place_ref, bf16[1,384,384]{2,1,0:T(8,128)(2,1)} %get-tuple-element.60.refs_0_, bf16[1,384,384]{2,1,0:T(8,128)(2,1)} %copy-done.9, bf16[1,384,384]{2,1,0:T(8,128)(2,1)} %copy-done.10, bf16[1,384,384]{2,1,0:T(8,128)(2,1)} %copy-done.11, ...), custom_call_target="tpu_custom_call" | custom-call | flops 2415919104 | bytes 3145728 | tf_op jit(solution)/shard_map/attend/pallas_call | solution.py:278
  92.6 0.7 collective-permute-done.10
  93.3 6.3 %collective-permute-done.9 = bf16[1,384,256]{2,1,0:T(8,128)(2,1)S(1)} collective-permute-done((bf16[1,384,256]{2,1,0:T(8,128)(2,1)S(1)}, bf16[1,384,256]{2,1,0:T(8,128)(2,1)S(1)}, u32[]{:S(2)}, u32[]{:S(2)}) %collective-permute-start.9) | collective-permute-done | bytes 196640 | tf_op jit(solution)/shard_map/ppermute | solution.py:28
  99.7 0.9 collective-permute-start.12
  100.6 0.5 collective-permute-start.15
  101.1 7.1 %all-to-all-done.1.refs_0_ = bf16[4,2,384,128]{3,2,1,0:T(8,128)(2,1)S(1)} async-done(((bf16[4,2,384,128]{3,2,1,0:T(8,128)(2,1)}), bf16[4,2,384,128]{3,2,1,0:T(8,128)(2,1)S(1)}, u32[]{:S(2)}, u32[]{:S(2)}) %all-to-all-start.1) | async-done | bytes 786464 | tf_op jit(solution)/shard_map/all_to_all | solution.py:414
  108.3 3.5 %all-to-all-start = ((bf16[4,384,128]{2,1,0:T(8,128)(2,1)}), bf16[4,384,128]{2,1,0:T(8,128)(2,1)S(1)}, u32[]{:S(2)}, u32[]{:S(2)}) async-start(bf16[4,384,128]{2,1,0:T(8,128)(2,1)} %attend.3), calls=%async_computation | async-start | bytes 786432 | tf_op jit(solution)/shard_map/all_to_all | solution.py:414
  111.8 7.3 %collective-permute-done.12.refs_3_ = bf16[4,384,256]{2,1,0:T(8,128)(2,1)} collective-permute-done((bf16[4,384,256]{2,1,0:T(8,128)(2,1)S(1)}, bf16[4,384,256]{2,1,0:T(8,128)(2,1)}, u32[]{:S(2)}, u32[]{:S(2)}) %collective-permute-start.12) | collective-permute-done | bytes 786464 | tf_op jit(solution)/shard_map/ppermute | solution.py:28
  119.1 0.5 broadcast_maximum_fusion.1.place_ref
  119.7 9.9 %attend.4 = bf16[4,384,128]{2,1,0:T(8,128)(2,1)} custom-call(s32[3]{0:T(128)} %broadcast_maximum_fusion.1.place_ref, bf16[4,2,384,128]{3,2,1,0:T(8,128)(2,1)} %copy-done.4, bf16[4,384,256]{2,1,0:T(8,128)(2,1)} %constant_dynamic-update-slice_fusion.refs_1_, bf16[4,384,256]{2,1,0:T(8,128)(2,1)} %collective-permute-done.13.refs_2_, ...), custom_call_target="tpu_custom_call" | custom-call | flops 2415919104 | bytes 3145728 | tf_op jit(solution)/shard_map/attend/pallas_call | solution.py:278
  129.6 3.5 %all-to-all-start.2 = ((bf16[4,384,128]{2,1,0:T(8,128)(2,1)}), bf16[4,384,128]{2,1,0:T(8,128)(2,1)S(1)}, u32[]{:S(2)}, u32[]{:S(2)}) async-start(bf16[4,384,128]{2,1,0:T(8,128)(2,1)} %attend.4), calls=%async_computation.2 | async-start | bytes 786432 | tf_op jit(solution)/shard_map/all_to_all | solution.py:414
  133.0 0.5 broadcast_maximum_fusion.place_ref
  133.6 9.8 %attend.5 = (bf16[1,384,128]{2,1,0:T(8,128)(2,1)}, bf16[1,384,128]{2,1,0:T(8,128)(2,1)}, bf16[1,384,128]{2,1,0:T(8,128)(2,1)}, bf16[1,384,128]{2,1,0:T(8,128)(2,1)}) custom-call(s32[3]{0:T(128)} %broadcast_maximum_fusion.place_ref, bf16[4,2,384,128]{3,2,1,0:T(8,128)(2,1)} %copy-done.4, bf16[4,384,256]{2,1,0:T(8,128)(2,1)} %copy-done.12, ...), custom_call_target="tpu_custom_call" | custom-call | flops 2415919104 | bytes 3145728 | tf_op jit(solution)/shard_map/attend/pallas_call | solution.py:278
  143.4 2.0 %collective-permute-start.18 = (bf16[1,384,128]{2,1,0:T(8,128)(2,1)}, bf16[1,384,128]{2,1,0:T(8,128)(2,1)S(1)}, u32[]{:S(2)}, u32[]{:S(2)}) collective-permute-start(bf16[1,384,128]{2,1,0:T(8,128)(2,1)} %get-tuple-element.83), channel_id=1, source_target_pairs={{0,8},{2,10},{4,12},{6,14},{8,0},{10,2},{12,4},{14,6},{16,24},{18,... | collective-permute-start | bytes 294920 | tf_op jit(solution)/shard_map/ppermute | solution.py:28
  145.4 2.4 %collective-permute-start.19 = (bf16[1,384,128]{2,1,0:T(8,128)(2,1)}, bf16[1,384,128]{2,1,0:T(8,128)(2,1)S(1)}, u32[]{:S(2)}, u32[]{:S(2)}) collective-permute-start(bf16[1,384,128]{2,1,0:T(8,128)(2,1)} %get-tuple-element.84), channel_id=1, source_target_pairs={{0,16},{2,18},{4,20},{6,22},{8,24},{10,26},{12,28},{14,30},{16,0},... | collective-permute-start | bytes 294920 | tf_op jit(solution)/shard_map/ppermute | solution.py:28
  147.9 0.9 constant_dynamic-update-slice_fusion.11
  148.9 7.5 %collective-permute-done.19 = bf16[1,384,128]{2,1,0:T(8,128)(2,1)S(1)} collective-permute-done((bf16[1,384,128]{2,1,0:T(8,128)(2,1)}, bf16[1,384,128]{2,1,0:T(8,128)(2,1)S(1)}, u32[]{:S(2)}, u32[]{:S(2)}) %collective-permute-start.19) | collective-permute-done | bytes 98336 | tf_op jit(solution)/shard_map/ppermute | solution.py:28
  156.4 0.7 copy-done.2
  157.2 0.8 copy-done.1
  157.9 7.0 %finish.2 = bf16[384,1536]{1,0:T(8,128)(2,1)} custom-call(s32[3]{0:T(128)} %pad_add_fusion.place_ref, bf16[4,384,128]{2,1,0:T(8,128)(2,1)} %copy-done, bf16[4,384,128]{2,1,0:T(8,128)(2,1)} %copy-done.1, bf16[4,384,128]{2,1,0:T(8,128)(2,1)} %copy-done.2, bf16[1536,3072]{1,0:T(8,128)(2,1)} %refs_3_.5), custom_call_target="tpu_custom_call" | custom-call | flops 1811939328 | bytes 7077888 | tf_op jit(solution)/shard_map/finish/pallas_call | solution.py:341
  165.0 1.5 collective-permute-start.21
  166.5 7.1 %finish.3.mine_ref = bf16[384,1536]{1,0:T(8,128)(2,1)} custom-call(s32[3]{0:T(128)} %pad_add_fusion.place_ref, bf16[4,384,128]{2,1,0:T(8,128)(2,1)} %copy-done, bf16[4,384,128]{2,1,0:T(8,128)(2,1)} %copy-done.1, bf16[4,384,128]{2,1,0:T(8,128)(2,1)} %copy-done.2, bf16[1536,3072]{1,0:T(8,128)(2,1)} %refs_3_.5), custom_call_target="tpu_custom_call" | custom-call | flops 1811939328 | bytes 7077888 | tf_op jit(solution)/shard_map/finish/pallas_call | solution.py:341
  173.6 17.7 %collective-permute-done.21.refs_0_ = bf16[384,1536]{1,0:T(8,128)(2,1)S(1)} collective-permute-done((bf16[384,1536]{1,0:T(8,128)(2,1)}, bf16[384,1536]{1,0:T(8,128)(2,1)S(1)}, u32[]{:S(2)}, u32[]{:S(2)}) %collective-permute-start.21) | collective-permute-done | bytes 1179680 | tf_op jit(solution)/shard_map/ppermute | solution.py:28
  191.2 1.0 copy-done.3
  192.3 4.4 %close.1 = bf16[384,1536]{1,0:T(8,128)(2,1)} custom-call(bf16[384,384]{1,0:T(8,128)(2,1)} %get-tuple-element.46.back_ref, bf16[384,1536]{1,0:T(8,128)(2,1)} %finish.3.mine_ref, bf16[384,1536]{1,0:T(8,128)(2,1)} %copy-done.3), custom_call_target="tpu_custom_call" | custom-call | flops 452984832 | bytes 5898240 | tf_op jit(solution)/shard_map/close/pallas_call | solution.py:371
  (71 shorter events, 0.6 us)
Async XLA Ops:
  14.0 15.9 %collective-permute-start = (bf16[1,384,384]{2,1,0:T(8,128)(2,1)}, bf16[1,384,384]{2,1,0:T(8,128)(2,1)S(1)}, u32[]{:S(2)}, u32[]{:S(2)}) collective-permute-start(bf16[1,384,384]{2,1,0:T(8,128)(2,1)} %get-tuple-element.47), channel_id=1, source_target_pairs={{0,8},{2,10},{4,12},{6,14},{8,0},{10,2},{12,4},{14,6},{16,24},{18,... | collective-permute-start | bytes 884744 | tf_op jit(solution)/shard_map/ppermute | solution.py:28
  17.0 30.9 %collective-permute-start.1 = (bf16[1,384,384]{2,1,0:T(8,128)(2,1)}, bf16[1,384,384]{2,1,0:T(8,128)(2,1)S(1)}, u32[]{:S(2)}, u32[]{:S(2)}) collective-permute-start(bf16[1,384,384]{2,1,0:T(8,128)(2,1)} %get-tuple-element.48), channel_id=1, source_target_pairs={{0,16},{2,18},{4,20},{6,22},{8,24},{10,26},{12,28},{14,30},{16,0},... | collective-permute-start | bytes 884744 | tf_op jit(solution)/shard_map/ppermute | solution.py:28
  19.6 28.4 %collective-permute-start.2 = (bf16[1,384,384]{2,1,0:T(8,128)(2,1)}, bf16[1,384,384]{2,1,0:T(8,128)(2,1)S(1)}, u32[]{:S(2)}, u32[]{:S(2)}) collective-permute-start(bf16[1,384,384]{2,1,0:T(8,128)(2,1)} %get-tuple-element.49), channel_id=1, source_target_pairs={{0,24},{2,26},{4,28},{6,30},{8,16},{10,18},{12,20},{14,22},{16,8},... | collective-permute-start | bytes 884744 | tf_op jit(solution)/shard_map/ppermute | solution.py:28
  29.8 18.2 %copy-start.9 = (bf16[1,384,384]{2,1,0:T(8,128)(2,1)}, bf16[1,384,384]{2,1,0:T(8,128)(2,1)S(1)}, u32[]{:S(2)}) copy-start(bf16[1,384,384]{2,1,0:T(8,128)(2,1)S(1)} %collective-permute-done.refs_1_) | copy-start | bytes 884740
  29.8 18.2 %copy-start.8 = (bf16[1,384,384]{2,1,0:T(8,128)(2,1)S(1)}, bf16[1,384,384]{2,1,0:T(8,128)(2,1)}, u32[]{:S(2)}) copy-start(bf16[1,384,384]{2,1,0:T(8,128)(2,1)} %get-tuple-element.60.refs_0_) | copy-start | bytes 884740
  47.9 2.1 %copy-start.19 = (bf16[1,384,256]{2,1,0:T(8,128)(2,1)S(1)}, bf16[1,384,256]{2,1,0:T(8,128)(2,1)}, u32[]{:S(2)}) copy-start(bf16[1,384,256]{2,1,0:T(8,128)(2,1)} %get-tuple-element.55) | copy-start | bytes 589828
  47.9 2.1 %copy-start.18 = (bf16[1,384,256]{2,1,0:T(8,128)(2,1)S(1)}, bf16[1,384,256]{2,1,0:T(8,128)(2,1)}, u32[]{:S(2)}) copy-start(bf16[1,384,256]{2,1,0:T(8,128)(2,1)} %get-tuple-element.56) | copy-start | bytes 589828
  48.0 5.7 %copy-start.17 = (bf16[1,384,256]{2,1,0:T(8,128)(2,1)S(1)}, bf16[1,384,256]{2,1,0:T(8,128)(2,1)}, u32[]{:S(2)}) copy-start(bf16[1,384,256]{2,1,0:T(8,128)(2,1)} %get-tuple-element.57) | copy-start | bytes 589828
  48.0 6.5 %copy-start.7 = (bf16[1,384,256]{2,1,0:T(8,128)(2,1)S(1)}, bf16[1,384,256]{2,1,0:T(8,128)(2,1)}, u32[]{:S(2)}) copy-start(bf16[1,384,256]{2,1,0:T(8,128)(2,1)} %get-tuple-element.54) | copy-start | bytes 589828
  48.0 21.1 %copy-start.10 = (bf16[1,384,384]{2,1,0:T(8,128)(2,1)}, bf16[1,384,384]{2,1,0:T(8,128)(2,1)S(1)}, u32[]{:S(2)}) copy-start(bf16[1,384,384]{2,1,0:T(8,128)(2,1)S(1)} %collective-permute-done.1.refs_2_) | copy-start | bytes 884740
  48.0 21.1 %copy-start.11 = (bf16[1,384,384]{2,1,0:T(8,128)(2,1)}, bf16[1,384,384]{2,1,0:T(8,128)(2,1)S(1)}, u32[]{:S(2)}) copy-start(bf16[1,384,384]{2,1,0:T(8,128)(2,1)S(1)} %collective-permute-done.2.refs_3_) | copy-start | bytes 884740
  48.0 25.6 %copy-start.16 = (bf16[1,384,256]{2,1,0:T(8,128)(2,1)S(1)}, bf16[1,384,256]{2,1,0:T(8,128)(2,1)}, u32[]{:S(2)}) copy-start(bf16[1,384,256]{2,1,0:T(8,128)(2,1)} %get-tuple-element.75) | copy-start | bytes 589828
  48.1 30.6 %copy-start.13 = (s32[3]{0:T(128)S(1)}, s32[3]{0:T(128)}, u32[]{:S(2)}) copy-start(s32[3]{0:T(128)} %pad_add_fusion.place_ref) | copy-start | bytes 40
  48.1 31.1 %copy-start.15 = (bf16[1,384,256]{2,1,0:T(8,128)(2,1)S(1)}, bf16[1,384,256]{2,1,0:T(8,128)(2,1)}, u32[]{:S(2)}) copy-start(bf16[1,384,256]{2,1,0:T(8,128)(2,1)} %get-tuple-element.73) | copy-start | bytes 589828
  48.3 33.1 %copy-start.5 = (bf16[4,384,256]{2,1,0:T(8,128)(2,1)}, bf16[4,384,256]{2,1,0:T(8,128)(2,1)S(1)}, u32[]{:S(2)}) copy-start(bf16[4,384,256]{2,1,0:T(8,128)(2,1)S(1)} %pad_maximum_fusion.refs_4_) | copy-start | bytes 2359300
  48.3 20.8 %collective-permute-start.7 = (bf16[4,384,256]{2,1,0:T(8,128)(2,1)S(1)}, bf16[4,384,256]{2,1,0:T(8,128)(2,1)}, u32[]{:S(2)}, u32[]{:S(2)}) collective-permute-start(bf16[4,384,256]{2,1,0:T(8,128)(2,1)S(1)} %pad_maximum_fusion.refs_4_), channel_id=1, source_target_pairs={{0,4},{2,6},{4,0},{6,2},{8,12},{10,14},{12,8},{14,10},{16,20},{18,... | collective-permute-start | bytes 2359304 | tf_op jit(solution)/shard_map/ppermute | solution.py:28
  50.0 8.4 %collective-permute-start.3 = (bf16[1,384,256]{2,1,0:T(8,128)(2,1)S(1)}, bf16[1,384,256]{2,1,0:T(8,128)(2,1)S(1)}, u32[]{:S(2)}, u32[]{:S(2)}) collective-permute-start(bf16[1,384,256]{2,1,0:T(8,128)(2,1)S(1)} %copy-done.19), channel_id=1, source_target_pairs={{0,8},{2,10},{4,12},{6,14},{8,0},{10,2},{12,4},{14,6},{16,24},{18,... | collective-permute-start | bytes 589832 | tf_op jit(solution)/shard_map/ppermute | solution.py:28
  50.0 17.6 %collective-permute-start.4 = (bf16[1,384,256]{2,1,0:T(8,128)(2,1)S(1)}, bf16[1,384,256]{2,1,0:T(8,128)(2,1)S(1)}, u32[]{:S(2)}, u32[]{:S(2)}) collective-permute-start(bf16[1,384,256]{2,1,0:T(8,128)(2,1)S(1)} %copy-done.18), channel_id=1, source_target_pairs={{0,16},{2,18},{4,20},{6,22},{8,24},{10,26},{12,28},{14,30},{16,0},... | collective-permute-start | bytes 589832 | tf_op jit(solution)/shard_map/ppermute | solution.py:28
  53.6 14.7 %collective-permute-start.5 = (bf16[1,384,256]{2,1,0:T(8,128)(2,1)S(1)}, bf16[1,384,256]{2,1,0:T(8,128)(2,1)S(1)}, u32[]{:S(2)}, u32[]{:S(2)}) collective-permute-start(bf16[1,384,256]{2,1,0:T(8,128)(2,1)S(1)} %copy-done.17), channel_id=1, source_target_pairs={{0,24},{2,26},{4,28},{6,30},{8,16},{10,18},{12,20},{14,22},{16,8},... | collective-permute-start | bytes 589832 | tf_op jit(solution)/shard_map/ppermute | solution.py:28
  69.1 10.2 %collective-permute-start.6 = (bf16[4,384,256]{2,1,0:T(8,128)(2,1)S(1)}, bf16[4,384,256]{2,1,0:T(8,128)(2,1)}, u32[]{:S(2)}, u32[]{:S(2)}) collective-permute-start(bf16[4,384,256]{2,1,0:T(8,128)(2,1)S(1)} %pad_maximum_fusion.refs_4_), channel_id=1, source_target_pairs={{0,2},{2,0},{4,6},{6,4},{8,10},{10,8},{12,14},{14,12},{16,18},{18,... | collective-permute-start | bytes 2359304 | tf_op jit(solution)/shard_map/ppermute | solution.py:28
  69.1 12.3 %collective-permute-start.8 = (bf16[4,384,256]{2,1,0:T(8,128)(2,1)}, bf16[4,384,256]{2,1,0:T(8,128)(2,1)S(1)}, u32[]{:S(2)}, u32[]{:S(2)}) collective-permute-start(bf16[4,384,256]{2,1,0:T(8,128)(2,1)} %collective-permute-done.7.refs_6_), channel_id=1, source_target_pairs={{0,2},{2,0},{4,6},{6,4},{8,10},{10,8},{12,14},{14,12},{16,18},{18,... | collective-permute-start | bytes 2359304 | tf_op jit(solution)/shard_map/ppermute | solution.py:28
  69.6 31.0 %collective-permute-start.14 = (bf16[4,384,256]{2,1,0:T(8,128)(2,1)}, bf16[4,384,256]{2,1,0:T(8,128)(2,1)}, u32[]{:S(2)}, u32[]{:S(2)}) collective-permute-start(bf16[4,384,256]{2,1,0:T(8,128)(2,1)} %constant_dynamic-update-slice_fusion.refs_1_), channel_id=1, source_target_pairs={{0,4},{2,6},{4,0},{6,2},{8,12},{10,14},{12,8},{14,10},{16,20},{18,... | collective-permute-start | bytes 2359304 | tf_op jit(solution)/shard_map/ppermute | solution.py:28
  70.4 22.9 %collective-permute-start.10 = (bf16[1,384,256]{2,1,0:T(8,128)(2,1)}, bf16[1,384,256]{2,1,0:T(8,128)(2,1)S(1)}, u32[]{:S(2)}, u32[]{:S(2)}) collective-permute-start(bf16[1,384,256]{2,1,0:T(8,128)(2,1)} %get-tuple-element.74), channel_id=1, source_target_pairs={{0,16},{2,18},{4,20},{6,22},{8,24},{10,26},{12,28},{14,30},{16,0},... | collective-permute-start | bytes 589832 | tf_op jit(solution)/shard_map/ppermute | solution.py:28
  73.6 19.7 %collective-permute-start.11 = (bf16[1,384,256]{2,1,0:T(8,128)(2,1)S(1)}, bf16[1,384,256]{2,1,0:T(8,128)(2,1)S(1)}, u32[]{:S(2)}, u32[]{:S(2)}) collective-permute-start(bf16[1,384,256]{2,1,0:T(8,128)(2,1)S(1)} %copy-done.16), channel_id=1, source_target_pairs={{0,24},{2,26},{4,28},{6,30},{8,16},{10,18},{12,20},{14,22},{16,8},... | collective-permute-start | bytes 589832 | tf_op jit(solution)/shard_map/ppermute | solution.py:28
  74.8 33.4 %all-to-all-start.1 = ((bf16[4,2,384,128]{3,2,1,0:T(8,128)(2,1)}), bf16[4,2,384,128]{3,2,1,0:T(8,128)(2,1)S(1)}, u32[]{:S(2)}, u32[]{:S(2)}) async-start(bf16[4,2,384,128]{3,2,1,0:T(8,128)(2,1)} %get-tuple-element.67), calls=%async_computation.1 | async-start | bytes 1572864 | tf_op jit(solution)/shard_map/all_to_all | solution.py:414
  79.3 20.3 %copy-start.6 = (bf16[1,384,256]{2,1,0:T(8,128)(2,1)S(1)}, bf16[1,384,256]{2,1,0:T(8,128)(2,1)}, u32[]{:S(2)}) copy-start(bf16[1,384,256]{2,1,0:T(8,128)(2,1)} %get-tuple-element.76) | copy-start | bytes 589828
  79.3 20.3 %collective-permute-start.9 = (bf16[1,384,256]{2,1,0:T(8,128)(2,1)S(1)}, bf16[1,384,256]{2,1,0:T(8,128)(2,1)S(1)}, u32[]{:S(2)}, u32[]{:S(2)}) collective-permute-start(bf16[1,384,256]{2,1,0:T(8,128)(2,1)S(1)} %copy-done.15), channel_id=1, source_target_pairs={{0,8},{2,10},{4,12},{6,14},{8,0},{10,2},{12,4},{14,6},{16,24},{18,... | collective-permute-start | bytes 589832 | tf_op jit(solution)/shard_map/ppermute | solution.py:28
  81.4 0.9 copy-start.14
  99.7 33.9 %copy-start.12 = (bf16[4,384,256]{2,1,0:T(8,128)(2,1)}, bf16[4,384,256]{2,1,0:T(8,128)(2,1)S(1)}, u32[]{:S(2)}) copy-start(bf16[4,384,256]{2,1,0:T(8,128)(2,1)S(1)} %constant_dynamic-update-slice_fusion.4.refs_1_) | copy-start | bytes 2359300
  99.7 19.4 %collective-permute-start.12 = (bf16[4,384,256]{2,1,0:T(8,128)(2,1)S(1)}, bf16[4,384,256]{2,1,0:T(8,128)(2,1)}, u32[]{:S(2)}, u32[]{:S(2)}) collective-permute-start(bf16[4,384,256]{2,1,0:T(8,128)(2,1)S(1)} %constant_dynamic-update-slice_fusion.4.refs_1_), channel_id=1, source_target_pairs={{0,4},{2,6},{4,0},{6,2},{8,12},{10,14},{12,8},{14,10},{16,20},{18,... | collective-permute-start | bytes 2359304 | tf_op jit(solution)/shard_map/ppermute | solution.py:28
  100.6 19.1 %collective-permute-start.13 = (bf16[4,384,256]{2,1,0:T(8,128)(2,1)}, bf16[4,384,256]{2,1,0:T(8,128)(2,1)}, u32[]{:S(2)}, u32[]{:S(2)}) collective-permute-start(bf16[4,384,256]{2,1,0:T(8,128)(2,1)} %constant_dynamic-update-slice_fusion.refs_1_), channel_id=1, source_target_pairs={{0,2},{2,0},{4,6},{6,4},{8,10},{10,8},{12,14},{14,12},{16,18},{18,... | collective-permute-start | bytes 2359304 | tf_op jit(solution)/shard_map/ppermute | solution.py:28
  100.6 19.1 %collective-permute-start.15 = (bf16[4,384,256]{2,1,0:T(8,128)(2,1)}, bf16[4,384,256]{2,1,0:T(8,128)(2,1)}, u32[]{:S(2)}, u32[]{:S(2)}) collective-permute-start(bf16[4,384,256]{2,1,0:T(8,128)(2,1)} %collective-permute-done.14.refs_3_), channel_id=1, source_target_pairs={{0,2},{2,0},{4,6},{6,4},{8,10},{10,8},{12,14},{14,12},{16,18},{18,... | collective-permute-start | bytes 2359304 | tf_op jit(solution)/shard_map/ppermute | solution.py:28
  108.3 11.4 %copy-start.4 = (bf16[4,2,384,128]{3,2,1,0:T(8,128)(2,1)}, bf16[4,2,384,128]{3,2,1,0:T(8,128)(2,1)S(1)}, u32[]{:S(2)}) copy-start(bf16[4,2,384,128]{3,2,1,0:T(8,128)(2,1)S(1)} %all-to-all-done.1.refs_0_) | copy-start | bytes 2359300
  108.3 21.3 %all-to-all-start = ((bf16[4,384,128]{2,1,0:T(8,128)(2,1)}), bf16[4,384,128]{2,1,0:T(8,128)(2,1)S(1)}, u32[]{:S(2)}, u32[]{:S(2)}) async-start(bf16[4,384,128]{2,1,0:T(8,128)(2,1)} %attend.3), calls=%async_computation | async-start | bytes 786432 | tf_op jit(solution)/shard_map/all_to_all | solution.py:414
  111.7 21.9 %collective-permute-start.16 = (bf16[4,384,256]{2,1,0:T(8,128)(2,1)S(1)}, bf16[4,384,256]{2,1,0:T(8,128)(2,1)}, u32[]{:S(2)}, u32[]{:S(2)}) collective-permute-start(bf16[4,384,256]{2,1,0:T(8,128)(2,1)S(1)} %constant_dynamic-update-slice_fusion.4.refs_1_), channel_id=1, source_target_pairs={{0,2},{2,0},{4,6},{6,4},{8,10},{10,8},{12,14},{14,12},{16,18},{18,... | collective-permute-start | bytes 2359304 | tf_op jit(solution)/shard_map/ppermute | solution.py:28
  119.1 14.4 %collective-permute-start.17 = (bf16[4,384,256]{2,1,0:T(8,128)(2,1)}, bf16[4,384,256]{2,1,0:T(8,128)(2,1)}, u32[]{:S(2)}, u32[]{:S(2)}) collective-permute-start(bf16[4,384,256]{2,1,0:T(8,128)(2,1)} %collective-permute-done.12.refs_3_), channel_id=1, source_target_pairs={{0,2},{2,0},{4,6},{6,4},{8,10},{10,8},{12,14},{14,12},{16,18},{18,... | collective-permute-start | bytes 2359304 | tf_op jit(solution)/shard_map/ppermute | solution.py:28
  129.6 13.9 %copy-start = (bf16[4,384,128]{2,1,0:T(8,128)(2,1)}, bf16[4,384,128]{2,1,0:T(8,128)(2,1)S(1)}, u32[]{:S(2)}) copy-start(bf16[4,384,128]{2,1,0:T(8,128)(2,1)S(1)} %all-to-all-done.refs_0_) | copy-start | bytes 1179652
  129.6 26.8 %all-to-all-start.2 = ((bf16[4,384,128]{2,1,0:T(8,128)(2,1)}), bf16[4,384,128]{2,1,0:T(8,128)(2,1)S(1)}, u32[]{:S(2)}, u32[]{:S(2)}) async-start(bf16[4,384,128]{2,1,0:T(8,128)(2,1)} %attend.4), calls=%async_computation.2 | async-start | bytes 786432 | tf_op jit(solution)/shard_map/all_to_all | solution.py:414
  143.4 5.4 %collective-permute-start.18 = (bf16[1,384,128]{2,1,0:T(8,128)(2,1)}, bf16[1,384,128]{2,1,0:T(8,128)(2,1)S(1)}, u32[]{:S(2)}, u32[]{:S(2)}) collective-permute-start(bf16[1,384,128]{2,1,0:T(8,128)(2,1)} %get-tuple-element.83), channel_id=1, source_target_pairs={{0,8},{2,10},{4,12},{6,14},{8,0},{10,2},{12,4},{14,6},{16,24},{18,... | collective-permute-start | bytes 294920 | tf_op jit(solution)/shard_map/ppermute | solution.py:28
  145.4 10.9 %collective-permute-start.19 = (bf16[1,384,128]{2,1,0:T(8,128)(2,1)}, bf16[1,384,128]{2,1,0:T(8,128)(2,1)S(1)}, u32[]{:S(2)}, u32[]{:S(2)}) collective-permute-start(bf16[1,384,128]{2,1,0:T(8,128)(2,1)} %get-tuple-element.84), channel_id=1, source_target_pairs={{0,16},{2,18},{4,20},{6,22},{8,24},{10,26},{12,28},{14,30},{16,0},... | collective-permute-start | bytes 294920 | tf_op jit(solution)/shard_map/ppermute | solution.py:28
  147.8 8.6 %collective-permute-start.20 = (bf16[1,384,128]{2,1,0:T(8,128)(2,1)}, bf16[1,384,128]{2,1,0:T(8,128)(2,1)S(1)}, u32[]{:S(2)}, u32[]{:S(2)}) collective-permute-start(bf16[1,384,128]{2,1,0:T(8,128)(2,1)} %get-tuple-element.85), channel_id=1, source_target_pairs={{0,24},{2,26},{4,28},{6,30},{8,16},{10,18},{12,20},{14,22},{16,8},... | collective-permute-start | bytes 294920 | tf_op jit(solution)/shard_map/ppermute | solution.py:28
  156.4 0.8 copy-start.2
  157.2 0.8 copy-start.1
  165.0 26.3 %collective-permute-start.21 = (bf16[384,1536]{1,0:T(8,128)(2,1)}, bf16[384,1536]{1,0:T(8,128)(2,1)S(1)}, u32[]{:S(2)}, u32[]{:S(2)}) collective-permute-start(bf16[384,1536]{1,0:T(8,128)(2,1)} %finish.2), channel_id=1, source_target_pairs={{0,1},{1,0},{2,3},{3,2},{4,5},{5,4},{6,7},{7,6},{8,9},{9,8},{10,11... | collective-permute-start | bytes 3538952 | tf_op jit(solution)/shard_map/ppermute | solution.py:28
  191.2 1.0 copy-start.3

commit v14 on v11

--- a/solution.py
+++ b/solution.py
@@ -448,7 +448,7 @@
         made, _ = project(
             place, (ready, normed, chosen), weights, gains, sets, groups, joined=True
         )
-        gate = made
+        gate = None
         stacks += [stack(list(chain(tuple(blocks), made))) for blocks in arrived[2:]]
         asked = [send_back(made)]
         hops = [flip(stacks[-1], "seq", ring // 2)] if ring > 1 else []

time: 190 us -> 193 us (1.016); the launches traced: 186 us -> 193 us
  waiting for transfers between devices: 44.2 us -> 56.4 us
  Pallas kernels: 83.9 us -> 80.2 us
    all_to_all x3, waiting for transfers between devices: 0.01 us -> 8.98 us  [send_back(): lax.all_to_all(blocks, 'seq', split_axis=0, concat_axis=0, axis_index_gro...]
    pallas_call x3, Pallas kernels: 29.9 us -> 26.1 us  [attend(): pl.pallas_call(functools.partial(attend_body, groups=groups, asked=len(qu...]
    ppermute x22, waiting for transfers between devices: 44.2 us -> 47.4 us  [flip(): return lax.ppermute(values, axis, [(i, i ^ mask) for i in range(size)])]
  transfers between devices with their start and end apart: 25 -> 25, of which waited for: 8 -> 8; matrix products, arithmetic and copies ran while one was open for 3% -> 3% of each run, Pallas kernels for 32% -> 29%
where the time goes in v14:
time: 193 us
  Pallas kernels  80.2 us (42%)
  waiting for transfers between devices  56.4 us (29%)
  starting transfers between devices  47.1 us (24%)
  local copies, waits for them, and re-layouts  6.47 us (3%)
  other arithmetic  2.34 us (1%)
    ppermute x22, waiting for transfers between devices, flip(): return lax.ppermute(values, axis, [(i, i ^ mask) for i in range(size)])  47.4 us
    pallas_call x3, Pallas kernels, project(): pl.pallas_call(functools.partial(project_body, steps=steps, groups=groups...  35.5 us
    ppermute x22, starting transfers between devices, flip(): return lax.ppermute(values, axis, [(i, i ^ mask) for i in range(size)])  27 us
    pallas_call x3, Pallas kernels, attend(): pl.pallas_call(functools.partial(attend_body, groups=groups, asked=len(qu...  26.1 us
    all_to_all x3, starting transfers between devices, send_back(): lax.all_to_all(blocks, 'seq', split_axis=0, concat_axis=0, axis_index_gro...  20.2 us
    pallas_call x2, Pallas kernels, finish(): pl.pallas_call(functools.partial(finish_body, ordered=ordered), grid_spec...  14.2 us
    all_to_all x3, waiting for transfers between devices, send_back(): lax.all_to_all(blocks, 'seq', split_axis=0, concat_axis=0, axis_index_gro...  8.98 us
    unnamed x45, local copies, waits for them, and re-layouts  5.71 us
  transfers between devices with their start and end apart: 25, of which 8 were waited for; matrix products, arithmetic and copies ran while one was open for 3% of the time, Pallas kernels for 29%

profile of v14, /device:TPU:0, one launch (start us, length us, event | category | flops | bytes accessed | tf_op | source)
XLA Modules:
  0.0 193.4 jit_solution(262892807857046828)
XLA Ops:
  0.0 0.6 pad_add_fusion.place_ref
  0.6 13.4 %project.3 = (bf16[1,384,384]{2,1,0:T(8,128)(2,1)}, bf16[1,384,384]{2,1,0:T(8,128)(2,1)}, bf16[1,384,384]{2,1,0:T(8,128)(2,1)}, bf16[1,384,384]{2,1,0:T(8,128)(2...) custom-call(s32[3]{0:T(128)} %pad_add_fusion.place_ref, ...), custom_call_target="tpu_custom_call" | custom-call | flops 3623878656 | bytes 11796480 | tf_op jit(solution)/shard_map/project/pallas_call | solution.py:150
  14.1 3.1 %collective-permute-start = (bf16[1,384,384]{2,1,0:T(8,128)(2,1)}, bf16[1,384,384]{2,1,0:T(8,128)(2,1)S(1)}, u32[]{:S(2)}, u32[]{:S(2)}) collective-permute-start(bf16[1,384,384]{2,1,0:T(8,128)(2,1)} %get-tuple-element.44), channel_id=1, source_target_pairs={{0,8},{2,10},{4,12},{6,14},{8,0},{10,2},{12,4},{14,6},{16,24},{18,... | collective-permute-start | bytes 884744 | tf_op jit(solution)/shard_map/ppermute | solution.py:28
  17.2 2.6 %collective-permute-start.1 = (bf16[1,384,384]{2,1,0:T(8,128)(2,1)}, bf16[1,384,384]{2,1,0:T(8,128)(2,1)S(1)}, u32[]{:S(2)}, u32[]{:S(2)}) collective-permute-start(bf16[1,384,384]{2,1,0:T(8,128)(2,1)} %get-tuple-element.45), channel_id=1, source_target_pairs={{0,16},{2,18},{4,20},{6,22},{8,24},{10,26},{12,28},{14,30},{16,0},... | collective-permute-start | bytes 884744 | tf_op jit(solution)/shard_map/ppermute | solution.py:28
  19.8 10.2 %collective-permute-done.refs_1_ = bf16[1,384,384]{2,1,0:T(8,128)(2,1)S(1)} collective-permute-done((bf16[1,384,384]{2,1,0:T(8,128)(2,1)}, bf16[1,384,384]{2,1,0:T(8,128)(2,1)S(1)}, u32[]{:S(2)}, u32[]{:S(2)}) %collective-permute-start) | collective-permute-done | bytes 294944 | tf_op jit(solution)/shard_map/ppermute | solution.py:28
  29.9 13.2 %project.4 = (bf16[1,384,256]{2,1,0:T(8,128)(2,1)}, bf16[1,384,256]{2,1,0:T(8,128)(2,1)}, bf16[1,384,256]{2,1,0:T(8,128)(2,1)}, bf16[1,384,256]{2,1,0:T(8,128)(2...) custom-call(s32[3]{0:T(128)} %pad_add_fusion.place_ref, ...), custom_call_target="tpu_custom_call" | custom-call | flops 4831838208 | bytes 14942208 | tf_op jit(solution)/shard_map/project/pallas_call | solution.py:150
  43.5 1.8 collective-permute-start.7
  45.2 2.9 %collective-permute-start.3 = (bf16[1,384,256]{2,1,0:T(8,128)(2,1)S(1)}, bf16[1,384,256]{2,1,0:T(8,128)(2,1)S(1)}, u32[]{:S(2)}, u32[]{:S(2)}) collective-permute-start(bf16[1,384,256]{2,1,0:T(8,128)(2,1)S(1)} %copy-done.17), channel_id=1, source_target_pairs={{0,8},{2,10},{4,12},{6,14},{8,0},{10,2},{12,4},{14,6},{16,24},{18,... | collective-permute-start | bytes 589832 | tf_op jit(solution)/shard_map/ppermute | solution.py:28
  48.1 1.1 collective-permute-start.8
  49.2 1.5 collective-permute-start.9
  50.7 0.7 constant_dynamic-update-slice_fusion.3
  51.4 1.5 collective-permute-done.3
  52.9 2.5 %collective-permute-start.4 = (bf16[1,384,256]{2,1,0:T(8,128)(2,1)}, bf16[1,384,256]{2,1,0:T(8,128)(2,1)S(1)}, u32[]{:S(2)}, u32[]{:S(2)}) collective-permute-start(bf16[1,384,256]{2,1,0:T(8,128)(2,1)} %get-tuple-element.57), channel_id=1, source_target_pairs={{0,8},{2,10},{4,12},{6,14},{8,0},{10,2},{12,4},{14,6},{16,24},{18,... | collective-permute-start | bytes 589832 | tf_op jit(solution)/shard_map/ppermute | solution.py:28
  55.4 0.7 constant_dynamic-update-slice_fusion.2
  56.1 8.7 %collective-permute-done.8 = bf16[1,384,256]{2,1,0:T(8,128)(2,1)S(1)} collective-permute-done((bf16[1,384,256]{2,1,0:T(8,128)(2,1)S(1)}, bf16[1,384,256]{2,1,0:T(8,128)(2,1)S(1)}, u32[]{:S(2)}, u32[]{:S(2)}) %collective-permute-start.8) | collective-permute-done | bytes 196640 | tf_op jit(solution)/shard_map/ppermute | solution.py:28
  64.8 0.7 constant_dynamic-update-slice_fusion.1
  65.5 2.4 %collective-permute-start.6 = (bf16[1,384,256]{2,1,0:T(8,128)(2,1)}, bf16[1,384,256]{2,1,0:T(8,128)(2,1)S(1)}, u32[]{:S(2)}, u32[]{:S(2)}) collective-permute-start(bf16[1,384,256]{2,1,0:T(8,128)(2,1)} %get-tuple-element.59), channel_id=1, source_target_pairs={{0,24},{2,26},{4,28},{6,30},{8,16},{10,18},{12,20},{14,22},{16,8},... | collective-permute-start | bytes 589832 | tf_op jit(solution)/shard_map/ppermute | solution.py:28
  67.9 0.7 constant_dynamic-update-slice_fusion.refs_1_
  68.6 0.6 collective-permute-start.14
  69.8 8.8 %project.5 = bf16[4,2,384,128]{3,2,1,0:T(8,128)(2,1)} custom-call(s32[3]{0:T(128)} %pad_add_fusion.place_ref, bf16[3,3072,1536]{2,1,0:T(8,128)(2,1)} %bitcast.7, f32[12,2,128]{2,1,0:T(2,128)} %bitcast.10, s32[1,1]{1,0:T(1,128)S(6)} %max.12.refs_2_, bf16[384,3072]{1,0:T(8,128)(2,1)} %get-tuple-element.49.refs_3_, bf16[384,384]{1,0:T(8,128)(2,1)} %get-tuple-element.50.refs_4_), custom_call_target="tpu_custom_call" | custom-call | flops 2415919104 | bytes 8650752 | tf_op jit(solution)/shard_map/project/pallas_call | solution.py:150
  78.6 13.0 %all-to-all-start.1 = ((bf16[4,2,384,128]{3,2,1,0:T(8,128)(2,1)}), bf16[4,2,384,128]{3,2,1,0:T(8,128)(2,1)S(1)}, u32[]{:S(2)}, u32[]{:S(2)}) async-start(bf16[4,2,384,128]{3,2,1,0:T(8,128)(2,1)} %project.5), calls=%async_computation.1 | async-start | bytes 1572864 | tf_op jit(solution)/shard_map/all_to_all | solution.py:413
  91.8 1.6 collective-permute-start.12
  93.4 0.2 collective-permute-start.13
  93.6 0.3 collective-permute-start.15
  93.9 0.5 broadcast_maximum_fusion.2.place_ref
  94.4 8.9 %attend.3 = bf16[4,384,128]{2,1,0:T(8,128)(2,1)} custom-call(s32[3]{0:T(128)} %broadcast_maximum_fusion.2.place_ref, bf16[1,384,384]{2,1,0:T(8,128)(2,1)} %get-tuple-element.62.refs_0_, bf16[1,384,384]{2,1,0:T(8,128)(2,1)} %copy-done.9, bf16[1,384,384]{2,1,0:T(8,128)(2,1)} %copy-done.10, bf16[1,384,384]{2,1,0:T(8,128)(2,1)} %copy-done.11, ...), custom_call_target="tpu_custom_call" | custom-call | flops 2415919104 | bytes 3145728 | tf_op jit(solution)/shard_map/attend/pallas_call | solution.py:277
  103.3 7.6 %all-to-all-done.1.refs_0_ = bf16[4,2,384,128]{3,2,1,0:T(8,128)(2,1)S(1)} async-done(((bf16[4,2,384,128]{3,2,1,0:T(8,128)(2,1)}), bf16[4,2,384,128]{3,2,1,0:T(8,128)(2,1)S(1)}, u32[]{:S(2)}, u32[]{:S(2)}) %all-to-all-start.1) | async-done | bytes 786464 | tf_op jit(solution)/shard_map/all_to_all | solution.py:413
  111.0 3.5 %all-to-all-start = ((bf16[4,384,128]{2,1,0:T(8,128)(2,1)}), bf16[4,384,128]{2,1,0:T(8,128)(2,1)S(1)}, u32[]{:S(2)}, u32[]{:S(2)}) async-start(bf16[4,384,128]{2,1,0:T(8,128)(2,1)} %attend.3), calls=%async_computation | async-start | bytes 786432 | tf_op jit(solution)/shard_map/all_to_all | solution.py:413
  114.6 0.5 collective-permute-start.17
  115.0 0.5 broadcast_maximum_fusion.1.place_ref
  115.6 8.7 %attend.4 = bf16[4,384,128]{2,1,0:T(8,128)(2,1)} custom-call(s32[3]{0:T(128)} %broadcast_maximum_fusion.1.place_ref, bf16[4,2,384,128]{3,2,1,0:T(8,128)(2,1)} %copy-done.5, bf16[4,384,256]{2,1,0:T(8,128)(2,1)} %constant_dynamic-update-slice_fusion.refs_1_, bf16[4,384,256]{2,1,0:T(8,128)(2,1)} %collective-permute-done.13.refs_2_, ...), custom_call_target="tpu_custom_call" | custom-call | flops 2415919104 | bytes 3145728 | tf_op jit(solution)/shard_map/attend/pallas_call | solution.py:277
  124.3 1.3 all-to-all-done.refs_0_
  125.6 3.7 %all-to-all-start.2 = ((bf16[4,384,128]{2,1,0:T(8,128)(2,1)}), bf16[4,384,128]{2,1,0:T(8,128)(2,1)S(1)}, u32[]{:S(2)}, u32[]{:S(2)}) async-start(bf16[4,384,128]{2,1,0:T(8,128)(2,1)} %attend.4), calls=%async_computation.2 | async-start | bytes 786432 | tf_op jit(solution)/shard_map/all_to_all | solution.py:413
  129.3 0.6 broadcast_maximum_fusion.place_ref
  129.9 8.6 %attend.5 = (bf16[1,384,128]{2,1,0:T(8,128)(2,1)}, bf16[1,384,128]{2,1,0:T(8,128)(2,1)}, bf16[1,384,128]{2,1,0:T(8,128)(2,1)}, bf16[1,384,128]{2,1,0:T(8,128)(2,1)}) custom-call(s32[3]{0:T(128)} %broadcast_maximum_fusion.place_ref, bf16[4,2,384,128]{3,2,1,0:T(8,128)(2,1)} %copy-done.5, bf16[4,384,256]{2,1,0:T(8,128)(2,1)} %copy-done.12, ...), custom_call_target="tpu_custom_call" | custom-call | flops 2415919104 | bytes 3145728 | tf_op jit(solution)/shard_map/attend/pallas_call | solution.py:277
  138.5 2.0 %collective-permute-start.18 = (bf16[1,384,128]{2,1,0:T(8,128)(2,1)}, bf16[1,384,128]{2,1,0:T(8,128)(2,1)S(1)}, u32[]{:S(2)}, u32[]{:S(2)}) collective-permute-start(bf16[1,384,128]{2,1,0:T(8,128)(2,1)} %get-tuple-element.77), channel_id=1, source_target_pairs={{0,8},{2,10},{4,12},{6,14},{8,0},{10,2},{12,4},{14,6},{16,24},{18,... | collective-permute-start | bytes 294920 | tf_op jit(solution)/shard_map/ppermute | solution.py:28
  140.5 2.4 %collective-permute-start.19 = (bf16[1,384,128]{2,1,0:T(8,128)(2,1)}, bf16[1,384,128]{2,1,0:T(8,128)(2,1)S(1)}, u32[]{:S(2)}, u32[]{:S(2)}) collective-permute-start(bf16[1,384,128]{2,1,0:T(8,128)(2,1)} %get-tuple-element.78), channel_id=1, source_target_pairs={{0,16},{2,18},{4,20},{6,22},{8,24},{10,26},{12,28},{14,30},{16,0},... | collective-permute-start | bytes 294920 | tf_op jit(solution)/shard_map/ppermute | solution.py:28
  142.9 0.9 constant_dynamic-update-slice_fusion.11
  143.8 3.8 %collective-permute-done.19 = bf16[1,384,128]{2,1,0:T(8,128)(2,1)S(1)} collective-permute-done((bf16[1,384,128]{2,1,0:T(8,128)(2,1)}, bf16[1,384,128]{2,1,0:T(8,128)(2,1)S(1)}, u32[]{:S(2)}, u32[]{:S(2)}) %collective-permute-start.19) | collective-permute-done | bytes 98336 | tf_op jit(solution)/shard_map/ppermute | solution.py:28
  147.7 2.9 %collective-permute-done.20 = bf16[1,384,128]{2,1,0:T(8,128)(2,1)S(1)} collective-permute-done((bf16[1,384,128]{2,1,0:T(8,128)(2,1)}, bf16[1,384,128]{2,1,0:T(8,128)(2,1)S(1)}, u32[]{:S(2)}, u32[]{:S(2)}) %collective-permute-start.20) | collective-permute-done | bytes 98336 | tf_op jit(solution)/shard_map/ppermute | solution.py:28
  150.6 0.7 copy-done.2
  151.4 0.8 copy-done.1
  152.2 7.1 %finish.2 = bf16[384,1536]{1,0:T(8,128)(2,1)} custom-call(s32[3]{0:T(128)} %pad_add_fusion.place_ref, bf16[4,384,128]{2,1,0:T(8,128)(2,1)} %copy-done, bf16[4,384,128]{2,1,0:T(8,128)(2,1)} %copy-done.1, bf16[4,384,128]{2,1,0:T(8,128)(2,1)} %copy-done.2, bf16[1536,3072]{1,0:T(8,128)(2,1)} %refs_3_.5), custom_call_target="tpu_custom_call" | custom-call | flops 1811939328 | bytes 7077888 | tf_op jit(solution)/shard_map/finish/pallas_call | solution.py:340
  159.2 1.5 collective-permute-start.21
  160.7 7.1 %finish.3.mine_ref = bf16[384,1536]{1,0:T(8,128)(2,1)} custom-call(s32[3]{0:T(128)} %pad_add_fusion.place_ref, bf16[4,384,128]{2,1,0:T(8,128)(2,1)} %copy-done, bf16[4,384,128]{2,1,0:T(8,128)(2,1)} %copy-done.1, bf16[4,384,128]{2,1,0:T(8,128)(2,1)} %copy-done.2, bf16[1536,3072]{1,0:T(8,128)(2,1)} %refs_3_.5), custom_call_target="tpu_custom_call" | custom-call | flops 1811939328 | bytes 7077888 | tf_op jit(solution)/shard_map/finish/pallas_call | solution.py:340
  167.8 20.2 %collective-permute-done.21.refs_0_ = bf16[384,1536]{1,0:T(8,128)(2,1)S(1)} collective-permute-done((bf16[384,1536]{1,0:T(8,128)(2,1)}, bf16[384,1536]{1,0:T(8,128)(2,1)S(1)}, u32[]{:S(2)}, u32[]{:S(2)}) %collective-permute-start.21) | collective-permute-done | bytes 1179680 | tf_op jit(solution)/shard_map/ppermute | solution.py:28
  188.0 1.0 copy-done.3
  189.0 4.4 %close.1 = bf16[384,1536]{1,0:T(8,128)(2,1)} custom-call(bf16[384,384]{1,0:T(8,128)(2,1)} %get-tuple-element.43.back_ref, bf16[384,1536]{1,0:T(8,128)(2,1)} %finish.3.mine_ref, bf16[384,1536]{1,0:T(8,128)(2,1)} %copy-done.3), custom_call_target="tpu_custom_call" | custom-call | flops 452984832 | bytes 5898240 | tf_op jit(solution)/shard_map/close/pallas_call | solution.py:370
  (68 shorter events, 0.6 us)
Async XLA Ops:
  14.1 15.9 %collective-permute-start = (bf16[1,384,384]{2,1,0:T(8,128)(2,1)}, bf16[1,384,384]{2,1,0:T(8,128)(2,1)S(1)}, u32[]{:S(2)}, u32[]{:S(2)}) collective-permute-start(bf16[1,384,384]{2,1,0:T(8,128)(2,1)} %get-tuple-element.44), channel_id=1, source_target_pairs={{0,8},{2,10},{4,12},{6,14},{8,0},{10,2},{12,4},{14,6},{16,24},{18,... | collective-permute-start | bytes 884744 | tf_op jit(solution)/shard_map/ppermute | solution.py:28
  17.2 26.0 %collective-permute-start.1 = (bf16[1,384,384]{2,1,0:T(8,128)(2,1)}, bf16[1,384,384]{2,1,0:T(8,128)(2,1)S(1)}, u32[]{:S(2)}, u32[]{:S(2)}) collective-permute-start(bf16[1,384,384]{2,1,0:T(8,128)(2,1)} %get-tuple-element.45), channel_id=1, source_target_pairs={{0,16},{2,18},{4,20},{6,22},{8,24},{10,26},{12,28},{14,30},{16,0},... | collective-permute-start | bytes 884744 | tf_op jit(solution)/shard_map/ppermute | solution.py:28
  19.8 23.5 %collective-permute-start.2 = (bf16[1,384,384]{2,1,0:T(8,128)(2,1)}, bf16[1,384,384]{2,1,0:T(8,128)(2,1)S(1)}, u32[]{:S(2)}, u32[]{:S(2)}) collective-permute-start(bf16[1,384,384]{2,1,0:T(8,128)(2,1)} %get-tuple-element.46), channel_id=1, source_target_pairs={{0,24},{2,26},{4,28},{6,30},{8,16},{10,18},{12,20},{14,22},{16,8},... | collective-permute-start | bytes 884744 | tf_op jit(solution)/shard_map/ppermute | solution.py:28
  29.9 13.3 %copy-start.9 = (bf16[1,384,384]{2,1,0:T(8,128)(2,1)}, bf16[1,384,384]{2,1,0:T(8,128)(2,1)S(1)}, u32[]{:S(2)}) copy-start(bf16[1,384,384]{2,1,0:T(8,128)(2,1)S(1)} %collective-permute-done.refs_1_) | copy-start | bytes 884740
  29.9 13.3 %copy-start.8 = (bf16[1,384,384]{2,1,0:T(8,128)(2,1)S(1)}, bf16[1,384,384]{2,1,0:T(8,128)(2,1)}, u32[]{:S(2)}) copy-start(bf16[1,384,384]{2,1,0:T(8,128)(2,1)} %get-tuple-element.62.refs_0_) | copy-start | bytes 884740
  43.2 2.1 %copy-start.17 = (bf16[1,384,256]{2,1,0:T(8,128)(2,1)S(1)}, bf16[1,384,256]{2,1,0:T(8,128)(2,1)}, u32[]{:S(2)}) copy-start(bf16[1,384,256]{2,1,0:T(8,128)(2,1)} %get-tuple-element.55) | copy-start | bytes 589828
  43.2 5.0 %copy-start.16 = (bf16[1,384,256]{2,1,0:T(8,128)(2,1)S(1)}, bf16[1,384,256]{2,1,0:T(8,128)(2,1)}, u32[]{:S(2)}) copy-start(bf16[1,384,256]{2,1,0:T(8,128)(2,1)} %get-tuple-element.66) | copy-start | bytes 589828
  43.2 6.1 %copy-start.15 = (bf16[1,384,256]{2,1,0:T(8,128)(2,1)S(1)}, bf16[1,384,256]{2,1,0:T(8,128)(2,1)}, u32[]{:S(2)}) copy-start(bf16[1,384,256]{2,1,0:T(8,128)(2,1)} %get-tuple-element.67) | copy-start | bytes 589828
  43.2 7.5 %copy-start.7 = (bf16[1,384,256]{2,1,0:T(8,128)(2,1)S(1)}, bf16[1,384,256]{2,1,0:T(8,128)(2,1)}, u32[]{:S(2)}) copy-start(bf16[1,384,256]{2,1,0:T(8,128)(2,1)} %get-tuple-element.61) | copy-start | bytes 589828
  43.2 25.4 %copy-start.10 = (bf16[1,384,384]{2,1,0:T(8,128)(2,1)}, bf16[1,384,384]{2,1,0:T(8,128)(2,1)S(1)}, u32[]{:S(2)}) copy-start(bf16[1,384,384]{2,1,0:T(8,128)(2,1)S(1)} %collective-permute-done.1.refs_2_) | copy-start | bytes 884740
  43.2 25.4 %copy-start.11 = (bf16[1,384,384]{2,1,0:T(8,128)(2,1)}, bf16[1,384,384]{2,1,0:T(8,128)(2,1)S(1)}, u32[]{:S(2)}) copy-start(bf16[1,384,384]{2,1,0:T(8,128)(2,1)S(1)} %collective-permute-done.2.refs_3_) | copy-start | bytes 884740
  43.4 35.2 %copy-start.4 = (bf16[4,384,256]{2,1,0:T(8,128)(2,1)}, bf16[4,384,256]{2,1,0:T(8,128)(2,1)S(1)}, u32[]{:S(2)}) copy-start(bf16[4,384,256]{2,1,0:T(8,128)(2,1)S(1)} %pad_maximum_fusion.refs_4_) | copy-start | bytes 2359300
  43.5 25.1 %collective-permute-start.7 = (bf16[4,384,256]{2,1,0:T(8,128)(2,1)S(1)}, bf16[4,384,256]{2,1,0:T(8,128)(2,1)}, u32[]{:S(2)}, u32[]{:S(2)}) collective-permute-start(bf16[4,384,256]{2,1,0:T(8,128)(2,1)S(1)} %pad_maximum_fusion.refs_4_), channel_id=1, source_target_pairs={{0,4},{2,6},{4,0},{6,2},{8,12},{10,14},{12,8},{14,10},{16,20},{18,... | collective-permute-start | bytes 2359304 | tf_op jit(solution)/shard_map/ppermute | solution.py:28
  45.2 7.7 %collective-permute-start.3 = (bf16[1,384,256]{2,1,0:T(8,128)(2,1)S(1)}, bf16[1,384,256]{2,1,0:T(8,128)(2,1)S(1)}, u32[]{:S(2)}, u32[]{:S(2)}) collective-permute-start(bf16[1,384,256]{2,1,0:T(8,128)(2,1)S(1)} %copy-done.17), channel_id=1, source_target_pairs={{0,8},{2,10},{4,12},{6,14},{8,0},{10,2},{12,4},{14,6},{16,24},{18,... | collective-permute-start | bytes 589832 | tf_op jit(solution)/shard_map/ppermute | solution.py:28
  48.1 46.3 %collective-permute-start.10 = (bf16[4,384,256]{2,1,0:T(8,128)(2,1)S(1)}, bf16[4,384,256]{2,1,0:T(8,128)(2,1)}, u32[]{:S(2)}, u32[]{:S(2)}) collective-permute-start(bf16[4,384,256]{2,1,0:T(8,128)(2,1)S(1)} %pad_maximum_fusion.refs_4_), channel_id=1, source_target_pairs={{0,2},{2,0},{4,6},{6,4},{8,10},{10,8},{12,14},{14,12},{16,18},{18,... | collective-permute-start | bytes 2359304 | tf_op jit(solution)/shard_map/ppermute | solution.py:28
  48.1 16.7 %collective-permute-start.8 = (bf16[1,384,256]{2,1,0:T(8,128)(2,1)S(1)}, bf16[1,384,256]{2,1,0:T(8,128)(2,1)S(1)}, u32[]{:S(2)}, u32[]{:S(2)}) collective-permute-start(bf16[1,384,256]{2,1,0:T(8,128)(2,1)S(1)} %copy-done.16), channel_id=1, source_target_pairs={{0,16},{2,18},{4,20},{6,22},{8,24},{10,26},{12,28},{14,30},{16,0},... | collective-permute-start | bytes 589832 | tf_op jit(solution)/shard_map/ppermute | solution.py:28
  49.2 16.3 %collective-permute-start.9 = (bf16[1,384,256]{2,1,0:T(8,128)(2,1)S(1)}, bf16[1,384,256]{2,1,0:T(8,128)(2,1)S(1)}, u32[]{:S(2)}, u32[]{:S(2)}) collective-permute-start(bf16[1,384,256]{2,1,0:T(8,128)(2,1)S(1)} %copy-done.15), channel_id=1, source_target_pairs={{0,24},{2,26},{4,28},{6,30},{8,16},{10,18},{12,20},{14,22},{16,8},... | collective-permute-start | bytes 589832 | tf_op jit(solution)/shard_map/ppermute | solution.py:28
  52.9 38.7 %collective-permute-start.4 = (bf16[1,384,256]{2,1,0:T(8,128)(2,1)}, bf16[1,384,256]{2,1,0:T(8,128)(2,1)S(1)}, u32[]{:S(2)}, u32[]{:S(2)}) collective-permute-start(bf16[1,384,256]{2,1,0:T(8,128)(2,1)} %get-tuple-element.57), channel_id=1, source_target_pairs={{0,8},{2,10},{4,12},{6,14},{8,0},{10,2},{12,4},{14,6},{16,24},{18,... | collective-permute-start | bytes 589832 | tf_op jit(solution)/shard_map/ppermute | solution.py:28
  64.8 26.8 %collective-permute-start.5 = (bf16[1,384,256]{2,1,0:T(8,128)(2,1)}, bf16[1,384,256]{2,1,0:T(8,128)(2,1)S(1)}, u32[]{:S(2)}, u32[]{:S(2)}) collective-permute-start(bf16[1,384,256]{2,1,0:T(8,128)(2,1)} %get-tuple-element.58), channel_id=1, source_target_pairs={{0,16},{2,18},{4,20},{6,22},{8,24},{10,26},{12,28},{14,30},{16,0},... | collective-permute-start | bytes 589832 | tf_op jit(solution)/shard_map/ppermute | solution.py:28
  65.5 26.1 %collective-permute-start.6 = (bf16[1,384,256]{2,1,0:T(8,128)(2,1)}, bf16[1,384,256]{2,1,0:T(8,128)(2,1)S(1)}, u32[]{:S(2)}, u32[]{:S(2)}) collective-permute-start(bf16[1,384,256]{2,1,0:T(8,128)(2,1)} %get-tuple-element.59), channel_id=1, source_target_pairs={{0,24},{2,26},{4,28},{6,30},{8,16},{10,18},{12,20},{14,22},{16,8},... | collective-permute-start | bytes 589832 | tf_op jit(solution)/shard_map/ppermute | solution.py:28
  68.6 25.0 %collective-permute-start.14 = (bf16[4,384,256]{2,1,0:T(8,128)(2,1)}, bf16[4,384,256]{2,1,0:T(8,128)(2,1)}, u32[]{:S(2)}, u32[]{:S(2)}) collective-permute-start(bf16[4,384,256]{2,1,0:T(8,128)(2,1)} %constant_dynamic-update-slice_fusion.refs_1_), channel_id=1, source_target_pairs={{0,4},{2,6},{4,0},{6,2},{8,12},{10,14},{12,8},{14,10},{16,20},{18,... | collective-permute-start | bytes 2359304 | tf_op jit(solution)/shard_map/ppermute | solution.py:28
  69.8 22.0 %copy-start.6 = (bf16[1,384,256]{2,1,0:T(8,128)(2,1)S(1)}, bf16[1,384,256]{2,1,0:T(8,128)(2,1)}, u32[]{:S(2)}) copy-start(bf16[1,384,256]{2,1,0:T(8,128)(2,1)} %get-tuple-element.69) | copy-start | bytes 589828
  78.6 15.3 %copy-start.13 = (s32[3]{0:T(128)S(1)}, s32[3]{0:T(128)}, u32[]{:S(2)}) copy-start(s32[3]{0:T(128)} %pad_add_fusion.place_ref) | copy-start | bytes 40
  78.6 32.4 %all-to-all-start.1 = ((bf16[4,2,384,128]{3,2,1,0:T(8,128)(2,1)}), bf16[4,2,384,128]{3,2,1,0:T(8,128)(2,1)S(1)}, u32[]{:S(2)}, u32[]{:S(2)}) async-start(bf16[4,2,384,128]{3,2,1,0:T(8,128)(2,1)} %project.5), calls=%async_computation.1 | async-start | bytes 1572864 | tf_op jit(solution)/shard_map/all_to_all | solution.py:413
  91.6 2.8 %collective-permute-start.11 = (bf16[4,384,256]{2,1,0:T(8,128)(2,1)}, bf16[4,384,256]{2,1,0:T(8,128)(2,1)}, u32[]{:S(2)}, u32[]{:S(2)}) collective-permute-start(bf16[4,384,256]{2,1,0:T(8,128)(2,1)} %collective-permute-done.7.refs_6_), channel_id=1, source_target_pairs={{0,2},{2,0},{4,6},{6,4},{8,10},{10,8},{12,14},{14,12},{16,18},{18,... | collective-permute-start | bytes 2359304 | tf_op jit(solution)/shard_map/ppermute | solution.py:28
  91.8 22.6 %copy-start.12 = (bf16[4,384,256]{2,1,0:T(8,128)(2,1)}, bf16[4,384,256]{2,1,0:T(8,128)(2,1)S(1)}, u32[]{:S(2)}) copy-start(bf16[4,384,256]{2,1,0:T(8,128)(2,1)S(1)} %constant_dynamic-update-slice_fusion.4.refs_1_) | copy-start | bytes 2359300
  91.8 22.7 %collective-permute-start.12 = (bf16[4,384,256]{2,1,0:T(8,128)(2,1)S(1)}, bf16[4,384,256]{2,1,0:T(8,128)(2,1)S(1)}, u32[]{:S(2)}, u32[]{:S(2)}) collective-permute-start(bf16[4,384,256]{2,1,0:T(8,128)(2,1)S(1)} %constant_dynamic-update-slice_fusion.4.refs_1_), channel_id=1, source_target_pairs={{0,4},{2,6},{4,0},{6,2},{8,12},{10,14},{12,8},{14,10},{16,20},{18,... | collective-permute-start | bytes 2359304 | tf_op jit(solution)/shard_map/ppermute | solution.py:28
  93.4 22.2 %collective-permute-start.13 = (bf16[4,384,256]{2,1,0:T(8,128)(2,1)}, bf16[4,384,256]{2,1,0:T(8,128)(2,1)}, u32[]{:S(2)}, u32[]{:S(2)}) collective-permute-start(bf16[4,384,256]{2,1,0:T(8,128)(2,1)} %constant_dynamic-update-slice_fusion.refs_1_), channel_id=1, source_target_pairs={{0,2},{2,0},{4,6},{6,4},{8,10},{10,8},{12,14},{14,12},{16,18},{18,... | collective-permute-start | bytes 2359304 | tf_op jit(solution)/shard_map/ppermute | solution.py:28
  93.6 22.0 %collective-permute-start.15 = (bf16[4,384,256]{2,1,0:T(8,128)(2,1)}, bf16[4,384,256]{2,1,0:T(8,128)(2,1)}, u32[]{:S(2)}, u32[]{:S(2)}) collective-permute-start(bf16[4,384,256]{2,1,0:T(8,128)(2,1)} %collective-permute-done.14.refs_3_), channel_id=1, source_target_pairs={{0,2},{2,0},{4,6},{6,4},{8,10},{10,8},{12,14},{14,12},{16,18},{18,... | collective-permute-start | bytes 2359304 | tf_op jit(solution)/shard_map/ppermute | solution.py:28
  111.0 4.6 %copy-start.5 = (bf16[4,2,384,128]{3,2,1,0:T(8,128)(2,1)}, bf16[4,2,384,128]{3,2,1,0:T(8,128)(2,1)S(1)}, u32[]{:S(2)}) copy-start(bf16[4,2,384,128]{3,2,1,0:T(8,128)(2,1)S(1)} %all-to-all-done.1.refs_0_) | copy-start | bytes 2359300
  111.0 14.6 %all-to-all-start = ((bf16[4,384,128]{2,1,0:T(8,128)(2,1)}), bf16[4,384,128]{2,1,0:T(8,128)(2,1)S(1)}, u32[]{:S(2)}, u32[]{:S(2)}) async-start(bf16[4,384,128]{2,1,0:T(8,128)(2,1)} %attend.3), calls=%async_computation | async-start | bytes 786432 | tf_op jit(solution)/shard_map/all_to_all | solution.py:413
  114.5 15.4 %collective-permute-start.16 = (bf16[4,384,256]{2,1,0:T(8,128)(2,1)S(1)}, bf16[4,384,256]{2,1,0:T(8,128)(2,1)}, u32[]{:S(2)}, u32[]{:S(2)}) collective-permute-start(bf16[4,384,256]{2,1,0:T(8,128)(2,1)S(1)} %constant_dynamic-update-slice_fusion.4.refs_1_), channel_id=1, source_target_pairs={{0,2},{2,0},{4,6},{6,4},{8,10},{10,8},{12,14},{14,12},{16,18},{18,... | collective-permute-start | bytes 2359304 | tf_op jit(solution)/shard_map/ppermute | solution.py:28
  114.6 9.7 %copy-start.14 = (bf16[4,384,256]{2,1,0:T(8,128)(2,1)}, bf16[4,384,256]{2,1,0:T(8,128)(2,1)S(1)}, u32[]{:S(2)}) copy-start(bf16[4,384,256]{2,1,0:T(8,128)(2,1)S(1)} %collective-permute-done.12.refs_3_) | copy-start | bytes 2359300
  114.6 15.3 %collective-permute-start.17 = (bf16[4,384,256]{2,1,0:T(8,128)(2,1)S(1)}, bf16[4,384,256]{2,1,0:T(8,128)(2,1)}, u32[]{:S(2)}, u32[]{:S(2)}) collective-permute-start(bf16[4,384,256]{2,1,0:T(8,128)(2,1)S(1)} %collective-permute-done.12.refs_3_), channel_id=1, source_target_pairs={{0,2},{2,0},{4,6},{6,4},{8,10},{10,8},{12,14},{14,12},{16,18},{18,... | collective-permute-start | bytes 2359304 | tf_op jit(solution)/shard_map/ppermute | solution.py:28
  125.6 12.9 %copy-start = (bf16[4,384,128]{2,1,0:T(8,128)(2,1)}, bf16[4,384,128]{2,1,0:T(8,128)(2,1)S(1)}, u32[]{:S(2)}) copy-start(bf16[4,384,128]{2,1,0:T(8,128)(2,1)S(1)} %all-to-all-done.refs_0_) | copy-start | bytes 1179652
  125.6 25.0 %all-to-all-start.2 = ((bf16[4,384,128]{2,1,0:T(8,128)(2,1)}), bf16[4,384,128]{2,1,0:T(8,128)(2,1)S(1)}, u32[]{:S(2)}, u32[]{:S(2)}) async-start(bf16[4,384,128]{2,1,0:T(8,128)(2,1)} %attend.4), calls=%async_computation.2 | async-start | bytes 786432 | tf_op jit(solution)/shard_map/all_to_all | solution.py:413
  138.5 5.4 %collective-permute-start.18 = (bf16[1,384,128]{2,1,0:T(8,128)(2,1)}, bf16[1,384,128]{2,1,0:T(8,128)(2,1)S(1)}, u32[]{:S(2)}, u32[]{:S(2)}) collective-permute-start(bf16[1,384,128]{2,1,0:T(8,128)(2,1)} %get-tuple-element.77), channel_id=1, source_target_pairs={{0,8},{2,10},{4,12},{6,14},{8,0},{10,2},{12,4},{14,6},{16,24},{18,... | collective-permute-start | bytes 294920 | tf_op jit(solution)/shard_map/ppermute | solution.py:28
  140.5 7.2 %collective-permute-start.19 = (bf16[1,384,128]{2,1,0:T(8,128)(2,1)}, bf16[1,384,128]{2,1,0:T(8,128)(2,1)S(1)}, u32[]{:S(2)}, u32[]{:S(2)}) collective-permute-start(bf16[1,384,128]{2,1,0:T(8,128)(2,1)} %get-tuple-element.78), channel_id=1, source_target_pairs={{0,16},{2,18},{4,20},{6,22},{8,24},{10,26},{12,28},{14,30},{16,0},... | collective-permute-start | bytes 294920 | tf_op jit(solution)/shard_map/ppermute | solution.py:28
  142.8 7.7 %collective-permute-start.20 = (bf16[1,384,128]{2,1,0:T(8,128)(2,1)}, bf16[1,384,128]{2,1,0:T(8,128)(2,1)S(1)}, u32[]{:S(2)}, u32[]{:S(2)}) collective-permute-start(bf16[1,384,128]{2,1,0:T(8,128)(2,1)} %get-tuple-element.79), channel_id=1, source_target_pairs={{0,24},{2,26},{4,28},{6,30},{8,16},{10,18},{12,20},{14,22},{16,8},... | collective-permute-start | bytes 294920 | tf_op jit(solution)/shard_map/ppermute | solution.py:28
  150.6 0.8 copy-start.2
  151.4 0.8 copy-start.1
  159.2 28.8 %collective-permute-start.21 = (bf16[384,1536]{1,0:T(8,128)(2,1)}, bf16[384,1536]{1,0:T(8,128)(2,1)S(1)}, u32[]{:S(2)}, u32[]{:S(2)}) collective-permute-start(bf16[384,1536]{1,0:T(8,128)(2,1)} %finish.2), channel_id=1, source_target_pairs={{0,1},{1,0},{2,3},{3,2},{4,5},{5,4},{6,7},{7,6},{8,9},{9,8},{10,11... | collective-permute-start | bytes 3538952 | tf_op jit(solution)/shard_map/ppermute | solution.py:28
  188.0 1.0 copy-start.3

commit v15 on v11

--- a/solution.py
+++ b/solution.py
@@ -334,7 +334,7 @@
     groups, rows, size = attended[0].shape
     depth = w_out.shape[0]
     out_width = w_out.shape[1] // lax.axis_size("head")
-    parts = 4 if out_width % 512 == 0 else 1
+    parts = 2 if out_width % 256 == 0 else 1
     tile = out_width // parts
     column = lambda i, place: (0, lax.bitwise_xor(place[2], mask) * parts + i)
     return pl.pallas_call(

time: 190 us -> 189 us (level)
  Pallas kernels: 83.9 us -> 78 us
  waiting for transfers between devices: 44.2 us -> 49.2 us
    ppermute x22, waiting for transfers between devices: 44.2 us -> 48.4 us  [flip(): return lax.ppermute(values, axis, [(i, i ^ mask) for i in range(size)])]
    pallas_call x3, Pallas kernels: 29.9 us -> 26.4 us  [attend(): pl.pallas_call(functools.partial(attend_body, groups=groups, asked=len(qu...]
    pallas_call x2, Pallas kernels: 14.2 us -> 11.8 us  [finish(): pl.pallas_call(functools.partial(finish_body, ordered=ordered), grid_spec...]
    ppermute x22, starting transfers between devices: 27 us -> 29.3 us  [flip(): return lax.ppermute(values, axis, [(i, i ^ mask) for i in range(size)])]
  transfers between devices with their start and end apart: 25 -> 25, of which waited for: 8 -> 10; matrix products, arithmetic and copies ran while one was open for 3% -> 3% of each run, Pallas kernels for 32% -> 29%
where the time goes in v15:
time: 189 us; the launch traced here: 187 us
  Pallas kernels  78 us (41%)
  starting transfers between devices  49.9 us (26%)
  waiting for transfers between devices  49.2 us (26%)
  local copies, waits for them, and re-layouts  6.46 us (3%)
  other arithmetic  2.39 us (1%)
    ppermute x22, waiting for transfers between devices, flip(): return lax.ppermute(values, axis, [(i, i ^ mask) for i in range(size)])  48.4 us
    pallas_call x3, Pallas kernels, project(): pl.pallas_call(functools.partial(project_body, steps=steps, groups=groups...  35.5 us
    ppermute x22, starting transfers between devices, flip(): return lax.ppermute(values, axis, [(i, i ^ mask) for i in range(size)])  29.3 us
    pallas_call x3, Pallas kernels, attend(): pl.pallas_call(functools.partial(attend_body, groups=groups, asked=len(qu...  26.4 us
    all_to_all x3, starting transfers between devices, send_back(): lax.all_to_all(blocks, 'seq', split_axis=0, concat_axis=0, axis_index_gro...  20.6 us
    pallas_call x2, Pallas kernels, finish(): pl.pallas_call(functools.partial(finish_body, ordered=ordered), grid_spec...  11.8 us
    unnamed x45, local copies, waits for them, and re-layouts  5.69 us
    pallas_call x1, Pallas kernels, close(): pl.pallas_call(close_body, grid=(parts,), in_specs=[pl.BlockSpec((rows, r...  4.37 us
  transfers between devices with their start and end apart: 25, of which 10 were waited for; matrix products, arithmetic and copies ran while one was open for 3% of the time, Pallas kernels for 29%

profile of v15, /device:TPU:0, one launch (start us, length us, event | category | flops | bytes accessed | tf_op | source)
XLA Modules:
  0.0 186.8 jit_solution(6124892452590575175)
XLA Ops:
  0.0 0.6 pad_add_fusion.place_ref
  0.6 13.4 %project.3 = (bf16[1,384,384]{2,1,0:T(8,128)(2,1)}, bf16[1,384,384]{2,1,0:T(8,128)(2,1)}, bf16[1,384,384]{2,1,0:T(8,128)(2,1)}, bf16[1,384,384]{2,1,0:T(8,128)(2...) custom-call(s32[3]{0:T(128)} %pad_add_fusion.place_ref, ...), custom_call_target="tpu_custom_call" | custom-call | flops 3623878656 | bytes 11796480 | tf_op jit(solution)/shard_map/project/pallas_call | solution.py:150
  14.1 3.1 %collective-permute-start = (bf16[1,384,384]{2,1,0:T(8,128)(2,1)}, bf16[1,384,384]{2,1,0:T(8,128)(2,1)S(1)}, u32[]{:S(2)}, u32[]{:S(2)}) collective-permute-start(bf16[1,384,384]{2,1,0:T(8,128)(2,1)} %get-tuple-element.46), channel_id=1, source_target_pairs={{0,8},{2,10},{4,12},{6,14},{8,0},{10,2},{12,4},{14,6},{16,24},{18,... | collective-permute-start | bytes 884744 | tf_op jit(solution)/shard_map/ppermute | solution.py:28
  17.2 2.6 %collective-permute-start.1 = (bf16[1,384,384]{2,1,0:T(8,128)(2,1)}, bf16[1,384,384]{2,1,0:T(8,128)(2,1)S(1)}, u32[]{:S(2)}, u32[]{:S(2)}) collective-permute-start(bf16[1,384,384]{2,1,0:T(8,128)(2,1)} %get-tuple-element.47), channel_id=1, source_target_pairs={{0,16},{2,18},{4,20},{6,22},{8,24},{10,26},{12,28},{14,30},{16,0},... | collective-permute-start | bytes 884744 | tf_op jit(solution)/shard_map/ppermute | solution.py:28
  19.8 10.2 %collective-permute-done.refs_1_ = bf16[1,384,384]{2,1,0:T(8,128)(2,1)S(1)} collective-permute-done((bf16[1,384,384]{2,1,0:T(8,128)(2,1)}, bf16[1,384,384]{2,1,0:T(8,128)(2,1)S(1)}, u32[]{:S(2)}, u32[]{:S(2)}) %collective-permute-start) | collective-permute-done | bytes 294944 | tf_op jit(solution)/shard_map/ppermute | solution.py:28
  29.9 13.2 %project.4 = (bf16[1,384,256]{2,1,0:T(8,128)(2,1)}, bf16[1,384,256]{2,1,0:T(8,128)(2,1)}, bf16[1,384,256]{2,1,0:T(8,128)(2,1)}, bf16[1,384,256]{2,1,0:T(8,128)(2...) custom-call(s32[3]{0:T(128)} %pad_add_fusion.place_ref, ...), custom_call_target="tpu_custom_call" | custom-call | flops 4831838208 | bytes 14942208 | tf_op jit(solution)/shard_map/project/pallas_call | solution.py:150
  43.4 1.8 collective-permute-start.7
  45.2 2.9 %collective-permute-start.3 = (bf16[1,384,256]{2,1,0:T(8,128)(2,1)S(1)}, bf16[1,384,256]{2,1,0:T(8,128)(2,1)S(1)}, u32[]{:S(2)}, u32[]{:S(2)}) collective-permute-start(bf16[1,384,256]{2,1,0:T(8,128)(2,1)S(1)} %copy-done.17), channel_id=1, source_target_pairs={{0,8},{2,10},{4,12},{6,14},{8,0},{10,2},{12,4},{14,6},{16,24},{18,... | collective-permute-start | bytes 589832 | tf_op jit(solution)/shard_map/ppermute | solution.py:28
  48.1 1.1 collective-permute-start.8
  49.2 1.5 collective-permute-start.9
  50.7 0.7 constant_dynamic-update-slice_fusion.3
  51.4 5.3 %collective-permute-done.3 = bf16[1,384,256]{2,1,0:T(8,128)(2,1)S(1)} collective-permute-done((bf16[1,384,256]{2,1,0:T(8,128)(2,1)S(1)}, bf16[1,384,256]{2,1,0:T(8,128)(2,1)S(1)}, u32[]{:S(2)}, u32[]{:S(2)}) %collective-permute-start.3) | collective-permute-done | bytes 196640 | tf_op jit(solution)/shard_map/ppermute | solution.py:28
  56.7 2.6 %collective-permute-start.5 = (bf16[1,384,256]{2,1,0:T(8,128)(2,1)}, bf16[1,384,256]{2,1,0:T(8,128)(2,1)S(1)}, u32[]{:S(2)}, u32[]{:S(2)}) collective-permute-start(bf16[1,384,256]{2,1,0:T(8,128)(2,1)} %get-tuple-element.60), channel_id=1, source_target_pairs={{0,16},{2,18},{4,20},{6,22},{8,24},{10,26},{12,28},{14,30},{16,0},... | collective-permute-start | bytes 589832 | tf_op jit(solution)/shard_map/ppermute | solution.py:28
  59.3 0.7 constant_dynamic-update-slice_fusion.2
  59.9 5.4 %collective-permute-done.8 = bf16[1,384,256]{2,1,0:T(8,128)(2,1)S(1)} collective-permute-done((bf16[1,384,256]{2,1,0:T(8,128)(2,1)S(1)}, bf16[1,384,256]{2,1,0:T(8,128)(2,1)S(1)}, u32[]{:S(2)}, u32[]{:S(2)}) %collective-permute-start.8) | collective-permute-done | bytes 196640 | tf_op jit(solution)/shard_map/ppermute | solution.py:28
  65.4 2.5 %collective-permute-start.6 = (bf16[1,384,256]{2,1,0:T(8,128)(2,1)}, bf16[1,384,256]{2,1,0:T(8,128)(2,1)S(1)}, u32[]{:S(2)}, u32[]{:S(2)}) collective-permute-start(bf16[1,384,256]{2,1,0:T(8,128)(2,1)} %get-tuple-element.61), channel_id=1, source_target_pairs={{0,24},{2,26},{4,28},{6,30},{8,16},{10,18},{12,20},{14,22},{16,8},... | collective-permute-start | bytes 589832 | tf_op jit(solution)/shard_map/ppermute | solution.py:28
  67.8 0.7 constant_dynamic-update-slice_fusion.1
  68.5 0.7 constant_dynamic-update-slice_fusion.refs_1_
  69.2 0.5 collective-permute-start.14
  70.3 8.8 %project.5 = bf16[4,2,384,128]{3,2,1,0:T(8,128)(2,1)} custom-call(s32[3]{0:T(128)} %pad_add_fusion.place_ref, bf16[3,3072,1536]{2,1,0:T(8,128)(2,1)} %bitcast.7, f32[12,2,128]{2,1,0:T(2,128)} %bitcast.10, s32[1,1]{1,0:T(1,128)S(6)} %max.12.refs_2_, bf16[384,3072]{1,0:T(8,128)(2,1)} %get-tuple-element.51.refs_3_, bf16[384,384]{1,0:T(8,128)(2,1)} %get-tuple-element.52.refs_4_), custom_call_target="tpu_custom_call" | custom-call | flops 2415919104 | bytes 8650752 | tf_op jit(solution)/shard_map/project/pallas_call | solution.py:150
  79.1 11.1 %all-to-all-start.1 = ((bf16[4,2,384,128]{3,2,1,0:T(8,128)(2,1)}), bf16[4,2,384,128]{3,2,1,0:T(8,128)(2,1)S(1)}, u32[]{:S(2)}, u32[]{:S(2)}) async-start(bf16[4,2,384,128]{3,2,1,0:T(8,128)(2,1)} %project.5), calls=%async_computation.1 | async-start | bytes 1572864 | tf_op jit(solution)/shard_map/all_to_all | solution.py:413
  90.2 0.5 collective-permute-start.10
  90.9 1.6 collective-permute-start.12
  92.4 0.5 collective-permute-start.15
  93.0 0.5 broadcast_maximum_fusion.2.place_ref
  93.8 8.9 %attend.3 = bf16[4,384,128]{2,1,0:T(8,128)(2,1)} custom-call(s32[3]{0:T(128)} %broadcast_maximum_fusion.2.place_ref, bf16[1,384,384]{2,1,0:T(8,128)(2,1)} %get-tuple-element.64.refs_0_, bf16[1,384,384]{2,1,0:T(8,128)(2,1)} %copy-done.9, bf16[1,384,384]{2,1,0:T(8,128)(2,1)} %copy-done.10, bf16[1,384,384]{2,1,0:T(8,128)(2,1)} %copy-done.11, ...), custom_call_target="tpu_custom_call" | custom-call | flops 2415919104 | bytes 3145728 | tf_op jit(solution)/shard_map/attend/pallas_call | solution.py:277
  102.7 0.7 all-to-all-done.1.refs_0_
  103.3 4.4 %all-to-all-start = ((bf16[4,384,128]{2,1,0:T(8,128)(2,1)}), bf16[4,384,128]{2,1,0:T(8,128)(2,1)S(1)}, u32[]{:S(2)}, u32[]{:S(2)}) async-start(bf16[4,384,128]{2,1,0:T(8,128)(2,1)} %attend.3), calls=%async_computation | async-start | bytes 786432 | tf_op jit(solution)/shard_map/all_to_all | solution.py:413
  107.8 2.3 %collective-permute-start.16 = (bf16[4,384,256]{2,1,0:T(8,128)(2,1)S(1)}, bf16[4,384,256]{2,1,0:T(8,128)(2,1)}, u32[]{:S(2)}, u32[]{:S(2)}) collective-permute-start(bf16[4,384,256]{2,1,0:T(8,128)(2,1)S(1)} %constant_dynamic-update-slice_fusion.4.refs_1_), channel_id=1, source_target_pairs={{0,2},{2,0},{4,6},{6,4},{8,10},{10,8},{12,14},{14,12},{16,18},{18,... | collective-permute-start | bytes 2359304 | tf_op jit(solution)/shard_map/ppermute | solution.py:28
  110.1 0.4 collective-permute-done.12.refs_3_
  110.4 0.6 broadcast_maximum_fusion.1.place_ref
  111.0 8.7 %attend.4 = bf16[4,384,128]{2,1,0:T(8,128)(2,1)} custom-call(s32[3]{0:T(128)} %broadcast_maximum_fusion.1.place_ref, bf16[4,2,384,128]{3,2,1,0:T(8,128)(2,1)} %copy-done.5, bf16[4,384,256]{2,1,0:T(8,128)(2,1)} %constant_dynamic-update-slice_fusion.refs_1_, bf16[4,384,256]{2,1,0:T(8,128)(2,1)} %collective-permute-done.13.refs_2_, ...), custom_call_target="tpu_custom_call" | custom-call | flops 2415919104 | bytes 3145728 | tf_op jit(solution)/shard_map/attend/pallas_call | solution.py:277
  119.8 5.0 %all-to-all-start.2 = ((bf16[4,384,128]{2,1,0:T(8,128)(2,1)}), bf16[4,384,128]{2,1,0:T(8,128)(2,1)S(1)}, u32[]{:S(2)}, u32[]{:S(2)}) async-start(bf16[4,384,128]{2,1,0:T(8,128)(2,1)} %attend.4), calls=%async_computation.2 | async-start | bytes 786432 | tf_op jit(solution)/shard_map/all_to_all | solution.py:413
  124.8 0.6 broadcast_maximum_fusion.place_ref
  125.4 8.8 %attend.5 = (bf16[1,384,128]{2,1,0:T(8,128)(2,1)}, bf16[1,384,128]{2,1,0:T(8,128)(2,1)}, bf16[1,384,128]{2,1,0:T(8,128)(2,1)}, bf16[1,384,128]{2,1,0:T(8,128)(2,1)}) custom-call(s32[3]{0:T(128)} %broadcast_maximum_fusion.place_ref, bf16[4,2,384,128]{3,2,1,0:T(8,128)(2,1)} %copy-done.5, bf16[4,384,256]{2,1,0:T(8,128)(2,1)} %copy-done.12, ...), custom_call_target="tpu_custom_call" | custom-call | flops 2415919104 | bytes 3145728 | tf_op jit(solution)/shard_map/attend/pallas_call | solution.py:277
  134.2 2.0 %collective-permute-start.18 = (bf16[1,384,128]{2,1,0:T(8,128)(2,1)}, bf16[1,384,128]{2,1,0:T(8,128)(2,1)S(1)}, u32[]{:S(2)}, u32[]{:S(2)}) collective-permute-start(bf16[1,384,128]{2,1,0:T(8,128)(2,1)} %get-tuple-element.81), channel_id=1, source_target_pairs={{0,8},{2,10},{4,12},{6,14},{8,0},{10,2},{12,4},{14,6},{16,24},{18,... | collective-permute-start | bytes 294920 | tf_op jit(solution)/shard_map/ppermute | solution.py:28
  136.2 2.4 %collective-permute-start.19 = (bf16[1,384,128]{2,1,0:T(8,128)(2,1)}, bf16[1,384,128]{2,1,0:T(8,128)(2,1)S(1)}, u32[]{:S(2)}, u32[]{:S(2)}) collective-permute-start(bf16[1,384,128]{2,1,0:T(8,128)(2,1)} %get-tuple-element.82), channel_id=1, source_target_pairs={{0,16},{2,18},{4,20},{6,22},{8,24},{10,26},{12,28},{14,30},{16,0},... | collective-permute-start | bytes 294920 | tf_op jit(solution)/shard_map/ppermute | solution.py:28
  138.7 0.9 constant_dynamic-update-slice_fusion.11
  139.6 3.5 %collective-permute-done.19 = bf16[1,384,128]{2,1,0:T(8,128)(2,1)S(1)} collective-permute-done((bf16[1,384,128]{2,1,0:T(8,128)(2,1)}, bf16[1,384,128]{2,1,0:T(8,128)(2,1)S(1)}, u32[]{:S(2)}, u32[]{:S(2)}) %collective-permute-start.19) | collective-permute-done | bytes 98336 | tf_op jit(solution)/shard_map/ppermute | solution.py:28
  143.1 3.1 %collective-permute-done.20 = bf16[1,384,128]{2,1,0:T(8,128)(2,1)S(1)} collective-permute-done((bf16[1,384,128]{2,1,0:T(8,128)(2,1)}, bf16[1,384,128]{2,1,0:T(8,128)(2,1)S(1)}, u32[]{:S(2)}, u32[]{:S(2)}) %collective-permute-start.20) | collective-permute-done | bytes 98336 | tf_op jit(solution)/shard_map/ppermute | solution.py:28
  146.2 0.8 copy-done.2
  147.0 0.7 copy-done.1
  147.7 5.9 %finish.2 = bf16[384,1536]{1,0:T(8,128)(2,1)} custom-call(s32[3]{0:T(128)} %pad_add_fusion.place_ref, bf16[4,384,128]{2,1,0:T(8,128)(2,1)} %copy-done, bf16[4,384,128]{2,1,0:T(8,128)(2,1)} %copy-done.1, bf16[4,384,128]{2,1,0:T(8,128)(2,1)} %copy-done.2, bf16[1536,3072]{1,0:T(8,128)(2,1)} %refs_3_.5), custom_call_target="tpu_custom_call" | custom-call | flops 1811939328 | bytes 7077888 | tf_op jit(solution)/shard_map/finish/pallas_call | solution.py:340
  153.6 1.5 collective-permute-start.21
  155.1 5.9 %finish.3.mine_ref = bf16[384,1536]{1,0:T(8,128)(2,1)} custom-call(s32[3]{0:T(128)} %pad_add_fusion.place_ref, bf16[4,384,128]{2,1,0:T(8,128)(2,1)} %copy-done, bf16[4,384,128]{2,1,0:T(8,128)(2,1)} %copy-done.1, bf16[4,384,128]{2,1,0:T(8,128)(2,1)} %copy-done.2, bf16[1536,3072]{1,0:T(8,128)(2,1)} %refs_3_.5), custom_call_target="tpu_custom_call" | custom-call | flops 1811939328 | bytes 7077888 | tf_op jit(solution)/shard_map/finish/pallas_call | solution.py:340
  161.0 20.3 %collective-permute-done.21.refs_0_ = bf16[384,1536]{1,0:T(8,128)(2,1)S(1)} collective-permute-done((bf16[384,1536]{1,0:T(8,128)(2,1)}, bf16[384,1536]{1,0:T(8,128)(2,1)S(1)}, u32[]{:S(2)}, u32[]{:S(2)}) %collective-permute-start.21) | collective-permute-done | bytes 1179680 | tf_op jit(solution)/shard_map/ppermute | solution.py:28
  181.4 1.0 copy-done.3
  182.4 4.4 %close.1 = bf16[384,1536]{1,0:T(8,128)(2,1)} custom-call(bf16[384,384]{1,0:T(8,128)(2,1)} %get-tuple-element.45.back_ref, bf16[384,1536]{1,0:T(8,128)(2,1)} %finish.3.mine_ref, bf16[384,1536]{1,0:T(8,128)(2,1)} %copy-done.3), custom_call_target="tpu_custom_call" | custom-call | flops 452984832 | bytes 5898240 | tf_op jit(solution)/shard_map/close/pallas_call | solution.py:370
  (68 shorter events, 0.8 us)
Async XLA Ops:
  14.1 15.9 %collective-permute-start = (bf16[1,384,384]{2,1,0:T(8,128)(2,1)}, bf16[1,384,384]{2,1,0:T(8,128)(2,1)S(1)}, u32[]{:S(2)}, u32[]{:S(2)}) collective-permute-start(bf16[1,384,384]{2,1,0:T(8,128)(2,1)} %get-tuple-element.46), channel_id=1, source_target_pairs={{0,8},{2,10},{4,12},{6,14},{8,0},{10,2},{12,4},{14,6},{16,24},{18,... | collective-permute-start | bytes 884744 | tf_op jit(solution)/shard_map/ppermute | solution.py:28
  17.2 26.0 %collective-permute-start.1 = (bf16[1,384,384]{2,1,0:T(8,128)(2,1)}, bf16[1,384,384]{2,1,0:T(8,128)(2,1)S(1)}, u32[]{:S(2)}, u32[]{:S(2)}) collective-permute-start(bf16[1,384,384]{2,1,0:T(8,128)(2,1)} %get-tuple-element.47), channel_id=1, source_target_pairs={{0,16},{2,18},{4,20},{6,22},{8,24},{10,26},{12,28},{14,30},{16,0},... | collective-permute-start | bytes 884744 | tf_op jit(solution)/shard_map/ppermute | solution.py:28
  19.8 23.4 %collective-permute-start.2 = (bf16[1,384,384]{2,1,0:T(8,128)(2,1)}, bf16[1,384,384]{2,1,0:T(8,128)(2,1)S(1)}, u32[]{:S(2)}, u32[]{:S(2)}) collective-permute-start(bf16[1,384,384]{2,1,0:T(8,128)(2,1)} %get-tuple-element.48), channel_id=1, source_target_pairs={{0,24},{2,26},{4,28},{6,30},{8,16},{10,18},{12,20},{14,22},{16,8},... | collective-permute-start | bytes 884744 | tf_op jit(solution)/shard_map/ppermute | solution.py:28
  29.9 13.3 %copy-start.9 = (bf16[1,384,384]{2,1,0:T(8,128)(2,1)}, bf16[1,384,384]{2,1,0:T(8,128)(2,1)S(1)}, u32[]{:S(2)}) copy-start(bf16[1,384,384]{2,1,0:T(8,128)(2,1)S(1)} %collective-permute-done.refs_1_) | copy-start | bytes 884740
  29.9 13.3 %copy-start.8 = (bf16[1,384,384]{2,1,0:T(8,128)(2,1)S(1)}, bf16[1,384,384]{2,1,0:T(8,128)(2,1)}, u32[]{:S(2)}) copy-start(bf16[1,384,384]{2,1,0:T(8,128)(2,1)} %get-tuple-element.64.refs_0_) | copy-start | bytes 884740
  43.1 2.1 %copy-start.17 = (bf16[1,384,256]{2,1,0:T(8,128)(2,1)S(1)}, bf16[1,384,256]{2,1,0:T(8,128)(2,1)}, u32[]{:S(2)}) copy-start(bf16[1,384,256]{2,1,0:T(8,128)(2,1)} %get-tuple-element.57) | copy-start | bytes 589828
  43.1 5.0 %copy-start.16 = (bf16[1,384,256]{2,1,0:T(8,128)(2,1)S(1)}, bf16[1,384,256]{2,1,0:T(8,128)(2,1)}, u32[]{:S(2)}) copy-start(bf16[1,384,256]{2,1,0:T(8,128)(2,1)} %get-tuple-element.68) | copy-start | bytes 589828
  43.1 6.1 %copy-start.15 = (bf16[1,384,256]{2,1,0:T(8,128)(2,1)S(1)}, bf16[1,384,256]{2,1,0:T(8,128)(2,1)}, u32[]{:S(2)}) copy-start(bf16[1,384,256]{2,1,0:T(8,128)(2,1)} %get-tuple-element.69) | copy-start | bytes 589828
  43.1 7.5 %copy-start.7 = (bf16[1,384,256]{2,1,0:T(8,128)(2,1)S(1)}, bf16[1,384,256]{2,1,0:T(8,128)(2,1)}, u32[]{:S(2)}) copy-start(bf16[1,384,256]{2,1,0:T(8,128)(2,1)} %get-tuple-element.63) | copy-start | bytes 589828
  43.2 26.0 %copy-start.10 = (bf16[1,384,384]{2,1,0:T(8,128)(2,1)}, bf16[1,384,384]{2,1,0:T(8,128)(2,1)S(1)}, u32[]{:S(2)}) copy-start(bf16[1,384,384]{2,1,0:T(8,128)(2,1)S(1)} %collective-permute-done.1.refs_2_) | copy-start | bytes 884740
  43.2 26.0 %copy-start.11 = (bf16[1,384,384]{2,1,0:T(8,128)(2,1)}, bf16[1,384,384]{2,1,0:T(8,128)(2,1)S(1)}, u32[]{:S(2)}) copy-start(bf16[1,384,384]{2,1,0:T(8,128)(2,1)S(1)} %collective-permute-done.2.refs_3_) | copy-start | bytes 884740
  43.4 46.8 %copy-start.4 = (bf16[4,384,256]{2,1,0:T(8,128)(2,1)}, bf16[4,384,256]{2,1,0:T(8,128)(2,1)S(1)}, u32[]{:S(2)}) copy-start(bf16[4,384,256]{2,1,0:T(8,128)(2,1)S(1)} %pad_maximum_fusion.refs_4_) | copy-start | bytes 2359300
  43.4 26.3 %collective-permute-start.7 = (bf16[4,384,256]{2,1,0:T(8,128)(2,1)S(1)}, bf16[4,384,256]{2,1,0:T(8,128)(2,1)}, u32[]{:S(2)}, u32[]{:S(2)}) collective-permute-start(bf16[4,384,256]{2,1,0:T(8,128)(2,1)S(1)} %pad_maximum_fusion.refs_4_), channel_id=1, source_target_pairs={{0,4},{2,6},{4,0},{6,2},{8,12},{10,14},{12,8},{14,10},{16,20},{18,... | collective-permute-start | bytes 2359304 | tf_op jit(solution)/shard_map/ppermute | solution.py:28
  45.2 11.5 %collective-permute-start.3 = (bf16[1,384,256]{2,1,0:T(8,128)(2,1)S(1)}, bf16[1,384,256]{2,1,0:T(8,128)(2,1)S(1)}, u32[]{:S(2)}, u32[]{:S(2)}) collective-permute-start(bf16[1,384,256]{2,1,0:T(8,128)(2,1)S(1)} %copy-done.17), channel_id=1, source_target_pairs={{0,8},{2,10},{4,12},{6,14},{8,0},{10,2},{12,4},{14,6},{16,24},{18,... | collective-permute-start | bytes 589832 | tf_op jit(solution)/shard_map/ppermute | solution.py:28
  48.1 17.2 %collective-permute-start.8 = (bf16[1,384,256]{2,1,0:T(8,128)(2,1)S(1)}, bf16[1,384,256]{2,1,0:T(8,128)(2,1)S(1)}, u32[]{:S(2)}, u32[]{:S(2)}) collective-permute-start(bf16[1,384,256]{2,1,0:T(8,128)(2,1)S(1)} %copy-done.16), channel_id=1, source_target_pairs={{0,16},{2,18},{4,20},{6,22},{8,24},{10,26},{12,28},{14,30},{16,0},... | collective-permute-start | bytes 589832 | tf_op jit(solution)/shard_map/ppermute | solution.py:28
  49.2 19.3 %collective-permute-start.9 = (bf16[1,384,256]{2,1,0:T(8,128)(2,1)S(1)}, bf16[1,384,256]{2,1,0:T(8,128)(2,1)S(1)}, u32[]{:S(2)}, u32[]{:S(2)}) collective-permute-start(bf16[1,384,256]{2,1,0:T(8,128)(2,1)S(1)} %copy-done.15), channel_id=1, source_target_pairs={{0,24},{2,26},{4,28},{6,30},{8,16},{10,18},{12,20},{14,22},{16,8},... | collective-permute-start | bytes 589832 | tf_op jit(solution)/shard_map/ppermute | solution.py:28
  56.7 33.5 %collective-permute-start.4 = (bf16[1,384,256]{2,1,0:T(8,128)(2,1)}, bf16[1,384,256]{2,1,0:T(8,128)(2,1)S(1)}, u32[]{:S(2)}, u32[]{:S(2)}) collective-permute-start(bf16[1,384,256]{2,1,0:T(8,128)(2,1)} %get-tuple-element.59), channel_id=1, source_target_pairs={{0,8},{2,10},{4,12},{6,14},{8,0},{10,2},{12,4},{14,6},{16,24},{18,... | collective-permute-start | bytes 589832 | tf_op jit(solution)/shard_map/ppermute | solution.py:28
  56.7 34.1 %collective-permute-start.5 = (bf16[1,384,256]{2,1,0:T(8,128)(2,1)}, bf16[1,384,256]{2,1,0:T(8,128)(2,1)S(1)}, u32[]{:S(2)}, u32[]{:S(2)}) collective-permute-start(bf16[1,384,256]{2,1,0:T(8,128)(2,1)} %get-tuple-element.60), channel_id=1, source_target_pairs={{0,16},{2,18},{4,20},{6,22},{8,24},{10,26},{12,28},{14,30},{16,0},... | collective-permute-start | bytes 589832 | tf_op jit(solution)/shard_map/ppermute | solution.py:28
  65.4 25.4 %collective-permute-start.6 = (bf16[1,384,256]{2,1,0:T(8,128)(2,1)}, bf16[1,384,256]{2,1,0:T(8,128)(2,1)S(1)}, u32[]{:S(2)}, u32[]{:S(2)}) collective-permute-start(bf16[1,384,256]{2,1,0:T(8,128)(2,1)} %get-tuple-element.61), channel_id=1, source_target_pairs={{0,24},{2,26},{4,28},{6,30},{8,16},{10,18},{12,20},{14,22},{16,8},... | collective-permute-start | bytes 589832 | tf_op jit(solution)/shard_map/ppermute | solution.py:28
  69.2 23.2 %collective-permute-start.14 = (bf16[4,384,256]{2,1,0:T(8,128)(2,1)}, bf16[4,384,256]{2,1,0:T(8,128)(2,1)}, u32[]{:S(2)}, u32[]{:S(2)}) collective-permute-start(bf16[4,384,256]{2,1,0:T(8,128)(2,1)} %constant_dynamic-update-slice_fusion.refs_1_), channel_id=1, source_target_pairs={{0,4},{2,6},{4,0},{6,2},{8,12},{10,14},{12,8},{14,10},{16,20},{18,... | collective-permute-start | bytes 2359304 | tf_op jit(solution)/shard_map/ppermute | solution.py:28
  70.3 20.5 %copy-start.6 = (bf16[1,384,256]{2,1,0:T(8,128)(2,1)S(1)}, bf16[1,384,256]{2,1,0:T(8,128)(2,1)}, u32[]{:S(2)}) copy-start(bf16[1,384,256]{2,1,0:T(8,128)(2,1)} %get-tuple-element.71) | copy-start | bytes 589828
  79.1 13.9 %copy-start.13 = (s32[3]{0:T(128)S(1)}, s32[3]{0:T(128)}, u32[]{:S(2)}) copy-start(s32[3]{0:T(128)} %pad_add_fusion.place_ref) | copy-start | bytes 40
  79.1 24.2 %all-to-all-start.1 = ((bf16[4,2,384,128]{3,2,1,0:T(8,128)(2,1)}), bf16[4,2,384,128]{3,2,1,0:T(8,128)(2,1)S(1)}, u32[]{:S(2)}, u32[]{:S(2)}) async-start(bf16[4,2,384,128]{3,2,1,0:T(8,128)(2,1)} %project.5), calls=%async_computation.1 | async-start | bytes 1572864 | tf_op jit(solution)/shard_map/all_to_all | solution.py:413
  90.2 3.3 %collective-permute-start.11 = (bf16[4,384,256]{2,1,0:T(8,128)(2,1)}, bf16[4,384,256]{2,1,0:T(8,128)(2,1)}, u32[]{:S(2)}, u32[]{:S(2)}) collective-permute-start(bf16[4,384,256]{2,1,0:T(8,128)(2,1)} %collective-permute-done.7.refs_6_), channel_id=1, source_target_pairs={{0,2},{2,0},{4,6},{6,4},{8,10},{10,8},{12,14},{14,12},{16,18},{18,... | collective-permute-start | bytes 2359304 | tf_op jit(solution)/shard_map/ppermute | solution.py:28
  90.2 3.5 %collective-permute-start.10 = (bf16[4,384,256]{2,1,0:T(8,128)(2,1)S(1)}, bf16[4,384,256]{2,1,0:T(8,128)(2,1)}, u32[]{:S(2)}, u32[]{:S(2)}) collective-permute-start(bf16[4,384,256]{2,1,0:T(8,128)(2,1)S(1)} %pad_maximum_fusion.refs_4_), channel_id=1, source_target_pairs={{0,2},{2,0},{4,6},{6,4},{8,10},{10,8},{12,14},{14,12},{16,18},{18,... | collective-permute-start | bytes 2359304 | tf_op jit(solution)/shard_map/ppermute | solution.py:28
  90.8 16.9 %copy-start.12 = (bf16[4,384,256]{2,1,0:T(8,128)(2,1)}, bf16[4,384,256]{2,1,0:T(8,128)(2,1)S(1)}, u32[]{:S(2)}) copy-start(bf16[4,384,256]{2,1,0:T(8,128)(2,1)S(1)} %constant_dynamic-update-slice_fusion.4.refs_1_) | copy-start | bytes 2359300
  90.9 19.6 %collective-permute-start.12 = (bf16[4,384,256]{2,1,0:T(8,128)(2,1)S(1)}, bf16[4,384,256]{2,1,0:T(8,128)(2,1)S(1)}, u32[]{:S(2)}, u32[]{:S(2)}) collective-permute-start(bf16[4,384,256]{2,1,0:T(8,128)(2,1)S(1)} %constant_dynamic-update-slice_fusion.4.refs_1_), channel_id=1, source_target_pairs={{0,4},{2,6},{4,0},{6,2},{8,12},{10,14},{12,8},{14,10},{16,20},{18,... | collective-permute-start | bytes 2359304 | tf_op jit(solution)/shard_map/ppermute | solution.py:28
  92.4 18.6 %collective-permute-start.13 = (bf16[4,384,256]{2,1,0:T(8,128)(2,1)}, bf16[4,384,256]{2,1,0:T(8,128)(2,1)}, u32[]{:S(2)}, u32[]{:S(2)}) collective-permute-start(bf16[4,384,256]{2,1,0:T(8,128)(2,1)} %constant_dynamic-update-slice_fusion.refs_1_), channel_id=1, source_target_pairs={{0,2},{2,0},{4,6},{6,4},{8,10},{10,8},{12,14},{14,12},{16,18},{18,... | collective-permute-start | bytes 2359304 | tf_op jit(solution)/shard_map/ppermute | solution.py:28
  92.4 18.6 %collective-permute-start.15 = (bf16[4,384,256]{2,1,0:T(8,128)(2,1)}, bf16[4,384,256]{2,1,0:T(8,128)(2,1)}, u32[]{:S(2)}, u32[]{:S(2)}) collective-permute-start(bf16[4,384,256]{2,1,0:T(8,128)(2,1)} %collective-permute-done.14.refs_3_), channel_id=1, source_target_pairs={{0,2},{2,0},{4,6},{6,4},{8,10},{10,8},{12,14},{14,12},{16,18},{18,... | collective-permute-start | bytes 2359304 | tf_op jit(solution)/shard_map/ppermute | solution.py:28
  103.3 7.7 %copy-start.5 = (bf16[4,2,384,128]{3,2,1,0:T(8,128)(2,1)}, bf16[4,2,384,128]{3,2,1,0:T(8,128)(2,1)S(1)}, u32[]{:S(2)}) copy-start(bf16[4,2,384,128]{3,2,1,0:T(8,128)(2,1)S(1)} %all-to-all-done.1.refs_0_) | copy-start | bytes 2359300
  103.3 16.5 %all-to-all-start = ((bf16[4,384,128]{2,1,0:T(8,128)(2,1)}), bf16[4,384,128]{2,1,0:T(8,128)(2,1)S(1)}, u32[]{:S(2)}, u32[]{:S(2)}) async-start(bf16[4,384,128]{2,1,0:T(8,128)(2,1)} %attend.3), calls=%async_computation | async-start | bytes 786432 | tf_op jit(solution)/shard_map/all_to_all | solution.py:413
  107.8 17.6 %collective-permute-start.16 = (bf16[4,384,256]{2,1,0:T(8,128)(2,1)S(1)}, bf16[4,384,256]{2,1,0:T(8,128)(2,1)}, u32[]{:S(2)}, u32[]{:S(2)}) collective-permute-start(bf16[4,384,256]{2,1,0:T(8,128)(2,1)S(1)} %constant_dynamic-update-slice_fusion.4.refs_1_), channel_id=1, source_target_pairs={{0,2},{2,0},{4,6},{6,4},{8,10},{10,8},{12,14},{14,12},{16,18},{18,... | collective-permute-start | bytes 2359304 | tf_op jit(solution)/shard_map/ppermute | solution.py:28
  110.4 9.3 %copy-start.14 = (bf16[4,384,256]{2,1,0:T(8,128)(2,1)}, bf16[4,384,256]{2,1,0:T(8,128)(2,1)S(1)}, u32[]{:S(2)}) copy-start(bf16[4,384,256]{2,1,0:T(8,128)(2,1)S(1)} %collective-permute-done.12.refs_3_) | copy-start | bytes 2359300
  110.4 15.0 %collective-permute-start.17 = (bf16[4,384,256]{2,1,0:T(8,128)(2,1)S(1)}, bf16[4,384,256]{2,1,0:T(8,128)(2,1)}, u32[]{:S(2)}, u32[]{:S(2)}) collective-permute-start(bf16[4,384,256]{2,1,0:T(8,128)(2,1)S(1)} %collective-permute-done.12.refs_3_), channel_id=1, source_target_pairs={{0,2},{2,0},{4,6},{6,4},{8,10},{10,8},{12,14},{14,12},{16,18},{18,... | collective-permute-start | bytes 2359304 | tf_op jit(solution)/shard_map/ppermute | solution.py:28
  119.8 14.4 %copy-start = (bf16[4,384,128]{2,1,0:T(8,128)(2,1)}, bf16[4,384,128]{2,1,0:T(8,128)(2,1)S(1)}, u32[]{:S(2)}) copy-start(bf16[4,384,128]{2,1,0:T(8,128)(2,1)S(1)} %all-to-all-done.refs_0_) | copy-start | bytes 1179652
  119.8 26.4 %all-to-all-start.2 = ((bf16[4,384,128]{2,1,0:T(8,128)(2,1)}), bf16[4,384,128]{2,1,0:T(8,128)(2,1)S(1)}, u32[]{:S(2)}, u32[]{:S(2)}) async-start(bf16[4,384,128]{2,1,0:T(8,128)(2,1)} %attend.4), calls=%async_computation.2 | async-start | bytes 786432 | tf_op jit(solution)/shard_map/all_to_all | solution.py:413
  134.2 5.4 %collective-permute-start.18 = (bf16[1,384,128]{2,1,0:T(8,128)(2,1)}, bf16[1,384,128]{2,1,0:T(8,128)(2,1)S(1)}, u32[]{:S(2)}, u32[]{:S(2)}) collective-permute-start(bf16[1,384,128]{2,1,0:T(8,128)(2,1)} %get-tuple-element.81), channel_id=1, source_target_pairs={{0,8},{2,10},{4,12},{6,14},{8,0},{10,2},{12,4},{14,6},{16,24},{18,... | collective-permute-start | bytes 294920 | tf_op jit(solution)/shard_map/ppermute | solution.py:28
  136.2 6.9 %collective-permute-start.19 = (bf16[1,384,128]{2,1,0:T(8,128)(2,1)}, bf16[1,384,128]{2,1,0:T(8,128)(2,1)S(1)}, u32[]{:S(2)}, u32[]{:S(2)}) collective-permute-start(bf16[1,384,128]{2,1,0:T(8,128)(2,1)} %get-tuple-element.82), channel_id=1, source_target_pairs={{0,16},{2,18},{4,20},{6,22},{8,24},{10,26},{12,28},{14,30},{16,0},... | collective-permute-start | bytes 294920 | tf_op jit(solution)/shard_map/ppermute | solution.py:28
  138.6 7.6 %collective-permute-start.20 = (bf16[1,384,128]{2,1,0:T(8,128)(2,1)}, bf16[1,384,128]{2,1,0:T(8,128)(2,1)S(1)}, u32[]{:S(2)}, u32[]{:S(2)}) collective-permute-start(bf16[1,384,128]{2,1,0:T(8,128)(2,1)} %get-tuple-element.83), channel_id=1, source_target_pairs={{0,24},{2,26},{4,28},{6,30},{8,16},{10,18},{12,20},{14,22},{16,8},... | collective-permute-start | bytes 294920 | tf_op jit(solution)/shard_map/ppermute | solution.py:28
  146.2 0.8 copy-start.2
  147.0 0.7 copy-start.1
  153.6 27.7 %collective-permute-start.21 = (bf16[384,1536]{1,0:T(8,128)(2,1)}, bf16[384,1536]{1,0:T(8,128)(2,1)S(1)}, u32[]{:S(2)}, u32[]{:S(2)}) collective-permute-start(bf16[384,1536]{1,0:T(8,128)(2,1)} %finish.2), channel_id=1, source_target_pairs={{0,1},{1,0},{2,3},{3,2},{4,5},{5,4},{6,7},{7,6},{8,9},{9,8},{10,11... | collective-permute-start | bytes 3538952 | tf_op jit(solution)/shard_map/ppermute | solution.py:28
  181.4 1.0 copy-start.3
